TPU v7x, 32 devices: a whole 2x2x4 slice. The times are simulated.
32 devices in a mesh: tm: 16 (over z, y, core), row: 2 (over x).
Axes of the slice: x: 2, y: 2, z: 4, core: 2. Of those that a mesh axis runs over, the one named last changes fastest.
Arguments:
- normals: float32 [16, 32, 1024], P('tm', None, 'row'), may hold values from -6 to 6
- inv_diag: float32 [16, 4, 256, 256], P('tm', 'row'), may hold values from -0.4 to 1.4, as said below
- lag_coupling: float32 [16, 4, 512, 256], P('tm', 'row'), may hold values from -0.25 to 0.25
- fill_mask: int32 [16, 4, 3], P('tm', 'row'), may hold values 0 or 1
Outputs:
- posterior: float32 [16, 32, 1024], P('tm', None, 'row')
Inputs may be any that keep to these rules, and one draw needn't show every extreme that they name: inv_diag[t, i] is the transposed inverse of the diagonal block of the factor for time t and spatial block i.
All inputs are finite; a program needn't handle non-finite values. No bound on the sum of `fill_mask` on one device may be relied on, other than what follows from the above.
Results may differ from a plain program's by a relative error of at most 0.00025.
Values sent between devices are 32-bit elements; how exact they have to be, the bound alone decides.
No kernel may reach another device: no remote copies, remote signals or barrier semaphores. Data moves between devices by JAX's collectives and lax.ppermute only.
A program may use at most 64 MiB of HBM per device.

v0:
```python
import jax
import jax.numpy as jnp
from jax import lax
from jax.sharding import PartitionSpec as P


def shifted(value, axis, steps):
    count = lax.axis_size(axis)
    leading, last = (max(0, -steps), min(count, count - steps))
    return lax.ppermute(value, axis, [(source, source + steps) for source in range(leading, last)])


def padded(block, sides, width):
    for axis, dim in sides:
        count = lax.axis_size(axis)
        forward = [(i, i + 1) for i in range(count - 1)]
        backward = [(target, source) for source, target in forward]
        low = lax.ppermute(
            lax.slice_in_dim(block, block.shape[dim] - width, None, axis=dim), axis, forward
        )
        high = lax.ppermute(lax.slice_in_dim(block, 0, width, axis=dim), axis, backward)
        block = jnp.concatenate([low, block, high], axis=dim)
    return block


def rim_weights(fill_mask, block_len, rim_len):
    flags = fill_mask.astype(jnp.float32)
    return jnp.concatenate(
        [
            jnp.repeat(flags[:, 0:1], rim_len, axis=1),
            jnp.repeat(flags[:, 1:2], block_len, axis=1),
            jnp.repeat(flags[:, 2:3], rim_len, axis=1),
        ],
        axis=1,
    )


def advance(extended, normals_panel, inv_blocks, lag_blocks, weights):
    block_count = inv_blocks.shape[0]
    block_len = inv_blocks.shape[1]
    win_len = lag_blocks.shape[1]
    panel_cols = extended.shape[0]
    windows = jnp.stack(
        [
            extended[:, position * block_len : position * block_len + win_len]
            for position in range(block_count)
        ],
        axis=1,
    )
    coupled = jnp.einsum(
        "cbw,bwk->cbk", windows * weights[None], lag_blocks, precision=lax.Precision.HIGHEST
    )
    residue = normals_panel.reshape(panel_cols, block_count, block_len) - coupled
    solved = jnp.einsum("cbk,bkj->cbj", residue, inv_blocks, precision=lax.Precision.HIGHEST)
    return solved.reshape(panel_cols, block_count * block_len)


def local(normals, inv_diag, lag_coupling, fill_mask):
    chain_len = lax.axis_size("tm")
    device = lax.axis_index("tm")
    columns = normals.shape[1]
    sites_here = normals.shape[2]
    block_len = inv_diag.shape[2]
    rim_len = (lag_coupling.shape[2] - block_len) // 2
    panels = 1
    panel_cols = columns // panels
    weights = rim_weights(fill_mask[0], block_len, rim_len)
    local_normals = normals[0]
    inv_blocks = inv_diag[0]
    lag_blocks = lag_coupling[0]

    def turn(section_num, carry):
        outgoing, result = carry
        incoming = shifted(outgoing, "tm", -1)
        extended = padded(incoming, (("row", 1),), rim_len)
        panel_num = section_num - (chain_len - 1 - device)
        active = (panel_num >= 0) & (panel_num < panels)
        solved = advance(extended, local_normals, inv_blocks, lag_blocks, weights)
        solved = jnp.where(active, solved, jnp.zeros_like(solved))
        result = jnp.where(active, solved, result)
        return (solved, result)

    outgoing = jnp.zeros((panel_cols, sites_here), jnp.float32)
    result = jnp.zeros((columns, sites_here), jnp.float32)
    _, result = lax.fori_loop(0, chain_len + panels - 1, turn, (outgoing, result))
    return result[None]


def solution(mesh):
    placed = (
        P("tm", None, "row"),
        P("tm", "row", None, None),
        P("tm", "row", None, None),
        P("tm", "row", None),
    )
    return jax.shard_map(
        local, mesh=mesh, in_specs=placed, out_specs=P("tm", None, "row"), check_vma=False
    )
```

profile of v0, /device:TPU:13, one launch (start us, length us, event | category | flops | bytes accessed | tf_op | source)
XLA Modules:
  0.0 246.2 jit_solution(17517435615280251396)
XLA Ops:
  2.0 243.5 %while.19 = (s32[]{:T(128)}, f32[32,512]{1,0:T(8,128)S(1)}, f32[32,512]{1,0:T(8,128)S(1)}, s32[]{:T(128)}, f32[1,32,512]{2,1,0:T(8,128)}, /*index=5*/f32[2,512]{...) while((s32[]{:T(128)}, f32[32,512]{1,0:T(8,128)S(1)}, ...), condition=%wide.wide.region_1.2_spmd.clone, body=%wide.wide.region_0.1_spmd.clone.sunk | while | flops 151158784 | bytes 5083438 | solution.py:85
  2.0 2.6 %collective-permute-start = (f32[32,512]{1,0:T(8,128)S(1)}, f32[32,512]{1,0:T(8,128)S(1)}, u32[]{:S(2)}, u32[]{:S(2)}) collective-permute-start(f32[32,512]{1,0:T(8,128)S(1)} %get-tuple-element.358), channel_id=1, source_target_pairs={{2,0},{4,2},{6,4},{8,6},{10,8},{12,10},{14,12},{16,14},{18,16},{20... | collective-permute-start | bytes 196616 | tf_op jit(solution)/shard_map/while/body/eval_jaxpr/ppermute | solution.py:10
  4.6 3.9 %collective-permute-done = f32[32,512]{1,0:T(8,128)S(1)} collective-permute-done((f32[32,512]{1,0:T(8,128)S(1)}, f32[32,512]{1,0:T(8,128)S(1)}, u32[]{:S(2)}, u32[]{:S(2)}) %collective-permute-start) | collective-permute-done | bytes 65568 | tf_op jit(solution)/shard_map/while/body/eval_jaxpr/ppermute | solution.py:10
  8.5 3.1 %collective-permute-start.1 = (f32[32,128]{1,0:T(8,128)S(1)}, f32[32,128]{1,0:T(8,128)S(1)}, u32[]{:S(2)}, u32[]{:S(2)}) collective-permute-start(f32[32,128]{1,0:T(8,128)S(1)} %get-tuple-element.342), channel_id=1, source_target_pairs={{0,1},{2,3},{4,5},{6,7},{8,9},{10,11},{12,13},{14,15},{16,17},{18,... | collective-permute-start | bytes 49160 | tf_op jit(solution)/shard_map/while/body/eval_jaxpr/ppermute | solution.py:18
  12.9 3.2 %collective-permute-done.2 = f32[32,128]{1,0:T(8,128)S(1)} collective-permute-done((f32[32,128]{1,0:T(8,128)S(1)}, f32[32,128]{1,0:T(8,128)S(1)}, u32[]{:S(2)}, u32[]{:S(2)}) %collective-permute-start.2) | collective-permute-done | bytes 16416 | tf_op jit(solution)/shard_map/while/body/eval_jaxpr/ppermute | solution.py:21
  16.1 2.0 fusion.31
  20.5 4.6 %collective-permute-done = f32[32,512]{1,0:T(8,128)S(1)} collective-permute-done((f32[32,512]{1,0:T(8,128)S(1)}, f32[32,512]{1,0:T(8,128)S(1)}, u32[]{:S(2)}, u32[]{:S(2)}) %collective-permute-start) | collective-permute-done | bytes 65568 | tf_op jit(solution)/shard_map/while/body/eval_jaxpr/ppermute | solution.py:10
  28.1 3.2 %collective-permute-done.2 = f32[32,128]{1,0:T(8,128)S(1)} collective-permute-done((f32[32,128]{1,0:T(8,128)S(1)}, f32[32,128]{1,0:T(8,128)S(1)}, u32[]{:S(2)}, u32[]{:S(2)}) %collective-permute-start.2) | collective-permute-done | bytes 16416 | tf_op jit(solution)/shard_map/while/body/eval_jaxpr/ppermute | solution.py:21
  31.2 2.0 fusion.31
  35.7 4.6 %collective-permute-done = f32[32,512]{1,0:T(8,128)S(1)} collective-permute-done((f32[32,512]{1,0:T(8,128)S(1)}, f32[32,512]{1,0:T(8,128)S(1)}, u32[]{:S(2)}, u32[]{:S(2)}) %collective-permute-start) | collective-permute-done | bytes 65568 | tf_op jit(solution)/shard_map/while/body/eval_jaxpr/ppermute | solution.py:10
  43.2 3.2 %collective-permute-done.2 = f32[32,128]{1,0:T(8,128)S(1)} collective-permute-done((f32[32,128]{1,0:T(8,128)S(1)}, f32[32,128]{1,0:T(8,128)S(1)}, u32[]{:S(2)}, u32[]{:S(2)}) %collective-permute-start.2) | collective-permute-done | bytes 16416 | tf_op jit(solution)/shard_map/while/body/eval_jaxpr/ppermute | solution.py:21
  46.4 2.0 fusion.31
  50.8 4.6 %collective-permute-done = f32[32,512]{1,0:T(8,128)S(1)} collective-permute-done((f32[32,512]{1,0:T(8,128)S(1)}, f32[32,512]{1,0:T(8,128)S(1)}, u32[]{:S(2)}, u32[]{:S(2)}) %collective-permute-start) | collective-permute-done | bytes 65568 | tf_op jit(solution)/shard_map/while/body/eval_jaxpr/ppermute | solution.py:10
  58.3 3.2 %collective-permute-done.2 = f32[32,128]{1,0:T(8,128)S(1)} collective-permute-done((f32[32,128]{1,0:T(8,128)S(1)}, f32[32,128]{1,0:T(8,128)S(1)}, u32[]{:S(2)}, u32[]{:S(2)}) %collective-permute-start.2) | collective-permute-done | bytes 16416 | tf_op jit(solution)/shard_map/while/body/eval_jaxpr/ppermute | solution.py:21
  61.5 2.0 fusion.31
  65.9 4.6 %collective-permute-done = f32[32,512]{1,0:T(8,128)S(1)} collective-permute-done((f32[32,512]{1,0:T(8,128)S(1)}, f32[32,512]{1,0:T(8,128)S(1)}, u32[]{:S(2)}, u32[]{:S(2)}) %collective-permute-start) | collective-permute-done | bytes 65568 | tf_op jit(solution)/shard_map/while/body/eval_jaxpr/ppermute | solution.py:10
  73.4 3.2 %collective-permute-done.2 = f32[32,128]{1,0:T(8,128)S(1)} collective-permute-done((f32[32,128]{1,0:T(8,128)S(1)}, f32[32,128]{1,0:T(8,128)S(1)}, u32[]{:S(2)}, u32[]{:S(2)}) %collective-permute-start.2) | collective-permute-done | bytes 16416 | tf_op jit(solution)/shard_map/while/body/eval_jaxpr/ppermute | solution.py:21
  76.6 2.0 fusion.31
  81.0 4.6 %collective-permute-done = f32[32,512]{1,0:T(8,128)S(1)} collective-permute-done((f32[32,512]{1,0:T(8,128)S(1)}, f32[32,512]{1,0:T(8,128)S(1)}, u32[]{:S(2)}, u32[]{:S(2)}) %collective-permute-start) | collective-permute-done | bytes 65568 | tf_op jit(solution)/shard_map/while/body/eval_jaxpr/ppermute | solution.py:10
  88.6 3.2 %collective-permute-done.2 = f32[32,128]{1,0:T(8,128)S(1)} collective-permute-done((f32[32,128]{1,0:T(8,128)S(1)}, f32[32,128]{1,0:T(8,128)S(1)}, u32[]{:S(2)}, u32[]{:S(2)}) %collective-permute-start.2) | collective-permute-done | bytes 16416 | tf_op jit(solution)/shard_map/while/body/eval_jaxpr/ppermute | solution.py:21
  91.8 2.0 fusion.31
  96.2 4.6 %collective-permute-done = f32[32,512]{1,0:T(8,128)S(1)} collective-permute-done((f32[32,512]{1,0:T(8,128)S(1)}, f32[32,512]{1,0:T(8,128)S(1)}, u32[]{:S(2)}, u32[]{:S(2)}) %collective-permute-start) | collective-permute-done | bytes 65568 | tf_op jit(solution)/shard_map/while/body/eval_jaxpr/ppermute | solution.py:10
  103.7 3.2 %collective-permute-done.2 = f32[32,128]{1,0:T(8,128)S(1)} collective-permute-done((f32[32,128]{1,0:T(8,128)S(1)}, f32[32,128]{1,0:T(8,128)S(1)}, u32[]{:S(2)}, u32[]{:S(2)}) %collective-permute-start.2) | collective-permute-done | bytes 16416 | tf_op jit(solution)/shard_map/while/body/eval_jaxpr/ppermute | solution.py:21
  106.9 2.0 fusion.31
  111.3 4.6 %collective-permute-done = f32[32,512]{1,0:T(8,128)S(1)} collective-permute-done((f32[32,512]{1,0:T(8,128)S(1)}, f32[32,512]{1,0:T(8,128)S(1)}, u32[]{:S(2)}, u32[]{:S(2)}) %collective-permute-start) | collective-permute-done | bytes 65568 | tf_op jit(solution)/shard_map/while/body/eval_jaxpr/ppermute | solution.py:10
  118.8 3.2 %collective-permute-done.2 = f32[32,128]{1,0:T(8,128)S(1)} collective-permute-done((f32[32,128]{1,0:T(8,128)S(1)}, f32[32,128]{1,0:T(8,128)S(1)}, u32[]{:S(2)}, u32[]{:S(2)}) %collective-permute-start.2) | collective-permute-done | bytes 16416 | tf_op jit(solution)/shard_map/while/body/eval_jaxpr/ppermute | solution.py:21
  122.0 2.0 fusion.31
  126.4 4.6 %collective-permute-done = f32[32,512]{1,0:T(8,128)S(1)} collective-permute-done((f32[32,512]{1,0:T(8,128)S(1)}, f32[32,512]{1,0:T(8,128)S(1)}, u32[]{:S(2)}, u32[]{:S(2)}) %collective-permute-start) | collective-permute-done | bytes 65568 | tf_op jit(solution)/shard_map/while/body/eval_jaxpr/ppermute | solution.py:10
  134.0 3.2 %collective-permute-done.2 = f32[32,128]{1,0:T(8,128)S(1)} collective-permute-done((f32[32,128]{1,0:T(8,128)S(1)}, f32[32,128]{1,0:T(8,128)S(1)}, u32[]{:S(2)}, u32[]{:S(2)}) %collective-permute-start.2) | collective-permute-done | bytes 16416 | tf_op jit(solution)/shard_map/while/body/eval_jaxpr/ppermute | solution.py:21
  137.1 2.0 fusion.31
  141.6 4.6 %collective-permute-done = f32[32,512]{1,0:T(8,128)S(1)} collective-permute-done((f32[32,512]{1,0:T(8,128)S(1)}, f32[32,512]{1,0:T(8,128)S(1)}, u32[]{:S(2)}, u32[]{:S(2)}) %collective-permute-start) | collective-permute-done | bytes 65568 | tf_op jit(solution)/shard_map/while/body/eval_jaxpr/ppermute | solution.py:10
  149.1 3.2 %collective-permute-done.2 = f32[32,128]{1,0:T(8,128)S(1)} collective-permute-done((f32[32,128]{1,0:T(8,128)S(1)}, f32[32,128]{1,0:T(8,128)S(1)}, u32[]{:S(2)}, u32[]{:S(2)}) %collective-permute-start.2) | collective-permute-done | bytes 16416 | tf_op jit(solution)/shard_map/while/body/eval_jaxpr/ppermute | solution.py:21
  152.3 2.0 fusion.31
  156.7 4.6 %collective-permute-done = f32[32,512]{1,0:T(8,128)S(1)} collective-permute-done((f32[32,512]{1,0:T(8,128)S(1)}, f32[32,512]{1,0:T(8,128)S(1)}, u32[]{:S(2)}, u32[]{:S(2)}) %collective-permute-start) | collective-permute-done | bytes 65568 | tf_op jit(solution)/shard_map/while/body/eval_jaxpr/ppermute | solution.py:10
  164.2 3.2 %collective-permute-done.2 = f32[32,128]{1,0:T(8,128)S(1)} collective-permute-done((f32[32,128]{1,0:T(8,128)S(1)}, f32[32,128]{1,0:T(8,128)S(1)}, u32[]{:S(2)}, u32[]{:S(2)}) %collective-permute-start.2) | collective-permute-done | bytes 16416 | tf_op jit(solution)/shard_map/while/body/eval_jaxpr/ppermute | solution.py:21
  167.4 2.0 fusion.31
  171.8 4.6 %collective-permute-done = f32[32,512]{1,0:T(8,128)S(1)} collective-permute-done((f32[32,512]{1,0:T(8,128)S(1)}, f32[32,512]{1,0:T(8,128)S(1)}, u32[]{:S(2)}, u32[]{:S(2)}) %collective-permute-start) | collective-permute-done | bytes 65568 | tf_op jit(solution)/shard_map/while/body/eval_jaxpr/ppermute | solution.py:10
  179.3 3.2 %collective-permute-done.2 = f32[32,128]{1,0:T(8,128)S(1)} collective-permute-done((f32[32,128]{1,0:T(8,128)S(1)}, f32[32,128]{1,0:T(8,128)S(1)}, u32[]{:S(2)}, u32[]{:S(2)}) %collective-permute-start.2) | collective-permute-done | bytes 16416 | tf_op jit(solution)/shard_map/while/body/eval_jaxpr/ppermute | solution.py:21
  186.9 4.6 %collective-permute-done = f32[32,512]{1,0:T(8,128)S(1)} collective-permute-done((f32[32,512]{1,0:T(8,128)S(1)}, f32[32,512]{1,0:T(8,128)S(1)}, u32[]{:S(2)}, u32[]{:S(2)}) %collective-permute-start) | collective-permute-done | bytes 65568 | tf_op jit(solution)/shard_map/while/body/eval_jaxpr/ppermute | solution.py:10
  194.5 3.2 %collective-permute-done.2 = f32[32,128]{1,0:T(8,128)S(1)} collective-permute-done((f32[32,128]{1,0:T(8,128)S(1)}, f32[32,128]{1,0:T(8,128)S(1)}, u32[]{:S(2)}, u32[]{:S(2)}) %collective-permute-start.2) | collective-permute-done | bytes 16416 | tf_op jit(solution)/shard_map/while/body/eval_jaxpr/ppermute | solution.py:21
  197.7 2.0 fusion.31
  202.1 4.6 %collective-permute-done = f32[32,512]{1,0:T(8,128)S(1)} collective-permute-done((f32[32,512]{1,0:T(8,128)S(1)}, f32[32,512]{1,0:T(8,128)S(1)}, u32[]{:S(2)}, u32[]{:S(2)}) %collective-permute-start) | collective-permute-done | bytes 65568 | tf_op jit(solution)/shard_map/while/body/eval_jaxpr/ppermute | solution.py:10
  209.6 3.2 %collective-permute-done.2 = f32[32,128]{1,0:T(8,128)S(1)} collective-permute-done((f32[32,128]{1,0:T(8,128)S(1)}, f32[32,128]{1,0:T(8,128)S(1)}, u32[]{:S(2)}, u32[]{:S(2)}) %collective-permute-start.2) | collective-permute-done | bytes 16416 | tf_op jit(solution)/shard_map/while/body/eval_jaxpr/ppermute | solution.py:21
  217.2 4.6 %collective-permute-done = f32[32,512]{1,0:T(8,128)S(1)} collective-permute-done((f32[32,512]{1,0:T(8,128)S(1)}, f32[32,512]{1,0:T(8,128)S(1)}, u32[]{:S(2)}, u32[]{:S(2)}) %collective-permute-start) | collective-permute-done | bytes 65568 | tf_op jit(solution)/shard_map/while/body/eval_jaxpr/ppermute | solution.py:10
  224.7 3.2 %collective-permute-done.2 = f32[32,128]{1,0:T(8,128)S(1)} collective-permute-done((f32[32,128]{1,0:T(8,128)S(1)}, f32[32,128]{1,0:T(8,128)S(1)}, u32[]{:S(2)}, u32[]{:S(2)}) %collective-permute-start.2) | collective-permute-done | bytes 16416 | tf_op jit(solution)/shard_map/while/body/eval_jaxpr/ppermute | solution.py:21
  227.9 2.0 fusion.31
  232.3 4.6 %collective-permute-done = f32[32,512]{1,0:T(8,128)S(1)} collective-permute-done((f32[32,512]{1,0:T(8,128)S(1)}, f32[32,512]{1,0:T(8,128)S(1)}, u32[]{:S(2)}, u32[]{:S(2)}) %collective-permute-start) | collective-permute-done | bytes 65568 | tf_op jit(solution)/shard_map/while/body/eval_jaxpr/ppermute | solution.py:10
  239.9 3.2 %collective-permute-done.2 = f32[32,128]{1,0:T(8,128)S(1)} collective-permute-done((f32[32,128]{1,0:T(8,128)S(1)}, f32[32,128]{1,0:T(8,128)S(1)}, u32[]{:S(2)}, u32[]{:S(2)}) %collective-permute-start.2) | collective-permute-done | bytes 16416 | tf_op jit(solution)/shard_map/while/body/eval_jaxpr/ppermute | solution.py:21
  (188 shorter events, 90.0 us)
Async XLA Ops:
  2.0 6.5 %collective-permute-start = (f32[32,512]{1,0:T(8,128)S(1)}, f32[32,512]{1,0:T(8,128)S(1)}, u32[]{:S(2)}, u32[]{:S(2)}) collective-permute-start(f32[32,512]{1,0:T(8,128)S(1)} %get-tuple-element.358), channel_id=1, source_target_pairs={{2,0},{4,2},{6,4},{8,6},{10,8},{12,10},{14,12},{16,14},{18,16},{20... | collective-permute-start | bytes 196616 | tf_op jit(solution)/shard_map/while/body/eval_jaxpr/ppermute | solution.py:10
  8.5 4.4 %collective-permute-start.1 = (f32[32,128]{1,0:T(8,128)S(1)}, f32[32,128]{1,0:T(8,128)S(1)}, u32[]{:S(2)}, u32[]{:S(2)}) collective-permute-start(f32[32,128]{1,0:T(8,128)S(1)} %get-tuple-element.342), channel_id=1, source_target_pairs={{0,1},{2,3},{4,5},{6,7},{8,9},{10,11},{12,13},{14,15},{16,17},{18,... | collective-permute-start | bytes 49160 | tf_op jit(solution)/shard_map/while/body/eval_jaxpr/ppermute | solution.py:18
  11.6 4.5 %collective-permute-start.2 = (f32[32,128]{1,0:T(8,128)S(1)}, f32[32,128]{1,0:T(8,128)S(1)}, u32[]{:S(2)}, u32[]{:S(2)}) collective-permute-start(f32[32,128]{1,0:T(8,128)S(1)} %get-tuple-element.343), channel_id=1, source_target_pairs={{1,0},{3,2},{5,4},{7,6},{9,8},{11,10},{13,12},{15,14},{17,16},{19,... | collective-permute-start | bytes 49160 | tf_op jit(solution)/shard_map/while/body/eval_jaxpr/ppermute | solution.py:21
  18.6 6.5 %collective-permute-start = (f32[32,512]{1,0:T(8,128)S(1)}, f32[32,512]{1,0:T(8,128)S(1)}, u32[]{:S(2)}, u32[]{:S(2)}) collective-permute-start(f32[32,512]{1,0:T(8,128)S(1)} %get-tuple-element.358), channel_id=1, source_target_pairs={{2,0},{4,2},{6,4},{8,6},{10,8},{12,10},{14,12},{16,14},{18,16},{20... | collective-permute-start | bytes 196616 | tf_op jit(solution)/shard_map/while/body/eval_jaxpr/ppermute | solution.py:10
  25.1 3.0 %collective-permute-start.1 = (f32[32,128]{1,0:T(8,128)S(1)}, f32[32,128]{1,0:T(8,128)S(1)}, u32[]{:S(2)}, u32[]{:S(2)}) collective-permute-start(f32[32,128]{1,0:T(8,128)S(1)} %get-tuple-element.342), channel_id=1, source_target_pairs={{0,1},{2,3},{4,5},{6,7},{8,9},{10,11},{12,13},{14,15},{16,17},{18,... | collective-permute-start | bytes 49160 | tf_op jit(solution)/shard_map/while/body/eval_jaxpr/ppermute | solution.py:18
  26.7 4.5 %collective-permute-start.2 = (f32[32,128]{1,0:T(8,128)S(1)}, f32[32,128]{1,0:T(8,128)S(1)}, u32[]{:S(2)}, u32[]{:S(2)}) collective-permute-start(f32[32,128]{1,0:T(8,128)S(1)} %get-tuple-element.343), channel_id=1, source_target_pairs={{1,0},{3,2},{5,4},{7,6},{9,8},{11,10},{13,12},{15,14},{17,16},{19,... | collective-permute-start | bytes 49160 | tf_op jit(solution)/shard_map/while/body/eval_jaxpr/ppermute | solution.py:21
  33.7 6.5 %collective-permute-start = (f32[32,512]{1,0:T(8,128)S(1)}, f32[32,512]{1,0:T(8,128)S(1)}, u32[]{:S(2)}, u32[]{:S(2)}) collective-permute-start(f32[32,512]{1,0:T(8,128)S(1)} %get-tuple-element.358), channel_id=1, source_target_pairs={{2,0},{4,2},{6,4},{8,6},{10,8},{12,10},{14,12},{16,14},{18,16},{20... | collective-permute-start | bytes 196616 | tf_op jit(solution)/shard_map/while/body/eval_jaxpr/ppermute | solution.py:10
  40.2 3.0 %collective-permute-start.1 = (f32[32,128]{1,0:T(8,128)S(1)}, f32[32,128]{1,0:T(8,128)S(1)}, u32[]{:S(2)}, u32[]{:S(2)}) collective-permute-start(f32[32,128]{1,0:T(8,128)S(1)} %get-tuple-element.342), channel_id=1, source_target_pairs={{0,1},{2,3},{4,5},{6,7},{8,9},{10,11},{12,13},{14,15},{16,17},{18,... | collective-permute-start | bytes 49160 | tf_op jit(solution)/shard_map/while/body/eval_jaxpr/ppermute | solution.py:18
  41.9 4.5 %collective-permute-start.2 = (f32[32,128]{1,0:T(8,128)S(1)}, f32[32,128]{1,0:T(8,128)S(1)}, u32[]{:S(2)}, u32[]{:S(2)}) collective-permute-start(f32[32,128]{1,0:T(8,128)S(1)} %get-tuple-element.343), channel_id=1, source_target_pairs={{1,0},{3,2},{5,4},{7,6},{9,8},{11,10},{13,12},{15,14},{17,16},{19,... | collective-permute-start | bytes 49160 | tf_op jit(solution)/shard_map/while/body/eval_jaxpr/ppermute | solution.py:21
  48.9 6.5 %collective-permute-start = (f32[32,512]{1,0:T(8,128)S(1)}, f32[32,512]{1,0:T(8,128)S(1)}, u32[]{:S(2)}, u32[]{:S(2)}) collective-permute-start(f32[32,512]{1,0:T(8,128)S(1)} %get-tuple-element.358), channel_id=1, source_target_pairs={{2,0},{4,2},{6,4},{8,6},{10,8},{12,10},{14,12},{16,14},{18,16},{20... | collective-permute-start | bytes 196616 | tf_op jit(solution)/shard_map/while/body/eval_jaxpr/ppermute | solution.py:10
  55.3 3.0 %collective-permute-start.1 = (f32[32,128]{1,0:T(8,128)S(1)}, f32[32,128]{1,0:T(8,128)S(1)}, u32[]{:S(2)}, u32[]{:S(2)}) collective-permute-start(f32[32,128]{1,0:T(8,128)S(1)} %get-tuple-element.342), channel_id=1, source_target_pairs={{0,1},{2,3},{4,5},{6,7},{8,9},{10,11},{12,13},{14,15},{16,17},{18,... | collective-permute-start | bytes 49160 | tf_op jit(solution)/shard_map/while/body/eval_jaxpr/ppermute | solution.py:18
  57.0 4.5 %collective-permute-start.2 = (f32[32,128]{1,0:T(8,128)S(1)}, f32[32,128]{1,0:T(8,128)S(1)}, u32[]{:S(2)}, u32[]{:S(2)}) collective-permute-start(f32[32,128]{1,0:T(8,128)S(1)} %get-tuple-element.343), channel_id=1, source_target_pairs={{1,0},{3,2},{5,4},{7,6},{9,8},{11,10},{13,12},{15,14},{17,16},{19,... | collective-permute-start | bytes 49160 | tf_op jit(solution)/shard_map/while/body/eval_jaxpr/ppermute | solution.py:21
  64.0 6.5 %collective-permute-start = (f32[32,512]{1,0:T(8,128)S(1)}, f32[32,512]{1,0:T(8,128)S(1)}, u32[]{:S(2)}, u32[]{:S(2)}) collective-permute-start(f32[32,512]{1,0:T(8,128)S(1)} %get-tuple-element.358), channel_id=1, source_target_pairs={{2,0},{4,2},{6,4},{8,6},{10,8},{12,10},{14,12},{16,14},{18,16},{20... | collective-permute-start | bytes 196616 | tf_op jit(solution)/shard_map/while/body/eval_jaxpr/ppermute | solution.py:10
  70.5 3.0 %collective-permute-start.1 = (f32[32,128]{1,0:T(8,128)S(1)}, f32[32,128]{1,0:T(8,128)S(1)}, u32[]{:S(2)}, u32[]{:S(2)}) collective-permute-start(f32[32,128]{1,0:T(8,128)S(1)} %get-tuple-element.342), channel_id=1, source_target_pairs={{0,1},{2,3},{4,5},{6,7},{8,9},{10,11},{12,13},{14,15},{16,17},{18,... | collective-permute-start | bytes 49160 | tf_op jit(solution)/shard_map/while/body/eval_jaxpr/ppermute | solution.py:18
  72.1 4.5 %collective-permute-start.2 = (f32[32,128]{1,0:T(8,128)S(1)}, f32[32,128]{1,0:T(8,128)S(1)}, u32[]{:S(2)}, u32[]{:S(2)}) collective-permute-start(f32[32,128]{1,0:T(8,128)S(1)} %get-tuple-element.343), channel_id=1, source_target_pairs={{1,0},{3,2},{5,4},{7,6},{9,8},{11,10},{13,12},{15,14},{17,16},{19,... | collective-permute-start | bytes 49160 | tf_op jit(solution)/shard_map/while/body/eval_jaxpr/ppermute | solution.py:21
  79.1 6.5 %collective-permute-start = (f32[32,512]{1,0:T(8,128)S(1)}, f32[32,512]{1,0:T(8,128)S(1)}, u32[]{:S(2)}, u32[]{:S(2)}) collective-permute-start(f32[32,512]{1,0:T(8,128)S(1)} %get-tuple-element.358), channel_id=1, source_target_pairs={{2,0},{4,2},{6,4},{8,6},{10,8},{12,10},{14,12},{16,14},{18,16},{20... | collective-permute-start | bytes 196616 | tf_op jit(solution)/shard_map/while/body/eval_jaxpr/ppermute | solution.py:10
  85.6 3.0 %collective-permute-start.1 = (f32[32,128]{1,0:T(8,128)S(1)}, f32[32,128]{1,0:T(8,128)S(1)}, u32[]{:S(2)}, u32[]{:S(2)}) collective-permute-start(f32[32,128]{1,0:T(8,128)S(1)} %get-tuple-element.342), channel_id=1, source_target_pairs={{0,1},{2,3},{4,5},{6,7},{8,9},{10,11},{12,13},{14,15},{16,17},{18,... | collective-permute-start | bytes 49160 | tf_op jit(solution)/shard_map/while/body/eval_jaxpr/ppermute | solution.py:18
  87.3 4.5 %collective-permute-start.2 = (f32[32,128]{1,0:T(8,128)S(1)}, f32[32,128]{1,0:T(8,128)S(1)}, u32[]{:S(2)}, u32[]{:S(2)}) collective-permute-start(f32[32,128]{1,0:T(8,128)S(1)} %get-tuple-element.343), channel_id=1, source_target_pairs={{1,0},{3,2},{5,4},{7,6},{9,8},{11,10},{13,12},{15,14},{17,16},{19,... | collective-permute-start | bytes 49160 | tf_op jit(solution)/shard_map/while/body/eval_jaxpr/ppermute | solution.py:21
  94.2 6.5 %collective-permute-start = (f32[32,512]{1,0:T(8,128)S(1)}, f32[32,512]{1,0:T(8,128)S(1)}, u32[]{:S(2)}, u32[]{:S(2)}) collective-permute-start(f32[32,512]{1,0:T(8,128)S(1)} %get-tuple-element.358), channel_id=1, source_target_pairs={{2,0},{4,2},{6,4},{8,6},{10,8},{12,10},{14,12},{16,14},{18,16},{20... | collective-permute-start | bytes 196616 | tf_op jit(solution)/shard_map/while/body/eval_jaxpr/ppermute | solution.py:10
  100.7 3.0 %collective-permute-start.1 = (f32[32,128]{1,0:T(8,128)S(1)}, f32[32,128]{1,0:T(8,128)S(1)}, u32[]{:S(2)}, u32[]{:S(2)}) collective-permute-start(f32[32,128]{1,0:T(8,128)S(1)} %get-tuple-element.342), channel_id=1, source_target_pairs={{0,1},{2,3},{4,5},{6,7},{8,9},{10,11},{12,13},{14,15},{16,17},{18,... | collective-permute-start | bytes 49160 | tf_op jit(solution)/shard_map/while/body/eval_jaxpr/ppermute | solution.py:18
  102.4 4.5 %collective-permute-start.2 = (f32[32,128]{1,0:T(8,128)S(1)}, f32[32,128]{1,0:T(8,128)S(1)}, u32[]{:S(2)}, u32[]{:S(2)}) collective-permute-start(f32[32,128]{1,0:T(8,128)S(1)} %get-tuple-element.343), channel_id=1, source_target_pairs={{1,0},{3,2},{5,4},{7,6},{9,8},{11,10},{13,12},{15,14},{17,16},{19,... | collective-permute-start | bytes 49160 | tf_op jit(solution)/shard_map/while/body/eval_jaxpr/ppermute | solution.py:21
  109.4 6.5 %collective-permute-start = (f32[32,512]{1,0:T(8,128)S(1)}, f32[32,512]{1,0:T(8,128)S(1)}, u32[]{:S(2)}, u32[]{:S(2)}) collective-permute-start(f32[32,512]{1,0:T(8,128)S(1)} %get-tuple-element.358), channel_id=1, source_target_pairs={{2,0},{4,2},{6,4},{8,6},{10,8},{12,10},{14,12},{16,14},{18,16},{20... | collective-permute-start | bytes 196616 | tf_op jit(solution)/shard_map/while/body/eval_jaxpr/ppermute | solution.py:10
  115.9 3.0 %collective-permute-start.1 = (f32[32,128]{1,0:T(8,128)S(1)}, f32[32,128]{1,0:T(8,128)S(1)}, u32[]{:S(2)}, u32[]{:S(2)}) collective-permute-start(f32[32,128]{1,0:T(8,128)S(1)} %get-tuple-element.342), channel_id=1, source_target_pairs={{0,1},{2,3},{4,5},{6,7},{8,9},{10,11},{12,13},{14,15},{16,17},{18,... | collective-permute-start | bytes 49160 | tf_op jit(solution)/shard_map/while/body/eval_jaxpr/ppermute | solution.py:18
  117.5 4.5 %collective-permute-start.2 = (f32[32,128]{1,0:T(8,128)S(1)}, f32[32,128]{1,0:T(8,128)S(1)}, u32[]{:S(2)}, u32[]{:S(2)}) collective-permute-start(f32[32,128]{1,0:T(8,128)S(1)} %get-tuple-element.343), channel_id=1, source_target_pairs={{1,0},{3,2},{5,4},{7,6},{9,8},{11,10},{13,12},{15,14},{17,16},{19,... | collective-permute-start | bytes 49160 | tf_op jit(solution)/shard_map/while/body/eval_jaxpr/ppermute | solution.py:21
  124.5 6.5 %collective-permute-start = (f32[32,512]{1,0:T(8,128)S(1)}, f32[32,512]{1,0:T(8,128)S(1)}, u32[]{:S(2)}, u32[]{:S(2)}) collective-permute-start(f32[32,512]{1,0:T(8,128)S(1)} %get-tuple-element.358), channel_id=1, source_target_pairs={{2,0},{4,2},{6,4},{8,6},{10,8},{12,10},{14,12},{16,14},{18,16},{20... | collective-permute-start | bytes 196616 | tf_op jit(solution)/shard_map/while/body/eval_jaxpr/ppermute | solution.py:10
  131.0 3.0 %collective-permute-start.1 = (f32[32,128]{1,0:T(8,128)S(1)}, f32[32,128]{1,0:T(8,128)S(1)}, u32[]{:S(2)}, u32[]{:S(2)}) collective-permute-start(f32[32,128]{1,0:T(8,128)S(1)} %get-tuple-element.342), channel_id=1, source_target_pairs={{0,1},{2,3},{4,5},{6,7},{8,9},{10,11},{12,13},{14,15},{16,17},{18,... | collective-permute-start | bytes 49160 | tf_op jit(solution)/shard_map/while/body/eval_jaxpr/ppermute | solution.py:18
  132.6 4.5 %collective-permute-start.2 = (f32[32,128]{1,0:T(8,128)S(1)}, f32[32,128]{1,0:T(8,128)S(1)}, u32[]{:S(2)}, u32[]{:S(2)}) collective-permute-start(f32[32,128]{1,0:T(8,128)S(1)} %get-tuple-element.343), channel_id=1, source_target_pairs={{1,0},{3,2},{5,4},{7,6},{9,8},{11,10},{13,12},{15,14},{17,16},{19,... | collective-permute-start | bytes 49160 | tf_op jit(solution)/shard_map/while/body/eval_jaxpr/ppermute | solution.py:21
  139.6 6.5 %collective-permute-start = (f32[32,512]{1,0:T(8,128)S(1)}, f32[32,512]{1,0:T(8,128)S(1)}, u32[]{:S(2)}, u32[]{:S(2)}) collective-permute-start(f32[32,512]{1,0:T(8,128)S(1)} %get-tuple-element.358), channel_id=1, source_target_pairs={{2,0},{4,2},{6,4},{8,6},{10,8},{12,10},{14,12},{16,14},{18,16},{20... | collective-permute-start | bytes 196616 | tf_op jit(solution)/shard_map/while/body/eval_jaxpr/ppermute | solution.py:10
  146.1 3.0 %collective-permute-start.1 = (f32[32,128]{1,0:T(8,128)S(1)}, f32[32,128]{1,0:T(8,128)S(1)}, u32[]{:S(2)}, u32[]{:S(2)}) collective-permute-start(f32[32,128]{1,0:T(8,128)S(1)} %get-tuple-element.342), channel_id=1, source_target_pairs={{0,1},{2,3},{4,5},{6,7},{8,9},{10,11},{12,13},{14,15},{16,17},{18,... | collective-permute-start | bytes 49160 | tf_op jit(solution)/shard_map/while/body/eval_jaxpr/ppermute | solution.py:18
  147.8 4.5 %collective-permute-start.2 = (f32[32,128]{1,0:T(8,128)S(1)}, f32[32,128]{1,0:T(8,128)S(1)}, u32[]{:S(2)}, u32[]{:S(2)}) collective-permute-start(f32[32,128]{1,0:T(8,128)S(1)} %get-tuple-element.343), channel_id=1, source_target_pairs={{1,0},{3,2},{5,4},{7,6},{9,8},{11,10},{13,12},{15,14},{17,16},{19,... | collective-permute-start | bytes 49160 | tf_op jit(solution)/shard_map/while/body/eval_jaxpr/ppermute | solution.py:21
  154.8 6.5 %collective-permute-start = (f32[32,512]{1,0:T(8,128)S(1)}, f32[32,512]{1,0:T(8,128)S(1)}, u32[]{:S(2)}, u32[]{:S(2)}) collective-permute-start(f32[32,512]{1,0:T(8,128)S(1)} %get-tuple-element.358), channel_id=1, source_target_pairs={{2,0},{4,2},{6,4},{8,6},{10,8},{12,10},{14,12},{16,14},{18,16},{20... | collective-permute-start | bytes 196616 | tf_op jit(solution)/shard_map/while/body/eval_jaxpr/ppermute | solution.py:10
  161.2 3.0 %collective-permute-start.1 = (f32[32,128]{1,0:T(8,128)S(1)}, f32[32,128]{1,0:T(8,128)S(1)}, u32[]{:S(2)}, u32[]{:S(2)}) collective-permute-start(f32[32,128]{1,0:T(8,128)S(1)} %get-tuple-element.342), channel_id=1, source_target_pairs={{0,1},{2,3},{4,5},{6,7},{8,9},{10,11},{12,13},{14,15},{16,17},{18,... | collective-permute-start | bytes 49160 | tf_op jit(solution)/shard_map/while/body/eval_jaxpr/ppermute | solution.py:18
  162.9 4.5 %collective-permute-start.2 = (f32[32,128]{1,0:T(8,128)S(1)}, f32[32,128]{1,0:T(8,128)S(1)}, u32[]{:S(2)}, u32[]{:S(2)}) collective-permute-start(f32[32,128]{1,0:T(8,128)S(1)} %get-tuple-element.343), channel_id=1, source_target_pairs={{1,0},{3,2},{5,4},{7,6},{9,8},{11,10},{13,12},{15,14},{17,16},{19,... | collective-permute-start | bytes 49160 | tf_op jit(solution)/shard_map/while/body/eval_jaxpr/ppermute | solution.py:21
  169.9 6.5 %collective-permute-start = (f32[32,512]{1,0:T(8,128)S(1)}, f32[32,512]{1,0:T(8,128)S(1)}, u32[]{:S(2)}, u32[]{:S(2)}) collective-permute-start(f32[32,512]{1,0:T(8,128)S(1)} %get-tuple-element.358), channel_id=1, source_target_pairs={{2,0},{4,2},{6,4},{8,6},{10,8},{12,10},{14,12},{16,14},{18,16},{20... | collective-permute-start | bytes 196616 | tf_op jit(solution)/shard_map/while/body/eval_jaxpr/ppermute | solution.py:10
  176.4 3.0 %collective-permute-start.1 = (f32[32,128]{1,0:T(8,128)S(1)}, f32[32,128]{1,0:T(8,128)S(1)}, u32[]{:S(2)}, u32[]{:S(2)}) collective-permute-start(f32[32,128]{1,0:T(8,128)S(1)} %get-tuple-element.342), channel_id=1, source_target_pairs={{0,1},{2,3},{4,5},{6,7},{8,9},{10,11},{12,13},{14,15},{16,17},{18,... | collective-permute-start | bytes 49160 | tf_op jit(solution)/shard_map/while/body/eval_jaxpr/ppermute | solution.py:18
  178.0 4.5 %collective-permute-start.2 = (f32[32,128]{1,0:T(8,128)S(1)}, f32[32,128]{1,0:T(8,128)S(1)}, u32[]{:S(2)}, u32[]{:S(2)}) collective-permute-start(f32[32,128]{1,0:T(8,128)S(1)} %get-tuple-element.343), channel_id=1, source_target_pairs={{1,0},{3,2},{5,4},{7,6},{9,8},{11,10},{13,12},{15,14},{17,16},{19,... | collective-permute-start | bytes 49160 | tf_op jit(solution)/shard_map/while/body/eval_jaxpr/ppermute | solution.py:21
  185.0 6.5 %collective-permute-start = (f32[32,512]{1,0:T(8,128)S(1)}, f32[32,512]{1,0:T(8,128)S(1)}, u32[]{:S(2)}, u32[]{:S(2)}) collective-permute-start(f32[32,512]{1,0:T(8,128)S(1)} %get-tuple-element.358), channel_id=1, source_target_pairs={{2,0},{4,2},{6,4},{8,6},{10,8},{12,10},{14,12},{16,14},{18,16},{20... | collective-permute-start | bytes 196616 | tf_op jit(solution)/shard_map/while/body/eval_jaxpr/ppermute | solution.py:10
  191.5 3.0 %collective-permute-start.1 = (f32[32,128]{1,0:T(8,128)S(1)}, f32[32,128]{1,0:T(8,128)S(1)}, u32[]{:S(2)}, u32[]{:S(2)}) collective-permute-start(f32[32,128]{1,0:T(8,128)S(1)} %get-tuple-element.342), channel_id=1, source_target_pairs={{0,1},{2,3},{4,5},{6,7},{8,9},{10,11},{12,13},{14,15},{16,17},{18,... | collective-permute-start | bytes 49160 | tf_op jit(solution)/shard_map/while/body/eval_jaxpr/ppermute | solution.py:18
  193.2 4.5 %collective-permute-start.2 = (f32[32,128]{1,0:T(8,128)S(1)}, f32[32,128]{1,0:T(8,128)S(1)}, u32[]{:S(2)}, u32[]{:S(2)}) collective-permute-start(f32[32,128]{1,0:T(8,128)S(1)} %get-tuple-element.343), channel_id=1, source_target_pairs={{1,0},{3,2},{5,4},{7,6},{9,8},{11,10},{13,12},{15,14},{17,16},{19,... | collective-permute-start | bytes 49160 | tf_op jit(solution)/shard_map/while/body/eval_jaxpr/ppermute | solution.py:21
  200.1 6.5 %collective-permute-start = (f32[32,512]{1,0:T(8,128)S(1)}, f32[32,512]{1,0:T(8,128)S(1)}, u32[]{:S(2)}, u32[]{:S(2)}) collective-permute-start(f32[32,512]{1,0:T(8,128)S(1)} %get-tuple-element.358), channel_id=1, source_target_pairs={{2,0},{4,2},{6,4},{8,6},{10,8},{12,10},{14,12},{16,14},{18,16},{20... | collective-permute-start | bytes 196616 | tf_op jit(solution)/shard_map/while/body/eval_jaxpr/ppermute | solution.py:10
  206.6 3.0 %collective-permute-start.1 = (f32[32,128]{1,0:T(8,128)S(1)}, f32[32,128]{1,0:T(8,128)S(1)}, u32[]{:S(2)}, u32[]{:S(2)}) collective-permute-start(f32[32,128]{1,0:T(8,128)S(1)} %get-tuple-element.342), channel_id=1, source_target_pairs={{0,1},{2,3},{4,5},{6,7},{8,9},{10,11},{12,13},{14,15},{16,17},{18,... | collective-permute-start | bytes 49160 | tf_op jit(solution)/shard_map/while/body/eval_jaxpr/ppermute | solution.py:18
  208.3 4.5 %collective-permute-start.2 = (f32[32,128]{1,0:T(8,128)S(1)}, f32[32,128]{1,0:T(8,128)S(1)}, u32[]{:S(2)}, u32[]{:S(2)}) collective-permute-start(f32[32,128]{1,0:T(8,128)S(1)} %get-tuple-element.343), channel_id=1, source_target_pairs={{1,0},{3,2},{5,4},{7,6},{9,8},{11,10},{13,12},{15,14},{17,16},{19,... | collective-permute-start | bytes 49160 | tf_op jit(solution)/shard_map/while/body/eval_jaxpr/ppermute | solution.py:21
  215.3 6.5 %collective-permute-start = (f32[32,512]{1,0:T(8,128)S(1)}, f32[32,512]{1,0:T(8,128)S(1)}, u32[]{:S(2)}, u32[]{:S(2)}) collective-permute-start(f32[32,512]{1,0:T(8,128)S(1)} %get-tuple-element.358), channel_id=1, source_target_pairs={{2,0},{4,2},{6,4},{8,6},{10,8},{12,10},{14,12},{16,14},{18,16},{20... | collective-permute-start | bytes 196616 | tf_op jit(solution)/shard_map/while/body/eval_jaxpr/ppermute | solution.py:10
  221.8 3.0 %collective-permute-start.1 = (f32[32,128]{1,0:T(8,128)S(1)}, f32[32,128]{1,0:T(8,128)S(1)}, u32[]{:S(2)}, u32[]{:S(2)}) collective-permute-start(f32[32,128]{1,0:T(8,128)S(1)} %get-tuple-element.342), channel_id=1, source_target_pairs={{0,1},{2,3},{4,5},{6,7},{8,9},{10,11},{12,13},{14,15},{16,17},{18,... | collective-permute-start | bytes 49160 | tf_op jit(solution)/shard_map/while/body/eval_jaxpr/ppermute | solution.py:18
  223.4 4.5 %collective-permute-start.2 = (f32[32,128]{1,0:T(8,128)S(1)}, f32[32,128]{1,0:T(8,128)S(1)}, u32[]{:S(2)}, u32[]{:S(2)}) collective-permute-start(f32[32,128]{1,0:T(8,128)S(1)} %get-tuple-element.343), channel_id=1, source_target_pairs={{1,0},{3,2},{5,4},{7,6},{9,8},{11,10},{13,12},{15,14},{17,16},{19,... | collective-permute-start | bytes 49160 | tf_op jit(solution)/shard_map/while/body/eval_jaxpr/ppermute | solution.py:21
  230.4 6.5 %collective-permute-start = (f32[32,512]{1,0:T(8,128)S(1)}, f32[32,512]{1,0:T(8,128)S(1)}, u32[]{:S(2)}, u32[]{:S(2)}) collective-permute-start(f32[32,512]{1,0:T(8,128)S(1)} %get-tuple-element.358), channel_id=1, source_target_pairs={{2,0},{4,2},{6,4},{8,6},{10,8},{12,10},{14,12},{16,14},{18,16},{20... | collective-permute-start | bytes 196616 | tf_op jit(solution)/shard_map/while/body/eval_jaxpr/ppermute | solution.py:10
  236.9 3.0 %collective-permute-start.1 = (f32[32,128]{1,0:T(8,128)S(1)}, f32[32,128]{1,0:T(8,128)S(1)}, u32[]{:S(2)}, u32[]{:S(2)}) collective-permute-start(f32[32,128]{1,0:T(8,128)S(1)} %get-tuple-element.342), channel_id=1, source_target_pairs={{0,1},{2,3},{4,5},{6,7},{8,9},{10,11},{12,13},{14,15},{16,17},{18,... | collective-permute-start | bytes 49160 | tf_op jit(solution)/shard_map/while/body/eval_jaxpr/ppermute | solution.py:18
  238.5 4.5 %collective-permute-start.2 = (f32[32,128]{1,0:T(8,128)S(1)}, f32[32,128]{1,0:T(8,128)S(1)}, u32[]{:S(2)}, u32[]{:S(2)}) collective-permute-start(f32[32,128]{1,0:T(8,128)S(1)} %get-tuple-element.343), channel_id=1, source_target_pairs={{1,0},{3,2},{5,4},{7,6},{9,8},{11,10},{13,12},{15,14},{17,16},{19,... | collective-permute-start | bytes 49160 | tf_op jit(solution)/shard_map/while/body/eval_jaxpr/ppermute | solution.py:21
  (17 other events, 32.9 us)
where the time goes:
time: 248 us; the launch traced here: 246 us
  waiting for transfers between devices  123 us (50%)
  starting transfers between devices  79.8 us (32%)
  matrix products  38.4 us (15%)
    ppermute x16, waiting for transfers between devices, shifted(): lax.ppermute(value, axis, [(source, source + steps) for source in range(l...  72.2 us
    ppermute x16, waiting for transfers between devices, padded(): lax.ppermute(lax.slice_in_dim(block, 0, width, axis=dim), axis, backward)  50.6 us
    dot_general x16, matrix products, advance(): jnp.einsum('cbw,bwk->cbk', windows * weights[None], lag_blocks, precision...  31.9 us
    ppermute x16, starting transfers between devices, shifted(): lax.ppermute(value, axis, [(source, source + steps) for source in range(l...  31.4 us
    ppermute x16, starting transfers between devices, padded(): lax.ppermute(lax.slice_in_dim(block, block.shape[dim] - width, None, axis...  27.7 us
    ppermute x16, starting transfers between devices, padded(): lax.ppermute(lax.slice_in_dim(block, 0, width, axis=dim), axis, backward)  20.7 us
    dot_general x16, matrix products, advance(): jnp.einsum('cbk,bkj->cbj', residue, inv_blocks, precision=lax.Precision.H...  6.5 us
  transfers between devices with their start and end apart: 48, of which 32 were waited for; matrix products, arithmetic and copies ran while one was open for 0% of the time, Pallas kernels for 0%

commit v1 on v0

v1 whole, which is shorter than its diff:
```python
import functools

import jax
import jax.numpy as jnp
from jax import lax
from jax.experimental import pallas as pl
from jax.experimental.pallas import tpu as pltpu
from jax.sharding import PartitionSpec as P

BOTH = ("tm", "row")
VMEM = pl.BlockSpec(memory_space=pltpu.VMEM)
SMEM = pl.BlockSpec(memory_space=pltpu.SMEM)
PARAMS = pltpu.CompilerParams(vmem_limit_bytes=32 * 1024 * 1024)


def halves(value):
    high = value.astype(jnp.bfloat16)
    low = (value - high.astype(jnp.float32)).astype(jnp.bfloat16)
    return high, low


def dot(a, b):
    return jnp.dot(a, b, preferred_element_type=jnp.float32)


def stacked_dot(pair, cols, high, low):
    rows = pair.shape[0] // 2
    wide = dot(pair[:, cols], high)
    return wide[:rows] + wide[rows:] + dot(pair[:rows, cols], low)


def fuse_kernel(sides, place, mask, normals, inv, lag, own, rim):
    blocks, length = inv.shape[1], inv.shape[2]
    window = lag.shape[2]
    edge = (window - length) // 2
    cols = normals.shape[1]
    cuts = (0, edge, edge + length, window)
    for b in range(blocks):
        inv_high, inv_low = halves(inv[0, b])
        for part in range(3):
            lo, hi = cuts[part], cuts[part + 1]
            flag = mask[0, b, part].astype(jnp.float32)
            high, low = halves(lag[0, b, lo:hi] * flag)
            own[b * window + lo : b * window + hi] = (
                dot(high, inv_high) + dot(low, inv_high) + dot(high, inv_low)
            )
        high, low = halves(normals[0, :, b * length : (b + 1) * length])
        at = blocks * window + b * cols
        own[at : at + cols] = dot(high, inv_high) + dot(low, inv_high) + dot(high, inv_low)

    def put(slot, block, start):
        rim[slot, :window] = own[block * window : (block + 1) * window, start : start + edge]
        at = blocks * window + block * cols
        rim[slot, window:] = own[at : at + cols, start : start + edge]

    if sides == 1:
        pl.when(place[1] == 0)(lambda: put(0, blocks - 1, length - edge))
        pl.when(place[1] != 0)(lambda: put(0, 0, 0))
    else:
        put(0, blocks - 1, length - edge)
        put(1, 0, 0)


def split_kernel(far, rim, near, far_high, far_low, rim_high, rim_low, near_high, near_low):
    count = far_high.shape[0]
    far_high[...], far_low[...] = halves(far[:count])
    near_high[...], near_low[...] = halves(near[:count])
    for side in range(rim.shape[0]):
        rim_high[side], rim_low[side] = halves(rim[side, : rim_high.shape[1]])


def turn_kernel(
    mine, first, sides, blocks, window, place, own_in, halo_in, far, rim, near,
    far_high, far_low, rim_high, rim_low, near_high, near_low,
    _upper, _lower, _send, upper, lower, send, late, mid,
):
    length = far.shape[1]
    edge = (window - length) // 2
    cols, sites = lower.shape
    halo = length + edge

    @pl.when(place[0] == mine)
    def _():
        def keep(ref, start, value):
            width = value.shape[1]
            high, low = halves(value)
            ref[:cols, pl.ds(start, width)] = high
            ref[cols:, pl.ds(start, width)] = low

        def const(pack, b):
            at = blocks * window + b * cols
            return pack[at : at + cols]

        mid[...] = jnp.zeros_like(mid)
        if not first:
            late[...] = jnp.zeros_like(late)
            keep(late, halo, own_in[...])
        right = jnp.int32(1) - jnp.minimum(place[1], 1)
        for side in range(sides):
            on_right = right if sides == 1 else side
            if not first:
                keep(late, pl.multiple_of(on_right * (halo + sites), 128), halo_in[side])
            value = rim[side, window:]
            if not first:
                start = pl.multiple_of(on_right * (2 * halo + sites - window), 128)
                value -= stacked_dot(late, pl.ds(start, window), rim_high[side], rim_low[side])
            keep(mid, pl.multiple_of(on_right * (edge + sites), 128), value)
        for b in range(blocks):
            value = const(far, b)
            if not first:
                at = halo - edge + b * length
                value -= stacked_dot(
                    late, pl.ds(at, window),
                    far_high[b * window : (b + 1) * window], far_low[b * window : (b + 1) * window],
                )
            keep(mid, edge + b * length, value)
            upper[:, b * length : (b + 1) * length] = value
        for b in range(blocks):
            lower[:, b * length : (b + 1) * length] = const(near, b) - stacked_dot(
                mid, pl.ds(b * length, window),
                near_high[b * window : (b + 1) * window], near_low[b * window : (b + 1) * window],
            )
        if sides == 1:
            start = pl.multiple_of(right * (sites - halo), 128)
            send[0] = lower[:, pl.ds(start, halo)]
        else:
            send[0] = lower[:, sites - halo :]
            send[1] = lower[:, :halo]


def local(normals, inv_diag, lag_coupling, fill_mask):
    times, rows = lax.axis_size("tm"), lax.axis_size("row")
    device, row = lax.axis_index("tm"), lax.axis_index("row")
    cols, sites = normals.shape[1:]
    blocks, length = inv_diag.shape[1:3]
    window = lag_coupling.shape[2]
    edge = (window - length) // 2
    halo = length + edge
    sides = 1 if rows == 2 else 2
    pairs = times // 2
    f32, bf16 = jnp.float32, jnp.bfloat16
    shape = jax.ShapeDtypeStruct
    place = jnp.stack([jnp.where(device % 2 == 0, device // 2, -1), row]).astype(jnp.int32)

    def link(source, target):
        return [(s * rows + r, t * rows + r) for s, t in zip(source, target) for r in range(rows)]

    def cross(value, source, target):
        if sides == 1:
            perm = [(s * rows + r, t * rows + 1 - r) for s, t in zip(source, target) for r in range(2)]
            return lax.ppermute(value, BOTH, perm)
        moved = []
        for side, step in enumerate((1, -1)):
            perm = [
                (s * rows + r, t * rows + r + step)
                for s, t in zip(source, target)
                for r in range(rows)
                if 0 <= r + step < rows
            ]
            moved.append(lax.ppermute(value[side : side + 1], BOTH, perm))
        return jnp.concatenate(moved)

    height = blocks * (window + cols)
    near, edges = pl.pallas_call(
        functools.partial(fuse_kernel, sides),
        out_shape=(shape((height, length), f32), shape((sides, window + cols, edge), f32)),
        in_specs=[SMEM, SMEM, VMEM, VMEM, VMEM],
        out_specs=(VMEM, VMEM),
        compiler_params=PARAMS,
    )(place, fill_mask, normals, inv_diag, lag_coupling)
    odd, even = range(1, times, 2), range(0, times, 2)
    far = lax.ppermute(near, BOTH, link(odd, even))
    rim = cross(edges, odd, even)
    tall = blocks * window
    parts = pl.pallas_call(
        split_kernel,
        out_shape=(
            shape((tall, length), bf16), shape((tall, length), bf16),
            shape((sides, window, edge), bf16), shape((sides, window, edge), bf16),
            shape((tall, length), bf16), shape((tall, length), bf16),
        ),
        in_specs=[VMEM] * 3,
        out_specs=(VMEM,) * 6,
        compiler_params=PARAMS,
    )(far, rim, near)

    state = (
        jnp.zeros((cols, sites), f32), jnp.zeros((cols, sites), f32), jnp.zeros((sides, cols, halo), f32)
    )
    own_in, halo_in = state[0], state[2]
    for step in range(pairs):
        mine = pairs - 1 - step
        state = pl.pallas_call(
            functools.partial(turn_kernel, mine, step == 0, sides, blocks, window),
            out_shape=tuple(shape(s.shape, f32) for s in state),
            in_specs=[SMEM] + [VMEM] * 14,
            out_specs=(VMEM,) * 3,
            scratch_shapes=[
                pltpu.VMEM((2 * cols, sites + 2 * halo), bf16),
                pltpu.VMEM((2 * cols, sites + 2 * edge), bf16),
            ],
            input_output_aliases={12: 0, 13: 1, 14: 2},
            compiler_params=PARAMS,
        )(place, own_in, halo_in, far, rim, near, *parts, *state)
        if mine:
            source, target = [2 * mine], [2 * mine - 2]
            own_in = lax.ppermute(state[1], BOTH, link(source, target))
            halo_in = cross(state[2], source, target)
    returned = lax.ppermute(state[0], BOTH, link(even, odd))
    return jnp.where(device % 2 == 0, state[1], returned)[None]


def solution(mesh):
    placed = (
        P("tm", None, "row"),
        P("tm", "row", None, None),
        P("tm", "row", None, None),
        P("tm", "row", None),
    )
    return jax.shard_map(
        local, mesh=mesh, in_specs=placed, out_specs=P("tm", None, "row"), check_vma=False
    )
```

time: 248 us -> 76.1 us (0.31)
  the two profiles are of different devices: /device:TPU:13 before, /device:TPU:0 now
where the time goes in v1:
time: 76.1 us; the launch traced here: 75.7 us
  waiting for transfers between devices  49.7 us (65%)
  starting transfers between devices  14.4 us (19%)
  Pallas kernels  6.68 us (9%)
  local copies, waits for them, and re-layouts  3.81 us (5%)
    ppermute x8, waiting for transfers between devices, cross(): return lax.ppermute(value, BOTH, perm)  48.8 us
    ppermute x8, starting transfers between devices, cross(): return lax.ppermute(value, BOTH, perm)  6.57 us
    ppermute x7, starting transfers between devices, local(): own_in = lax.ppermute(state[1], BOTH, link(source, target))  5.28 us
    pallas_call x8, Pallas kernels, local(): pl.pallas_call(functools.partial(turn_kernel, mine, step == 0, sides, blo...  5.07 us
    unnamed x8, local copies, waits for them, and re-layouts  3.78 us
  transfers between devices with their start and end apart: 17, of which 3 were waited for; matrix products, arithmetic and copies ran while one was open for 0% of the time, Pallas kernels for 0%

profile of v1, /device:TPU:0, one launch (start us, length us, event | category | flops | bytes accessed | tf_op | source)
XLA Modules:
  0.0 75.7 jit_solution(14865662780201050415)
XLA Ops:
  0.0 0.1 pad_add_fusion.place
  0.1 1.2 %copy-done = f32[1,2,512,256]{3,2,1,0:T(8,128)S(1)} copy-done((f32[1,2,512,256]{3,2,1,0:T(8,128)S(1)}, f32[1,2,512,256]{3,2,1,0:T(8,128)}, u32[]{:S(2)}) %copy-start) | copy-done | bytes 1048600
  1.3 1.0 %copy-done.1 = f32[1,2,256,256]{3,2,1,0:T(8,128)S(1)} copy-done((f32[1,2,256,256]{3,2,1,0:T(8,128)S(1)}, f32[1,2,256,256]{3,2,1,0:T(8,128)}, u32[]{:S(2)}) %copy-start.1) | copy-done | bytes 524312
  2.3 0.8 %copy-done.2 = f32[1,32,512]{2,1,0:T(8,128)S(1)} copy-done((f32[1,32,512]{2,1,0:T(8,128)S(1)}, f32[1,32,512]{2,1,0:T(8,128)}, u32[]{:S(2)}) %copy-start.2) | copy-done | bytes 65560
  3.2 0.7 copy-done.3
  3.9 1.3 %shard_map.46 = (f32[1088,256]{1,0:T(8,128)S(1)}, f32[1,544,128]{2,1,0:T(8,128)S(1)}) custom-call(s32[2]{0:T(128)S(1)} %pad_add_fusion.place, s32[1,2,3]{2,1,0:T(2,128)S(1)} %copy-done.3, f32[1,32,512]{2,1,0:T(8,128)S(1)} %copy-done.2, f32[1,2,256,256]{3,2,1,0:T(8,128)S(1)} %copy-done.1, f32[1,2,512,256]{3,2,1,0:T(8,128)S(1)} %copy-done), custom_call_target="tpu_custom_call" | custom-call | tf_op jit(solution)/shard_map/pallas_call | solution.py:164
  5.1 1.3 %collective-permute-start = (f32[1088,256]{1,0:T(8,128)S(1)}, f32[1088,256]{1,0:T(8,128)S(1)}, u32[]{:S(2)}, u32[]{:S(2)}) collective-permute-start(f32[1088,256]{1,0:T(8,128)S(1)} %get-tuple-element.36.near), channel_id=1, source_target_pairs={{2,0},{3,1},{6,4},{7,5},{10,8},{11,9},{14,12},{15,13},{18,16},{19,... | collective-permute-start | bytes 3342344 | tf_op jit(solution)/shard_map/ppermute | solution.py:172
  6.4 1.3 %collective-permute-start.1 = (f32[1,544,128]{2,1,0:T(8,128)S(1)}, f32[1,544,128]{2,1,0:T(8,128)S(1)}, u32[]{:S(2)}, u32[]{:S(2)}) collective-permute-start(f32[1,544,128]{2,1,0:T(8,128)S(1)} %get-tuple-element.37), channel_id=1, source_target_pairs={{2,1},{3,0},{6,5},{7,4},{10,9},{11,8},{14,13},{15,12},{18,17},{19,... | collective-permute-start | bytes 835592 | tf_op jit(solution)/shard_map/ppermute | solution.py:151
  7.7 7.9 %collective-permute-done.1.rim = f32[1,544,128]{2,1,0:T(8,128)S(1)} collective-permute-done((f32[1,544,128]{2,1,0:T(8,128)S(1)}, f32[1,544,128]{2,1,0:T(8,128)S(1)}, u32[]{:S(2)}, u32[]{:S(2)}) %collective-permute-start.1) | collective-permute-done | bytes 278560 | tf_op jit(solution)/shard_map/ppermute | solution.py:151
  15.7 0.0 collective-permute-done.far
  15.7 0.3 shard_map.47
  16.1 0.6 shard_map.48
  16.7 0.7 collective-permute-start.2
  17.3 0.7 collective-permute-start.3
  18.0 0.0 collective-permute-done.3.halo_in
  18.0 0.0 collective-permute-done.2.own_in
  18.0 0.6 shard_map.49
  18.6 0.7 collective-permute-start.4
  19.3 0.7 collective-permute-start.5
  19.9 0.0 collective-permute-done.5.halo_in
  20.0 0.0 collective-permute-done.4.own_in
  20.0 0.6 shard_map.50
  20.5 0.7 collective-permute-start.6
  21.2 0.7 collective-permute-start.7
  21.9 0.0 collective-permute-done.7.halo_in
  21.9 0.0 collective-permute-done.6.own_in
  21.9 0.6 shard_map.51
  22.5 0.7 collective-permute-start.8
  23.1 0.7 collective-permute-start.9
  23.8 0.0 collective-permute-done.9.halo_in
  23.8 0.0 collective-permute-done.8.own_in
  23.8 0.6 shard_map.52
  24.4 0.7 collective-permute-start.10
  25.1 0.7 collective-permute-start.11
  25.7 0.0 collective-permute-done.10.own_in
  25.8 0.6 shard_map.53
  26.3 0.7 collective-permute-start.12
  27.0 0.7 collective-permute-start.13
  27.7 0.0 collective-permute-done.13.halo_in
  27.7 0.6 shard_map.54
  28.3 1.3 %collective-permute-start.14 = (f32[32,512]{1,0:T(8,128)S(1)}, f32[32,512]{1,0:T(8,128)S(1)}, u32[]{:S(2)}, u32[]{:S(2)}) collective-permute-start(f32[32,512]{1,0:T(8,128)S(1)} %get-tuple-element.62._lower), channel_id=1, source_target_pairs={{4,0},{5,1}} | collective-permute-start | bytes 196616 | tf_op jit(solution)/shard_map/ppermute | solution.py:207
  29.6 1.3 %collective-permute-start.15 = (f32[1,32,384]{2,1,0:T(8,128)S(1)}, f32[1,32,384]{2,1,0:T(8,128)S(1)}, u32[]{:S(2)}, u32[]{:S(2)}) collective-permute-start(f32[1,32,384]{2,1,0:T(8,128)S(1)} %get-tuple-element.63._send), channel_id=1, source_target_pairs={{4,1},{5,0}} | collective-permute-start | bytes 147464 | tf_op jit(solution)/shard_map/ppermute | solution.py:151
  30.9 40.8 %collective-permute-done.15.halo_in = f32[1,32,384]{2,1,0:T(8,128)S(1)} collective-permute-done((f32[1,32,384]{2,1,0:T(8,128)S(1)}, f32[1,32,384]{2,1,0:T(8,128)S(1)}, u32[]{:S(2)}, u32[]{:S(2)}) %collective-permute-start.15) | collective-permute-done | bytes 49184 | tf_op jit(solution)/shard_map/ppermute | solution.py:151
  71.7 0.0 collective-permute-done.14.own_in
  71.7 1.2 %shard_map.55 = (f32[32,512]{1,0:T(8,128)S(1)}, f32[32,512]{1,0:T(8,128)S(1)}, f32[1,32,384]{2,1,0:T(8,128)S(1)}) custom-call(s32[2]{0:T(128)S(1)} %pad_add_fusion.place, f32[32,512]{1,0:T(8,128)S(1)} %collective-permute-done.14.own_in, ...), custom_call_target="tpu_custom_call", output_to_operand_aliasing={{0}: (12, {}), {1}: (13, {}), {2}: (14, {})} | custom-call | tf_op jit(solution)/shard_map/pallas_call | solution.py:193
  72.8 1.3 %collective-permute-start.16 = (f32[32,512]{1,0:T(8,128)S(1)}, f32[32,512]{1,0:T(8,128)S(1)}, u32[]{:S(2)}, u32[]{:S(2)}) collective-permute-start(f32[32,512]{1,0:T(8,128)S(1)} %get-tuple-element.66), channel_id=1, source_target_pairs={{0,2},{1,3},{4,6},{5,7},{8,10},{9,11},{12,14},{13,15},{16,18},{17,... | collective-permute-start | bytes 196616 | tf_op jit(solution)/shard_map/ppermute | solution.py:209
  74.1 0.9 %collective-permute-done.16 = f32[32,512]{1,0:T(8,128)S(1)} collective-permute-done((f32[32,512]{1,0:T(8,128)S(1)}, f32[32,512]{1,0:T(8,128)S(1)}, u32[]{:S(2)}, u32[]{:S(2)}) %collective-permute-start.16) | collective-permute-done | bytes 65568 | tf_op jit(solution)/shard_map/ppermute | solution.py:209
  75.0 0.6 select_bitcast_fusion
  (11 shorter events, 0.0 us)
Async XLA Ops:
  0.1 1.2 %copy-start = (f32[1,2,512,256]{3,2,1,0:T(8,128)S(1)}, f32[1,2,512,256]{3,2,1,0:T(8,128)}, u32[]{:S(2)}) copy-start(f32[1,2,512,256]{3,2,1,0:T(8,128)} %lag.1) | copy-start | bytes 3145732
  1.3 1.0 %copy-start.1 = (f32[1,2,256,256]{3,2,1,0:T(8,128)S(1)}, f32[1,2,256,256]{3,2,1,0:T(8,128)}, u32[]{:S(2)}) copy-start(f32[1,2,256,256]{3,2,1,0:T(8,128)} %inv.1) | copy-start | bytes 1572868
  2.3 0.8 %copy-start.2 = (f32[1,32,512]{2,1,0:T(8,128)S(1)}, f32[1,32,512]{2,1,0:T(8,128)}, u32[]{:S(2)}) copy-start(f32[1,32,512]{2,1,0:T(8,128)} %normals.1) | copy-start | bytes 196612
  3.2 0.7 copy-start.3
  5.1 10.5 %collective-permute-start = (f32[1088,256]{1,0:T(8,128)S(1)}, f32[1088,256]{1,0:T(8,128)S(1)}, u32[]{:S(2)}, u32[]{:S(2)}) collective-permute-start(f32[1088,256]{1,0:T(8,128)S(1)} %get-tuple-element.36.near), channel_id=1, source_target_pairs={{2,0},{3,1},{6,4},{7,5},{10,8},{11,9},{14,12},{15,13},{18,16},{19,... | collective-permute-start | bytes 3342344 | tf_op jit(solution)/shard_map/ppermute | solution.py:172
  6.4 9.2 %collective-permute-start.1 = (f32[1,544,128]{2,1,0:T(8,128)S(1)}, f32[1,544,128]{2,1,0:T(8,128)S(1)}, u32[]{:S(2)}, u32[]{:S(2)}) collective-permute-start(f32[1,544,128]{2,1,0:T(8,128)S(1)} %get-tuple-element.37), channel_id=1, source_target_pairs={{2,1},{3,0},{6,5},{7,4},{10,9},{11,8},{14,13},{15,12},{18,17},{19,... | collective-permute-start | bytes 835592 | tf_op jit(solution)/shard_map/ppermute | solution.py:151
  16.7 1.4 %collective-permute-start.2 = (f32[32,512]{1,0:T(8,128)S(1)}, f32[32,512]{1,0:T(8,128)S(1)}, u32[]{:S(2)}, u32[]{:S(2)}) collective-permute-start(f32[32,512]{1,0:T(8,128)S(1)} %get-tuple-element.44._lower), channel_id=1, source_target_pairs={{28,24},{29,25}} | collective-permute-start | bytes 196616 | tf_op jit(solution)/shard_map/ppermute | solution.py:207
  17.3 0.7 collective-permute-start.3
  18.6 1.4 %collective-permute-start.4 = (f32[32,512]{1,0:T(8,128)S(1)}, f32[32,512]{1,0:T(8,128)S(1)}, u32[]{:S(2)}, u32[]{:S(2)}) collective-permute-start(f32[32,512]{1,0:T(8,128)S(1)} %get-tuple-element.47._lower), channel_id=1, source_target_pairs={{24,20},{25,21}} | collective-permute-start | bytes 196616 | tf_op jit(solution)/shard_map/ppermute | solution.py:207
  19.3 0.7 collective-permute-start.5
  20.5 1.4 %collective-permute-start.6 = (f32[32,512]{1,0:T(8,128)S(1)}, f32[32,512]{1,0:T(8,128)S(1)}, u32[]{:S(2)}, u32[]{:S(2)}) collective-permute-start(f32[32,512]{1,0:T(8,128)S(1)} %get-tuple-element.50._lower), channel_id=1, source_target_pairs={{20,16},{21,17}} | collective-permute-start | bytes 196616 | tf_op jit(solution)/shard_map/ppermute | solution.py:207
  21.2 0.7 collective-permute-start.7
  22.5 1.4 %collective-permute-start.8 = (f32[32,512]{1,0:T(8,128)S(1)}, f32[32,512]{1,0:T(8,128)S(1)}, u32[]{:S(2)}, u32[]{:S(2)}) collective-permute-start(f32[32,512]{1,0:T(8,128)S(1)} %get-tuple-element.53._lower), channel_id=1, source_target_pairs={{16,12},{17,13}} | collective-permute-start | bytes 196616 | tf_op jit(solution)/shard_map/ppermute | solution.py:207
  23.1 0.7 collective-permute-start.9
  24.4 1.4 %collective-permute-start.10 = (f32[32,512]{1,0:T(8,128)S(1)}, f32[32,512]{1,0:T(8,128)S(1)}, u32[]{:S(2)}, u32[]{:S(2)}) collective-permute-start(f32[32,512]{1,0:T(8,128)S(1)} %get-tuple-element.56._lower), channel_id=1, source_target_pairs={{12,8},{13,9}} | collective-permute-start | bytes 196616 | tf_op jit(solution)/shard_map/ppermute | solution.py:207
  25.1 0.7 collective-permute-start.11
  26.3 1.4 %collective-permute-start.12 = (f32[32,512]{1,0:T(8,128)S(1)}, f32[32,512]{1,0:T(8,128)S(1)}, u32[]{:S(2)}, u32[]{:S(2)}) collective-permute-start(f32[32,512]{1,0:T(8,128)S(1)} %get-tuple-element.59._lower), channel_id=1, source_target_pairs={{8,4},{9,5}} | collective-permute-start | bytes 196616 | tf_op jit(solution)/shard_map/ppermute | solution.py:207
  27.0 0.7 collective-permute-start.13
  28.3 43.4 %collective-permute-start.14 = (f32[32,512]{1,0:T(8,128)S(1)}, f32[32,512]{1,0:T(8,128)S(1)}, u32[]{:S(2)}, u32[]{:S(2)}) collective-permute-start(f32[32,512]{1,0:T(8,128)S(1)} %get-tuple-element.62._lower), channel_id=1, source_target_pairs={{4,0},{5,1}} | collective-permute-start | bytes 196616 | tf_op jit(solution)/shard_map/ppermute | solution.py:207
  29.6 42.1 %collective-permute-start.15 = (f32[1,32,384]{2,1,0:T(8,128)S(1)}, f32[1,32,384]{2,1,0:T(8,128)S(1)}, u32[]{:S(2)}, u32[]{:S(2)}) collective-permute-start(f32[1,32,384]{2,1,0:T(8,128)S(1)} %get-tuple-element.63._send), channel_id=1, source_target_pairs={{4,1},{5,0}} | collective-permute-start | bytes 147464 | tf_op jit(solution)/shard_map/ppermute | solution.py:151
  72.8 2.2 %collective-permute-start.16 = (f32[32,512]{1,0:T(8,128)S(1)}, f32[32,512]{1,0:T(8,128)S(1)}, u32[]{:S(2)}, u32[]{:S(2)}) collective-permute-start(f32[32,512]{1,0:T(8,128)S(1)} %get-tuple-element.66), channel_id=1, source_target_pairs={{0,2},{1,3},{4,6},{5,7},{8,10},{9,11},{12,14},{13,15},{16,18},{17,... | collective-permute-start | bytes 196616 | tf_op jit(solution)/shard_map/ppermute | solution.py:209

commit v2 on v1

v2 whole, which is shorter than its diff:
```python
import functools

import jax
import jax.numpy as jnp
from jax import lax
from jax.experimental import pallas as pl
from jax.experimental.pallas import tpu as pltpu
from jax.sharding import PartitionSpec as P

BOTH = ("tm", "row")
VMEM = pl.BlockSpec(memory_space=pltpu.VMEM)
HBM = pl.BlockSpec(memory_space=pltpu.HBM)
PARAMS = pltpu.CompilerParams(vmem_limit_bytes=32 * 1024 * 1024)


def halves(value):
    high = value.astype(jnp.bfloat16)
    low = (value - high.astype(jnp.float32)).astype(jnp.bfloat16)
    return high, low


def dot(a, b):
    return jnp.dot(a, b, preferred_element_type=jnp.float32)


def stacked_dot(pair, cols, high, low):
    rows = pair.shape[0] // 2
    wide = dot(pair[:, cols], high)
    return wide[:rows] + wide[rows:] + dot(pair[:rows, cols], low)


def triple(high, low, inv_high, inv_low):
    return dot(high, inv_high) + dot(low, inv_high) + dot(high, inv_low)


def put_rim(sides, rim, columns):
    if sides == 1:
        row = lax.axis_index("row")

        @pl.when(row == 0)
        def _():
            rim[0] = columns(True)

        @pl.when(row != 0)
        def _():
            rim[0] = columns(False)
    else:
        rim[0] = columns(True)
        rim[1] = columns(False)


def const_kernel(
    sides, edge, mask, normals, inv, lag, const, rim, inv_high, inv_low, lag_out, mask_out, normals_in, inv_in, sems
):
    blocks, length = inv.shape[1], inv.shape[2]
    sites = normals.shape[2]
    moves = [pltpu.make_async_copy(normals.at[0], normals_in, sems.at[0])]
    for b in range(blocks):
        moves.append(pltpu.make_async_copy(inv.at[0, b], inv_in.at[b], sems.at[1 + b]))
    for b in range(blocks):
        moves.append(pltpu.make_async_copy(lag.at[0, b], lag_out.at[b], sems.at[1 + blocks + b]))
    moves.append(pltpu.make_async_copy(mask.at[0], mask_out, sems.at[1 + 2 * blocks]))
    for move in moves:
        move.start()
    moves[0].wait()
    for b in range(blocks):
        at = slice(b * length, (b + 1) * length)
        high, low = halves(normals_in[:, at])
        moves[1 + b].wait()
        inv_high[b], inv_low[b] = halves(inv_in[b])
        const[:, at] = triple(high, low, inv_high[b], inv_low[b])
    put_rim(sides, rim, lambda last: const[:, sites - edge :] if last else const[:, :edge])
    for move in moves[1 + blocks :]:
        move.wait()


def fuse_kernel(mask, const, inv_high, inv_low, lag, own, near_high, near_low):
    blocks, window, length = lag.shape
    edge = (window - length) // 2
    cols = const.shape[0]
    cuts = (0, edge, edge + length, window)
    flags = mask[...].astype(jnp.float32)
    for b in range(blocks):
        at = blocks * window + b * cols
        own[at : at + cols] = const[:, b * length : (b + 1) * length]
        for part in range(3):
            lo, hi = cuts[part], cuts[part + 1]
            rows = slice(b * window + lo, b * window + hi)
            high, low = halves(lag[b, lo:hi] * flags[b : b + 1, part : part + 1])
            value = triple(high, low, inv_high[b], inv_low[b])
            own[rows] = value
            near_high[rows], near_low[rows] = halves(value)


def edge_kernel(sides, blocks, cols, _own, _first_far, _first_rim, own, rim):
    length, edge = own.shape[1], rim.shape[2]
    window = length + 2 * edge

    def columns(last):
        b = blocks - 1 if last else 0
        cut = slice(length - edge, length) if last else slice(0, edge)
        at = blocks * window + b * cols
        return jnp.concatenate([own[b * window : (b + 1) * window, cut], own[at : at + cols, cut]])

    put_rim(sides, rim, columns)


def split_kernel(far, rim, far_high, far_low, rim_high, rim_low):
    far_high[...], far_low[...] = halves(far[: far_high.shape[0]])
    for side in range(rim.shape[0]):
        rim_high[side], rim_low[side] = halves(rim[side, : rim_high.shape[1]])


def turn_kernel(mine, sides, far_rows, rim_rows, next_in, own_in, far, rim, const, near_high, near_low, *rest):
    parts, (_upper, _lower, upper, lower, late, mid) = rest[:-6], rest[-6:]
    first = not parts
    cols, sites = lower.shape
    length = near_high.shape[1]
    blocks = sites // length
    window = near_high.shape[0] // blocks
    edge = (window - length) // 2
    halo = length + edge

    @pl.when(lax.axis_index("tm") == 2 * mine)
    def _():
        def keep(ref, start, value):
            width = value.shape[1]
            high, low = halves(value)
            ref[:cols, pl.ds(start, width)] = high
            ref[cols:, pl.ds(start, width)] = low

        mid[...] = jnp.zeros_like(mid)
        if not first:
            far_high, far_low, rim_high, rim_low = parts
            late[...] = jnp.zeros_like(late)
            keep(late, halo, own_in[...])
        right = jnp.int32(1) - lax.axis_index("row").astype(jnp.int32)
        for side in range(sides):
            on_right = right if sides == 1 else side
            if not first:
                start = pl.multiple_of((1 - on_right) * (sites - halo), 128)
                value = next_in[side, :, pl.ds(start, halo)]
                keep(late, pl.multiple_of(on_right * (halo + sites), 128), value)
            value = rim[side, rim_rows : rim_rows + cols]
            if not first:
                start = pl.multiple_of(on_right * (2 * halo + sites - window), 128)
                value -= stacked_dot(late, pl.ds(start, window), rim_high[side], rim_low[side])
            keep(mid, pl.multiple_of(on_right * (edge + sites), 128), value)
        for b in range(blocks):
            if first:
                value = far[:, b * length : (b + 1) * length]
            else:
                value = far[far_rows + b * cols : far_rows + (b + 1) * cols]
                at = halo - edge + b * length
                value -= stacked_dot(
                    late, pl.ds(at, window),
                    far_high[b * window : (b + 1) * window], far_low[b * window : (b + 1) * window],
                )
            keep(mid, edge + b * length, value)
            upper[:, b * length : (b + 1) * length] = value
        for b in range(blocks):
            lower[:, b * length : (b + 1) * length] = const[:, b * length : (b + 1) * length] - stacked_dot(
                mid, pl.ds(b * length, window),
                near_high[b * window : (b + 1) * window], near_low[b * window : (b + 1) * window],
            )


def local(normals, inv_diag, lag_coupling, fill_mask):
    times, rows = lax.axis_size("tm"), lax.axis_size("row")
    device = lax.axis_index("tm")
    cols, sites = normals.shape[1:]
    blocks, length = inv_diag.shape[1:3]
    window = lag_coupling.shape[2]
    edge = (window - length) // 2
    halo = length + edge
    sides = 1 if rows == 2 else 2
    pairs = times // 2
    f32, bf16 = jnp.float32, jnp.bfloat16
    shape = jax.ShapeDtypeStruct

    def link(source, target):
        return [(s * rows + r, t * rows + r) for s, t in zip(source, target) for r in range(rows)]

    def cross(value, source, target):
        if sides == 1:
            perm = [(s * rows + r, t * rows + 1 - r) for s, t in zip(source, target) for r in range(2)]
            return lax.ppermute(value, BOTH, perm)
        moved = []
        for side, step in enumerate((1, -1)):
            perm = [
                (s * rows + r, t * rows + r + step)
                for s, t in zip(source, target)
                for r in range(rows)
                if 0 <= r + step < rows
            ]
            moved.append(lax.ppermute(value[side : side + 1] if value.shape[0] > 1 else value, BOTH, perm))
        return jnp.concatenate(moved)

    tall = blocks * window
    const, const_rim, inv_high, inv_low, lag, mask = pl.pallas_call(
        functools.partial(const_kernel, sides, edge),
        out_shape=(
            shape((cols, sites), f32), shape((sides, cols, edge), f32),
            shape((blocks, length, length), bf16), shape((blocks, length, length), bf16),
            shape(lag_coupling.shape[1:], f32), shape(fill_mask.shape[1:], fill_mask.dtype),
        ),
        in_specs=[HBM] * 4,
        out_specs=(VMEM,) * 6,
        scratch_shapes=[
            pltpu.VMEM(normals.shape[1:], f32),
            pltpu.VMEM(inv_diag.shape[1:], f32),
            pltpu.SemaphoreType.DMA((2 + 2 * blocks,)),
        ],
        compiler_params=PARAMS,
    )(*[pltpu.with_memory_space_constraint(a, pltpu.HBM) for a in (fill_mask, normals, inv_diag, lag_coupling)])
    odd, even = range(1, times, 2), range(0, times, 2)
    first_rim = cross(const_rim, odd[-1:], even[-1:])
    first_far = lax.ppermute(const, BOTH, link(odd[-1:], even[-1:]))
    near, near_high, near_low = pl.pallas_call(
        fuse_kernel,
        out_shape=(
            shape((tall + blocks * cols, length), f32), shape((tall, length), bf16), shape((tall, length), bf16),
        ),
        in_specs=[VMEM] * 5,
        out_specs=(VMEM,) * 3,
        compiler_params=PARAMS,
        cost_estimate=pl.CostEstimate(
            flops=6 * (tall + cols * blocks) * length * length, bytes_accessed=16 * tall * length, transcendentals=0
        ),
    )(mask, const, inv_high, inv_low, lag)
    near, edges = pl.pallas_call(
        functools.partial(edge_kernel, sides, blocks, cols),
        out_shape=(shape(near.shape, f32), shape((sides, window + cols, edge), f32)),
        in_specs=[VMEM] * 3,
        out_specs=(VMEM,) * 2,
        input_output_aliases={0: 0},
        compiler_params=PARAMS,
    )(near, first_far, first_rim)
    rim = cross(edges, odd[:-1], even[:-1])
    far = lax.ppermute(near, BOTH, link(odd[:-1], even[:-1]))
    parts = pl.pallas_call(
        split_kernel,
        out_shape=(
            shape((tall, length), bf16), shape((tall, length), bf16),
            shape((sides, window, edge), bf16), shape((sides, window, edge), bf16),
        ),
        in_specs=[VMEM] * 2,
        out_specs=(VMEM,) * 4,
        compiler_params=PARAMS,
    )(far, rim)

    state = (jnp.zeros((cols, sites), f32), jnp.zeros((cols, sites), f32))
    own_in, next_in = state[0], jnp.zeros((sides, cols, sites), f32)
    for step in range(pairs):
        mine = pairs - 1 - step
        if step == 0:
            given = (next_in, own_in, first_far, first_rim, const, near_high, near_low)
            starts = (None, 0)
        else:
            given = (next_in, own_in, far, rim, const, near_high, near_low, *parts)
            starts = (tall, window)
        state = pl.pallas_call(
            functools.partial(turn_kernel, mine, sides, *starts),
            out_shape=tuple(shape(s.shape, f32) for s in state),
            in_specs=[VMEM] * (len(given) + len(state)),
            out_specs=(VMEM,) * 2,
            scratch_shapes=[
                pltpu.VMEM((2 * cols, sites + 2 * halo), bf16),
                pltpu.VMEM((2 * cols, sites + 2 * edge), bf16),
            ],
            input_output_aliases={len(given) + i: i for i in range(2)},
            compiler_params=PARAMS,
        )(*given, *state)
        if mine:
            source, target = [2 * mine], [2 * mine - 2]
            next_in = cross(state[1][None], source, target)
            own_in = lax.ppermute(state[1], BOTH, link(source, target))
    returned = lax.ppermute(state[0], BOTH, link(even, odd))
    return jnp.where(device % 2 == 0, state[1], returned)[None]


def solution(mesh):
    placed = (
        P("tm", None, "row"),
        P("tm", "row", None, None),
        P("tm", "row", None, None),
        P("tm", "row", None),
    )
    return jax.shard_map(
        local, mesh=mesh, in_specs=placed, out_specs=P("tm", None, "row"), check_vma=False
    )
```

time: 76.1 us -> 63.2 us (0.83)
  waiting for transfers between devices: 49.7 us -> 42.9 us
  local copies, waits for them, and re-layouts: 3.81 us -> 0.03 us
  Pallas kernels: 6.68 us -> 3.16 us
  starting transfers between devices: 14.4 us -> 15.8 us
    ppermute x8 -> x9, waiting for transfers between devices: 48.8 us -> 41.3 us  [cross(): return lax.ppermute(value, BOTH, perm)]
    unnamed x8 -> x0, local copies, waits for them, and re-layouts: 3.78 us -> none
    pallas_call x9 -> x11, Pallas kernels: 6.34 us -> 2.98 us  [the longest x1 1.52 us: local(): pl.pallas_call(functools.partial(const_kernel, sides, edge), out_shape=(s...]
    ppermute x8 -> x9, starting transfers between devices: 6.57 us -> 7.23 us  [cross(): return lax.ppermute(value, BOTH, perm)]
    ppermute x1 -> x2, starting transfers between devices: 1.29 us -> 1.96 us  [the longest x1 1.29 us: local(): far = lax.ppermute(near, BOTH, link(odd[:-1], even[:-1]))]
  transfers between devices with their start and end apart: 17 -> 19, of which waited for: 3 -> 4; matrix products, arithmetic and copies ran while one was open for 0% -> 0% of each run, Pallas kernels for 0% -> 1%
where the time goes in v2:
time: 63.2 us; the launch traced here: 62.8 us
  waiting for transfers between devices  42.9 us (68%)
  starting transfers between devices  15.8 us (25%)
  Pallas kernels  3.16 us (5%)
  other arithmetic  0.64 us (1%)
    ppermute x9, waiting for transfers between devices, cross(): return lax.ppermute(value, BOTH, perm)  41.3 us
    ppermute x9, starting transfers between devices, cross(): return lax.ppermute(value, BOTH, perm)  7.23 us
    ppermute x7, starting transfers between devices, local(): own_in = lax.ppermute(state[1], BOTH, link(source, target))  5.28 us
    pallas_call x1, Pallas kernels, local(): pl.pallas_call(functools.partial(const_kernel, sides, edge), out_shape=(s...  1.52 us
    ppermute x1, starting transfers between devices, local(): far = lax.ppermute(near, BOTH, link(odd[:-1], even[:-1]))  1.29 us
    ppermute x1, starting transfers between devices, local(): returned = lax.ppermute(state[0], BOTH, link(even, odd))  1.29 us
  transfers between devices with their start and end apart: 19, of which 4 were waited for; matrix products, arithmetic and copies ran while one was open for 0% of the time, Pallas kernels for 1%

profile of v2, /device:TPU:0, one launch (start us, length us, event | category | flops | bytes accessed | tf_op | source)
XLA Modules:
  0.0 62.8 jit_solution(16124672689594175774)
XLA Ops:
  0.0 1.5 %shard_map.46 = (f32[32,512]{1,0:T(8,128)S(1)}, f32[1,32,128]{2,1,0:T(8,128)S(1)}, bf16[2,256,256]{2,1,0:T(8,128)(2,1)S(1)}, bf16[2,256,256]{2,1,0:T(8,128)(2,1)...) custom-call(s32[1,2,3]{2,1,0:T(2,128)} %mask.1, f32[1,32,512]{2,1,0:T(8,128)} %normals.1, f32[1,2,256,256]{3,2,1,0:T(8,128)} %inv.1, ...), custom_call_target="tpu_custom_call" | custom-call | tf_op jit(solution)/shard_map/pallas_call | solution.py:200
  1.5 0.7 %collective-permute-start = (f32[32,512]{1,0:T(8,128)S(1)}, f32[32,512]{1,0:T(8,128)S(1)}, u32[]{:S(2)}, u32[]{:S(2)}) collective-permute-start(f32[32,512]{1,0:T(8,128)S(1)} %get-tuple-element.36.const), channel_id=1, source_target_pairs={{30,28},{31,29}} | collective-permute-start | bytes 196616 | tf_op jit(solution)/shard_map/ppermute | solution.py:218
  2.2 0.7 %collective-permute-start.1 = (f32[1,32,128]{2,1,0:T(8,128)S(1)}, f32[1,32,128]{2,1,0:T(8,128)S(1)}, u32[]{:S(2)}, u32[]{:S(2)}) collective-permute-start(f32[1,32,128]{2,1,0:T(8,128)S(1)} %get-tuple-element.37), channel_id=1, source_target_pairs={{30,29},{31,28}} | collective-permute-start | bytes 49160 | tf_op jit(solution)/shard_map/ppermute | solution.py:187
  2.9 0.7 %shard_map.47 = (f32[1088,256]{1,0:T(8,128)S(1)}, bf16[1024,256]{1,0:T(8,128)(2,1)S(1)}, bf16[1024,256]{1,0:T(8,128)(2,1)S(1)}) custom-call(s32[2,3]{1,0:T(2,128)S(1)} %get-tuple-element.38.mask, f32[32,512]{1,0:T(8,128)S(1)} %get-tuple-element.36.const, bf16[2,256,256]{2,1,0:T(8,128)(2,1)S(1)} %get-tuple-element.39.inv_high, ...), custom_call_target="tpu_custom_call" | custom-call | flops 427819008 | bytes 4194304 | tf_op jit(solution)/shard_map/pallas_call | solution.py:219
  3.6 0.0 collective-permute-done.1.rim._first_rim
  3.6 0.0 collective-permute-done.far._first_far
  3.6 1.3 %collective-permute-start.4 = (f32[1088,256]{1,0:T(8,128)S(1)}, f32[1088,256]{1,0:T(8,128)S(1)}, u32[]{:S(2)}, u32[]{:S(2)}) collective-permute-start(f32[1088,256]{1,0:T(8,128)S(1)} %get-tuple-element.46), channel_id=1, source_target_pairs={{2,0},{3,1},{6,4},{7,5},{10,8},{11,9},{14,12},{15,13},{18,16},{19,... | collective-permute-start | bytes 3342344 | tf_op jit(solution)/shard_map/ppermute | solution.py:240
  4.9 1.3 %collective-permute-start.5 = (f32[1,544,128]{2,1,0:T(8,128)S(1)}, f32[1,544,128]{2,1,0:T(8,128)S(1)}, u32[]{:S(2)}, u32[]{:S(2)}) collective-permute-start(f32[1,544,128]{2,1,0:T(8,128)S(1)} %get-tuple-element.47), channel_id=1, source_target_pairs={{2,1},{3,0},{6,5},{7,4},{10,9},{11,8},{14,13},{15,12},{18,17},{19,... | collective-permute-start | bytes 835592 | tf_op jit(solution)/shard_map/ppermute | solution.py:187
  6.3 0.7 %collective-permute-start.2 = (f32[1,32,512]{2,1,0:T(8,128)S(1)}, f32[1,32,512]{2,1,0:T(8,128)S(1)}, u32[]{:S(2)}, u32[]{:S(2)}) collective-permute-start(f32[1,32,512]{2,1,0:T(8,128)S(1)} %bitcast.9), channel_id=1, source_target_pairs={{28,25},{29,24}} | collective-permute-start | bytes 196616 | tf_op jit(solution)/shard_map/ppermute | solution.py:187
  7.0 0.7 %collective-permute-start.3 = (f32[32,512]{1,0:T(8,128)S(1)}, f32[32,512]{1,0:T(8,128)S(1)}, u32[]{:S(2)}, u32[]{:S(2)}) collective-permute-start(f32[32,512]{1,0:T(8,128)S(1)} %get-tuple-element.44.rest_5_), channel_id=1, source_target_pairs={{28,24},{29,25}} | collective-permute-start | bytes 196616 | tf_op jit(solution)/shard_map/ppermute | solution.py:277
  7.7 6.5 %collective-permute-done.5.rim = f32[1,544,128]{2,1,0:T(8,128)S(1)} collective-permute-done((f32[1,544,128]{2,1,0:T(8,128)S(1)}, f32[1,544,128]{2,1,0:T(8,128)S(1)}, u32[]{:S(2)}, u32[]{:S(2)}) %collective-permute-start.5) | collective-permute-done | bytes 278560 | tf_op jit(solution)/shard_map/ppermute | solution.py:187
  14.2 0.0 collective-permute-done.4.far
  14.2 0.2 shard_map.50
  14.3 0.0 collective-permute-done.2.next_in
  14.4 0.0 collective-permute-done.3.own_in
  14.4 0.7 %collective-permute-start.6 = (f32[1,32,512]{2,1,0:T(8,128)S(1)}, f32[1,32,512]{2,1,0:T(8,128)S(1)}, u32[]{:S(2)}, u32[]{:S(2)}) collective-permute-start(f32[1,32,512]{2,1,0:T(8,128)S(1)} %bitcast.10), channel_id=1, source_target_pairs={{24,21},{25,20}} | collective-permute-start | bytes 196616 | tf_op jit(solution)/shard_map/ppermute | solution.py:187
  15.1 0.7 %collective-permute-start.7 = (f32[32,512]{1,0:T(8,128)S(1)}, f32[32,512]{1,0:T(8,128)S(1)}, u32[]{:S(2)}, u32[]{:S(2)}) collective-permute-start(f32[32,512]{1,0:T(8,128)S(1)} %get-tuple-element.53.rest_5_), channel_id=1, source_target_pairs={{24,20},{25,21}} | collective-permute-start | bytes 196616 | tf_op jit(solution)/shard_map/ppermute | solution.py:277
  15.7 0.0 collective-permute-done.6.next_in
  15.8 0.0 collective-permute-done.7.own_in
  15.8 0.7 %collective-permute-start.8 = (f32[1,32,512]{2,1,0:T(8,128)S(1)}, f32[1,32,512]{2,1,0:T(8,128)S(1)}, u32[]{:S(2)}, u32[]{:S(2)}) collective-permute-start(f32[1,32,512]{2,1,0:T(8,128)S(1)} %bitcast.11), channel_id=1, source_target_pairs={{20,17},{21,16}} | collective-permute-start | bytes 196616 | tf_op jit(solution)/shard_map/ppermute | solution.py:187
  16.5 0.7 %collective-permute-start.9 = (f32[32,512]{1,0:T(8,128)S(1)}, f32[32,512]{1,0:T(8,128)S(1)}, u32[]{:S(2)}, u32[]{:S(2)}) collective-permute-start(f32[32,512]{1,0:T(8,128)S(1)} %get-tuple-element.55.rest_5_), channel_id=1, source_target_pairs={{20,16},{21,17}} | collective-permute-start | bytes 196616 | tf_op jit(solution)/shard_map/ppermute | solution.py:277
  17.1 0.0 collective-permute-done.8.next_in
  17.1 0.0 collective-permute-done.9.own_in
  17.2 0.7 %collective-permute-start.10 = (f32[1,32,512]{2,1,0:T(8,128)S(1)}, f32[1,32,512]{2,1,0:T(8,128)S(1)}, u32[]{:S(2)}, u32[]{:S(2)}) collective-permute-start(f32[1,32,512]{2,1,0:T(8,128)S(1)} %bitcast.12), channel_id=1, source_target_pairs={{16,13},{17,12}} | collective-permute-start | bytes 196616 | tf_op jit(solution)/shard_map/ppermute | solution.py:187
  17.9 0.7 %collective-permute-start.11 = (f32[32,512]{1,0:T(8,128)S(1)}, f32[32,512]{1,0:T(8,128)S(1)}, u32[]{:S(2)}, u32[]{:S(2)}) collective-permute-start(f32[32,512]{1,0:T(8,128)S(1)} %get-tuple-element.57.rest_5_), channel_id=1, source_target_pairs={{16,12},{17,13}} | collective-permute-start | bytes 196616 | tf_op jit(solution)/shard_map/ppermute | solution.py:277
  18.5 0.0 collective-permute-done.10.next_in
  18.5 0.0 collective-permute-done.11.own_in
  18.6 0.7 %collective-permute-start.12 = (f32[1,32,512]{2,1,0:T(8,128)S(1)}, f32[1,32,512]{2,1,0:T(8,128)S(1)}, u32[]{:S(2)}, u32[]{:S(2)}) collective-permute-start(f32[1,32,512]{2,1,0:T(8,128)S(1)} %bitcast.13), channel_id=1, source_target_pairs={{12,9},{13,8}} | collective-permute-start | bytes 196616 | tf_op jit(solution)/shard_map/ppermute | solution.py:187
  19.3 0.7 %collective-permute-start.13 = (f32[32,512]{1,0:T(8,128)S(1)}, f32[32,512]{1,0:T(8,128)S(1)}, u32[]{:S(2)}, u32[]{:S(2)}) collective-permute-start(f32[32,512]{1,0:T(8,128)S(1)} %get-tuple-element.59.rest_5_), channel_id=1, source_target_pairs={{12,8},{13,9}} | collective-permute-start | bytes 196616 | tf_op jit(solution)/shard_map/ppermute | solution.py:277
  19.9 0.0 collective-permute-done.12.next_in
  19.9 0.0 collective-permute-done.13.own_in
  20.0 0.7 %collective-permute-start.14 = (f32[1,32,512]{2,1,0:T(8,128)S(1)}, f32[1,32,512]{2,1,0:T(8,128)S(1)}, u32[]{:S(2)}, u32[]{:S(2)}) collective-permute-start(f32[1,32,512]{2,1,0:T(8,128)S(1)} %bitcast.14), channel_id=1, source_target_pairs={{8,5},{9,4}} | collective-permute-start | bytes 196616 | tf_op jit(solution)/shard_map/ppermute | solution.py:187
  20.6 0.7 %collective-permute-start.15 = (f32[32,512]{1,0:T(8,128)S(1)}, f32[32,512]{1,0:T(8,128)S(1)}, u32[]{:S(2)}, u32[]{:S(2)}) collective-permute-start(f32[32,512]{1,0:T(8,128)S(1)} %get-tuple-element.61.rest_5_), channel_id=1, source_target_pairs={{8,4},{9,5}} | collective-permute-start | bytes 196616 | tf_op jit(solution)/shard_map/ppermute | solution.py:277
  21.3 0.0 collective-permute-done.14.next_in
  21.3 0.0 collective-permute-done.15.own_in
  21.4 1.3 %collective-permute-start.16 = (f32[1,32,512]{2,1,0:T(8,128)S(1)}, f32[1,32,512]{2,1,0:T(8,128)S(1)}, u32[]{:S(2)}, u32[]{:S(2)}) collective-permute-start(f32[1,32,512]{2,1,0:T(8,128)S(1)} %bitcast.15), channel_id=1, source_target_pairs={{4,1},{5,0}} | collective-permute-start | bytes 196616 | tf_op jit(solution)/shard_map/ppermute | solution.py:187
  22.7 1.3 %collective-permute-start.17 = (f32[32,512]{1,0:T(8,128)S(1)}, f32[32,512]{1,0:T(8,128)S(1)}, u32[]{:S(2)}, u32[]{:S(2)}) collective-permute-start(f32[32,512]{1,0:T(8,128)S(1)} %get-tuple-element.63.rest_5_), channel_id=1, source_target_pairs={{4,0},{5,1}} | collective-permute-start | bytes 196616 | tf_op jit(solution)/shard_map/ppermute | solution.py:277
  24.0 34.7 %collective-permute-done.16.next_in = f32[1,32,512]{2,1,0:T(8,128)S(1)} collective-permute-done((f32[1,32,512]{2,1,0:T(8,128)S(1)}, f32[1,32,512]{2,1,0:T(8,128)S(1)}, u32[]{:S(2)}, u32[]{:S(2)}) %collective-permute-start.16) | collective-permute-done | bytes 65568 | tf_op jit(solution)/shard_map/ppermute | solution.py:187
  58.7 0.7 %collective-permute-done.17.own_in = f32[32,512]{1,0:T(8,128)S(1)} collective-permute-done((f32[32,512]{1,0:T(8,128)S(1)}, f32[32,512]{1,0:T(8,128)S(1)}, u32[]{:S(2)}, u32[]{:S(2)}) %collective-permute-start.17) | collective-permute-done | bytes 65568 | tf_op jit(solution)/shard_map/ppermute | solution.py:277
  59.4 0.6 shard_map.57
  60.0 1.3 %collective-permute-start.18 = (f32[32,512]{1,0:T(8,128)S(1)}, f32[32,512]{1,0:T(8,128)S(1)}, u32[]{:S(2)}, u32[]{:S(2)}) collective-permute-start(f32[32,512]{1,0:T(8,128)S(1)} %get-tuple-element.66), channel_id=1, source_target_pairs={{0,2},{1,3},{4,6},{5,7},{8,10},{9,11},{12,14},{13,15},{16,18},{17,... | collective-permute-start | bytes 196616 | tf_op jit(solution)/shard_map/ppermute | solution.py:278
  61.3 0.9 %collective-permute-done.18 = f32[32,512]{1,0:T(8,128)S(1)} collective-permute-done((f32[32,512]{1,0:T(8,128)S(1)}, f32[32,512]{1,0:T(8,128)S(1)}, u32[]{:S(2)}, u32[]{:S(2)}) %collective-permute-start.18) | collective-permute-done | bytes 65568 | tf_op jit(solution)/shard_map/ppermute | solution.py:278
  62.2 0.6 %select_bitcast_fusion = f32[1,32,512]{2,1,0:T(8,128)} fusion(f32[32,512]{1,0:T(8,128)S(1)} %get-tuple-element.65, f32[32,512]{1,0:T(8,128)S(1)} %collective-permute-done.18, pred[]{:T(512)S(6)} %eq.5), kind=kLoop, calls=%fused_computation | loop fusion | flops 16384 | bytes 196609 | tf_op jit(solution)/shard_map/broadcast_in_dim | solution.py:279
  (12 shorter events, 0.2 us)
Async XLA Ops:
  1.5 2.0 %collective-permute-start = (f32[32,512]{1,0:T(8,128)S(1)}, f32[32,512]{1,0:T(8,128)S(1)}, u32[]{:S(2)}, u32[]{:S(2)}) collective-permute-start(f32[32,512]{1,0:T(8,128)S(1)} %get-tuple-element.36.const), channel_id=1, source_target_pairs={{30,28},{31,29}} | collective-permute-start | bytes 196616 | tf_op jit(solution)/shard_map/ppermute | solution.py:218
  2.2 1.4 %collective-permute-start.1 = (f32[1,32,128]{2,1,0:T(8,128)S(1)}, f32[1,32,128]{2,1,0:T(8,128)S(1)}, u32[]{:S(2)}, u32[]{:S(2)}) collective-permute-start(f32[1,32,128]{2,1,0:T(8,128)S(1)} %get-tuple-element.37), channel_id=1, source_target_pairs={{30,29},{31,28}} | collective-permute-start | bytes 49160 | tf_op jit(solution)/shard_map/ppermute | solution.py:187
  3.6 10.5 %collective-permute-start.4 = (f32[1088,256]{1,0:T(8,128)S(1)}, f32[1088,256]{1,0:T(8,128)S(1)}, u32[]{:S(2)}, u32[]{:S(2)}) collective-permute-start(f32[1088,256]{1,0:T(8,128)S(1)} %get-tuple-element.46), channel_id=1, source_target_pairs={{2,0},{3,1},{6,4},{7,5},{10,8},{11,9},{14,12},{15,13},{18,16},{19,... | collective-permute-start | bytes 3342344 | tf_op jit(solution)/shard_map/ppermute | solution.py:240
  4.9 9.2 %collective-permute-start.5 = (f32[1,544,128]{2,1,0:T(8,128)S(1)}, f32[1,544,128]{2,1,0:T(8,128)S(1)}, u32[]{:S(2)}, u32[]{:S(2)}) collective-permute-start(f32[1,544,128]{2,1,0:T(8,128)S(1)} %get-tuple-element.47), channel_id=1, source_target_pairs={{2,1},{3,0},{6,5},{7,4},{10,9},{11,8},{14,13},{15,12},{18,17},{19,... | collective-permute-start | bytes 835592 | tf_op jit(solution)/shard_map/ppermute | solution.py:187
  6.3 8.0 %collective-permute-start.2 = (f32[1,32,512]{2,1,0:T(8,128)S(1)}, f32[1,32,512]{2,1,0:T(8,128)S(1)}, u32[]{:S(2)}, u32[]{:S(2)}) collective-permute-start(f32[1,32,512]{2,1,0:T(8,128)S(1)} %bitcast.9), channel_id=1, source_target_pairs={{28,25},{29,24}} | collective-permute-start | bytes 196616 | tf_op jit(solution)/shard_map/ppermute | solution.py:187
  7.0 7.4 %collective-permute-start.3 = (f32[32,512]{1,0:T(8,128)S(1)}, f32[32,512]{1,0:T(8,128)S(1)}, u32[]{:S(2)}, u32[]{:S(2)}) collective-permute-start(f32[32,512]{1,0:T(8,128)S(1)} %get-tuple-element.44.rest_5_), channel_id=1, source_target_pairs={{28,24},{29,25}} | collective-permute-start | bytes 196616 | tf_op jit(solution)/shard_map/ppermute | solution.py:277
  14.4 1.3 %collective-permute-start.6 = (f32[1,32,512]{2,1,0:T(8,128)S(1)}, f32[1,32,512]{2,1,0:T(8,128)S(1)}, u32[]{:S(2)}, u32[]{:S(2)}) collective-permute-start(f32[1,32,512]{2,1,0:T(8,128)S(1)} %bitcast.10), channel_id=1, source_target_pairs={{24,21},{25,20}} | collective-permute-start | bytes 196616 | tf_op jit(solution)/shard_map/ppermute | solution.py:187
  15.1 0.7 %collective-permute-start.7 = (f32[32,512]{1,0:T(8,128)S(1)}, f32[32,512]{1,0:T(8,128)S(1)}, u32[]{:S(2)}, u32[]{:S(2)}) collective-permute-start(f32[32,512]{1,0:T(8,128)S(1)} %get-tuple-element.53.rest_5_), channel_id=1, source_target_pairs={{24,20},{25,21}} | collective-permute-start | bytes 196616 | tf_op jit(solution)/shard_map/ppermute | solution.py:277
  15.8 1.3 %collective-permute-start.8 = (f32[1,32,512]{2,1,0:T(8,128)S(1)}, f32[1,32,512]{2,1,0:T(8,128)S(1)}, u32[]{:S(2)}, u32[]{:S(2)}) collective-permute-start(f32[1,32,512]{2,1,0:T(8,128)S(1)} %bitcast.11), channel_id=1, source_target_pairs={{20,17},{21,16}} | collective-permute-start | bytes 196616 | tf_op jit(solution)/shard_map/ppermute | solution.py:187
  16.5 0.7 %collective-permute-start.9 = (f32[32,512]{1,0:T(8,128)S(1)}, f32[32,512]{1,0:T(8,128)S(1)}, u32[]{:S(2)}, u32[]{:S(2)}) collective-permute-start(f32[32,512]{1,0:T(8,128)S(1)} %get-tuple-element.55.rest_5_), channel_id=1, source_target_pairs={{20,16},{21,17}} | collective-permute-start | bytes 196616 | tf_op jit(solution)/shard_map/ppermute | solution.py:277
  17.2 1.3 %collective-permute-start.10 = (f32[1,32,512]{2,1,0:T(8,128)S(1)}, f32[1,32,512]{2,1,0:T(8,128)S(1)}, u32[]{:S(2)}, u32[]{:S(2)}) collective-permute-start(f32[1,32,512]{2,1,0:T(8,128)S(1)} %bitcast.12), channel_id=1, source_target_pairs={{16,13},{17,12}} | collective-permute-start | bytes 196616 | tf_op jit(solution)/shard_map/ppermute | solution.py:187
  17.9 0.7 %collective-permute-start.11 = (f32[32,512]{1,0:T(8,128)S(1)}, f32[32,512]{1,0:T(8,128)S(1)}, u32[]{:S(2)}, u32[]{:S(2)}) collective-permute-start(f32[32,512]{1,0:T(8,128)S(1)} %get-tuple-element.57.rest_5_), channel_id=1, source_target_pairs={{16,12},{17,13}} | collective-permute-start | bytes 196616 | tf_op jit(solution)/shard_map/ppermute | solution.py:277
  18.6 1.3 %collective-permute-start.12 = (f32[1,32,512]{2,1,0:T(8,128)S(1)}, f32[1,32,512]{2,1,0:T(8,128)S(1)}, u32[]{:S(2)}, u32[]{:S(2)}) collective-permute-start(f32[1,32,512]{2,1,0:T(8,128)S(1)} %bitcast.13), channel_id=1, source_target_pairs={{12,9},{13,8}} | collective-permute-start | bytes 196616 | tf_op jit(solution)/shard_map/ppermute | solution.py:187
  19.3 0.7 %collective-permute-start.13 = (f32[32,512]{1,0:T(8,128)S(1)}, f32[32,512]{1,0:T(8,128)S(1)}, u32[]{:S(2)}, u32[]{:S(2)}) collective-permute-start(f32[32,512]{1,0:T(8,128)S(1)} %get-tuple-element.59.rest_5_), channel_id=1, source_target_pairs={{12,8},{13,9}} | collective-permute-start | bytes 196616 | tf_op jit(solution)/shard_map/ppermute | solution.py:277
  20.0 1.3 %collective-permute-start.14 = (f32[1,32,512]{2,1,0:T(8,128)S(1)}, f32[1,32,512]{2,1,0:T(8,128)S(1)}, u32[]{:S(2)}, u32[]{:S(2)}) collective-permute-start(f32[1,32,512]{2,1,0:T(8,128)S(1)} %bitcast.14), channel_id=1, source_target_pairs={{8,5},{9,4}} | collective-permute-start | bytes 196616 | tf_op jit(solution)/shard_map/ppermute | solution.py:187
  20.6 0.7 %collective-permute-start.15 = (f32[32,512]{1,0:T(8,128)S(1)}, f32[32,512]{1,0:T(8,128)S(1)}, u32[]{:S(2)}, u32[]{:S(2)}) collective-permute-start(f32[32,512]{1,0:T(8,128)S(1)} %get-tuple-element.61.rest_5_), channel_id=1, source_target_pairs={{8,4},{9,5}} | collective-permute-start | bytes 196616 | tf_op jit(solution)/shard_map/ppermute | solution.py:277
  21.4 37.3 %collective-permute-start.16 = (f32[1,32,512]{2,1,0:T(8,128)S(1)}, f32[1,32,512]{2,1,0:T(8,128)S(1)}, u32[]{:S(2)}, u32[]{:S(2)}) collective-permute-start(f32[1,32,512]{2,1,0:T(8,128)S(1)} %bitcast.15), channel_id=1, source_target_pairs={{4,1},{5,0}} | collective-permute-start | bytes 196616 | tf_op jit(solution)/shard_map/ppermute | solution.py:187
  22.7 36.8 %collective-permute-start.17 = (f32[32,512]{1,0:T(8,128)S(1)}, f32[32,512]{1,0:T(8,128)S(1)}, u32[]{:S(2)}, u32[]{:S(2)}) collective-permute-start(f32[32,512]{1,0:T(8,128)S(1)} %get-tuple-element.63.rest_5_), channel_id=1, source_target_pairs={{4,0},{5,1}} | collective-permute-start | bytes 196616 | tf_op jit(solution)/shard_map/ppermute | solution.py:277
  60.0 2.2 %collective-permute-start.18 = (f32[32,512]{1,0:T(8,128)S(1)}, f32[32,512]{1,0:T(8,128)S(1)}, u32[]{:S(2)}, u32[]{:S(2)}) collective-permute-start(f32[32,512]{1,0:T(8,128)S(1)} %get-tuple-element.66), channel_id=1, source_target_pairs={{0,2},{1,3},{4,6},{5,7},{8,10},{9,11},{12,14},{13,15},{16,18},{17,... | collective-permute-start | bytes 196616 | tf_op jit(solution)/shard_map/ppermute | solution.py:278

commit v3 on v2

v3 whole, which is shorter than its diff:
```python
import functools

import jax
import jax.numpy as jnp
from jax import lax
from jax.experimental import pallas as pl
from jax.experimental.pallas import tpu as pltpu
from jax.sharding import PartitionSpec as P

BOTH = ("tm", "row")
VMEM = pl.BlockSpec(memory_space=pltpu.VMEM)
HBM = pl.BlockSpec(memory_space=pltpu.HBM)
PARAMS = pltpu.CompilerParams(vmem_limit_bytes=32 * 1024 * 1024)


def halves(value):
    high = value.astype(jnp.bfloat16)
    low = (value - high.astype(jnp.float32)).astype(jnp.bfloat16)
    return high, low


def dot(a, b):
    return jnp.dot(a, b, preferred_element_type=jnp.float32)


def stacked_dot(pair, cols, high, low):
    rows = pair.shape[0] // 2
    wide = dot(pair[:, cols], high)
    return wide[:rows] + wide[rows:] + dot(pair[:rows, cols], low)


def triple(high, low, inv_high, inv_low):
    return dot(high, inv_high) + dot(low, inv_high) + dot(high, inv_low)


def put_rim(sides, rim, columns):
    if sides == 1:
        row = lax.axis_index("row")

        @pl.when(row == 0)
        def _():
            rim[0] = columns(True)

        @pl.when(row != 0)
        def _():
            rim[0] = columns(False)
    else:
        rim[0] = columns(True)
        rim[1] = columns(False)


def const_kernel(
    mask, normals, inv, lag, const, inv_high, inv_low, lag_out, mask_out, normals_in, inv_in, sems
):
    blocks, length = inv.shape[1], inv.shape[2]
    moves = [pltpu.make_async_copy(normals.at[0], normals_in, sems.at[0])]
    for b in range(blocks):
        moves.append(pltpu.make_async_copy(inv.at[0, b], inv_in.at[b], sems.at[1 + b]))
    for b in range(blocks):
        moves.append(pltpu.make_async_copy(lag.at[0, b], lag_out.at[b], sems.at[1 + blocks + b]))
    moves.append(pltpu.make_async_copy(mask.at[0], mask_out, sems.at[1 + 2 * blocks]))
    for move in moves:
        move.start()
    moves[0].wait()
    for b in range(blocks):
        at = slice(b * length, (b + 1) * length)
        high, low = halves(normals_in[:, at])
        moves[1 + b].wait()
        inv_high[b], inv_low[b] = halves(inv_in[b])
        const[:, at] = triple(high, low, inv_high[b], inv_low[b])
    for move in moves[1 + blocks :]:
        move.wait()


def fuse_kernel(mask, const, inv_high, inv_low, lag, own, near_high, near_low):
    blocks, window, length = lag.shape
    edge = (window - length) // 2
    cols = const.shape[0]
    cuts = (0, edge, edge + length, window)
    flags = mask[...].astype(jnp.float32)
    for b in range(blocks):
        at = blocks * window + b * cols
        own[at : at + cols] = const[:, b * length : (b + 1) * length]
        for part in range(3):
            lo, hi = cuts[part], cuts[part + 1]
            rows = slice(b * window + lo, b * window + hi)
            high, low = halves(lag[b, lo:hi] * flags[b : b + 1, part : part + 1])
            value = triple(high, low, inv_high[b], inv_low[b])
            own[rows] = value
            near_high[rows], near_low[rows] = halves(value)


def edge_kernel(sides, blocks, cols, _own, _first_next, _first_far, own, rim):
    length, edge = own.shape[1], rim.shape[2]
    window = length + 2 * edge

    def columns(last):
        b = blocks - 1 if last else 0
        cut = slice(length - edge, length) if last else slice(0, edge)
        at = blocks * window + b * cols
        return jnp.concatenate([own[b * window : (b + 1) * window, cut], own[at : at + cols, cut]])

    put_rim(sides, rim, columns)


def pair_kernel(far, rim, near_high, near_low, const, high, low, both, far_high, far_low, total):
    cols, sites = const.shape
    length = far.shape[1]
    blocks = sites // length
    window = near_high.shape[0] // blocks
    edge = (window - length) // 2
    span = 2 * window
    tall = blocks * window
    far_high[...], far_low[...] = halves(far[:tall])
    if rim.shape[0] == 1:
        flag = jnp.minimum(lax.axis_index("row"), 1).astype(jnp.float32)
        left, right = rim[0] * flag, rim[0] * (1 - flag)
    else:
        left, right = rim[0], rim[1]
    left_pair, right_pair = halves(left[:window]), halves(right[:window])
    for b in range(blocks):
        here = slice(b * window, (b + 1) * window)
        column = slice(b * length, (b + 1) * length)

        def part(lo, hi):
            rows = slice(b * window + lo, b * window + hi)
            return near_high[rows], near_low[rows]

        def constant(block):
            if block < 0:
                return left[window:]
            if block == blocks:
                return right[window:]
            return far[tall + block * cols : tall + (block + 1) * cols]

        if b > 0:
            before = slice((b - 1) * window, b * window)
            low_pair = far_high[before, length - edge :], far_low[before, length - edge :]
            low_const = constant(b - 1)[:, length - edge :]
        else:
            low_pair, low_const = left_pair, constant(-1)
        if b + 1 < blocks:
            after = slice((b + 1) * window, (b + 2) * window)
            high_pair = far_high[after, :edge], far_low[after, :edge]
            high_const = constant(b + 1)[:, :edge]
        else:
            high_pair, high_const = right_pair, constant(blocks)
        first = triple(*low_pair, *part(0, edge))
        middle = triple(far_high[here], far_low[here], *part(edge, edge + length))
        last = triple(*high_pair, *part(edge + length, window))
        total[:window] = first
        total[window:] = last
        total[length : length + window] += middle
        high[b * span : (b + 1) * span], low[b * span : (b + 1) * span] = halves(total[...])
        both[:, column] = const[:, column] - (
            triple(*halves(low_const), *part(0, edge))
            + triple(*halves(constant(b)), *part(edge, edge + length))
            + triple(*halves(high_const), *part(edge + length, window))
        )


def keep(ref, start, value):
    cols, width = value.shape
    high, low = halves(value)
    ref[:cols, pl.ds(start, width)] = high
    ref[cols:, pl.ds(start, width)] = low


def load(sides, next_in, own_in, halo, ref):
    sites = own_in.shape[1]
    ref[...] = jnp.zeros_like(ref)
    keep(ref, halo, own_in[...])
    for side in range(sides):
        on_right = 1 - jnp.minimum(lax.axis_index("row"), 1).astype(jnp.int32) if sides == 1 else side
        start = pl.multiple_of((1 - on_right) * (sites - halo), 128)
        keep(ref, pl.multiple_of(on_right * (halo + sites), 128), next_in[side, :, pl.ds(start, halo)])


def top_kernel(mine, sides, next_in, own_in, const, near_high, near_low, _upper, _lower, upper, lower, mid):
    sites = lower.shape[1]
    length = near_high.shape[1]
    blocks = sites // length
    window = near_high.shape[0] // blocks
    edge = (window - length) // 2

    @pl.when(lax.axis_index("tm") == 2 * mine)
    def _():
        load(sides, next_in, own_in, edge, mid)
        upper[...] = own_in[...]
        for b in range(blocks):
            at, rows = slice(b * length, (b + 1) * length), slice(b * window, (b + 1) * window)
            product = stacked_dot(mid, slice(b * length, b * length + window), near_high[rows], near_low[rows])
            lower[:, at] = const[:, at] - product


def chain_kernel(mine, both, high, low, *rest):
    sides, given = rest[0], rest[1:]
    if sides:
        next_in, own_in, _late, _lower, late, lower = given
    else:
        late, _lower, lower = given
    sites = lower.shape[1]
    blocks = sites // high.shape[1]
    length, span = high.shape[1], high.shape[0] // blocks
    halo = (late.shape[1] - sites) // 2

    @pl.when(lax.axis_index("tm") == 2 * mine)
    def _():
        if sides:
            load(sides, next_in, own_in, halo, late)
        for b in range(blocks):
            at, rows = slice(b * length, (b + 1) * length), slice(b * span, (b + 1) * span)
            lower[:, at] = both[:, at] + stacked_dot(late, slice(b * length, b * length + span), high[rows], low[rows])


def upper_kernel(
    sides, top, next_in, own_in, far, far_high, far_low, _late, _upper, late, upper
):
    cols, sites = upper.shape
    length = far.shape[1]
    blocks = sites // length
    window = far_high.shape[0] // blocks
    halo = (late.shape[1] - sites) // 2
    at_window = halo - (window - length) // 2

    @pl.when(lax.axis_index("tm") == 0)
    def _():
        load(sides, next_in, own_in, halo, late)

    @pl.when(lax.axis_index("tm") != 2 * top)
    def _():
        for b in range(blocks):
            rows = slice(b * window, (b + 1) * window)
            at = blocks * window + b * cols
            start = at_window + b * length
            upper[:, b * length : (b + 1) * length] = far[at : at + cols] - stacked_dot(
                late, slice(start, start + window), far_high[rows], far_low[rows]
            )


def local(normals, inv_diag, lag_coupling, fill_mask):
    times, rows = lax.axis_size("tm"), lax.axis_size("row")
    device = lax.axis_index("tm")
    cols, sites = normals.shape[1:]
    blocks, length = inv_diag.shape[1:3]
    window = lag_coupling.shape[2]
    edge = (window - length) // 2
    halo = length + edge
    sides = 1 if rows == 2 else 2
    pairs = times // 2
    f32, bf16 = jnp.float32, jnp.bfloat16
    shape = jax.ShapeDtypeStruct

    def link(source, target):
        return [(s * rows + r, t * rows + r) for s, t in zip(source, target) for r in range(rows)]

    def cross(value, source, target):
        if sides == 1:
            perm = [(s * rows + r, t * rows + 1 - r) for s, t in zip(source, target) for r in range(2)]
            return lax.ppermute(value, BOTH, perm)
        moved = []
        for side, step in enumerate((1, -1)):
            perm = [
                (s * rows + r, t * rows + r + step)
                for s, t in zip(source, target)
                for r in range(rows)
                if 0 <= r + step < rows
            ]
            moved.append(lax.ppermute(value[side : side + 1] if value.shape[0] > 1 else value, BOTH, perm))
        return jnp.concatenate(moved)

    tall = blocks * window
    const, inv_high, inv_low, lag, mask = pl.pallas_call(
        const_kernel,
        out_shape=(
            shape((cols, sites), f32),
            shape((blocks, length, length), bf16), shape((blocks, length, length), bf16),
            shape(lag_coupling.shape[1:], f32), shape(fill_mask.shape[1:], fill_mask.dtype),
        ),
        in_specs=[HBM] * 4,
        out_specs=(VMEM,) * 5,
        scratch_shapes=[
            pltpu.VMEM(normals.shape[1:], f32),
            pltpu.VMEM(inv_diag.shape[1:], f32),
            pltpu.SemaphoreType.DMA((2 + 2 * blocks,)),
        ],
        compiler_params=PARAMS,
    )(*[pltpu.with_memory_space_constraint(a, pltpu.HBM) for a in (fill_mask, normals, inv_diag, lag_coupling)])
    odd, even = range(1, times, 2), range(0, times, 2)
    first_next = cross(const[None], odd[-1:], even[-1:])
    first_own = lax.ppermute(const, BOTH, link(odd[-1:], even[-1:]))
    near, near_high, near_low = pl.pallas_call(
        fuse_kernel,
        out_shape=(
            shape((tall + blocks * cols, length), f32), shape((tall, length), bf16), shape((tall, length), bf16),
        ),
        in_specs=[VMEM] * 5,
        out_specs=(VMEM,) * 3,
        compiler_params=PARAMS,
        cost_estimate=pl.CostEstimate(
            flops=6 * (tall + cols * blocks) * length * length, bytes_accessed=16 * tall * length, transcendentals=0
        ),
    )(mask, const, inv_high, inv_low, lag)
    near, edges = pl.pallas_call(
        functools.partial(edge_kernel, sides, blocks, cols),
        out_shape=(shape(near.shape, f32), shape((sides, window + cols, edge), f32)),
        in_specs=[VMEM] * 3,
        out_specs=(VMEM,) * 2,
        input_output_aliases={0: 0},
        compiler_params=PARAMS,
    )(near, first_next, first_own)
    rim = cross(edges, odd[:-1], even[:-1])
    far = lax.ppermute(near, BOTH, link(odd[:-1], even[:-1]))

    blank = jnp.zeros((cols, sites), f32)
    upper, lower = pl.pallas_call(
        functools.partial(top_kernel, pairs - 1, sides),
        out_shape=(shape((cols, sites), f32),) * 2,
        in_specs=[VMEM] * 7,
        out_specs=(VMEM,) * 2,
        scratch_shapes=[pltpu.VMEM((2 * cols, sites + 2 * edge), bf16)],
        input_output_aliases={5: 0, 6: 1},
        compiler_params=PARAMS,
    )(first_next, first_own, const, near_high, near_low, blank, blank)
    high, low, both, far_high, far_low = pl.pallas_call(
        pair_kernel,
        out_shape=(
            shape((2 * tall, length), bf16), shape((2 * tall, length), bf16), shape((cols, sites), f32),
            shape((tall, length), bf16), shape((tall, length), bf16),
        ),
        in_specs=[VMEM] * 5,
        out_specs=(VMEM,) * 5,
        scratch_shapes=[pltpu.VMEM((2 * window, length), f32)],
        compiler_params=PARAMS,
    )(far, rim, near_high, near_low, const)

    late = jnp.zeros((2 * cols, sites + 2 * halo), bf16)
    for mine in range(pairs - 1, 0, -1):
        source, target = [2 * mine], [2 * mine - 2]
        next_in = cross(lower[None], source, target)
        own_in = lax.ppermute(lower, BOTH, link(source, target))
        if mine > 1:
            late, lower = pl.pallas_call(
                lambda both, high, low, *rest, mine=mine: chain_kernel(mine - 1, both, high, low, sides, *rest),
                out_shape=(shape(late.shape, bf16), shape(lower.shape, f32)),
                in_specs=[VMEM] * 7,
                out_specs=(VMEM,) * 2,
                input_output_aliases={5: 0, 6: 1},
                compiler_params=PARAMS,
            )(both, high, low, next_in, own_in, late, lower)
    late, upper = pl.pallas_call(
        functools.partial(upper_kernel, sides, pairs - 1),
        out_shape=(shape(late.shape, bf16), shape(upper.shape, f32)),
        in_specs=[VMEM] * 7,
        out_specs=(VMEM,) * 2,
        input_output_aliases={5: 0, 6: 1},
        compiler_params=PARAMS,
    )(next_in, own_in, far, far_high, far_low, late, upper)
    returned = lax.ppermute(upper, BOTH, link(even, odd))
    lower = pl.pallas_call(
        lambda both, high, low, *rest: chain_kernel(0, both, high, low, 0, *rest),
        out_shape=shape(lower.shape, f32),
        in_specs=[VMEM] * 5,
        out_specs=VMEM,
        input_output_aliases={4: 0},
        compiler_params=PARAMS,
        cost_estimate=pl.CostEstimate(flops=12 * cols * tall * length, bytes_accessed=8 * tall * length, transcendentals=0),
    )(both, high, low, late, lower)
    return jnp.where(device % 2 == 0, lower, returned)[None]


def solution(mesh):
    placed = (
        P("tm", None, "row"),
        P("tm", "row", None, None),
        P("tm", "row", None, None),
        P("tm", "row", None),
    )
    return jax.shard_map(
        local, mesh=mesh, in_specs=placed, out_specs=P("tm", None, "row"), check_vma=False
    )
```

time: 63.2 us -> 62.6 us (level)
  waiting for transfers between devices: 42.9 us -> 40.7 us
  Pallas kernels: 3.16 us -> 4.74 us
    ppermute x9, waiting for transfers between devices: 41.3 us -> 39.3 us  [cross(): return lax.ppermute(value, BOTH, perm)]
    pallas_call x10 -> x11, Pallas kernels: 2.44 us -> 4.02 us  [the longest x1 1.6 us: local(): pl.pallas_call(pair_kernel, out_shape=(shape((2 * tall, length), bf16), s...]
  transfers between devices with their start and end apart: 19 -> 19, of which waited for: 4 -> 4; matrix products, arithmetic and copies ran while one was open for 0% -> 0% of each run, Pallas kernels for 1% -> 4%
where the time goes in v3:
time: 62.6 us; the launch traced here: 62.3 us
  waiting for transfers between devices  40.7 us (65%)
  starting transfers between devices  15.8 us (25%)
  Pallas kernels  4.74 us (8%)
  other arithmetic  0.64 us (1%)
    ppermute x9, waiting for transfers between devices, cross(): return lax.ppermute(value, BOTH, perm)  39.3 us
    ppermute x9, starting transfers between devices, cross(): return lax.ppermute(value, BOTH, perm)  7.24 us
    ppermute x7, starting transfers between devices, local(): own_in = lax.ppermute(lower, BOTH, link(source, target))  5.28 us
    pallas_call x1, Pallas kernels, local(): pl.pallas_call(pair_kernel, out_shape=(shape((2 * tall, length), bf16), s...  1.6 us
    pallas_call x1, Pallas kernels, local(): pl.pallas_call(const_kernel, out_shape=(shape((cols, sites), f32), shape(...  1.51 us
    ppermute x1, starting transfers between devices, local(): far = lax.ppermute(near, BOTH, link(odd[:-1], even[:-1]))  1.29 us
    ppermute x1, starting transfers between devices, local(): returned = lax.ppermute(upper, BOTH, link(even, odd))  1.29 us
  transfers between devices with their start and end apart: 19, of which 4 were waited for; matrix products, arithmetic and copies ran while one was open for 0% of the time, Pallas kernels for 4%

profile of v3, /device:TPU:0, one launch (start us, length us, event | category | flops | bytes accessed | tf_op | source)
XLA Modules:
  0.0 62.3 jit_solution(2731695836301577576)
XLA Ops:
  0.0 1.5 %shard_map.46 = (f32[32,512]{1,0:T(8,128)S(1)}, bf16[2,256,256]{2,1,0:T(8,128)(2,1)S(1)}, bf16[2,256,256]{2,1,0:T(8,128)(2,1)S(1)}, f32[2,512,256]{2,1,0:T(8,128)S(1)}, s32[2,3]{1,0:T(2,128)S(1)}) custom-call(s32[1,2,3]{2,1,0:T(2,128)} %mask.1, f32[1,32,512]{2,1,0:T(8,128)} %normals.1, f32[1,2,256,256]{3,2,1,0:T(8,128)} %inv.1, f32[1,2,512,256]{3,2,1,0:T(8,128)} %lag.1), custom_call_target="tpu_custom_call" | custom-call | tf_op jit(solution)/shard_map/pallas_call | solution.py:273
  1.5 0.7 %collective-permute-start = (f32[1,32,512]{2,1,0:T(8,128)S(1)}, f32[1,32,512]{2,1,0:T(8,128)S(1)}, u32[]{:S(2)}, u32[]{:S(2)}) collective-permute-start(f32[1,32,512]{2,1,0:T(8,128)S(1)} %bitcast.17), channel_id=1, source_target_pairs={{30,29},{31,28}} | collective-permute-start | bytes 196616 | tf_op jit(solution)/shard_map/ppermute | solution.py:260
  2.2 0.7 %collective-permute-start.1 = (f32[32,512]{1,0:T(8,128)S(1)}, f32[32,512]{1,0:T(8,128)S(1)}, u32[]{:S(2)}, u32[]{:S(2)}) collective-permute-start(f32[32,512]{1,0:T(8,128)S(1)} %get-tuple-element.37.const), channel_id=1, source_target_pairs={{30,28},{31,29}} | collective-permute-start | bytes 196616 | tf_op jit(solution)/shard_map/ppermute | solution.py:291
  2.9 0.7 %shard_map.47 = (f32[1088,256]{1,0:T(8,128)S(1)}, bf16[1024,256]{1,0:T(8,128)(2,1)S(1)}, bf16[1024,256]{1,0:T(8,128)(2,1)S(1)}) custom-call(s32[2,3]{1,0:T(2,128)S(1)} %get-tuple-element.36.mask, f32[32,512]{1,0:T(8,128)S(1)} %get-tuple-element.37.const, bf16[2,256,256]{2,1,0:T(8,128)(2,1)S(1)} %get-tuple-element.38.inv_high, ...), custom_call_target="tpu_custom_call" | custom-call | flops 427819008 | bytes 4194304 | tf_op jit(solution)/shard_map/pallas_call | solution.py:292
  3.6 0.0 collective-permute-done._first_next.next_in
  3.6 0.0 collective-permute-done.1._first_far.own_in
  3.6 1.3 %collective-permute-start.2 = (f32[1088,256]{1,0:T(8,128)S(1)}, f32[1088,256]{1,0:T(8,128)S(1)}, u32[]{:S(2)}, u32[]{:S(2)}) collective-permute-start(f32[1088,256]{1,0:T(8,128)S(1)} %get-tuple-element.42), channel_id=1, source_target_pairs={{2,0},{3,1},{6,4},{7,5},{10,8},{11,9},{14,12},{15,13},{18,16},{19,... | collective-permute-start | bytes 3342344 | tf_op jit(solution)/shard_map/ppermute | solution.py:313
  4.9 1.3 %collective-permute-start.3 = (f32[1,544,128]{2,1,0:T(8,128)S(1)}, f32[1,544,128]{2,1,0:T(8,128)S(1)}, u32[]{:S(2)}, u32[]{:S(2)}) collective-permute-start(f32[1,544,128]{2,1,0:T(8,128)S(1)} %get-tuple-element.43), channel_id=1, source_target_pairs={{2,1},{3,0},{6,5},{7,4},{10,9},{11,8},{14,13},{15,12},{18,17},{19,... | collective-permute-start | bytes 835592 | tf_op jit(solution)/shard_map/ppermute | solution.py:260
  6.3 0.7 %collective-permute-start.4 = (f32[1,32,512]{2,1,0:T(8,128)S(1)}, f32[1,32,512]{2,1,0:T(8,128)S(1)}, u32[]{:S(2)}, u32[]{:S(2)}) collective-permute-start(f32[1,32,512]{2,1,0:T(8,128)S(1)} %bitcast.10), channel_id=1, source_target_pairs={{28,25},{29,24}} | collective-permute-start | bytes 196616 | tf_op jit(solution)/shard_map/ppermute | solution.py:260
  6.9 0.7 %collective-permute-start.5 = (f32[32,512]{1,0:T(8,128)S(1)}, f32[32,512]{1,0:T(8,128)S(1)}, u32[]{:S(2)}, u32[]{:S(2)}) collective-permute-start(f32[32,512]{1,0:T(8,128)S(1)} %get-tuple-element.49.rest_3_), channel_id=1, source_target_pairs={{28,24},{29,25}} | collective-permute-start | bytes 196616 | tf_op jit(solution)/shard_map/ppermute | solution.py:341
  7.6 6.5 %collective-permute-done.3.rim = f32[1,544,128]{2,1,0:T(8,128)S(1)} collective-permute-done((f32[1,544,128]{2,1,0:T(8,128)S(1)}, f32[1,544,128]{2,1,0:T(8,128)S(1)}, u32[]{:S(2)}, u32[]{:S(2)}) %collective-permute-start.3) | collective-permute-done | bytes 278560 | tf_op jit(solution)/shard_map/ppermute | solution.py:260
  14.2 0.0 collective-permute-done.2.far
  14.2 1.6 %shard_map.49 = (bf16[2048,256]{1,0:T(8,128)(2,1)S(1)}, bf16[2048,256]{1,0:T(8,128)(2,1)S(1)}, f32[32,512]{1,0:T(8,128)S(1)}, bf16[1024,256]{1,0:T(8,128)(2,1)S(1)}, bf16[1024,256]{1,0:T(8,128)(2,1)S(1)}) custom-call(f32[1088,256]{1,0:T(8,128)S(1)} %collective-permute-done.2.far, f32[1,544,128]{2,1,0:T(8,128)S(1)} %collective-permute-done.3.rim, ...), custom_call_target="tpu_custom_call" | custom-call | tf_op jit(solution)/shard_map/pallas_call | solution.py:325
  15.8 0.0 collective-permute-done.4.rest_0_
  15.8 0.0 collective-permute-done.5.rest_1_
  15.8 0.7 %collective-permute-start.6 = (f32[1,32,512]{2,1,0:T(8,128)S(1)}, f32[1,32,512]{2,1,0:T(8,128)S(1)}, u32[]{:S(2)}, u32[]{:S(2)}) collective-permute-start(f32[1,32,512]{2,1,0:T(8,128)S(1)} %bitcast.11), channel_id=1, source_target_pairs={{24,21},{25,20}} | collective-permute-start | bytes 196616 | tf_op jit(solution)/shard_map/ppermute | solution.py:260
  16.5 0.7 %collective-permute-start.7 = (f32[32,512]{1,0:T(8,128)S(1)}, f32[32,512]{1,0:T(8,128)S(1)}, u32[]{:S(2)}, u32[]{:S(2)}) collective-permute-start(f32[32,512]{1,0:T(8,128)S(1)} %get-tuple-element.50.rest_3_), channel_id=1, source_target_pairs={{24,20},{25,21}} | collective-permute-start | bytes 196616 | tf_op jit(solution)/shard_map/ppermute | solution.py:341
  17.2 0.0 collective-permute-done.6.rest_0_
  17.2 0.0 collective-permute-done.7.rest_1_
  17.2 0.7 %collective-permute-start.8 = (f32[1,32,512]{2,1,0:T(8,128)S(1)}, f32[1,32,512]{2,1,0:T(8,128)S(1)}, u32[]{:S(2)}, u32[]{:S(2)}) collective-permute-start(f32[1,32,512]{2,1,0:T(8,128)S(1)} %bitcast.12), channel_id=1, source_target_pairs={{20,17},{21,16}} | collective-permute-start | bytes 196616 | tf_op jit(solution)/shard_map/ppermute | solution.py:260
  17.9 0.7 %collective-permute-start.9 = (f32[32,512]{1,0:T(8,128)S(1)}, f32[32,512]{1,0:T(8,128)S(1)}, u32[]{:S(2)}, u32[]{:S(2)}) collective-permute-start(f32[32,512]{1,0:T(8,128)S(1)} %get-tuple-element.52.rest_3_), channel_id=1, source_target_pairs={{20,16},{21,17}} | collective-permute-start | bytes 196616 | tf_op jit(solution)/shard_map/ppermute | solution.py:341
  18.6 0.0 collective-permute-done.8.rest_0_
  18.6 0.0 collective-permute-done.9.rest_1_
  18.6 0.7 %collective-permute-start.10 = (f32[1,32,512]{2,1,0:T(8,128)S(1)}, f32[1,32,512]{2,1,0:T(8,128)S(1)}, u32[]{:S(2)}, u32[]{:S(2)}) collective-permute-start(f32[1,32,512]{2,1,0:T(8,128)S(1)} %bitcast.13), channel_id=1, source_target_pairs={{16,13},{17,12}} | collective-permute-start | bytes 196616 | tf_op jit(solution)/shard_map/ppermute | solution.py:260
  19.3 0.7 %collective-permute-start.11 = (f32[32,512]{1,0:T(8,128)S(1)}, f32[32,512]{1,0:T(8,128)S(1)}, u32[]{:S(2)}, u32[]{:S(2)}) collective-permute-start(f32[32,512]{1,0:T(8,128)S(1)} %get-tuple-element.54.rest_3_), channel_id=1, source_target_pairs={{16,12},{17,13}} | collective-permute-start | bytes 196616 | tf_op jit(solution)/shard_map/ppermute | solution.py:341
  20.0 0.0 collective-permute-done.10.rest_0_
  20.0 0.0 collective-permute-done.11.rest_1_
  20.0 0.7 %collective-permute-start.12 = (f32[1,32,512]{2,1,0:T(8,128)S(1)}, f32[1,32,512]{2,1,0:T(8,128)S(1)}, u32[]{:S(2)}, u32[]{:S(2)}) collective-permute-start(f32[1,32,512]{2,1,0:T(8,128)S(1)} %bitcast.14), channel_id=1, source_target_pairs={{12,9},{13,8}} | collective-permute-start | bytes 196616 | tf_op jit(solution)/shard_map/ppermute | solution.py:260
  20.7 0.7 %collective-permute-start.13 = (f32[32,512]{1,0:T(8,128)S(1)}, f32[32,512]{1,0:T(8,128)S(1)}, u32[]{:S(2)}, u32[]{:S(2)}) collective-permute-start(f32[32,512]{1,0:T(8,128)S(1)} %get-tuple-element.56.rest_3_), channel_id=1, source_target_pairs={{12,8},{13,9}} | collective-permute-start | bytes 196616 | tf_op jit(solution)/shard_map/ppermute | solution.py:341
  21.4 0.0 collective-permute-done.12.rest_0_
  21.4 0.0 collective-permute-done.13.rest_1_
  21.4 0.7 %collective-permute-start.14 = (f32[1,32,512]{2,1,0:T(8,128)S(1)}, f32[1,32,512]{2,1,0:T(8,128)S(1)}, u32[]{:S(2)}, u32[]{:S(2)}) collective-permute-start(f32[1,32,512]{2,1,0:T(8,128)S(1)} %bitcast.15), channel_id=1, source_target_pairs={{8,5},{9,4}} | collective-permute-start | bytes 196616 | tf_op jit(solution)/shard_map/ppermute | solution.py:260
  22.1 0.7 %collective-permute-start.15 = (f32[32,512]{1,0:T(8,128)S(1)}, f32[32,512]{1,0:T(8,128)S(1)}, u32[]{:S(2)}, u32[]{:S(2)}) collective-permute-start(f32[32,512]{1,0:T(8,128)S(1)} %get-tuple-element.58.rest_3_), channel_id=1, source_target_pairs={{8,4},{9,5}} | collective-permute-start | bytes 196616 | tf_op jit(solution)/shard_map/ppermute | solution.py:341
  22.8 0.0 collective-permute-done.14.rest_0_
  22.8 0.0 collective-permute-done.15.rest_1_
  22.8 1.3 %collective-permute-start.16 = (f32[1,32,512]{2,1,0:T(8,128)S(1)}, f32[1,32,512]{2,1,0:T(8,128)S(1)}, u32[]{:S(2)}, u32[]{:S(2)}) collective-permute-start(f32[1,32,512]{2,1,0:T(8,128)S(1)} %bitcast.16), channel_id=1, source_target_pairs={{4,1},{5,0}} | collective-permute-start | bytes 196616 | tf_op jit(solution)/shard_map/ppermute | solution.py:260
  24.1 1.3 %collective-permute-start.17 = (f32[32,512]{1,0:T(8,128)S(1)}, f32[32,512]{1,0:T(8,128)S(1)}, u32[]{:S(2)}, u32[]{:S(2)}) collective-permute-start(f32[32,512]{1,0:T(8,128)S(1)} %get-tuple-element.60.rest_1_), channel_id=1, source_target_pairs={{4,0},{5,1}} | collective-permute-start | bytes 196616 | tf_op jit(solution)/shard_map/ppermute | solution.py:341
  25.4 32.7 %collective-permute-done.16.next_in = f32[1,32,512]{2,1,0:T(8,128)S(1)} collective-permute-done((f32[1,32,512]{2,1,0:T(8,128)S(1)}, f32[1,32,512]{2,1,0:T(8,128)S(1)}, u32[]{:S(2)}, u32[]{:S(2)}) %collective-permute-start.16) | collective-permute-done | bytes 65568 | tf_op jit(solution)/shard_map/ppermute | solution.py:260
  58.2 1.0 %collective-permute-done.17.own_in = f32[32,512]{1,0:T(8,128)S(1)} collective-permute-done((f32[32,512]{1,0:T(8,128)S(1)}, f32[32,512]{1,0:T(8,128)S(1)}, u32[]{:S(2)}, u32[]{:S(2)}) %collective-permute-start.17) | collective-permute-done | bytes 65568 | tf_op jit(solution)/shard_map/ppermute | solution.py:341
  59.1 0.3 shard_map.57
  59.4 1.3 %collective-permute-start.18 = (f32[32,512]{1,0:T(8,128)S(1)}, f32[32,512]{1,0:T(8,128)S(1)}, u32[]{:S(2)}, u32[]{:S(2)}) collective-permute-start(f32[32,512]{1,0:T(8,128)S(1)} %get-tuple-element.66), channel_id=1, source_target_pairs={{0,2},{1,3},{4,6},{5,7},{8,10},{9,11},{12,14},{13,15},{16,18},{17,... | collective-permute-start | bytes 196616 | tf_op jit(solution)/shard_map/ppermute | solution.py:359
  60.8 0.5 shard_map.58
  61.2 0.4 collective-permute-done.18
  61.6 0.6 %select_bitcast_fusion = f32[1,32,512]{2,1,0:T(8,128)} fusion(f32[32,512]{1,0:T(8,128)S(1)} %shard_map.58, f32[32,512]{1,0:T(8,128)S(1)} %collective-permute-done.18, pred[]{:T(512)S(6)} %eq.5), kind=kLoop, calls=%fused_computation | loop fusion | flops 16384 | bytes 196609 | tf_op jit(solution)/shard_map/broadcast_in_dim | solution.py:369
  (11 shorter events, 0.2 us)
Async XLA Ops:
  1.5 2.0 %collective-permute-start = (f32[1,32,512]{2,1,0:T(8,128)S(1)}, f32[1,32,512]{2,1,0:T(8,128)S(1)}, u32[]{:S(2)}, u32[]{:S(2)}) collective-permute-start(f32[1,32,512]{2,1,0:T(8,128)S(1)} %bitcast.17), channel_id=1, source_target_pairs={{30,29},{31,28}} | collective-permute-start | bytes 196616 | tf_op jit(solution)/shard_map/ppermute | solution.py:260
  2.2 1.4 %collective-permute-start.1 = (f32[32,512]{1,0:T(8,128)S(1)}, f32[32,512]{1,0:T(8,128)S(1)}, u32[]{:S(2)}, u32[]{:S(2)}) collective-permute-start(f32[32,512]{1,0:T(8,128)S(1)} %get-tuple-element.37.const), channel_id=1, source_target_pairs={{30,28},{31,29}} | collective-permute-start | bytes 196616 | tf_op jit(solution)/shard_map/ppermute | solution.py:291
  3.6 10.5 %collective-permute-start.2 = (f32[1088,256]{1,0:T(8,128)S(1)}, f32[1088,256]{1,0:T(8,128)S(1)}, u32[]{:S(2)}, u32[]{:S(2)}) collective-permute-start(f32[1088,256]{1,0:T(8,128)S(1)} %get-tuple-element.42), channel_id=1, source_target_pairs={{2,0},{3,1},{6,4},{7,5},{10,8},{11,9},{14,12},{15,13},{18,16},{19,... | collective-permute-start | bytes 3342344 | tf_op jit(solution)/shard_map/ppermute | solution.py:313
  4.9 9.2 %collective-permute-start.3 = (f32[1,544,128]{2,1,0:T(8,128)S(1)}, f32[1,544,128]{2,1,0:T(8,128)S(1)}, u32[]{:S(2)}, u32[]{:S(2)}) collective-permute-start(f32[1,544,128]{2,1,0:T(8,128)S(1)} %get-tuple-element.43), channel_id=1, source_target_pairs={{2,1},{3,0},{6,5},{7,4},{10,9},{11,8},{14,13},{15,12},{18,17},{19,... | collective-permute-start | bytes 835592 | tf_op jit(solution)/shard_map/ppermute | solution.py:260
  6.3 9.5 %collective-permute-start.4 = (f32[1,32,512]{2,1,0:T(8,128)S(1)}, f32[1,32,512]{2,1,0:T(8,128)S(1)}, u32[]{:S(2)}, u32[]{:S(2)}) collective-permute-start(f32[1,32,512]{2,1,0:T(8,128)S(1)} %bitcast.10), channel_id=1, source_target_pairs={{28,25},{29,24}} | collective-permute-start | bytes 196616 | tf_op jit(solution)/shard_map/ppermute | solution.py:260
  6.9 8.8 %collective-permute-start.5 = (f32[32,512]{1,0:T(8,128)S(1)}, f32[32,512]{1,0:T(8,128)S(1)}, u32[]{:S(2)}, u32[]{:S(2)}) collective-permute-start(f32[32,512]{1,0:T(8,128)S(1)} %get-tuple-element.49.rest_3_), channel_id=1, source_target_pairs={{28,24},{29,25}} | collective-permute-start | bytes 196616 | tf_op jit(solution)/shard_map/ppermute | solution.py:341
  15.8 1.3 %collective-permute-start.6 = (f32[1,32,512]{2,1,0:T(8,128)S(1)}, f32[1,32,512]{2,1,0:T(8,128)S(1)}, u32[]{:S(2)}, u32[]{:S(2)}) collective-permute-start(f32[1,32,512]{2,1,0:T(8,128)S(1)} %bitcast.11), channel_id=1, source_target_pairs={{24,21},{25,20}} | collective-permute-start | bytes 196616 | tf_op jit(solution)/shard_map/ppermute | solution.py:260
  16.5 0.7 %collective-permute-start.7 = (f32[32,512]{1,0:T(8,128)S(1)}, f32[32,512]{1,0:T(8,128)S(1)}, u32[]{:S(2)}, u32[]{:S(2)}) collective-permute-start(f32[32,512]{1,0:T(8,128)S(1)} %get-tuple-element.50.rest_3_), channel_id=1, source_target_pairs={{24,20},{25,21}} | collective-permute-start | bytes 196616 | tf_op jit(solution)/shard_map/ppermute | solution.py:341
  17.2 1.3 %collective-permute-start.8 = (f32[1,32,512]{2,1,0:T(8,128)S(1)}, f32[1,32,512]{2,1,0:T(8,128)S(1)}, u32[]{:S(2)}, u32[]{:S(2)}) collective-permute-start(f32[1,32,512]{2,1,0:T(8,128)S(1)} %bitcast.12), channel_id=1, source_target_pairs={{20,17},{21,16}} | collective-permute-start | bytes 196616 | tf_op jit(solution)/shard_map/ppermute | solution.py:260
  17.9 0.7 %collective-permute-start.9 = (f32[32,512]{1,0:T(8,128)S(1)}, f32[32,512]{1,0:T(8,128)S(1)}, u32[]{:S(2)}, u32[]{:S(2)}) collective-permute-start(f32[32,512]{1,0:T(8,128)S(1)} %get-tuple-element.52.rest_3_), channel_id=1, source_target_pairs={{20,16},{21,17}} | collective-permute-start | bytes 196616 | tf_op jit(solution)/shard_map/ppermute | solution.py:341
  18.6 1.3 %collective-permute-start.10 = (f32[1,32,512]{2,1,0:T(8,128)S(1)}, f32[1,32,512]{2,1,0:T(8,128)S(1)}, u32[]{:S(2)}, u32[]{:S(2)}) collective-permute-start(f32[1,32,512]{2,1,0:T(8,128)S(1)} %bitcast.13), channel_id=1, source_target_pairs={{16,13},{17,12}} | collective-permute-start | bytes 196616 | tf_op jit(solution)/shard_map/ppermute | solution.py:260
  19.3 0.7 %collective-permute-start.11 = (f32[32,512]{1,0:T(8,128)S(1)}, f32[32,512]{1,0:T(8,128)S(1)}, u32[]{:S(2)}, u32[]{:S(2)}) collective-permute-start(f32[32,512]{1,0:T(8,128)S(1)} %get-tuple-element.54.rest_3_), channel_id=1, source_target_pairs={{16,12},{17,13}} | collective-permute-start | bytes 196616 | tf_op jit(solution)/shard_map/ppermute | solution.py:341
  20.0 1.3 %collective-permute-start.12 = (f32[1,32,512]{2,1,0:T(8,128)S(1)}, f32[1,32,512]{2,1,0:T(8,128)S(1)}, u32[]{:S(2)}, u32[]{:S(2)}) collective-permute-start(f32[1,32,512]{2,1,0:T(8,128)S(1)} %bitcast.14), channel_id=1, source_target_pairs={{12,9},{13,8}} | collective-permute-start | bytes 196616 | tf_op jit(solution)/shard_map/ppermute | solution.py:260
  20.7 0.7 %collective-permute-start.13 = (f32[32,512]{1,0:T(8,128)S(1)}, f32[32,512]{1,0:T(8,128)S(1)}, u32[]{:S(2)}, u32[]{:S(2)}) collective-permute-start(f32[32,512]{1,0:T(8,128)S(1)} %get-tuple-element.56.rest_3_), channel_id=1, source_target_pairs={{12,8},{13,9}} | collective-permute-start | bytes 196616 | tf_op jit(solution)/shard_map/ppermute | solution.py:341
  21.4 1.3 %collective-permute-start.14 = (f32[1,32,512]{2,1,0:T(8,128)S(1)}, f32[1,32,512]{2,1,0:T(8,128)S(1)}, u32[]{:S(2)}, u32[]{:S(2)}) collective-permute-start(f32[1,32,512]{2,1,0:T(8,128)S(1)} %bitcast.15), channel_id=1, source_target_pairs={{8,5},{9,4}} | collective-permute-start | bytes 196616 | tf_op jit(solution)/shard_map/ppermute | solution.py:260
  22.1 0.7 %collective-permute-start.15 = (f32[32,512]{1,0:T(8,128)S(1)}, f32[32,512]{1,0:T(8,128)S(1)}, u32[]{:S(2)}, u32[]{:S(2)}) collective-permute-start(f32[32,512]{1,0:T(8,128)S(1)} %get-tuple-element.58.rest_3_), channel_id=1, source_target_pairs={{8,4},{9,5}} | collective-permute-start | bytes 196616 | tf_op jit(solution)/shard_map/ppermute | solution.py:341
  22.8 35.3 %collective-permute-start.16 = (f32[1,32,512]{2,1,0:T(8,128)S(1)}, f32[1,32,512]{2,1,0:T(8,128)S(1)}, u32[]{:S(2)}, u32[]{:S(2)}) collective-permute-start(f32[1,32,512]{2,1,0:T(8,128)S(1)} %bitcast.16), channel_id=1, source_target_pairs={{4,1},{5,0}} | collective-permute-start | bytes 196616 | tf_op jit(solution)/shard_map/ppermute | solution.py:260
  24.1 35.0 %collective-permute-start.17 = (f32[32,512]{1,0:T(8,128)S(1)}, f32[32,512]{1,0:T(8,128)S(1)}, u32[]{:S(2)}, u32[]{:S(2)}) collective-permute-start(f32[32,512]{1,0:T(8,128)S(1)} %get-tuple-element.60.rest_1_), channel_id=1, source_target_pairs={{4,0},{5,1}} | collective-permute-start | bytes 196616 | tf_op jit(solution)/shard_map/ppermute | solution.py:341
  59.4 2.2 %collective-permute-start.18 = (f32[32,512]{1,0:T(8,128)S(1)}, f32[32,512]{1,0:T(8,128)S(1)}, u32[]{:S(2)}, u32[]{:S(2)}) collective-permute-start(f32[32,512]{1,0:T(8,128)S(1)} %get-tuple-element.66), channel_id=1, source_target_pairs={{0,2},{1,3},{4,6},{5,7},{8,10},{9,11},{12,14},{13,15},{16,18},{17,... | collective-permute-start | bytes 196616 | tf_op jit(solution)/shard_map/ppermute | solution.py:359

commit v4 on v3

--- a/solution.py
+++ b/solution.py
@@ -90,7 +90,7 @@
             near_high[rows], near_low[rows] = halves(value)
 
 
-def edge_kernel(sides, blocks, cols, _own, _first_next, _first_far, own, rim):
+def edge_kernel(sides, blocks, cols, _own, own, rim):
     length, edge = own.shape[1], rim.shape[2]
     window = length + 2 * edge
 
@@ -103,7 +103,13 @@
     put_rim(sides, rim, columns)
 
 
-def pair_kernel(far, rim, near_high, near_low, const, high, low, both, far_high, far_low, total):
+def split_kernel(rim, far, far_high, far_low, rim_high, rim_low):
+    far_high[...], far_low[...] = halves(far[: far_high.shape[0]])
+    for side in range(rim.shape[0]):
+        rim_high[side], rim_low[side] = halves(rim[side, : rim_high.shape[1]])
+
+
+def pair_kernel(rim, far, far_high, far_low, near_high, near_low, const, high, low, both, total):
     cols, sites = const.shape
     length = far.shape[1]
     blocks = sites // length
@@ -111,7 +117,6 @@
     edge = (window - length) // 2
     span = 2 * window
     tall = blocks * window
-    far_high[...], far_low[...] = halves(far[:tall])
     if rim.shape[0] == 1:
         flag = jnp.minimum(lax.axis_index("row"), 1).astype(jnp.float32)
         left, right = rim[0] * flag, rim[0] * (1 - flag)
@@ -193,24 +198,54 @@
             lower[:, at] = const[:, at] - product
 
 
-def chain_kernel(mine, both, high, low, *rest):
-    sides, given = rest[0], rest[1:]
-    if sides:
-        next_in, own_in, _late, _lower, late, lower = given
-    else:
-        late, _lower, lower = given
-    sites = lower.shape[1]
-    blocks = sites // high.shape[1]
-    length, span = high.shape[1], high.shape[0] // blocks
-    halo = (late.shape[1] - sites) // 2
+def direct_kernel(
+    mine, sides, next_in, own_in, rim, far, far_high, far_low, rim_high, rim_low, near_high, near_low, const,
+    _late, _lower, late, lower, mid
+):
+    cols, sites = lower.shape
+    length = near_high.shape[1]
+    blocks = sites // length
+    window = near_high.shape[0] // blocks
+    edge = (window - length) // 2
+    halo = length + edge
 
     @pl.when(lax.axis_index("tm") == 2 * mine)
     def _():
-        if sides:
-            load(sides, next_in, own_in, halo, late)
+        load(sides, next_in, own_in, halo, late)
+        mid[...] = jnp.zeros_like(mid)
+        for side in range(sides):
+            on_right = 1 - jnp.minimum(lax.axis_index("row"), 1).astype(jnp.int32) if sides == 1 else side
+            start = pl.multiple_of(on_right * (2 * halo + sites - window), 128)
+            product = stacked_dot(late, pl.ds(start, window), rim_high[side], rim_low[side])
+            keep(mid, pl.multiple_of(on_right * (edge + sites), 128), rim[side, window:] - product)
         for b in range(blocks):
-            at, rows = slice(b * length, (b + 1) * length), slice(b * span, (b + 1) * span)
-            lower[:, at] = both[:, at] + stacked_dot(late, slice(b * length, b * length + span), high[rows], low[rows])
+            rows, start = slice(b * window, (b + 1) * window), halo - edge + b * length
+            at = blocks * window + b * cols
+            product = stacked_dot(late, slice(start, start + window), far_high[rows], far_low[rows])
+            keep(mid, edge + b * length, far[at : at + cols] - product)
+        for b in range(blocks):
+            at, rows = slice(b * length, (b + 1) * length), slice(b * window, (b + 1) * window)
+            product = stacked_dot(mid, slice(b * length, b * length + window), near_high[rows], near_low[rows])
+            lower[:, at] = const[:, at] - product
+
+
+def step(both, high, low, late, lower):
+    blocks = lower.shape[1] // high.shape[1]
+    length, span = high.shape[1], high.shape[0] // blocks
+    for b in range(blocks):
+        at, rows = slice(b * length, (b + 1) * length), slice(b * span, (b + 1) * span)
+        lower[:, at] = both[:, at] + stacked_dot(late, slice(b * length, b * length + span), high[rows], low[rows])
+
+
+def chain_kernel(mine, sides, next_in, own_in, both, high, low, _late, _lower, late, lower):
+    @pl.when(lax.axis_index("tm") == 2 * mine)
+    def _():
+        load(sides, next_in, own_in, (late.shape[1] - own_in.shape[1]) // 2, late)
+        step(both, high, low, late, lower)
+
+
+def last_kernel(both, high, low, late, _lower, lower):
+    pl.when(lax.axis_index("tm") == 0)(lambda: step(both, high, low, late, lower))
 
 
 def upper_kernel(
@@ -304,11 +339,11 @@
     near, edges = pl.pallas_call(
         functools.partial(edge_kernel, sides, blocks, cols),
         out_shape=(shape(near.shape, f32), shape((sides, window + cols, edge), f32)),
-        in_specs=[VMEM] * 3,
+        in_specs=[VMEM],
         out_specs=(VMEM,) * 2,
         input_output_aliases={0: 0},
         compiler_params=PARAMS,
-    )(near, first_next, first_own)
+    )(near)
     rim = cross(edges, odd[:-1], even[:-1])
     far = lax.ppermute(near, BOTH, link(odd[:-1], even[:-1]))
 
@@ -321,33 +356,54 @@
         scratch_shapes=[pltpu.VMEM((2 * cols, sites + 2 * edge), bf16)],
         input_output_aliases={5: 0, 6: 1},
         compiler_params=PARAMS,
+        cost_estimate=pl.CostEstimate(flops=50 * 10**9, bytes_accessed=0, transcendentals=0),
     )(first_next, first_own, const, near_high, near_low, blank, blank)
-    high, low, both, far_high, far_low = pl.pallas_call(
+    far_high, far_low, rim_high, rim_low = pl.pallas_call(
+        split_kernel,
+        out_shape=(
+            shape((tall, length), bf16), shape((tall, length), bf16),
+            shape((sides, window, edge), bf16), shape((sides, window, edge), bf16),
+        ),
+        in_specs=[VMEM] * 2,
+        out_specs=(VMEM,) * 4,
+        compiler_params=PARAMS,
+    )(rim, far)
+    high, low, both = pl.pallas_call(
         pair_kernel,
         out_shape=(
             shape((2 * tall, length), bf16), shape((2 * tall, length), bf16), shape((cols, sites), f32),
-            shape((tall, length), bf16), shape((tall, length), bf16),
         ),
-        in_specs=[VMEM] * 5,
-        out_specs=(VMEM,) * 5,
+        in_specs=[VMEM] * 7,
+        out_specs=(VMEM,) * 3,
         scratch_shapes=[pltpu.VMEM((2 * window, length), f32)],
         compiler_params=PARAMS,
-    )(far, rim, near_high, near_low, const)
+        cost_estimate=pl.CostEstimate(flops=10**9, bytes_accessed=0, transcendentals=0),
+    )(rim, far, far_high, far_low, near_high, near_low, const)
 
     late = jnp.zeros((2 * cols, sites + 2 * halo), bf16)
     for mine in range(pairs - 1, 0, -1):
         source, target = [2 * mine], [2 * mine - 2]
         next_in = cross(lower[None], source, target)
         own_in = lax.ppermute(lower, BOTH, link(source, target))
-        if mine > 1:
-            late, lower = pl.pallas_call(
-                lambda both, high, low, *rest, mine=mine: chain_kernel(mine - 1, both, high, low, sides, *rest),
-                out_shape=(shape(late.shape, bf16), shape(lower.shape, f32)),
-                in_specs=[VMEM] * 7,
-                out_specs=(VMEM,) * 2,
-                input_output_aliases={5: 0, 6: 1},
-                compiler_params=PARAMS,
-            )(both, high, low, next_in, own_in, late, lower)
+        if mine == 1:
+            break
+        if mine == pairs - 1:
+            kernel, given = functools.partial(direct_kernel, mine - 1, sides), (
+                next_in, own_in, rim, far, far_high, far_low, rim_high, rim_low, near_high, near_low, const
+            )
+            scratch = [pltpu.VMEM((2 * cols, sites + 2 * edge), bf16)]
+        else:
+            kernel, given = functools.partial(chain_kernel, mine - 1, sides), (next_in, own_in, both, high, low)
+            scratch = []
+        late, lower = pl.pallas_call(
+            kernel,
+            out_shape=(shape(late.shape, bf16), shape(lower.shape, f32)),
+            in_specs=[VMEM] * (len(given) + 2),
+            out_specs=(VMEM,) * 2,
+            scratch_shapes=scratch,
+            input_output_aliases={len(given): 0, len(given) + 1: 1},
+            compiler_params=PARAMS,
+        )(*given, late, lower)
     late, upper = pl.pallas_call(
         functools.partial(upper_kernel, sides, pairs - 1),
         out_shape=(shape(late.shape, bf16), shape(upper.shape, f32)),
@@ -358,7 +414,7 @@
     )(next_in, own_in, far, far_high, far_low, late, upper)
     returned = lax.ppermute(upper, BOTH, link(even, odd))
     lower = pl.pallas_call(
-        lambda both, high, low, *rest: chain_kernel(0, both, high, low, 0, *rest),
+        last_kernel,
         out_shape=shape(lower.shape, f32),
         in_specs=[VMEM] * 5,
         out_specs=VMEM,

time: 62.6 us -> 61.5 us (0.982)
  waiting for transfers between devices: 40.7 us -> 39.4 us
    ppermute x9, waiting for transfers between devices: 39.3 us -> 38.3 us  [cross(): return lax.ppermute(value, BOTH, perm)]
  transfers between devices with their start and end apart: 19 -> 19, of which waited for: 4 -> 4; matrix products, arithmetic and copies ran while one was open for 0% -> 0% of each run, Pallas kernels for 4% -> 5%
where the time goes in v4:
time: 61.5 us; the launch traced here: 61.1 us
  waiting for transfers between devices  39.4 us (64%)
  starting transfers between devices  15.8 us (26%)
  Pallas kernels  4.89 us (8%)
  other arithmetic  0.64 us (1%)
    ppermute x9, waiting for transfers between devices, cross(): return lax.ppermute(value, BOTH, perm)  38.3 us
    ppermute x9, starting transfers between devices, cross(): return lax.ppermute(value, BOTH, perm)  7.24 us
    ppermute x7, starting transfers between devices, local(): own_in = lax.ppermute(lower, BOTH, link(source, target))  5.28 us
    pallas_call x1, Pallas kernels, local(): pl.pallas_call(pair_kernel, out_shape=(shape((2 * tall, length), bf16), s...  1.59 us
    pallas_call x1, Pallas kernels, local(): pl.pallas_call(const_kernel, out_shape=(shape((cols, sites), f32), shape(...  1.51 us
    ppermute x1, starting transfers between devices, local(): far = lax.ppermute(near, BOTH, link(odd[:-1], even[:-1]))  1.29 us
    ppermute x1, starting transfers between devices, local(): returned = lax.ppermute(upper, BOTH, link(even, odd))  1.29 us
  transfers between devices with their start and end apart: 19, of which 4 were waited for; matrix products, arithmetic and copies ran while one was open for 0% of the time, Pallas kernels for 5%

profile of v4, /device:TPU:0, one launch (start us, length us, event | category | flops | bytes accessed | tf_op | source)
XLA Modules:
  0.0 61.1 jit_solution(7455199724335481635)
XLA Ops:
  0.0 1.5 %shard_map.46 = (f32[32,512]{1,0:T(8,128)S(1)}, bf16[2,256,256]{2,1,0:T(8,128)(2,1)S(1)}, bf16[2,256,256]{2,1,0:T(8,128)(2,1)S(1)}, f32[2,512,256]{2,1,0:T(8,128)S(1)}, s32[2,3]{1,0:T(2,128)S(1)}) custom-call(s32[1,2,3]{2,1,0:T(2,128)} %mask.1, f32[1,32,512]{2,1,0:T(8,128)} %normals.1, f32[1,2,256,256]{3,2,1,0:T(8,128)} %inv.1, f32[1,2,512,256]{3,2,1,0:T(8,128)} %lag.1), custom_call_target="tpu_custom_call" | custom-call | tf_op jit(solution)/shard_map/pallas_call | solution.py:308
  1.5 0.7 %collective-permute-start.2 = (f32[1,32,512]{2,1,0:T(8,128)S(1)}, f32[1,32,512]{2,1,0:T(8,128)S(1)}, u32[]{:S(2)}, u32[]{:S(2)}) collective-permute-start(f32[1,32,512]{2,1,0:T(8,128)S(1)} %bitcast.17), channel_id=1, source_target_pairs={{30,29},{31,28}} | collective-permute-start | bytes 196616 | tf_op jit(solution)/shard_map/ppermute | solution.py:295
  2.2 0.7 %collective-permute-start.3 = (f32[32,512]{1,0:T(8,128)S(1)}, f32[32,512]{1,0:T(8,128)S(1)}, u32[]{:S(2)}, u32[]{:S(2)}) collective-permute-start(f32[32,512]{1,0:T(8,128)S(1)} %get-tuple-element.39.const), channel_id=1, source_target_pairs={{30,28},{31,29}} | collective-permute-start | bytes 196616 | tf_op jit(solution)/shard_map/ppermute | solution.py:326
  2.9 0.7 %shard_map.47 = (f32[1088,256]{1,0:T(8,128)S(1)}, bf16[1024,256]{1,0:T(8,128)(2,1)S(1)}, bf16[1024,256]{1,0:T(8,128)(2,1)S(1)}) custom-call(s32[2,3]{1,0:T(2,128)S(1)} %get-tuple-element.38.mask, f32[32,512]{1,0:T(8,128)S(1)} %get-tuple-element.39.const, bf16[2,256,256]{2,1,0:T(8,128)(2,1)S(1)} %get-tuple-element.40.inv_high, ...), custom_call_target="tpu_custom_call" | custom-call | flops 427819008 | bytes 4194304 | tf_op jit(solution)/shard_map/pallas_call | solution.py:327
  3.6 1.3 %collective-permute-start.1 = (f32[1088,256]{1,0:T(8,128)S(1)}, f32[1088,256]{1,0:T(8,128)S(1)}, u32[]{:S(2)}, u32[]{:S(2)}) collective-permute-start(f32[1088,256]{1,0:T(8,128)S(1)} %get-tuple-element.45), channel_id=1, source_target_pairs={{2,0},{3,1},{6,4},{7,5},{10,8},{11,9},{14,12},{15,13},{18,16},{19,... | collective-permute-start | bytes 3342344 | tf_op jit(solution)/shard_map/ppermute | solution.py:348
  4.9 1.3 %collective-permute-start = (f32[1,544,128]{2,1,0:T(8,128)S(1)}, f32[1,544,128]{2,1,0:T(8,128)S(1)}, u32[]{:S(2)}, u32[]{:S(2)}) collective-permute-start(f32[1,544,128]{2,1,0:T(8,128)S(1)} %get-tuple-element.44), channel_id=1, source_target_pairs={{2,1},{3,0},{6,5},{7,4},{10,9},{11,8},{14,13},{15,12},{18,17},{19,... | collective-permute-start | bytes 835592 | tf_op jit(solution)/shard_map/ppermute | solution.py:295
  6.2 0.0 collective-permute-done.2.next_in
  6.2 0.0 collective-permute-done.3.own_in
  6.3 0.7 %collective-permute-start.4 = (f32[1,32,512]{2,1,0:T(8,128)S(1)}, f32[1,32,512]{2,1,0:T(8,128)S(1)}, u32[]{:S(2)}, u32[]{:S(2)}) collective-permute-start(f32[1,32,512]{2,1,0:T(8,128)S(1)} %bitcast.10), channel_id=1, source_target_pairs={{28,25},{29,24}} | collective-permute-start | bytes 196616 | tf_op jit(solution)/shard_map/ppermute | solution.py:295
  6.9 0.7 %collective-permute-start.5 = (f32[32,512]{1,0:T(8,128)S(1)}, f32[32,512]{1,0:T(8,128)S(1)}, u32[]{:S(2)}, u32[]{:S(2)}) collective-permute-start(f32[32,512]{1,0:T(8,128)S(1)} %get-tuple-element.53._lower), channel_id=1, source_target_pairs={{28,24},{29,25}} | collective-permute-start | bytes 196616 | tf_op jit(solution)/shard_map/ppermute | solution.py:387
  7.6 6.5 %collective-permute-done.rim = f32[1,544,128]{2,1,0:T(8,128)S(1)} collective-permute-done((f32[1,544,128]{2,1,0:T(8,128)S(1)}, f32[1,544,128]{2,1,0:T(8,128)S(1)}, u32[]{:S(2)}, u32[]{:S(2)}) %collective-permute-start) | collective-permute-done | bytes 278560 | tf_op jit(solution)/shard_map/ppermute | solution.py:295
  14.1 0.0 collective-permute-done.1.far
  14.1 0.2 shard_map.49
  14.3 0.0 collective-permute-done.4.next_in
  14.3 0.0 collective-permute-done.5.own_in
  14.4 0.7 %collective-permute-start.7 = (f32[32,512]{1,0:T(8,128)S(1)}, f32[32,512]{1,0:T(8,128)S(1)}, u32[]{:S(2)}, u32[]{:S(2)}) collective-permute-start(f32[32,512]{1,0:T(8,128)S(1)} %get-tuple-element.56._lower), channel_id=1, source_target_pairs={{24,20},{25,21}} | collective-permute-start | bytes 196616 | tf_op jit(solution)/shard_map/ppermute | solution.py:387
  15.1 0.7 %collective-permute-start.6 = (f32[1,32,512]{2,1,0:T(8,128)S(1)}, f32[1,32,512]{2,1,0:T(8,128)S(1)}, u32[]{:S(2)}, u32[]{:S(2)}) collective-permute-start(f32[1,32,512]{2,1,0:T(8,128)S(1)} %bitcast.11), channel_id=1, source_target_pairs={{24,21},{25,20}} | collective-permute-start | bytes 196616 | tf_op jit(solution)/shard_map/ppermute | solution.py:295
  15.7 1.6 %shard_map.50 = (bf16[2048,256]{1,0:T(8,128)(2,1)S(1)}, bf16[2048,256]{1,0:T(8,128)(2,1)S(1)}, f32[32,512]{1,0:T(8,128)S(1)}) custom-call(f32[1,544,128]{2,1,0:T(8,128)S(1)} %collective-permute-done.rim, f32[1088,256]{1,0:T(8,128)S(1)} %collective-permute-done.1.far, bf16[1024,256]{1,0:T(8,128)(2,1)S(1)} %get-tuple-element.46.far_high, ...), custom_call_target="tpu_custom_call" | custom-call | flops 1000000000 | tf_op jit(solution)/shard_map/pallas_call | solution.py:371
  17.3 0.0 collective-permute-done.6.next_in
  17.3 0.0 collective-permute-done.7.own_in
  17.4 0.7 %collective-permute-start.8 = (f32[1,32,512]{2,1,0:T(8,128)S(1)}, f32[1,32,512]{2,1,0:T(8,128)S(1)}, u32[]{:S(2)}, u32[]{:S(2)}) collective-permute-start(f32[1,32,512]{2,1,0:T(8,128)S(1)} %bitcast.12), channel_id=1, source_target_pairs={{20,17},{21,16}} | collective-permute-start | bytes 196616 | tf_op jit(solution)/shard_map/ppermute | solution.py:295
  18.1 0.7 %collective-permute-start.9 = (f32[32,512]{1,0:T(8,128)S(1)}, f32[32,512]{1,0:T(8,128)S(1)}, u32[]{:S(2)}, u32[]{:S(2)}) collective-permute-start(f32[32,512]{1,0:T(8,128)S(1)} %get-tuple-element.58._lower), channel_id=1, source_target_pairs={{20,16},{21,17}} | collective-permute-start | bytes 196616 | tf_op jit(solution)/shard_map/ppermute | solution.py:387
  18.7 0.0 collective-permute-done.8.next_in
  18.7 0.0 collective-permute-done.9.own_in
  18.8 0.7 %collective-permute-start.10 = (f32[1,32,512]{2,1,0:T(8,128)S(1)}, f32[1,32,512]{2,1,0:T(8,128)S(1)}, u32[]{:S(2)}, u32[]{:S(2)}) collective-permute-start(f32[1,32,512]{2,1,0:T(8,128)S(1)} %bitcast.13), channel_id=1, source_target_pairs={{16,13},{17,12}} | collective-permute-start | bytes 196616 | tf_op jit(solution)/shard_map/ppermute | solution.py:295
  19.4 0.7 %collective-permute-start.11 = (f32[32,512]{1,0:T(8,128)S(1)}, f32[32,512]{1,0:T(8,128)S(1)}, u32[]{:S(2)}, u32[]{:S(2)}) collective-permute-start(f32[32,512]{1,0:T(8,128)S(1)} %get-tuple-element.60._lower), channel_id=1, source_target_pairs={{16,12},{17,13}} | collective-permute-start | bytes 196616 | tf_op jit(solution)/shard_map/ppermute | solution.py:387
  20.1 0.0 collective-permute-done.10.next_in
  20.1 0.0 collective-permute-done.11.own_in
  20.2 0.7 %collective-permute-start.12 = (f32[1,32,512]{2,1,0:T(8,128)S(1)}, f32[1,32,512]{2,1,0:T(8,128)S(1)}, u32[]{:S(2)}, u32[]{:S(2)}) collective-permute-start(f32[1,32,512]{2,1,0:T(8,128)S(1)} %bitcast.14), channel_id=1, source_target_pairs={{12,9},{13,8}} | collective-permute-start | bytes 196616 | tf_op jit(solution)/shard_map/ppermute | solution.py:295
  20.8 0.7 %collective-permute-start.13 = (f32[32,512]{1,0:T(8,128)S(1)}, f32[32,512]{1,0:T(8,128)S(1)}, u32[]{:S(2)}, u32[]{:S(2)}) collective-permute-start(f32[32,512]{1,0:T(8,128)S(1)} %get-tuple-element.62._lower), channel_id=1, source_target_pairs={{12,8},{13,9}} | collective-permute-start | bytes 196616 | tf_op jit(solution)/shard_map/ppermute | solution.py:387
  21.5 0.0 collective-permute-done.12.next_in
  21.5 0.0 collective-permute-done.13.own_in
  21.6 0.7 %collective-permute-start.14 = (f32[1,32,512]{2,1,0:T(8,128)S(1)}, f32[1,32,512]{2,1,0:T(8,128)S(1)}, u32[]{:S(2)}, u32[]{:S(2)}) collective-permute-start(f32[1,32,512]{2,1,0:T(8,128)S(1)} %bitcast.15), channel_id=1, source_target_pairs={{8,5},{9,4}} | collective-permute-start | bytes 196616 | tf_op jit(solution)/shard_map/ppermute | solution.py:295
  22.2 0.7 %collective-permute-start.15 = (f32[32,512]{1,0:T(8,128)S(1)}, f32[32,512]{1,0:T(8,128)S(1)}, u32[]{:S(2)}, u32[]{:S(2)}) collective-permute-start(f32[32,512]{1,0:T(8,128)S(1)} %get-tuple-element.64._lower), channel_id=1, source_target_pairs={{8,4},{9,5}} | collective-permute-start | bytes 196616 | tf_op jit(solution)/shard_map/ppermute | solution.py:387
  22.9 0.0 collective-permute-done.14.next_in
  22.9 0.0 collective-permute-done.15.own_in
  22.9 1.3 %collective-permute-start.16 = (f32[1,32,512]{2,1,0:T(8,128)S(1)}, f32[1,32,512]{2,1,0:T(8,128)S(1)}, u32[]{:S(2)}, u32[]{:S(2)}) collective-permute-start(f32[1,32,512]{2,1,0:T(8,128)S(1)} %bitcast.16), channel_id=1, source_target_pairs={{4,1},{5,0}} | collective-permute-start | bytes 196616 | tf_op jit(solution)/shard_map/ppermute | solution.py:295
  24.2 1.3 %collective-permute-start.17 = (f32[32,512]{1,0:T(8,128)S(1)}, f32[32,512]{1,0:T(8,128)S(1)}, u32[]{:S(2)}, u32[]{:S(2)}) collective-permute-start(f32[32,512]{1,0:T(8,128)S(1)} %get-tuple-element.66._lower), channel_id=1, source_target_pairs={{4,0},{5,1}} | collective-permute-start | bytes 196616 | tf_op jit(solution)/shard_map/ppermute | solution.py:387
  25.6 31.8 %collective-permute-done.16.next_in = f32[1,32,512]{2,1,0:T(8,128)S(1)} collective-permute-done((f32[1,32,512]{2,1,0:T(8,128)S(1)}, f32[1,32,512]{2,1,0:T(8,128)S(1)}, u32[]{:S(2)}, u32[]{:S(2)}) %collective-permute-start.16) | collective-permute-done | bytes 65568 | tf_op jit(solution)/shard_map/ppermute | solution.py:295
  57.3 0.7 %collective-permute-done.17.own_in = f32[32,512]{1,0:T(8,128)S(1)} collective-permute-done((f32[32,512]{1,0:T(8,128)S(1)}, f32[32,512]{1,0:T(8,128)S(1)}, u32[]{:S(2)}, u32[]{:S(2)}) %collective-permute-start.17) | collective-permute-done | bytes 65568 | tf_op jit(solution)/shard_map/ppermute | solution.py:387
  58.0 0.3 shard_map.58
  58.3 1.3 %collective-permute-start.18 = (f32[32,512]{1,0:T(8,128)S(1)}, f32[32,512]{1,0:T(8,128)S(1)}, u32[]{:S(2)}, u32[]{:S(2)}) collective-permute-start(f32[32,512]{1,0:T(8,128)S(1)} %get-tuple-element.70), channel_id=1, source_target_pairs={{0,2},{1,3},{4,6},{5,7},{8,10},{9,11},{12,14},{13,15},{16,18},{17,... | collective-permute-start | bytes 196616 | tf_op jit(solution)/shard_map/ppermute | solution.py:415
  59.6 0.5 shard_map.59
  60.1 0.4 collective-permute-done.18
  60.5 0.6 %select_bitcast_fusion = f32[1,32,512]{2,1,0:T(8,128)} fusion(f32[32,512]{1,0:T(8,128)S(1)} %shard_map.59, f32[32,512]{1,0:T(8,128)S(1)} %collective-permute-done.18, pred[]{:T(512)S(6)} %eq.5), kind=kLoop, calls=%fused_computation | loop fusion | flops 16384 | bytes 196609 | tf_op jit(solution)/shard_map/broadcast_in_dim | solution.py:425
  (11 shorter events, 0.2 us)
Async XLA Ops:
  1.5 4.7 %collective-permute-start.2 = (f32[1,32,512]{2,1,0:T(8,128)S(1)}, f32[1,32,512]{2,1,0:T(8,128)S(1)}, u32[]{:S(2)}, u32[]{:S(2)}) collective-permute-start(f32[1,32,512]{2,1,0:T(8,128)S(1)} %bitcast.17), channel_id=1, source_target_pairs={{30,29},{31,28}} | collective-permute-start | bytes 196616 | tf_op jit(solution)/shard_map/ppermute | solution.py:295
  2.2 4.0 %collective-permute-start.3 = (f32[32,512]{1,0:T(8,128)S(1)}, f32[32,512]{1,0:T(8,128)S(1)}, u32[]{:S(2)}, u32[]{:S(2)}) collective-permute-start(f32[32,512]{1,0:T(8,128)S(1)} %get-tuple-element.39.const), channel_id=1, source_target_pairs={{30,28},{31,29}} | collective-permute-start | bytes 196616 | tf_op jit(solution)/shard_map/ppermute | solution.py:326
  3.6 10.5 %collective-permute-start.1 = (f32[1088,256]{1,0:T(8,128)S(1)}, f32[1088,256]{1,0:T(8,128)S(1)}, u32[]{:S(2)}, u32[]{:S(2)}) collective-permute-start(f32[1088,256]{1,0:T(8,128)S(1)} %get-tuple-element.45), channel_id=1, source_target_pairs={{2,0},{3,1},{6,4},{7,5},{10,8},{11,9},{14,12},{15,13},{18,16},{19,... | collective-permute-start | bytes 3342344 | tf_op jit(solution)/shard_map/ppermute | solution.py:348
  4.9 9.2 %collective-permute-start = (f32[1,544,128]{2,1,0:T(8,128)S(1)}, f32[1,544,128]{2,1,0:T(8,128)S(1)}, u32[]{:S(2)}, u32[]{:S(2)}) collective-permute-start(f32[1,544,128]{2,1,0:T(8,128)S(1)} %get-tuple-element.44), channel_id=1, source_target_pairs={{2,1},{3,0},{6,5},{7,4},{10,9},{11,8},{14,13},{15,12},{18,17},{19,... | collective-permute-start | bytes 835592 | tf_op jit(solution)/shard_map/ppermute | solution.py:295
  6.3 8.1 %collective-permute-start.4 = (f32[1,32,512]{2,1,0:T(8,128)S(1)}, f32[1,32,512]{2,1,0:T(8,128)S(1)}, u32[]{:S(2)}, u32[]{:S(2)}) collective-permute-start(f32[1,32,512]{2,1,0:T(8,128)S(1)} %bitcast.10), channel_id=1, source_target_pairs={{28,25},{29,24}} | collective-permute-start | bytes 196616 | tf_op jit(solution)/shard_map/ppermute | solution.py:295
  6.9 7.4 %collective-permute-start.5 = (f32[32,512]{1,0:T(8,128)S(1)}, f32[32,512]{1,0:T(8,128)S(1)}, u32[]{:S(2)}, u32[]{:S(2)}) collective-permute-start(f32[32,512]{1,0:T(8,128)S(1)} %get-tuple-element.53._lower), channel_id=1, source_target_pairs={{28,24},{29,25}} | collective-permute-start | bytes 196616 | tf_op jit(solution)/shard_map/ppermute | solution.py:387
  14.4 3.0 %collective-permute-start.7 = (f32[32,512]{1,0:T(8,128)S(1)}, f32[32,512]{1,0:T(8,128)S(1)}, u32[]{:S(2)}, u32[]{:S(2)}) collective-permute-start(f32[32,512]{1,0:T(8,128)S(1)} %get-tuple-element.56._lower), channel_id=1, source_target_pairs={{24,20},{25,21}} | collective-permute-start | bytes 196616 | tf_op jit(solution)/shard_map/ppermute | solution.py:387
  15.1 2.3 %collective-permute-start.6 = (f32[1,32,512]{2,1,0:T(8,128)S(1)}, f32[1,32,512]{2,1,0:T(8,128)S(1)}, u32[]{:S(2)}, u32[]{:S(2)}) collective-permute-start(f32[1,32,512]{2,1,0:T(8,128)S(1)} %bitcast.11), channel_id=1, source_target_pairs={{24,21},{25,20}} | collective-permute-start | bytes 196616 | tf_op jit(solution)/shard_map/ppermute | solution.py:295
  17.4 1.3 %collective-permute-start.8 = (f32[1,32,512]{2,1,0:T(8,128)S(1)}, f32[1,32,512]{2,1,0:T(8,128)S(1)}, u32[]{:S(2)}, u32[]{:S(2)}) collective-permute-start(f32[1,32,512]{2,1,0:T(8,128)S(1)} %bitcast.12), channel_id=1, source_target_pairs={{20,17},{21,16}} | collective-permute-start | bytes 196616 | tf_op jit(solution)/shard_map/ppermute | solution.py:295
  18.1 0.7 %collective-permute-start.9 = (f32[32,512]{1,0:T(8,128)S(1)}, f32[32,512]{1,0:T(8,128)S(1)}, u32[]{:S(2)}, u32[]{:S(2)}) collective-permute-start(f32[32,512]{1,0:T(8,128)S(1)} %get-tuple-element.58._lower), channel_id=1, source_target_pairs={{20,16},{21,17}} | collective-permute-start | bytes 196616 | tf_op jit(solution)/shard_map/ppermute | solution.py:387
  18.8 1.3 %collective-permute-start.10 = (f32[1,32,512]{2,1,0:T(8,128)S(1)}, f32[1,32,512]{2,1,0:T(8,128)S(1)}, u32[]{:S(2)}, u32[]{:S(2)}) collective-permute-start(f32[1,32,512]{2,1,0:T(8,128)S(1)} %bitcast.13), channel_id=1, source_target_pairs={{16,13},{17,12}} | collective-permute-start | bytes 196616 | tf_op jit(solution)/shard_map/ppermute | solution.py:295
  19.4 0.7 %collective-permute-start.11 = (f32[32,512]{1,0:T(8,128)S(1)}, f32[32,512]{1,0:T(8,128)S(1)}, u32[]{:S(2)}, u32[]{:S(2)}) collective-permute-start(f32[32,512]{1,0:T(8,128)S(1)} %get-tuple-element.60._lower), channel_id=1, source_target_pairs={{16,12},{17,13}} | collective-permute-start | bytes 196616 | tf_op jit(solution)/shard_map/ppermute | solution.py:387
  20.2 1.3 %collective-permute-start.12 = (f32[1,32,512]{2,1,0:T(8,128)S(1)}, f32[1,32,512]{2,1,0:T(8,128)S(1)}, u32[]{:S(2)}, u32[]{:S(2)}) collective-permute-start(f32[1,32,512]{2,1,0:T(8,128)S(1)} %bitcast.14), channel_id=1, source_target_pairs={{12,9},{13,8}} | collective-permute-start | bytes 196616 | tf_op jit(solution)/shard_map/ppermute | solution.py:295
  20.8 0.7 %collective-permute-start.13 = (f32[32,512]{1,0:T(8,128)S(1)}, f32[32,512]{1,0:T(8,128)S(1)}, u32[]{:S(2)}, u32[]{:S(2)}) collective-permute-start(f32[32,512]{1,0:T(8,128)S(1)} %get-tuple-element.62._lower), channel_id=1, source_target_pairs={{12,8},{13,9}} | collective-permute-start | bytes 196616 | tf_op jit(solution)/shard_map/ppermute | solution.py:387
  21.6 1.3 %collective-permute-start.14 = (f32[1,32,512]{2,1,0:T(8,128)S(1)}, f32[1,32,512]{2,1,0:T(8,128)S(1)}, u32[]{:S(2)}, u32[]{:S(2)}) collective-permute-start(f32[1,32,512]{2,1,0:T(8,128)S(1)} %bitcast.15), channel_id=1, source_target_pairs={{8,5},{9,4}} | collective-permute-start | bytes 196616 | tf_op jit(solution)/shard_map/ppermute | solution.py:295
  22.2 0.7 %collective-permute-start.15 = (f32[32,512]{1,0:T(8,128)S(1)}, f32[32,512]{1,0:T(8,128)S(1)}, u32[]{:S(2)}, u32[]{:S(2)}) collective-permute-start(f32[32,512]{1,0:T(8,128)S(1)} %get-tuple-element.64._lower), channel_id=1, source_target_pairs={{8,4},{9,5}} | collective-permute-start | bytes 196616 | tf_op jit(solution)/shard_map/ppermute | solution.py:387
  22.9 34.4 %collective-permute-start.16 = (f32[1,32,512]{2,1,0:T(8,128)S(1)}, f32[1,32,512]{2,1,0:T(8,128)S(1)}, u32[]{:S(2)}, u32[]{:S(2)}) collective-permute-start(f32[1,32,512]{2,1,0:T(8,128)S(1)} %bitcast.16), channel_id=1, source_target_pairs={{4,1},{5,0}} | collective-permute-start | bytes 196616 | tf_op jit(solution)/shard_map/ppermute | solution.py:295
  24.2 33.8 %collective-permute-start.17 = (f32[32,512]{1,0:T(8,128)S(1)}, f32[32,512]{1,0:T(8,128)S(1)}, u32[]{:S(2)}, u32[]{:S(2)}) collective-permute-start(f32[32,512]{1,0:T(8,128)S(1)} %get-tuple-element.66._lower), channel_id=1, source_target_pairs={{4,0},{5,1}} | collective-permute-start | bytes 196616 | tf_op jit(solution)/shard_map/ppermute | solution.py:387
  58.3 2.2 %collective-permute-start.18 = (f32[32,512]{1,0:T(8,128)S(1)}, f32[32,512]{1,0:T(8,128)S(1)}, u32[]{:S(2)}, u32[]{:S(2)}) collective-permute-start(f32[32,512]{1,0:T(8,128)S(1)} %get-tuple-element.70), channel_id=1, source_target_pairs={{0,2},{1,3},{4,6},{5,7},{8,10},{9,11},{12,14},{13,15},{16,18},{17,... | collective-permute-start | bytes 196616 | tf_op jit(solution)/shard_map/ppermute | solution.py:415

commit v5 on v4

--- a/solution.py
+++ b/solution.py
@@ -109,7 +109,27 @@
         rim_high[side], rim_low[side] = halves(rim[side, : rim_high.shape[1]])
 
 
-def pair_kernel(rim, far, far_high, far_low, near_high, near_low, const, high, low, both, total):
+def cuts_of(blocks, length, sites, span, last):
+    packed, cuts = 0, []
+    for b in range(blocks):
+        start = span // 2 - length // 2 - b * length
+        lo, hi = (start + sites, span) if last else (0, start)
+        cuts.append((lo, hi, packed))
+        packed += hi - lo
+    return cuts
+
+
+def put_rows(b, start, sites, span, other_rows, total):
+    length = total.shape[1]
+    for last in (True, False):
+        lo, hi, packed = cuts_of(sites // length, length, sites, span, last)[b]
+
+        @pl.when((lax.axis_index("row") == 0) == last)
+        def _():
+            other_rows[packed : packed + hi - lo] = total[lo:hi]
+
+
+def pair_kernel(jump, rim, far, far_high, far_low, near_high, near_low, const, high, low, both, *rest):
     cols, sites = const.shape
     length = far.shape[1]
     blocks = sites // length
@@ -117,6 +137,7 @@
     edge = (window - length) // 2
     span = 2 * window
     tall = blocks * window
+    total = rest[-1]
     if rim.shape[0] == 1:
         flag = jnp.minimum(lax.axis_index("row"), 1).astype(jnp.float32)
         left, right = rim[0] * flag, rim[0] * (1 - flag)
@@ -157,11 +178,19 @@
         total[window:] = last
         total[length : length + window] += middle
         high[b * span : (b + 1) * span], low[b * span : (b + 1) * span] = halves(total[...])
+        if jump:
+            own_rows, other_rows = rest[:2]
+            start = length + edge - b * length
+            own_rows[b * sites : (b + 1) * sites] = total[start : start + sites]
+            put_rows(b, start, sites, span, other_rows, total)
         both[:, column] = const[:, column] - (
             triple(*halves(low_const), *part(0, edge))
             + triple(*halves(constant(b)), *part(edge, edge + length))
             + triple(*halves(high_const), *part(edge + length, window))
         )
+        if jump:
+            at = blocks * sites + b * cols
+            own_rows[at : at + cols] = both[:, column]
 
 
 def keep(ref, start, value):
@@ -171,14 +200,18 @@
     ref[cols:, pl.ds(start, width)] = low
 
 
-def load(sides, next_in, own_in, halo, ref):
-    sites = own_in.shape[1]
+def load(sides, pick, own, halo, ref):
+    sites = own.shape[1]
     ref[...] = jnp.zeros_like(ref)
-    keep(ref, halo, own_in[...])
+    keep(ref, halo, own)
     for side in range(sides):
         on_right = 1 - jnp.minimum(lax.axis_index("row"), 1).astype(jnp.int32) if sides == 1 else side
         start = pl.multiple_of((1 - on_right) * (sites - halo), 128)
-        keep(ref, pl.multiple_of(on_right * (halo + sites), 128), next_in[side, :, pl.ds(start, halo)])
+        keep(ref, pl.multiple_of(on_right * (halo + sites), 128), pick(side, pl.ds(start, halo)))
+
+
+def plain(next_in):
+    return lambda side, cut: next_in[side, :, cut]
 
 
 def top_kernel(mine, sides, next_in, own_in, const, near_high, near_low, _upper, _lower, upper, lower, mid):
@@ -190,7 +223,7 @@
 
     @pl.when(lax.axis_index("tm") == 2 * mine)
     def _():
-        load(sides, next_in, own_in, edge, mid)
+        load(sides, plain(next_in), own_in[...], edge, mid)
         upper[...] = own_in[...]
         for b in range(blocks):
             at, rows = slice(b * length, (b + 1) * length), slice(b * window, (b + 1) * window)
@@ -211,7 +244,7 @@
 
     @pl.when(lax.axis_index("tm") == 2 * mine)
     def _():
-        load(sides, next_in, own_in, halo, late)
+        load(sides, plain(next_in), own_in[...], halo, late)
         mid[...] = jnp.zeros_like(mid)
         for side in range(sides):
             on_right = 1 - jnp.minimum(lax.axis_index("row"), 1).astype(jnp.int32) if sides == 1 else side
@@ -240,7 +273,57 @@
 def chain_kernel(mine, sides, next_in, own_in, both, high, low, _late, _lower, late, lower):
     @pl.when(lax.axis_index("tm") == 2 * mine)
     def _():
-        load(sides, next_in, own_in, (late.shape[1] - own_in.shape[1]) // 2, late)
+        load(sides, plain(next_in), own_in[...], (late.shape[1] - own_in.shape[1]) // 2, late)
+        step(both, high, low, late, lower)
+
+
+def rows_kernel(own_rows, other_rows, own_high, own_low, other_high, other_low):
+    own_high[...], own_low[...] = halves(own_rows[: own_high.shape[0]])
+    other_high[...], other_low[...] = halves(other_rows[...])
+
+
+def jump_kernel(
+    mine, sides, next_in, own_in, both, high, low, own_rows, own_high, own_low, other_high, other_low,
+    _late, _lower, late, lower, parts, mid
+):
+    cols, sites = lower.shape
+    length = high.shape[1]
+    blocks = sites // length
+    span = high.shape[0] // blocks
+
+    @pl.when(lax.axis_index("tm") != 2 * mine)
+    def _():
+        parts[...] = jnp.zeros_like(parts)
+
+    @pl.when(lax.axis_index("tm") == 2 * mine)
+    def _():
+        load(sides, plain(next_in), own_in[...], (late.shape[1] - sites) // 2, late)
+        step(both, high, low, late, lower)
+        keep(mid, 0, lower[...])
+        for b in range(blocks):
+            at, rows = slice(b * length, (b + 1) * length), slice(b * sites, (b + 1) * sites)
+            const = slice(blocks * sites + b * cols, blocks * sites + (b + 1) * cols)
+            parts[:cols, at] = own_rows[const] + stacked_dot(mid, slice(0, sites), own_high[rows], own_low[rows])
+        for last in (True, False):
+
+            @pl.when((lax.axis_index("row") == 0) != last)
+            def _():
+                for b, (lo, hi, packed) in enumerate(cuts_of(blocks, length, sites, span, last)):
+                    from_sites = slice(0, hi - lo) if last else slice(sites - (hi - lo), sites)
+                    rows = slice(packed, packed + hi - lo)
+                    parts[cols:, b * length : (b + 1) * length] = stacked_dot(
+                        mid, from_sites, other_high[rows], other_low[rows]
+                    )
+
+
+def landing_kernel(mine, sides, next_in, own_in, both, high, low, _late, _lower, late, lower):
+    cols, sites = lower.shape
+
+    @pl.when(lax.axis_index("tm") == 2 * mine)
+    def _():
+        own = own_in[:cols] + next_in[cols:]
+        pick = lambda side, cut: next_in[:cols, cut] + own_in[cols:, cut]
+        load(sides, pick, own, (late.shape[1] - sites) // 2, late)
         step(both, high, low, late, lower)
 
 
@@ -260,7 +343,7 @@
 
     @pl.when(lax.axis_index("tm") == 0)
     def _():
-        load(sides, next_in, own_in, halo, late)
+        load(sides, plain(next_in), own_in[...], halo, late)
 
     @pl.when(lax.axis_index("tm") != 2 * top)
     def _():
@@ -305,6 +388,8 @@
         return jnp.concatenate(moved)
 
     tall = blocks * window
+    jump = pairs // 2 - 1
+    jumps = rows == 2 and 3 <= jump < pairs - 2
     const, inv_high, inv_low, lag, mask = pl.pallas_call(
         const_kernel,
         out_shape=(
@@ -368,42 +453,89 @@
         out_specs=(VMEM,) * 4,
         compiler_params=PARAMS,
     )(rim, far)
-    high, low, both = pl.pallas_call(
-        pair_kernel,
+    packs = (shape((blocks * (sites + cols), length), f32), shape((halo + edge, length), f32)) if jumps else ()
+    high, low, both, *packs = pl.pallas_call(
+        functools.partial(pair_kernel, jumps),
         out_shape=(
-            shape((2 * tall, length), bf16), shape((2 * tall, length), bf16), shape((cols, sites), f32),
+            shape((2 * tall, length), bf16), shape((2 * tall, length), bf16), shape((cols, sites), f32), *packs
         ),
         in_specs=[VMEM] * 7,
-        out_specs=(VMEM,) * 3,
+        out_specs=(VMEM,) * (3 + len(packs)),
         scratch_shapes=[pltpu.VMEM((2 * window, length), f32)],
         compiler_params=PARAMS,
         cost_estimate=pl.CostEstimate(flops=10**9, bytes_accessed=0, transcendentals=0),
     )(rim, far, far_high, far_low, near_high, near_low, const)
+    if jumps:
+        source, target = [2 * jump - 2], [2 * jump]
+        own_rows = lax.ppermute(packs[0], BOTH, link(source, target))
+        other_rows = cross(packs[1], source, target)
+        ship = pl.pallas_call(
+            rows_kernel,
+            out_shape=(shape((blocks * sites, length), bf16),) * 2 + (shape(other_rows.shape, bf16),) * 2,
+            in_specs=[VMEM] * 2,
+            out_specs=(VMEM,) * 4,
+            compiler_params=PARAMS,
+        )(own_rows, other_rows)
+
+    def turn(kernel, given, state, scratch=(), extra=(), flops=0):
+        return pl.pallas_call(
+            kernel,
+            out_shape=tuple(shape(v.shape, v.dtype) for v in state) + tuple(extra),
+            in_specs=[VMEM] * (len(given) + 2),
+            out_specs=(VMEM,) * (2 + len(extra)),
+            scratch_shapes=list(scratch),
+            input_output_aliases={len(given): 0, len(given) + 1: 1},
+            compiler_params=PARAMS,
+            cost_estimate=pl.CostEstimate(flops=flops, bytes_accessed=0, transcendentals=0) if flops else None,
+        )(*given, *state)
 
     late = jnp.zeros((2 * cols, sites + 2 * halo), bf16)
-    for mine in range(pairs - 1, 0, -1):
+    mine = pairs - 1
+    while mine > 0:
+        if jumps and mine == jump:
+            source, target = [2 * mine], [2 * mine - 4]
+            next_in = cross(parts, source, target)
+            own_in = lax.ppermute(parts, BOTH, link(source, target))
+            beside_next = cross(lower[None], source, [2 * mine - 2])
+            beside_own = lax.ppermute(lower, BOTH, link(source, [2 * mine - 2]))
+            late, lower = turn(
+                functools.partial(landing_kernel, mine - 2, sides), (next_in, own_in, both, high, low), (late, lower)
+            )
+            late, lower = turn(
+                functools.partial(chain_kernel, mine - 1, sides),
+                (beside_next, beside_own, both, high, low),
+                (late, lower),
+            )
+            mine -= 2
+            continue
         source, target = [2 * mine], [2 * mine - 2]
         next_in = cross(lower[None], source, target)
         own_in = lax.ppermute(lower, BOTH, link(source, target))
-        if mine == 1:
+        mine -= 1
+        if mine == 0:
             break
-        if mine == pairs - 1:
-            kernel, given = functools.partial(direct_kernel, mine - 1, sides), (
-                next_in, own_in, rim, far, far_high, far_low, rim_high, rim_low, near_high, near_low, const
+        if mine == pairs - 2:
+            late, lower = turn(
+                functools.partial(direct_kernel, mine, sides),
+                (next_in, own_in, rim, far, far_high, far_low, rim_high, rim_low, near_high, near_low, const),
+                (late, lower),
+                [pltpu.VMEM((2 * cols, sites + 2 * edge), bf16)],
             )
-            scratch = [pltpu.VMEM((2 * cols, sites + 2 * edge), bf16)]
+        elif jumps and mine == jump:
+            late, lower, parts = turn(
+                functools.partial(jump_kernel, mine, sides),
+                (next_in, own_in, both, high, low, own_rows, *ship),
+                (late, lower),
+                [pltpu.VMEM((2 * cols, sites), bf16)],
+                [shape((2 * cols, sites), f32)],
+            )
         else:
-            kernel, given = functools.partial(chain_kernel, mine - 1, sides), (next_in, own_in, both, high, low)
-            scratch = []
-        late, lower = pl.pallas_call(
-            kernel,
-            out_shape=(shape(late.shape, bf16), shape(lower.shape, f32)),
-            in_specs=[VMEM] * (len(given) + 2),
-            out_specs=(VMEM,) * 2,
-            scratch_shapes=scratch,
-            input_output_aliases={len(given): 0, len(given) + 1: 1},
-            compiler_params=PARAMS,
-        )(*given, late, lower)
+            late, lower = turn(
+                functools.partial(chain_kernel, mine, sides),
+                (next_in, own_in, both, high, low),
+                (late, lower),
+                flops=50 * 10**9 if jumps and mine == pairs - 3 else 0,
+            )
     late, upper = pl.pallas_call(
         functools.partial(upper_kernel, sides, pairs - 1),
         out_shape=(shape(late.shape, bf16), shape(upper.shape, f32)),

time: 61.5 us -> 62.7 us (1.020)
  waiting for transfers between devices: 39.4 us -> 37.2 us
  Pallas kernels: 4.89 us -> 6.8 us
  starting transfers between devices: 15.8 us -> 17.2 us
    ppermute x9 -> x10, waiting for transfers between devices: 38.3 us -> 34.9 us  [cross(): return lax.ppermute(value, BOTH, perm)]
    ppermute x0 -> x3, starting transfers between devices: none -> 2.07 us  [the longest x1 0.73 us: local(): own_rows = lax.ppermute(packs[0], BOTH, link(source, target))]
    pallas_call x7 -> x8, Pallas kernels: 1.7 us -> 3.61 us  [the longest x1 3.25 us: local(): pl.pallas_call(functools.partial(pair_kernel, jumps), out_shape=(shape((2...]
    ppermute x7 -> x5, starting transfers between devices: 5.28 us -> 3.95 us  [local(): own_in = lax.ppermute(lower, BOTH, link(source, target))]
    ppermute x9 -> x10, starting transfers between devices: 7.24 us -> 7.94 us  [cross(): return lax.ppermute(value, BOTH, perm)]
    ppermute x7 -> x5, waiting for transfers between devices: 0.72 us -> 1.36 us  [local(): own_in = lax.ppermute(lower, BOTH, link(source, target))]
  transfers between devices with their start and end apart: 19 -> 21, of which waited for: 4 -> 5; matrix products, arithmetic and copies ran while one was open for 0% -> 0% of each run, Pallas kernels for 5% -> 8%
where the time goes in v5:
time: 62.7 us; the launch traced here: 62.3 us
  waiting for transfers between devices  37.2 us (59%)
  starting transfers between devices  17.2 us (27%)
  Pallas kernels  6.8 us (11%)
  other arithmetic  0.64 us (1%)
    ppermute x10, waiting for transfers between devices, cross(): return lax.ppermute(value, BOTH, perm)  34.9 us
    ppermute x10, starting transfers between devices, cross(): return lax.ppermute(value, BOTH, perm)  7.94 us
    ppermute x5, starting transfers between devices, local(): own_in = lax.ppermute(lower, BOTH, link(source, target))  3.95 us
    pallas_call x1, Pallas kernels, local(): pl.pallas_call(functools.partial(pair_kernel, jumps), out_shape=(shape((2...  3.25 us
    pallas_call x1, Pallas kernels, local(): pl.pallas_call(const_kernel, out_shape=(shape((cols, sites), f32), shape(...  1.51 us
    ppermute x5, waiting for transfers between devices, local(): own_in = lax.ppermute(lower, BOTH, link(source, target))  1.36 us
    ppermute x1, starting transfers between devices, local(): far = lax.ppermute(near, BOTH, link(odd[:-1], even[:-1]))  1.29 us
    ppermute x1, starting transfers between devices, local(): returned = lax.ppermute(upper, BOTH, link(even, odd))  1.29 us
  transfers between devices with their start and end apart: 21, of which 5 were waited for; matrix products, arithmetic and copies ran while one was open for 0% of the time, Pallas kernels for 8%

profile of v5, /device:TPU:0, one launch (start us, length us, event | category | flops | bytes accessed | tf_op | source)
XLA Modules:
  0.0 62.3 jit_solution(10540517069597153677)
XLA Ops:
  0.0 1.5 %shard_map.46 = (f32[32,512]{1,0:T(8,128)S(1)}, bf16[2,256,256]{2,1,0:T(8,128)(2,1)S(1)}, bf16[2,256,256]{2,1,0:T(8,128)(2,1)S(1)}, f32[2,512,256]{2,1,0:T(8,128)S(1)}, s32[2,3]{1,0:T(2,128)S(1)}) custom-call(s32[1,2,3]{2,1,0:T(2,128)} %mask.1, f32[1,32,512]{2,1,0:T(8,128)} %normals.1, f32[1,2,256,256]{3,2,1,0:T(8,128)} %inv.1, f32[1,2,512,256]{3,2,1,0:T(8,128)} %lag.1), custom_call_target="tpu_custom_call" | custom-call | tf_op jit(solution)/shard_map/pallas_call | solution.py:393
  1.5 0.7 %collective-permute-start.2 = (f32[1,32,512]{2,1,0:T(8,128)S(1)}, f32[1,32,512]{2,1,0:T(8,128)S(1)}, u32[]{:S(2)}, u32[]{:S(2)}) collective-permute-start(f32[1,32,512]{2,1,0:T(8,128)S(1)} %bitcast.15), channel_id=1, source_target_pairs={{30,29},{31,28}} | collective-permute-start | bytes 196616 | tf_op jit(solution)/shard_map/ppermute | solution.py:378
  2.2 0.7 %collective-permute-start.3 = (f32[32,512]{1,0:T(8,128)S(1)}, f32[32,512]{1,0:T(8,128)S(1)}, u32[]{:S(2)}, u32[]{:S(2)}) collective-permute-start(f32[32,512]{1,0:T(8,128)S(1)} %get-tuple-element.46.const), channel_id=1, source_target_pairs={{30,28},{31,29}} | collective-permute-start | bytes 196616 | tf_op jit(solution)/shard_map/ppermute | solution.py:411
  2.9 0.7 %shard_map.47 = (f32[1088,256]{1,0:T(8,128)S(1)}, bf16[1024,256]{1,0:T(8,128)(2,1)S(1)}, bf16[1024,256]{1,0:T(8,128)(2,1)S(1)}) custom-call(s32[2,3]{1,0:T(2,128)S(1)} %get-tuple-element.45.mask, f32[32,512]{1,0:T(8,128)S(1)} %get-tuple-element.46.const, bf16[2,256,256]{2,1,0:T(8,128)(2,1)S(1)} %get-tuple-element.47.inv_high, ...), custom_call_target="tpu_custom_call" | custom-call | flops 427819008 | bytes 4194304 | tf_op jit(solution)/shard_map/pallas_call | solution.py:412
  3.6 1.3 %collective-permute-start = (f32[1,544,128]{2,1,0:T(8,128)S(1)}, f32[1,544,128]{2,1,0:T(8,128)S(1)}, u32[]{:S(2)}, u32[]{:S(2)}) collective-permute-start(f32[1,544,128]{2,1,0:T(8,128)S(1)} %get-tuple-element.51), channel_id=1, source_target_pairs={{2,1},{3,0},{6,5},{7,4},{10,9},{11,8},{14,13},{15,12},{18,17},{19,... | collective-permute-start | bytes 835592 | tf_op jit(solution)/shard_map/ppermute | solution.py:378
  4.9 1.3 %collective-permute-start.1 = (f32[1088,256]{1,0:T(8,128)S(1)}, f32[1088,256]{1,0:T(8,128)S(1)}, u32[]{:S(2)}, u32[]{:S(2)}) collective-permute-start(f32[1088,256]{1,0:T(8,128)S(1)} %get-tuple-element.52), channel_id=1, source_target_pairs={{2,0},{3,1},{6,4},{7,5},{10,8},{11,9},{14,12},{15,13},{18,16},{19,... | collective-permute-start | bytes 3342344 | tf_op jit(solution)/shard_map/ppermute | solution.py:433
  6.2 0.0 collective-permute-done.2.next_in
  6.2 0.0 collective-permute-done.3.own_in
  6.3 0.7 %collective-permute-start.4 = (f32[1,32,512]{2,1,0:T(8,128)S(1)}, f32[1,32,512]{2,1,0:T(8,128)S(1)}, u32[]{:S(2)}, u32[]{:S(2)}) collective-permute-start(f32[1,32,512]{2,1,0:T(8,128)S(1)} %bitcast.9), channel_id=1, source_target_pairs={{28,25},{29,24}} | collective-permute-start | bytes 196616 | tf_op jit(solution)/shard_map/ppermute | solution.py:378
  6.9 0.7 %collective-permute-start.5 = (f32[32,512]{1,0:T(8,128)S(1)}, f32[32,512]{1,0:T(8,128)S(1)}, u32[]{:S(2)}, u32[]{:S(2)}) collective-permute-start(f32[32,512]{1,0:T(8,128)S(1)} %get-tuple-element.60._lower), channel_id=1, source_target_pairs={{28,24},{29,25}} | collective-permute-start | bytes 196616 | tf_op jit(solution)/shard_map/ppermute | solution.py:513
  7.6 3.9 %collective-permute-done.rim = f32[1,544,128]{2,1,0:T(8,128)S(1)} collective-permute-done((f32[1,544,128]{2,1,0:T(8,128)S(1)}, f32[1,544,128]{2,1,0:T(8,128)S(1)}, u32[]{:S(2)}, u32[]{:S(2)}) %collective-permute-start) | collective-permute-done | bytes 278560 | tf_op jit(solution)/shard_map/ppermute | solution.py:378
  11.5 0.6 collective-permute-done.1.far
  12.1 0.2 shard_map.49
  12.3 0.0 collective-permute-done.4.next_in
  12.3 0.0 collective-permute-done.5.own_in
  12.4 0.7 %collective-permute-start.7 = (f32[32,512]{1,0:T(8,128)S(1)}, f32[32,512]{1,0:T(8,128)S(1)}, u32[]{:S(2)}, u32[]{:S(2)}) collective-permute-start(f32[32,512]{1,0:T(8,128)S(1)} %get-tuple-element.63._lower), channel_id=1, source_target_pairs={{24,20},{25,21}} | collective-permute-start | bytes 196616 | tf_op jit(solution)/shard_map/ppermute | solution.py:513
  13.0 0.7 %collective-permute-start.6 = (f32[1,32,512]{2,1,0:T(8,128)S(1)}, f32[1,32,512]{2,1,0:T(8,128)S(1)}, u32[]{:S(2)}, u32[]{:S(2)}) collective-permute-start(f32[1,32,512]{2,1,0:T(8,128)S(1)} %bitcast.10), channel_id=1, source_target_pairs={{24,21},{25,20}} | collective-permute-start | bytes 196616 | tf_op jit(solution)/shard_map/ppermute | solution.py:378
  13.7 3.2 %shard_map.50 = (bf16[2048,256]{1,0:T(8,128)(2,1)S(1)}, bf16[2048,256]{1,0:T(8,128)(2,1)S(1)}, f32[32,512]{1,0:T(8,128)S(1)}, f32[1088,256]{1,0:T(8,128)S(1)}, f32[512,256]{1,0:T(8,128)S(1)}) custom-call(f32[1,544,128]{2,1,0:T(8,128)S(1)} %collective-permute-done.rim, f32[1088,256]{1,0:T(8,128)S(1)} %collective-permute-done.1.far, ...), custom_call_target="tpu_custom_call" | custom-call | flops 1000000000 | tf_op jit(solution)/shard_map/pallas_call | solution.py:457
  16.9 0.7 %collective-permute-start.13 = (f32[512,256]{1,0:T(8,128)S(1)}, f32[512,256]{1,0:T(8,128)S(1)}, u32[]{:S(2)}, u32[]{:S(2)}) collective-permute-start(f32[512,256]{1,0:T(8,128)S(1)} %get-tuple-element.69), channel_id=1, source_target_pairs={{8,13},{9,12}} | collective-permute-start | bytes 1572872 | tf_op jit(solution)/shard_map/ppermute | solution.py:378
  17.7 0.7 %collective-permute-start.12 = (f32[1088,256]{1,0:T(8,128)S(1)}, f32[1088,256]{1,0:T(8,128)S(1)}, u32[]{:S(2)}, u32[]{:S(2)}) collective-permute-start(f32[1088,256]{1,0:T(8,128)S(1)} %get-tuple-element.68), channel_id=1, source_target_pairs={{8,12},{9,13}} | collective-permute-start | bytes 3342344 | tf_op jit(solution)/shard_map/ppermute | solution.py:470
  18.4 0.0 collective-permute-done.6.next_in
  18.4 0.0 collective-permute-done.7.own_in
  18.4 0.7 %collective-permute-start.8 = (f32[1,32,512]{2,1,0:T(8,128)S(1)}, f32[1,32,512]{2,1,0:T(8,128)S(1)}, u32[]{:S(2)}, u32[]{:S(2)}) collective-permute-start(f32[1,32,512]{2,1,0:T(8,128)S(1)} %bitcast.11), channel_id=1, source_target_pairs={{20,17},{21,16}} | collective-permute-start | bytes 196616 | tf_op jit(solution)/shard_map/ppermute | solution.py:378
  19.1 0.7 %collective-permute-start.9 = (f32[32,512]{1,0:T(8,128)S(1)}, f32[32,512]{1,0:T(8,128)S(1)}, u32[]{:S(2)}, u32[]{:S(2)}) collective-permute-start(f32[32,512]{1,0:T(8,128)S(1)} %get-tuple-element.65._lower), channel_id=1, source_target_pairs={{20,16},{21,17}} | collective-permute-start | bytes 196616 | tf_op jit(solution)/shard_map/ppermute | solution.py:513
  19.8 0.0 collective-permute-done.8.next_in
  19.8 0.0 collective-permute-done.9.own_in
  19.8 0.7 %collective-permute-start.10 = (f32[1,32,512]{2,1,0:T(8,128)S(1)}, f32[1,32,512]{2,1,0:T(8,128)S(1)}, u32[]{:S(2)}, u32[]{:S(2)}) collective-permute-start(f32[1,32,512]{2,1,0:T(8,128)S(1)} %bitcast.12), channel_id=1, source_target_pairs={{16,13},{17,12}} | collective-permute-start | bytes 196616 | tf_op jit(solution)/shard_map/ppermute | solution.py:378
  20.5 0.7 %collective-permute-start.11 = (f32[32,512]{1,0:T(8,128)S(1)}, f32[32,512]{1,0:T(8,128)S(1)}, u32[]{:S(2)}, u32[]{:S(2)}) collective-permute-start(f32[32,512]{1,0:T(8,128)S(1)} %get-tuple-element.67._lower), channel_id=1, source_target_pairs={{16,12},{17,13}} | collective-permute-start | bytes 196616 | tf_op jit(solution)/shard_map/ppermute | solution.py:513
  21.2 0.0 collective-permute-done.13.other_rows
  21.2 0.0 collective-permute-done.12.own_rows
  21.2 0.2 shard_map.55
  21.4 0.0 collective-permute-done.10.next_in
  21.5 0.7 %collective-permute-start.17 = (f32[64,512]{1,0:T(8,128)S(1)}, f32[64,512]{1,0:T(8,128)S(1)}, u32[]{:S(2)}, u32[]{:S(2)}) collective-permute-start(f32[64,512]{1,0:T(8,128)S(1)} %get-tuple-element.76), channel_id=1, source_target_pairs={{12,4},{13,5}} | collective-permute-start | bytes 393224 | tf_op jit(solution)/shard_map/ppermute | solution.py:498
  22.2 0.7 %collective-permute-start.16 = (f32[64,512]{1,0:T(8,128)S(1)}, f32[64,512]{1,0:T(8,128)S(1)}, u32[]{:S(2)}, u32[]{:S(2)}) collective-permute-start(f32[64,512]{1,0:T(8,128)S(1)} %get-tuple-element.76), channel_id=1, source_target_pairs={{12,5},{13,4}} | collective-permute-start | bytes 393224 | tf_op jit(solution)/shard_map/ppermute | solution.py:378
  22.9 0.7 %collective-permute-start.14 = (f32[1,32,512]{2,1,0:T(8,128)S(1)}, f32[1,32,512]{2,1,0:T(8,128)S(1)}, u32[]{:S(2)}, u32[]{:S(2)}) collective-permute-start(f32[1,32,512]{2,1,0:T(8,128)S(1)} %bitcast.13), channel_id=1, source_target_pairs={{12,9},{13,8}} | collective-permute-start | bytes 196616 | tf_op jit(solution)/shard_map/ppermute | solution.py:378
  23.5 0.7 %collective-permute-start.15 = (f32[32,512]{1,0:T(8,128)S(1)}, f32[32,512]{1,0:T(8,128)S(1)}, u32[]{:S(2)}, u32[]{:S(2)}) collective-permute-start(f32[32,512]{1,0:T(8,128)S(1)} %get-tuple-element.75._lower), channel_id=1, source_target_pairs={{12,8},{13,9}} | collective-permute-start | bytes 196616 | tf_op jit(solution)/shard_map/ppermute | solution.py:500
  24.2 0.0 collective-permute-done.14.next_in
  24.2 0.0 collective-permute-done.15.own_in
  24.2 0.0 collective-permute-done.16.next_in
  24.3 1.3 %collective-permute-start.18 = (f32[1,32,512]{2,1,0:T(8,128)S(1)}, f32[1,32,512]{2,1,0:T(8,128)S(1)}, u32[]{:S(2)}, u32[]{:S(2)}) collective-permute-start(f32[1,32,512]{2,1,0:T(8,128)S(1)} %bitcast.14), channel_id=1, source_target_pairs={{4,1},{5,0}} | collective-permute-start | bytes 196616 | tf_op jit(solution)/shard_map/ppermute | solution.py:378
  25.6 1.3 %collective-permute-start.19 = (f32[32,512]{1,0:T(8,128)S(1)}, f32[32,512]{1,0:T(8,128)S(1)}, u32[]{:S(2)}, u32[]{:S(2)}) collective-permute-start(f32[32,512]{1,0:T(8,128)S(1)} %get-tuple-element.80._lower), channel_id=1, source_target_pairs={{4,0},{5,1}} | collective-permute-start | bytes 196616 | tf_op jit(solution)/shard_map/ppermute | solution.py:513
  26.9 31.0 %collective-permute-done.18.next_in = f32[1,32,512]{2,1,0:T(8,128)S(1)} collective-permute-done((f32[1,32,512]{2,1,0:T(8,128)S(1)}, f32[1,32,512]{2,1,0:T(8,128)S(1)}, u32[]{:S(2)}, u32[]{:S(2)}) %collective-permute-start.18) | collective-permute-done | bytes 65568 | tf_op jit(solution)/shard_map/ppermute | solution.py:378
  57.9 1.3 %collective-permute-done.19.own_in = f32[32,512]{1,0:T(8,128)S(1)} collective-permute-done((f32[32,512]{1,0:T(8,128)S(1)}, f32[32,512]{1,0:T(8,128)S(1)}, u32[]{:S(2)}, u32[]{:S(2)}) %collective-permute-start.19) | collective-permute-done | bytes 65568 | tf_op jit(solution)/shard_map/ppermute | solution.py:513
  59.2 0.3 shard_map.59
  59.5 1.3 %collective-permute-start.20 = (f32[32,512]{1,0:T(8,128)S(1)}, f32[32,512]{1,0:T(8,128)S(1)}, u32[]{:S(2)}, u32[]{:S(2)}) collective-permute-start(f32[32,512]{1,0:T(8,128)S(1)} %get-tuple-element.84), channel_id=1, source_target_pairs={{0,2},{1,3},{4,6},{5,7},{8,10},{9,11},{12,14},{13,15},{16,18},{17,... | collective-permute-start | bytes 196616 | tf_op jit(solution)/shard_map/ppermute | solution.py:547
  60.8 0.5 shard_map.60
  61.3 0.4 collective-permute-done.20
  61.7 0.6 %select_bitcast_fusion = f32[1,32,512]{2,1,0:T(8,128)} fusion(f32[32,512]{1,0:T(8,128)S(1)} %shard_map.60, f32[32,512]{1,0:T(8,128)S(1)} %collective-permute-done.20, pred[]{:T(512)S(6)} %eq.5), kind=kLoop, calls=%fused_computation | loop fusion | flops 16384 | bytes 196609 | tf_op jit(solution)/shard_map/broadcast_in_dim | solution.py:557
  (13 shorter events, 0.2 us)
Async XLA Ops:
  1.5 4.7 %collective-permute-start.2 = (f32[1,32,512]{2,1,0:T(8,128)S(1)}, f32[1,32,512]{2,1,0:T(8,128)S(1)}, u32[]{:S(2)}, u32[]{:S(2)}) collective-permute-start(f32[1,32,512]{2,1,0:T(8,128)S(1)} %bitcast.15), channel_id=1, source_target_pairs={{30,29},{31,28}} | collective-permute-start | bytes 196616 | tf_op jit(solution)/shard_map/ppermute | solution.py:378
  2.2 4.0 %collective-permute-start.3 = (f32[32,512]{1,0:T(8,128)S(1)}, f32[32,512]{1,0:T(8,128)S(1)}, u32[]{:S(2)}, u32[]{:S(2)}) collective-permute-start(f32[32,512]{1,0:T(8,128)S(1)} %get-tuple-element.46.const), channel_id=1, source_target_pairs={{30,28},{31,29}} | collective-permute-start | bytes 196616 | tf_op jit(solution)/shard_map/ppermute | solution.py:411
  3.6 7.9 %collective-permute-start = (f32[1,544,128]{2,1,0:T(8,128)S(1)}, f32[1,544,128]{2,1,0:T(8,128)S(1)}, u32[]{:S(2)}, u32[]{:S(2)}) collective-permute-start(f32[1,544,128]{2,1,0:T(8,128)S(1)} %get-tuple-element.51), channel_id=1, source_target_pairs={{2,1},{3,0},{6,5},{7,4},{10,9},{11,8},{14,13},{15,12},{18,17},{19,... | collective-permute-start | bytes 835592 | tf_op jit(solution)/shard_map/ppermute | solution.py:378
  4.9 7.2 %collective-permute-start.1 = (f32[1088,256]{1,0:T(8,128)S(1)}, f32[1088,256]{1,0:T(8,128)S(1)}, u32[]{:S(2)}, u32[]{:S(2)}) collective-permute-start(f32[1088,256]{1,0:T(8,128)S(1)} %get-tuple-element.52), channel_id=1, source_target_pairs={{2,0},{3,1},{6,4},{7,5},{10,8},{11,9},{14,12},{15,13},{18,16},{19,... | collective-permute-start | bytes 3342344 | tf_op jit(solution)/shard_map/ppermute | solution.py:433
  6.3 6.0 %collective-permute-start.4 = (f32[1,32,512]{2,1,0:T(8,128)S(1)}, f32[1,32,512]{2,1,0:T(8,128)S(1)}, u32[]{:S(2)}, u32[]{:S(2)}) collective-permute-start(f32[1,32,512]{2,1,0:T(8,128)S(1)} %bitcast.9), channel_id=1, source_target_pairs={{28,25},{29,24}} | collective-permute-start | bytes 196616 | tf_op jit(solution)/shard_map/ppermute | solution.py:378
  6.9 5.3 %collective-permute-start.5 = (f32[32,512]{1,0:T(8,128)S(1)}, f32[32,512]{1,0:T(8,128)S(1)}, u32[]{:S(2)}, u32[]{:S(2)}) collective-permute-start(f32[32,512]{1,0:T(8,128)S(1)} %get-tuple-element.60._lower), channel_id=1, source_target_pairs={{28,24},{29,25}} | collective-permute-start | bytes 196616 | tf_op jit(solution)/shard_map/ppermute | solution.py:513
  12.4 6.1 %collective-permute-start.7 = (f32[32,512]{1,0:T(8,128)S(1)}, f32[32,512]{1,0:T(8,128)S(1)}, u32[]{:S(2)}, u32[]{:S(2)}) collective-permute-start(f32[32,512]{1,0:T(8,128)S(1)} %get-tuple-element.63._lower), channel_id=1, source_target_pairs={{24,20},{25,21}} | collective-permute-start | bytes 196616 | tf_op jit(solution)/shard_map/ppermute | solution.py:513
  13.0 5.4 %collective-permute-start.6 = (f32[1,32,512]{2,1,0:T(8,128)S(1)}, f32[1,32,512]{2,1,0:T(8,128)S(1)}, u32[]{:S(2)}, u32[]{:S(2)}) collective-permute-start(f32[1,32,512]{2,1,0:T(8,128)S(1)} %bitcast.10), channel_id=1, source_target_pairs={{24,21},{25,20}} | collective-permute-start | bytes 196616 | tf_op jit(solution)/shard_map/ppermute | solution.py:378
  16.9 4.2 %collective-permute-start.13 = (f32[512,256]{1,0:T(8,128)S(1)}, f32[512,256]{1,0:T(8,128)S(1)}, u32[]{:S(2)}, u32[]{:S(2)}) collective-permute-start(f32[512,256]{1,0:T(8,128)S(1)} %get-tuple-element.69), channel_id=1, source_target_pairs={{8,13},{9,12}} | collective-permute-start | bytes 1572872 | tf_op jit(solution)/shard_map/ppermute | solution.py:378
  17.7 3.5 %collective-permute-start.12 = (f32[1088,256]{1,0:T(8,128)S(1)}, f32[1088,256]{1,0:T(8,128)S(1)}, u32[]{:S(2)}, u32[]{:S(2)}) collective-permute-start(f32[1088,256]{1,0:T(8,128)S(1)} %get-tuple-element.68), channel_id=1, source_target_pairs={{8,12},{9,13}} | collective-permute-start | bytes 3342344 | tf_op jit(solution)/shard_map/ppermute | solution.py:470
  18.4 1.3 %collective-permute-start.8 = (f32[1,32,512]{2,1,0:T(8,128)S(1)}, f32[1,32,512]{2,1,0:T(8,128)S(1)}, u32[]{:S(2)}, u32[]{:S(2)}) collective-permute-start(f32[1,32,512]{2,1,0:T(8,128)S(1)} %bitcast.11), channel_id=1, source_target_pairs={{20,17},{21,16}} | collective-permute-start | bytes 196616 | tf_op jit(solution)/shard_map/ppermute | solution.py:378
  19.1 0.7 %collective-permute-start.9 = (f32[32,512]{1,0:T(8,128)S(1)}, f32[32,512]{1,0:T(8,128)S(1)}, u32[]{:S(2)}, u32[]{:S(2)}) collective-permute-start(f32[32,512]{1,0:T(8,128)S(1)} %get-tuple-element.65._lower), channel_id=1, source_target_pairs={{20,16},{21,17}} | collective-permute-start | bytes 196616 | tf_op jit(solution)/shard_map/ppermute | solution.py:513
  19.8 1.6 %collective-permute-start.10 = (f32[1,32,512]{2,1,0:T(8,128)S(1)}, f32[1,32,512]{2,1,0:T(8,128)S(1)}, u32[]{:S(2)}, u32[]{:S(2)}) collective-permute-start(f32[1,32,512]{2,1,0:T(8,128)S(1)} %bitcast.12), channel_id=1, source_target_pairs={{16,13},{17,12}} | collective-permute-start | bytes 196616 | tf_op jit(solution)/shard_map/ppermute | solution.py:378
  20.5 0.9 %collective-permute-start.11 = (f32[32,512]{1,0:T(8,128)S(1)}, f32[32,512]{1,0:T(8,128)S(1)}, u32[]{:S(2)}, u32[]{:S(2)}) collective-permute-start(f32[32,512]{1,0:T(8,128)S(1)} %get-tuple-element.67._lower), channel_id=1, source_target_pairs={{16,12},{17,13}} | collective-permute-start | bytes 196616 | tf_op jit(solution)/shard_map/ppermute | solution.py:513
  21.5 2.7 %collective-permute-start.17 = (f32[64,512]{1,0:T(8,128)S(1)}, f32[64,512]{1,0:T(8,128)S(1)}, u32[]{:S(2)}, u32[]{:S(2)}) collective-permute-start(f32[64,512]{1,0:T(8,128)S(1)} %get-tuple-element.76), channel_id=1, source_target_pairs={{12,4},{13,5}} | collective-permute-start | bytes 393224 | tf_op jit(solution)/shard_map/ppermute | solution.py:498
  22.2 2.1 %collective-permute-start.16 = (f32[64,512]{1,0:T(8,128)S(1)}, f32[64,512]{1,0:T(8,128)S(1)}, u32[]{:S(2)}, u32[]{:S(2)}) collective-permute-start(f32[64,512]{1,0:T(8,128)S(1)} %get-tuple-element.76), channel_id=1, source_target_pairs={{12,5},{13,4}} | collective-permute-start | bytes 393224 | tf_op jit(solution)/shard_map/ppermute | solution.py:378
  22.9 1.3 %collective-permute-start.14 = (f32[1,32,512]{2,1,0:T(8,128)S(1)}, f32[1,32,512]{2,1,0:T(8,128)S(1)}, u32[]{:S(2)}, u32[]{:S(2)}) collective-permute-start(f32[1,32,512]{2,1,0:T(8,128)S(1)} %bitcast.13), channel_id=1, source_target_pairs={{12,9},{13,8}} | collective-permute-start | bytes 196616 | tf_op jit(solution)/shard_map/ppermute | solution.py:378
  23.5 0.7 %collective-permute-start.15 = (f32[32,512]{1,0:T(8,128)S(1)}, f32[32,512]{1,0:T(8,128)S(1)}, u32[]{:S(2)}, u32[]{:S(2)}) collective-permute-start(f32[32,512]{1,0:T(8,128)S(1)} %get-tuple-element.75._lower), channel_id=1, source_target_pairs={{12,8},{13,9}} | collective-permute-start | bytes 196616 | tf_op jit(solution)/shard_map/ppermute | solution.py:500
  24.3 33.6 %collective-permute-start.18 = (f32[1,32,512]{2,1,0:T(8,128)S(1)}, f32[1,32,512]{2,1,0:T(8,128)S(1)}, u32[]{:S(2)}, u32[]{:S(2)}) collective-permute-start(f32[1,32,512]{2,1,0:T(8,128)S(1)} %bitcast.14), channel_id=1, source_target_pairs={{4,1},{5,0}} | collective-permute-start | bytes 196616 | tf_op jit(solution)/shard_map/ppermute | solution.py:378
  25.6 33.6 %collective-permute-start.19 = (f32[32,512]{1,0:T(8,128)S(1)}, f32[32,512]{1,0:T(8,128)S(1)}, u32[]{:S(2)}, u32[]{:S(2)}) collective-permute-start(f32[32,512]{1,0:T(8,128)S(1)} %get-tuple-element.80._lower), channel_id=1, source_target_pairs={{4,0},{5,1}} | collective-permute-start | bytes 196616 | tf_op jit(solution)/shard_map/ppermute | solution.py:513
  59.5 2.2 %collective-permute-start.20 = (f32[32,512]{1,0:T(8,128)S(1)}, f32[32,512]{1,0:T(8,128)S(1)}, u32[]{:S(2)}, u32[]{:S(2)}) collective-permute-start(f32[32,512]{1,0:T(8,128)S(1)} %get-tuple-element.84), channel_id=1, source_target_pairs={{0,2},{1,3},{4,6},{5,7},{8,10},{9,11},{12,14},{13,15},{16,18},{17,... | collective-permute-start | bytes 196616 | tf_op jit(solution)/shard_map/ppermute | solution.py:547

commit v6 on v5

--- a/solution.py
+++ b/solution.py
@@ -117,16 +117,6 @@
         cuts.append((lo, hi, packed))
         packed += hi - lo
     return cuts
-
-
-def put_rows(b, start, sites, span, other_rows, total):
-    length = total.shape[1]
-    for last in (True, False):
-        lo, hi, packed = cuts_of(sites // length, length, sites, span, last)[b]
-
-        @pl.when((lax.axis_index("row") == 0) == last)
-        def _():
-            other_rows[packed : packed + hi - lo] = total[lo:hi]
 
 
 def pair_kernel(jump, rim, far, far_high, far_low, near_high, near_low, const, high, low, both, *rest):
@@ -178,19 +168,30 @@
         total[window:] = last
         total[length : length + window] += middle
         high[b * span : (b + 1) * span], low[b * span : (b + 1) * span] = halves(total[...])
-        if jump:
-            own_rows, other_rows = rest[:2]
-            start = length + edge - b * length
-            own_rows[b * sites : (b + 1) * sites] = total[start : start + sites]
-            put_rows(b, start, sites, span, other_rows, total)
         both[:, column] = const[:, column] - (
             triple(*halves(low_const), *part(0, edge))
             + triple(*halves(constant(b)), *part(edge, edge + length))
             + triple(*halves(high_const), *part(edge + length, window))
         )
-        if jump:
+    if jump:
+        own_rows, other_rows = rest[:2]
+
+        def value(start, count):
+            rows = pl.ds(start, count)
+            return high[rows].astype(jnp.float32) + low[rows].astype(jnp.float32)
+
+        for b in range(blocks):
+            own_rows[b * sites : (b + 1) * sites] = value(b * span + window - edge - b * length, sites)
             at = blocks * sites + b * cols
-            own_rows[at : at + cols] = both[:, column]
+            own_rows[at : at + cols] = both[:, b * length : (b + 1) * length]
+        starts = [
+            [b * span + at for b, (lo, hi, _) in enumerate(cuts_of(blocks, length, sites, span, last)) for at in range(lo, hi, edge)]
+            for last in (True, False)
+        ]
+        row = lax.axis_index("row")
+        for chunk, (on_right, on_left) in enumerate(zip(*starts)):
+            start = pl.multiple_of(jnp.where(row == 0, on_right, on_left), edge)
+            other_rows[chunk * edge : (chunk + 1) * edge] = value(start, edge)
 
 
 def keep(ref, start, value):
@@ -316,24 +317,15 @@
                     )
 
 
-def landing_kernel(mine, sides, next_in, own_in, both, high, low, _late, _lower, late, lower):
-    cols, sites = lower.shape
-
-    @pl.when(lax.axis_index("tm") == 2 * mine)
-    def _():
-        own = own_in[:cols] + next_in[cols:]
-        pick = lambda side, cut: next_in[:cols, cut] + own_in[cols:, cut]
-        load(sides, pick, own, (late.shape[1] - sites) // 2, late)
-        step(both, high, low, late, lower)
-
-
-def last_kernel(both, high, low, late, _lower, lower):
-    pl.when(lax.axis_index("tm") == 0)(lambda: step(both, high, low, late, lower))
-
-
-def upper_kernel(
-    sides, top, next_in, own_in, far, far_high, far_low, _late, _upper, late, upper
-):
+def last_kernel(jumps, both, high, low, late, _lower, lower):
+    device = lax.axis_index("tm")
+    pl.when((device == 0) | (device == 2) if jumps else device == 0)(lambda: step(both, high, low, late, lower))
+
+
+def upper_kernel(sides, top, jumps, next_in, own_in, *rest):
+    if jumps:
+        beside_next, beside_own = rest[:2]
+    far, far_high, far_low, _late, _upper, late, upper = rest[-7:]
     cols, sites = upper.shape
     length = far.shape[1]
     blocks = sites // length
@@ -343,7 +335,17 @@
 
     @pl.when(lax.axis_index("tm") == 0)
     def _():
-        load(sides, plain(next_in), own_in[...], halo, late)
+        if jumps:
+            own = own_in[:cols] + next_in[cols:]
+            load(sides, lambda side, cut: next_in[:cols, cut] + own_in[cols:, cut], own, halo, late)
+        else:
+            load(sides, plain(next_in), own_in[...], halo, late)
+
+    if jumps:
+
+        @pl.when(lax.axis_index("tm") == 2)
+        def _():
+            load(sides, plain(beside_next), beside_own[...], halo, late)
 
     @pl.when(lax.axis_index("tm") != 2 * top)
     def _():
@@ -388,8 +390,8 @@
         return jnp.concatenate(moved)
 
     tall = blocks * window
-    jump = pairs // 2 - 1
-    jumps = rows == 2 and 3 <= jump < pairs - 2
+    jump = 2
+    jumps = rows == 2 and pairs > 5
     const, inv_high, inv_low, lag, mask = pl.pallas_call(
         const_kernel,
         out_shape=(
@@ -498,16 +500,7 @@
             own_in = lax.ppermute(parts, BOTH, link(source, target))
             beside_next = cross(lower[None], source, [2 * mine - 2])
             beside_own = lax.ppermute(lower, BOTH, link(source, [2 * mine - 2]))
-            late, lower = turn(
-                functools.partial(landing_kernel, mine - 2, sides), (next_in, own_in, both, high, low), (late, lower)
-            )
-            late, lower = turn(
-                functools.partial(chain_kernel, mine - 1, sides),
-                (beside_next, beside_own, both, high, low),
-                (late, lower),
-            )
-            mine -= 2
-            continue
+            break
         source, target = [2 * mine], [2 * mine - 2]
         next_in = cross(lower[None], source, target)
         own_in = lax.ppermute(lower, BOTH, link(source, target))
@@ -536,17 +529,13 @@
                 (late, lower),
                 flops=50 * 10**9 if jumps and mine == pairs - 3 else 0,
             )
-    late, upper = pl.pallas_call(
-        functools.partial(upper_kernel, sides, pairs - 1),
-        out_shape=(shape(late.shape, bf16), shape(upper.shape, f32)),
-        in_specs=[VMEM] * 7,
-        out_specs=(VMEM,) * 2,
-        input_output_aliases={5: 0, 6: 1},
-        compiler_params=PARAMS,
-    )(next_in, own_in, far, far_high, far_low, late, upper)
+    given = (next_in, own_in) + ((beside_next, beside_own) if jumps else ())
+    late, upper = turn(
+        functools.partial(upper_kernel, sides, pairs - 1, jumps), (*given, far, far_high, far_low), (late, upper)
+    )
     returned = lax.ppermute(upper, BOTH, link(even, odd))
     lower = pl.pallas_call(
-        last_kernel,
+        functools.partial(last_kernel, jumps),
         out_shape=shape(lower.shape, f32),
         in_specs=[VMEM] * 5,
         out_specs=VMEM,

time: 62.7 us -> 56.4 us (0.90)
  waiting for transfers between devices: 37.2 us -> 32.1 us
  Pallas kernels: 6.8 us -> 5.19 us
    ppermute x10, waiting for transfers between devices: 34.9 us -> 5.9 us  [cross(): return lax.ppermute(value, BOTH, perm)]
    ppermute x1, waiting for transfers between devices: 0.01 us -> 25.2 us  [local(): own_in = lax.ppermute(parts, BOTH, link(source, target))]
    pallas_call x1, Pallas kernels: 3.25 us -> 1.65 us  [local(): pl.pallas_call(functools.partial(pair_kernel, jumps), out_shape=(shape((2...]
    ppermute x5, waiting for transfers between devices: 1.36 us -> 0.01 us  [local(): own_in = lax.ppermute(lower, BOTH, link(source, target))]
    ppermute x5, starting transfers between devices: 3.95 us -> 3.32 us  [local(): own_in = lax.ppermute(lower, BOTH, link(source, target))]
  transfers between devices with their start and end apart: 21 -> 21, of which waited for: 5 -> 5; matrix products, arithmetic and copies ran while one was open for 0% -> 0% of each run, Pallas kernels for 8% -> 6%
where the time goes in v6:
time: 56.4 us; the launch traced here: 55.6 us
  waiting for transfers between devices  32.1 us (57%)
  starting transfers between devices  17.2 us (30%)
  Pallas kernels  5.19 us (9%)
  other arithmetic  0.64 us (1%)
    ppermute x1, waiting for transfers between devices, local(): own_in = lax.ppermute(parts, BOTH, link(source, target))  25.2 us
    ppermute x10, starting transfers between devices, cross(): return lax.ppermute(value, BOTH, perm)  7.93 us
    ppermute x10, waiting for transfers between devices, cross(): return lax.ppermute(value, BOTH, perm)  5.9 us
    ppermute x5, starting transfers between devices, local(): own_in = lax.ppermute(lower, BOTH, link(source, target))  3.32 us
    pallas_call x1, Pallas kernels, local(): pl.pallas_call(functools.partial(pair_kernel, jumps), out_shape=(shape((2...  1.65 us
    pallas_call x1, Pallas kernels, local(): pl.pallas_call(const_kernel, out_shape=(shape((cols, sites), f32), shape(...  1.51 us
    ppermute x1, starting transfers between devices, local(): far = lax.ppermute(near, BOTH, link(odd[:-1], even[:-1]))  1.29 us
    ppermute x1, starting transfers between devices, local(): own_in = lax.ppermute(parts, BOTH, link(source, target))  1.29 us
  transfers between devices with their start and end apart: 21, of which 5 were waited for; matrix products, arithmetic and copies ran while one was open for 0% of the time, Pallas kernels for 6%

profile of v6, /device:TPU:0, one launch (start us, length us, event | category | flops | bytes accessed | tf_op | source)
XLA Modules:
  0.0 55.6 jit_solution(15342728064650915463)
XLA Ops:
  0.0 1.5 %shard_map.46 = (f32[32,512]{1,0:T(8,128)S(1)}, bf16[2,256,256]{2,1,0:T(8,128)(2,1)S(1)}, bf16[2,256,256]{2,1,0:T(8,128)(2,1)S(1)}, f32[2,512,256]{2,1,0:T(8,128)S(1)}, s32[2,3]{1,0:T(2,128)S(1)}) custom-call(s32[1,2,3]{2,1,0:T(2,128)} %mask.1, f32[1,32,512]{2,1,0:T(8,128)} %normals.1, f32[1,2,256,256]{3,2,1,0:T(8,128)} %inv.1, f32[1,2,512,256]{3,2,1,0:T(8,128)} %lag.1), custom_call_target="tpu_custom_call" | custom-call | tf_op jit(solution)/shard_map/pallas_call | solution.py:395
  1.5 0.7 %collective-permute-start.2 = (f32[1,32,512]{2,1,0:T(8,128)S(1)}, f32[1,32,512]{2,1,0:T(8,128)S(1)}, u32[]{:S(2)}, u32[]{:S(2)}) collective-permute-start(f32[1,32,512]{2,1,0:T(8,128)S(1)} %bitcast.15), channel_id=1, source_target_pairs={{30,29},{31,28}} | collective-permute-start | bytes 196616 | tf_op jit(solution)/shard_map/ppermute | solution.py:380
  2.2 0.7 %collective-permute-start.3 = (f32[32,512]{1,0:T(8,128)S(1)}, f32[32,512]{1,0:T(8,128)S(1)}, u32[]{:S(2)}, u32[]{:S(2)}) collective-permute-start(f32[32,512]{1,0:T(8,128)S(1)} %get-tuple-element.44.const), channel_id=1, source_target_pairs={{30,28},{31,29}} | collective-permute-start | bytes 196616 | tf_op jit(solution)/shard_map/ppermute | solution.py:413
  2.9 0.7 %shard_map.47 = (f32[1088,256]{1,0:T(8,128)S(1)}, bf16[1024,256]{1,0:T(8,128)(2,1)S(1)}, bf16[1024,256]{1,0:T(8,128)(2,1)S(1)}) custom-call(s32[2,3]{1,0:T(2,128)S(1)} %get-tuple-element.43.mask, f32[32,512]{1,0:T(8,128)S(1)} %get-tuple-element.44.const, bf16[2,256,256]{2,1,0:T(8,128)(2,1)S(1)} %get-tuple-element.45.inv_high, ...), custom_call_target="tpu_custom_call" | custom-call | flops 427819008 | bytes 4194304 | tf_op jit(solution)/shard_map/pallas_call | solution.py:414
  3.6 1.3 %collective-permute-start = (f32[1,544,128]{2,1,0:T(8,128)S(1)}, f32[1,544,128]{2,1,0:T(8,128)S(1)}, u32[]{:S(2)}, u32[]{:S(2)}) collective-permute-start(f32[1,544,128]{2,1,0:T(8,128)S(1)} %get-tuple-element.49), channel_id=1, source_target_pairs={{2,1},{3,0},{6,5},{7,4},{10,9},{11,8},{14,13},{15,12},{18,17},{19,... | collective-permute-start | bytes 835592 | tf_op jit(solution)/shard_map/ppermute | solution.py:380
  4.9 1.3 %collective-permute-start.1 = (f32[1088,256]{1,0:T(8,128)S(1)}, f32[1088,256]{1,0:T(8,128)S(1)}, u32[]{:S(2)}, u32[]{:S(2)}) collective-permute-start(f32[1088,256]{1,0:T(8,128)S(1)} %get-tuple-element.50), channel_id=1, source_target_pairs={{2,0},{3,1},{6,4},{7,5},{10,8},{11,9},{14,12},{15,13},{18,16},{19,... | collective-permute-start | bytes 3342344 | tf_op jit(solution)/shard_map/ppermute | solution.py:435
  6.2 0.0 collective-permute-done.2.next_in
  6.2 0.0 collective-permute-done.3.own_in
  6.3 0.7 %collective-permute-start.4 = (f32[1,32,512]{2,1,0:T(8,128)S(1)}, f32[1,32,512]{2,1,0:T(8,128)S(1)}, u32[]{:S(2)}, u32[]{:S(2)}) collective-permute-start(f32[1,32,512]{2,1,0:T(8,128)S(1)} %bitcast.9), channel_id=1, source_target_pairs={{28,25},{29,24}} | collective-permute-start | bytes 196616 | tf_op jit(solution)/shard_map/ppermute | solution.py:380
  6.9 0.7 %collective-permute-start.5 = (f32[32,512]{1,0:T(8,128)S(1)}, f32[32,512]{1,0:T(8,128)S(1)}, u32[]{:S(2)}, u32[]{:S(2)}) collective-permute-start(f32[32,512]{1,0:T(8,128)S(1)} %get-tuple-element.58._lower), channel_id=1, source_target_pairs={{28,24},{29,25}} | collective-permute-start | bytes 196616 | tf_op jit(solution)/shard_map/ppermute | solution.py:506
  7.6 3.9 %collective-permute-done.rim = f32[1,544,128]{2,1,0:T(8,128)S(1)} collective-permute-done((f32[1,544,128]{2,1,0:T(8,128)S(1)}, f32[1,544,128]{2,1,0:T(8,128)S(1)}, u32[]{:S(2)}, u32[]{:S(2)}) %collective-permute-start) | collective-permute-done | bytes 278560 | tf_op jit(solution)/shard_map/ppermute | solution.py:380
  11.5 0.6 %collective-permute-done.1.far.rest_2_ = f32[1088,256]{1,0:T(8,128)S(1)} collective-permute-done((f32[1088,256]{1,0:T(8,128)S(1)}, f32[1088,256]{1,0:T(8,128)S(1)}, u32[]{:S(2)}, u32[]{:S(2)}) %collective-permute-start.1) | collective-permute-done | bytes 1114144 | tf_op jit(solution)/shard_map/ppermute | solution.py:435
  12.1 0.2 shard_map.49
  12.3 0.0 collective-permute-done.4.next_in
  12.3 0.0 collective-permute-done.5.own_in
  12.4 0.7 %collective-permute-start.7 = (f32[32,512]{1,0:T(8,128)S(1)}, f32[32,512]{1,0:T(8,128)S(1)}, u32[]{:S(2)}, u32[]{:S(2)}) collective-permute-start(f32[32,512]{1,0:T(8,128)S(1)} %get-tuple-element.61._lower), channel_id=1, source_target_pairs={{24,20},{25,21}} | collective-permute-start | bytes 196616 | tf_op jit(solution)/shard_map/ppermute | solution.py:506
  13.0 0.7 %collective-permute-start.6 = (f32[1,32,512]{2,1,0:T(8,128)S(1)}, f32[1,32,512]{2,1,0:T(8,128)S(1)}, u32[]{:S(2)}, u32[]{:S(2)}) collective-permute-start(f32[1,32,512]{2,1,0:T(8,128)S(1)} %bitcast.10), channel_id=1, source_target_pairs={{24,21},{25,20}} | collective-permute-start | bytes 196616 | tf_op jit(solution)/shard_map/ppermute | solution.py:380
  13.7 1.6 %shard_map.50 = (bf16[2048,256]{1,0:T(8,128)(2,1)S(1)}, bf16[2048,256]{1,0:T(8,128)(2,1)S(1)}, f32[32,512]{1,0:T(8,128)S(1)}, f32[1088,256]{1,0:T(8,128)S(1)}, f32[512,256]{1,0:T(8,128)S(1)}) custom-call(f32[1,544,128]{2,1,0:T(8,128)S(1)} %collective-permute-done.rim, f32[1088,256]{1,0:T(8,128)S(1)} %collective-permute-done.1.far.rest_2_, ...), custom_call_target="tpu_custom_call" | custom-call | flops 1000000000 | tf_op jit(solution)/shard_map/pallas_call | solution.py:459
  15.4 0.7 %collective-permute-start.15 = (f32[512,256]{1,0:T(8,128)S(1)}, f32[512,256]{1,0:T(8,128)S(1)}, u32[]{:S(2)}, u32[]{:S(2)}) collective-permute-start(f32[512,256]{1,0:T(8,128)S(1)} %get-tuple-element.69), channel_id=1, source_target_pairs={{4,9},{5,8}} | collective-permute-start | bytes 1572872 | tf_op jit(solution)/shard_map/ppermute | solution.py:380
  16.1 0.7 %collective-permute-start.14 = (f32[1088,256]{1,0:T(8,128)S(1)}, f32[1088,256]{1,0:T(8,128)S(1)}, u32[]{:S(2)}, u32[]{:S(2)}) collective-permute-start(f32[1088,256]{1,0:T(8,128)S(1)} %get-tuple-element.68), channel_id=1, source_target_pairs={{4,8},{5,9}} | collective-permute-start | bytes 3342344 | tf_op jit(solution)/shard_map/ppermute | solution.py:472
  16.8 0.0 collective-permute-done.6.next_in
  16.8 0.0 collective-permute-done.7.own_in
  16.8 0.7 %collective-permute-start.8 = (f32[1,32,512]{2,1,0:T(8,128)S(1)}, f32[1,32,512]{2,1,0:T(8,128)S(1)}, u32[]{:S(2)}, u32[]{:S(2)}) collective-permute-start(f32[1,32,512]{2,1,0:T(8,128)S(1)} %bitcast.11), channel_id=1, source_target_pairs={{20,17},{21,16}} | collective-permute-start | bytes 196616 | tf_op jit(solution)/shard_map/ppermute | solution.py:380
  17.5 0.7 %collective-permute-start.9 = (f32[32,512]{1,0:T(8,128)S(1)}, f32[32,512]{1,0:T(8,128)S(1)}, u32[]{:S(2)}, u32[]{:S(2)}) collective-permute-start(f32[32,512]{1,0:T(8,128)S(1)} %get-tuple-element.63._lower), channel_id=1, source_target_pairs={{20,16},{21,17}} | collective-permute-start | bytes 196616 | tf_op jit(solution)/shard_map/ppermute | solution.py:506
  18.2 0.0 collective-permute-done.8.next_in
  18.2 0.0 collective-permute-done.9.own_in
  18.2 0.7 %collective-permute-start.10 = (f32[1,32,512]{2,1,0:T(8,128)S(1)}, f32[1,32,512]{2,1,0:T(8,128)S(1)}, u32[]{:S(2)}, u32[]{:S(2)}) collective-permute-start(f32[1,32,512]{2,1,0:T(8,128)S(1)} %bitcast.12), channel_id=1, source_target_pairs={{16,13},{17,12}} | collective-permute-start | bytes 196616 | tf_op jit(solution)/shard_map/ppermute | solution.py:380
  18.9 0.7 %collective-permute-start.11 = (f32[32,512]{1,0:T(8,128)S(1)}, f32[32,512]{1,0:T(8,128)S(1)}, u32[]{:S(2)}, u32[]{:S(2)}) collective-permute-start(f32[32,512]{1,0:T(8,128)S(1)} %get-tuple-element.65._lower), channel_id=1, source_target_pairs={{16,12},{17,13}} | collective-permute-start | bytes 196616 | tf_op jit(solution)/shard_map/ppermute | solution.py:506
  19.6 0.0 collective-permute-done.10.next_in
  19.6 0.0 collective-permute-done.11.own_in
  19.6 0.7 %collective-permute-start.12 = (f32[1,32,512]{2,1,0:T(8,128)S(1)}, f32[1,32,512]{2,1,0:T(8,128)S(1)}, u32[]{:S(2)}, u32[]{:S(2)}) collective-permute-start(f32[1,32,512]{2,1,0:T(8,128)S(1)} %bitcast.13), channel_id=1, source_target_pairs={{12,9},{13,8}} | collective-permute-start | bytes 196616 | tf_op jit(solution)/shard_map/ppermute | solution.py:380
  20.3 0.7 %collective-permute-start.13 = (f32[32,512]{1,0:T(8,128)S(1)}, f32[32,512]{1,0:T(8,128)S(1)}, u32[]{:S(2)}, u32[]{:S(2)}) collective-permute-start(f32[32,512]{1,0:T(8,128)S(1)} %get-tuple-element.67._lower), channel_id=1, source_target_pairs={{12,8},{13,9}} | collective-permute-start | bytes 196616 | tf_op jit(solution)/shard_map/ppermute | solution.py:506
  21.0 0.0 collective-permute-done.15.other_rows
  21.0 0.0 collective-permute-done.14.own_rows
  21.0 0.2 shard_map.56
  21.2 0.0 collective-permute-done.12.next_in
  21.3 1.3 %collective-permute-start.17 = (f32[64,512]{1,0:T(8,128)S(1)}, f32[64,512]{1,0:T(8,128)S(1)}, u32[]{:S(2)}, u32[]{:S(2)}) collective-permute-start(f32[64,512]{1,0:T(8,128)S(1)} %get-tuple-element.75), channel_id=1, source_target_pairs={{8,0},{9,1}} | collective-permute-start | bytes 393224 | tf_op jit(solution)/shard_map/ppermute | solution.py:500
  22.6 1.3 %collective-permute-start.16 = (f32[64,512]{1,0:T(8,128)S(1)}, f32[64,512]{1,0:T(8,128)S(1)}, u32[]{:S(2)}, u32[]{:S(2)}) collective-permute-start(f32[64,512]{1,0:T(8,128)S(1)} %get-tuple-element.75), channel_id=1, source_target_pairs={{8,1},{9,0}} | collective-permute-start | bytes 393224 | tf_op jit(solution)/shard_map/ppermute | solution.py:380
  23.9 0.7 %collective-permute-start.18 = (f32[1,32,512]{2,1,0:T(8,128)S(1)}, f32[1,32,512]{2,1,0:T(8,128)S(1)}, u32[]{:S(2)}, u32[]{:S(2)}) collective-permute-start(f32[1,32,512]{2,1,0:T(8,128)S(1)} %bitcast.14), channel_id=1, source_target_pairs={{8,5},{9,4}} | collective-permute-start | bytes 196616 | tf_op jit(solution)/shard_map/ppermute | solution.py:380
  24.6 0.7 %collective-permute-start.19 = (f32[32,512]{1,0:T(8,128)S(1)}, f32[32,512]{1,0:T(8,128)S(1)}, u32[]{:S(2)}, u32[]{:S(2)}) collective-permute-start(f32[32,512]{1,0:T(8,128)S(1)} %get-tuple-element.76._lower), channel_id=1, source_target_pairs={{8,4},{9,5}} | collective-permute-start | bytes 196616 | tf_op jit(solution)/shard_map/ppermute | solution.py:502
  25.2 0.0 collective-permute-done.18.rest_0_
  25.3 25.2 %collective-permute-done.17.own_in = f32[64,512]{1,0:T(8,128)S(1)} collective-permute-done((f32[64,512]{1,0:T(8,128)S(1)}, f32[64,512]{1,0:T(8,128)S(1)}, u32[]{:S(2)}, u32[]{:S(2)}) %collective-permute-start.17) | collective-permute-done | bytes 131104 | tf_op jit(solution)/shard_map/ppermute | solution.py:500
  50.4 2.0 %collective-permute-done.16.next_in = f32[64,512]{1,0:T(8,128)S(1)} collective-permute-done((f32[64,512]{1,0:T(8,128)S(1)}, f32[64,512]{1,0:T(8,128)S(1)}, u32[]{:S(2)}, u32[]{:S(2)}) %collective-permute-start.16) | collective-permute-done | bytes 131104 | tf_op jit(solution)/shard_map/ppermute | solution.py:380
  52.5 0.3 shard_map.58
  52.8 1.3 %collective-permute-start.20 = (f32[32,512]{1,0:T(8,128)S(1)}, f32[32,512]{1,0:T(8,128)S(1)}, u32[]{:S(2)}, u32[]{:S(2)}) collective-permute-start(f32[32,512]{1,0:T(8,128)S(1)} %get-tuple-element.80), channel_id=1, source_target_pairs={{0,2},{1,3},{4,6},{5,7},{8,10},{9,11},{12,14},{13,15},{16,18},{17,... | collective-permute-start | bytes 196616 | tf_op jit(solution)/shard_map/ppermute | solution.py:536
  54.1 0.5 shard_map.59
  54.5 0.4 collective-permute-done.20
  54.9 0.6 %select_bitcast_fusion = f32[1,32,512]{2,1,0:T(8,128)} fusion(f32[32,512]{1,0:T(8,128)S(1)} %shard_map.59, f32[32,512]{1,0:T(8,128)S(1)} %collective-permute-done.20, pred[]{:T(512)S(6)} %eq.5), kind=kLoop, calls=%fused_computation | loop fusion | flops 16384 | bytes 196609 | tf_op jit(solution)/shard_map/broadcast_in_dim | solution.py:546
  (12 shorter events, 0.2 us)
Async XLA Ops:
  1.5 4.7 %collective-permute-start.2 = (f32[1,32,512]{2,1,0:T(8,128)S(1)}, f32[1,32,512]{2,1,0:T(8,128)S(1)}, u32[]{:S(2)}, u32[]{:S(2)}) collective-permute-start(f32[1,32,512]{2,1,0:T(8,128)S(1)} %bitcast.15), channel_id=1, source_target_pairs={{30,29},{31,28}} | collective-permute-start | bytes 196616 | tf_op jit(solution)/shard_map/ppermute | solution.py:380
  2.2 4.0 %collective-permute-start.3 = (f32[32,512]{1,0:T(8,128)S(1)}, f32[32,512]{1,0:T(8,128)S(1)}, u32[]{:S(2)}, u32[]{:S(2)}) collective-permute-start(f32[32,512]{1,0:T(8,128)S(1)} %get-tuple-element.44.const), channel_id=1, source_target_pairs={{30,28},{31,29}} | collective-permute-start | bytes 196616 | tf_op jit(solution)/shard_map/ppermute | solution.py:413
  3.6 7.9 %collective-permute-start = (f32[1,544,128]{2,1,0:T(8,128)S(1)}, f32[1,544,128]{2,1,0:T(8,128)S(1)}, u32[]{:S(2)}, u32[]{:S(2)}) collective-permute-start(f32[1,544,128]{2,1,0:T(8,128)S(1)} %get-tuple-element.49), channel_id=1, source_target_pairs={{2,1},{3,0},{6,5},{7,4},{10,9},{11,8},{14,13},{15,12},{18,17},{19,... | collective-permute-start | bytes 835592 | tf_op jit(solution)/shard_map/ppermute | solution.py:380
  4.9 7.2 %collective-permute-start.1 = (f32[1088,256]{1,0:T(8,128)S(1)}, f32[1088,256]{1,0:T(8,128)S(1)}, u32[]{:S(2)}, u32[]{:S(2)}) collective-permute-start(f32[1088,256]{1,0:T(8,128)S(1)} %get-tuple-element.50), channel_id=1, source_target_pairs={{2,0},{3,1},{6,4},{7,5},{10,8},{11,9},{14,12},{15,13},{18,16},{19,... | collective-permute-start | bytes 3342344 | tf_op jit(solution)/shard_map/ppermute | solution.py:435
  6.3 6.0 %collective-permute-start.4 = (f32[1,32,512]{2,1,0:T(8,128)S(1)}, f32[1,32,512]{2,1,0:T(8,128)S(1)}, u32[]{:S(2)}, u32[]{:S(2)}) collective-permute-start(f32[1,32,512]{2,1,0:T(8,128)S(1)} %bitcast.9), channel_id=1, source_target_pairs={{28,25},{29,24}} | collective-permute-start | bytes 196616 | tf_op jit(solution)/shard_map/ppermute | solution.py:380
  6.9 5.3 %collective-permute-start.5 = (f32[32,512]{1,0:T(8,128)S(1)}, f32[32,512]{1,0:T(8,128)S(1)}, u32[]{:S(2)}, u32[]{:S(2)}) collective-permute-start(f32[32,512]{1,0:T(8,128)S(1)} %get-tuple-element.58._lower), channel_id=1, source_target_pairs={{28,24},{29,25}} | collective-permute-start | bytes 196616 | tf_op jit(solution)/shard_map/ppermute | solution.py:506
  12.4 4.5 %collective-permute-start.7 = (f32[32,512]{1,0:T(8,128)S(1)}, f32[32,512]{1,0:T(8,128)S(1)}, u32[]{:S(2)}, u32[]{:S(2)}) collective-permute-start(f32[32,512]{1,0:T(8,128)S(1)} %get-tuple-element.61._lower), channel_id=1, source_target_pairs={{24,20},{25,21}} | collective-permute-start | bytes 196616 | tf_op jit(solution)/shard_map/ppermute | solution.py:506
  13.0 3.8 %collective-permute-start.6 = (f32[1,32,512]{2,1,0:T(8,128)S(1)}, f32[1,32,512]{2,1,0:T(8,128)S(1)}, u32[]{:S(2)}, u32[]{:S(2)}) collective-permute-start(f32[1,32,512]{2,1,0:T(8,128)S(1)} %bitcast.10), channel_id=1, source_target_pairs={{24,21},{25,20}} | collective-permute-start | bytes 196616 | tf_op jit(solution)/shard_map/ppermute | solution.py:380
  15.4 5.6 %collective-permute-start.15 = (f32[512,256]{1,0:T(8,128)S(1)}, f32[512,256]{1,0:T(8,128)S(1)}, u32[]{:S(2)}, u32[]{:S(2)}) collective-permute-start(f32[512,256]{1,0:T(8,128)S(1)} %get-tuple-element.69), channel_id=1, source_target_pairs={{4,9},{5,8}} | collective-permute-start | bytes 1572872 | tf_op jit(solution)/shard_map/ppermute | solution.py:380
  16.1 4.9 %collective-permute-start.14 = (f32[1088,256]{1,0:T(8,128)S(1)}, f32[1088,256]{1,0:T(8,128)S(1)}, u32[]{:S(2)}, u32[]{:S(2)}) collective-permute-start(f32[1088,256]{1,0:T(8,128)S(1)} %get-tuple-element.68), channel_id=1, source_target_pairs={{4,8},{5,9}} | collective-permute-start | bytes 3342344 | tf_op jit(solution)/shard_map/ppermute | solution.py:472
  16.8 1.3 %collective-permute-start.8 = (f32[1,32,512]{2,1,0:T(8,128)S(1)}, f32[1,32,512]{2,1,0:T(8,128)S(1)}, u32[]{:S(2)}, u32[]{:S(2)}) collective-permute-start(f32[1,32,512]{2,1,0:T(8,128)S(1)} %bitcast.11), channel_id=1, source_target_pairs={{20,17},{21,16}} | collective-permute-start | bytes 196616 | tf_op jit(solution)/shard_map/ppermute | solution.py:380
  17.5 0.7 %collective-permute-start.9 = (f32[32,512]{1,0:T(8,128)S(1)}, f32[32,512]{1,0:T(8,128)S(1)}, u32[]{:S(2)}, u32[]{:S(2)}) collective-permute-start(f32[32,512]{1,0:T(8,128)S(1)} %get-tuple-element.63._lower), channel_id=1, source_target_pairs={{20,16},{21,17}} | collective-permute-start | bytes 196616 | tf_op jit(solution)/shard_map/ppermute | solution.py:506
  18.2 1.3 %collective-permute-start.10 = (f32[1,32,512]{2,1,0:T(8,128)S(1)}, f32[1,32,512]{2,1,0:T(8,128)S(1)}, u32[]{:S(2)}, u32[]{:S(2)}) collective-permute-start(f32[1,32,512]{2,1,0:T(8,128)S(1)} %bitcast.12), channel_id=1, source_target_pairs={{16,13},{17,12}} | collective-permute-start | bytes 196616 | tf_op jit(solution)/shard_map/ppermute | solution.py:380
  18.9 0.7 %collective-permute-start.11 = (f32[32,512]{1,0:T(8,128)S(1)}, f32[32,512]{1,0:T(8,128)S(1)}, u32[]{:S(2)}, u32[]{:S(2)}) collective-permute-start(f32[32,512]{1,0:T(8,128)S(1)} %get-tuple-element.65._lower), channel_id=1, source_target_pairs={{16,12},{17,13}} | collective-permute-start | bytes 196616 | tf_op jit(solution)/shard_map/ppermute | solution.py:506
  19.6 1.6 %collective-permute-start.12 = (f32[1,32,512]{2,1,0:T(8,128)S(1)}, f32[1,32,512]{2,1,0:T(8,128)S(1)}, u32[]{:S(2)}, u32[]{:S(2)}) collective-permute-start(f32[1,32,512]{2,1,0:T(8,128)S(1)} %bitcast.13), channel_id=1, source_target_pairs={{12,9},{13,8}} | collective-permute-start | bytes 196616 | tf_op jit(solution)/shard_map/ppermute | solution.py:380
  20.3 0.9 %collective-permute-start.13 = (f32[32,512]{1,0:T(8,128)S(1)}, f32[32,512]{1,0:T(8,128)S(1)}, u32[]{:S(2)}, u32[]{:S(2)}) collective-permute-start(f32[32,512]{1,0:T(8,128)S(1)} %get-tuple-element.67._lower), channel_id=1, source_target_pairs={{12,8},{13,9}} | collective-permute-start | bytes 196616 | tf_op jit(solution)/shard_map/ppermute | solution.py:506
  21.3 29.1 %collective-permute-start.17 = (f32[64,512]{1,0:T(8,128)S(1)}, f32[64,512]{1,0:T(8,128)S(1)}, u32[]{:S(2)}, u32[]{:S(2)}) collective-permute-start(f32[64,512]{1,0:T(8,128)S(1)} %get-tuple-element.75), channel_id=1, source_target_pairs={{8,0},{9,1}} | collective-permute-start | bytes 393224 | tf_op jit(solution)/shard_map/ppermute | solution.py:500
  22.6 29.9 %collective-permute-start.16 = (f32[64,512]{1,0:T(8,128)S(1)}, f32[64,512]{1,0:T(8,128)S(1)}, u32[]{:S(2)}, u32[]{:S(2)}) collective-permute-start(f32[64,512]{1,0:T(8,128)S(1)} %get-tuple-element.75), channel_id=1, source_target_pairs={{8,1},{9,0}} | collective-permute-start | bytes 393224 | tf_op jit(solution)/shard_map/ppermute | solution.py:380
  23.9 1.3 %collective-permute-start.18 = (f32[1,32,512]{2,1,0:T(8,128)S(1)}, f32[1,32,512]{2,1,0:T(8,128)S(1)}, u32[]{:S(2)}, u32[]{:S(2)}) collective-permute-start(f32[1,32,512]{2,1,0:T(8,128)S(1)} %bitcast.14), channel_id=1, source_target_pairs={{8,5},{9,4}} | collective-permute-start | bytes 196616 | tf_op jit(solution)/shard_map/ppermute | solution.py:380
  24.6 0.7 %collective-permute-start.19 = (f32[32,512]{1,0:T(8,128)S(1)}, f32[32,512]{1,0:T(8,128)S(1)}, u32[]{:S(2)}, u32[]{:S(2)}) collective-permute-start(f32[32,512]{1,0:T(8,128)S(1)} %get-tuple-element.76._lower), channel_id=1, source_target_pairs={{8,4},{9,5}} | collective-permute-start | bytes 196616 | tf_op jit(solution)/shard_map/ppermute | solution.py:502
  52.8 2.2 %collective-permute-start.20 = (f32[32,512]{1,0:T(8,128)S(1)}, f32[32,512]{1,0:T(8,128)S(1)}, u32[]{:S(2)}, u32[]{:S(2)}) collective-permute-start(f32[32,512]{1,0:T(8,128)S(1)} %get-tuple-element.80), channel_id=1, source_target_pairs={{0,2},{1,3},{4,6},{5,7},{8,10},{9,11},{12,14},{13,15},{16,18},{17,... | collective-permute-start | bytes 196616 | tf_op jit(solution)/shard_map/ppermute | solution.py:536

commit v7 on v6

--- a/solution.py
+++ b/solution.py
@@ -212,10 +212,10 @@
 
 
 def plain(next_in):
-    return lambda side, cut: next_in[side, :, cut]
-
-
-def top_kernel(mine, sides, next_in, own_in, const, near_high, near_low, _upper, _lower, upper, lower, mid):
+    return lambda side, cut: next_in[:, cut] if len(next_in.shape) == 2 else next_in[side, :, cut]
+
+
+def top_kernel(mine, sides, own_in, next_in, const, near_high, near_low, _upper, _lower, upper, lower, mid):
     sites = lower.shape[1]
     length = near_high.shape[1]
     blocks = sites // length
@@ -233,7 +233,7 @@
 
 
 def direct_kernel(
-    mine, sides, next_in, own_in, rim, far, far_high, far_low, rim_high, rim_low, near_high, near_low, const,
+    mine, sides, own_in, next_in, rim, far, far_high, far_low, rim_high, rim_low, near_high, near_low, const,
     _late, _lower, late, lower, mid
 ):
     cols, sites = lower.shape
@@ -271,7 +271,7 @@
         lower[:, at] = both[:, at] + stacked_dot(late, slice(b * length, b * length + span), high[rows], low[rows])
 
 
-def chain_kernel(mine, sides, next_in, own_in, both, high, low, _late, _lower, late, lower):
+def chain_kernel(mine, sides, own_in, next_in, both, high, low, _late, _lower, late, lower):
     @pl.when(lax.axis_index("tm") == 2 * mine)
     def _():
         load(sides, plain(next_in), own_in[...], (late.shape[1] - own_in.shape[1]) // 2, late)
@@ -283,38 +283,51 @@
     other_high[...], other_low[...] = halves(other_rows[...])
 
 
-def jump_kernel(
-    mine, sides, next_in, own_in, both, high, low, own_rows, own_high, own_low, other_high, other_low,
-    _late, _lower, late, lower, parts, mid
-):
+def add_parts(lower, own_rows, own_high, own_low, other_high, other_low, parts, mid, span):
     cols, sites = lower.shape
-    length = high.shape[1]
+    length = own_rows.shape[1]
     blocks = sites // length
-    span = high.shape[0] // blocks
+    keep(mid, 0, lower[...])
+    for b in range(blocks):
+        at, rows = slice(b * length, (b + 1) * length), slice(b * sites, (b + 1) * sites)
+        const = slice(blocks * sites + b * cols, blocks * sites + (b + 1) * cols)
+        parts[:cols, at] = own_rows[const] + stacked_dot(mid, slice(0, sites), own_high[rows], own_low[rows])
+    for last in (True, False):
+
+        @pl.when((lax.axis_index("row") == 0) != last)
+        def _():
+            for b, (lo, hi, packed) in enumerate(cuts_of(blocks, length, sites, span, last)):
+                from_sites = slice(0, hi - lo) if last else slice(sites - (hi - lo), sites)
+                rows = slice(packed, packed + hi - lo)
+                parts[cols:, b * length : (b + 1) * length] = stacked_dot(
+                    mid, from_sites, other_high[rows], other_low[rows]
+                )
+
+
+def jump_kernel(mine, sides, own_in, next_in, both, high, low, *rest):
+    ship, (_late, _lower, late, lower, parts, mid) = rest[:-6], rest[-6:]
+
+    @pl.when(lax.axis_index("tm") == 2 * mine)
+    def _():
+        load(sides, plain(next_in), own_in[...], (late.shape[1] - own_in.shape[1]) // 2, late)
+        step(both, high, low, late, lower)
+        add_parts(lower, *ship, parts, mid, high.shape[0] * high.shape[1] // own_in.shape[1])
 
     @pl.when(lax.axis_index("tm") != 2 * mine)
     def _():
         parts[...] = jnp.zeros_like(parts)
 
+
+def parts_kernel(mine, span, lower, *rest):
+    ship, (parts, mid) = rest[:-2], rest[-2:]
+
     @pl.when(lax.axis_index("tm") == 2 * mine)
     def _():
-        load(sides, plain(next_in), own_in[...], (late.shape[1] - sites) // 2, late)
-        step(both, high, low, late, lower)
-        keep(mid, 0, lower[...])
-        for b in range(blocks):
-            at, rows = slice(b * length, (b + 1) * length), slice(b * sites, (b + 1) * sites)
-            const = slice(blocks * sites + b * cols, blocks * sites + (b + 1) * cols)
-            parts[:cols, at] = own_rows[const] + stacked_dot(mid, slice(0, sites), own_high[rows], own_low[rows])
-        for last in (True, False):
-
-            @pl.when((lax.axis_index("row") == 0) != last)
-            def _():
-                for b, (lo, hi, packed) in enumerate(cuts_of(blocks, length, sites, span, last)):
-                    from_sites = slice(0, hi - lo) if last else slice(sites - (hi - lo), sites)
-                    rows = slice(packed, packed + hi - lo)
-                    parts[cols:, b * length : (b + 1) * length] = stacked_dot(
-                        mid, from_sites, other_high[rows], other_low[rows]
-                    )
+        add_parts(lower, *ship, parts, mid, span)
+
+    @pl.when(lax.axis_index("tm") != 2 * mine)
+    def _():
+        parts[...] = jnp.zeros_like(parts)
 
 
 def last_kernel(jumps, both, high, low, late, _lower, lower):
@@ -322,9 +335,7 @@
     pl.when((device == 0) | (device == 2) if jumps else device == 0)(lambda: step(both, high, low, late, lower))
 
 
-def upper_kernel(sides, top, jumps, next_in, own_in, *rest):
-    if jumps:
-        beside_next, beside_own = rest[:2]
+def upper_kernel(sides, top, *rest):
     far, far_high, far_low, _late, _upper, late, upper = rest[-7:]
     cols, sites = upper.shape
     length = far.shape[1]
@@ -333,19 +344,18 @@
     halo = (late.shape[1] - sites) // 2
     at_window = halo - (window - length) // 2
 
-    @pl.when(lax.axis_index("tm") == 0)
-    def _():
-        if jumps:
-            own = own_in[:cols] + next_in[cols:]
-            load(sides, lambda side, cut: next_in[:cols, cut] + own_in[cols:, cut], own, halo, late)
-        else:
-            load(sides, plain(next_in), own_in[...], halo, late)
-
-    if jumps:
-
-        @pl.when(lax.axis_index("tm") == 2)
+    def take(mine, own_in, next_in):
+        @pl.when(lax.axis_index("tm") == 2 * mine)
         def _():
-            load(sides, plain(beside_next), beside_own[...], halo, late)
+            if own_in.shape[0] == cols:
+                load(sides, plain(next_in), own_in[...], halo, late)
+            else:
+                own = own_in[:cols] + next_in[cols:]
+                load(sides, lambda side, cut: next_in[:cols, cut] + own_in[cols:, cut], own, halo, late)
+
+    messages = rest[:-7]
+    for mine in range(len(messages) // 2):
+        take(mine, *messages[2 * mine : 2 * mine + 2])
 
     @pl.when(lax.axis_index("tm") != 2 * top)
     def _():
@@ -374,7 +384,7 @@
     def link(source, target):
         return [(s * rows + r, t * rows + r) for s, t in zip(source, target) for r in range(rows)]
 
-    def cross(value, source, target):
+    def cross(value, source, target, split=False):
         if sides == 1:
             perm = [(s * rows + r, t * rows + 1 - r) for s, t in zip(source, target) for r in range(2)]
             return lax.ppermute(value, BOTH, perm)
@@ -386,7 +396,7 @@
                 for r in range(rows)
                 if 0 <= r + step < rows
             ]
-            moved.append(lax.ppermute(value[side : side + 1] if value.shape[0] > 1 else value, BOTH, perm))
+            moved.append(lax.ppermute(value[side : side + 1] if split else value[None], BOTH, perm))
         return jnp.concatenate(moved)
 
     tall = blocks * window
@@ -409,7 +419,7 @@
         compiler_params=PARAMS,
     )(*[pltpu.with_memory_space_constraint(a, pltpu.HBM) for a in (fill_mask, normals, inv_diag, lag_coupling)])
     odd, even = range(1, times, 2), range(0, times, 2)
-    first_next = cross(const[None], odd[-1:], even[-1:])
+    first_next = cross(const, odd[-1:], even[-1:])
     first_own = lax.ppermute(const, BOTH, link(odd[-1:], even[-1:]))
     near, near_high, near_low = pl.pallas_call(
         fuse_kernel,
@@ -431,7 +441,7 @@
         input_output_aliases={0: 0},
         compiler_params=PARAMS,
     )(near)
-    rim = cross(edges, odd[:-1], even[:-1])
+    rim = cross(edges, odd[:-1], even[:-1], True)
     far = lax.ppermute(near, BOTH, link(odd[:-1], even[:-1]))
 
     blank = jnp.zeros((cols, sites), f32)
@@ -444,7 +454,7 @@
         input_output_aliases={5: 0, 6: 1},
         compiler_params=PARAMS,
         cost_estimate=pl.CostEstimate(flops=50 * 10**9, bytes_accessed=0, transcendentals=0),
-    )(first_next, first_own, const, near_high, near_low, blank, blank)
+    )(first_own, first_next, const, near_high, near_low, blank, blank)
     far_high, far_low, rim_high, rim_low = pl.pallas_call(
         split_kernel,
         out_shape=(
@@ -468,7 +478,7 @@
         cost_estimate=pl.CostEstimate(flops=10**9, bytes_accessed=0, transcendentals=0),
     )(rim, far, far_high, far_low, near_high, near_low, const)
     if jumps:
-        source, target = [2 * jump - 2], [2 * jump]
+        source, target = [2 * jump - 2, 2 * jump], [2 * jump, 2 * jump + 2]
         own_rows = lax.ppermute(packs[0], BOTH, link(source, target))
         other_rows = cross(packs[1], source, target)
         ship = pl.pallas_call(
@@ -498,40 +508,51 @@
             source, target = [2 * mine], [2 * mine - 4]
             next_in = cross(parts, source, target)
             own_in = lax.ppermute(parts, BOTH, link(source, target))
-            beside_next = cross(lower[None], source, [2 * mine - 2])
-            beside_own = lax.ppermute(lower, BOTH, link(source, [2 * mine - 2]))
             break
         source, target = [2 * mine], [2 * mine - 2]
-        next_in = cross(lower[None], source, target)
+        next_in = cross(lower, source, target)
         own_in = lax.ppermute(lower, BOTH, link(source, target))
+        if jumps and mine == jump + 1:
+            beside = pl.pallas_call(
+                functools.partial(parts_kernel, mine, 2 * window),
+                out_shape=shape((2 * cols, sites), f32),
+                in_specs=[VMEM] * 6,
+                out_specs=VMEM,
+                scratch_shapes=[pltpu.VMEM((2 * cols, sites), bf16)],
+                compiler_params=PARAMS,
+            )(lower, own_rows, *ship)
+            source, target = [2 * mine], [2 * mine - 4]
+            beside_next = cross(beside, source, target)
+            beside_own = lax.ppermute(beside, BOTH, link(source, target))
         mine -= 1
         if mine == 0:
             break
         if mine == pairs - 2:
             late, lower = turn(
                 functools.partial(direct_kernel, mine, sides),
-                (next_in, own_in, rim, far, far_high, far_low, rim_high, rim_low, near_high, near_low, const),
+                (own_in, next_in, rim, far, far_high, far_low, rim_high, rim_low, near_high, near_low, const),
                 (late, lower),
                 [pltpu.VMEM((2 * cols, sites + 2 * edge), bf16)],
             )
         elif jumps and mine == jump:
             late, lower, parts = turn(
                 functools.partial(jump_kernel, mine, sides),
-                (next_in, own_in, both, high, low, own_rows, *ship),
+                (own_in, next_in, both, high, low, own_rows, *ship),
                 (late, lower),
                 [pltpu.VMEM((2 * cols, sites), bf16)],
                 [shape((2 * cols, sites), f32)],
             )
         else:
+            early = jumps and mine == pairs - 3
             late, lower = turn(
                 functools.partial(chain_kernel, mine, sides),
-                (next_in, own_in, both, high, low),
+                (own_in, next_in, both, high, low),
                 (late, lower),
-                flops=50 * 10**9 if jumps and mine == pairs - 3 else 0,
+                flops=50 * 10**9 if early else 0,
             )
-    given = (next_in, own_in) + ((beside_next, beside_own) if jumps else ())
+    given = (own_in, next_in) + ((beside_own, beside_next) if jumps else ())
     late, upper = turn(
-        functools.partial(upper_kernel, sides, pairs - 1, jumps), (*given, far, far_high, far_low), (late, upper)
+        functools.partial(upper_kernel, sides, pairs - 1), (*given, far, far_high, far_low), (late, upper)
     )
     returned = lax.ppermute(upper, BOTH, link(even, odd))
     lower = pl.pallas_call(

time: 56.4 us -> 55.1 us (0.977)
  waiting for transfers between devices: 32.1 us -> 31.2 us
    ppermute x1, waiting for transfers between devices: 25.2 us -> 1.04 us  [local(): own_in = lax.ppermute(parts, BOTH, link(source, target))]
    ppermute x10, waiting for transfers between devices: 5.9 us -> 29.2 us  [cross(): return lax.ppermute(value, BOTH, perm)]
where the time goes in v7:
time: 55.1 us; the launch traced here: 54.7 us
  waiting for transfers between devices  31.2 us (57%)
  starting transfers between devices  17.2 us (31%)
  Pallas kernels  5.22 us (9%)
  other arithmetic  0.64 us (1%)
    ppermute x10, waiting for transfers between devices, cross(): return lax.ppermute(value, BOTH, perm)  29.2 us
    ppermute x10, starting transfers between devices, cross(): return lax.ppermute(value, BOTH, perm)  7.94 us
    ppermute x5, starting transfers between devices, local(): own_in = lax.ppermute(lower, BOTH, link(source, target))  3.32 us
    pallas_call x1, Pallas kernels, local(): pl.pallas_call(functools.partial(pair_kernel, jumps), out_shape=(shape((2...  1.65 us
    pallas_call x1, Pallas kernels, local(): pl.pallas_call(const_kernel, out_shape=(shape((cols, sites), f32), shape(...  1.51 us
    ppermute x1, starting transfers between devices, local(): far = lax.ppermute(near, BOTH, link(odd[:-1], even[:-1]))  1.29 us
    ppermute x1, starting transfers between devices, local(): own_in = lax.ppermute(parts, BOTH, link(source, target))  1.29 us
    ppermute x1, starting transfers between devices, local(): returned = lax.ppermute(upper, BOTH, link(even, odd))  1.29 us
  transfers between devices with their start and end apart: 21, of which 5 were waited for; matrix products, arithmetic and copies ran while one was open for 0% of the time, Pallas kernels for 6%

profile of v7, /device:TPU:0, one launch (start us, length us, event | category | flops | bytes accessed | tf_op | source)
XLA Modules:
  0.0 54.7 jit_solution(4589401686958657667)
XLA Ops:
  0.0 1.5 %shard_map.46 = (f32[32,512]{1,0:T(8,128)S(1)}, bf16[2,256,256]{2,1,0:T(8,128)(2,1)S(1)}, bf16[2,256,256]{2,1,0:T(8,128)(2,1)S(1)}, f32[2,512,256]{2,1,0:T(8,128)S(1)}, s32[2,3]{1,0:T(2,128)S(1)}) custom-call(s32[1,2,3]{2,1,0:T(2,128)} %mask.1, f32[1,32,512]{2,1,0:T(8,128)} %normals.1, f32[1,2,256,256]{3,2,1,0:T(8,128)} %inv.1, f32[1,2,512,256]{3,2,1,0:T(8,128)} %lag.1), custom_call_target="tpu_custom_call" | custom-call | tf_op jit(solution)/shard_map/pallas_call | solution.py:405
  1.5 0.7 %collective-permute-start.3 = (f32[32,512]{1,0:T(8,128)S(1)}, f32[32,512]{1,0:T(8,128)S(1)}, u32[]{:S(2)}, u32[]{:S(2)}) collective-permute-start(f32[32,512]{1,0:T(8,128)S(1)} %get-tuple-element.44.const), channel_id=1, source_target_pairs={{30,29},{31,28}} | collective-permute-start | bytes 196616 | tf_op jit(solution)/shard_map/ppermute | solution.py:390
  2.2 0.7 %collective-permute-start.2 = (f32[32,512]{1,0:T(8,128)S(1)}, f32[32,512]{1,0:T(8,128)S(1)}, u32[]{:S(2)}, u32[]{:S(2)}) collective-permute-start(f32[32,512]{1,0:T(8,128)S(1)} %get-tuple-element.44.const), channel_id=1, source_target_pairs={{30,28},{31,29}} | collective-permute-start | bytes 196616 | tf_op jit(solution)/shard_map/ppermute | solution.py:423
  2.9 0.7 %shard_map.47 = (f32[1088,256]{1,0:T(8,128)S(1)}, bf16[1024,256]{1,0:T(8,128)(2,1)S(1)}, bf16[1024,256]{1,0:T(8,128)(2,1)S(1)}) custom-call(s32[2,3]{1,0:T(2,128)S(1)} %get-tuple-element.43.mask, f32[32,512]{1,0:T(8,128)S(1)} %get-tuple-element.44.const, bf16[2,256,256]{2,1,0:T(8,128)(2,1)S(1)} %get-tuple-element.45.inv_high, ...), custom_call_target="tpu_custom_call" | custom-call | flops 427819008 | bytes 4194304 | tf_op jit(solution)/shard_map/pallas_call | solution.py:424
  3.6 1.3 %collective-permute-start = (f32[1,544,128]{2,1,0:T(8,128)S(1)}, f32[1,544,128]{2,1,0:T(8,128)S(1)}, u32[]{:S(2)}, u32[]{:S(2)}) collective-permute-start(f32[1,544,128]{2,1,0:T(8,128)S(1)} %get-tuple-element.49), channel_id=1, source_target_pairs={{2,1},{3,0},{6,5},{7,4},{10,9},{11,8},{14,13},{15,12},{18,17},{19,... | collective-permute-start | bytes 835592 | tf_op jit(solution)/shard_map/ppermute | solution.py:390
  4.9 1.3 %collective-permute-start.1 = (f32[1088,256]{1,0:T(8,128)S(1)}, f32[1088,256]{1,0:T(8,128)S(1)}, u32[]{:S(2)}, u32[]{:S(2)}) collective-permute-start(f32[1088,256]{1,0:T(8,128)S(1)} %get-tuple-element.50), channel_id=1, source_target_pairs={{2,0},{3,1},{6,4},{7,5},{10,8},{11,9},{14,12},{15,13},{18,16},{19,... | collective-permute-start | bytes 3342344 | tf_op jit(solution)/shard_map/ppermute | solution.py:445
  6.2 0.0 collective-permute-done.3.next_in
  6.2 0.0 collective-permute-done.2.own_in
  6.3 0.7 %collective-permute-start.5 = (f32[32,512]{1,0:T(8,128)S(1)}, f32[32,512]{1,0:T(8,128)S(1)}, u32[]{:S(2)}, u32[]{:S(2)}) collective-permute-start(f32[32,512]{1,0:T(8,128)S(1)} %get-tuple-element.58._lower), channel_id=1, source_target_pairs={{28,25},{29,24}} | collective-permute-start | bytes 196616 | tf_op jit(solution)/shard_map/ppermute | solution.py:390
  6.9 0.7 %collective-permute-start.4 = (f32[32,512]{1,0:T(8,128)S(1)}, f32[32,512]{1,0:T(8,128)S(1)}, u32[]{:S(2)}, u32[]{:S(2)}) collective-permute-start(f32[32,512]{1,0:T(8,128)S(1)} %get-tuple-element.58._lower), channel_id=1, source_target_pairs={{28,24},{29,25}} | collective-permute-start | bytes 196616 | tf_op jit(solution)/shard_map/ppermute | solution.py:514
  7.6 3.9 %collective-permute-done.rim = f32[1,544,128]{2,1,0:T(8,128)S(1)} collective-permute-done((f32[1,544,128]{2,1,0:T(8,128)S(1)}, f32[1,544,128]{2,1,0:T(8,128)S(1)}, u32[]{:S(2)}, u32[]{:S(2)}) %collective-permute-start) | collective-permute-done | bytes 278560 | tf_op jit(solution)/shard_map/ppermute | solution.py:390
  11.5 0.6 %collective-permute-done.1.far.rest_4_ = f32[1088,256]{1,0:T(8,128)S(1)} collective-permute-done((f32[1088,256]{1,0:T(8,128)S(1)}, f32[1088,256]{1,0:T(8,128)S(1)}, u32[]{:S(2)}, u32[]{:S(2)}) %collective-permute-start.1) | collective-permute-done | bytes 1114144 | tf_op jit(solution)/shard_map/ppermute | solution.py:445
  12.1 0.2 shard_map.49
  12.3 0.0 collective-permute-done.5.next_in
  12.3 0.0 collective-permute-done.4.own_in
  12.4 0.7 %collective-permute-start.7 = (f32[32,512]{1,0:T(8,128)S(1)}, f32[32,512]{1,0:T(8,128)S(1)}, u32[]{:S(2)}, u32[]{:S(2)}) collective-permute-start(f32[32,512]{1,0:T(8,128)S(1)} %get-tuple-element.61._lower), channel_id=1, source_target_pairs={{24,21},{25,20}} | collective-permute-start | bytes 196616 | tf_op jit(solution)/shard_map/ppermute | solution.py:390
  13.0 0.7 %collective-permute-start.6 = (f32[32,512]{1,0:T(8,128)S(1)}, f32[32,512]{1,0:T(8,128)S(1)}, u32[]{:S(2)}, u32[]{:S(2)}) collective-permute-start(f32[32,512]{1,0:T(8,128)S(1)} %get-tuple-element.61._lower), channel_id=1, source_target_pairs={{24,20},{25,21}} | collective-permute-start | bytes 196616 | tf_op jit(solution)/shard_map/ppermute | solution.py:514
  13.7 1.6 %shard_map.50 = (bf16[2048,256]{1,0:T(8,128)(2,1)S(1)}, bf16[2048,256]{1,0:T(8,128)(2,1)S(1)}, f32[32,512]{1,0:T(8,128)S(1)}, f32[1088,256]{1,0:T(8,128)S(1)}, f32[512,256]{1,0:T(8,128)S(1)}) custom-call(f32[1,544,128]{2,1,0:T(8,128)S(1)} %collective-permute-done.rim, f32[1088,256]{1,0:T(8,128)S(1)} %collective-permute-done.1.far.rest_4_, ...), custom_call_target="tpu_custom_call" | custom-call | flops 1000000000 | tf_op jit(solution)/shard_map/pallas_call | solution.py:469
  15.4 0.7 %collective-permute-start.15 = (f32[512,256]{1,0:T(8,128)S(1)}, f32[512,256]{1,0:T(8,128)S(1)}, u32[]{:S(2)}, u32[]{:S(2)}) collective-permute-start(f32[512,256]{1,0:T(8,128)S(1)} %get-tuple-element.69), channel_id=1, source_target_pairs={{4,9},{5,8},{8,13},{9,12}} | collective-permute-start | bytes 1572872 | tf_op jit(solution)/shard_map/ppermute | solution.py:390
  16.1 0.7 %collective-permute-start.14 = (f32[1088,256]{1,0:T(8,128)S(1)}, f32[1088,256]{1,0:T(8,128)S(1)}, u32[]{:S(2)}, u32[]{:S(2)}) collective-permute-start(f32[1088,256]{1,0:T(8,128)S(1)} %get-tuple-element.68), channel_id=1, source_target_pairs={{4,8},{5,9},{8,12},{9,13}} | collective-permute-start | bytes 3342344 | tf_op jit(solution)/shard_map/ppermute | solution.py:482
  16.8 0.0 collective-permute-done.7.next_in
  16.8 0.0 collective-permute-done.6.own_in
  16.8 0.7 %collective-permute-start.9 = (f32[32,512]{1,0:T(8,128)S(1)}, f32[32,512]{1,0:T(8,128)S(1)}, u32[]{:S(2)}, u32[]{:S(2)}) collective-permute-start(f32[32,512]{1,0:T(8,128)S(1)} %get-tuple-element.63._lower), channel_id=1, source_target_pairs={{20,17},{21,16}} | collective-permute-start | bytes 196616 | tf_op jit(solution)/shard_map/ppermute | solution.py:390
  17.5 0.7 %collective-permute-start.8 = (f32[32,512]{1,0:T(8,128)S(1)}, f32[32,512]{1,0:T(8,128)S(1)}, u32[]{:S(2)}, u32[]{:S(2)}) collective-permute-start(f32[32,512]{1,0:T(8,128)S(1)} %get-tuple-element.63._lower), channel_id=1, source_target_pairs={{20,16},{21,17}} | collective-permute-start | bytes 196616 | tf_op jit(solution)/shard_map/ppermute | solution.py:514
  18.2 0.0 collective-permute-done.9.next_in
  18.2 0.0 collective-permute-done.8.own_in
  18.2 0.7 %collective-permute-start.11 = (f32[32,512]{1,0:T(8,128)S(1)}, f32[32,512]{1,0:T(8,128)S(1)}, u32[]{:S(2)}, u32[]{:S(2)}) collective-permute-start(f32[32,512]{1,0:T(8,128)S(1)} %get-tuple-element.65._lower), channel_id=1, source_target_pairs={{16,13},{17,12}} | collective-permute-start | bytes 196616 | tf_op jit(solution)/shard_map/ppermute | solution.py:390
  18.9 0.7 %collective-permute-start.10 = (f32[32,512]{1,0:T(8,128)S(1)}, f32[32,512]{1,0:T(8,128)S(1)}, u32[]{:S(2)}, u32[]{:S(2)}) collective-permute-start(f32[32,512]{1,0:T(8,128)S(1)} %get-tuple-element.65._lower), channel_id=1, source_target_pairs={{16,12},{17,13}} | collective-permute-start | bytes 196616 | tf_op jit(solution)/shard_map/ppermute | solution.py:514
  19.6 0.0 collective-permute-done.11.next_in
  19.6 0.0 collective-permute-done.10.own_in
  19.6 0.7 %collective-permute-start.13 = (f32[32,512]{1,0:T(8,128)S(1)}, f32[32,512]{1,0:T(8,128)S(1)}, u32[]{:S(2)}, u32[]{:S(2)}) collective-permute-start(f32[32,512]{1,0:T(8,128)S(1)} %get-tuple-element.67.rest_6_.lower), channel_id=1, source_target_pairs={{12,9},{13,8}} | collective-permute-start | bytes 196616 | tf_op jit(solution)/shard_map/ppermute | solution.py:390
  20.3 0.7 %collective-permute-start.12 = (f32[32,512]{1,0:T(8,128)S(1)}, f32[32,512]{1,0:T(8,128)S(1)}, u32[]{:S(2)}, u32[]{:S(2)}) collective-permute-start(f32[32,512]{1,0:T(8,128)S(1)} %get-tuple-element.67.rest_6_.lower), channel_id=1, source_target_pairs={{12,8},{13,9}} | collective-permute-start | bytes 196616 | tf_op jit(solution)/shard_map/ppermute | solution.py:514
  21.0 0.0 collective-permute-done.15.other_rows
  21.0 0.0 collective-permute-done.14.own_rows.rest_0_
  21.0 0.2 shard_map.56
  21.3 0.0 collective-permute-done.13.next_in
  21.3 0.0 collective-permute-done.12.own_in
  21.3 1.3 %collective-permute-start.17 = (f32[64,512]{1,0:T(8,128)S(1)}, f32[64,512]{1,0:T(8,128)S(1)}, u32[]{:S(2)}, u32[]{:S(2)}) collective-permute-start(f32[64,512]{1,0:T(8,128)S(1)} %get-tuple-element.75), channel_id=1, source_target_pairs={{8,1},{9,0}} | collective-permute-start | bytes 393224 | tf_op jit(solution)/shard_map/ppermute | solution.py:390
  22.6 1.3 %collective-permute-start.16 = (f32[64,512]{1,0:T(8,128)S(1)}, f32[64,512]{1,0:T(8,128)S(1)}, u32[]{:S(2)}, u32[]{:S(2)}) collective-permute-start(f32[64,512]{1,0:T(8,128)S(1)} %get-tuple-element.75), channel_id=1, source_target_pairs={{8,0},{9,1}} | collective-permute-start | bytes 393224 | tf_op jit(solution)/shard_map/ppermute | solution.py:510
  23.9 0.7 %collective-permute-start.19 = (f32[64,512]{1,0:T(8,128)S(1)}, f32[64,512]{1,0:T(8,128)S(1)}, u32[]{:S(2)}, u32[]{:S(2)}) collective-permute-start(f32[64,512]{1,0:T(8,128)S(1)} %shard_map.58), channel_id=1, source_target_pairs={{12,5},{13,4}} | collective-permute-start | bytes 393224 | tf_op jit(solution)/shard_map/ppermute | solution.py:390
  24.6 0.7 %collective-permute-start.18 = (f32[64,512]{1,0:T(8,128)S(1)}, f32[64,512]{1,0:T(8,128)S(1)}, u32[]{:S(2)}, u32[]{:S(2)}) collective-permute-start(f32[64,512]{1,0:T(8,128)S(1)} %shard_map.58), channel_id=1, source_target_pairs={{12,4},{13,5}} | collective-permute-start | bytes 393224 | tf_op jit(solution)/shard_map/ppermute | solution.py:526
  25.3 25.3 %collective-permute-done.17.rest_1_ = f32[64,512]{1,0:T(8,128)S(1)} collective-permute-done((f32[64,512]{1,0:T(8,128)S(1)}, f32[64,512]{1,0:T(8,128)S(1)}, u32[]{:S(2)}, u32[]{:S(2)}) %collective-permute-start.17) | collective-permute-done | bytes 131104 | tf_op jit(solution)/shard_map/ppermute | solution.py:390
  50.5 1.0 %collective-permute-done.16.rest_0_ = f32[64,512]{1,0:T(8,128)S(1)} collective-permute-done((f32[64,512]{1,0:T(8,128)S(1)}, f32[64,512]{1,0:T(8,128)S(1)}, u32[]{:S(2)}, u32[]{:S(2)}) %collective-permute-start.16) | collective-permute-done | bytes 131104 | tf_op jit(solution)/shard_map/ppermute | solution.py:510
  51.6 0.3 shard_map.59
  51.9 1.3 %collective-permute-start.20 = (f32[32,512]{1,0:T(8,128)S(1)}, f32[32,512]{1,0:T(8,128)S(1)}, u32[]{:S(2)}, u32[]{:S(2)}) collective-permute-start(f32[32,512]{1,0:T(8,128)S(1)} %get-tuple-element.80), channel_id=1, source_target_pairs={{0,2},{1,3},{4,6},{5,7},{8,10},{9,11},{12,14},{13,15},{16,18},{17,... | collective-permute-start | bytes 196616 | tf_op jit(solution)/shard_map/ppermute | solution.py:557
  53.2 0.5 shard_map.60
  53.7 0.4 collective-permute-done.20
  54.1 0.6 %select_bitcast_fusion = f32[1,32,512]{2,1,0:T(8,128)} fusion(f32[32,512]{1,0:T(8,128)S(1)} %shard_map.60, f32[32,512]{1,0:T(8,128)S(1)} %collective-permute-done.20, pred[]{:T(512)S(6)} %eq.5), kind=kLoop, calls=%fused_computation | loop fusion | flops 16384 | bytes 196609 | tf_op jit(solution)/shard_map/broadcast_in_dim | solution.py:567
  (13 shorter events, 0.2 us)
Async XLA Ops:
  1.5 4.7 %collective-permute-start.3 = (f32[32,512]{1,0:T(8,128)S(1)}, f32[32,512]{1,0:T(8,128)S(1)}, u32[]{:S(2)}, u32[]{:S(2)}) collective-permute-start(f32[32,512]{1,0:T(8,128)S(1)} %get-tuple-element.44.const), channel_id=1, source_target_pairs={{30,29},{31,28}} | collective-permute-start | bytes 196616 | tf_op jit(solution)/shard_map/ppermute | solution.py:390
  2.2 4.0 %collective-permute-start.2 = (f32[32,512]{1,0:T(8,128)S(1)}, f32[32,512]{1,0:T(8,128)S(1)}, u32[]{:S(2)}, u32[]{:S(2)}) collective-permute-start(f32[32,512]{1,0:T(8,128)S(1)} %get-tuple-element.44.const), channel_id=1, source_target_pairs={{30,28},{31,29}} | collective-permute-start | bytes 196616 | tf_op jit(solution)/shard_map/ppermute | solution.py:423
  3.6 7.9 %collective-permute-start = (f32[1,544,128]{2,1,0:T(8,128)S(1)}, f32[1,544,128]{2,1,0:T(8,128)S(1)}, u32[]{:S(2)}, u32[]{:S(2)}) collective-permute-start(f32[1,544,128]{2,1,0:T(8,128)S(1)} %get-tuple-element.49), channel_id=1, source_target_pairs={{2,1},{3,0},{6,5},{7,4},{10,9},{11,8},{14,13},{15,12},{18,17},{19,... | collective-permute-start | bytes 835592 | tf_op jit(solution)/shard_map/ppermute | solution.py:390
  4.9 7.2 %collective-permute-start.1 = (f32[1088,256]{1,0:T(8,128)S(1)}, f32[1088,256]{1,0:T(8,128)S(1)}, u32[]{:S(2)}, u32[]{:S(2)}) collective-permute-start(f32[1088,256]{1,0:T(8,128)S(1)} %get-tuple-element.50), channel_id=1, source_target_pairs={{2,0},{3,1},{6,4},{7,5},{10,8},{11,9},{14,12},{15,13},{18,16},{19,... | collective-permute-start | bytes 3342344 | tf_op jit(solution)/shard_map/ppermute | solution.py:445
  6.3 6.0 %collective-permute-start.5 = (f32[32,512]{1,0:T(8,128)S(1)}, f32[32,512]{1,0:T(8,128)S(1)}, u32[]{:S(2)}, u32[]{:S(2)}) collective-permute-start(f32[32,512]{1,0:T(8,128)S(1)} %get-tuple-element.58._lower), channel_id=1, source_target_pairs={{28,25},{29,24}} | collective-permute-start | bytes 196616 | tf_op jit(solution)/shard_map/ppermute | solution.py:390
  6.9 5.3 %collective-permute-start.4 = (f32[32,512]{1,0:T(8,128)S(1)}, f32[32,512]{1,0:T(8,128)S(1)}, u32[]{:S(2)}, u32[]{:S(2)}) collective-permute-start(f32[32,512]{1,0:T(8,128)S(1)} %get-tuple-element.58._lower), channel_id=1, source_target_pairs={{28,24},{29,25}} | collective-permute-start | bytes 196616 | tf_op jit(solution)/shard_map/ppermute | solution.py:514
  12.4 4.4 %collective-permute-start.7 = (f32[32,512]{1,0:T(8,128)S(1)}, f32[32,512]{1,0:T(8,128)S(1)}, u32[]{:S(2)}, u32[]{:S(2)}) collective-permute-start(f32[32,512]{1,0:T(8,128)S(1)} %get-tuple-element.61._lower), channel_id=1, source_target_pairs={{24,21},{25,20}} | collective-permute-start | bytes 196616 | tf_op jit(solution)/shard_map/ppermute | solution.py:390
  13.0 3.8 %collective-permute-start.6 = (f32[32,512]{1,0:T(8,128)S(1)}, f32[32,512]{1,0:T(8,128)S(1)}, u32[]{:S(2)}, u32[]{:S(2)}) collective-permute-start(f32[32,512]{1,0:T(8,128)S(1)} %get-tuple-element.61._lower), channel_id=1, source_target_pairs={{24,20},{25,21}} | collective-permute-start | bytes 196616 | tf_op jit(solution)/shard_map/ppermute | solution.py:514
  15.4 5.6 %collective-permute-start.15 = (f32[512,256]{1,0:T(8,128)S(1)}, f32[512,256]{1,0:T(8,128)S(1)}, u32[]{:S(2)}, u32[]{:S(2)}) collective-permute-start(f32[512,256]{1,0:T(8,128)S(1)} %get-tuple-element.69), channel_id=1, source_target_pairs={{4,9},{5,8},{8,13},{9,12}} | collective-permute-start | bytes 1572872 | tf_op jit(solution)/shard_map/ppermute | solution.py:390
  16.1 4.9 %collective-permute-start.14 = (f32[1088,256]{1,0:T(8,128)S(1)}, f32[1088,256]{1,0:T(8,128)S(1)}, u32[]{:S(2)}, u32[]{:S(2)}) collective-permute-start(f32[1088,256]{1,0:T(8,128)S(1)} %get-tuple-element.68), channel_id=1, source_target_pairs={{4,8},{5,9},{8,12},{9,13}} | collective-permute-start | bytes 3342344 | tf_op jit(solution)/shard_map/ppermute | solution.py:482
  16.8 1.3 %collective-permute-start.9 = (f32[32,512]{1,0:T(8,128)S(1)}, f32[32,512]{1,0:T(8,128)S(1)}, u32[]{:S(2)}, u32[]{:S(2)}) collective-permute-start(f32[32,512]{1,0:T(8,128)S(1)} %get-tuple-element.63._lower), channel_id=1, source_target_pairs={{20,17},{21,16}} | collective-permute-start | bytes 196616 | tf_op jit(solution)/shard_map/ppermute | solution.py:390
  17.5 0.7 %collective-permute-start.8 = (f32[32,512]{1,0:T(8,128)S(1)}, f32[32,512]{1,0:T(8,128)S(1)}, u32[]{:S(2)}, u32[]{:S(2)}) collective-permute-start(f32[32,512]{1,0:T(8,128)S(1)} %get-tuple-element.63._lower), channel_id=1, source_target_pairs={{20,16},{21,17}} | collective-permute-start | bytes 196616 | tf_op jit(solution)/shard_map/ppermute | solution.py:514
  18.2 1.3 %collective-permute-start.11 = (f32[32,512]{1,0:T(8,128)S(1)}, f32[32,512]{1,0:T(8,128)S(1)}, u32[]{:S(2)}, u32[]{:S(2)}) collective-permute-start(f32[32,512]{1,0:T(8,128)S(1)} %get-tuple-element.65._lower), channel_id=1, source_target_pairs={{16,13},{17,12}} | collective-permute-start | bytes 196616 | tf_op jit(solution)/shard_map/ppermute | solution.py:390
  18.9 0.7 %collective-permute-start.10 = (f32[32,512]{1,0:T(8,128)S(1)}, f32[32,512]{1,0:T(8,128)S(1)}, u32[]{:S(2)}, u32[]{:S(2)}) collective-permute-start(f32[32,512]{1,0:T(8,128)S(1)} %get-tuple-element.65._lower), channel_id=1, source_target_pairs={{16,12},{17,13}} | collective-permute-start | bytes 196616 | tf_op jit(solution)/shard_map/ppermute | solution.py:514
  19.6 1.6 %collective-permute-start.13 = (f32[32,512]{1,0:T(8,128)S(1)}, f32[32,512]{1,0:T(8,128)S(1)}, u32[]{:S(2)}, u32[]{:S(2)}) collective-permute-start(f32[32,512]{1,0:T(8,128)S(1)} %get-tuple-element.67.rest_6_.lower), channel_id=1, source_target_pairs={{12,9},{13,8}} | collective-permute-start | bytes 196616 | tf_op jit(solution)/shard_map/ppermute | solution.py:390
  20.3 1.0 %collective-permute-start.12 = (f32[32,512]{1,0:T(8,128)S(1)}, f32[32,512]{1,0:T(8,128)S(1)}, u32[]{:S(2)}, u32[]{:S(2)}) collective-permute-start(f32[32,512]{1,0:T(8,128)S(1)} %get-tuple-element.67.rest_6_.lower), channel_id=1, source_target_pairs={{12,8},{13,9}} | collective-permute-start | bytes 196616 | tf_op jit(solution)/shard_map/ppermute | solution.py:514
  21.3 29.2 %collective-permute-start.17 = (f32[64,512]{1,0:T(8,128)S(1)}, f32[64,512]{1,0:T(8,128)S(1)}, u32[]{:S(2)}, u32[]{:S(2)}) collective-permute-start(f32[64,512]{1,0:T(8,128)S(1)} %get-tuple-element.75), channel_id=1, source_target_pairs={{8,1},{9,0}} | collective-permute-start | bytes 393224 | tf_op jit(solution)/shard_map/ppermute | solution.py:390
  22.6 29.0 %collective-permute-start.16 = (f32[64,512]{1,0:T(8,128)S(1)}, f32[64,512]{1,0:T(8,128)S(1)}, u32[]{:S(2)}, u32[]{:S(2)}) collective-permute-start(f32[64,512]{1,0:T(8,128)S(1)} %get-tuple-element.75), channel_id=1, source_target_pairs={{8,0},{9,1}} | collective-permute-start | bytes 393224 | tf_op jit(solution)/shard_map/ppermute | solution.py:510
  23.9 27.7 %collective-permute-start.19 = (f32[64,512]{1,0:T(8,128)S(1)}, f32[64,512]{1,0:T(8,128)S(1)}, u32[]{:S(2)}, u32[]{:S(2)}) collective-permute-start(f32[64,512]{1,0:T(8,128)S(1)} %shard_map.58), channel_id=1, source_target_pairs={{12,5},{13,4}} | collective-permute-start | bytes 393224 | tf_op jit(solution)/shard_map/ppermute | solution.py:390
  24.6 27.0 %collective-permute-start.18 = (f32[64,512]{1,0:T(8,128)S(1)}, f32[64,512]{1,0:T(8,128)S(1)}, u32[]{:S(2)}, u32[]{:S(2)}) collective-permute-start(f32[64,512]{1,0:T(8,128)S(1)} %shard_map.58), channel_id=1, source_target_pairs={{12,4},{13,5}} | collective-permute-start | bytes 393224 | tf_op jit(solution)/shard_map/ppermute | solution.py:526
  51.9 2.2 %collective-permute-start.20 = (f32[32,512]{1,0:T(8,128)S(1)}, f32[32,512]{1,0:T(8,128)S(1)}, u32[]{:S(2)}, u32[]{:S(2)}) collective-permute-start(f32[32,512]{1,0:T(8,128)S(1)} %get-tuple-element.80), channel_id=1, source_target_pairs={{0,2},{1,3},{4,6},{5,7},{8,10},{9,11},{12,14},{13,15},{16,18},{17,... | collective-permute-start | bytes 196616 | tf_op jit(solution)/shard_map/ppermute | solution.py:557

commit v8 on v7

--- a/solution.py
+++ b/solution.py
@@ -49,16 +49,11 @@
         rim[1] = columns(False)
 
 
-def const_kernel(
-    mask, normals, inv, lag, const, inv_high, inv_low, lag_out, mask_out, normals_in, inv_in, sems
-):
+def const_kernel(normals, inv, const, inv_high, inv_low, normals_in, inv_in, sems):
     blocks, length = inv.shape[1], inv.shape[2]
     moves = [pltpu.make_async_copy(normals.at[0], normals_in, sems.at[0])]
     for b in range(blocks):
         moves.append(pltpu.make_async_copy(inv.at[0, b], inv_in.at[b], sems.at[1 + b]))
-    for b in range(blocks):
-        moves.append(pltpu.make_async_copy(lag.at[0, b], lag_out.at[b], sems.at[1 + blocks + b]))
-    moves.append(pltpu.make_async_copy(mask.at[0], mask_out, sems.at[1 + 2 * blocks]))
     for move in moves:
         move.start()
     moves[0].wait()
@@ -68,23 +63,21 @@
         moves[1 + b].wait()
         inv_high[b], inv_low[b] = halves(inv_in[b])
         const[:, at] = triple(high, low, inv_high[b], inv_low[b])
-    for move in moves[1 + blocks :]:
-        move.wait()
 
 
 def fuse_kernel(mask, const, inv_high, inv_low, lag, own, near_high, near_low):
-    blocks, window, length = lag.shape
+    blocks, window, length = lag.shape[1:]
     edge = (window - length) // 2
     cols = const.shape[0]
     cuts = (0, edge, edge + length, window)
-    flags = mask[...].astype(jnp.float32)
+    flags = mask[0].astype(jnp.float32)
     for b in range(blocks):
         at = blocks * window + b * cols
         own[at : at + cols] = const[:, b * length : (b + 1) * length]
         for part in range(3):
             lo, hi = cuts[part], cuts[part + 1]
             rows = slice(b * window + lo, b * window + hi)
-            high, low = halves(lag[b, lo:hi] * flags[b : b + 1, part : part + 1])
+            high, low = halves(lag[0, b, lo:hi] * flags[b : b + 1, part : part + 1])
             value = triple(high, low, inv_high[b], inv_low[b])
             own[rows] = value
             near_high[rows], near_low[rows] = halves(value)
@@ -203,7 +196,6 @@
 
 def load(sides, pick, own, halo, ref):
     sites = own.shape[1]
-    ref[...] = jnp.zeros_like(ref)
     keep(ref, halo, own)
     for side in range(sides):
         on_right = 1 - jnp.minimum(lax.axis_index("row"), 1).astype(jnp.int32) if sides == 1 else side
@@ -224,6 +216,7 @@
 
     @pl.when(lax.axis_index("tm") == 2 * mine)
     def _():
+        mid[...] = jnp.zeros_like(mid)
         load(sides, plain(next_in), own_in[...], edge, mid)
         upper[...] = own_in[...]
         for b in range(blocks):
@@ -283,51 +276,70 @@
     other_high[...], other_low[...] = halves(other_rows[...])
 
 
-def add_parts(lower, own_rows, own_high, own_low, other_high, other_low, parts, mid, span):
+def add_parts(lower, own_rows, own_high, own_low, other_high, other_low, to_next, to_own, mid, far_mid, span):
     cols, sites = lower.shape
     length = own_rows.shape[1]
     blocks = sites // length
+    halo = to_own.shape[1] - sites
+    edge = halo - length
+    row = lax.axis_index("row")
     keep(mid, 0, lower[...])
+    near = pl.multiple_of(jnp.where(row == 0, sites - halo, 0), edge)
     for b in range(blocks):
         at, rows = slice(b * length, (b + 1) * length), slice(b * sites, (b + 1) * sites)
         const = slice(blocks * sites + b * cols, blocks * sites + (b + 1) * cols)
-        parts[:cols, at] = own_rows[const] + stacked_dot(mid, slice(0, sites), own_high[rows], own_low[rows])
-    for last in (True, False):
-
-        @pl.when((lax.axis_index("row") == 0) != last)
-        def _():
-            for b, (lo, hi, packed) in enumerate(cuts_of(blocks, length, sites, span, last)):
-                from_sites = slice(0, hi - lo) if last else slice(sites - (hi - lo), sites)
-                rows = slice(packed, packed + hi - lo)
-                parts[cols:, b * length : (b + 1) * length] = stacked_dot(
-                    mid, from_sites, other_high[rows], other_low[rows]
-                )
+        to_own[:, at] = own_rows[const] + stacked_dot(mid, slice(0, sites), own_high[rows], own_low[rows])
+    to_next[:, :halo] = to_own[:, pl.ds(near, halo)]
+    for b in range(blocks):
+        value = None
+        cuts = [cuts_of(blocks, length, sites, span, last)[b] for last in (True, False)]
+        for chunk in range(0, max(hi - lo for lo, hi, _ in cuts), edge):
+            starts, froms, there = [], [], []
+            for last, (lo, hi, packed) in zip((True, False), cuts):
+                count = hi - lo
+                there.append(chunk < count)
+                starts.append(packed + chunk if chunk < count else 0)
+                froms.append((0 if last else sites - count) + chunk if chunk < count else 0)
+            start = pl.multiple_of(jnp.where(row == 0, starts[1], starts[0]), edge)
+            source = pl.multiple_of(jnp.where(row == 0, froms[1], froms[0]), edge)
+            rows = pl.ds(start, edge)
+            product = stacked_dot(mid, pl.ds(source, edge), other_high[rows], other_low[rows])
+            if not all(there):
+                product = jnp.where((row == 0) == there[1], product, 0.0)
+            value = product if value is None else value + product
+        far_mid[:, b * length : (b + 1) * length] = value
+    to_next[:, halo:] = far_mid[...]
+    away = pl.multiple_of(jnp.where(row == 0, 0, sites - halo), edge)
+    to_own[:, sites:] = far_mid[:, pl.ds(away, halo)]
 
 
 def jump_kernel(mine, sides, own_in, next_in, both, high, low, *rest):
-    ship, (_late, _lower, late, lower, parts, mid) = rest[:-6], rest[-6:]
+    ship, (_late, _lower, late, lower, to_next, to_own, to_last, *scratch) = rest[:-9], rest[-9:]
 
     @pl.when(lax.axis_index("tm") == 2 * mine)
     def _():
         load(sides, plain(next_in), own_in[...], (late.shape[1] - own_in.shape[1]) // 2, late)
         step(both, high, low, late, lower)
-        add_parts(lower, *ship, parts, mid, high.shape[0] * high.shape[1] // own_in.shape[1])
+        add_parts(lower, *ship, to_next, to_own, *scratch, high.shape[0] * high.shape[1] // own_in.shape[1])
+        to_last[...] = to_next[...]
 
     @pl.when(lax.axis_index("tm") != 2 * mine)
     def _():
-        parts[...] = jnp.zeros_like(parts)
+        for part in (to_next, to_own, to_last):
+            part[...] = jnp.zeros_like(part)
 
 
 def parts_kernel(mine, span, lower, *rest):
-    ship, (parts, mid) = rest[:-2], rest[-2:]
+    ship, parts = rest[:-4], rest[-4:]
 
     @pl.when(lax.axis_index("tm") == 2 * mine)
     def _():
-        add_parts(lower, *ship, parts, mid, span)
+        add_parts(lower, *ship, *parts, span)
 
     @pl.when(lax.axis_index("tm") != 2 * mine)
     def _():
-        parts[...] = jnp.zeros_like(parts)
+        for part in parts[:2]:
+            part[...] = jnp.zeros_like(part)
 
 
 def last_kernel(jumps, both, high, low, late, _lower, lower):
@@ -343,19 +355,22 @@
     window = far_high.shape[0] // blocks
     halo = (late.shape[1] - sites) // 2
     at_window = halo - (window - length) // 2
-
-    def take(mine, own_in, next_in):
+    messages = rest[:-7]
+
+    if len(messages) == 2:
+
+        @pl.when(lax.axis_index("tm") == 0)
+        def _():
+            load(sides, plain(messages[1]), messages[0][...], halo, late)
+
+    for mine, (*next_in, own_in) in enumerate(((messages[0], messages[2], messages[1]), messages[3:]) if len(messages) > 2 else ()):
+
         @pl.when(lax.axis_index("tm") == 2 * mine)
         def _():
-            if own_in.shape[0] == cols:
-                load(sides, plain(next_in), own_in[...], halo, late)
-            else:
-                own = own_in[:cols] + next_in[cols:]
-                load(sides, lambda side, cut: next_in[:cols, cut] + own_in[cols:, cut], own, halo, late)
-
-    messages = rest[:-7]
-    for mine in range(len(messages) // 2):
-        take(mine, *messages[2 * mine : 2 * mine + 2])
+            from_next = next_in[0][...] + next_in[1][...] if len(next_in) == 2 else next_in[0][...]
+            own = own_in[:, :sites] + from_next[:, halo:]
+            near = own_in[:, sites:] + from_next[:, :halo]
+            load(sides, lambda side, cut: near, own, halo, late)
 
     @pl.when(lax.axis_index("tm") != 2 * top)
     def _():
@@ -402,22 +417,22 @@
     tall = blocks * window
     jump = 2
     jumps = rows == 2 and pairs > 5
-    const, inv_high, inv_low, lag, mask = pl.pallas_call(
+    const, inv_high, inv_low = pl.pallas_call(
         const_kernel,
         out_shape=(
             shape((cols, sites), f32),
             shape((blocks, length, length), bf16), shape((blocks, length, length), bf16),
-            shape(lag_coupling.shape[1:], f32), shape(fill_mask.shape[1:], fill_mask.dtype),
         ),
-        in_specs=[HBM] * 4,
-        out_specs=(VMEM,) * 5,
+        in_specs=[HBM] * 2,
+        out_specs=(VMEM,) * 3,
         scratch_shapes=[
             pltpu.VMEM(normals.shape[1:], f32),
             pltpu.VMEM(inv_diag.shape[1:], f32),
-            pltpu.SemaphoreType.DMA((2 + 2 * blocks,)),
+            pltpu.SemaphoreType.DMA((1 + blocks,)),
         ],
         compiler_params=PARAMS,
-    )(*[pltpu.with_memory_space_constraint(a, pltpu.HBM) for a in (fill_mask, normals, inv_diag, lag_coupling)])
+        cost_estimate=pl.CostEstimate(flops=5*10**9, bytes_accessed=0, transcendentals=0),
+    )(*[pltpu.with_memory_space_constraint(a, pltpu.HBM) for a in (normals, inv_diag)])
     odd, even = range(1, times, 2), range(0, times, 2)
     first_next = cross(const, odd[-1:], even[-1:])
     first_own = lax.ppermute(const, BOTH, link(odd[-1:], even[-1:]))
@@ -432,7 +447,7 @@
         cost_estimate=pl.CostEstimate(
             flops=6 * (tall + cols * blocks) * length * length, bytes_accessed=16 * tall * length, transcendentals=0
         ),
-    )(mask, const, inv_high, inv_low, lag)
+    )(fill_mask, const, inv_high, inv_low, lag_coupling)
     near, edges = pl.pallas_call(
         functools.partial(edge_kernel, sides, blocks, cols),
         out_shape=(shape(near.shape, f32), shape((sides, window + cols, edge), f32)),
@@ -501,13 +516,16 @@
             cost_estimate=pl.CostEstimate(flops=flops, bytes_accessed=0, transcendentals=0) if flops else None,
         )(*given, *state)
 
+    parts = (shape((cols, sites + halo), f32),) * 2
+    parts_scratch = [pltpu.VMEM((2 * cols, sites), bf16), pltpu.VMEM((cols, sites), f32)]
     late = jnp.zeros((2 * cols, sites + 2 * halo), bf16)
     mine = pairs - 1
     while mine > 0:
         if jumps and mine == jump:
             source, target = [2 * mine], [2 * mine - 4]
-            next_in = cross(parts, source, target)
-            own_in = lax.ppermute(parts, BOTH, link(source, target))
+            first_in = lax.ppermute(to_next, BOTH, [(2 * source[0] + 1, 2 * target[0])])
+            own_in = lax.ppermute(to_own, BOTH, link(source, target))
+            next_in = lax.ppermute(to_last, BOTH, [(2 * source[0], 2 * target[0] + 1)])
             break
         source, target = [2 * mine], [2 * mine - 2]
         next_in = cross(lower, source, target)
@@ -515,15 +533,15 @@
         if jumps and mine == jump + 1:
             beside = pl.pallas_call(
                 functools.partial(parts_kernel, mine, 2 * window),
-                out_shape=shape((2 * cols, sites), f32),
+                out_shape=parts,
                 in_specs=[VMEM] * 6,
-                out_specs=VMEM,
-                scratch_shapes=[pltpu.VMEM((2 * cols, sites), bf16)],
+                out_specs=(VMEM,) * 2,
+                scratch_shapes=parts_scratch,
                 compiler_params=PARAMS,
             )(lower, own_rows, *ship)
             source, target = [2 * mine], [2 * mine - 4]
-            beside_next = cross(beside, source, target)
-            beside_own = lax.ppermute(beside, BOTH, link(source, target))
+            beside_next = cross(beside[0], source, target)
+            beside_own = lax.ppermute(beside[1], BOTH, link(source, target))
         mine -= 1
         if mine == 0:
             break
@@ -535,12 +553,12 @@
                 [pltpu.VMEM((2 * cols, sites + 2 * edge), bf16)],
             )
         elif jumps and mine == jump:
-            late, lower, parts = turn(
+            late, lower, to_next, to_own, to_last = turn(
                 functools.partial(jump_kernel, mine, sides),
                 (own_in, next_in, both, high, low, own_rows, *ship),
                 (late, lower),
-                [pltpu.VMEM((2 * cols, sites), bf16)],
-                [shape((2 * cols, sites), f32)],
+                parts_scratch,
+                parts + parts[:1],
             )
         else:
             early = jumps and mine == pairs - 3
@@ -550,7 +568,7 @@
                 (late, lower),
                 flops=50 * 10**9 if early else 0,
             )
-    given = (own_in, next_in) + ((beside_own, beside_next) if jumps else ())
+    given = (first_in, own_in, next_in, beside_next, beside_own) if jumps else (own_in, next_in)
     late, upper = turn(
         functools.partial(upper_kernel, sides, pairs - 1), (*given, far, far_high, far_low), (late, upper)
     )

time: 55.1 us -> 54.6 us (level)
  waiting for transfers between devices: 31.2 us -> 29.6 us
  starting transfers between devices: 17.2 us -> 17.9 us
    ppermute x10 -> x9, waiting for transfers between devices: 29.2 us -> 3.88 us  [cross(): return lax.ppermute(value, BOTH, perm)]
    ppermute x2 -> x4, waiting for transfers between devices: 1.05 us -> 24.7 us  [the longest x1 24.3 us: local(): first_in = lax.ppermute(to_next, BOTH, [(2 * source[0] + 1, 2 * target[0])])]
    ppermute x2 -> x4, starting transfers between devices: 1.96 us -> 3.92 us  [the longest x1 1.29 us: local(): first_in = lax.ppermute(to_next, BOTH, [(2 * source[0] + 1, 2 * target[0])])]
    ppermute x10 -> x9, starting transfers between devices: 7.94 us -> 6.64 us  [cross(): return lax.ppermute(value, BOTH, perm)]
  transfers between devices with their start and end apart: 21 -> 22, of which waited for: 5 -> 5; matrix products, arithmetic and copies ran while one was open for 0% -> 0% of each run, Pallas kernels for 6% -> 6%
where the time goes in v8:
time: 54.6 us; the launch traced here: 53.9 us
  waiting for transfers between devices  29.6 us (54%)
  starting transfers between devices  17.9 us (33%)
  Pallas kernels  5.3 us (10%)
  other arithmetic  0.64 us (1%)
    ppermute x1, waiting for transfers between devices, local(): first_in = lax.ppermute(to_next, BOTH, [(2 * source[0] + 1, 2 * target[0])])  24.3 us
    ppermute x9, starting transfers between devices, cross(): return lax.ppermute(value, BOTH, perm)  6.64 us
    ppermute x9, waiting for transfers between devices, cross(): return lax.ppermute(value, BOTH, perm)  3.88 us
    ppermute x5, starting transfers between devices, local(): own_in = lax.ppermute(lower, BOTH, link(source, target))  3.32 us
    pallas_call x1, Pallas kernels, local(): pl.pallas_call(functools.partial(pair_kernel, jumps), out_shape=(shape((2...  1.65 us
    pallas_call x1, Pallas kernels, local(): pl.pallas_call(const_kernel, out_shape=(shape((cols, sites), f32), shape(...  1.56 us
    ppermute x1, starting transfers between devices, local(): first_in = lax.ppermute(to_next, BOTH, [(2 * source[0] + 1, 2 * target[0])])  1.29 us
    ppermute x1, starting transfers between devices, local(): own_in = lax.ppermute(to_own, BOTH, link(source, target))  1.29 us
  transfers between devices with their start and end apart: 22, of which 5 were waited for; matrix products, arithmetic and copies ran while one was open for 0% of the time, Pallas kernels for 6%

profile of v8, /device:TPU:0, one launch (start us, length us, event | category | flops | bytes accessed | tf_op | source)
XLA Modules:
  0.0 53.9 jit_solution(16455927852339925547)
XLA Ops:
  0.0 1.6 %shard_map.46 = (f32[32,512]{1,0:T(8,128)S(1)}, bf16[2,256,256]{2,1,0:T(8,128)(2,1)S(1)}, bf16[2,256,256]{2,1,0:T(8,128)(2,1)S(1)}) custom-call(f32[1,32,512]{2,1,0:T(8,128)} %normals.1, f32[1,2,256,256]{3,2,1,0:T(8,128)} %inv.1), custom_call_target="tpu_custom_call" | custom-call | flops 5000000000 | tf_op jit(solution)/shard_map/pallas_call | solution.py:420
  1.6 0.7 %collective-permute-start.3 = (f32[32,512]{1,0:T(8,128)S(1)}, f32[32,512]{1,0:T(8,128)S(1)}, u32[]{:S(2)}, u32[]{:S(2)}) collective-permute-start(f32[32,512]{1,0:T(8,128)S(1)} %get-tuple-element.45.const), channel_id=1, source_target_pairs={{30,29},{31,28}} | collective-permute-start | bytes 196616 | tf_op jit(solution)/shard_map/ppermute | solution.py:405
  2.2 0.7 %collective-permute-start.2 = (f32[32,512]{1,0:T(8,128)S(1)}, f32[32,512]{1,0:T(8,128)S(1)}, u32[]{:S(2)}, u32[]{:S(2)}) collective-permute-start(f32[32,512]{1,0:T(8,128)S(1)} %get-tuple-element.45.const), channel_id=1, source_target_pairs={{30,28},{31,29}} | collective-permute-start | bytes 196616 | tf_op jit(solution)/shard_map/ppermute | solution.py:438
  2.9 0.7 %shard_map.47 = (f32[1088,256]{1,0:T(8,128)S(1)}, bf16[1024,256]{1,0:T(8,128)(2,1)S(1)}, bf16[1024,256]{1,0:T(8,128)(2,1)S(1)}) custom-call(s32[1,2,3]{2,1,0:T(2,128)S(1)} %copy-done.1, f32[32,512]{1,0:T(8,128)S(1)} %get-tuple-element.45.const, bf16[2,256,256]{2,1,0:T(8,128)(2,1)S(1)} %get-tuple-element.46.inv_high, ...), custom_call_target="tpu_custom_call" | custom-call | flops 427819008 | bytes 4194304 | tf_op jit(solution)/shard_map/pallas_call | solution.py:439
  3.7 1.3 %collective-permute-start = (f32[1,544,128]{2,1,0:T(8,128)S(1)}, f32[1,544,128]{2,1,0:T(8,128)S(1)}, u32[]{:S(2)}, u32[]{:S(2)}) collective-permute-start(f32[1,544,128]{2,1,0:T(8,128)S(1)} %get-tuple-element.49), channel_id=1, source_target_pairs={{2,1},{3,0},{6,5},{7,4},{10,9},{11,8},{14,13},{15,12},{18,17},{19,... | collective-permute-start | bytes 835592 | tf_op jit(solution)/shard_map/ppermute | solution.py:405
  5.0 1.3 %collective-permute-start.1 = (f32[1088,256]{1,0:T(8,128)S(1)}, f32[1088,256]{1,0:T(8,128)S(1)}, u32[]{:S(2)}, u32[]{:S(2)}) collective-permute-start(f32[1088,256]{1,0:T(8,128)S(1)} %get-tuple-element.50), channel_id=1, source_target_pairs={{2,0},{3,1},{6,4},{7,5},{10,8},{11,9},{14,12},{15,13},{18,16},{19,... | collective-permute-start | bytes 3342344 | tf_op jit(solution)/shard_map/ppermute | solution.py:460
  6.3 0.0 collective-permute-done.3.next_in
  6.3 0.0 collective-permute-done.2.own_in
  6.4 0.7 %collective-permute-start.5 = (f32[32,512]{1,0:T(8,128)S(1)}, f32[32,512]{1,0:T(8,128)S(1)}, u32[]{:S(2)}, u32[]{:S(2)}) collective-permute-start(f32[32,512]{1,0:T(8,128)S(1)} %get-tuple-element.58._lower), channel_id=1, source_target_pairs={{28,25},{29,24}} | collective-permute-start | bytes 196616 | tf_op jit(solution)/shard_map/ppermute | solution.py:405
  7.0 0.7 %collective-permute-start.4 = (f32[32,512]{1,0:T(8,128)S(1)}, f32[32,512]{1,0:T(8,128)S(1)}, u32[]{:S(2)}, u32[]{:S(2)}) collective-permute-start(f32[32,512]{1,0:T(8,128)S(1)} %get-tuple-element.58._lower), channel_id=1, source_target_pairs={{28,24},{29,25}} | collective-permute-start | bytes 196616 | tf_op jit(solution)/shard_map/ppermute | solution.py:532
  7.7 3.9 %collective-permute-done.rim = f32[1,544,128]{2,1,0:T(8,128)S(1)} collective-permute-done((f32[1,544,128]{2,1,0:T(8,128)S(1)}, f32[1,544,128]{2,1,0:T(8,128)S(1)}, u32[]{:S(2)}, u32[]{:S(2)}) %collective-permute-start) | collective-permute-done | bytes 278560 | tf_op jit(solution)/shard_map/ppermute | solution.py:405
  11.6 0.6 %collective-permute-done.1.far.rest_5_ = f32[1088,256]{1,0:T(8,128)S(1)} collective-permute-done((f32[1088,256]{1,0:T(8,128)S(1)}, f32[1088,256]{1,0:T(8,128)S(1)}, u32[]{:S(2)}, u32[]{:S(2)}) %collective-permute-start.1) | collective-permute-done | bytes 1114144 | tf_op jit(solution)/shard_map/ppermute | solution.py:460
  12.2 0.2 shard_map.49
  12.4 0.0 collective-permute-done.5.next_in
  12.4 0.0 collective-permute-done.4.own_in
  12.4 0.7 %collective-permute-start.7 = (f32[32,512]{1,0:T(8,128)S(1)}, f32[32,512]{1,0:T(8,128)S(1)}, u32[]{:S(2)}, u32[]{:S(2)}) collective-permute-start(f32[32,512]{1,0:T(8,128)S(1)} %get-tuple-element.61._lower), channel_id=1, source_target_pairs={{24,21},{25,20}} | collective-permute-start | bytes 196616 | tf_op jit(solution)/shard_map/ppermute | solution.py:405
  13.1 0.7 %collective-permute-start.6 = (f32[32,512]{1,0:T(8,128)S(1)}, f32[32,512]{1,0:T(8,128)S(1)}, u32[]{:S(2)}, u32[]{:S(2)}) collective-permute-start(f32[32,512]{1,0:T(8,128)S(1)} %get-tuple-element.61._lower), channel_id=1, source_target_pairs={{24,20},{25,21}} | collective-permute-start | bytes 196616 | tf_op jit(solution)/shard_map/ppermute | solution.py:532
  13.8 1.6 %shard_map.50 = (bf16[2048,256]{1,0:T(8,128)(2,1)S(1)}, bf16[2048,256]{1,0:T(8,128)(2,1)S(1)}, f32[32,512]{1,0:T(8,128)S(1)}, f32[1088,256]{1,0:T(8,128)S(1)}, f32[512,256]{1,0:T(8,128)S(1)}) custom-call(f32[1,544,128]{2,1,0:T(8,128)S(1)} %collective-permute-done.rim, f32[1088,256]{1,0:T(8,128)S(1)} %collective-permute-done.1.far.rest_5_, ...), custom_call_target="tpu_custom_call" | custom-call | flops 1000000000 | tf_op jit(solution)/shard_map/pallas_call | solution.py:484
  15.4 0.7 %collective-permute-start.15 = (f32[512,256]{1,0:T(8,128)S(1)}, f32[512,256]{1,0:T(8,128)S(1)}, u32[]{:S(2)}, u32[]{:S(2)}) collective-permute-start(f32[512,256]{1,0:T(8,128)S(1)} %get-tuple-element.69), channel_id=1, source_target_pairs={{4,9},{5,8},{8,13},{9,12}} | collective-permute-start | bytes 1572872 | tf_op jit(solution)/shard_map/ppermute | solution.py:405
  16.1 0.7 %collective-permute-start.14 = (f32[1088,256]{1,0:T(8,128)S(1)}, f32[1088,256]{1,0:T(8,128)S(1)}, u32[]{:S(2)}, u32[]{:S(2)}) collective-permute-start(f32[1088,256]{1,0:T(8,128)S(1)} %get-tuple-element.68), channel_id=1, source_target_pairs={{4,8},{5,9},{8,12},{9,13}} | collective-permute-start | bytes 3342344 | tf_op jit(solution)/shard_map/ppermute | solution.py:497
  16.9 0.0 collective-permute-done.7.next_in
  16.9 0.0 collective-permute-done.6.own_in
  16.9 0.7 %collective-permute-start.9 = (f32[32,512]{1,0:T(8,128)S(1)}, f32[32,512]{1,0:T(8,128)S(1)}, u32[]{:S(2)}, u32[]{:S(2)}) collective-permute-start(f32[32,512]{1,0:T(8,128)S(1)} %get-tuple-element.63._lower), channel_id=1, source_target_pairs={{20,17},{21,16}} | collective-permute-start | bytes 196616 | tf_op jit(solution)/shard_map/ppermute | solution.py:405
  17.6 0.7 %collective-permute-start.8 = (f32[32,512]{1,0:T(8,128)S(1)}, f32[32,512]{1,0:T(8,128)S(1)}, u32[]{:S(2)}, u32[]{:S(2)}) collective-permute-start(f32[32,512]{1,0:T(8,128)S(1)} %get-tuple-element.63._lower), channel_id=1, source_target_pairs={{20,16},{21,17}} | collective-permute-start | bytes 196616 | tf_op jit(solution)/shard_map/ppermute | solution.py:532
  18.3 0.0 collective-permute-done.9.next_in
  18.3 0.0 collective-permute-done.8.own_in
  18.3 0.7 %collective-permute-start.11 = (f32[32,512]{1,0:T(8,128)S(1)}, f32[32,512]{1,0:T(8,128)S(1)}, u32[]{:S(2)}, u32[]{:S(2)}) collective-permute-start(f32[32,512]{1,0:T(8,128)S(1)} %get-tuple-element.65._lower), channel_id=1, source_target_pairs={{16,13},{17,12}} | collective-permute-start | bytes 196616 | tf_op jit(solution)/shard_map/ppermute | solution.py:405
  19.0 0.7 %collective-permute-start.10 = (f32[32,512]{1,0:T(8,128)S(1)}, f32[32,512]{1,0:T(8,128)S(1)}, u32[]{:S(2)}, u32[]{:S(2)}) collective-permute-start(f32[32,512]{1,0:T(8,128)S(1)} %get-tuple-element.65._lower), channel_id=1, source_target_pairs={{16,12},{17,13}} | collective-permute-start | bytes 196616 | tf_op jit(solution)/shard_map/ppermute | solution.py:532
  19.7 0.0 collective-permute-done.11.next_in
  19.7 0.7 %collective-permute-start.13 = (f32[32,512]{1,0:T(8,128)S(1)}, f32[32,512]{1,0:T(8,128)S(1)}, u32[]{:S(2)}, u32[]{:S(2)}) collective-permute-start(f32[32,512]{1,0:T(8,128)S(1)} %get-tuple-element.67.rest_6_.lower), channel_id=1, source_target_pairs={{12,9},{13,8}} | collective-permute-start | bytes 196616 | tf_op jit(solution)/shard_map/ppermute | solution.py:405
  20.4 0.7 %collective-permute-start.12 = (f32[32,512]{1,0:T(8,128)S(1)}, f32[32,512]{1,0:T(8,128)S(1)}, u32[]{:S(2)}, u32[]{:S(2)}) collective-permute-start(f32[32,512]{1,0:T(8,128)S(1)} %get-tuple-element.67.rest_6_.lower), channel_id=1, source_target_pairs={{12,8},{13,9}} | collective-permute-start | bytes 196616 | tf_op jit(solution)/shard_map/ppermute | solution.py:532
  21.1 0.0 collective-permute-done.14.own_rows.rest_0_
  21.1 0.2 shard_map.56
  21.4 0.7 %collective-permute-start.19 = (f32[32,896]{1,0:T(8,128)S(1)}, f32[32,896]{1,0:T(8,128)S(1)}, u32[]{:S(2)}, u32[]{:S(2)}) collective-permute-start(f32[32,896]{1,0:T(8,128)S(1)} %get-tuple-element.78), channel_id=1, source_target_pairs={{12,5},{13,4}} | collective-permute-start | bytes 344072 | tf_op jit(solution)/shard_map/ppermute | solution.py:405
  22.0 0.7 %collective-permute-start.20 = (f32[32,896]{1,0:T(8,128)S(1)}, f32[32,896]{1,0:T(8,128)S(1)}, u32[]{:S(2)}, u32[]{:S(2)}) collective-permute-start(f32[32,896]{1,0:T(8,128)S(1)} %get-tuple-element.79), channel_id=1, source_target_pairs={{12,4},{13,5}} | collective-permute-start | bytes 344072 | tf_op jit(solution)/shard_map/ppermute | solution.py:544
  22.7 0.0 collective-permute-done.12.own_in
  22.8 1.3 %collective-permute-start.16 = (f32[32,896]{1,0:T(8,128)S(1)}, f32[32,896]{1,0:T(8,128)S(1)}, u32[]{:S(2)}, u32[]{:S(2)}) collective-permute-start(f32[32,896]{1,0:T(8,128)S(1)} %get-tuple-element.75), channel_id=1, source_target_pairs={{9,0}} | collective-permute-start | bytes 344072 | tf_op jit(solution)/shard_map/ppermute | solution.py:526
  24.1 1.3 %collective-permute-start.17 = (f32[32,896]{1,0:T(8,128)S(1)}, f32[32,896]{1,0:T(8,128)S(1)}, u32[]{:S(2)}, u32[]{:S(2)}) collective-permute-start(f32[32,896]{1,0:T(8,128)S(1)} %get-tuple-element.76), channel_id=1, source_target_pairs={{8,0},{9,1}} | collective-permute-start | bytes 344072 | tf_op jit(solution)/shard_map/ppermute | solution.py:527
  25.4 0.7 %collective-permute-start.18 = (f32[32,896]{1,0:T(8,128)S(1)}, f32[32,896]{1,0:T(8,128)S(1)}, u32[]{:S(2)}, u32[]{:S(2)}) collective-permute-start(f32[32,896]{1,0:T(8,128)S(1)} %get-tuple-element.77), channel_id=1, source_target_pairs={{8,1}} | collective-permute-start | bytes 344072 | tf_op jit(solution)/shard_map/ppermute | solution.py:528
  26.1 0.0 collective-permute-done.20.rest_4_
  26.1 24.3 %collective-permute-done.16.rest_0_ = f32[32,896]{1,0:T(8,128)S(1)} collective-permute-done((f32[32,896]{1,0:T(8,128)S(1)}, f32[32,896]{1,0:T(8,128)S(1)}, u32[]{:S(2)}, u32[]{:S(2)}) %collective-permute-start.16) | collective-permute-done | bytes 114720 | tf_op jit(solution)/shard_map/ppermute | solution.py:526
  50.4 0.3 collective-permute-done.17.rest_1_
  50.7 0.0 collective-permute-done.18.rest_2_
  50.7 0.3 shard_map.59
  51.1 1.3 %collective-permute-start.21 = (f32[32,512]{1,0:T(8,128)S(1)}, f32[32,512]{1,0:T(8,128)S(1)}, u32[]{:S(2)}, u32[]{:S(2)}) collective-permute-start(f32[32,512]{1,0:T(8,128)S(1)} %get-tuple-element.84), channel_id=1, source_target_pairs={{0,2},{1,3},{4,6},{5,7},{8,10},{9,11},{12,14},{13,15},{16,18},{17,... | collective-permute-start | bytes 196616 | tf_op jit(solution)/shard_map/ppermute | solution.py:575
  52.4 0.5 shard_map.60
  52.8 0.4 collective-permute-done.21
  53.2 0.6 %select_bitcast_fusion = f32[1,32,512]{2,1,0:T(8,128)} fusion(f32[32,512]{1,0:T(8,128)S(1)} %shard_map.60, f32[32,512]{1,0:T(8,128)S(1)} %collective-permute-done.21, pred[]{:T(512)S(6)} %eq.5), kind=kLoop, calls=%fused_computation | loop fusion | flops 16384 | bytes 196609 | tf_op jit(solution)/shard_map/broadcast_in_dim | solution.py:585
  (19 shorter events, 0.2 us)
Async XLA Ops:
  0.0 2.9 %copy-start.1 = (s32[1,2,3]{2,1,0:T(2,128)S(1)}, s32[1,2,3]{2,1,0:T(2,128)}, u32[]{:S(2)}) copy-start(s32[1,2,3]{2,1,0:T(2,128)} %mask.1) | copy-start | bytes 76
  0.0 2.9 %copy-start = (f32[1,2,512,256]{3,2,1,0:T(8,128)S(1)}, f32[1,2,512,256]{3,2,1,0:T(8,128)}, u32[]{:S(2)}) copy-start(f32[1,2,512,256]{3,2,1,0:T(8,128)} %lag.1) | copy-start | bytes 3145732
  1.6 4.7 %collective-permute-start.3 = (f32[32,512]{1,0:T(8,128)S(1)}, f32[32,512]{1,0:T(8,128)S(1)}, u32[]{:S(2)}, u32[]{:S(2)}) collective-permute-start(f32[32,512]{1,0:T(8,128)S(1)} %get-tuple-element.45.const), channel_id=1, source_target_pairs={{30,29},{31,28}} | collective-permute-start | bytes 196616 | tf_op jit(solution)/shard_map/ppermute | solution.py:405
  2.2 4.0 %collective-permute-start.2 = (f32[32,512]{1,0:T(8,128)S(1)}, f32[32,512]{1,0:T(8,128)S(1)}, u32[]{:S(2)}, u32[]{:S(2)}) collective-permute-start(f32[32,512]{1,0:T(8,128)S(1)} %get-tuple-element.45.const), channel_id=1, source_target_pairs={{30,28},{31,29}} | collective-permute-start | bytes 196616 | tf_op jit(solution)/shard_map/ppermute | solution.py:438
  3.7 7.9 %collective-permute-start = (f32[1,544,128]{2,1,0:T(8,128)S(1)}, f32[1,544,128]{2,1,0:T(8,128)S(1)}, u32[]{:S(2)}, u32[]{:S(2)}) collective-permute-start(f32[1,544,128]{2,1,0:T(8,128)S(1)} %get-tuple-element.49), channel_id=1, source_target_pairs={{2,1},{3,0},{6,5},{7,4},{10,9},{11,8},{14,13},{15,12},{18,17},{19,... | collective-permute-start | bytes 835592 | tf_op jit(solution)/shard_map/ppermute | solution.py:405
  5.0 7.2 %collective-permute-start.1 = (f32[1088,256]{1,0:T(8,128)S(1)}, f32[1088,256]{1,0:T(8,128)S(1)}, u32[]{:S(2)}, u32[]{:S(2)}) collective-permute-start(f32[1088,256]{1,0:T(8,128)S(1)} %get-tuple-element.50), channel_id=1, source_target_pairs={{2,0},{3,1},{6,4},{7,5},{10,8},{11,9},{14,12},{15,13},{18,16},{19,... | collective-permute-start | bytes 3342344 | tf_op jit(solution)/shard_map/ppermute | solution.py:460
  6.4 6.0 %collective-permute-start.5 = (f32[32,512]{1,0:T(8,128)S(1)}, f32[32,512]{1,0:T(8,128)S(1)}, u32[]{:S(2)}, u32[]{:S(2)}) collective-permute-start(f32[32,512]{1,0:T(8,128)S(1)} %get-tuple-element.58._lower), channel_id=1, source_target_pairs={{28,25},{29,24}} | collective-permute-start | bytes 196616 | tf_op jit(solution)/shard_map/ppermute | solution.py:405
  7.0 5.3 %collective-permute-start.4 = (f32[32,512]{1,0:T(8,128)S(1)}, f32[32,512]{1,0:T(8,128)S(1)}, u32[]{:S(2)}, u32[]{:S(2)}) collective-permute-start(f32[32,512]{1,0:T(8,128)S(1)} %get-tuple-element.58._lower), channel_id=1, source_target_pairs={{28,24},{29,25}} | collective-permute-start | bytes 196616 | tf_op jit(solution)/shard_map/ppermute | solution.py:532
  12.4 4.4 %collective-permute-start.7 = (f32[32,512]{1,0:T(8,128)S(1)}, f32[32,512]{1,0:T(8,128)S(1)}, u32[]{:S(2)}, u32[]{:S(2)}) collective-permute-start(f32[32,512]{1,0:T(8,128)S(1)} %get-tuple-element.61._lower), channel_id=1, source_target_pairs={{24,21},{25,20}} | collective-permute-start | bytes 196616 | tf_op jit(solution)/shard_map/ppermute | solution.py:405
  13.1 3.8 %collective-permute-start.6 = (f32[32,512]{1,0:T(8,128)S(1)}, f32[32,512]{1,0:T(8,128)S(1)}, u32[]{:S(2)}, u32[]{:S(2)}) collective-permute-start(f32[32,512]{1,0:T(8,128)S(1)} %get-tuple-element.61._lower), channel_id=1, source_target_pairs={{24,20},{25,21}} | collective-permute-start | bytes 196616 | tf_op jit(solution)/shard_map/ppermute | solution.py:532
  15.4 5.6 %collective-permute-start.15 = (f32[512,256]{1,0:T(8,128)S(1)}, f32[512,256]{1,0:T(8,128)S(1)}, u32[]{:S(2)}, u32[]{:S(2)}) collective-permute-start(f32[512,256]{1,0:T(8,128)S(1)} %get-tuple-element.69), channel_id=1, source_target_pairs={{4,9},{5,8},{8,13},{9,12}} | collective-permute-start | bytes 1572872 | tf_op jit(solution)/shard_map/ppermute | solution.py:405
  16.1 4.9 %collective-permute-start.14 = (f32[1088,256]{1,0:T(8,128)S(1)}, f32[1088,256]{1,0:T(8,128)S(1)}, u32[]{:S(2)}, u32[]{:S(2)}) collective-permute-start(f32[1088,256]{1,0:T(8,128)S(1)} %get-tuple-element.68), channel_id=1, source_target_pairs={{4,8},{5,9},{8,12},{9,13}} | collective-permute-start | bytes 3342344 | tf_op jit(solution)/shard_map/ppermute | solution.py:497
  16.9 1.3 %collective-permute-start.9 = (f32[32,512]{1,0:T(8,128)S(1)}, f32[32,512]{1,0:T(8,128)S(1)}, u32[]{:S(2)}, u32[]{:S(2)}) collective-permute-start(f32[32,512]{1,0:T(8,128)S(1)} %get-tuple-element.63._lower), channel_id=1, source_target_pairs={{20,17},{21,16}} | collective-permute-start | bytes 196616 | tf_op jit(solution)/shard_map/ppermute | solution.py:405
  17.6 0.7 %collective-permute-start.8 = (f32[32,512]{1,0:T(8,128)S(1)}, f32[32,512]{1,0:T(8,128)S(1)}, u32[]{:S(2)}, u32[]{:S(2)}) collective-permute-start(f32[32,512]{1,0:T(8,128)S(1)} %get-tuple-element.63._lower), channel_id=1, source_target_pairs={{20,16},{21,17}} | collective-permute-start | bytes 196616 | tf_op jit(solution)/shard_map/ppermute | solution.py:532
  18.3 1.3 %collective-permute-start.11 = (f32[32,512]{1,0:T(8,128)S(1)}, f32[32,512]{1,0:T(8,128)S(1)}, u32[]{:S(2)}, u32[]{:S(2)}) collective-permute-start(f32[32,512]{1,0:T(8,128)S(1)} %get-tuple-element.65._lower), channel_id=1, source_target_pairs={{16,13},{17,12}} | collective-permute-start | bytes 196616 | tf_op jit(solution)/shard_map/ppermute | solution.py:405
  19.0 0.7 %collective-permute-start.10 = (f32[32,512]{1,0:T(8,128)S(1)}, f32[32,512]{1,0:T(8,128)S(1)}, u32[]{:S(2)}, u32[]{:S(2)}) collective-permute-start(f32[32,512]{1,0:T(8,128)S(1)} %get-tuple-element.65._lower), channel_id=1, source_target_pairs={{16,12},{17,13}} | collective-permute-start | bytes 196616 | tf_op jit(solution)/shard_map/ppermute | solution.py:532
  19.7 3.0 %collective-permute-start.13 = (f32[32,512]{1,0:T(8,128)S(1)}, f32[32,512]{1,0:T(8,128)S(1)}, u32[]{:S(2)}, u32[]{:S(2)}) collective-permute-start(f32[32,512]{1,0:T(8,128)S(1)} %get-tuple-element.67.rest_6_.lower), channel_id=1, source_target_pairs={{12,9},{13,8}} | collective-permute-start | bytes 196616 | tf_op jit(solution)/shard_map/ppermute | solution.py:405
  20.4 2.3 %collective-permute-start.12 = (f32[32,512]{1,0:T(8,128)S(1)}, f32[32,512]{1,0:T(8,128)S(1)}, u32[]{:S(2)}, u32[]{:S(2)}) collective-permute-start(f32[32,512]{1,0:T(8,128)S(1)} %get-tuple-element.67.rest_6_.lower), channel_id=1, source_target_pairs={{12,8},{13,9}} | collective-permute-start | bytes 196616 | tf_op jit(solution)/shard_map/ppermute | solution.py:532
  21.4 4.7 %collective-permute-start.19 = (f32[32,896]{1,0:T(8,128)S(1)}, f32[32,896]{1,0:T(8,128)S(1)}, u32[]{:S(2)}, u32[]{:S(2)}) collective-permute-start(f32[32,896]{1,0:T(8,128)S(1)} %get-tuple-element.78), channel_id=1, source_target_pairs={{12,5},{13,4}} | collective-permute-start | bytes 344072 | tf_op jit(solution)/shard_map/ppermute | solution.py:405
  22.0 4.0 %collective-permute-start.20 = (f32[32,896]{1,0:T(8,128)S(1)}, f32[32,896]{1,0:T(8,128)S(1)}, u32[]{:S(2)}, u32[]{:S(2)}) collective-permute-start(f32[32,896]{1,0:T(8,128)S(1)} %get-tuple-element.79), channel_id=1, source_target_pairs={{12,4},{13,5}} | collective-permute-start | bytes 344072 | tf_op jit(solution)/shard_map/ppermute | solution.py:544
  22.8 27.6 %collective-permute-start.16 = (f32[32,896]{1,0:T(8,128)S(1)}, f32[32,896]{1,0:T(8,128)S(1)}, u32[]{:S(2)}, u32[]{:S(2)}) collective-permute-start(f32[32,896]{1,0:T(8,128)S(1)} %get-tuple-element.75), channel_id=1, source_target_pairs={{9,0}} | collective-permute-start | bytes 344072 | tf_op jit(solution)/shard_map/ppermute | solution.py:526
  24.1 26.7 %collective-permute-start.17 = (f32[32,896]{1,0:T(8,128)S(1)}, f32[32,896]{1,0:T(8,128)S(1)}, u32[]{:S(2)}, u32[]{:S(2)}) collective-permute-start(f32[32,896]{1,0:T(8,128)S(1)} %get-tuple-element.76), channel_id=1, source_target_pairs={{8,0},{9,1}} | collective-permute-start | bytes 344072 | tf_op jit(solution)/shard_map/ppermute | solution.py:527
  25.4 25.4 %collective-permute-start.18 = (f32[32,896]{1,0:T(8,128)S(1)}, f32[32,896]{1,0:T(8,128)S(1)}, u32[]{:S(2)}, u32[]{:S(2)}) collective-permute-start(f32[32,896]{1,0:T(8,128)S(1)} %get-tuple-element.77), channel_id=1, source_target_pairs={{8,1}} | collective-permute-start | bytes 344072 | tf_op jit(solution)/shard_map/ppermute | solution.py:528
  51.1 2.2 %collective-permute-start.21 = (f32[32,512]{1,0:T(8,128)S(1)}, f32[32,512]{1,0:T(8,128)S(1)}, u32[]{:S(2)}, u32[]{:S(2)}) collective-permute-start(f32[32,512]{1,0:T(8,128)S(1)} %get-tuple-element.84), channel_id=1, source_target_pairs={{0,2},{1,3},{4,6},{5,7},{8,10},{9,11},{12,14},{13,15},{16,18},{17,... | collective-permute-start | bytes 196616 | tf_op jit(solution)/shard_map/ppermute | solution.py:575

commit v9 on v8

--- a/solution.py
+++ b/solution.py
@@ -83,7 +83,7 @@
             near_high[rows], near_low[rows] = halves(value)
 
 
-def edge_kernel(sides, blocks, cols, _own, own, rim):
+def edge_kernel(sides, blocks, cols, own, rim):
     length, edge = own.shape[1], rim.shape[2]
     window = length + 2 * edge
 
@@ -112,7 +112,7 @@
     return cuts
 
 
-def pair_kernel(jump, rim, far, far_high, far_low, near_high, near_low, const, high, low, both, *rest):
+def pair_kernel(jump, far, rim, far_high, far_low, near_high, near_low, const, high, low, both, *rest):
     cols, sites = const.shape
     length = far.shape[1]
     blocks = sites // length
@@ -207,7 +207,7 @@
     return lambda side, cut: next_in[:, cut] if len(next_in.shape) == 2 else next_in[side, :, cut]
 
 
-def top_kernel(mine, sides, own_in, next_in, const, near_high, near_low, _upper, _lower, upper, lower, mid):
+def top_kernel(mine, sides, next_in, own_in, const, near_high, near_low, _upper, _lower, upper, lower, mid):
     sites = lower.shape[1]
     length = near_high.shape[1]
     blocks = sites // length
@@ -226,7 +226,7 @@
 
 
 def direct_kernel(
-    mine, sides, own_in, next_in, rim, far, far_high, far_low, rim_high, rim_low, near_high, near_low, const,
+    mine, sides, next_in, own_in, far, rim, far_high, far_low, rim_high, rim_low, near_high, near_low, const,
     _late, _lower, late, lower, mid
 ):
     cols, sites = lower.shape
@@ -264,11 +264,58 @@
         lower[:, at] = both[:, at] + stacked_dot(late, slice(b * length, b * length + span), high[rows], low[rows])
 
 
-def chain_kernel(mine, sides, own_in, next_in, both, high, low, _late, _lower, late, lower):
+def load_rims(sides, next_in, sites, halo, late):
+    for side in range(sides):
+        on_right = 1 - jnp.minimum(lax.axis_index("row"), 1).astype(jnp.int32) if sides == 1 else side
+        start = pl.multiple_of((1 - on_right) * (sites - halo), 128)
+        keep(late, pl.multiple_of(on_right * (halo + sites), 128), plain(next_in)(side, pl.ds(start, halo)))
+
+
+def rim_kernel(mine, sides, next_in, both, high, low, _late, late, base):
+    sites, length = base.shape[1], high.shape[1]
+    blocks = sites // length
+    span = high.shape[0] // blocks
+    halo = (late.shape[1] - sites) // 2
+    edge = halo - length
+
     @pl.when(lax.axis_index("tm") == 2 * mine)
     def _():
-        load(sides, plain(next_in), own_in[...], (late.shape[1] - own_in.shape[1]) // 2, late)
-        step(both, high, low, late, lower)
+        load_rims(sides, next_in, sites, halo, late)
+        cuts = [cuts_of(blocks, length, sites, span, last) for last in (False, True)]
+        for b in range(blocks):
+            value = both[:, b * length : (b + 1) * length]
+            if sides == 2:
+                for lo, hi, _ in (cuts[0][b], cuts[1][b]):
+                    rows = slice(b * span + lo, b * span + hi)
+                    value += stacked_dot(late, slice(b * length + lo, b * length + hi), high[rows], low[rows])
+            else:
+                on_left = lax.axis_index("row") != 0
+                counts = [cut[b][1] - cut[b][0] for cut in cuts]
+                for chunk in range(0, max(counts), edge):
+                    starts = [cut[b][0] + chunk if chunk < count else 0 for cut, count in zip(cuts, counts)]
+                    start = pl.multiple_of(jnp.where(on_left, starts[0], starts[1]), edge)
+                    rows = pl.ds(b * span + start, edge)
+                    product = stacked_dot(late, pl.ds(b * length + start, edge), high[rows], low[rows])
+                    if chunk >= min(counts):
+                        product = jnp.where(on_left == (counts[0] > counts[1]), product, 0.0)
+                    value += product
+            base[:, b * length : (b + 1) * length] = value
+
+
+def add_own(own_in, base, high, low, late, lower):
+    sites, length = lower.shape[1], high.shape[1]
+    blocks = sites // length
+    span = high.shape[0] // blocks
+    halo = (late.shape[1] - sites) // 2
+    keep(late, halo, own_in[...])
+    for b in range(blocks):
+        at, start = slice(b * length, (b + 1) * length), halo - b * length
+        rows = slice(b * span + start, b * span + start + sites)
+        lower[:, at] = base[:, at] + stacked_dot(late, slice(halo, halo + sites), high[rows], low[rows])
+
+
+def chain_kernel(mine, own_in, base, high, low, _late, _lower, late, lower):
+    pl.when(lax.axis_index("tm") == 2 * mine)(lambda: add_own(own_in, base, high, low, late, lower))
 
 
 def rows_kernel(own_rows, other_rows, own_high, own_low, other_high, other_low):
@@ -313,13 +360,12 @@
     to_own[:, sites:] = far_mid[:, pl.ds(away, halo)]
 
 
-def jump_kernel(mine, sides, own_in, next_in, both, high, low, *rest):
+def jump_kernel(mine, own_in, base, high, low, *rest):
     ship, (_late, _lower, late, lower, to_next, to_own, to_last, *scratch) = rest[:-9], rest[-9:]
 
     @pl.when(lax.axis_index("tm") == 2 * mine)
     def _():
-        load(sides, plain(next_in), own_in[...], (late.shape[1] - own_in.shape[1]) // 2, late)
-        step(both, high, low, late, lower)
+        add_own(own_in, base, high, low, late, lower)
         add_parts(lower, *ship, to_next, to_own, *scratch, high.shape[0] * high.shape[1] // own_in.shape[1])
         to_last[...] = to_next[...]
 
@@ -448,14 +494,21 @@
             flops=6 * (tall + cols * blocks) * length * length, bytes_accessed=16 * tall * length, transcendentals=0
         ),
     )(fill_mask, const, inv_high, inv_low, lag_coupling)
-    near, edges = pl.pallas_call(
+    edges = pl.pallas_call(
         functools.partial(edge_kernel, sides, blocks, cols),
-        out_shape=(shape(near.shape, f32), shape((sides, window + cols, edge), f32)),
+        out_shape=shape((sides, window + cols, edge), f32),
         in_specs=[VMEM],
-        out_specs=(VMEM,) * 2,
+        out_specs=VMEM,
+        compiler_params=PARAMS,
+    )(near)
+    near = pl.pallas_call(
+        lambda _own, _edges, own: None,
+        out_shape=shape(near.shape, f32),
+        in_specs=[VMEM] * 2,
+        out_specs=VMEM,
         input_output_aliases={0: 0},
         compiler_params=PARAMS,
-    )(near)
+    )(near, edges)
     rim = cross(edges, odd[:-1], even[:-1], True)
     far = lax.ppermute(near, BOTH, link(odd[:-1], even[:-1]))
 
@@ -469,7 +522,7 @@
         input_output_aliases={5: 0, 6: 1},
         compiler_params=PARAMS,
         cost_estimate=pl.CostEstimate(flops=50 * 10**9, bytes_accessed=0, transcendentals=0),
-    )(first_own, first_next, const, near_high, near_low, blank, blank)
+    )(first_next, first_own, const, near_high, near_low, blank, blank)
     far_high, far_low, rim_high, rim_low = pl.pallas_call(
         split_kernel,
         out_shape=(
@@ -491,7 +544,7 @@
         scratch_shapes=[pltpu.VMEM((2 * window, length), f32)],
         compiler_params=PARAMS,
         cost_estimate=pl.CostEstimate(flops=10**9, bytes_accessed=0, transcendentals=0),
-    )(rim, far, far_high, far_low, near_high, near_low, const)
+    )(far, rim, far_high, far_low, near_high, near_low, const)
     if jumps:
         source, target = [2 * jump - 2, 2 * jump], [2 * jump, 2 * jump + 2]
         own_rows = lax.ppermute(packs[0], BOTH, link(source, target))
@@ -508,10 +561,10 @@
         return pl.pallas_call(
             kernel,
             out_shape=tuple(shape(v.shape, v.dtype) for v in state) + tuple(extra),
-            in_specs=[VMEM] * (len(given) + 2),
-            out_specs=(VMEM,) * (2 + len(extra)),
+            in_specs=[VMEM] * (len(given) + len(state)),
+            out_specs=(VMEM,) * (len(state) + len(extra)),
             scratch_shapes=list(scratch),
-            input_output_aliases={len(given): 0, len(given) + 1: 1},
+            input_output_aliases={len(given) + i: i for i in range(len(state))},
             compiler_params=PARAMS,
             cost_estimate=pl.CostEstimate(flops=flops, bytes_accessed=0, transcendentals=0) if flops else None,
         )(*given, *state)
@@ -548,25 +601,31 @@
         if mine == pairs - 2:
             late, lower = turn(
                 functools.partial(direct_kernel, mine, sides),
-                (own_in, next_in, rim, far, far_high, far_low, rim_high, rim_low, near_high, near_low, const),
+                (next_in, own_in, far, rim, far_high, far_low, rim_high, rim_low, near_high, near_low, const),
                 (late, lower),
                 [pltpu.VMEM((2 * cols, sites + 2 * edge), bf16)],
             )
-        elif jumps and mine == jump:
+            continue
+        late, base = turn(
+            functools.partial(rim_kernel, mine, sides),
+            (next_in, both, high, low),
+            (late,),
+            extra=[shape((cols, sites), f32)],
+        )
+        if jumps and mine == jump:
             late, lower, to_next, to_own, to_last = turn(
-                functools.partial(jump_kernel, mine, sides),
-                (own_in, next_in, both, high, low, own_rows, *ship),
+                functools.partial(jump_kernel, mine),
+                (own_in, base, high, low, own_rows, *ship),
                 (late, lower),
                 parts_scratch,
                 parts + parts[:1],
             )
         else:
-            early = jumps and mine == pairs - 3
             late, lower = turn(
-                functools.partial(chain_kernel, mine, sides),
-                (own_in, next_in, both, high, low),
+                functools.partial(chain_kernel, mine),
+                (own_in, base, high, low),
                 (late, lower),
-                flops=50 * 10**9 if early else 0,
+                flops=50 * 10**9 if jumps and mine == pairs - 3 else 0,
             )
     given = (first_in, own_in, next_in, beside_next, beside_own) if jumps else (own_in, next_in)
     late, upper = turn(

time: 54.6 us -> 54 us (0.989)
  waiting for transfers between devices: 29.6 us -> 28.9 us
    ppermute x1, waiting for transfers between devices: 24.3 us -> 23.6 us  [local(): first_in = lax.ppermute(to_next, BOTH, [(2 * source[0] + 1, 2 * target[0])])]
where the time goes in v9:
time: 54 us; the launch traced here: 53.3 us
  waiting for transfers between devices  28.9 us (54%)
  starting transfers between devices  17.9 us (33%)
  Pallas kernels  5.37 us (10%)
  other arithmetic  0.64 us (1%)
    ppermute x1, waiting for transfers between devices, local(): first_in = lax.ppermute(to_next, BOTH, [(2 * source[0] + 1, 2 * target[0])])  23.6 us
    ppermute x9, starting transfers between devices, cross(): return lax.ppermute(value, BOTH, perm)  6.64 us
    ppermute x9, waiting for transfers between devices, cross(): return lax.ppermute(value, BOTH, perm)  3.87 us
    ppermute x5, starting transfers between devices, local(): own_in = lax.ppermute(lower, BOTH, link(source, target))  3.32 us
    pallas_call x1, Pallas kernels, local(): pl.pallas_call(functools.partial(pair_kernel, jumps), out_shape=(shape((2...  1.64 us
    pallas_call x1, Pallas kernels, local(): pl.pallas_call(const_kernel, out_shape=(shape((cols, sites), f32), shape(...  1.56 us
    ppermute x1, starting transfers between devices, local(): far = lax.ppermute(near, BOTH, link(odd[:-1], even[:-1]))  1.29 us
    ppermute x1, starting transfers between devices, local(): first_in = lax.ppermute(to_next, BOTH, [(2 * source[0] + 1, 2 * target[0])])  1.29 us
  transfers between devices with their start and end apart: 22, of which 5 were waited for; matrix products, arithmetic and copies ran while one was open for 0% of the time, Pallas kernels for 6%

profile of v9, /device:TPU:0, one launch (start us, length us, event | category | flops | bytes accessed | tf_op | source)
XLA Modules:
  0.0 53.3 jit_solution(17275347904174392034)
XLA Ops:
  0.0 1.6 %shard_map.46 = (f32[32,512]{1,0:T(8,128)S(1)}, bf16[2,256,256]{2,1,0:T(8,128)(2,1)S(1)}, bf16[2,256,256]{2,1,0:T(8,128)(2,1)S(1)}) custom-call(f32[1,32,512]{2,1,0:T(8,128)} %normals.1, f32[1,2,256,256]{3,2,1,0:T(8,128)} %inv.1), custom_call_target="tpu_custom_call" | custom-call | flops 5000000000 | tf_op jit(solution)/shard_map/pallas_call | solution.py:466
  1.6 0.7 %collective-permute-start.2 = (f32[32,512]{1,0:T(8,128)S(1)}, f32[32,512]{1,0:T(8,128)S(1)}, u32[]{:S(2)}, u32[]{:S(2)}) collective-permute-start(f32[32,512]{1,0:T(8,128)S(1)} %get-tuple-element.51.const), channel_id=1, source_target_pairs={{30,29},{31,28}} | collective-permute-start | bytes 196616 | tf_op jit(solution)/shard_map/ppermute | solution.py:451
  2.2 0.7 %collective-permute-start.3 = (f32[32,512]{1,0:T(8,128)S(1)}, f32[32,512]{1,0:T(8,128)S(1)}, u32[]{:S(2)}, u32[]{:S(2)}) collective-permute-start(f32[32,512]{1,0:T(8,128)S(1)} %get-tuple-element.51.const), channel_id=1, source_target_pairs={{30,28},{31,29}} | collective-permute-start | bytes 196616 | tf_op jit(solution)/shard_map/ppermute | solution.py:484
  2.9 0.7 %shard_map.47 = (f32[1088,256]{1,0:T(8,128)S(1)}, bf16[1024,256]{1,0:T(8,128)(2,1)S(1)}, bf16[1024,256]{1,0:T(8,128)(2,1)S(1)}) custom-call(s32[1,2,3]{2,1,0:T(2,128)S(1)} %copy-done.1, f32[32,512]{1,0:T(8,128)S(1)} %get-tuple-element.51.const, bf16[2,256,256]{2,1,0:T(8,128)(2,1)S(1)} %get-tuple-element.52.inv_high, ...), custom_call_target="tpu_custom_call" | custom-call | flops 427819008 | bytes 4194304 | tf_op jit(solution)/shard_map/pallas_call | solution.py:485
  3.7 1.3 %collective-permute-start.1 = (f32[1,544,128]{2,1,0:T(8,128)S(1)}, f32[1,544,128]{2,1,0:T(8,128)S(1)}, u32[]{:S(2)}, u32[]{:S(2)}) collective-permute-start(f32[1,544,128]{2,1,0:T(8,128)S(1)} %shard_map.48._edges), channel_id=1, source_target_pairs={{2,1},{3,0},{6,5},{7,4},{10,9},{11,8},{14,13},{15,12},{18,17},{19,... | collective-permute-start | bytes 835592 | tf_op jit(solution)/shard_map/ppermute | solution.py:451
  5.0 1.3 %collective-permute-start = (f32[1088,256]{1,0:T(8,128)S(1)}, f32[1088,256]{1,0:T(8,128)S(1)}, u32[]{:S(2)}, u32[]{:S(2)}) collective-permute-start(f32[1088,256]{1,0:T(8,128)S(1)} %shard_map.49), channel_id=1, source_target_pairs={{2,0},{3,1},{6,4},{7,5},{10,8},{11,9},{14,12},{15,13},{18,16},{19,... | collective-permute-start | bytes 3342344 | tf_op jit(solution)/shard_map/ppermute | solution.py:513
  6.3 0.0 collective-permute-done.2.next_in
  6.3 0.0 collective-permute-done.3.own_in
  6.4 0.7 %collective-permute-start.4 = (f32[32,512]{1,0:T(8,128)S(1)}, f32[32,512]{1,0:T(8,128)S(1)}, u32[]{:S(2)}, u32[]{:S(2)}) collective-permute-start(f32[32,512]{1,0:T(8,128)S(1)} %get-tuple-element.62._lower), channel_id=1, source_target_pairs={{28,25},{29,24}} | collective-permute-start | bytes 196616 | tf_op jit(solution)/shard_map/ppermute | solution.py:451
  7.0 0.7 %collective-permute-start.5 = (f32[32,512]{1,0:T(8,128)S(1)}, f32[32,512]{1,0:T(8,128)S(1)}, u32[]{:S(2)}, u32[]{:S(2)}) collective-permute-start(f32[32,512]{1,0:T(8,128)S(1)} %get-tuple-element.62._lower), channel_id=1, source_target_pairs={{28,24},{29,25}} | collective-permute-start | bytes 196616 | tf_op jit(solution)/shard_map/ppermute | solution.py:585
  7.7 3.9 %collective-permute-done.1.rim = f32[1,544,128]{2,1,0:T(8,128)S(1)} collective-permute-done((f32[1,544,128]{2,1,0:T(8,128)S(1)}, f32[1,544,128]{2,1,0:T(8,128)S(1)}, u32[]{:S(2)}, u32[]{:S(2)}) %collective-permute-start.1) | collective-permute-done | bytes 278560 | tf_op jit(solution)/shard_map/ppermute | solution.py:451
  11.6 0.6 %collective-permute-done.far.rest_5_ = f32[1088,256]{1,0:T(8,128)S(1)} collective-permute-done((f32[1088,256]{1,0:T(8,128)S(1)}, f32[1088,256]{1,0:T(8,128)S(1)}, u32[]{:S(2)}, u32[]{:S(2)}) %collective-permute-start) | collective-permute-done | bytes 1114144 | tf_op jit(solution)/shard_map/ppermute | solution.py:513
  12.2 0.2 shard_map.50
  12.4 0.0 collective-permute-done.4.next_in
  12.4 0.0 collective-permute-done.5.own_in
  12.4 0.7 %collective-permute-start.7 = (f32[32,512]{1,0:T(8,128)S(1)}, f32[32,512]{1,0:T(8,128)S(1)}, u32[]{:S(2)}, u32[]{:S(2)}) collective-permute-start(f32[32,512]{1,0:T(8,128)S(1)} %get-tuple-element.65._lower), channel_id=1, source_target_pairs={{24,21},{25,20}} | collective-permute-start | bytes 196616 | tf_op jit(solution)/shard_map/ppermute | solution.py:451
  13.1 0.7 %collective-permute-start.6 = (f32[32,512]{1,0:T(8,128)S(1)}, f32[32,512]{1,0:T(8,128)S(1)}, u32[]{:S(2)}, u32[]{:S(2)}) collective-permute-start(f32[32,512]{1,0:T(8,128)S(1)} %get-tuple-element.65._lower), channel_id=1, source_target_pairs={{24,20},{25,21}} | collective-permute-start | bytes 196616 | tf_op jit(solution)/shard_map/ppermute | solution.py:585
  13.8 1.6 %shard_map.51 = (bf16[2048,256]{1,0:T(8,128)(2,1)S(1)}, bf16[2048,256]{1,0:T(8,128)(2,1)S(1)}, f32[32,512]{1,0:T(8,128)S(1)}, f32[1088,256]{1,0:T(8,128)S(1)}, f32[512,256]{1,0:T(8,128)S(1)}) custom-call(f32[1088,256]{1,0:T(8,128)S(1)} %collective-permute-done.far.rest_5_, f32[1,544,128]{2,1,0:T(8,128)S(1)} %collective-permute-done.1.rim, ...), custom_call_target="tpu_custom_call" | custom-call | flops 1000000000 | tf_op jit(solution)/shard_map/pallas_call | solution.py:537
  15.4 0.7 %collective-permute-start.14 = (f32[1088,256]{1,0:T(8,128)S(1)}, f32[1088,256]{1,0:T(8,128)S(1)}, u32[]{:S(2)}, u32[]{:S(2)}) collective-permute-start(f32[1088,256]{1,0:T(8,128)S(1)} %get-tuple-element.80), channel_id=1, source_target_pairs={{4,8},{5,9},{8,12},{9,13}} | collective-permute-start | bytes 3342344 | tf_op jit(solution)/shard_map/ppermute | solution.py:550
  16.2 0.7 %collective-permute-start.15 = (f32[512,256]{1,0:T(8,128)S(1)}, f32[512,256]{1,0:T(8,128)S(1)}, u32[]{:S(2)}, u32[]{:S(2)}) collective-permute-start(f32[512,256]{1,0:T(8,128)S(1)} %get-tuple-element.81), channel_id=1, source_target_pairs={{4,9},{5,8},{8,13},{9,12}} | collective-permute-start | bytes 1572872 | tf_op jit(solution)/shard_map/ppermute | solution.py:451
  16.9 0.0 collective-permute-done.7.next_in
  16.9 0.0 collective-permute-done.6.own_in
  16.9 0.7 %collective-permute-start.9 = (f32[32,512]{1,0:T(8,128)S(1)}, f32[32,512]{1,0:T(8,128)S(1)}, u32[]{:S(2)}, u32[]{:S(2)}) collective-permute-start(f32[32,512]{1,0:T(8,128)S(1)} %get-tuple-element.69._lower), channel_id=1, source_target_pairs={{20,17},{21,16}} | collective-permute-start | bytes 196616 | tf_op jit(solution)/shard_map/ppermute | solution.py:451
  17.6 0.7 %collective-permute-start.8 = (f32[32,512]{1,0:T(8,128)S(1)}, f32[32,512]{1,0:T(8,128)S(1)}, u32[]{:S(2)}, u32[]{:S(2)}) collective-permute-start(f32[32,512]{1,0:T(8,128)S(1)} %get-tuple-element.69._lower), channel_id=1, source_target_pairs={{20,16},{21,17}} | collective-permute-start | bytes 196616 | tf_op jit(solution)/shard_map/ppermute | solution.py:585
  18.3 0.0 collective-permute-done.9.next_in
  18.3 0.0 collective-permute-done.8.own_in
  18.4 0.7 %collective-permute-start.11 = (f32[32,512]{1,0:T(8,128)S(1)}, f32[32,512]{1,0:T(8,128)S(1)}, u32[]{:S(2)}, u32[]{:S(2)}) collective-permute-start(f32[32,512]{1,0:T(8,128)S(1)} %get-tuple-element.73._lower), channel_id=1, source_target_pairs={{16,13},{17,12}} | collective-permute-start | bytes 196616 | tf_op jit(solution)/shard_map/ppermute | solution.py:451
  19.0 0.7 %collective-permute-start.10 = (f32[32,512]{1,0:T(8,128)S(1)}, f32[32,512]{1,0:T(8,128)S(1)}, u32[]{:S(2)}, u32[]{:S(2)}) collective-permute-start(f32[32,512]{1,0:T(8,128)S(1)} %get-tuple-element.73._lower), channel_id=1, source_target_pairs={{16,12},{17,13}} | collective-permute-start | bytes 196616 | tf_op jit(solution)/shard_map/ppermute | solution.py:585
  19.7 0.0 collective-permute-done.11.next_in
  19.7 0.0 collective-permute-done.10.own_in
  19.8 0.7 %collective-permute-start.13 = (f32[32,512]{1,0:T(8,128)S(1)}, f32[32,512]{1,0:T(8,128)S(1)}, u32[]{:S(2)}, u32[]{:S(2)}) collective-permute-start(f32[32,512]{1,0:T(8,128)S(1)} %get-tuple-element.77.rest_6_.lower), channel_id=1, source_target_pairs={{12,9},{13,8}} | collective-permute-start | bytes 196616 | tf_op jit(solution)/shard_map/ppermute | solution.py:451
  20.4 0.7 %collective-permute-start.12 = (f32[32,512]{1,0:T(8,128)S(1)}, f32[32,512]{1,0:T(8,128)S(1)}, u32[]{:S(2)}, u32[]{:S(2)}) collective-permute-start(f32[32,512]{1,0:T(8,128)S(1)} %get-tuple-element.77.rest_6_.lower), channel_id=1, source_target_pairs={{12,8},{13,9}} | collective-permute-start | bytes 196616 | tf_op jit(solution)/shard_map/ppermute | solution.py:585
  21.1 0.0 collective-permute-done.13.next_in
  21.2 0.0 collective-permute-done.15.other_rows
  21.2 0.0 collective-permute-done.14.own_rows.rest_0_
  21.2 0.2 shard_map.61
  21.5 1.3 %collective-permute-start.16 = (f32[32,896]{1,0:T(8,128)S(1)}, f32[32,896]{1,0:T(8,128)S(1)}, u32[]{:S(2)}, u32[]{:S(2)}) collective-permute-start(f32[32,896]{1,0:T(8,128)S(1)} %get-tuple-element.87), channel_id=1, source_target_pairs={{9,0}} | collective-permute-start | bytes 344072 | tf_op jit(solution)/shard_map/ppermute | solution.py:579
  22.8 1.3 %collective-permute-start.17 = (f32[32,896]{1,0:T(8,128)S(1)}, f32[32,896]{1,0:T(8,128)S(1)}, u32[]{:S(2)}, u32[]{:S(2)}) collective-permute-start(f32[32,896]{1,0:T(8,128)S(1)} %get-tuple-element.88), channel_id=1, source_target_pairs={{8,0},{9,1}} | collective-permute-start | bytes 344072 | tf_op jit(solution)/shard_map/ppermute | solution.py:580
  24.1 0.7 %collective-permute-start.18 = (f32[32,896]{1,0:T(8,128)S(1)}, f32[32,896]{1,0:T(8,128)S(1)}, u32[]{:S(2)}, u32[]{:S(2)}) collective-permute-start(f32[32,896]{1,0:T(8,128)S(1)} %get-tuple-element.89), channel_id=1, source_target_pairs={{8,1}} | collective-permute-start | bytes 344072 | tf_op jit(solution)/shard_map/ppermute | solution.py:581
  24.8 0.7 %collective-permute-start.19 = (f32[32,896]{1,0:T(8,128)S(1)}, f32[32,896]{1,0:T(8,128)S(1)}, u32[]{:S(2)}, u32[]{:S(2)}) collective-permute-start(f32[32,896]{1,0:T(8,128)S(1)} %get-tuple-element.90), channel_id=1, source_target_pairs={{12,5},{13,4}} | collective-permute-start | bytes 344072 | tf_op jit(solution)/shard_map/ppermute | solution.py:451
  25.5 0.7 %collective-permute-start.20 = (f32[32,896]{1,0:T(8,128)S(1)}, f32[32,896]{1,0:T(8,128)S(1)}, u32[]{:S(2)}, u32[]{:S(2)}) collective-permute-start(f32[32,896]{1,0:T(8,128)S(1)} %get-tuple-element.91), channel_id=1, source_target_pairs={{12,4},{13,5}} | collective-permute-start | bytes 344072 | tf_op jit(solution)/shard_map/ppermute | solution.py:597
  26.2 23.6 %collective-permute-done.16.rest_0_ = f32[32,896]{1,0:T(8,128)S(1)} collective-permute-done((f32[32,896]{1,0:T(8,128)S(1)}, f32[32,896]{1,0:T(8,128)S(1)}, u32[]{:S(2)}, u32[]{:S(2)}) %collective-permute-start.16) | collective-permute-done | bytes 114720 | tf_op jit(solution)/shard_map/ppermute | solution.py:579
  49.8 0.3 collective-permute-done.17.rest_1_
  50.1 0.3 shard_map.64
  50.4 1.3 %collective-permute-start.21 = (f32[32,512]{1,0:T(8,128)S(1)}, f32[32,512]{1,0:T(8,128)S(1)}, u32[]{:S(2)}, u32[]{:S(2)}) collective-permute-start(f32[32,512]{1,0:T(8,128)S(1)} %get-tuple-element.96), channel_id=1, source_target_pairs={{0,2},{1,3},{4,6},{5,7},{8,10},{9,11},{12,14},{13,15},{16,18},{17,... | collective-permute-start | bytes 196616 | tf_op jit(solution)/shard_map/ppermute | solution.py:634
  51.7 0.5 shard_map.65
  52.2 0.4 collective-permute-done.21
  52.6 0.6 %select_bitcast_fusion = f32[1,32,512]{2,1,0:T(8,128)} fusion(f32[32,512]{1,0:T(8,128)S(1)} %shard_map.65, f32[32,512]{1,0:T(8,128)S(1)} %collective-permute-done.21, pred[]{:T(512)S(6)} %eq.5), kind=kLoop, calls=%fused_computation | loop fusion | flops 16384 | bytes 196609 | tf_op jit(solution)/shard_map/broadcast_in_dim | solution.py:644
  (24 shorter events, 0.3 us)
Async XLA Ops:
  0.0 2.9 %copy-start = (f32[1,2,512,256]{3,2,1,0:T(8,128)S(1)}, f32[1,2,512,256]{3,2,1,0:T(8,128)}, u32[]{:S(2)}) copy-start(f32[1,2,512,256]{3,2,1,0:T(8,128)} %lag.1) | copy-start | bytes 3145732
  0.0 2.9 %copy-start.1 = (s32[1,2,3]{2,1,0:T(2,128)S(1)}, s32[1,2,3]{2,1,0:T(2,128)}, u32[]{:S(2)}) copy-start(s32[1,2,3]{2,1,0:T(2,128)} %mask.1) | copy-start | bytes 76
  1.6 4.7 %collective-permute-start.2 = (f32[32,512]{1,0:T(8,128)S(1)}, f32[32,512]{1,0:T(8,128)S(1)}, u32[]{:S(2)}, u32[]{:S(2)}) collective-permute-start(f32[32,512]{1,0:T(8,128)S(1)} %get-tuple-element.51.const), channel_id=1, source_target_pairs={{30,29},{31,28}} | collective-permute-start | bytes 196616 | tf_op jit(solution)/shard_map/ppermute | solution.py:451
  2.2 4.0 %collective-permute-start.3 = (f32[32,512]{1,0:T(8,128)S(1)}, f32[32,512]{1,0:T(8,128)S(1)}, u32[]{:S(2)}, u32[]{:S(2)}) collective-permute-start(f32[32,512]{1,0:T(8,128)S(1)} %get-tuple-element.51.const), channel_id=1, source_target_pairs={{30,28},{31,29}} | collective-permute-start | bytes 196616 | tf_op jit(solution)/shard_map/ppermute | solution.py:484
  3.7 7.9 %collective-permute-start.1 = (f32[1,544,128]{2,1,0:T(8,128)S(1)}, f32[1,544,128]{2,1,0:T(8,128)S(1)}, u32[]{:S(2)}, u32[]{:S(2)}) collective-permute-start(f32[1,544,128]{2,1,0:T(8,128)S(1)} %shard_map.48._edges), channel_id=1, source_target_pairs={{2,1},{3,0},{6,5},{7,4},{10,9},{11,8},{14,13},{15,12},{18,17},{19,... | collective-permute-start | bytes 835592 | tf_op jit(solution)/shard_map/ppermute | solution.py:451
  5.0 7.2 %collective-permute-start = (f32[1088,256]{1,0:T(8,128)S(1)}, f32[1088,256]{1,0:T(8,128)S(1)}, u32[]{:S(2)}, u32[]{:S(2)}) collective-permute-start(f32[1088,256]{1,0:T(8,128)S(1)} %shard_map.49), channel_id=1, source_target_pairs={{2,0},{3,1},{6,4},{7,5},{10,8},{11,9},{14,12},{15,13},{18,16},{19,... | collective-permute-start | bytes 3342344 | tf_op jit(solution)/shard_map/ppermute | solution.py:513
  6.4 6.0 %collective-permute-start.4 = (f32[32,512]{1,0:T(8,128)S(1)}, f32[32,512]{1,0:T(8,128)S(1)}, u32[]{:S(2)}, u32[]{:S(2)}) collective-permute-start(f32[32,512]{1,0:T(8,128)S(1)} %get-tuple-element.62._lower), channel_id=1, source_target_pairs={{28,25},{29,24}} | collective-permute-start | bytes 196616 | tf_op jit(solution)/shard_map/ppermute | solution.py:451
  7.0 5.4 %collective-permute-start.5 = (f32[32,512]{1,0:T(8,128)S(1)}, f32[32,512]{1,0:T(8,128)S(1)}, u32[]{:S(2)}, u32[]{:S(2)}) collective-permute-start(f32[32,512]{1,0:T(8,128)S(1)} %get-tuple-element.62._lower), channel_id=1, source_target_pairs={{28,24},{29,25}} | collective-permute-start | bytes 196616 | tf_op jit(solution)/shard_map/ppermute | solution.py:585
  12.4 4.4 %collective-permute-start.7 = (f32[32,512]{1,0:T(8,128)S(1)}, f32[32,512]{1,0:T(8,128)S(1)}, u32[]{:S(2)}, u32[]{:S(2)}) collective-permute-start(f32[32,512]{1,0:T(8,128)S(1)} %get-tuple-element.65._lower), channel_id=1, source_target_pairs={{24,21},{25,20}} | collective-permute-start | bytes 196616 | tf_op jit(solution)/shard_map/ppermute | solution.py:451
  13.1 3.8 %collective-permute-start.6 = (f32[32,512]{1,0:T(8,128)S(1)}, f32[32,512]{1,0:T(8,128)S(1)}, u32[]{:S(2)}, u32[]{:S(2)}) collective-permute-start(f32[32,512]{1,0:T(8,128)S(1)} %get-tuple-element.65._lower), channel_id=1, source_target_pairs={{24,20},{25,21}} | collective-permute-start | bytes 196616 | tf_op jit(solution)/shard_map/ppermute | solution.py:585
  15.4 5.7 %collective-permute-start.14 = (f32[1088,256]{1,0:T(8,128)S(1)}, f32[1088,256]{1,0:T(8,128)S(1)}, u32[]{:S(2)}, u32[]{:S(2)}) collective-permute-start(f32[1088,256]{1,0:T(8,128)S(1)} %get-tuple-element.80), channel_id=1, source_target_pairs={{4,8},{5,9},{8,12},{9,13}} | collective-permute-start | bytes 3342344 | tf_op jit(solution)/shard_map/ppermute | solution.py:550
  16.2 5.0 %collective-permute-start.15 = (f32[512,256]{1,0:T(8,128)S(1)}, f32[512,256]{1,0:T(8,128)S(1)}, u32[]{:S(2)}, u32[]{:S(2)}) collective-permute-start(f32[512,256]{1,0:T(8,128)S(1)} %get-tuple-element.81), channel_id=1, source_target_pairs={{4,9},{5,8},{8,13},{9,12}} | collective-permute-start | bytes 1572872 | tf_op jit(solution)/shard_map/ppermute | solution.py:451
  16.9 1.3 %collective-permute-start.9 = (f32[32,512]{1,0:T(8,128)S(1)}, f32[32,512]{1,0:T(8,128)S(1)}, u32[]{:S(2)}, u32[]{:S(2)}) collective-permute-start(f32[32,512]{1,0:T(8,128)S(1)} %get-tuple-element.69._lower), channel_id=1, source_target_pairs={{20,17},{21,16}} | collective-permute-start | bytes 196616 | tf_op jit(solution)/shard_map/ppermute | solution.py:451
  17.6 0.7 %collective-permute-start.8 = (f32[32,512]{1,0:T(8,128)S(1)}, f32[32,512]{1,0:T(8,128)S(1)}, u32[]{:S(2)}, u32[]{:S(2)}) collective-permute-start(f32[32,512]{1,0:T(8,128)S(1)} %get-tuple-element.69._lower), channel_id=1, source_target_pairs={{20,16},{21,17}} | collective-permute-start | bytes 196616 | tf_op jit(solution)/shard_map/ppermute | solution.py:585
  18.4 1.3 %collective-permute-start.11 = (f32[32,512]{1,0:T(8,128)S(1)}, f32[32,512]{1,0:T(8,128)S(1)}, u32[]{:S(2)}, u32[]{:S(2)}) collective-permute-start(f32[32,512]{1,0:T(8,128)S(1)} %get-tuple-element.73._lower), channel_id=1, source_target_pairs={{16,13},{17,12}} | collective-permute-start | bytes 196616 | tf_op jit(solution)/shard_map/ppermute | solution.py:451
  19.0 0.7 %collective-permute-start.10 = (f32[32,512]{1,0:T(8,128)S(1)}, f32[32,512]{1,0:T(8,128)S(1)}, u32[]{:S(2)}, u32[]{:S(2)}) collective-permute-start(f32[32,512]{1,0:T(8,128)S(1)} %get-tuple-element.73._lower), channel_id=1, source_target_pairs={{16,12},{17,13}} | collective-permute-start | bytes 196616 | tf_op jit(solution)/shard_map/ppermute | solution.py:585
  19.8 1.3 %collective-permute-start.13 = (f32[32,512]{1,0:T(8,128)S(1)}, f32[32,512]{1,0:T(8,128)S(1)}, u32[]{:S(2)}, u32[]{:S(2)}) collective-permute-start(f32[32,512]{1,0:T(8,128)S(1)} %get-tuple-element.77.rest_6_.lower), channel_id=1, source_target_pairs={{12,9},{13,8}} | collective-permute-start | bytes 196616 | tf_op jit(solution)/shard_map/ppermute | solution.py:451
  20.4 1.0 %collective-permute-start.12 = (f32[32,512]{1,0:T(8,128)S(1)}, f32[32,512]{1,0:T(8,128)S(1)}, u32[]{:S(2)}, u32[]{:S(2)}) collective-permute-start(f32[32,512]{1,0:T(8,128)S(1)} %get-tuple-element.77.rest_6_.lower), channel_id=1, source_target_pairs={{12,8},{13,9}} | collective-permute-start | bytes 196616 | tf_op jit(solution)/shard_map/ppermute | solution.py:585
  21.5 28.2 %collective-permute-start.16 = (f32[32,896]{1,0:T(8,128)S(1)}, f32[32,896]{1,0:T(8,128)S(1)}, u32[]{:S(2)}, u32[]{:S(2)}) collective-permute-start(f32[32,896]{1,0:T(8,128)S(1)} %get-tuple-element.87), channel_id=1, source_target_pairs={{9,0}} | collective-permute-start | bytes 344072 | tf_op jit(solution)/shard_map/ppermute | solution.py:579
  22.8 27.3 %collective-permute-start.17 = (f32[32,896]{1,0:T(8,128)S(1)}, f32[32,896]{1,0:T(8,128)S(1)}, u32[]{:S(2)}, u32[]{:S(2)}) collective-permute-start(f32[32,896]{1,0:T(8,128)S(1)} %get-tuple-element.88), channel_id=1, source_target_pairs={{8,0},{9,1}} | collective-permute-start | bytes 344072 | tf_op jit(solution)/shard_map/ppermute | solution.py:580
  24.1 26.0 %collective-permute-start.18 = (f32[32,896]{1,0:T(8,128)S(1)}, f32[32,896]{1,0:T(8,128)S(1)}, u32[]{:S(2)}, u32[]{:S(2)}) collective-permute-start(f32[32,896]{1,0:T(8,128)S(1)} %get-tuple-element.89), channel_id=1, source_target_pairs={{8,1}} | collective-permute-start | bytes 344072 | tf_op jit(solution)/shard_map/ppermute | solution.py:581
  24.8 25.3 %collective-permute-start.19 = (f32[32,896]{1,0:T(8,128)S(1)}, f32[32,896]{1,0:T(8,128)S(1)}, u32[]{:S(2)}, u32[]{:S(2)}) collective-permute-start(f32[32,896]{1,0:T(8,128)S(1)} %get-tuple-element.90), channel_id=1, source_target_pairs={{12,5},{13,4}} | collective-permute-start | bytes 344072 | tf_op jit(solution)/shard_map/ppermute | solution.py:451
  25.5 24.6 %collective-permute-start.20 = (f32[32,896]{1,0:T(8,128)S(1)}, f32[32,896]{1,0:T(8,128)S(1)}, u32[]{:S(2)}, u32[]{:S(2)}) collective-permute-start(f32[32,896]{1,0:T(8,128)S(1)} %get-tuple-element.91), channel_id=1, source_target_pairs={{12,4},{13,5}} | collective-permute-start | bytes 344072 | tf_op jit(solution)/shard_map/ppermute | solution.py:597
  50.4 2.2 %collective-permute-start.21 = (f32[32,512]{1,0:T(8,128)S(1)}, f32[32,512]{1,0:T(8,128)S(1)}, u32[]{:S(2)}, u32[]{:S(2)}) collective-permute-start(f32[32,512]{1,0:T(8,128)S(1)} %get-tuple-element.96), channel_id=1, source_target_pairs={{0,2},{1,3},{4,6},{5,7},{8,10},{9,11},{12,14},{13,15},{16,18},{17,... | collective-permute-start | bytes 196616 | tf_op jit(solution)/shard_map/ppermute | solution.py:634

commit v10 on v9

--- a/solution.py
+++ b/solution.py
@@ -49,7 +49,7 @@
         rim[1] = columns(False)
 
 
-def const_kernel(normals, inv, const, inv_high, inv_low, normals_in, inv_in, sems):
+def const_kernel(normals, inv, const, again, inv_high, inv_low, normals_in, inv_in, sems):
     blocks, length = inv.shape[1], inv.shape[2]
     moves = [pltpu.make_async_copy(normals.at[0], normals_in, sems.at[0])]
     for b in range(blocks):
@@ -63,6 +63,7 @@
         moves[1 + b].wait()
         inv_high[b], inv_low[b] = halves(inv_in[b])
         const[:, at] = triple(high, low, inv_high[b], inv_low[b])
+    again[...] = const[...]
 
 
 def fuse_kernel(mask, const, inv_high, inv_low, lag, own, near_high, near_low):
@@ -96,10 +97,8 @@
     put_rim(sides, rim, columns)
 
 
-def split_kernel(rim, far, far_high, far_low, rim_high, rim_low):
+def split_kernel(far, far_high, far_low):
     far_high[...], far_low[...] = halves(far[: far_high.shape[0]])
-    for side in range(rim.shape[0]):
-        rim_high[side], rim_low[side] = halves(rim[side, : rim_high.shape[1]])
 
 
 def cuts_of(blocks, length, sites, span, last):
@@ -112,7 +111,12 @@
     return cuts
 
 
-def pair_kernel(jump, far, rim, far_high, far_low, near_high, near_low, const, high, low, both, *rest):
+def pair_kernel(first, jump, *refs):
+    here = lax.axis_index("tm") == 2 * first[0]
+    pl.when(here if first[1] else jnp.logical_not(here))(lambda: make_pair(jump, *refs))
+
+
+def make_pair(jump, far, rim, far_high, far_low, near_high, near_low, const, high, low, both, *rest):
     cols, sites = const.shape
     length = far.shape[1]
     blocks = sites // length
@@ -225,37 +229,6 @@
             lower[:, at] = const[:, at] - product
 
 
-def direct_kernel(
-    mine, sides, next_in, own_in, far, rim, far_high, far_low, rim_high, rim_low, near_high, near_low, const,
-    _late, _lower, late, lower, mid
-):
-    cols, sites = lower.shape
-    length = near_high.shape[1]
-    blocks = sites // length
-    window = near_high.shape[0] // blocks
-    edge = (window - length) // 2
-    halo = length + edge
-
-    @pl.when(lax.axis_index("tm") == 2 * mine)
-    def _():
-        load(sides, plain(next_in), own_in[...], halo, late)
-        mid[...] = jnp.zeros_like(mid)
-        for side in range(sides):
-            on_right = 1 - jnp.minimum(lax.axis_index("row"), 1).astype(jnp.int32) if sides == 1 else side
-            start = pl.multiple_of(on_right * (2 * halo + sites - window), 128)
-            product = stacked_dot(late, pl.ds(start, window), rim_high[side], rim_low[side])
-            keep(mid, pl.multiple_of(on_right * (edge + sites), 128), rim[side, window:] - product)
-        for b in range(blocks):
-            rows, start = slice(b * window, (b + 1) * window), halo - edge + b * length
-            at = blocks * window + b * cols
-            product = stacked_dot(late, slice(start, start + window), far_high[rows], far_low[rows])
-            keep(mid, edge + b * length, far[at : at + cols] - product)
-        for b in range(blocks):
-            at, rows = slice(b * length, (b + 1) * length), slice(b * window, (b + 1) * window)
-            product = stacked_dot(mid, slice(b * length, b * length + window), near_high[rows], near_low[rows])
-            lower[:, at] = const[:, at] - product
-
-
 def step(both, high, low, late, lower):
     blocks = lower.shape[1] // high.shape[1]
     length, span = high.shape[1], high.shape[0] // blocks
@@ -463,14 +436,14 @@
     tall = blocks * window
     jump = 2
     jumps = rows == 2 and pairs > 5
-    const, inv_high, inv_low = pl.pallas_call(
+    const, again, inv_high, inv_low = pl.pallas_call(
         const_kernel,
         out_shape=(
-            shape((cols, sites), f32),
+            shape((cols, sites), f32), shape((cols, sites), f32),
             shape((blocks, length, length), bf16), shape((blocks, length, length), bf16),
         ),
         in_specs=[HBM] * 2,
-        out_specs=(VMEM,) * 3,
+        out_specs=(VMEM,) * 4,
         scratch_shapes=[
             pltpu.VMEM(normals.shape[1:], f32),
             pltpu.VMEM(inv_diag.shape[1:], f32),
@@ -481,7 +454,7 @@
     )(*[pltpu.with_memory_space_constraint(a, pltpu.HBM) for a in (normals, inv_diag)])
     odd, even = range(1, times, 2), range(0, times, 2)
     first_next = cross(const, odd[-1:], even[-1:])
-    first_own = lax.ppermute(const, BOTH, link(odd[-1:], even[-1:]))
+    first_own = lax.ppermute(again, BOTH, link(odd[-1:], even[-1:]))
     near, near_high, near_low = pl.pallas_call(
         fuse_kernel,
         out_shape=(
@@ -523,28 +496,30 @@
         compiler_params=PARAMS,
         cost_estimate=pl.CostEstimate(flops=50 * 10**9, bytes_accessed=0, transcendentals=0),
     )(first_next, first_own, const, near_high, near_low, blank, blank)
-    far_high, far_low, rim_high, rim_low = pl.pallas_call(
+    far_high, far_low = pl.pallas_call(
         split_kernel,
-        out_shape=(
-            shape((tall, length), bf16), shape((tall, length), bf16),
-            shape((sides, window, edge), bf16), shape((sides, window, edge), bf16),
-        ),
-        in_specs=[VMEM] * 2,
-        out_specs=(VMEM,) * 4,
+        out_shape=(shape((tall, length), bf16), shape((tall, length), bf16)),
+        in_specs=[VMEM],
+        out_specs=(VMEM,) * 2,
         compiler_params=PARAMS,
-    )(rim, far)
+    )(far)
     packs = (shape((blocks * (sites + cols), length), f32), shape((halo + edge, length), f32)) if jumps else ()
-    high, low, both, *packs = pl.pallas_call(
-        functools.partial(pair_kernel, jumps),
-        out_shape=(
-            shape((2 * tall, length), bf16), shape((2 * tall, length), bf16), shape((cols, sites), f32), *packs
-        ),
-        in_specs=[VMEM] * 7,
-        out_specs=(VMEM,) * (3 + len(packs)),
-        scratch_shapes=[pltpu.VMEM((2 * window, length), f32)],
-        compiler_params=PARAMS,
-        cost_estimate=pl.CostEstimate(flops=10**9, bytes_accessed=0, transcendentals=0),
-    )(far, rim, far_high, far_low, near_high, near_low, const)
+
+    def pair_matrix(first, jumps, packs):
+        return pl.pallas_call(
+            functools.partial(pair_kernel, (pairs - 2, first), jumps),
+            out_shape=(
+                shape((2 * tall, length), bf16), shape((2 * tall, length), bf16), shape((cols, sites), f32), *packs
+            ),
+            in_specs=[VMEM] * 7,
+            out_specs=(VMEM,) * (3 + len(packs)),
+            scratch_shapes=[pltpu.VMEM((2 * window, length), f32)],
+            compiler_params=PARAMS,
+            cost_estimate=pl.CostEstimate(flops=10**9, bytes_accessed=0, transcendentals=0),
+        )(far, rim, far_high, far_low, near_high, near_low, const)
+
+    early = pair_matrix(True, False, ())
+    high, low, both, *packs = pair_matrix(False, jumps, packs)
     if jumps:
         source, target = [2 * jump - 2, 2 * jump], [2 * jump, 2 * jump + 2]
         own_rows = lax.ppermute(packs[0], BOTH, link(source, target))
@@ -598,17 +573,10 @@
         mine -= 1
         if mine == 0:
             break
-        if mine == pairs - 2:
-            late, lower = turn(
-                functools.partial(direct_kernel, mine, sides),
-                (next_in, own_in, far, rim, far_high, far_low, rim_high, rim_low, near_high, near_low, const),
-                (late, lower),
-                [pltpu.VMEM((2 * cols, sites + 2 * edge), bf16)],
-            )
-            continue
+        here = early if mine == pairs - 2 else (high, low, both)
         late, base = turn(
             functools.partial(rim_kernel, mine, sides),
-            (next_in, both, high, low),
+            (next_in, here[2], *here[:2]),
             (late,),
             extra=[shape((cols, sites), f32)],
         )
@@ -623,7 +591,7 @@
         else:
             late, lower = turn(
                 functools.partial(chain_kernel, mine),
-                (own_in, base, high, low),
+                (own_in, base, *here[:2]),
                 (late, lower),
                 flops=50 * 10**9 if jumps and mine == pairs - 3 else 0,
             )

time: 54 us -> 53.6 us (level)
    ppermute x1, waiting for transfers between devices: 0.63 us -> 4.48 us  [local(): far = lax.ppermute(near, BOTH, link(odd[:-1], even[:-1]))]
    ppermute x9, waiting for transfers between devices: 3.87 us -> 0.02 us  [cross(): return lax.ppermute(value, BOTH, perm)]
    pallas_call x1 -> x2, Pallas kernels: 1.64 us -> 1.66 us  [pair_matrix(): pl.pallas_call(functools.partial(pair_kernel, (pairs - 2, first), jumps),...]
  transfers between devices with their start and end apart: 22 -> 22, of which waited for: 5 -> 4; matrix products, arithmetic and copies ran while one was open for 0% -> 0% of each run, Pallas kernels for 6% -> 6%
where the time goes in v10:
time: 53.6 us; the launch traced here: 52.9 us
  waiting for transfers between devices  28.5 us (53%)
  starting transfers between devices  17.9 us (33%)
  Pallas kernels  5.38 us (10%)
  other arithmetic  0.64 us (1%)
    ppermute x1, waiting for transfers between devices, local(): first_in = lax.ppermute(to_next, BOTH, [(2 * source[0] + 1, 2 * target[0])])  23.2 us
    ppermute x9, starting transfers between devices, cross(): return lax.ppermute(value, BOTH, perm)  6.64 us
    ppermute x1, waiting for transfers between devices, local(): far = lax.ppermute(near, BOTH, link(odd[:-1], even[:-1]))  4.48 us
    ppermute x5, starting transfers between devices, local(): own_in = lax.ppermute(lower, BOTH, link(source, target))  3.32 us
    pallas_call x2, Pallas kernels, pair_matrix(): pl.pallas_call(functools.partial(pair_kernel, (pairs - 2, first), jumps),...  1.66 us
    pallas_call x1, Pallas kernels, local(): pl.pallas_call(const_kernel, out_shape=(shape((cols, sites), f32), shape(...  1.56 us
    ppermute x1, starting transfers between devices, local(): far = lax.ppermute(near, BOTH, link(odd[:-1], even[:-1]))  1.29 us
    ppermute x1, starting transfers between devices, local(): first_in = lax.ppermute(to_next, BOTH, [(2 * source[0] + 1, 2 * target[0])])  1.29 us
  transfers between devices with their start and end apart: 22, of which 4 were waited for; matrix products, arithmetic and copies ran while one was open for 0% of the time, Pallas kernels for 6%

profile of v10, /device:TPU:0, one launch (start us, length us, event | category | flops | bytes accessed | tf_op | source)
XLA Modules:
  0.0 52.9 jit_solution(18180101348496924741)
XLA Ops:
  0.0 1.6 %shard_map.46 = (f32[32,512]{1,0:T(8,128)S(1)}, f32[32,512]{1,0:T(8,128)S(1)}, bf16[2,256,256]{2,1,0:T(8,128)(2,1)S(1)}, bf16[2,256,256]{2,1,0:T(8,128)(2,1)S(1)}) custom-call(f32[1,32,512]{2,1,0:T(8,128)} %normals.1, f32[1,2,256,256]{3,2,1,0:T(8,128)} %inv.1), custom_call_target="tpu_custom_call" | custom-call | flops 5000000000 | tf_op jit(solution)/shard_map/pallas_call | solution.py:439
  1.6 0.7 %collective-permute-start.2 = (f32[32,512]{1,0:T(8,128)S(1)}, f32[32,512]{1,0:T(8,128)S(1)}, u32[]{:S(2)}, u32[]{:S(2)}) collective-permute-start(f32[32,512]{1,0:T(8,128)S(1)} %get-tuple-element.55.const.refs_6_), channel_id=1, source_target_pairs={{30,29},{31,28}} | collective-permute-start | bytes 196616 | tf_op jit(solution)/shard_map/ppermute | solution.py:424
  2.2 0.7 %collective-permute-start.3 = (f32[32,512]{1,0:T(8,128)S(1)}, f32[32,512]{1,0:T(8,128)S(1)}, u32[]{:S(2)}, u32[]{:S(2)}) collective-permute-start(f32[32,512]{1,0:T(8,128)S(1)} %get-tuple-element.66), channel_id=1, source_target_pairs={{30,28},{31,29}} | collective-permute-start | bytes 196616 | tf_op jit(solution)/shard_map/ppermute | solution.py:457
  2.9 0.7 %shard_map.47 = (f32[1088,256]{1,0:T(8,128)S(1)}, bf16[1024,256]{1,0:T(8,128)(2,1)S(1)}, bf16[1024,256]{1,0:T(8,128)(2,1)S(1)}) custom-call(s32[1,2,3]{2,1,0:T(2,128)S(1)} %copy-done.1, f32[32,512]{1,0:T(8,128)S(1)} %get-tuple-element.55.const.refs_6_, bf16[2,256,256]{2,1,0:T(8,128)(2,1)S(1)} %get-tuple-element.56.inv_high, ...), custom_call_target="tpu_custom_call" | custom-call | flops 427819008 | bytes 4194304 | tf_op jit(solution)/shard_map/pallas_call | solution.py:458
  3.7 1.3 %collective-permute-start.1 = (f32[1,544,128]{2,1,0:T(8,128)S(1)}, f32[1,544,128]{2,1,0:T(8,128)S(1)}, u32[]{:S(2)}, u32[]{:S(2)}) collective-permute-start(f32[1,544,128]{2,1,0:T(8,128)S(1)} %shard_map.48._edges), channel_id=1, source_target_pairs={{2,1},{3,0},{6,5},{7,4},{10,9},{11,8},{14,13},{15,12},{18,17},{19,... | collective-permute-start | bytes 835592 | tf_op jit(solution)/shard_map/ppermute | solution.py:424
  5.0 1.3 %collective-permute-start = (f32[1088,256]{1,0:T(8,128)S(1)}, f32[1088,256]{1,0:T(8,128)S(1)}, u32[]{:S(2)}, u32[]{:S(2)}) collective-permute-start(f32[1088,256]{1,0:T(8,128)S(1)} %shard_map.49), channel_id=1, source_target_pairs={{2,0},{3,1},{6,4},{7,5},{10,8},{11,9},{14,12},{15,13},{18,16},{19,... | collective-permute-start | bytes 3342344 | tf_op jit(solution)/shard_map/ppermute | solution.py:486
  6.3 0.0 collective-permute-done.2.next_in
  6.3 0.0 collective-permute-done.3.own_in
  6.4 0.7 %collective-permute-start.5 = (f32[32,512]{1,0:T(8,128)S(1)}, f32[32,512]{1,0:T(8,128)S(1)}, u32[]{:S(2)}, u32[]{:S(2)}) collective-permute-start(f32[32,512]{1,0:T(8,128)S(1)} %get-tuple-element.67._lower), channel_id=1, source_target_pairs={{28,25},{29,24}} | collective-permute-start | bytes 196616 | tf_op jit(solution)/shard_map/ppermute | solution.py:424
  7.0 0.7 %collective-permute-start.4 = (f32[32,512]{1,0:T(8,128)S(1)}, f32[32,512]{1,0:T(8,128)S(1)}, u32[]{:S(2)}, u32[]{:S(2)}) collective-permute-start(f32[32,512]{1,0:T(8,128)S(1)} %get-tuple-element.67._lower), channel_id=1, source_target_pairs={{28,24},{29,25}} | collective-permute-start | bytes 196616 | tf_op jit(solution)/shard_map/ppermute | solution.py:560
  7.7 4.5 %collective-permute-done.far.refs_0_.rest_5_ = f32[1088,256]{1,0:T(8,128)S(1)} collective-permute-done((f32[1088,256]{1,0:T(8,128)S(1)}, f32[1088,256]{1,0:T(8,128)S(1)}, u32[]{:S(2)}, u32[]{:S(2)}) %collective-permute-start) | collective-permute-done | bytes 1114144 | tf_op jit(solution)/shard_map/ppermute | solution.py:486
  12.2 0.1 shard_map.50
  12.3 0.0 collective-permute-done.1.refs_1_
  12.4 0.0 collective-permute-done.5.next_in
  12.4 0.0 collective-permute-done.4.own_in
  12.5 0.7 %collective-permute-start.7 = (f32[32,512]{1,0:T(8,128)S(1)}, f32[32,512]{1,0:T(8,128)S(1)}, u32[]{:S(2)}, u32[]{:S(2)}) collective-permute-start(f32[32,512]{1,0:T(8,128)S(1)} %get-tuple-element.73._lower), channel_id=1, source_target_pairs={{24,21},{25,20}} | collective-permute-start | bytes 196616 | tf_op jit(solution)/shard_map/ppermute | solution.py:424
  13.1 0.7 %collective-permute-start.6 = (f32[32,512]{1,0:T(8,128)S(1)}, f32[32,512]{1,0:T(8,128)S(1)}, u32[]{:S(2)}, u32[]{:S(2)}) collective-permute-start(f32[32,512]{1,0:T(8,128)S(1)} %get-tuple-element.73._lower), channel_id=1, source_target_pairs={{24,20},{25,21}} | collective-permute-start | bytes 196616 | tf_op jit(solution)/shard_map/ppermute | solution.py:560
  13.8 1.6 %shard_map.51 = (bf16[2048,256]{1,0:T(8,128)(2,1)S(1)}, bf16[2048,256]{1,0:T(8,128)(2,1)S(1)}, f32[32,512]{1,0:T(8,128)S(1)}, f32[1088,256]{1,0:T(8,128)S(1)}, f32[512,256]{1,0:T(8,128)S(1)}) custom-call(f32[1088,256]{1,0:T(8,128)S(1)} %collective-permute-done.far.refs_0_.rest_5_, f32[1,544,128]{2,1,0:T(8,128)S(1)} %collective-permute-done.1.refs_1_, ...), custom_call_target="tpu_custom_call" | custom-call | flops 1000000000 | tf_op jit(solution)/shard_map/pallas_call | solution.py:509
  15.5 0.7 %collective-permute-start.14 = (f32[1088,256]{1,0:T(8,128)S(1)}, f32[1088,256]{1,0:T(8,128)S(1)}, u32[]{:S(2)}, u32[]{:S(2)}) collective-permute-start(f32[1088,256]{1,0:T(8,128)S(1)} %get-tuple-element.88), channel_id=1, source_target_pairs={{4,8},{5,9},{8,12},{9,13}} | collective-permute-start | bytes 3342344 | tf_op jit(solution)/shard_map/ppermute | solution.py:525
  16.2 0.7 %collective-permute-start.15 = (f32[512,256]{1,0:T(8,128)S(1)}, f32[512,256]{1,0:T(8,128)S(1)}, u32[]{:S(2)}, u32[]{:S(2)}) collective-permute-start(f32[512,256]{1,0:T(8,128)S(1)} %get-tuple-element.89), channel_id=1, source_target_pairs={{4,9},{5,8},{8,13},{9,12}} | collective-permute-start | bytes 1572872 | tf_op jit(solution)/shard_map/ppermute | solution.py:424
  16.9 0.0 collective-permute-done.7.next_in
  16.9 0.0 collective-permute-done.6.own_in
  17.0 0.7 %collective-permute-start.9 = (f32[32,512]{1,0:T(8,128)S(1)}, f32[32,512]{1,0:T(8,128)S(1)}, u32[]{:S(2)}, u32[]{:S(2)}) collective-permute-start(f32[32,512]{1,0:T(8,128)S(1)} %get-tuple-element.77._lower), channel_id=1, source_target_pairs={{20,17},{21,16}} | collective-permute-start | bytes 196616 | tf_op jit(solution)/shard_map/ppermute | solution.py:424
  17.6 0.7 %collective-permute-start.8 = (f32[32,512]{1,0:T(8,128)S(1)}, f32[32,512]{1,0:T(8,128)S(1)}, u32[]{:S(2)}, u32[]{:S(2)}) collective-permute-start(f32[32,512]{1,0:T(8,128)S(1)} %get-tuple-element.77._lower), channel_id=1, source_target_pairs={{20,16},{21,17}} | collective-permute-start | bytes 196616 | tf_op jit(solution)/shard_map/ppermute | solution.py:560
  18.3 0.0 collective-permute-done.9.next_in
  18.4 0.0 collective-permute-done.8.own_in
  18.4 0.7 %collective-permute-start.11 = (f32[32,512]{1,0:T(8,128)S(1)}, f32[32,512]{1,0:T(8,128)S(1)}, u32[]{:S(2)}, u32[]{:S(2)}) collective-permute-start(f32[32,512]{1,0:T(8,128)S(1)} %get-tuple-element.81._lower), channel_id=1, source_target_pairs={{16,13},{17,12}} | collective-permute-start | bytes 196616 | tf_op jit(solution)/shard_map/ppermute | solution.py:424
  19.1 0.7 %collective-permute-start.10 = (f32[32,512]{1,0:T(8,128)S(1)}, f32[32,512]{1,0:T(8,128)S(1)}, u32[]{:S(2)}, u32[]{:S(2)}) collective-permute-start(f32[32,512]{1,0:T(8,128)S(1)} %get-tuple-element.81._lower), channel_id=1, source_target_pairs={{16,12},{17,13}} | collective-permute-start | bytes 196616 | tf_op jit(solution)/shard_map/ppermute | solution.py:560
  19.7 0.0 collective-permute-done.11.next_in
  19.8 0.0 collective-permute-done.10.own_in
  19.8 0.7 %collective-permute-start.13 = (f32[32,512]{1,0:T(8,128)S(1)}, f32[32,512]{1,0:T(8,128)S(1)}, u32[]{:S(2)}, u32[]{:S(2)}) collective-permute-start(f32[32,512]{1,0:T(8,128)S(1)} %get-tuple-element.85.rest_6_.lower), channel_id=1, source_target_pairs={{12,9},{13,8}} | collective-permute-start | bytes 196616 | tf_op jit(solution)/shard_map/ppermute | solution.py:424
  20.5 0.7 %collective-permute-start.12 = (f32[32,512]{1,0:T(8,128)S(1)}, f32[32,512]{1,0:T(8,128)S(1)}, u32[]{:S(2)}, u32[]{:S(2)}) collective-permute-start(f32[32,512]{1,0:T(8,128)S(1)} %get-tuple-element.85.rest_6_.lower), channel_id=1, source_target_pairs={{12,8},{13,9}} | collective-permute-start | bytes 196616 | tf_op jit(solution)/shard_map/ppermute | solution.py:560
  21.2 0.2 shard_map.63
  21.6 1.3 %collective-permute-start.16 = (f32[32,896]{1,0:T(8,128)S(1)}, f32[32,896]{1,0:T(8,128)S(1)}, u32[]{:S(2)}, u32[]{:S(2)}) collective-permute-start(f32[32,896]{1,0:T(8,128)S(1)} %get-tuple-element.95), channel_id=1, source_target_pairs={{9,0}} | collective-permute-start | bytes 344072 | tf_op jit(solution)/shard_map/ppermute | solution.py:554
  22.9 1.3 %collective-permute-start.17 = (f32[32,896]{1,0:T(8,128)S(1)}, f32[32,896]{1,0:T(8,128)S(1)}, u32[]{:S(2)}, u32[]{:S(2)}) collective-permute-start(f32[32,896]{1,0:T(8,128)S(1)} %get-tuple-element.96), channel_id=1, source_target_pairs={{8,0},{9,1}} | collective-permute-start | bytes 344072 | tf_op jit(solution)/shard_map/ppermute | solution.py:555
  24.2 0.7 %collective-permute-start.18 = (f32[32,896]{1,0:T(8,128)S(1)}, f32[32,896]{1,0:T(8,128)S(1)}, u32[]{:S(2)}, u32[]{:S(2)}) collective-permute-start(f32[32,896]{1,0:T(8,128)S(1)} %get-tuple-element.97), channel_id=1, source_target_pairs={{8,1}} | collective-permute-start | bytes 344072 | tf_op jit(solution)/shard_map/ppermute | solution.py:556
  24.8 0.7 %collective-permute-start.19 = (f32[32,896]{1,0:T(8,128)S(1)}, f32[32,896]{1,0:T(8,128)S(1)}, u32[]{:S(2)}, u32[]{:S(2)}) collective-permute-start(f32[32,896]{1,0:T(8,128)S(1)} %get-tuple-element.98), channel_id=1, source_target_pairs={{12,5},{13,4}} | collective-permute-start | bytes 344072 | tf_op jit(solution)/shard_map/ppermute | solution.py:424
  25.5 0.7 %collective-permute-start.20 = (f32[32,896]{1,0:T(8,128)S(1)}, f32[32,896]{1,0:T(8,128)S(1)}, u32[]{:S(2)}, u32[]{:S(2)}) collective-permute-start(f32[32,896]{1,0:T(8,128)S(1)} %get-tuple-element.99), channel_id=1, source_target_pairs={{12,4},{13,5}} | collective-permute-start | bytes 344072 | tf_op jit(solution)/shard_map/ppermute | solution.py:572
  26.2 23.2 %collective-permute-done.16.rest_0_ = f32[32,896]{1,0:T(8,128)S(1)} collective-permute-done((f32[32,896]{1,0:T(8,128)S(1)}, f32[32,896]{1,0:T(8,128)S(1)}, u32[]{:S(2)}, u32[]{:S(2)}) %collective-permute-start.16) | collective-permute-done | bytes 114720 | tf_op jit(solution)/shard_map/ppermute | solution.py:554
  49.4 0.3 collective-permute-done.17.rest_1_
  49.7 0.0 collective-permute-done.18.rest_2_
  49.7 0.0 collective-permute-done.19.rest_3_
  49.7 0.0 collective-permute-done.20.rest_4_
  49.7 0.3 shard_map.66
  50.1 1.3 %collective-permute-start.21 = (f32[32,512]{1,0:T(8,128)S(1)}, f32[32,512]{1,0:T(8,128)S(1)}, u32[]{:S(2)}, u32[]{:S(2)}) collective-permute-start(f32[32,512]{1,0:T(8,128)S(1)} %get-tuple-element.104), channel_id=1, source_target_pairs={{0,2},{1,3},{4,6},{5,7},{8,10},{9,11},{12,14},{13,15},{16,18},{17,... | collective-permute-start | bytes 196616 | tf_op jit(solution)/shard_map/ppermute | solution.py:602
  51.4 0.5 shard_map.67
  51.9 0.4 collective-permute-done.21
  52.3 0.6 %select_bitcast_fusion = f32[1,32,512]{2,1,0:T(8,128)} fusion(f32[32,512]{1,0:T(8,128)S(1)} %shard_map.67, f32[32,512]{1,0:T(8,128)S(1)} %collective-permute-done.21, pred[]{:T(512)S(6)} %eq.5), kind=kLoop, calls=%fused_computation | loop fusion | flops 16384 | bytes 196609 | tf_op jit(solution)/shard_map/broadcast_in_dim | solution.py:612
  (26 shorter events, 0.4 us)
Async XLA Ops:
  0.0 2.9 %copy-start = (f32[1,2,512,256]{3,2,1,0:T(8,128)S(1)}, f32[1,2,512,256]{3,2,1,0:T(8,128)}, u32[]{:S(2)}) copy-start(f32[1,2,512,256]{3,2,1,0:T(8,128)} %lag.1) | copy-start | bytes 3145732
  0.0 2.9 %copy-start.1 = (s32[1,2,3]{2,1,0:T(2,128)S(1)}, s32[1,2,3]{2,1,0:T(2,128)}, u32[]{:S(2)}) copy-start(s32[1,2,3]{2,1,0:T(2,128)} %mask.1) | copy-start | bytes 76
  1.6 4.7 %collective-permute-start.2 = (f32[32,512]{1,0:T(8,128)S(1)}, f32[32,512]{1,0:T(8,128)S(1)}, u32[]{:S(2)}, u32[]{:S(2)}) collective-permute-start(f32[32,512]{1,0:T(8,128)S(1)} %get-tuple-element.55.const.refs_6_), channel_id=1, source_target_pairs={{30,29},{31,28}} | collective-permute-start | bytes 196616 | tf_op jit(solution)/shard_map/ppermute | solution.py:424
  2.2 4.0 %collective-permute-start.3 = (f32[32,512]{1,0:T(8,128)S(1)}, f32[32,512]{1,0:T(8,128)S(1)}, u32[]{:S(2)}, u32[]{:S(2)}) collective-permute-start(f32[32,512]{1,0:T(8,128)S(1)} %get-tuple-element.66), channel_id=1, source_target_pairs={{30,28},{31,29}} | collective-permute-start | bytes 196616 | tf_op jit(solution)/shard_map/ppermute | solution.py:457
  3.7 8.7 %collective-permute-start.1 = (f32[1,544,128]{2,1,0:T(8,128)S(1)}, f32[1,544,128]{2,1,0:T(8,128)S(1)}, u32[]{:S(2)}, u32[]{:S(2)}) collective-permute-start(f32[1,544,128]{2,1,0:T(8,128)S(1)} %shard_map.48._edges), channel_id=1, source_target_pairs={{2,1},{3,0},{6,5},{7,4},{10,9},{11,8},{14,13},{15,12},{18,17},{19,... | collective-permute-start | bytes 835592 | tf_op jit(solution)/shard_map/ppermute | solution.py:424
  5.0 7.2 %collective-permute-start = (f32[1088,256]{1,0:T(8,128)S(1)}, f32[1088,256]{1,0:T(8,128)S(1)}, u32[]{:S(2)}, u32[]{:S(2)}) collective-permute-start(f32[1088,256]{1,0:T(8,128)S(1)} %shard_map.49), channel_id=1, source_target_pairs={{2,0},{3,1},{6,4},{7,5},{10,8},{11,9},{14,12},{15,13},{18,16},{19,... | collective-permute-start | bytes 3342344 | tf_op jit(solution)/shard_map/ppermute | solution.py:486
  6.4 6.0 %collective-permute-start.5 = (f32[32,512]{1,0:T(8,128)S(1)}, f32[32,512]{1,0:T(8,128)S(1)}, u32[]{:S(2)}, u32[]{:S(2)}) collective-permute-start(f32[32,512]{1,0:T(8,128)S(1)} %get-tuple-element.67._lower), channel_id=1, source_target_pairs={{28,25},{29,24}} | collective-permute-start | bytes 196616 | tf_op jit(solution)/shard_map/ppermute | solution.py:424
  7.0 5.4 %collective-permute-start.4 = (f32[32,512]{1,0:T(8,128)S(1)}, f32[32,512]{1,0:T(8,128)S(1)}, u32[]{:S(2)}, u32[]{:S(2)}) collective-permute-start(f32[32,512]{1,0:T(8,128)S(1)} %get-tuple-element.67._lower), channel_id=1, source_target_pairs={{28,24},{29,25}} | collective-permute-start | bytes 196616 | tf_op jit(solution)/shard_map/ppermute | solution.py:560
  12.5 4.4 %collective-permute-start.7 = (f32[32,512]{1,0:T(8,128)S(1)}, f32[32,512]{1,0:T(8,128)S(1)}, u32[]{:S(2)}, u32[]{:S(2)}) collective-permute-start(f32[32,512]{1,0:T(8,128)S(1)} %get-tuple-element.73._lower), channel_id=1, source_target_pairs={{24,21},{25,20}} | collective-permute-start | bytes 196616 | tf_op jit(solution)/shard_map/ppermute | solution.py:424
  13.1 3.8 %collective-permute-start.6 = (f32[32,512]{1,0:T(8,128)S(1)}, f32[32,512]{1,0:T(8,128)S(1)}, u32[]{:S(2)}, u32[]{:S(2)}) collective-permute-start(f32[32,512]{1,0:T(8,128)S(1)} %get-tuple-element.73._lower), channel_id=1, source_target_pairs={{24,20},{25,21}} | collective-permute-start | bytes 196616 | tf_op jit(solution)/shard_map/ppermute | solution.py:560
  15.5 5.7 %collective-permute-start.14 = (f32[1088,256]{1,0:T(8,128)S(1)}, f32[1088,256]{1,0:T(8,128)S(1)}, u32[]{:S(2)}, u32[]{:S(2)}) collective-permute-start(f32[1088,256]{1,0:T(8,128)S(1)} %get-tuple-element.88), channel_id=1, source_target_pairs={{4,8},{5,9},{8,12},{9,13}} | collective-permute-start | bytes 3342344 | tf_op jit(solution)/shard_map/ppermute | solution.py:525
  16.2 5.0 %collective-permute-start.15 = (f32[512,256]{1,0:T(8,128)S(1)}, f32[512,256]{1,0:T(8,128)S(1)}, u32[]{:S(2)}, u32[]{:S(2)}) collective-permute-start(f32[512,256]{1,0:T(8,128)S(1)} %get-tuple-element.89), channel_id=1, source_target_pairs={{4,9},{5,8},{8,13},{9,12}} | collective-permute-start | bytes 1572872 | tf_op jit(solution)/shard_map/ppermute | solution.py:424
  17.0 1.3 %collective-permute-start.9 = (f32[32,512]{1,0:T(8,128)S(1)}, f32[32,512]{1,0:T(8,128)S(1)}, u32[]{:S(2)}, u32[]{:S(2)}) collective-permute-start(f32[32,512]{1,0:T(8,128)S(1)} %get-tuple-element.77._lower), channel_id=1, source_target_pairs={{20,17},{21,16}} | collective-permute-start | bytes 196616 | tf_op jit(solution)/shard_map/ppermute | solution.py:424
  17.6 0.7 %collective-permute-start.8 = (f32[32,512]{1,0:T(8,128)S(1)}, f32[32,512]{1,0:T(8,128)S(1)}, u32[]{:S(2)}, u32[]{:S(2)}) collective-permute-start(f32[32,512]{1,0:T(8,128)S(1)} %get-tuple-element.77._lower), channel_id=1, source_target_pairs={{20,16},{21,17}} | collective-permute-start | bytes 196616 | tf_op jit(solution)/shard_map/ppermute | solution.py:560
  18.4 1.3 %collective-permute-start.11 = (f32[32,512]{1,0:T(8,128)S(1)}, f32[32,512]{1,0:T(8,128)S(1)}, u32[]{:S(2)}, u32[]{:S(2)}) collective-permute-start(f32[32,512]{1,0:T(8,128)S(1)} %get-tuple-element.81._lower), channel_id=1, source_target_pairs={{16,13},{17,12}} | collective-permute-start | bytes 196616 | tf_op jit(solution)/shard_map/ppermute | solution.py:424
  19.1 0.7 %collective-permute-start.10 = (f32[32,512]{1,0:T(8,128)S(1)}, f32[32,512]{1,0:T(8,128)S(1)}, u32[]{:S(2)}, u32[]{:S(2)}) collective-permute-start(f32[32,512]{1,0:T(8,128)S(1)} %get-tuple-element.81._lower), channel_id=1, source_target_pairs={{16,12},{17,13}} | collective-permute-start | bytes 196616 | tf_op jit(solution)/shard_map/ppermute | solution.py:560
  19.8 1.3 %collective-permute-start.13 = (f32[32,512]{1,0:T(8,128)S(1)}, f32[32,512]{1,0:T(8,128)S(1)}, u32[]{:S(2)}, u32[]{:S(2)}) collective-permute-start(f32[32,512]{1,0:T(8,128)S(1)} %get-tuple-element.85.rest_6_.lower), channel_id=1, source_target_pairs={{12,9},{13,8}} | collective-permute-start | bytes 196616 | tf_op jit(solution)/shard_map/ppermute | solution.py:424
  20.5 1.0 %collective-permute-start.12 = (f32[32,512]{1,0:T(8,128)S(1)}, f32[32,512]{1,0:T(8,128)S(1)}, u32[]{:S(2)}, u32[]{:S(2)}) collective-permute-start(f32[32,512]{1,0:T(8,128)S(1)} %get-tuple-element.85.rest_6_.lower), channel_id=1, source_target_pairs={{12,8},{13,9}} | collective-permute-start | bytes 196616 | tf_op jit(solution)/shard_map/ppermute | solution.py:560
  21.6 27.9 %collective-permute-start.16 = (f32[32,896]{1,0:T(8,128)S(1)}, f32[32,896]{1,0:T(8,128)S(1)}, u32[]{:S(2)}, u32[]{:S(2)}) collective-permute-start(f32[32,896]{1,0:T(8,128)S(1)} %get-tuple-element.95), channel_id=1, source_target_pairs={{9,0}} | collective-permute-start | bytes 344072 | tf_op jit(solution)/shard_map/ppermute | solution.py:554
  22.9 26.9 %collective-permute-start.17 = (f32[32,896]{1,0:T(8,128)S(1)}, f32[32,896]{1,0:T(8,128)S(1)}, u32[]{:S(2)}, u32[]{:S(2)}) collective-permute-start(f32[32,896]{1,0:T(8,128)S(1)} %get-tuple-element.96), channel_id=1, source_target_pairs={{8,0},{9,1}} | collective-permute-start | bytes 344072 | tf_op jit(solution)/shard_map/ppermute | solution.py:555
  24.2 25.6 %collective-permute-start.18 = (f32[32,896]{1,0:T(8,128)S(1)}, f32[32,896]{1,0:T(8,128)S(1)}, u32[]{:S(2)}, u32[]{:S(2)}) collective-permute-start(f32[32,896]{1,0:T(8,128)S(1)} %get-tuple-element.97), channel_id=1, source_target_pairs={{8,1}} | collective-permute-start | bytes 344072 | tf_op jit(solution)/shard_map/ppermute | solution.py:556
  24.8 24.9 %collective-permute-start.19 = (f32[32,896]{1,0:T(8,128)S(1)}, f32[32,896]{1,0:T(8,128)S(1)}, u32[]{:S(2)}, u32[]{:S(2)}) collective-permute-start(f32[32,896]{1,0:T(8,128)S(1)} %get-tuple-element.98), channel_id=1, source_target_pairs={{12,5},{13,4}} | collective-permute-start | bytes 344072 | tf_op jit(solution)/shard_map/ppermute | solution.py:424
  25.5 24.2 %collective-permute-start.20 = (f32[32,896]{1,0:T(8,128)S(1)}, f32[32,896]{1,0:T(8,128)S(1)}, u32[]{:S(2)}, u32[]{:S(2)}) collective-permute-start(f32[32,896]{1,0:T(8,128)S(1)} %get-tuple-element.99), channel_id=1, source_target_pairs={{12,4},{13,5}} | collective-permute-start | bytes 344072 | tf_op jit(solution)/shard_map/ppermute | solution.py:572
  50.1 2.2 %collective-permute-start.21 = (f32[32,512]{1,0:T(8,128)S(1)}, f32[32,512]{1,0:T(8,128)S(1)}, u32[]{:S(2)}, u32[]{:S(2)}) collective-permute-start(f32[32,512]{1,0:T(8,128)S(1)} %get-tuple-element.104), channel_id=1, source_target_pairs={{0,2},{1,3},{4,6},{5,7},{8,10},{9,11},{12,14},{13,15},{16,18},{17,... | collective-permute-start | bytes 196616 | tf_op jit(solution)/shard_map/ppermute | solution.py:602

commit v11 on v10

--- a/solution.py
+++ b/solution.py
@@ -49,37 +49,41 @@
         rim[1] = columns(False)
 
 
-def const_kernel(normals, inv, const, again, inv_high, inv_low, normals_in, inv_in, sems):
+def fuse_kernel(
+    mask, normals, inv, lag, const, again, own, near_high, near_low, mask_in, normals_in, inv_in, lag_in, sems
+):
     blocks, length = inv.shape[1], inv.shape[2]
+    window, cols = lag.shape[2], normals.shape[1]
+    edge = (window - length) // 2
+    cuts = (0, edge, edge + length, window)
     moves = [pltpu.make_async_copy(normals.at[0], normals_in, sems.at[0])]
     for b in range(blocks):
         moves.append(pltpu.make_async_copy(inv.at[0, b], inv_in.at[b], sems.at[1 + b]))
+    moves.append(pltpu.make_async_copy(mask.at[0], mask_in, sems.at[1 + blocks]))
+    for b in range(blocks):
+        moves.append(pltpu.make_async_copy(lag.at[0, b], lag_in.at[b], sems.at[2 + blocks + b]))
     for move in moves:
         move.start()
     moves[0].wait()
+    pairs = []
     for b in range(blocks):
         at = slice(b * length, (b + 1) * length)
         high, low = halves(normals_in[:, at])
         moves[1 + b].wait()
-        inv_high[b], inv_low[b] = halves(inv_in[b])
-        const[:, at] = triple(high, low, inv_high[b], inv_low[b])
-    again[...] = const[...]
-
-
-def fuse_kernel(mask, const, inv_high, inv_low, lag, own, near_high, near_low):
-    blocks, window, length = lag.shape[1:]
-    edge = (window - length) // 2
-    cols = const.shape[0]
-    cuts = (0, edge, edge + length, window)
-    flags = mask[0].astype(jnp.float32)
-    for b in range(blocks):
-        at = blocks * window + b * cols
-        own[at : at + cols] = const[:, b * length : (b + 1) * length]
+        pairs.append(halves(inv_in[b]))
+        value = triple(high, low, *pairs[b])
+        const[:, at] = value
+        again[:, at] = value
+        own[blocks * window + b * cols : blocks * window + (b + 1) * cols] = value
+    moves[1 + blocks].wait()
+    flags = mask_in[...].astype(jnp.float32)
+    for b in range(blocks):
+        moves[2 + blocks + b].wait()
         for part in range(3):
             lo, hi = cuts[part], cuts[part + 1]
             rows = slice(b * window + lo, b * window + hi)
-            high, low = halves(lag[0, b, lo:hi] * flags[b : b + 1, part : part + 1])
-            value = triple(high, low, inv_high[b], inv_low[b])
+            high, low = halves(lag_in[b, lo:hi] * flags[b : b + 1, part : part + 1])
+            value = triple(high, low, *pairs[b])
             own[rows] = value
             near_high[rows], near_low[rows] = halves(value)
 
@@ -310,24 +314,33 @@
         const = slice(blocks * sites + b * cols, blocks * sites + (b + 1) * cols)
         to_own[:, at] = own_rows[const] + stacked_dot(mid, slice(0, sites), own_high[rows], own_low[rows])
     to_next[:, :halo] = to_own[:, pl.ds(near, halo)]
-    for b in range(blocks):
-        value = None
-        cuts = [cuts_of(blocks, length, sites, span, last)[b] for last in (True, False)]
-        for chunk in range(0, max(hi - lo for lo, hi, _ in cuts), edge):
-            starts, froms, there = [], [], []
-            for last, (lo, hi, packed) in zip((True, False), cuts):
-                count = hi - lo
-                there.append(chunk < count)
-                starts.append(packed + chunk if chunk < count else 0)
-                froms.append((0 if last else sites - count) + chunk if chunk < count else 0)
-            start = pl.multiple_of(jnp.where(row == 0, starts[1], starts[0]), edge)
-            source = pl.multiple_of(jnp.where(row == 0, froms[1], froms[0]), edge)
-            rows = pl.ds(start, edge)
-            product = stacked_dot(mid, pl.ds(source, edge), other_high[rows], other_low[rows])
-            if not all(there):
-                product = jnp.where((row == 0) == there[1], product, 0.0)
-            value = product if value is None else value + product
-        far_mid[:, b * length : (b + 1) * length] = value
+    left, right = (cuts_of(blocks, length, sites, span, last) for last in (False, True))
+    for b in range(blocks):
+        far_mid[:, b * length : (b + 1) * length] = jnp.zeros((cols, length), jnp.float32)
+        spans = [(lo_hi[1] - lo_hi[0], lo_hi[2]) for lo_hi in (left[b], right[b])]
+        both = min(spans[0][0], spans[1][0])
+        more = max(spans[0][0], spans[1][0]) - both
+        long_left = spans[0][0] > spans[1][0]
+        for count, offset, only in ((both, 0, False), (more, both, True)):
+            if not count:
+                continue
+            at = slice(b * length, (b + 1) * length)
+            starts = [packed + offset for _, packed in spans]
+            froms = [sites - spans[0][0] + offset, offset]
+            if only:
+                starts = [starts[0] if long_left else starts[1]] * 2
+                froms = [froms[0] if long_left else froms[1]] * 2
+
+            def add(b=b, at=at, starts=starts, froms=froms, count=count):
+                start = pl.multiple_of(jnp.where(row == 0, starts[0], starts[1]), edge)
+                source = pl.multiple_of(jnp.where(row == 0, froms[0], froms[1]), edge)
+                rows = pl.ds(start, count)
+                far_mid[:, at] += stacked_dot(mid, pl.ds(source, count), other_high[rows], other_low[rows])
+
+            if only:
+                pl.when((row == 0) == long_left)(add)
+            else:
+                add()
     to_next[:, halo:] = far_mid[...]
     away = pl.multiple_of(jnp.where(row == 0, 0, sites - halo), edge)
     to_own[:, sites:] = far_mid[:, pl.ds(away, halo)]
@@ -436,37 +449,26 @@
     tall = blocks * window
     jump = 2
     jumps = rows == 2 and pairs > 5
-    const, again, inv_high, inv_low = pl.pallas_call(
-        const_kernel,
+    const, again, near, near_high, near_low = pl.pallas_call(
+        fuse_kernel,
         out_shape=(
-            shape((cols, sites), f32), shape((cols, sites), f32),
-            shape((blocks, length, length), bf16), shape((blocks, length, length), bf16),
+            shape((cols, sites), f32), shape((cols, sites), f32), shape((tall + blocks * cols, length), f32),
+            shape((tall, length), bf16), shape((tall, length), bf16),
         ),
-        in_specs=[HBM] * 2,
-        out_specs=(VMEM,) * 4,
+        in_specs=[HBM] * 4,
+        out_specs=(VMEM,) * 5,
         scratch_shapes=[
+            pltpu.VMEM(fill_mask.shape[1:], fill_mask.dtype),
             pltpu.VMEM(normals.shape[1:], f32),
             pltpu.VMEM(inv_diag.shape[1:], f32),
-            pltpu.SemaphoreType.DMA((1 + blocks,)),
+            pltpu.VMEM(lag_coupling.shape[1:], f32),
+            pltpu.SemaphoreType.DMA((2 + 2 * blocks,)),
         ],
         compiler_params=PARAMS,
-        cost_estimate=pl.CostEstimate(flops=5*10**9, bytes_accessed=0, transcendentals=0),
-    )(*[pltpu.with_memory_space_constraint(a, pltpu.HBM) for a in (normals, inv_diag)])
+    )(*[pltpu.with_memory_space_constraint(a, pltpu.HBM) for a in (fill_mask, normals, inv_diag, lag_coupling)])
     odd, even = range(1, times, 2), range(0, times, 2)
     first_next = cross(const, odd[-1:], even[-1:])
     first_own = lax.ppermute(again, BOTH, link(odd[-1:], even[-1:]))
-    near, near_high, near_low = pl.pallas_call(
-        fuse_kernel,
-        out_shape=(
-            shape((tall + blocks * cols, length), f32), shape((tall, length), bf16), shape((tall, length), bf16),
-        ),
-        in_specs=[VMEM] * 5,
-        out_specs=(VMEM,) * 3,
-        compiler_params=PARAMS,
-        cost_estimate=pl.CostEstimate(
-            flops=6 * (tall + cols * blocks) * length * length, bytes_accessed=16 * tall * length, transcendentals=0
-        ),
-    )(fill_mask, const, inv_high, inv_low, lag_coupling)
     edges = pl.pallas_call(
         functools.partial(edge_kernel, sides, blocks, cols),
         out_shape=shape((sides, window + cols, edge), f32),

time: 53.6 us -> 54.1 us (level)
    ppermute x1, waiting for transfers between devices: 23.2 us -> 23.8 us  [local(): first_in = lax.ppermute(to_next, BOTH, [(2 * source[0] + 1, 2 * target[0])])]
    pallas_call x2 -> x1, Pallas kernels: 2.25 us -> 2.39 us  [local(): pl.pallas_call(fuse_kernel, out_shape=(shape((cols, sites), f32), shape((...]
  transfers between devices with their start and end apart: 22 -> 22, of which waited for: 4 -> 4; matrix products, arithmetic and copies ran while one was open for 0% -> 0% of each run, Pallas kernels for 6% -> 5%
where the time goes in v11:
time: 54.1 us; the launch traced here: 53.4 us
  waiting for transfers between devices  28.9 us (53%)
  starting transfers between devices  17.9 us (33%)
  Pallas kernels  5.52 us (10%)
  other arithmetic  0.64 us (1%)
    ppermute x1, waiting for transfers between devices, local(): first_in = lax.ppermute(to_next, BOTH, [(2 * source[0] + 1, 2 * target[0])])  23.8 us
    ppermute x9, starting transfers between devices, cross(): return lax.ppermute(value, BOTH, perm)  6.64 us
    ppermute x1, waiting for transfers between devices, local(): far = lax.ppermute(near, BOTH, link(odd[:-1], even[:-1]))  4.49 us
    ppermute x5, starting transfers between devices, local(): own_in = lax.ppermute(lower, BOTH, link(source, target))  3.32 us
    pallas_call x1, Pallas kernels, local(): pl.pallas_call(fuse_kernel, out_shape=(shape((cols, sites), f32), shape((...  2.39 us
    pallas_call x2, Pallas kernels, pair_matrix(): pl.pallas_call(functools.partial(pair_kernel, (pairs - 2, first), jumps),...  1.67 us
    ppermute x1, starting transfers between devices, local(): far = lax.ppermute(near, BOTH, link(odd[:-1], even[:-1]))  1.29 us
    ppermute x1, starting transfers between devices, local(): first_in = lax.ppermute(to_next, BOTH, [(2 * source[0] + 1, 2 * target[0])])  1.29 us
  transfers between devices with their start and end apart: 22, of which 4 were waited for; matrix products, arithmetic and copies ran while one was open for 0% of the time, Pallas kernels for 5%

profile of v11, /device:TPU:0, one launch (start us, length us, event | category | flops | bytes accessed | tf_op | source)
XLA Modules:
  0.0 53.4 jit_solution(8216167899551327749)
XLA Ops:
  0.0 2.4 %shard_map.46 = (f32[32,512]{1,0:T(8,128)S(1)}, f32[32,512]{1,0:T(8,128)S(1)}, f32[1088,256]{1,0:T(8,128)S(1)}, bf16[1024,256]{1,0:T(8,128)(2,1)S(1)}, bf16[1024,256]{1,0:T(8,128)(2,1)S(1)}) custom-call(s32[1,2,3]{2,1,0:T(2,128)} %mask.1, f32[1,32,512]{2,1,0:T(8,128)} %normals.1, f32[1,2,256,256]{3,2,1,0:T(8,128)} %inv.1, f32[1,2,512,256]{3,2,1,0:T(8,128)} %lag.1), custom_call_target="tpu_custom_call" | custom-call | tf_op jit(solution)/shard_map/pallas_call | solution.py:452
  2.4 0.7 %collective-permute-start.2 = (f32[32,512]{1,0:T(8,128)S(1)}, f32[32,512]{1,0:T(8,128)S(1)}, u32[]{:S(2)}, u32[]{:S(2)}) collective-permute-start(f32[32,512]{1,0:T(8,128)S(1)} %get-tuple-element.58.refs_6_.const), channel_id=1, source_target_pairs={{30,29},{31,28}} | collective-permute-start | bytes 196616 | tf_op jit(solution)/shard_map/ppermute | solution.py:437
  3.1 0.7 %collective-permute-start.3 = (f32[32,512]{1,0:T(8,128)S(1)}, f32[32,512]{1,0:T(8,128)S(1)}, u32[]{:S(2)}, u32[]{:S(2)}) collective-permute-start(f32[32,512]{1,0:T(8,128)S(1)} %get-tuple-element.62), channel_id=1, source_target_pairs={{30,28},{31,29}} | collective-permute-start | bytes 196616 | tf_op jit(solution)/shard_map/ppermute | solution.py:471
  3.8 1.3 %collective-permute-start.1 = (f32[1,544,128]{2,1,0:T(8,128)S(1)}, f32[1,544,128]{2,1,0:T(8,128)S(1)}, u32[]{:S(2)}, u32[]{:S(2)}) collective-permute-start(f32[1,544,128]{2,1,0:T(8,128)S(1)} %shard_map.47._edges), channel_id=1, source_target_pairs={{2,1},{3,0},{6,5},{7,4},{10,9},{11,8},{14,13},{15,12},{18,17},{19,... | collective-permute-start | bytes 835592 | tf_op jit(solution)/shard_map/ppermute | solution.py:437
  5.1 1.3 %collective-permute-start = (f32[1088,256]{1,0:T(8,128)S(1)}, f32[1088,256]{1,0:T(8,128)S(1)}, u32[]{:S(2)}, u32[]{:S(2)}) collective-permute-start(f32[1088,256]{1,0:T(8,128)S(1)} %shard_map.48), channel_id=1, source_target_pairs={{2,0},{3,1},{6,4},{7,5},{10,8},{11,9},{14,12},{15,13},{18,16},{19,... | collective-permute-start | bytes 3342344 | tf_op jit(solution)/shard_map/ppermute | solution.py:488
  6.4 0.0 collective-permute-done.2.next_in
  6.4 0.0 collective-permute-done.3.own_in
  6.5 0.7 %collective-permute-start.5 = (f32[32,512]{1,0:T(8,128)S(1)}, f32[32,512]{1,0:T(8,128)S(1)}, u32[]{:S(2)}, u32[]{:S(2)}) collective-permute-start(f32[32,512]{1,0:T(8,128)S(1)} %get-tuple-element.63._lower), channel_id=1, source_target_pairs={{28,25},{29,24}} | collective-permute-start | bytes 196616 | tf_op jit(solution)/shard_map/ppermute | solution.py:437
  7.1 0.7 %collective-permute-start.4 = (f32[32,512]{1,0:T(8,128)S(1)}, f32[32,512]{1,0:T(8,128)S(1)}, u32[]{:S(2)}, u32[]{:S(2)}) collective-permute-start(f32[32,512]{1,0:T(8,128)S(1)} %get-tuple-element.63._lower), channel_id=1, source_target_pairs={{28,24},{29,25}} | collective-permute-start | bytes 196616 | tf_op jit(solution)/shard_map/ppermute | solution.py:562
  7.8 4.5 %collective-permute-done.far.refs_0_.rest_5_ = f32[1088,256]{1,0:T(8,128)S(1)} collective-permute-done((f32[1088,256]{1,0:T(8,128)S(1)}, f32[1088,256]{1,0:T(8,128)S(1)}, u32[]{:S(2)}, u32[]{:S(2)}) %collective-permute-start) | collective-permute-done | bytes 1114144 | tf_op jit(solution)/shard_map/ppermute | solution.py:488
  12.3 0.1 shard_map.49
  12.4 0.0 collective-permute-done.1.refs_1_
  12.5 0.0 collective-permute-done.5.next_in
  12.5 0.0 collective-permute-done.4.own_in
  12.6 0.7 %collective-permute-start.7 = (f32[32,512]{1,0:T(8,128)S(1)}, f32[32,512]{1,0:T(8,128)S(1)}, u32[]{:S(2)}, u32[]{:S(2)}) collective-permute-start(f32[32,512]{1,0:T(8,128)S(1)} %get-tuple-element.69._lower), channel_id=1, source_target_pairs={{24,21},{25,20}} | collective-permute-start | bytes 196616 | tf_op jit(solution)/shard_map/ppermute | solution.py:437
  13.3 0.7 %collective-permute-start.6 = (f32[32,512]{1,0:T(8,128)S(1)}, f32[32,512]{1,0:T(8,128)S(1)}, u32[]{:S(2)}, u32[]{:S(2)}) collective-permute-start(f32[32,512]{1,0:T(8,128)S(1)} %get-tuple-element.69._lower), channel_id=1, source_target_pairs={{24,20},{25,21}} | collective-permute-start | bytes 196616 | tf_op jit(solution)/shard_map/ppermute | solution.py:562
  13.9 1.6 %shard_map.50 = (bf16[2048,256]{1,0:T(8,128)(2,1)S(1)}, bf16[2048,256]{1,0:T(8,128)(2,1)S(1)}, f32[32,512]{1,0:T(8,128)S(1)}, f32[1088,256]{1,0:T(8,128)S(1)}, f32[512,256]{1,0:T(8,128)S(1)}) custom-call(f32[1088,256]{1,0:T(8,128)S(1)} %collective-permute-done.far.refs_0_.rest_5_, f32[1,544,128]{2,1,0:T(8,128)S(1)} %collective-permute-done.1.refs_1_, ...), custom_call_target="tpu_custom_call" | custom-call | flops 1000000000 | tf_op jit(solution)/shard_map/pallas_call | solution.py:511
  15.6 0.7 %collective-permute-start.14 = (f32[1088,256]{1,0:T(8,128)S(1)}, f32[1088,256]{1,0:T(8,128)S(1)}, u32[]{:S(2)}, u32[]{:S(2)}) collective-permute-start(f32[1088,256]{1,0:T(8,128)S(1)} %get-tuple-element.84), channel_id=1, source_target_pairs={{4,8},{5,9},{8,12},{9,13}} | collective-permute-start | bytes 3342344 | tf_op jit(solution)/shard_map/ppermute | solution.py:527
  16.3 0.7 %collective-permute-start.15 = (f32[512,256]{1,0:T(8,128)S(1)}, f32[512,256]{1,0:T(8,128)S(1)}, u32[]{:S(2)}, u32[]{:S(2)}) collective-permute-start(f32[512,256]{1,0:T(8,128)S(1)} %get-tuple-element.85), channel_id=1, source_target_pairs={{4,9},{5,8},{8,13},{9,12}} | collective-permute-start | bytes 1572872 | tf_op jit(solution)/shard_map/ppermute | solution.py:437
  17.0 0.0 collective-permute-done.7.next_in
  17.1 0.0 collective-permute-done.6.own_in
  17.1 0.7 %collective-permute-start.9 = (f32[32,512]{1,0:T(8,128)S(1)}, f32[32,512]{1,0:T(8,128)S(1)}, u32[]{:S(2)}, u32[]{:S(2)}) collective-permute-start(f32[32,512]{1,0:T(8,128)S(1)} %get-tuple-element.73._lower), channel_id=1, source_target_pairs={{20,17},{21,16}} | collective-permute-start | bytes 196616 | tf_op jit(solution)/shard_map/ppermute | solution.py:437
  17.8 0.7 %collective-permute-start.8 = (f32[32,512]{1,0:T(8,128)S(1)}, f32[32,512]{1,0:T(8,128)S(1)}, u32[]{:S(2)}, u32[]{:S(2)}) collective-permute-start(f32[32,512]{1,0:T(8,128)S(1)} %get-tuple-element.73._lower), channel_id=1, source_target_pairs={{20,16},{21,17}} | collective-permute-start | bytes 196616 | tf_op jit(solution)/shard_map/ppermute | solution.py:562
  18.4 0.0 collective-permute-done.9.next_in
  18.5 0.0 collective-permute-done.8.own_in
  18.5 0.7 %collective-permute-start.11 = (f32[32,512]{1,0:T(8,128)S(1)}, f32[32,512]{1,0:T(8,128)S(1)}, u32[]{:S(2)}, u32[]{:S(2)}) collective-permute-start(f32[32,512]{1,0:T(8,128)S(1)} %get-tuple-element.77._lower), channel_id=1, source_target_pairs={{16,13},{17,12}} | collective-permute-start | bytes 196616 | tf_op jit(solution)/shard_map/ppermute | solution.py:437
  19.2 0.7 %collective-permute-start.10 = (f32[32,512]{1,0:T(8,128)S(1)}, f32[32,512]{1,0:T(8,128)S(1)}, u32[]{:S(2)}, u32[]{:S(2)}) collective-permute-start(f32[32,512]{1,0:T(8,128)S(1)} %get-tuple-element.77._lower), channel_id=1, source_target_pairs={{16,12},{17,13}} | collective-permute-start | bytes 196616 | tf_op jit(solution)/shard_map/ppermute | solution.py:562
  19.9 0.0 collective-permute-done.11.next_in
  19.9 0.0 collective-permute-done.10.own_in
  19.9 0.7 %collective-permute-start.13 = (f32[32,512]{1,0:T(8,128)S(1)}, f32[32,512]{1,0:T(8,128)S(1)}, u32[]{:S(2)}, u32[]{:S(2)}) collective-permute-start(f32[32,512]{1,0:T(8,128)S(1)} %get-tuple-element.81.rest_6_.lower), channel_id=1, source_target_pairs={{12,9},{13,8}} | collective-permute-start | bytes 196616 | tf_op jit(solution)/shard_map/ppermute | solution.py:437
  20.6 0.7 %collective-permute-start.12 = (f32[32,512]{1,0:T(8,128)S(1)}, f32[32,512]{1,0:T(8,128)S(1)}, u32[]{:S(2)}, u32[]{:S(2)}) collective-permute-start(f32[32,512]{1,0:T(8,128)S(1)} %get-tuple-element.81.rest_6_.lower), channel_id=1, source_target_pairs={{12,8},{13,9}} | collective-permute-start | bytes 196616 | tf_op jit(solution)/shard_map/ppermute | solution.py:562
  21.3 0.0 collective-permute-done.13.next_in
  21.3 0.0 collective-permute-done.15.other_rows
  21.3 0.0 collective-permute-done.14.own_rows.rest_0_
  21.3 0.2 shard_map.62
  21.6 0.0 collective-permute-done.12.own_in
  21.7 1.3 %collective-permute-start.16 = (f32[32,896]{1,0:T(8,128)S(1)}, f32[32,896]{1,0:T(8,128)S(1)}, u32[]{:S(2)}, u32[]{:S(2)}) collective-permute-start(f32[32,896]{1,0:T(8,128)S(1)} %get-tuple-element.91), channel_id=1, source_target_pairs={{9,0}} | collective-permute-start | bytes 344072 | tf_op jit(solution)/shard_map/ppermute | solution.py:556
  23.0 1.3 %collective-permute-start.17 = (f32[32,896]{1,0:T(8,128)S(1)}, f32[32,896]{1,0:T(8,128)S(1)}, u32[]{:S(2)}, u32[]{:S(2)}) collective-permute-start(f32[32,896]{1,0:T(8,128)S(1)} %get-tuple-element.92), channel_id=1, source_target_pairs={{8,0},{9,1}} | collective-permute-start | bytes 344072 | tf_op jit(solution)/shard_map/ppermute | solution.py:557
  24.3 0.7 %collective-permute-start.18 = (f32[32,896]{1,0:T(8,128)S(1)}, f32[32,896]{1,0:T(8,128)S(1)}, u32[]{:S(2)}, u32[]{:S(2)}) collective-permute-start(f32[32,896]{1,0:T(8,128)S(1)} %get-tuple-element.93), channel_id=1, source_target_pairs={{8,1}} | collective-permute-start | bytes 344072 | tf_op jit(solution)/shard_map/ppermute | solution.py:558
  24.9 0.7 %collective-permute-start.19 = (f32[32,896]{1,0:T(8,128)S(1)}, f32[32,896]{1,0:T(8,128)S(1)}, u32[]{:S(2)}, u32[]{:S(2)}) collective-permute-start(f32[32,896]{1,0:T(8,128)S(1)} %get-tuple-element.94), channel_id=1, source_target_pairs={{12,5},{13,4}} | collective-permute-start | bytes 344072 | tf_op jit(solution)/shard_map/ppermute | solution.py:437
  25.6 0.7 %collective-permute-start.20 = (f32[32,896]{1,0:T(8,128)S(1)}, f32[32,896]{1,0:T(8,128)S(1)}, u32[]{:S(2)}, u32[]{:S(2)}) collective-permute-start(f32[32,896]{1,0:T(8,128)S(1)} %get-tuple-element.95), channel_id=1, source_target_pairs={{12,4},{13,5}} | collective-permute-start | bytes 344072 | tf_op jit(solution)/shard_map/ppermute | solution.py:574
  26.3 23.8 %collective-permute-done.16.rest_0_ = f32[32,896]{1,0:T(8,128)S(1)} collective-permute-done((f32[32,896]{1,0:T(8,128)S(1)}, f32[32,896]{1,0:T(8,128)S(1)}, u32[]{:S(2)}, u32[]{:S(2)}) %collective-permute-start.16) | collective-permute-done | bytes 114720 | tf_op jit(solution)/shard_map/ppermute | solution.py:556
  50.1 0.1 collective-permute-done.17.rest_1_
  50.2 0.3 shard_map.65
  50.6 1.3 %collective-permute-start.21 = (f32[32,512]{1,0:T(8,128)S(1)}, f32[32,512]{1,0:T(8,128)S(1)}, u32[]{:S(2)}, u32[]{:S(2)}) collective-permute-start(f32[32,512]{1,0:T(8,128)S(1)} %get-tuple-element.100), channel_id=1, source_target_pairs={{0,2},{1,3},{4,6},{5,7},{8,10},{9,11},{12,14},{13,15},{16,18},{17,... | collective-permute-start | bytes 196616 | tf_op jit(solution)/shard_map/ppermute | solution.py:604
  51.9 0.5 shard_map.66
  52.4 0.4 collective-permute-done.21
  52.7 0.6 %select_bitcast_fusion = f32[1,32,512]{2,1,0:T(8,128)} fusion(f32[32,512]{1,0:T(8,128)S(1)} %shard_map.66, f32[32,512]{1,0:T(8,128)S(1)} %collective-permute-done.21, pred[]{:T(512)S(6)} %eq.5), kind=kLoop, calls=%fused_computation | loop fusion | flops 16384 | bytes 196609 | tf_op jit(solution)/shard_map/broadcast_in_dim | solution.py:614
  (21 shorter events, 0.3 us)
Async XLA Ops:
  2.4 4.0 %collective-permute-start.2 = (f32[32,512]{1,0:T(8,128)S(1)}, f32[32,512]{1,0:T(8,128)S(1)}, u32[]{:S(2)}, u32[]{:S(2)}) collective-permute-start(f32[32,512]{1,0:T(8,128)S(1)} %get-tuple-element.58.refs_6_.const), channel_id=1, source_target_pairs={{30,29},{31,28}} | collective-permute-start | bytes 196616 | tf_op jit(solution)/shard_map/ppermute | solution.py:437
  3.1 3.3 %collective-permute-start.3 = (f32[32,512]{1,0:T(8,128)S(1)}, f32[32,512]{1,0:T(8,128)S(1)}, u32[]{:S(2)}, u32[]{:S(2)}) collective-permute-start(f32[32,512]{1,0:T(8,128)S(1)} %get-tuple-element.62), channel_id=1, source_target_pairs={{30,28},{31,29}} | collective-permute-start | bytes 196616 | tf_op jit(solution)/shard_map/ppermute | solution.py:471
  3.8 8.7 %collective-permute-start.1 = (f32[1,544,128]{2,1,0:T(8,128)S(1)}, f32[1,544,128]{2,1,0:T(8,128)S(1)}, u32[]{:S(2)}, u32[]{:S(2)}) collective-permute-start(f32[1,544,128]{2,1,0:T(8,128)S(1)} %shard_map.47._edges), channel_id=1, source_target_pairs={{2,1},{3,0},{6,5},{7,4},{10,9},{11,8},{14,13},{15,12},{18,17},{19,... | collective-permute-start | bytes 835592 | tf_op jit(solution)/shard_map/ppermute | solution.py:437
  5.1 7.2 %collective-permute-start = (f32[1088,256]{1,0:T(8,128)S(1)}, f32[1088,256]{1,0:T(8,128)S(1)}, u32[]{:S(2)}, u32[]{:S(2)}) collective-permute-start(f32[1088,256]{1,0:T(8,128)S(1)} %shard_map.48), channel_id=1, source_target_pairs={{2,0},{3,1},{6,4},{7,5},{10,8},{11,9},{14,12},{15,13},{18,16},{19,... | collective-permute-start | bytes 3342344 | tf_op jit(solution)/shard_map/ppermute | solution.py:488
  6.5 6.0 %collective-permute-start.5 = (f32[32,512]{1,0:T(8,128)S(1)}, f32[32,512]{1,0:T(8,128)S(1)}, u32[]{:S(2)}, u32[]{:S(2)}) collective-permute-start(f32[32,512]{1,0:T(8,128)S(1)} %get-tuple-element.63._lower), channel_id=1, source_target_pairs={{28,25},{29,24}} | collective-permute-start | bytes 196616 | tf_op jit(solution)/shard_map/ppermute | solution.py:437
  7.1 5.4 %collective-permute-start.4 = (f32[32,512]{1,0:T(8,128)S(1)}, f32[32,512]{1,0:T(8,128)S(1)}, u32[]{:S(2)}, u32[]{:S(2)}) collective-permute-start(f32[32,512]{1,0:T(8,128)S(1)} %get-tuple-element.63._lower), channel_id=1, source_target_pairs={{28,24},{29,25}} | collective-permute-start | bytes 196616 | tf_op jit(solution)/shard_map/ppermute | solution.py:562
  12.6 4.4 %collective-permute-start.7 = (f32[32,512]{1,0:T(8,128)S(1)}, f32[32,512]{1,0:T(8,128)S(1)}, u32[]{:S(2)}, u32[]{:S(2)}) collective-permute-start(f32[32,512]{1,0:T(8,128)S(1)} %get-tuple-element.69._lower), channel_id=1, source_target_pairs={{24,21},{25,20}} | collective-permute-start | bytes 196616 | tf_op jit(solution)/shard_map/ppermute | solution.py:437
  13.3 3.8 %collective-permute-start.6 = (f32[32,512]{1,0:T(8,128)S(1)}, f32[32,512]{1,0:T(8,128)S(1)}, u32[]{:S(2)}, u32[]{:S(2)}) collective-permute-start(f32[32,512]{1,0:T(8,128)S(1)} %get-tuple-element.69._lower), channel_id=1, source_target_pairs={{24,20},{25,21}} | collective-permute-start | bytes 196616 | tf_op jit(solution)/shard_map/ppermute | solution.py:562
  15.6 5.7 %collective-permute-start.14 = (f32[1088,256]{1,0:T(8,128)S(1)}, f32[1088,256]{1,0:T(8,128)S(1)}, u32[]{:S(2)}, u32[]{:S(2)}) collective-permute-start(f32[1088,256]{1,0:T(8,128)S(1)} %get-tuple-element.84), channel_id=1, source_target_pairs={{4,8},{5,9},{8,12},{9,13}} | collective-permute-start | bytes 3342344 | tf_op jit(solution)/shard_map/ppermute | solution.py:527
  16.3 5.0 %collective-permute-start.15 = (f32[512,256]{1,0:T(8,128)S(1)}, f32[512,256]{1,0:T(8,128)S(1)}, u32[]{:S(2)}, u32[]{:S(2)}) collective-permute-start(f32[512,256]{1,0:T(8,128)S(1)} %get-tuple-element.85), channel_id=1, source_target_pairs={{4,9},{5,8},{8,13},{9,12}} | collective-permute-start | bytes 1572872 | tf_op jit(solution)/shard_map/ppermute | solution.py:437
  17.1 1.3 %collective-permute-start.9 = (f32[32,512]{1,0:T(8,128)S(1)}, f32[32,512]{1,0:T(8,128)S(1)}, u32[]{:S(2)}, u32[]{:S(2)}) collective-permute-start(f32[32,512]{1,0:T(8,128)S(1)} %get-tuple-element.73._lower), channel_id=1, source_target_pairs={{20,17},{21,16}} | collective-permute-start | bytes 196616 | tf_op jit(solution)/shard_map/ppermute | solution.py:437
  17.8 0.7 %collective-permute-start.8 = (f32[32,512]{1,0:T(8,128)S(1)}, f32[32,512]{1,0:T(8,128)S(1)}, u32[]{:S(2)}, u32[]{:S(2)}) collective-permute-start(f32[32,512]{1,0:T(8,128)S(1)} %get-tuple-element.73._lower), channel_id=1, source_target_pairs={{20,16},{21,17}} | collective-permute-start | bytes 196616 | tf_op jit(solution)/shard_map/ppermute | solution.py:562
  18.5 1.3 %collective-permute-start.11 = (f32[32,512]{1,0:T(8,128)S(1)}, f32[32,512]{1,0:T(8,128)S(1)}, u32[]{:S(2)}, u32[]{:S(2)}) collective-permute-start(f32[32,512]{1,0:T(8,128)S(1)} %get-tuple-element.77._lower), channel_id=1, source_target_pairs={{16,13},{17,12}} | collective-permute-start | bytes 196616 | tf_op jit(solution)/shard_map/ppermute | solution.py:437
  19.2 0.7 %collective-permute-start.10 = (f32[32,512]{1,0:T(8,128)S(1)}, f32[32,512]{1,0:T(8,128)S(1)}, u32[]{:S(2)}, u32[]{:S(2)}) collective-permute-start(f32[32,512]{1,0:T(8,128)S(1)} %get-tuple-element.77._lower), channel_id=1, source_target_pairs={{16,12},{17,13}} | collective-permute-start | bytes 196616 | tf_op jit(solution)/shard_map/ppermute | solution.py:562
  19.9 1.3 %collective-permute-start.13 = (f32[32,512]{1,0:T(8,128)S(1)}, f32[32,512]{1,0:T(8,128)S(1)}, u32[]{:S(2)}, u32[]{:S(2)}) collective-permute-start(f32[32,512]{1,0:T(8,128)S(1)} %get-tuple-element.81.rest_6_.lower), channel_id=1, source_target_pairs={{12,9},{13,8}} | collective-permute-start | bytes 196616 | tf_op jit(solution)/shard_map/ppermute | solution.py:437
  20.6 1.0 %collective-permute-start.12 = (f32[32,512]{1,0:T(8,128)S(1)}, f32[32,512]{1,0:T(8,128)S(1)}, u32[]{:S(2)}, u32[]{:S(2)}) collective-permute-start(f32[32,512]{1,0:T(8,128)S(1)} %get-tuple-element.81.rest_6_.lower), channel_id=1, source_target_pairs={{12,8},{13,9}} | collective-permute-start | bytes 196616 | tf_op jit(solution)/shard_map/ppermute | solution.py:562
  21.7 28.4 %collective-permute-start.16 = (f32[32,896]{1,0:T(8,128)S(1)}, f32[32,896]{1,0:T(8,128)S(1)}, u32[]{:S(2)}, u32[]{:S(2)}) collective-permute-start(f32[32,896]{1,0:T(8,128)S(1)} %get-tuple-element.91), channel_id=1, source_target_pairs={{9,0}} | collective-permute-start | bytes 344072 | tf_op jit(solution)/shard_map/ppermute | solution.py:556
  23.0 27.3 %collective-permute-start.17 = (f32[32,896]{1,0:T(8,128)S(1)}, f32[32,896]{1,0:T(8,128)S(1)}, u32[]{:S(2)}, u32[]{:S(2)}) collective-permute-start(f32[32,896]{1,0:T(8,128)S(1)} %get-tuple-element.92), channel_id=1, source_target_pairs={{8,0},{9,1}} | collective-permute-start | bytes 344072 | tf_op jit(solution)/shard_map/ppermute | solution.py:557
  24.3 26.0 %collective-permute-start.18 = (f32[32,896]{1,0:T(8,128)S(1)}, f32[32,896]{1,0:T(8,128)S(1)}, u32[]{:S(2)}, u32[]{:S(2)}) collective-permute-start(f32[32,896]{1,0:T(8,128)S(1)} %get-tuple-element.93), channel_id=1, source_target_pairs={{8,1}} | collective-permute-start | bytes 344072 | tf_op jit(solution)/shard_map/ppermute | solution.py:558
  24.9 25.3 %collective-permute-start.19 = (f32[32,896]{1,0:T(8,128)S(1)}, f32[32,896]{1,0:T(8,128)S(1)}, u32[]{:S(2)}, u32[]{:S(2)}) collective-permute-start(f32[32,896]{1,0:T(8,128)S(1)} %get-tuple-element.94), channel_id=1, source_target_pairs={{12,5},{13,4}} | collective-permute-start | bytes 344072 | tf_op jit(solution)/shard_map/ppermute | solution.py:437
  25.6 24.6 %collective-permute-start.20 = (f32[32,896]{1,0:T(8,128)S(1)}, f32[32,896]{1,0:T(8,128)S(1)}, u32[]{:S(2)}, u32[]{:S(2)}) collective-permute-start(f32[32,896]{1,0:T(8,128)S(1)} %get-tuple-element.95), channel_id=1, source_target_pairs={{12,4},{13,5}} | collective-permute-start | bytes 344072 | tf_op jit(solution)/shard_map/ppermute | solution.py:574
  50.6 2.2 %collective-permute-start.21 = (f32[32,512]{1,0:T(8,128)S(1)}, f32[32,512]{1,0:T(8,128)S(1)}, u32[]{:S(2)}, u32[]{:S(2)}) collective-permute-start(f32[32,512]{1,0:T(8,128)S(1)} %get-tuple-element.100), channel_id=1, source_target_pairs={{0,2},{1,3},{4,6},{5,7},{8,10},{9,11},{12,14},{13,15},{16,18},{17,... | collective-permute-start | bytes 196616 | tf_op jit(solution)/shard_map/ppermute | solution.py:604

commit v12 on v10

--- a/solution.py
+++ b/solution.py
@@ -310,24 +310,16 @@
         const = slice(blocks * sites + b * cols, blocks * sites + (b + 1) * cols)
         to_own[:, at] = own_rows[const] + stacked_dot(mid, slice(0, sites), own_high[rows], own_low[rows])
     to_next[:, :halo] = to_own[:, pl.ds(near, halo)]
-    for b in range(blocks):
-        value = None
-        cuts = [cuts_of(blocks, length, sites, span, last)[b] for last in (True, False)]
-        for chunk in range(0, max(hi - lo for lo, hi, _ in cuts), edge):
-            starts, froms, there = [], [], []
-            for last, (lo, hi, packed) in zip((True, False), cuts):
-                count = hi - lo
-                there.append(chunk < count)
-                starts.append(packed + chunk if chunk < count else 0)
-                froms.append((0 if last else sites - count) + chunk if chunk < count else 0)
-            start = pl.multiple_of(jnp.where(row == 0, starts[1], starts[0]), edge)
-            source = pl.multiple_of(jnp.where(row == 0, froms[1], froms[0]), edge)
-            rows = pl.ds(start, edge)
-            product = stacked_dot(mid, pl.ds(source, edge), other_high[rows], other_low[rows])
-            if not all(there):
-                product = jnp.where((row == 0) == there[1], product, 0.0)
-            value = product if value is None else value + product
-        far_mid[:, b * length : (b + 1) * length] = value
+    pieces = []
+    for rows, from_last, from_first in (
+        (slice(0, edge), sites - halo, 0),
+        (slice(edge, halo), sites - length, 0),
+        (slice(halo, halo + edge), sites - edge, length),
+    ):
+        source = pl.multiple_of(jnp.where(row == 0, from_last, from_first), edge)
+        pieces.append(stacked_dot(mid, pl.ds(source, rows.stop - rows.start), other_high[rows], other_low[rows]))
+    far_mid[:, :length] = pieces[0] + jnp.where(row == 0, pieces[1], 0.0)
+    far_mid[:, length:] = pieces[2] + jnp.where(row == 0, 0.0, pieces[1])
     to_next[:, halo:] = far_mid[...]
     away = pl.multiple_of(jnp.where(row == 0, 0, sites - halo), edge)
     to_own[:, sites:] = far_mid[:, pl.ds(away, halo)]
@@ -435,7 +427,7 @@
 
     tall = blocks * window
     jump = 2
-    jumps = rows == 2 and pairs > 5
+    jumps = rows == 2 and pairs > 5 and blocks == 2
     const, again, inv_high, inv_low = pl.pallas_call(
         const_kernel,
         out_shape=(

time: 53.6 us -> 53.6 us (level)
  no operation moved by 1% of the time
where the time goes in v12:
time: 53.6 us; the launch traced here: 52.8 us
  waiting for transfers between devices  28.4 us (53%)
  starting transfers between devices  17.9 us (33%)
  Pallas kernels  5.38 us (10%)
  other arithmetic  0.64 us (1%)
    ppermute x1, waiting for transfers between devices, local(): first_in = lax.ppermute(to_next, BOTH, [(2 * source[0] + 1, 2 * target[0])])  23.2 us
    ppermute x9, starting transfers between devices, cross(): return lax.ppermute(value, BOTH, perm)  6.64 us
    ppermute x1, waiting for transfers between devices, local(): far = lax.ppermute(near, BOTH, link(odd[:-1], even[:-1]))  4.48 us
    ppermute x5, starting transfers between devices, local(): own_in = lax.ppermute(lower, BOTH, link(source, target))  3.32 us
    pallas_call x2, Pallas kernels, pair_matrix(): pl.pallas_call(functools.partial(pair_kernel, (pairs - 2, first), jumps),...  1.66 us
    pallas_call x1, Pallas kernels, local(): pl.pallas_call(const_kernel, out_shape=(shape((cols, sites), f32), shape(...  1.56 us
    ppermute x1, starting transfers between devices, local(): far = lax.ppermute(near, BOTH, link(odd[:-1], even[:-1]))  1.29 us
    ppermute x1, starting transfers between devices, local(): first_in = lax.ppermute(to_next, BOTH, [(2 * source[0] + 1, 2 * target[0])])  1.29 us
  transfers between devices with their start and end apart: 22, of which 4 were waited for; matrix products, arithmetic and copies ran while one was open for 0% of the time, Pallas kernels for 6%

profile of v12, /device:TPU:0, one launch (start us, length us, event | category | flops | bytes accessed | tf_op | source)
XLA Modules:
  0.0 52.8 jit_solution(16335961672009644680)
XLA Ops:
  0.0 1.6 %shard_map.46 = (f32[32,512]{1,0:T(8,128)S(1)}, f32[32,512]{1,0:T(8,128)S(1)}, bf16[2,256,256]{2,1,0:T(8,128)(2,1)S(1)}, bf16[2,256,256]{2,1,0:T(8,128)(2,1)S(1)}) custom-call(f32[1,32,512]{2,1,0:T(8,128)} %normals.1, f32[1,2,256,256]{3,2,1,0:T(8,128)} %inv.1), custom_call_target="tpu_custom_call" | custom-call | flops 5000000000 | tf_op jit(solution)/shard_map/pallas_call | solution.py:431
  1.6 0.7 %collective-permute-start.2 = (f32[32,512]{1,0:T(8,128)S(1)}, f32[32,512]{1,0:T(8,128)S(1)}, u32[]{:S(2)}, u32[]{:S(2)}) collective-permute-start(f32[32,512]{1,0:T(8,128)S(1)} %get-tuple-element.55.const.refs_6_), channel_id=1, source_target_pairs={{30,29},{31,28}} | collective-permute-start | bytes 196616 | tf_op jit(solution)/shard_map/ppermute | solution.py:416
  2.2 0.7 %collective-permute-start.3 = (f32[32,512]{1,0:T(8,128)S(1)}, f32[32,512]{1,0:T(8,128)S(1)}, u32[]{:S(2)}, u32[]{:S(2)}) collective-permute-start(f32[32,512]{1,0:T(8,128)S(1)} %get-tuple-element.66), channel_id=1, source_target_pairs={{30,28},{31,29}} | collective-permute-start | bytes 196616 | tf_op jit(solution)/shard_map/ppermute | solution.py:449
  2.9 0.7 %shard_map.47 = (f32[1088,256]{1,0:T(8,128)S(1)}, bf16[1024,256]{1,0:T(8,128)(2,1)S(1)}, bf16[1024,256]{1,0:T(8,128)(2,1)S(1)}) custom-call(s32[1,2,3]{2,1,0:T(2,128)S(1)} %copy-done.1, f32[32,512]{1,0:T(8,128)S(1)} %get-tuple-element.55.const.refs_6_, bf16[2,256,256]{2,1,0:T(8,128)(2,1)S(1)} %get-tuple-element.56.inv_high, ...), custom_call_target="tpu_custom_call" | custom-call | flops 427819008 | bytes 4194304 | tf_op jit(solution)/shard_map/pallas_call | solution.py:450
  3.7 1.3 %collective-permute-start.1 = (f32[1,544,128]{2,1,0:T(8,128)S(1)}, f32[1,544,128]{2,1,0:T(8,128)S(1)}, u32[]{:S(2)}, u32[]{:S(2)}) collective-permute-start(f32[1,544,128]{2,1,0:T(8,128)S(1)} %shard_map.48._edges), channel_id=1, source_target_pairs={{2,1},{3,0},{6,5},{7,4},{10,9},{11,8},{14,13},{15,12},{18,17},{19,... | collective-permute-start | bytes 835592 | tf_op jit(solution)/shard_map/ppermute | solution.py:416
  5.0 1.3 %collective-permute-start = (f32[1088,256]{1,0:T(8,128)S(1)}, f32[1088,256]{1,0:T(8,128)S(1)}, u32[]{:S(2)}, u32[]{:S(2)}) collective-permute-start(f32[1088,256]{1,0:T(8,128)S(1)} %shard_map.49), channel_id=1, source_target_pairs={{2,0},{3,1},{6,4},{7,5},{10,8},{11,9},{14,12},{15,13},{18,16},{19,... | collective-permute-start | bytes 3342344 | tf_op jit(solution)/shard_map/ppermute | solution.py:478
  6.3 0.0 collective-permute-done.2.next_in
  6.3 0.0 collective-permute-done.3.own_in
  6.4 0.7 %collective-permute-start.5 = (f32[32,512]{1,0:T(8,128)S(1)}, f32[32,512]{1,0:T(8,128)S(1)}, u32[]{:S(2)}, u32[]{:S(2)}) collective-permute-start(f32[32,512]{1,0:T(8,128)S(1)} %get-tuple-element.67._lower), channel_id=1, source_target_pairs={{28,25},{29,24}} | collective-permute-start | bytes 196616 | tf_op jit(solution)/shard_map/ppermute | solution.py:416
  7.0 0.7 %collective-permute-start.4 = (f32[32,512]{1,0:T(8,128)S(1)}, f32[32,512]{1,0:T(8,128)S(1)}, u32[]{:S(2)}, u32[]{:S(2)}) collective-permute-start(f32[32,512]{1,0:T(8,128)S(1)} %get-tuple-element.67._lower), channel_id=1, source_target_pairs={{28,24},{29,25}} | collective-permute-start | bytes 196616 | tf_op jit(solution)/shard_map/ppermute | solution.py:552
  7.7 4.5 %collective-permute-done.far.refs_0_.rest_5_ = f32[1088,256]{1,0:T(8,128)S(1)} collective-permute-done((f32[1088,256]{1,0:T(8,128)S(1)}, f32[1088,256]{1,0:T(8,128)S(1)}, u32[]{:S(2)}, u32[]{:S(2)}) %collective-permute-start) | collective-permute-done | bytes 1114144 | tf_op jit(solution)/shard_map/ppermute | solution.py:478
  12.2 0.1 shard_map.50
  12.3 0.0 collective-permute-done.1.refs_1_
  12.4 0.0 collective-permute-done.5.next_in
  12.4 0.0 collective-permute-done.4.own_in
  12.5 0.7 %collective-permute-start.7 = (f32[32,512]{1,0:T(8,128)S(1)}, f32[32,512]{1,0:T(8,128)S(1)}, u32[]{:S(2)}, u32[]{:S(2)}) collective-permute-start(f32[32,512]{1,0:T(8,128)S(1)} %get-tuple-element.73._lower), channel_id=1, source_target_pairs={{24,21},{25,20}} | collective-permute-start | bytes 196616 | tf_op jit(solution)/shard_map/ppermute | solution.py:416
  13.1 0.7 %collective-permute-start.6 = (f32[32,512]{1,0:T(8,128)S(1)}, f32[32,512]{1,0:T(8,128)S(1)}, u32[]{:S(2)}, u32[]{:S(2)}) collective-permute-start(f32[32,512]{1,0:T(8,128)S(1)} %get-tuple-element.73._lower), channel_id=1, source_target_pairs={{24,20},{25,21}} | collective-permute-start | bytes 196616 | tf_op jit(solution)/shard_map/ppermute | solution.py:552
  13.8 1.6 %shard_map.51 = (bf16[2048,256]{1,0:T(8,128)(2,1)S(1)}, bf16[2048,256]{1,0:T(8,128)(2,1)S(1)}, f32[32,512]{1,0:T(8,128)S(1)}, f32[1088,256]{1,0:T(8,128)S(1)}, f32[512,256]{1,0:T(8,128)S(1)}) custom-call(f32[1088,256]{1,0:T(8,128)S(1)} %collective-permute-done.far.refs_0_.rest_5_, f32[1,544,128]{2,1,0:T(8,128)S(1)} %collective-permute-done.1.refs_1_, ...), custom_call_target="tpu_custom_call" | custom-call | flops 1000000000 | tf_op jit(solution)/shard_map/pallas_call | solution.py:501
  15.5 0.7 %collective-permute-start.14 = (f32[1088,256]{1,0:T(8,128)S(1)}, f32[1088,256]{1,0:T(8,128)S(1)}, u32[]{:S(2)}, u32[]{:S(2)}) collective-permute-start(f32[1088,256]{1,0:T(8,128)S(1)} %get-tuple-element.88), channel_id=1, source_target_pairs={{4,8},{5,9},{8,12},{9,13}} | collective-permute-start | bytes 3342344 | tf_op jit(solution)/shard_map/ppermute | solution.py:517
  16.2 0.7 %collective-permute-start.15 = (f32[512,256]{1,0:T(8,128)S(1)}, f32[512,256]{1,0:T(8,128)S(1)}, u32[]{:S(2)}, u32[]{:S(2)}) collective-permute-start(f32[512,256]{1,0:T(8,128)S(1)} %get-tuple-element.89), channel_id=1, source_target_pairs={{4,9},{5,8},{8,13},{9,12}} | collective-permute-start | bytes 1572872 | tf_op jit(solution)/shard_map/ppermute | solution.py:416
  17.0 0.7 %collective-permute-start.9 = (f32[32,512]{1,0:T(8,128)S(1)}, f32[32,512]{1,0:T(8,128)S(1)}, u32[]{:S(2)}, u32[]{:S(2)}) collective-permute-start(f32[32,512]{1,0:T(8,128)S(1)} %get-tuple-element.77._lower), channel_id=1, source_target_pairs={{20,17},{21,16}} | collective-permute-start | bytes 196616 | tf_op jit(solution)/shard_map/ppermute | solution.py:416
  17.6 0.7 %collective-permute-start.8 = (f32[32,512]{1,0:T(8,128)S(1)}, f32[32,512]{1,0:T(8,128)S(1)}, u32[]{:S(2)}, u32[]{:S(2)}) collective-permute-start(f32[32,512]{1,0:T(8,128)S(1)} %get-tuple-element.77._lower), channel_id=1, source_target_pairs={{20,16},{21,17}} | collective-permute-start | bytes 196616 | tf_op jit(solution)/shard_map/ppermute | solution.py:552
  18.3 0.0 collective-permute-done.9.next_in
  18.4 0.0 collective-permute-done.8.own_in
  18.4 0.7 %collective-permute-start.11 = (f32[32,512]{1,0:T(8,128)S(1)}, f32[32,512]{1,0:T(8,128)S(1)}, u32[]{:S(2)}, u32[]{:S(2)}) collective-permute-start(f32[32,512]{1,0:T(8,128)S(1)} %get-tuple-element.81._lower), channel_id=1, source_target_pairs={{16,13},{17,12}} | collective-permute-start | bytes 196616 | tf_op jit(solution)/shard_map/ppermute | solution.py:416
  19.1 0.7 %collective-permute-start.10 = (f32[32,512]{1,0:T(8,128)S(1)}, f32[32,512]{1,0:T(8,128)S(1)}, u32[]{:S(2)}, u32[]{:S(2)}) collective-permute-start(f32[32,512]{1,0:T(8,128)S(1)} %get-tuple-element.81._lower), channel_id=1, source_target_pairs={{16,12},{17,13}} | collective-permute-start | bytes 196616 | tf_op jit(solution)/shard_map/ppermute | solution.py:552
  19.8 0.7 %collective-permute-start.13 = (f32[32,512]{1,0:T(8,128)S(1)}, f32[32,512]{1,0:T(8,128)S(1)}, u32[]{:S(2)}, u32[]{:S(2)}) collective-permute-start(f32[32,512]{1,0:T(8,128)S(1)} %get-tuple-element.85.rest_6_.lower), channel_id=1, source_target_pairs={{12,9},{13,8}} | collective-permute-start | bytes 196616 | tf_op jit(solution)/shard_map/ppermute | solution.py:416
  20.5 0.7 %collective-permute-start.12 = (f32[32,512]{1,0:T(8,128)S(1)}, f32[32,512]{1,0:T(8,128)S(1)}, u32[]{:S(2)}, u32[]{:S(2)}) collective-permute-start(f32[32,512]{1,0:T(8,128)S(1)} %get-tuple-element.85.rest_6_.lower), channel_id=1, source_target_pairs={{12,8},{13,9}} | collective-permute-start | bytes 196616 | tf_op jit(solution)/shard_map/ppermute | solution.py:552
  21.2 0.0 collective-permute-done.13.next_in
  21.2 0.0 collective-permute-done.15.other_rows
  21.2 0.0 collective-permute-done.14.own_rows.rest_0_
  21.2 0.2 shard_map.63
  21.5 0.0 collective-permute-done.12.own_in
  21.6 1.3 %collective-permute-start.16 = (f32[32,896]{1,0:T(8,128)S(1)}, f32[32,896]{1,0:T(8,128)S(1)}, u32[]{:S(2)}, u32[]{:S(2)}) collective-permute-start(f32[32,896]{1,0:T(8,128)S(1)} %get-tuple-element.95), channel_id=1, source_target_pairs={{9,0}} | collective-permute-start | bytes 344072 | tf_op jit(solution)/shard_map/ppermute | solution.py:546
  22.9 1.3 %collective-permute-start.17 = (f32[32,896]{1,0:T(8,128)S(1)}, f32[32,896]{1,0:T(8,128)S(1)}, u32[]{:S(2)}, u32[]{:S(2)}) collective-permute-start(f32[32,896]{1,0:T(8,128)S(1)} %get-tuple-element.96), channel_id=1, source_target_pairs={{8,0},{9,1}} | collective-permute-start | bytes 344072 | tf_op jit(solution)/shard_map/ppermute | solution.py:547
  24.2 0.7 %collective-permute-start.18 = (f32[32,896]{1,0:T(8,128)S(1)}, f32[32,896]{1,0:T(8,128)S(1)}, u32[]{:S(2)}, u32[]{:S(2)}) collective-permute-start(f32[32,896]{1,0:T(8,128)S(1)} %get-tuple-element.97), channel_id=1, source_target_pairs={{8,1}} | collective-permute-start | bytes 344072 | tf_op jit(solution)/shard_map/ppermute | solution.py:548
  24.8 0.7 %collective-permute-start.19 = (f32[32,896]{1,0:T(8,128)S(1)}, f32[32,896]{1,0:T(8,128)S(1)}, u32[]{:S(2)}, u32[]{:S(2)}) collective-permute-start(f32[32,896]{1,0:T(8,128)S(1)} %get-tuple-element.98), channel_id=1, source_target_pairs={{12,5},{13,4}} | collective-permute-start | bytes 344072 | tf_op jit(solution)/shard_map/ppermute | solution.py:416
  25.5 0.7 %collective-permute-start.20 = (f32[32,896]{1,0:T(8,128)S(1)}, f32[32,896]{1,0:T(8,128)S(1)}, u32[]{:S(2)}, u32[]{:S(2)}) collective-permute-start(f32[32,896]{1,0:T(8,128)S(1)} %get-tuple-element.99), channel_id=1, source_target_pairs={{12,4},{13,5}} | collective-permute-start | bytes 344072 | tf_op jit(solution)/shard_map/ppermute | solution.py:564
  26.2 23.2 %collective-permute-done.16.rest_0_ = f32[32,896]{1,0:T(8,128)S(1)} collective-permute-done((f32[32,896]{1,0:T(8,128)S(1)}, f32[32,896]{1,0:T(8,128)S(1)}, u32[]{:S(2)}, u32[]{:S(2)}) %collective-permute-start.16) | collective-permute-done | bytes 114720 | tf_op jit(solution)/shard_map/ppermute | solution.py:546
  49.4 0.3 collective-permute-done.17.rest_1_
  49.7 0.0 collective-permute-done.18.rest_2_
  49.7 0.0 collective-permute-done.19.rest_3_
  49.7 0.0 collective-permute-done.20.rest_4_
  49.7 0.3 shard_map.66
  50.0 1.3 %collective-permute-start.21 = (f32[32,512]{1,0:T(8,128)S(1)}, f32[32,512]{1,0:T(8,128)S(1)}, u32[]{:S(2)}, u32[]{:S(2)}) collective-permute-start(f32[32,512]{1,0:T(8,128)S(1)} %get-tuple-element.104), channel_id=1, source_target_pairs={{0,2},{1,3},{4,6},{5,7},{8,10},{9,11},{12,14},{13,15},{16,18},{17,... | collective-permute-start | bytes 196616 | tf_op jit(solution)/shard_map/ppermute | solution.py:594
  51.3 0.5 shard_map.67
  51.8 0.4 collective-permute-done.21
  52.2 0.6 %select_bitcast_fusion = f32[1,32,512]{2,1,0:T(8,128)} fusion(f32[32,512]{1,0:T(8,128)S(1)} %shard_map.67, f32[32,512]{1,0:T(8,128)S(1)} %collective-permute-done.21, pred[]{:T(512)S(6)} %eq.5), kind=kLoop, calls=%fused_computation | loop fusion | flops 16384 | bytes 196609 | tf_op jit(solution)/shard_map/broadcast_in_dim | solution.py:604
  (26 shorter events, 0.4 us)
Async XLA Ops:
  0.0 2.9 %copy-start = (f32[1,2,512,256]{3,2,1,0:T(8,128)S(1)}, f32[1,2,512,256]{3,2,1,0:T(8,128)}, u32[]{:S(2)}) copy-start(f32[1,2,512,256]{3,2,1,0:T(8,128)} %lag.1) | copy-start | bytes 3145732
  0.0 2.9 %copy-start.1 = (s32[1,2,3]{2,1,0:T(2,128)S(1)}, s32[1,2,3]{2,1,0:T(2,128)}, u32[]{:S(2)}) copy-start(s32[1,2,3]{2,1,0:T(2,128)} %mask.1) | copy-start | bytes 76
  1.6 4.7 %collective-permute-start.2 = (f32[32,512]{1,0:T(8,128)S(1)}, f32[32,512]{1,0:T(8,128)S(1)}, u32[]{:S(2)}, u32[]{:S(2)}) collective-permute-start(f32[32,512]{1,0:T(8,128)S(1)} %get-tuple-element.55.const.refs_6_), channel_id=1, source_target_pairs={{30,29},{31,28}} | collective-permute-start | bytes 196616 | tf_op jit(solution)/shard_map/ppermute | solution.py:416
  2.2 4.0 %collective-permute-start.3 = (f32[32,512]{1,0:T(8,128)S(1)}, f32[32,512]{1,0:T(8,128)S(1)}, u32[]{:S(2)}, u32[]{:S(2)}) collective-permute-start(f32[32,512]{1,0:T(8,128)S(1)} %get-tuple-element.66), channel_id=1, source_target_pairs={{30,28},{31,29}} | collective-permute-start | bytes 196616 | tf_op jit(solution)/shard_map/ppermute | solution.py:449
  3.7 8.7 %collective-permute-start.1 = (f32[1,544,128]{2,1,0:T(8,128)S(1)}, f32[1,544,128]{2,1,0:T(8,128)S(1)}, u32[]{:S(2)}, u32[]{:S(2)}) collective-permute-start(f32[1,544,128]{2,1,0:T(8,128)S(1)} %shard_map.48._edges), channel_id=1, source_target_pairs={{2,1},{3,0},{6,5},{7,4},{10,9},{11,8},{14,13},{15,12},{18,17},{19,... | collective-permute-start | bytes 835592 | tf_op jit(solution)/shard_map/ppermute | solution.py:416
  5.0 7.2 %collective-permute-start = (f32[1088,256]{1,0:T(8,128)S(1)}, f32[1088,256]{1,0:T(8,128)S(1)}, u32[]{:S(2)}, u32[]{:S(2)}) collective-permute-start(f32[1088,256]{1,0:T(8,128)S(1)} %shard_map.49), channel_id=1, source_target_pairs={{2,0},{3,1},{6,4},{7,5},{10,8},{11,9},{14,12},{15,13},{18,16},{19,... | collective-permute-start | bytes 3342344 | tf_op jit(solution)/shard_map/ppermute | solution.py:478
  6.4 6.0 %collective-permute-start.5 = (f32[32,512]{1,0:T(8,128)S(1)}, f32[32,512]{1,0:T(8,128)S(1)}, u32[]{:S(2)}, u32[]{:S(2)}) collective-permute-start(f32[32,512]{1,0:T(8,128)S(1)} %get-tuple-element.67._lower), channel_id=1, source_target_pairs={{28,25},{29,24}} | collective-permute-start | bytes 196616 | tf_op jit(solution)/shard_map/ppermute | solution.py:416
  7.0 5.4 %collective-permute-start.4 = (f32[32,512]{1,0:T(8,128)S(1)}, f32[32,512]{1,0:T(8,128)S(1)}, u32[]{:S(2)}, u32[]{:S(2)}) collective-permute-start(f32[32,512]{1,0:T(8,128)S(1)} %get-tuple-element.67._lower), channel_id=1, source_target_pairs={{28,24},{29,25}} | collective-permute-start | bytes 196616 | tf_op jit(solution)/shard_map/ppermute | solution.py:552
  12.5 4.4 %collective-permute-start.7 = (f32[32,512]{1,0:T(8,128)S(1)}, f32[32,512]{1,0:T(8,128)S(1)}, u32[]{:S(2)}, u32[]{:S(2)}) collective-permute-start(f32[32,512]{1,0:T(8,128)S(1)} %get-tuple-element.73._lower), channel_id=1, source_target_pairs={{24,21},{25,20}} | collective-permute-start | bytes 196616 | tf_op jit(solution)/shard_map/ppermute | solution.py:416
  13.1 3.8 %collective-permute-start.6 = (f32[32,512]{1,0:T(8,128)S(1)}, f32[32,512]{1,0:T(8,128)S(1)}, u32[]{:S(2)}, u32[]{:S(2)}) collective-permute-start(f32[32,512]{1,0:T(8,128)S(1)} %get-tuple-element.73._lower), channel_id=1, source_target_pairs={{24,20},{25,21}} | collective-permute-start | bytes 196616 | tf_op jit(solution)/shard_map/ppermute | solution.py:552
  15.5 5.7 %collective-permute-start.14 = (f32[1088,256]{1,0:T(8,128)S(1)}, f32[1088,256]{1,0:T(8,128)S(1)}, u32[]{:S(2)}, u32[]{:S(2)}) collective-permute-start(f32[1088,256]{1,0:T(8,128)S(1)} %get-tuple-element.88), channel_id=1, source_target_pairs={{4,8},{5,9},{8,12},{9,13}} | collective-permute-start | bytes 3342344 | tf_op jit(solution)/shard_map/ppermute | solution.py:517
  16.2 5.0 %collective-permute-start.15 = (f32[512,256]{1,0:T(8,128)S(1)}, f32[512,256]{1,0:T(8,128)S(1)}, u32[]{:S(2)}, u32[]{:S(2)}) collective-permute-start(f32[512,256]{1,0:T(8,128)S(1)} %get-tuple-element.89), channel_id=1, source_target_pairs={{4,9},{5,8},{8,13},{9,12}} | collective-permute-start | bytes 1572872 | tf_op jit(solution)/shard_map/ppermute | solution.py:416
  17.0 1.3 %collective-permute-start.9 = (f32[32,512]{1,0:T(8,128)S(1)}, f32[32,512]{1,0:T(8,128)S(1)}, u32[]{:S(2)}, u32[]{:S(2)}) collective-permute-start(f32[32,512]{1,0:T(8,128)S(1)} %get-tuple-element.77._lower), channel_id=1, source_target_pairs={{20,17},{21,16}} | collective-permute-start | bytes 196616 | tf_op jit(solution)/shard_map/ppermute | solution.py:416
  17.6 0.7 %collective-permute-start.8 = (f32[32,512]{1,0:T(8,128)S(1)}, f32[32,512]{1,0:T(8,128)S(1)}, u32[]{:S(2)}, u32[]{:S(2)}) collective-permute-start(f32[32,512]{1,0:T(8,128)S(1)} %get-tuple-element.77._lower), channel_id=1, source_target_pairs={{20,16},{21,17}} | collective-permute-start | bytes 196616 | tf_op jit(solution)/shard_map/ppermute | solution.py:552
  18.4 1.3 %collective-permute-start.11 = (f32[32,512]{1,0:T(8,128)S(1)}, f32[32,512]{1,0:T(8,128)S(1)}, u32[]{:S(2)}, u32[]{:S(2)}) collective-permute-start(f32[32,512]{1,0:T(8,128)S(1)} %get-tuple-element.81._lower), channel_id=1, source_target_pairs={{16,13},{17,12}} | collective-permute-start | bytes 196616 | tf_op jit(solution)/shard_map/ppermute | solution.py:416
  19.1 0.7 %collective-permute-start.10 = (f32[32,512]{1,0:T(8,128)S(1)}, f32[32,512]{1,0:T(8,128)S(1)}, u32[]{:S(2)}, u32[]{:S(2)}) collective-permute-start(f32[32,512]{1,0:T(8,128)S(1)} %get-tuple-element.81._lower), channel_id=1, source_target_pairs={{16,12},{17,13}} | collective-permute-start | bytes 196616 | tf_op jit(solution)/shard_map/ppermute | solution.py:552
  19.8 1.3 %collective-permute-start.13 = (f32[32,512]{1,0:T(8,128)S(1)}, f32[32,512]{1,0:T(8,128)S(1)}, u32[]{:S(2)}, u32[]{:S(2)}) collective-permute-start(f32[32,512]{1,0:T(8,128)S(1)} %get-tuple-element.85.rest_6_.lower), channel_id=1, source_target_pairs={{12,9},{13,8}} | collective-permute-start | bytes 196616 | tf_op jit(solution)/shard_map/ppermute | solution.py:416
  20.5 1.0 %collective-permute-start.12 = (f32[32,512]{1,0:T(8,128)S(1)}, f32[32,512]{1,0:T(8,128)S(1)}, u32[]{:S(2)}, u32[]{:S(2)}) collective-permute-start(f32[32,512]{1,0:T(8,128)S(1)} %get-tuple-element.85.rest_6_.lower), channel_id=1, source_target_pairs={{12,8},{13,9}} | collective-permute-start | bytes 196616 | tf_op jit(solution)/shard_map/ppermute | solution.py:552
  21.6 27.8 %collective-permute-start.16 = (f32[32,896]{1,0:T(8,128)S(1)}, f32[32,896]{1,0:T(8,128)S(1)}, u32[]{:S(2)}, u32[]{:S(2)}) collective-permute-start(f32[32,896]{1,0:T(8,128)S(1)} %get-tuple-element.95), channel_id=1, source_target_pairs={{9,0}} | collective-permute-start | bytes 344072 | tf_op jit(solution)/shard_map/ppermute | solution.py:546
  22.9 26.8 %collective-permute-start.17 = (f32[32,896]{1,0:T(8,128)S(1)}, f32[32,896]{1,0:T(8,128)S(1)}, u32[]{:S(2)}, u32[]{:S(2)}) collective-permute-start(f32[32,896]{1,0:T(8,128)S(1)} %get-tuple-element.96), channel_id=1, source_target_pairs={{8,0},{9,1}} | collective-permute-start | bytes 344072 | tf_op jit(solution)/shard_map/ppermute | solution.py:547
  24.2 25.5 %collective-permute-start.18 = (f32[32,896]{1,0:T(8,128)S(1)}, f32[32,896]{1,0:T(8,128)S(1)}, u32[]{:S(2)}, u32[]{:S(2)}) collective-permute-start(f32[32,896]{1,0:T(8,128)S(1)} %get-tuple-element.97), channel_id=1, source_target_pairs={{8,1}} | collective-permute-start | bytes 344072 | tf_op jit(solution)/shard_map/ppermute | solution.py:548
  24.8 24.9 %collective-permute-start.19 = (f32[32,896]{1,0:T(8,128)S(1)}, f32[32,896]{1,0:T(8,128)S(1)}, u32[]{:S(2)}, u32[]{:S(2)}) collective-permute-start(f32[32,896]{1,0:T(8,128)S(1)} %get-tuple-element.98), channel_id=1, source_target_pairs={{12,5},{13,4}} | collective-permute-start | bytes 344072 | tf_op jit(solution)/shard_map/ppermute | solution.py:416
  25.5 24.2 %collective-permute-start.20 = (f32[32,896]{1,0:T(8,128)S(1)}, f32[32,896]{1,0:T(8,128)S(1)}, u32[]{:S(2)}, u32[]{:S(2)}) collective-permute-start(f32[32,896]{1,0:T(8,128)S(1)} %get-tuple-element.99), channel_id=1, source_target_pairs={{12,4},{13,5}} | collective-permute-start | bytes 344072 | tf_op jit(solution)/shard_map/ppermute | solution.py:564
  50.0 2.2 %collective-permute-start.21 = (f32[32,512]{1,0:T(8,128)S(1)}, f32[32,512]{1,0:T(8,128)S(1)}, u32[]{:S(2)}, u32[]{:S(2)}) collective-permute-start(f32[32,512]{1,0:T(8,128)S(1)} %get-tuple-element.104), channel_id=1, source_target_pairs={{0,2},{1,3},{4,6},{5,7},{8,10},{9,11},{12,14},{13,15},{16,18},{17,... | collective-permute-start | bytes 196616 | tf_op jit(solution)/shard_map/ppermute | solution.py:594

commit v13 on v12

--- a/solution.py
+++ b/solution.py
@@ -49,7 +49,7 @@
         rim[1] = columns(False)
 
 
-def const_kernel(normals, inv, const, again, inv_high, inv_low, normals_in, inv_in, sems):
+def const_kernel(normals, inv, const, inv_high, inv_low, normals_in, inv_in, sems):
     blocks, length = inv.shape[1], inv.shape[2]
     moves = [pltpu.make_async_copy(normals.at[0], normals_in, sems.at[0])]
     for b in range(blocks):
@@ -63,6 +63,9 @@
         moves[1 + b].wait()
         inv_high[b], inv_low[b] = halves(inv_in[b])
         const[:, at] = triple(high, low, inv_high[b], inv_low[b])
+
+
+def again_kernel(const, again):
     again[...] = const[...]
 
 
@@ -428,25 +431,32 @@
     tall = blocks * window
     jump = 2
     jumps = rows == 2 and pairs > 5 and blocks == 2
-    const, again, inv_high, inv_low = pl.pallas_call(
+    const, inv_high, inv_low = pl.pallas_call(
         const_kernel,
         out_shape=(
-            shape((cols, sites), f32), shape((cols, sites), f32),
+            shape((cols, sites), f32),
             shape((blocks, length, length), bf16), shape((blocks, length, length), bf16),
         ),
         in_specs=[HBM] * 2,
-        out_specs=(VMEM,) * 4,
+        out_specs=(VMEM,) * 3,
         scratch_shapes=[
             pltpu.VMEM(normals.shape[1:], f32),
             pltpu.VMEM(inv_diag.shape[1:], f32),
             pltpu.SemaphoreType.DMA((1 + blocks,)),
         ],
         compiler_params=PARAMS,
-        cost_estimate=pl.CostEstimate(flops=5*10**9, bytes_accessed=0, transcendentals=0),
     )(*[pltpu.with_memory_space_constraint(a, pltpu.HBM) for a in (normals, inv_diag)])
+    again = pl.pallas_call(
+        again_kernel,
+        out_shape=shape((cols, sites), f32),
+        in_specs=[VMEM],
+        out_specs=VMEM,
+        compiler_params=PARAMS,
+        cost_estimate=pl.CostEstimate(flops=5 * 10**9, bytes_accessed=0, transcendentals=0),
+    )(const)
     odd, even = range(1, times, 2), range(0, times, 2)
-    first_next = cross(const, odd[-1:], even[-1:])
-    first_own = lax.ppermute(again, BOTH, link(odd[-1:], even[-1:]))
+    first_next = cross(again, odd[-1:], even[-1:])
+    first_own = lax.ppermute(const, BOTH, link(odd[-1:], even[-1:]))
     near, near_high, near_low = pl.pallas_call(
         fuse_kernel,
         out_shape=(

time: 53.6 us -> 53.6 us (level)
  no operation moved by 1% of the time
where the time goes in v13:
time: 53.6 us; the launch traced here: 52.9 us
  waiting for transfers between devices  28.4 us (53%)
  starting transfers between devices  18 us (34%)
  Pallas kernels  5.3 us (10%)
  other arithmetic  0.64 us (1%)
    ppermute x1, waiting for transfers between devices, local(): first_in = lax.ppermute(to_next, BOTH, [(2 * source[0] + 1, 2 * target[0])])  23.2 us
    ppermute x9, starting transfers between devices, cross(): return lax.ppermute(value, BOTH, perm)  6.77 us
    ppermute x1, waiting for transfers between devices, local(): far = lax.ppermute(near, BOTH, link(odd[:-1], even[:-1]))  4.48 us
    ppermute x5, starting transfers between devices, local(): own_in = lax.ppermute(lower, BOTH, link(source, target))  3.32 us
    pallas_call x2, Pallas kernels, pair_matrix(): pl.pallas_call(functools.partial(pair_kernel, (pairs - 2, first), jumps),...  1.67 us
    pallas_call x1, Pallas kernels, local(): pl.pallas_call(const_kernel, out_shape=(shape((cols, sites), f32), shape(...  1.48 us
    ppermute x1, starting transfers between devices, local(): far = lax.ppermute(near, BOTH, link(odd[:-1], even[:-1]))  1.29 us
    ppermute x1, starting transfers between devices, local(): first_in = lax.ppermute(to_next, BOTH, [(2 * source[0] + 1, 2 * target[0])])  1.29 us
  transfers between devices with their start and end apart: 22, of which 4 were waited for; matrix products, arithmetic and copies ran while one was open for 0% of the time, Pallas kernels for 6%

profile of v13, /device:TPU:0, one launch (start us, length us, event | category | flops | bytes accessed | tf_op | source)
XLA Modules:
  0.0 52.9 jit_solution(17288445460946966467)
XLA Ops:
  0.0 1.5 %shard_map.46 = (f32[32,512]{1,0:T(8,128)S(1)}, bf16[2,256,256]{2,1,0:T(8,128)(2,1)S(1)}, bf16[2,256,256]{2,1,0:T(8,128)(2,1)S(1)}) custom-call(f32[1,32,512]{2,1,0:T(8,128)} %normals.1, f32[1,2,256,256]{3,2,1,0:T(8,128)} %inv.1), custom_call_target="tpu_custom_call" | custom-call | tf_op jit(solution)/shard_map/pallas_call | solution.py:434
  1.5 0.0 copy-start
  1.5 0.0 copy-start.1
  1.5 0.8 %collective-permute-start.2 = (f32[32,512]{1,0:T(8,128)S(1)}, f32[32,512]{1,0:T(8,128)S(1)}, u32[]{:S(2)}, u32[]{:S(2)}) collective-permute-start(f32[32,512]{1,0:T(8,128)S(1)} %shard_map.52), channel_id=1, source_target_pairs={{30,29},{31,28}} | collective-permute-start | bytes 196616 | tf_op jit(solution)/shard_map/ppermute | solution.py:419
  2.3 0.7 %collective-permute-start.3 = (f32[32,512]{1,0:T(8,128)S(1)}, f32[32,512]{1,0:T(8,128)S(1)}, u32[]{:S(2)}, u32[]{:S(2)}) collective-permute-start(f32[32,512]{1,0:T(8,128)S(1)} %get-tuple-element.54.const.refs_6_), channel_id=1, source_target_pairs={{30,28},{31,29}} | collective-permute-start | bytes 196616 | tf_op jit(solution)/shard_map/ppermute | solution.py:459
  3.0 0.7 %shard_map.47 = (f32[1088,256]{1,0:T(8,128)S(1)}, bf16[1024,256]{1,0:T(8,128)(2,1)S(1)}, bf16[1024,256]{1,0:T(8,128)(2,1)S(1)}) custom-call(s32[1,2,3]{2,1,0:T(2,128)S(1)} %copy-done.1, f32[32,512]{1,0:T(8,128)S(1)} %get-tuple-element.54.const.refs_6_, bf16[2,256,256]{2,1,0:T(8,128)(2,1)S(1)} %get-tuple-element.55.inv_high, ...), custom_call_target="tpu_custom_call" | custom-call | flops 427819008 | bytes 4194304 | tf_op jit(solution)/shard_map/pallas_call | solution.py:460
  3.8 1.3 %collective-permute-start.1 = (f32[1,544,128]{2,1,0:T(8,128)S(1)}, f32[1,544,128]{2,1,0:T(8,128)S(1)}, u32[]{:S(2)}, u32[]{:S(2)}) collective-permute-start(f32[1,544,128]{2,1,0:T(8,128)S(1)} %shard_map.48._edges), channel_id=1, source_target_pairs={{2,1},{3,0},{6,5},{7,4},{10,9},{11,8},{14,13},{15,12},{18,17},{19,... | collective-permute-start | bytes 835592 | tf_op jit(solution)/shard_map/ppermute | solution.py:419
  5.1 1.3 %collective-permute-start = (f32[1088,256]{1,0:T(8,128)S(1)}, f32[1088,256]{1,0:T(8,128)S(1)}, u32[]{:S(2)}, u32[]{:S(2)}) collective-permute-start(f32[1088,256]{1,0:T(8,128)S(1)} %shard_map.49), channel_id=1, source_target_pairs={{2,0},{3,1},{6,4},{7,5},{10,8},{11,9},{14,12},{15,13},{18,16},{19,... | collective-permute-start | bytes 3342344 | tf_op jit(solution)/shard_map/ppermute | solution.py:488
  6.4 0.0 collective-permute-done.2.next_in
  6.4 0.0 collective-permute-done.3.own_in
  6.4 0.7 %collective-permute-start.5 = (f32[32,512]{1,0:T(8,128)S(1)}, f32[32,512]{1,0:T(8,128)S(1)}, u32[]{:S(2)}, u32[]{:S(2)}) collective-permute-start(f32[32,512]{1,0:T(8,128)S(1)} %get-tuple-element.65._lower), channel_id=1, source_target_pairs={{28,25},{29,24}} | collective-permute-start | bytes 196616 | tf_op jit(solution)/shard_map/ppermute | solution.py:419
  7.1 0.7 %collective-permute-start.4 = (f32[32,512]{1,0:T(8,128)S(1)}, f32[32,512]{1,0:T(8,128)S(1)}, u32[]{:S(2)}, u32[]{:S(2)}) collective-permute-start(f32[32,512]{1,0:T(8,128)S(1)} %get-tuple-element.65._lower), channel_id=1, source_target_pairs={{28,24},{29,25}} | collective-permute-start | bytes 196616 | tf_op jit(solution)/shard_map/ppermute | solution.py:562
  7.8 4.5 %collective-permute-done.far.refs_0_.rest_5_ = f32[1088,256]{1,0:T(8,128)S(1)} collective-permute-done((f32[1088,256]{1,0:T(8,128)S(1)}, f32[1088,256]{1,0:T(8,128)S(1)}, u32[]{:S(2)}, u32[]{:S(2)}) %collective-permute-start) | collective-permute-done | bytes 1114144 | tf_op jit(solution)/shard_map/ppermute | solution.py:488
  12.3 0.1 shard_map.50
  12.4 0.0 collective-permute-done.1.refs_1_
  12.5 0.0 collective-permute-done.4.own_in
  12.5 0.7 %collective-permute-start.7 = (f32[32,512]{1,0:T(8,128)S(1)}, f32[32,512]{1,0:T(8,128)S(1)}, u32[]{:S(2)}, u32[]{:S(2)}) collective-permute-start(f32[32,512]{1,0:T(8,128)S(1)} %get-tuple-element.71._lower), channel_id=1, source_target_pairs={{24,21},{25,20}} | collective-permute-start | bytes 196616 | tf_op jit(solution)/shard_map/ppermute | solution.py:419
  13.2 0.7 %collective-permute-start.6 = (f32[32,512]{1,0:T(8,128)S(1)}, f32[32,512]{1,0:T(8,128)S(1)}, u32[]{:S(2)}, u32[]{:S(2)}) collective-permute-start(f32[32,512]{1,0:T(8,128)S(1)} %get-tuple-element.71._lower), channel_id=1, source_target_pairs={{24,20},{25,21}} | collective-permute-start | bytes 196616 | tf_op jit(solution)/shard_map/ppermute | solution.py:562
  13.9 1.6 %shard_map.51 = (bf16[2048,256]{1,0:T(8,128)(2,1)S(1)}, bf16[2048,256]{1,0:T(8,128)(2,1)S(1)}, f32[32,512]{1,0:T(8,128)S(1)}, f32[1088,256]{1,0:T(8,128)S(1)}, f32[512,256]{1,0:T(8,128)S(1)}) custom-call(f32[1088,256]{1,0:T(8,128)S(1)} %collective-permute-done.far.refs_0_.rest_5_, f32[1,544,128]{2,1,0:T(8,128)S(1)} %collective-permute-done.1.refs_1_, ...), custom_call_target="tpu_custom_call" | custom-call | flops 1000000000 | tf_op jit(solution)/shard_map/pallas_call | solution.py:511
  15.5 0.7 %collective-permute-start.14 = (f32[1088,256]{1,0:T(8,128)S(1)}, f32[1088,256]{1,0:T(8,128)S(1)}, u32[]{:S(2)}, u32[]{:S(2)}) collective-permute-start(f32[1088,256]{1,0:T(8,128)S(1)} %get-tuple-element.86), channel_id=1, source_target_pairs={{4,8},{5,9},{8,12},{9,13}} | collective-permute-start | bytes 3342344 | tf_op jit(solution)/shard_map/ppermute | solution.py:527
  16.3 0.7 %collective-permute-start.15 = (f32[512,256]{1,0:T(8,128)S(1)}, f32[512,256]{1,0:T(8,128)S(1)}, u32[]{:S(2)}, u32[]{:S(2)}) collective-permute-start(f32[512,256]{1,0:T(8,128)S(1)} %get-tuple-element.87), channel_id=1, source_target_pairs={{4,9},{5,8},{8,13},{9,12}} | collective-permute-start | bytes 1572872 | tf_op jit(solution)/shard_map/ppermute | solution.py:419
  17.0 0.0 collective-permute-done.7.next_in
  17.1 0.7 %collective-permute-start.9 = (f32[32,512]{1,0:T(8,128)S(1)}, f32[32,512]{1,0:T(8,128)S(1)}, u32[]{:S(2)}, u32[]{:S(2)}) collective-permute-start(f32[32,512]{1,0:T(8,128)S(1)} %get-tuple-element.75._lower), channel_id=1, source_target_pairs={{20,17},{21,16}} | collective-permute-start | bytes 196616 | tf_op jit(solution)/shard_map/ppermute | solution.py:419
  17.7 0.7 %collective-permute-start.8 = (f32[32,512]{1,0:T(8,128)S(1)}, f32[32,512]{1,0:T(8,128)S(1)}, u32[]{:S(2)}, u32[]{:S(2)}) collective-permute-start(f32[32,512]{1,0:T(8,128)S(1)} %get-tuple-element.75._lower), channel_id=1, source_target_pairs={{20,16},{21,17}} | collective-permute-start | bytes 196616 | tf_op jit(solution)/shard_map/ppermute | solution.py:562
  18.4 0.0 collective-permute-done.9.next_in
  18.4 0.0 collective-permute-done.8.own_in
  18.5 0.7 %collective-permute-start.11 = (f32[32,512]{1,0:T(8,128)S(1)}, f32[32,512]{1,0:T(8,128)S(1)}, u32[]{:S(2)}, u32[]{:S(2)}) collective-permute-start(f32[32,512]{1,0:T(8,128)S(1)} %get-tuple-element.79._lower), channel_id=1, source_target_pairs={{16,13},{17,12}} | collective-permute-start | bytes 196616 | tf_op jit(solution)/shard_map/ppermute | solution.py:419
  19.1 0.7 %collective-permute-start.10 = (f32[32,512]{1,0:T(8,128)S(1)}, f32[32,512]{1,0:T(8,128)S(1)}, u32[]{:S(2)}, u32[]{:S(2)}) collective-permute-start(f32[32,512]{1,0:T(8,128)S(1)} %get-tuple-element.79._lower), channel_id=1, source_target_pairs={{16,12},{17,13}} | collective-permute-start | bytes 196616 | tf_op jit(solution)/shard_map/ppermute | solution.py:562
  19.9 0.7 %collective-permute-start.13 = (f32[32,512]{1,0:T(8,128)S(1)}, f32[32,512]{1,0:T(8,128)S(1)}, u32[]{:S(2)}, u32[]{:S(2)}) collective-permute-start(f32[32,512]{1,0:T(8,128)S(1)} %get-tuple-element.83.rest_6_.lower), channel_id=1, source_target_pairs={{12,9},{13,8}} | collective-permute-start | bytes 196616 | tf_op jit(solution)/shard_map/ppermute | solution.py:419
  20.6 0.7 %collective-permute-start.12 = (f32[32,512]{1,0:T(8,128)S(1)}, f32[32,512]{1,0:T(8,128)S(1)}, u32[]{:S(2)}, u32[]{:S(2)}) collective-permute-start(f32[32,512]{1,0:T(8,128)S(1)} %get-tuple-element.83.rest_6_.lower), channel_id=1, source_target_pairs={{12,8},{13,9}} | collective-permute-start | bytes 196616 | tf_op jit(solution)/shard_map/ppermute | solution.py:562
  21.2 0.0 collective-permute-done.13.next_in
  21.3 0.0 collective-permute-done.15.other_rows
  21.3 0.0 collective-permute-done.14.own_rows.rest_0_
  21.3 0.2 shard_map.64
  21.6 0.0 collective-permute-done.12.own_in
  21.6 1.3 %collective-permute-start.16 = (f32[32,896]{1,0:T(8,128)S(1)}, f32[32,896]{1,0:T(8,128)S(1)}, u32[]{:S(2)}, u32[]{:S(2)}) collective-permute-start(f32[32,896]{1,0:T(8,128)S(1)} %get-tuple-element.93), channel_id=1, source_target_pairs={{9,0}} | collective-permute-start | bytes 344072 | tf_op jit(solution)/shard_map/ppermute | solution.py:556
  22.9 1.3 %collective-permute-start.17 = (f32[32,896]{1,0:T(8,128)S(1)}, f32[32,896]{1,0:T(8,128)S(1)}, u32[]{:S(2)}, u32[]{:S(2)}) collective-permute-start(f32[32,896]{1,0:T(8,128)S(1)} %get-tuple-element.94), channel_id=1, source_target_pairs={{8,0},{9,1}} | collective-permute-start | bytes 344072 | tf_op jit(solution)/shard_map/ppermute | solution.py:557
  24.2 0.7 %collective-permute-start.18 = (f32[32,896]{1,0:T(8,128)S(1)}, f32[32,896]{1,0:T(8,128)S(1)}, u32[]{:S(2)}, u32[]{:S(2)}) collective-permute-start(f32[32,896]{1,0:T(8,128)S(1)} %get-tuple-element.95), channel_id=1, source_target_pairs={{8,1}} | collective-permute-start | bytes 344072 | tf_op jit(solution)/shard_map/ppermute | solution.py:558
  24.9 0.7 %collective-permute-start.19 = (f32[32,896]{1,0:T(8,128)S(1)}, f32[32,896]{1,0:T(8,128)S(1)}, u32[]{:S(2)}, u32[]{:S(2)}) collective-permute-start(f32[32,896]{1,0:T(8,128)S(1)} %get-tuple-element.96), channel_id=1, source_target_pairs={{12,5},{13,4}} | collective-permute-start | bytes 344072 | tf_op jit(solution)/shard_map/ppermute | solution.py:419
  25.6 0.7 %collective-permute-start.20 = (f32[32,896]{1,0:T(8,128)S(1)}, f32[32,896]{1,0:T(8,128)S(1)}, u32[]{:S(2)}, u32[]{:S(2)}) collective-permute-start(f32[32,896]{1,0:T(8,128)S(1)} %get-tuple-element.97), channel_id=1, source_target_pairs={{12,4},{13,5}} | collective-permute-start | bytes 344072 | tf_op jit(solution)/shard_map/ppermute | solution.py:574
  26.3 23.2 %collective-permute-done.16.rest_0_ = f32[32,896]{1,0:T(8,128)S(1)} collective-permute-done((f32[32,896]{1,0:T(8,128)S(1)}, f32[32,896]{1,0:T(8,128)S(1)}, u32[]{:S(2)}, u32[]{:S(2)}) %collective-permute-start.16) | collective-permute-done | bytes 114720 | tf_op jit(solution)/shard_map/ppermute | solution.py:556
  49.4 0.3 collective-permute-done.17.rest_1_
  49.8 0.0 collective-permute-done.18.rest_2_
  49.8 0.3 shard_map.67
  50.1 1.3 %collective-permute-start.21 = (f32[32,512]{1,0:T(8,128)S(1)}, f32[32,512]{1,0:T(8,128)S(1)}, u32[]{:S(2)}, u32[]{:S(2)}) collective-permute-start(f32[32,512]{1,0:T(8,128)S(1)} %get-tuple-element.102), channel_id=1, source_target_pairs={{0,2},{1,3},{4,6},{5,7},{8,10},{9,11},{12,14},{13,15},{16,18},{17,... | collective-permute-start | bytes 196616 | tf_op jit(solution)/shard_map/ppermute | solution.py:604
  51.4 0.5 shard_map.68
  51.9 0.4 collective-permute-done.21
  52.3 0.6 %select_bitcast_fusion = f32[1,32,512]{2,1,0:T(8,128)} fusion(f32[32,512]{1,0:T(8,128)S(1)} %shard_map.68, f32[32,512]{1,0:T(8,128)S(1)} %collective-permute-done.21, pred[]{:T(512)S(6)} %eq.5), kind=kLoop, calls=%fused_computation | loop fusion | flops 16384 | bytes 196609 | tf_op jit(solution)/shard_map/broadcast_in_dim | solution.py:614
  (27 shorter events, 0.4 us)
Async XLA Ops:
  1.5 1.5 %copy-start = (f32[1,2,512,256]{3,2,1,0:T(8,128)S(1)}, f32[1,2,512,256]{3,2,1,0:T(8,128)}, u32[]{:S(2)}) copy-start(f32[1,2,512,256]{3,2,1,0:T(8,128)} %lag.1) | copy-start | bytes 3145732
  1.5 1.5 %copy-start.1 = (s32[1,2,3]{2,1,0:T(2,128)S(1)}, s32[1,2,3]{2,1,0:T(2,128)}, u32[]{:S(2)}) copy-start(s32[1,2,3]{2,1,0:T(2,128)} %mask.1) | copy-start | bytes 76
  1.5 4.8 %collective-permute-start.2 = (f32[32,512]{1,0:T(8,128)S(1)}, f32[32,512]{1,0:T(8,128)S(1)}, u32[]{:S(2)}, u32[]{:S(2)}) collective-permute-start(f32[32,512]{1,0:T(8,128)S(1)} %shard_map.52), channel_id=1, source_target_pairs={{30,29},{31,28}} | collective-permute-start | bytes 196616 | tf_op jit(solution)/shard_map/ppermute | solution.py:419
  2.3 4.0 %collective-permute-start.3 = (f32[32,512]{1,0:T(8,128)S(1)}, f32[32,512]{1,0:T(8,128)S(1)}, u32[]{:S(2)}, u32[]{:S(2)}) collective-permute-start(f32[32,512]{1,0:T(8,128)S(1)} %get-tuple-element.54.const.refs_6_), channel_id=1, source_target_pairs={{30,28},{31,29}} | collective-permute-start | bytes 196616 | tf_op jit(solution)/shard_map/ppermute | solution.py:459
  3.8 8.7 %collective-permute-start.1 = (f32[1,544,128]{2,1,0:T(8,128)S(1)}, f32[1,544,128]{2,1,0:T(8,128)S(1)}, u32[]{:S(2)}, u32[]{:S(2)}) collective-permute-start(f32[1,544,128]{2,1,0:T(8,128)S(1)} %shard_map.48._edges), channel_id=1, source_target_pairs={{2,1},{3,0},{6,5},{7,4},{10,9},{11,8},{14,13},{15,12},{18,17},{19,... | collective-permute-start | bytes 835592 | tf_op jit(solution)/shard_map/ppermute | solution.py:419
  5.1 7.2 %collective-permute-start = (f32[1088,256]{1,0:T(8,128)S(1)}, f32[1088,256]{1,0:T(8,128)S(1)}, u32[]{:S(2)}, u32[]{:S(2)}) collective-permute-start(f32[1088,256]{1,0:T(8,128)S(1)} %shard_map.49), channel_id=1, source_target_pairs={{2,0},{3,1},{6,4},{7,5},{10,8},{11,9},{14,12},{15,13},{18,16},{19,... | collective-permute-start | bytes 3342344 | tf_op jit(solution)/shard_map/ppermute | solution.py:488
  6.4 6.0 %collective-permute-start.5 = (f32[32,512]{1,0:T(8,128)S(1)}, f32[32,512]{1,0:T(8,128)S(1)}, u32[]{:S(2)}, u32[]{:S(2)}) collective-permute-start(f32[32,512]{1,0:T(8,128)S(1)} %get-tuple-element.65._lower), channel_id=1, source_target_pairs={{28,25},{29,24}} | collective-permute-start | bytes 196616 | tf_op jit(solution)/shard_map/ppermute | solution.py:419
  7.1 5.4 %collective-permute-start.4 = (f32[32,512]{1,0:T(8,128)S(1)}, f32[32,512]{1,0:T(8,128)S(1)}, u32[]{:S(2)}, u32[]{:S(2)}) collective-permute-start(f32[32,512]{1,0:T(8,128)S(1)} %get-tuple-element.65._lower), channel_id=1, source_target_pairs={{28,24},{29,25}} | collective-permute-start | bytes 196616 | tf_op jit(solution)/shard_map/ppermute | solution.py:562
  12.5 4.4 %collective-permute-start.7 = (f32[32,512]{1,0:T(8,128)S(1)}, f32[32,512]{1,0:T(8,128)S(1)}, u32[]{:S(2)}, u32[]{:S(2)}) collective-permute-start(f32[32,512]{1,0:T(8,128)S(1)} %get-tuple-element.71._lower), channel_id=1, source_target_pairs={{24,21},{25,20}} | collective-permute-start | bytes 196616 | tf_op jit(solution)/shard_map/ppermute | solution.py:419
  13.2 3.8 %collective-permute-start.6 = (f32[32,512]{1,0:T(8,128)S(1)}, f32[32,512]{1,0:T(8,128)S(1)}, u32[]{:S(2)}, u32[]{:S(2)}) collective-permute-start(f32[32,512]{1,0:T(8,128)S(1)} %get-tuple-element.71._lower), channel_id=1, source_target_pairs={{24,20},{25,21}} | collective-permute-start | bytes 196616 | tf_op jit(solution)/shard_map/ppermute | solution.py:562
  15.5 5.7 %collective-permute-start.14 = (f32[1088,256]{1,0:T(8,128)S(1)}, f32[1088,256]{1,0:T(8,128)S(1)}, u32[]{:S(2)}, u32[]{:S(2)}) collective-permute-start(f32[1088,256]{1,0:T(8,128)S(1)} %get-tuple-element.86), channel_id=1, source_target_pairs={{4,8},{5,9},{8,12},{9,13}} | collective-permute-start | bytes 3342344 | tf_op jit(solution)/shard_map/ppermute | solution.py:527
  16.3 5.0 %collective-permute-start.15 = (f32[512,256]{1,0:T(8,128)S(1)}, f32[512,256]{1,0:T(8,128)S(1)}, u32[]{:S(2)}, u32[]{:S(2)}) collective-permute-start(f32[512,256]{1,0:T(8,128)S(1)} %get-tuple-element.87), channel_id=1, source_target_pairs={{4,9},{5,8},{8,13},{9,12}} | collective-permute-start | bytes 1572872 | tf_op jit(solution)/shard_map/ppermute | solution.py:419
  17.1 1.3 %collective-permute-start.9 = (f32[32,512]{1,0:T(8,128)S(1)}, f32[32,512]{1,0:T(8,128)S(1)}, u32[]{:S(2)}, u32[]{:S(2)}) collective-permute-start(f32[32,512]{1,0:T(8,128)S(1)} %get-tuple-element.75._lower), channel_id=1, source_target_pairs={{20,17},{21,16}} | collective-permute-start | bytes 196616 | tf_op jit(solution)/shard_map/ppermute | solution.py:419
  17.7 0.7 %collective-permute-start.8 = (f32[32,512]{1,0:T(8,128)S(1)}, f32[32,512]{1,0:T(8,128)S(1)}, u32[]{:S(2)}, u32[]{:S(2)}) collective-permute-start(f32[32,512]{1,0:T(8,128)S(1)} %get-tuple-element.75._lower), channel_id=1, source_target_pairs={{20,16},{21,17}} | collective-permute-start | bytes 196616 | tf_op jit(solution)/shard_map/ppermute | solution.py:562
  18.5 1.3 %collective-permute-start.11 = (f32[32,512]{1,0:T(8,128)S(1)}, f32[32,512]{1,0:T(8,128)S(1)}, u32[]{:S(2)}, u32[]{:S(2)}) collective-permute-start(f32[32,512]{1,0:T(8,128)S(1)} %get-tuple-element.79._lower), channel_id=1, source_target_pairs={{16,13},{17,12}} | collective-permute-start | bytes 196616 | tf_op jit(solution)/shard_map/ppermute | solution.py:419
  19.1 0.7 %collective-permute-start.10 = (f32[32,512]{1,0:T(8,128)S(1)}, f32[32,512]{1,0:T(8,128)S(1)}, u32[]{:S(2)}, u32[]{:S(2)}) collective-permute-start(f32[32,512]{1,0:T(8,128)S(1)} %get-tuple-element.79._lower), channel_id=1, source_target_pairs={{16,12},{17,13}} | collective-permute-start | bytes 196616 | tf_op jit(solution)/shard_map/ppermute | solution.py:562
  19.9 1.3 %collective-permute-start.13 = (f32[32,512]{1,0:T(8,128)S(1)}, f32[32,512]{1,0:T(8,128)S(1)}, u32[]{:S(2)}, u32[]{:S(2)}) collective-permute-start(f32[32,512]{1,0:T(8,128)S(1)} %get-tuple-element.83.rest_6_.lower), channel_id=1, source_target_pairs={{12,9},{13,8}} | collective-permute-start | bytes 196616 | tf_op jit(solution)/shard_map/ppermute | solution.py:419
  20.6 1.0 %collective-permute-start.12 = (f32[32,512]{1,0:T(8,128)S(1)}, f32[32,512]{1,0:T(8,128)S(1)}, u32[]{:S(2)}, u32[]{:S(2)}) collective-permute-start(f32[32,512]{1,0:T(8,128)S(1)} %get-tuple-element.83.rest_6_.lower), channel_id=1, source_target_pairs={{12,8},{13,9}} | collective-permute-start | bytes 196616 | tf_op jit(solution)/shard_map/ppermute | solution.py:562
  21.6 27.8 %collective-permute-start.16 = (f32[32,896]{1,0:T(8,128)S(1)}, f32[32,896]{1,0:T(8,128)S(1)}, u32[]{:S(2)}, u32[]{:S(2)}) collective-permute-start(f32[32,896]{1,0:T(8,128)S(1)} %get-tuple-element.93), channel_id=1, source_target_pairs={{9,0}} | collective-permute-start | bytes 344072 | tf_op jit(solution)/shard_map/ppermute | solution.py:556
  22.9 26.8 %collective-permute-start.17 = (f32[32,896]{1,0:T(8,128)S(1)}, f32[32,896]{1,0:T(8,128)S(1)}, u32[]{:S(2)}, u32[]{:S(2)}) collective-permute-start(f32[32,896]{1,0:T(8,128)S(1)} %get-tuple-element.94), channel_id=1, source_target_pairs={{8,0},{9,1}} | collective-permute-start | bytes 344072 | tf_op jit(solution)/shard_map/ppermute | solution.py:557
  24.2 25.5 %collective-permute-start.18 = (f32[32,896]{1,0:T(8,128)S(1)}, f32[32,896]{1,0:T(8,128)S(1)}, u32[]{:S(2)}, u32[]{:S(2)}) collective-permute-start(f32[32,896]{1,0:T(8,128)S(1)} %get-tuple-element.95), channel_id=1, source_target_pairs={{8,1}} | collective-permute-start | bytes 344072 | tf_op jit(solution)/shard_map/ppermute | solution.py:558
  24.9 24.9 %collective-permute-start.19 = (f32[32,896]{1,0:T(8,128)S(1)}, f32[32,896]{1,0:T(8,128)S(1)}, u32[]{:S(2)}, u32[]{:S(2)}) collective-permute-start(f32[32,896]{1,0:T(8,128)S(1)} %get-tuple-element.96), channel_id=1, source_target_pairs={{12,5},{13,4}} | collective-permute-start | bytes 344072 | tf_op jit(solution)/shard_map/ppermute | solution.py:419
  25.6 24.2 %collective-permute-start.20 = (f32[32,896]{1,0:T(8,128)S(1)}, f32[32,896]{1,0:T(8,128)S(1)}, u32[]{:S(2)}, u32[]{:S(2)}) collective-permute-start(f32[32,896]{1,0:T(8,128)S(1)} %get-tuple-element.97), channel_id=1, source_target_pairs={{12,4},{13,5}} | collective-permute-start | bytes 344072 | tf_op jit(solution)/shard_map/ppermute | solution.py:574
  50.1 2.2 %collective-permute-start.21 = (f32[32,512]{1,0:T(8,128)S(1)}, f32[32,512]{1,0:T(8,128)S(1)}, u32[]{:S(2)}, u32[]{:S(2)}) collective-permute-start(f32[32,512]{1,0:T(8,128)S(1)} %get-tuple-element.102), channel_id=1, source_target_pairs={{0,2},{1,3},{4,6},{5,7},{8,10},{9,11},{12,14},{13,15},{16,18},{17,... | collective-permute-start | bytes 196616 | tf_op jit(solution)/shard_map/ppermute | solution.py:604

commit v14 on v13

--- a/solution.py
+++ b/solution.py
@@ -69,7 +69,13 @@
     again[...] = const[...]
 
 
-def fuse_kernel(mask, const, inv_high, inv_low, lag, own, near_high, near_low):
+def fuse_kernel(late, *refs):
+    here = lax.axis_index("tm") == late[0]
+    given = refs[:5] + refs[6:] if late[1] else refs
+    pl.when(here if late[1] else jnp.logical_not(here))(lambda: make_fused(*given))
+
+
+def make_fused(mask, const, inv_high, inv_low, lag, near_high, near_low, own=None):
     blocks, window, length = lag.shape[1:]
     edge = (window - length) // 2
     cols = const.shape[0]
@@ -77,13 +83,15 @@
     flags = mask[0].astype(jnp.float32)
     for b in range(blocks):
         at = blocks * window + b * cols
-        own[at : at + cols] = const[:, b * length : (b + 1) * length]
+        if own is not None:
+            own[at : at + cols] = const[:, b * length : (b + 1) * length]
         for part in range(3):
             lo, hi = cuts[part], cuts[part + 1]
             rows = slice(b * window + lo, b * window + hi)
             high, low = halves(lag[0, b, lo:hi] * flags[b : b + 1, part : part + 1])
             value = triple(high, low, inv_high[b], inv_low[b])
-            own[rows] = value
+            if own is not None:
+                own[rows] = value
             near_high[rows], near_low[rows] = halves(value)
 
 
@@ -329,17 +337,16 @@
 
 
 def jump_kernel(mine, own_in, base, high, low, *rest):
-    ship, (_late, _lower, late, lower, to_next, to_own, to_last, *scratch) = rest[:-9], rest[-9:]
+    ship, (_late, _lower, late, lower, to_next, to_own, *scratch) = rest[:-8], rest[-8:]
 
     @pl.when(lax.axis_index("tm") == 2 * mine)
     def _():
         add_own(own_in, base, high, low, late, lower)
         add_parts(lower, *ship, to_next, to_own, *scratch, high.shape[0] * high.shape[1] // own_in.shape[1])
-        to_last[...] = to_next[...]
 
     @pl.when(lax.axis_index("tm") != 2 * mine)
     def _():
-        for part in (to_next, to_own, to_last):
+        for part in (to_next, to_own):
             part[...] = jnp.zeros_like(part)
 
 
@@ -377,11 +384,10 @@
         def _():
             load(sides, plain(messages[1]), messages[0][...], halo, late)
 
-    for mine, (*next_in, own_in) in enumerate(((messages[0], messages[2], messages[1]), messages[3:]) if len(messages) > 2 else ()):
+    for mine, (from_next, own_in) in enumerate((messages[:2], messages[2:]) if len(messages) > 2 else ()):
 
         @pl.when(lax.axis_index("tm") == 2 * mine)
         def _():
-            from_next = next_in[0][...] + next_in[1][...] if len(next_in) == 2 else next_in[0][...]
             own = own_in[:, :sites] + from_next[:, halo:]
             near = own_in[:, sites:] + from_next[:, :halo]
             load(sides, lambda side, cut: near, own, halo, late)
@@ -457,18 +463,20 @@
     odd, even = range(1, times, 2), range(0, times, 2)
     first_next = cross(again, odd[-1:], even[-1:])
     first_own = lax.ppermute(const, BOTH, link(odd[-1:], even[-1:]))
-    near, near_high, near_low = pl.pallas_call(
-        fuse_kernel,
-        out_shape=(
-            shape((tall + blocks * cols, length), f32), shape((tall, length), bf16), shape((tall, length), bf16),
-        ),
-        in_specs=[VMEM] * 5,
-        out_specs=(VMEM,) * 3,
-        compiler_params=PARAMS,
-        cost_estimate=pl.CostEstimate(
-            flops=6 * (tall + cols * blocks) * length * length, bytes_accessed=16 * tall * length, transcendentals=0
-        ),
-    )(fill_mask, const, inv_high, inv_low, lag_coupling)
+
+    def fused(late, extra, after=()):
+        return pl.pallas_call(
+            functools.partial(fuse_kernel, (2 * pairs - 4, late)),
+            out_shape=(shape((tall, length), bf16), shape((tall, length), bf16), *extra),
+            in_specs=[VMEM] * (5 + len(after)),
+            out_specs=(VMEM,) * (2 + len(extra)),
+            compiler_params=PARAMS,
+            cost_estimate=pl.CostEstimate(
+                flops=6 * (tall + cols * blocks) * length * length, bytes_accessed=16 * tall * length, transcendentals=0
+            ),
+        )(fill_mask, const, inv_high, inv_low, lag_coupling, *after)
+
+    near_high, near_low, near = fused(False, (shape((tall + blocks * cols, length), f32),))
     edges = pl.pallas_call(
         functools.partial(edge_kernel, sides, blocks, cols),
         out_shape=shape((sides, window + cols, edge), f32),
@@ -507,7 +515,7 @@
     )(far)
     packs = (shape((blocks * (sites + cols), length), f32), shape((halo + edge, length), f32)) if jumps else ()
 
-    def pair_matrix(first, jumps, packs):
+    def pair_matrix(first, jumps, packs, mine):
         return pl.pallas_call(
             functools.partial(pair_kernel, (pairs - 2, first), jumps),
             out_shape=(
@@ -518,10 +526,10 @@
             scratch_shapes=[pltpu.VMEM((2 * window, length), f32)],
             compiler_params=PARAMS,
             cost_estimate=pl.CostEstimate(flops=10**9, bytes_accessed=0, transcendentals=0),
-        )(far, rim, far_high, far_low, near_high, near_low, const)
-
-    early = pair_matrix(True, False, ())
-    high, low, both, *packs = pair_matrix(False, jumps, packs)
+        )(far, rim, far_high, far_low, *mine, const)
+
+    early = pair_matrix(True, False, (), fused(True, (), (lower,)))
+    high, low, both, *packs = pair_matrix(False, jumps, packs, (near_high, near_low))
     if jumps:
         source, target = [2 * jump - 2, 2 * jump], [2 * jump, 2 * jump + 2]
         own_rows = lax.ppermute(packs[0], BOTH, link(source, target))
@@ -553,9 +561,8 @@
     while mine > 0:
         if jumps and mine == jump:
             source, target = [2 * mine], [2 * mine - 4]
-            first_in = lax.ppermute(to_next, BOTH, [(2 * source[0] + 1, 2 * target[0])])
+            next_in = cross(to_next, source, target)
             own_in = lax.ppermute(to_own, BOTH, link(source, target))
-            next_in = lax.ppermute(to_last, BOTH, [(2 * source[0], 2 * target[0] + 1)])
             break
         source, target = [2 * mine], [2 * mine - 2]
         next_in = cross(lower, source, target)
@@ -583,12 +590,12 @@
             extra=[shape((cols, sites), f32)],
         )
         if jumps and mine == jump:
-            late, lower, to_next, to_own, to_last = turn(
+            late, lower, to_next, to_own = turn(
                 functools.partial(jump_kernel, mine),
                 (own_in, base, high, low, own_rows, *ship),
                 (late, lower),
                 parts_scratch,
-                parts + parts[:1],
+                parts,
             )
         else:
             late, lower = turn(
@@ -597,7 +604,7 @@
                 (late, lower),
                 flops=50 * 10**9 if jumps and mine == pairs - 3 else 0,
             )
-    given = (first_in, own_in, next_in, beside_next, beside_own) if jumps else (own_in, next_in)
+    given = (next_in, own_in, beside_next, beside_own) if jumps else (own_in, next_in)
     late, upper = turn(
         functools.partial(upper_kernel, sides, pairs - 1), (*given, far, far_high, far_low), (late, upper)
     )

time: 53.6 us -> 53.5 us (level)
  waiting for transfers between devices: 28.4 us -> 29.2 us
  starting transfers between devices: 18 us -> 17.3 us
    ppermute x9 -> x10, waiting for transfers between devices: 0.02 us -> 23.5 us  [cross(): return lax.ppermute(value, BOTH, perm)]
    ppermute x2 -> x0, waiting for transfers between devices: 23.2 us -> none  [the longest x1 23.2 us: local(): first_in = lax.ppermute(to_next, BOTH, [(2 * source[0] + 1, 2 * target[0])])]
    ppermute x2 -> x0, starting transfers between devices: 1.96 us -> none  [the longest x1 1.29 us: local(): first_in = lax.ppermute(to_next, BOTH, [(2 * source[0] + 1, 2 * target[0])])]
    ppermute x9 -> x10, starting transfers between devices: 6.77 us -> 8.07 us  [cross(): return lax.ppermute(value, BOTH, perm)]
    ppermute x1, waiting for transfers between devices: 0.32 us -> 0.88 us  [local(): own_in = lax.ppermute(to_own, BOTH, link(source, target))]
  transfers between devices with their start and end apart: 22 -> 21, of which waited for: 4 -> 4; matrix products, arithmetic and copies ran while one was open for 0% -> 0% of each run, Pallas kernels for 6% -> 7%
where the time goes in v14:
time: 53.5 us; the launch traced here: 53.1 us
  waiting for transfers between devices  29.2 us (55%)
  starting transfers between devices  17.3 us (32%)
  Pallas kernels  5.34 us (10%)
  other arithmetic  0.64 us (1%)
    ppermute x10, waiting for transfers between devices, cross(): return lax.ppermute(value, BOTH, perm)  23.5 us
    ppermute x10, starting transfers between devices, cross(): return lax.ppermute(value, BOTH, perm)  8.07 us
    ppermute x1, waiting for transfers between devices, local(): far = lax.ppermute(near, BOTH, link(odd[:-1], even[:-1]))  4.46 us
    ppermute x5, starting transfers between devices, local(): own_in = lax.ppermute(lower, BOTH, link(source, target))  3.32 us
    pallas_call x2, Pallas kernels, pair_matrix(): pl.pallas_call(functools.partial(pair_kernel, (pairs - 2, first), jumps),...  1.69 us
    pallas_call x1, Pallas kernels, local(): pl.pallas_call(const_kernel, out_shape=(shape((cols, sites), f32), shape(...  1.48 us
    ppermute x1, starting transfers between devices, local(): far = lax.ppermute(near, BOTH, link(odd[:-1], even[:-1]))  1.29 us
    ppermute x1, starting transfers between devices, local(): own_in = lax.ppermute(to_own, BOTH, link(source, target))  1.29 us
  transfers between devices with their start and end apart: 21, of which 4 were waited for; matrix products, arithmetic and copies ran while one was open for 0% of the time, Pallas kernels for 7%

profile of v14, /device:TPU:0, one launch (start us, length us, event | category | flops | bytes accessed | tf_op | source)
XLA Modules:
  0.0 53.1 jit_solution(16490341983141462234)
XLA Ops:
  0.0 1.5 %shard_map.46 = (f32[32,512]{1,0:T(8,128)S(1)}, bf16[2,256,256]{2,1,0:T(8,128)(2,1)S(1)}, bf16[2,256,256]{2,1,0:T(8,128)(2,1)S(1)}) custom-call(f32[1,32,512]{2,1,0:T(8,128)} %normals.1, f32[1,2,256,256]{3,2,1,0:T(8,128)} %inv.1), custom_call_target="tpu_custom_call" | custom-call | tf_op jit(solution)/shard_map/pallas_call | solution.py:440
  1.5 0.0 copy-start
  1.5 0.0 copy-start.1
  1.5 0.8 %collective-permute-start.2 = (f32[32,512]{1,0:T(8,128)S(1)}, f32[32,512]{1,0:T(8,128)S(1)}, u32[]{:S(2)}, u32[]{:S(2)}) collective-permute-start(f32[32,512]{1,0:T(8,128)S(1)} %shard_map.52), channel_id=1, source_target_pairs={{30,29},{31,28}} | collective-permute-start | bytes 196616 | tf_op jit(solution)/shard_map/ppermute | solution.py:425
  2.3 0.7 %collective-permute-start.3 = (f32[32,512]{1,0:T(8,128)S(1)}, f32[32,512]{1,0:T(8,128)S(1)}, u32[]{:S(2)}, u32[]{:S(2)}) collective-permute-start(f32[32,512]{1,0:T(8,128)S(1)} %get-tuple-element.55.refs_1_.refs_6_.const), channel_id=1, source_target_pairs={{30,28},{31,29}} | collective-permute-start | bytes 196616 | tf_op jit(solution)/shard_map/ppermute | solution.py:465
  3.0 0.7 %shard_map.47 = (bf16[1024,256]{1,0:T(8,128)(2,1)S(1)}, bf16[1024,256]{1,0:T(8,128)(2,1)S(1)}, f32[1088,256]{1,0:T(8,128)S(1)}) custom-call(s32[1,2,3]{2,1,0:T(2,128)S(1)} %copy-done.1, f32[32,512]{1,0:T(8,128)S(1)} %get-tuple-element.55.refs_1_.refs_6_.const, bf16[2,256,256]{2,1,0:T(8,128)(2,1)S(1)} %get-tuple-element.56.refs_2_, ...), custom_call_target="tpu_custom_call" | custom-call | flops 427819008 | bytes 4194304 | tf_op jit(solution)/shard_map/pallas_call | solution.py:468
  3.8 1.3 %collective-permute-start.1 = (f32[1,544,128]{2,1,0:T(8,128)S(1)}, f32[1,544,128]{2,1,0:T(8,128)S(1)}, u32[]{:S(2)}, u32[]{:S(2)}) collective-permute-start(f32[1,544,128]{2,1,0:T(8,128)S(1)} %shard_map.48._edges), channel_id=1, source_target_pairs={{2,1},{3,0},{6,5},{7,4},{10,9},{11,8},{14,13},{15,12},{18,17},{19,... | collective-permute-start | bytes 835592 | tf_op jit(solution)/shard_map/ppermute | solution.py:425
  5.1 1.3 %collective-permute-start = (f32[1088,256]{1,0:T(8,128)S(1)}, f32[1088,256]{1,0:T(8,128)S(1)}, u32[]{:S(2)}, u32[]{:S(2)}) collective-permute-start(f32[1088,256]{1,0:T(8,128)S(1)} %shard_map.49), channel_id=1, source_target_pairs={{2,0},{3,1},{6,4},{7,5},{10,8},{11,9},{14,12},{15,13},{18,16},{19,... | collective-permute-start | bytes 3342344 | tf_op jit(solution)/shard_map/ppermute | solution.py:496
  6.4 0.0 collective-permute-done.2.next_in
  6.4 0.0 collective-permute-done.3.own_in
  6.5 0.7 %collective-permute-start.5 = (f32[32,512]{1,0:T(8,128)S(1)}, f32[32,512]{1,0:T(8,128)S(1)}, u32[]{:S(2)}, u32[]{:S(2)}) collective-permute-start(f32[32,512]{1,0:T(8,128)S(1)} %get-tuple-element.66.refs_5_._lower), channel_id=1, source_target_pairs={{28,25},{29,24}} | collective-permute-start | bytes 196616 | tf_op jit(solution)/shard_map/ppermute | solution.py:425
  7.1 0.7 %collective-permute-start.4 = (f32[32,512]{1,0:T(8,128)S(1)}, f32[32,512]{1,0:T(8,128)S(1)}, u32[]{:S(2)}, u32[]{:S(2)}) collective-permute-start(f32[32,512]{1,0:T(8,128)S(1)} %get-tuple-element.66.refs_5_._lower), channel_id=1, source_target_pairs={{28,24},{29,25}} | collective-permute-start | bytes 196616 | tf_op jit(solution)/shard_map/ppermute | solution.py:569
  7.8 4.5 %collective-permute-done.far.refs_0_.rest_4_ = f32[1088,256]{1,0:T(8,128)S(1)} collective-permute-done((f32[1088,256]{1,0:T(8,128)S(1)}, f32[1088,256]{1,0:T(8,128)S(1)}, u32[]{:S(2)}, u32[]{:S(2)}) %collective-permute-start) | collective-permute-done | bytes 1114144 | tf_op jit(solution)/shard_map/ppermute | solution.py:496
  12.3 0.1 shard_map.50
  12.4 0.0 collective-permute-done.1.refs_1_
  12.5 0.0 collective-permute-done.5.next_in
  12.5 0.0 collective-permute-done.4.own_in
  12.6 0.7 %collective-permute-start.7 = (f32[32,512]{1,0:T(8,128)S(1)}, f32[32,512]{1,0:T(8,128)S(1)}, u32[]{:S(2)}, u32[]{:S(2)}) collective-permute-start(f32[32,512]{1,0:T(8,128)S(1)} %get-tuple-element.74._lower), channel_id=1, source_target_pairs={{24,21},{25,20}} | collective-permute-start | bytes 196616 | tf_op jit(solution)/shard_map/ppermute | solution.py:425
  13.2 0.7 %collective-permute-start.6 = (f32[32,512]{1,0:T(8,128)S(1)}, f32[32,512]{1,0:T(8,128)S(1)}, u32[]{:S(2)}, u32[]{:S(2)}) collective-permute-start(f32[32,512]{1,0:T(8,128)S(1)} %get-tuple-element.74._lower), channel_id=1, source_target_pairs={{24,20},{25,21}} | collective-permute-start | bytes 196616 | tf_op jit(solution)/shard_map/ppermute | solution.py:569
  13.9 1.7 %shard_map.51 = (bf16[2048,256]{1,0:T(8,128)(2,1)S(1)}, bf16[2048,256]{1,0:T(8,128)(2,1)S(1)}, f32[32,512]{1,0:T(8,128)S(1)}, f32[1088,256]{1,0:T(8,128)S(1)}, f32[512,256]{1,0:T(8,128)S(1)}) custom-call(f32[1088,256]{1,0:T(8,128)S(1)} %collective-permute-done.far.refs_0_.rest_4_, f32[1,544,128]{2,1,0:T(8,128)S(1)} %collective-permute-done.1.refs_1_, ...), custom_call_target="tpu_custom_call" | custom-call | flops 1000000000 | tf_op jit(solution)/shard_map/pallas_call | solution.py:519
  15.6 0.7 %collective-permute-start.14 = (f32[1088,256]{1,0:T(8,128)S(1)}, f32[1088,256]{1,0:T(8,128)S(1)}, u32[]{:S(2)}, u32[]{:S(2)}) collective-permute-start(f32[1088,256]{1,0:T(8,128)S(1)} %get-tuple-element.89), channel_id=1, source_target_pairs={{4,8},{5,9},{8,12},{9,13}} | collective-permute-start | bytes 3342344 | tf_op jit(solution)/shard_map/ppermute | solution.py:535
  16.3 0.7 %collective-permute-start.15 = (f32[512,256]{1,0:T(8,128)S(1)}, f32[512,256]{1,0:T(8,128)S(1)}, u32[]{:S(2)}, u32[]{:S(2)}) collective-permute-start(f32[512,256]{1,0:T(8,128)S(1)} %get-tuple-element.90), channel_id=1, source_target_pairs={{4,9},{5,8},{8,13},{9,12}} | collective-permute-start | bytes 1572872 | tf_op jit(solution)/shard_map/ppermute | solution.py:425
  17.0 0.0 collective-permute-done.7.next_in
  17.1 0.0 collective-permute-done.6.own_in
  17.1 0.7 %collective-permute-start.9 = (f32[32,512]{1,0:T(8,128)S(1)}, f32[32,512]{1,0:T(8,128)S(1)}, u32[]{:S(2)}, u32[]{:S(2)}) collective-permute-start(f32[32,512]{1,0:T(8,128)S(1)} %get-tuple-element.78._lower), channel_id=1, source_target_pairs={{20,17},{21,16}} | collective-permute-start | bytes 196616 | tf_op jit(solution)/shard_map/ppermute | solution.py:425
  17.8 0.7 %collective-permute-start.8 = (f32[32,512]{1,0:T(8,128)S(1)}, f32[32,512]{1,0:T(8,128)S(1)}, u32[]{:S(2)}, u32[]{:S(2)}) collective-permute-start(f32[32,512]{1,0:T(8,128)S(1)} %get-tuple-element.78._lower), channel_id=1, source_target_pairs={{20,16},{21,17}} | collective-permute-start | bytes 196616 | tf_op jit(solution)/shard_map/ppermute | solution.py:569
  18.4 0.0 collective-permute-done.9.next_in
  18.5 0.0 collective-permute-done.8.own_in
  18.5 0.7 %collective-permute-start.11 = (f32[32,512]{1,0:T(8,128)S(1)}, f32[32,512]{1,0:T(8,128)S(1)}, u32[]{:S(2)}, u32[]{:S(2)}) collective-permute-start(f32[32,512]{1,0:T(8,128)S(1)} %get-tuple-element.82._lower), channel_id=1, source_target_pairs={{16,13},{17,12}} | collective-permute-start | bytes 196616 | tf_op jit(solution)/shard_map/ppermute | solution.py:425
  19.2 0.7 %collective-permute-start.10 = (f32[32,512]{1,0:T(8,128)S(1)}, f32[32,512]{1,0:T(8,128)S(1)}, u32[]{:S(2)}, u32[]{:S(2)}) collective-permute-start(f32[32,512]{1,0:T(8,128)S(1)} %get-tuple-element.82._lower), channel_id=1, source_target_pairs={{16,12},{17,13}} | collective-permute-start | bytes 196616 | tf_op jit(solution)/shard_map/ppermute | solution.py:569
  19.9 0.0 collective-permute-done.11.next_in
  19.9 0.0 collective-permute-done.10.own_in
  19.9 0.7 %collective-permute-start.13 = (f32[32,512]{1,0:T(8,128)S(1)}, f32[32,512]{1,0:T(8,128)S(1)}, u32[]{:S(2)}, u32[]{:S(2)}) collective-permute-start(f32[32,512]{1,0:T(8,128)S(1)} %get-tuple-element.86.rest_6_.lower), channel_id=1, source_target_pairs={{12,9},{13,8}} | collective-permute-start | bytes 196616 | tf_op jit(solution)/shard_map/ppermute | solution.py:425
  20.6 0.7 %collective-permute-start.12 = (f32[32,512]{1,0:T(8,128)S(1)}, f32[32,512]{1,0:T(8,128)S(1)}, u32[]{:S(2)}, u32[]{:S(2)}) collective-permute-start(f32[32,512]{1,0:T(8,128)S(1)} %get-tuple-element.86.rest_6_.lower), channel_id=1, source_target_pairs={{12,8},{13,9}} | collective-permute-start | bytes 196616 | tf_op jit(solution)/shard_map/ppermute | solution.py:569
  21.3 0.2 shard_map.65
  21.7 1.3 %collective-permute-start.16 = (f32[32,896]{1,0:T(8,128)S(1)}, f32[32,896]{1,0:T(8,128)S(1)}, u32[]{:S(2)}, u32[]{:S(2)}) collective-permute-start(f32[32,896]{1,0:T(8,128)S(1)} %get-tuple-element.96), channel_id=1, source_target_pairs={{8,1},{9,0}} | collective-permute-start | bytes 344072 | tf_op jit(solution)/shard_map/ppermute | solution.py:425
  23.0 1.3 %collective-permute-start.17 = (f32[32,896]{1,0:T(8,128)S(1)}, f32[32,896]{1,0:T(8,128)S(1)}, u32[]{:S(2)}, u32[]{:S(2)}) collective-permute-start(f32[32,896]{1,0:T(8,128)S(1)} %get-tuple-element.97), channel_id=1, source_target_pairs={{8,0},{9,1}} | collective-permute-start | bytes 344072 | tf_op jit(solution)/shard_map/ppermute | solution.py:565
  24.3 0.7 %collective-permute-start.18 = (f32[32,896]{1,0:T(8,128)S(1)}, f32[32,896]{1,0:T(8,128)S(1)}, u32[]{:S(2)}, u32[]{:S(2)}) collective-permute-start(f32[32,896]{1,0:T(8,128)S(1)} %get-tuple-element.98), channel_id=1, source_target_pairs={{12,5},{13,4}} | collective-permute-start | bytes 344072 | tf_op jit(solution)/shard_map/ppermute | solution.py:425
  25.0 0.7 %collective-permute-start.19 = (f32[32,896]{1,0:T(8,128)S(1)}, f32[32,896]{1,0:T(8,128)S(1)}, u32[]{:S(2)}, u32[]{:S(2)}) collective-permute-start(f32[32,896]{1,0:T(8,128)S(1)} %get-tuple-element.99), channel_id=1, source_target_pairs={{12,4},{13,5}} | collective-permute-start | bytes 344072 | tf_op jit(solution)/shard_map/ppermute | solution.py:581
  25.6 23.5 %collective-permute-done.16.rest_0_ = f32[32,896]{1,0:T(8,128)S(1)} collective-permute-done((f32[32,896]{1,0:T(8,128)S(1)}, f32[32,896]{1,0:T(8,128)S(1)}, u32[]{:S(2)}, u32[]{:S(2)}) %collective-permute-start.16) | collective-permute-done | bytes 114720 | tf_op jit(solution)/shard_map/ppermute | solution.py:425
  49.1 0.9 %collective-permute-done.17.rest_1_ = f32[32,896]{1,0:T(8,128)S(1)} collective-permute-done((f32[32,896]{1,0:T(8,128)S(1)}, f32[32,896]{1,0:T(8,128)S(1)}, u32[]{:S(2)}, u32[]{:S(2)}) %collective-permute-start.17) | collective-permute-done | bytes 114720 | tf_op jit(solution)/shard_map/ppermute | solution.py:565
  50.0 0.0 collective-permute-done.18.rest_2_
  50.0 0.0 collective-permute-done.19.rest_3_
  50.0 0.3 shard_map.68
  50.3 1.3 %collective-permute-start.20 = (f32[32,512]{1,0:T(8,128)S(1)}, f32[32,512]{1,0:T(8,128)S(1)}, u32[]{:S(2)}, u32[]{:S(2)}) collective-permute-start(f32[32,512]{1,0:T(8,128)S(1)} %get-tuple-element.104), channel_id=1, source_target_pairs={{0,2},{1,3},{4,6},{5,7},{8,10},{9,11},{12,14},{13,15},{16,18},{17,... | collective-permute-start | bytes 196616 | tf_op jit(solution)/shard_map/ppermute | solution.py:611
  51.6 0.5 shard_map.69
  52.1 0.4 collective-permute-done.20
  52.5 0.6 %select_bitcast_fusion = f32[1,32,512]{2,1,0:T(8,128)} fusion(f32[32,512]{1,0:T(8,128)S(1)} %shard_map.69, f32[32,512]{1,0:T(8,128)S(1)} %collective-permute-done.20, pred[]{:T(512)S(6)} %eq.5), kind=kLoop, calls=%fused_computation | loop fusion | flops 16384 | bytes 196609 | tf_op jit(solution)/shard_map/broadcast_in_dim | solution.py:621
  (26 shorter events, 0.4 us)
Async XLA Ops:
  1.5 1.5 %copy-start = (f32[1,2,512,256]{3,2,1,0:T(8,128)S(1)}, f32[1,2,512,256]{3,2,1,0:T(8,128)}, u32[]{:S(2)}) copy-start(f32[1,2,512,256]{3,2,1,0:T(8,128)} %refs_4_.3) | copy-start | bytes 3145732
  1.5 1.5 %copy-start.1 = (s32[1,2,3]{2,1,0:T(2,128)S(1)}, s32[1,2,3]{2,1,0:T(2,128)}, u32[]{:S(2)}) copy-start(s32[1,2,3]{2,1,0:T(2,128)} %refs_0_.3) | copy-start | bytes 76
  1.5 4.9 %collective-permute-start.2 = (f32[32,512]{1,0:T(8,128)S(1)}, f32[32,512]{1,0:T(8,128)S(1)}, u32[]{:S(2)}, u32[]{:S(2)}) collective-permute-start(f32[32,512]{1,0:T(8,128)S(1)} %shard_map.52), channel_id=1, source_target_pairs={{30,29},{31,28}} | collective-permute-start | bytes 196616 | tf_op jit(solution)/shard_map/ppermute | solution.py:425
  2.3 4.1 %collective-permute-start.3 = (f32[32,512]{1,0:T(8,128)S(1)}, f32[32,512]{1,0:T(8,128)S(1)}, u32[]{:S(2)}, u32[]{:S(2)}) collective-permute-start(f32[32,512]{1,0:T(8,128)S(1)} %get-tuple-element.55.refs_1_.refs_6_.const), channel_id=1, source_target_pairs={{30,28},{31,29}} | collective-permute-start | bytes 196616 | tf_op jit(solution)/shard_map/ppermute | solution.py:465
  3.8 8.7 %collective-permute-start.1 = (f32[1,544,128]{2,1,0:T(8,128)S(1)}, f32[1,544,128]{2,1,0:T(8,128)S(1)}, u32[]{:S(2)}, u32[]{:S(2)}) collective-permute-start(f32[1,544,128]{2,1,0:T(8,128)S(1)} %shard_map.48._edges), channel_id=1, source_target_pairs={{2,1},{3,0},{6,5},{7,4},{10,9},{11,8},{14,13},{15,12},{18,17},{19,... | collective-permute-start | bytes 835592 | tf_op jit(solution)/shard_map/ppermute | solution.py:425
  5.1 7.2 %collective-permute-start = (f32[1088,256]{1,0:T(8,128)S(1)}, f32[1088,256]{1,0:T(8,128)S(1)}, u32[]{:S(2)}, u32[]{:S(2)}) collective-permute-start(f32[1088,256]{1,0:T(8,128)S(1)} %shard_map.49), channel_id=1, source_target_pairs={{2,0},{3,1},{6,4},{7,5},{10,8},{11,9},{14,12},{15,13},{18,16},{19,... | collective-permute-start | bytes 3342344 | tf_op jit(solution)/shard_map/ppermute | solution.py:496
  6.5 6.0 %collective-permute-start.5 = (f32[32,512]{1,0:T(8,128)S(1)}, f32[32,512]{1,0:T(8,128)S(1)}, u32[]{:S(2)}, u32[]{:S(2)}) collective-permute-start(f32[32,512]{1,0:T(8,128)S(1)} %get-tuple-element.66.refs_5_._lower), channel_id=1, source_target_pairs={{28,25},{29,24}} | collective-permute-start | bytes 196616 | tf_op jit(solution)/shard_map/ppermute | solution.py:425
  7.1 5.4 %collective-permute-start.4 = (f32[32,512]{1,0:T(8,128)S(1)}, f32[32,512]{1,0:T(8,128)S(1)}, u32[]{:S(2)}, u32[]{:S(2)}) collective-permute-start(f32[32,512]{1,0:T(8,128)S(1)} %get-tuple-element.66.refs_5_._lower), channel_id=1, source_target_pairs={{28,24},{29,25}} | collective-permute-start | bytes 196616 | tf_op jit(solution)/shard_map/ppermute | solution.py:569
  12.6 4.5 %collective-permute-start.7 = (f32[32,512]{1,0:T(8,128)S(1)}, f32[32,512]{1,0:T(8,128)S(1)}, u32[]{:S(2)}, u32[]{:S(2)}) collective-permute-start(f32[32,512]{1,0:T(8,128)S(1)} %get-tuple-element.74._lower), channel_id=1, source_target_pairs={{24,21},{25,20}} | collective-permute-start | bytes 196616 | tf_op jit(solution)/shard_map/ppermute | solution.py:425
  13.2 3.8 %collective-permute-start.6 = (f32[32,512]{1,0:T(8,128)S(1)}, f32[32,512]{1,0:T(8,128)S(1)}, u32[]{:S(2)}, u32[]{:S(2)}) collective-permute-start(f32[32,512]{1,0:T(8,128)S(1)} %get-tuple-element.74._lower), channel_id=1, source_target_pairs={{24,20},{25,21}} | collective-permute-start | bytes 196616 | tf_op jit(solution)/shard_map/ppermute | solution.py:569
  15.6 5.7 %collective-permute-start.14 = (f32[1088,256]{1,0:T(8,128)S(1)}, f32[1088,256]{1,0:T(8,128)S(1)}, u32[]{:S(2)}, u32[]{:S(2)}) collective-permute-start(f32[1088,256]{1,0:T(8,128)S(1)} %get-tuple-element.89), channel_id=1, source_target_pairs={{4,8},{5,9},{8,12},{9,13}} | collective-permute-start | bytes 3342344 | tf_op jit(solution)/shard_map/ppermute | solution.py:535
  16.3 5.0 %collective-permute-start.15 = (f32[512,256]{1,0:T(8,128)S(1)}, f32[512,256]{1,0:T(8,128)S(1)}, u32[]{:S(2)}, u32[]{:S(2)}) collective-permute-start(f32[512,256]{1,0:T(8,128)S(1)} %get-tuple-element.90), channel_id=1, source_target_pairs={{4,9},{5,8},{8,13},{9,12}} | collective-permute-start | bytes 1572872 | tf_op jit(solution)/shard_map/ppermute | solution.py:425
  17.1 1.3 %collective-permute-start.9 = (f32[32,512]{1,0:T(8,128)S(1)}, f32[32,512]{1,0:T(8,128)S(1)}, u32[]{:S(2)}, u32[]{:S(2)}) collective-permute-start(f32[32,512]{1,0:T(8,128)S(1)} %get-tuple-element.78._lower), channel_id=1, source_target_pairs={{20,17},{21,16}} | collective-permute-start | bytes 196616 | tf_op jit(solution)/shard_map/ppermute | solution.py:425
  17.8 0.7 %collective-permute-start.8 = (f32[32,512]{1,0:T(8,128)S(1)}, f32[32,512]{1,0:T(8,128)S(1)}, u32[]{:S(2)}, u32[]{:S(2)}) collective-permute-start(f32[32,512]{1,0:T(8,128)S(1)} %get-tuple-element.78._lower), channel_id=1, source_target_pairs={{20,16},{21,17}} | collective-permute-start | bytes 196616 | tf_op jit(solution)/shard_map/ppermute | solution.py:569
  18.5 1.3 %collective-permute-start.11 = (f32[32,512]{1,0:T(8,128)S(1)}, f32[32,512]{1,0:T(8,128)S(1)}, u32[]{:S(2)}, u32[]{:S(2)}) collective-permute-start(f32[32,512]{1,0:T(8,128)S(1)} %get-tuple-element.82._lower), channel_id=1, source_target_pairs={{16,13},{17,12}} | collective-permute-start | bytes 196616 | tf_op jit(solution)/shard_map/ppermute | solution.py:425
  19.2 0.7 %collective-permute-start.10 = (f32[32,512]{1,0:T(8,128)S(1)}, f32[32,512]{1,0:T(8,128)S(1)}, u32[]{:S(2)}, u32[]{:S(2)}) collective-permute-start(f32[32,512]{1,0:T(8,128)S(1)} %get-tuple-element.82._lower), channel_id=1, source_target_pairs={{16,12},{17,13}} | collective-permute-start | bytes 196616 | tf_op jit(solution)/shard_map/ppermute | solution.py:569
  19.9 1.3 %collective-permute-start.13 = (f32[32,512]{1,0:T(8,128)S(1)}, f32[32,512]{1,0:T(8,128)S(1)}, u32[]{:S(2)}, u32[]{:S(2)}) collective-permute-start(f32[32,512]{1,0:T(8,128)S(1)} %get-tuple-element.86.rest_6_.lower), channel_id=1, source_target_pairs={{12,9},{13,8}} | collective-permute-start | bytes 196616 | tf_op jit(solution)/shard_map/ppermute | solution.py:425
  20.6 1.0 %collective-permute-start.12 = (f32[32,512]{1,0:T(8,128)S(1)}, f32[32,512]{1,0:T(8,128)S(1)}, u32[]{:S(2)}, u32[]{:S(2)}) collective-permute-start(f32[32,512]{1,0:T(8,128)S(1)} %get-tuple-element.86.rest_6_.lower), channel_id=1, source_target_pairs={{12,8},{13,9}} | collective-permute-start | bytes 196616 | tf_op jit(solution)/shard_map/ppermute | solution.py:569
  21.7 27.4 %collective-permute-start.16 = (f32[32,896]{1,0:T(8,128)S(1)}, f32[32,896]{1,0:T(8,128)S(1)}, u32[]{:S(2)}, u32[]{:S(2)}) collective-permute-start(f32[32,896]{1,0:T(8,128)S(1)} %get-tuple-element.96), channel_id=1, source_target_pairs={{8,1},{9,0}} | collective-permute-start | bytes 344072 | tf_op jit(solution)/shard_map/ppermute | solution.py:425
  23.0 27.0 %collective-permute-start.17 = (f32[32,896]{1,0:T(8,128)S(1)}, f32[32,896]{1,0:T(8,128)S(1)}, u32[]{:S(2)}, u32[]{:S(2)}) collective-permute-start(f32[32,896]{1,0:T(8,128)S(1)} %get-tuple-element.97), channel_id=1, source_target_pairs={{8,0},{9,1}} | collective-permute-start | bytes 344072 | tf_op jit(solution)/shard_map/ppermute | solution.py:565
  24.3 25.7 %collective-permute-start.18 = (f32[32,896]{1,0:T(8,128)S(1)}, f32[32,896]{1,0:T(8,128)S(1)}, u32[]{:S(2)}, u32[]{:S(2)}) collective-permute-start(f32[32,896]{1,0:T(8,128)S(1)} %get-tuple-element.98), channel_id=1, source_target_pairs={{12,5},{13,4}} | collective-permute-start | bytes 344072 | tf_op jit(solution)/shard_map/ppermute | solution.py:425
  25.0 25.0 %collective-permute-start.19 = (f32[32,896]{1,0:T(8,128)S(1)}, f32[32,896]{1,0:T(8,128)S(1)}, u32[]{:S(2)}, u32[]{:S(2)}) collective-permute-start(f32[32,896]{1,0:T(8,128)S(1)} %get-tuple-element.99), channel_id=1, source_target_pairs={{12,4},{13,5}} | collective-permute-start | bytes 344072 | tf_op jit(solution)/shard_map/ppermute | solution.py:581
  50.3 2.2 %collective-permute-start.20 = (f32[32,512]{1,0:T(8,128)S(1)}, f32[32,512]{1,0:T(8,128)S(1)}, u32[]{:S(2)}, u32[]{:S(2)}) collective-permute-start(f32[32,512]{1,0:T(8,128)S(1)} %get-tuple-element.104), channel_id=1, source_target_pairs={{0,2},{1,3},{4,6},{5,7},{8,10},{9,11},{12,14},{13,15},{16,18},{17,... | collective-permute-start | bytes 196616 | tf_op jit(solution)/shard_map/ppermute | solution.py:611

commit v15 on v14

--- a/solution.py
+++ b/solution.py
@@ -337,16 +337,17 @@
 
 
 def jump_kernel(mine, own_in, base, high, low, *rest):
-    ship, (_late, _lower, late, lower, to_next, to_own, *scratch) = rest[:-8], rest[-8:]
+    ship, (_late, _lower, late, lower, to_next, to_own, to_last, *scratch) = rest[:-9], rest[-9:]
 
     @pl.when(lax.axis_index("tm") == 2 * mine)
     def _():
         add_own(own_in, base, high, low, late, lower)
         add_parts(lower, *ship, to_next, to_own, *scratch, high.shape[0] * high.shape[1] // own_in.shape[1])
+        to_last[...] = to_next[...]
 
     @pl.when(lax.axis_index("tm") != 2 * mine)
     def _():
-        for part in (to_next, to_own):
+        for part in (to_next, to_own, to_last):
             part[...] = jnp.zeros_like(part)
 
 
@@ -384,10 +385,12 @@
         def _():
             load(sides, plain(messages[1]), messages[0][...], halo, late)
 
-    for mine, (from_next, own_in) in enumerate((messages[:2], messages[2:]) if len(messages) > 2 else ()):
+    sums = ((messages[0], messages[2], messages[1]), messages[3:]) if len(messages) > 2 else ()
+    for mine, (*next_in, own_in) in enumerate(sums):
 
         @pl.when(lax.axis_index("tm") == 2 * mine)
         def _():
+            from_next = next_in[0][...] + next_in[1][...] if len(next_in) == 2 else next_in[0][...]
             own = own_in[:, :sites] + from_next[:, halo:]
             near = own_in[:, sites:] + from_next[:, :halo]
             load(sides, lambda side, cut: near, own, halo, late)
@@ -561,8 +564,9 @@
     while mine > 0:
         if jumps and mine == jump:
             source, target = [2 * mine], [2 * mine - 4]
-            next_in = cross(to_next, source, target)
+            first_in = lax.ppermute(to_next, BOTH, [(2 * source[0] + 1, 2 * target[0])])
             own_in = lax.ppermute(to_own, BOTH, link(source, target))
+            next_in = lax.ppermute(to_last, BOTH, [(2 * source[0], 2 * target[0] + 1)])
             break
         source, target = [2 * mine], [2 * mine - 2]
         next_in = cross(lower, source, target)
@@ -590,12 +594,12 @@
             extra=[shape((cols, sites), f32)],
         )
         if jumps and mine == jump:
-            late, lower, to_next, to_own = turn(
+            late, lower, to_next, to_own, to_last = turn(
                 functools.partial(jump_kernel, mine),
                 (own_in, base, high, low, own_rows, *ship),
                 (late, lower),
                 parts_scratch,
-                parts,
+                parts + parts[:1],
             )
         else:
             late, lower = turn(
@@ -604,7 +608,7 @@
                 (late, lower),
                 flops=50 * 10**9 if jumps and mine == pairs - 3 else 0,
             )
-    given = (next_in, own_in, beside_next, beside_own) if jumps else (own_in, next_in)
+    given = (first_in, own_in, next_in, beside_next, beside_own) if jumps else (own_in, next_in)
     late, upper = turn(
         functools.partial(upper_kernel, sides, pairs - 1), (*given, far, far_high, far_low), (late, upper)
     )

time: 53.5 us -> 53.2 us (level)
  waiting for transfers between devices: 29.2 us -> 27.9 us
  starting transfers between devices: 17.3 us -> 18 us
    ppermute x10 -> x9, waiting for transfers between devices: 23.5 us -> 0.02 us  [cross(): return lax.ppermute(value, BOTH, perm)]
    ppermute x0 -> x2, waiting for transfers between devices: none -> 22.8 us  [the longest x1 22.8 us: local(): first_in = lax.ppermute(to_next, BOTH, [(2 * source[0] + 1, 2 * target[0])])]
    ppermute x0 -> x2, starting transfers between devices: none -> 1.96 us  [the longest x1 1.29 us: local(): first_in = lax.ppermute(to_next, BOTH, [(2 * source[0] + 1, 2 * target[0])])]
    ppermute x10 -> x9, starting transfers between devices: 8.07 us -> 6.77 us  [cross(): return lax.ppermute(value, BOTH, perm)]
    ppermute x1, waiting for transfers between devices: 0.88 us -> 0.26 us  [local(): own_in = lax.ppermute(to_own, BOTH, link(source, target))]
  transfers between devices with their start and end apart: 21 -> 22, of which waited for: 4 -> 4; matrix products, arithmetic and copies ran while one was open for 0% -> 0% of each run, Pallas kernels for 7% -> 7%
where the time goes in v15:
time: 53.2 us; the launch traced here: 52.5 us
  waiting for transfers between devices  27.9 us (52%)
  starting transfers between devices  18 us (34%)
  Pallas kernels  5.36 us (10%)
  other arithmetic  0.64 us (1%)
    ppermute x1, waiting for transfers between devices, local(): first_in = lax.ppermute(to_next, BOTH, [(2 * source[0] + 1, 2 * target[0])])  22.8 us
    ppermute x9, starting transfers between devices, cross(): return lax.ppermute(value, BOTH, perm)  6.77 us
    ppermute x1, waiting for transfers between devices, local(): far = lax.ppermute(near, BOTH, link(odd[:-1], even[:-1]))  4.46 us
    ppermute x5, starting transfers between devices, local(): own_in = lax.ppermute(lower, BOTH, link(source, target))  3.32 us
    pallas_call x2, Pallas kernels, pair_matrix(): pl.pallas_call(functools.partial(pair_kernel, (pairs - 2, first), jumps),...  1.69 us
    pallas_call x1, Pallas kernels, local(): pl.pallas_call(const_kernel, out_shape=(shape((cols, sites), f32), shape(...  1.48 us
    ppermute x1, starting transfers between devices, local(): far = lax.ppermute(near, BOTH, link(odd[:-1], even[:-1]))  1.29 us
    ppermute x1, starting transfers between devices, local(): first_in = lax.ppermute(to_next, BOTH, [(2 * source[0] + 1, 2 * target[0])])  1.29 us
  transfers between devices with their start and end apart: 22, of which 4 were waited for; matrix products, arithmetic and copies ran while one was open for 0% of the time, Pallas kernels for 7%

profile of v15, /device:TPU:0, one launch (start us, length us, event | category | flops | bytes accessed | tf_op | source)
XLA Modules:
  0.0 52.5 jit_solution(5539392042684323535)
XLA Ops:
  0.0 1.5 %shard_map.46 = (f32[32,512]{1,0:T(8,128)S(1)}, bf16[2,256,256]{2,1,0:T(8,128)(2,1)S(1)}, bf16[2,256,256]{2,1,0:T(8,128)(2,1)S(1)}) custom-call(f32[1,32,512]{2,1,0:T(8,128)} %normals.1, f32[1,2,256,256]{3,2,1,0:T(8,128)} %inv.1), custom_call_target="tpu_custom_call" | custom-call | tf_op jit(solution)/shard_map/pallas_call | solution.py:443
  1.5 0.0 copy-start
  1.5 0.0 copy-start.1
  1.5 0.8 %collective-permute-start.2 = (f32[32,512]{1,0:T(8,128)S(1)}, f32[32,512]{1,0:T(8,128)S(1)}, u32[]{:S(2)}, u32[]{:S(2)}) collective-permute-start(f32[32,512]{1,0:T(8,128)S(1)} %shard_map.52), channel_id=1, source_target_pairs={{30,29},{31,28}} | collective-permute-start | bytes 196616 | tf_op jit(solution)/shard_map/ppermute | solution.py:428
  2.3 0.7 %collective-permute-start.3 = (f32[32,512]{1,0:T(8,128)S(1)}, f32[32,512]{1,0:T(8,128)S(1)}, u32[]{:S(2)}, u32[]{:S(2)}) collective-permute-start(f32[32,512]{1,0:T(8,128)S(1)} %get-tuple-element.56.refs_1_.refs_6_.const), channel_id=1, source_target_pairs={{30,28},{31,29}} | collective-permute-start | bytes 196616 | tf_op jit(solution)/shard_map/ppermute | solution.py:468
  3.0 0.7 %shard_map.47 = (bf16[1024,256]{1,0:T(8,128)(2,1)S(1)}, bf16[1024,256]{1,0:T(8,128)(2,1)S(1)}, f32[1088,256]{1,0:T(8,128)S(1)}) custom-call(s32[1,2,3]{2,1,0:T(2,128)S(1)} %copy-done.1, f32[32,512]{1,0:T(8,128)S(1)} %get-tuple-element.56.refs_1_.refs_6_.const, bf16[2,256,256]{2,1,0:T(8,128)(2,1)S(1)} %get-tuple-element.57.refs_2_, ...), custom_call_target="tpu_custom_call" | custom-call | flops 427819008 | bytes 4194304 | tf_op jit(solution)/shard_map/pallas_call | solution.py:471
  3.8 1.3 %collective-permute-start.1 = (f32[1,544,128]{2,1,0:T(8,128)S(1)}, f32[1,544,128]{2,1,0:T(8,128)S(1)}, u32[]{:S(2)}, u32[]{:S(2)}) collective-permute-start(f32[1,544,128]{2,1,0:T(8,128)S(1)} %shard_map.48._edges), channel_id=1, source_target_pairs={{2,1},{3,0},{6,5},{7,4},{10,9},{11,8},{14,13},{15,12},{18,17},{19,... | collective-permute-start | bytes 835592 | tf_op jit(solution)/shard_map/ppermute | solution.py:428
  5.1 1.3 %collective-permute-start = (f32[1088,256]{1,0:T(8,128)S(1)}, f32[1088,256]{1,0:T(8,128)S(1)}, u32[]{:S(2)}, u32[]{:S(2)}) collective-permute-start(f32[1088,256]{1,0:T(8,128)S(1)} %shard_map.49), channel_id=1, source_target_pairs={{2,0},{3,1},{6,4},{7,5},{10,8},{11,9},{14,12},{15,13},{18,16},{19,... | collective-permute-start | bytes 3342344 | tf_op jit(solution)/shard_map/ppermute | solution.py:499
  6.4 0.0 collective-permute-done.2.next_in
  6.4 0.0 collective-permute-done.3.own_in
  6.5 0.7 %collective-permute-start.5 = (f32[32,512]{1,0:T(8,128)S(1)}, f32[32,512]{1,0:T(8,128)S(1)}, u32[]{:S(2)}, u32[]{:S(2)}) collective-permute-start(f32[32,512]{1,0:T(8,128)S(1)} %get-tuple-element.67.refs_5_._lower), channel_id=1, source_target_pairs={{28,25},{29,24}} | collective-permute-start | bytes 196616 | tf_op jit(solution)/shard_map/ppermute | solution.py:428
  7.1 0.7 %collective-permute-start.4 = (f32[32,512]{1,0:T(8,128)S(1)}, f32[32,512]{1,0:T(8,128)S(1)}, u32[]{:S(2)}, u32[]{:S(2)}) collective-permute-start(f32[32,512]{1,0:T(8,128)S(1)} %get-tuple-element.67.refs_5_._lower), channel_id=1, source_target_pairs={{28,24},{29,25}} | collective-permute-start | bytes 196616 | tf_op jit(solution)/shard_map/ppermute | solution.py:573
  7.8 4.5 %collective-permute-done.far.refs_0_.rest_5_ = f32[1088,256]{1,0:T(8,128)S(1)} collective-permute-done((f32[1088,256]{1,0:T(8,128)S(1)}, f32[1088,256]{1,0:T(8,128)S(1)}, u32[]{:S(2)}, u32[]{:S(2)}) %collective-permute-start) | collective-permute-done | bytes 1114144 | tf_op jit(solution)/shard_map/ppermute | solution.py:499
  12.3 0.1 shard_map.50
  12.4 0.0 collective-permute-done.1.refs_1_
  12.5 0.0 collective-permute-done.5.next_in
  12.6 0.7 %collective-permute-start.7 = (f32[32,512]{1,0:T(8,128)S(1)}, f32[32,512]{1,0:T(8,128)S(1)}, u32[]{:S(2)}, u32[]{:S(2)}) collective-permute-start(f32[32,512]{1,0:T(8,128)S(1)} %get-tuple-element.75._lower), channel_id=1, source_target_pairs={{24,21},{25,20}} | collective-permute-start | bytes 196616 | tf_op jit(solution)/shard_map/ppermute | solution.py:428
  13.2 0.7 %collective-permute-start.6 = (f32[32,512]{1,0:T(8,128)S(1)}, f32[32,512]{1,0:T(8,128)S(1)}, u32[]{:S(2)}, u32[]{:S(2)}) collective-permute-start(f32[32,512]{1,0:T(8,128)S(1)} %get-tuple-element.75._lower), channel_id=1, source_target_pairs={{24,20},{25,21}} | collective-permute-start | bytes 196616 | tf_op jit(solution)/shard_map/ppermute | solution.py:573
  13.9 1.7 %shard_map.51 = (bf16[2048,256]{1,0:T(8,128)(2,1)S(1)}, bf16[2048,256]{1,0:T(8,128)(2,1)S(1)}, f32[32,512]{1,0:T(8,128)S(1)}, f32[1088,256]{1,0:T(8,128)S(1)}, f32[512,256]{1,0:T(8,128)S(1)}) custom-call(f32[1088,256]{1,0:T(8,128)S(1)} %collective-permute-done.far.refs_0_.rest_5_, f32[1,544,128]{2,1,0:T(8,128)S(1)} %collective-permute-done.1.refs_1_, ...), custom_call_target="tpu_custom_call" | custom-call | flops 1000000000 | tf_op jit(solution)/shard_map/pallas_call | solution.py:522
  15.6 0.7 %collective-permute-start.14 = (f32[1088,256]{1,0:T(8,128)S(1)}, f32[1088,256]{1,0:T(8,128)S(1)}, u32[]{:S(2)}, u32[]{:S(2)}) collective-permute-start(f32[1088,256]{1,0:T(8,128)S(1)} %get-tuple-element.90), channel_id=1, source_target_pairs={{4,8},{5,9},{8,12},{9,13}} | collective-permute-start | bytes 3342344 | tf_op jit(solution)/shard_map/ppermute | solution.py:538
  16.3 0.7 %collective-permute-start.15 = (f32[512,256]{1,0:T(8,128)S(1)}, f32[512,256]{1,0:T(8,128)S(1)}, u32[]{:S(2)}, u32[]{:S(2)}) collective-permute-start(f32[512,256]{1,0:T(8,128)S(1)} %get-tuple-element.91), channel_id=1, source_target_pairs={{4,9},{5,8},{8,13},{9,12}} | collective-permute-start | bytes 1572872 | tf_op jit(solution)/shard_map/ppermute | solution.py:428
  17.0 0.0 collective-permute-done.7.next_in
  17.1 0.0 collective-permute-done.6.own_in
  17.1 0.7 %collective-permute-start.9 = (f32[32,512]{1,0:T(8,128)S(1)}, f32[32,512]{1,0:T(8,128)S(1)}, u32[]{:S(2)}, u32[]{:S(2)}) collective-permute-start(f32[32,512]{1,0:T(8,128)S(1)} %get-tuple-element.79._lower), channel_id=1, source_target_pairs={{20,17},{21,16}} | collective-permute-start | bytes 196616 | tf_op jit(solution)/shard_map/ppermute | solution.py:428
  17.8 0.7 %collective-permute-start.8 = (f32[32,512]{1,0:T(8,128)S(1)}, f32[32,512]{1,0:T(8,128)S(1)}, u32[]{:S(2)}, u32[]{:S(2)}) collective-permute-start(f32[32,512]{1,0:T(8,128)S(1)} %get-tuple-element.79._lower), channel_id=1, source_target_pairs={{20,16},{21,17}} | collective-permute-start | bytes 196616 | tf_op jit(solution)/shard_map/ppermute | solution.py:573
  18.5 0.0 collective-permute-done.8.own_in
  18.5 0.7 %collective-permute-start.11 = (f32[32,512]{1,0:T(8,128)S(1)}, f32[32,512]{1,0:T(8,128)S(1)}, u32[]{:S(2)}, u32[]{:S(2)}) collective-permute-start(f32[32,512]{1,0:T(8,128)S(1)} %get-tuple-element.83._lower), channel_id=1, source_target_pairs={{16,13},{17,12}} | collective-permute-start | bytes 196616 | tf_op jit(solution)/shard_map/ppermute | solution.py:428
  19.2 0.7 %collective-permute-start.10 = (f32[32,512]{1,0:T(8,128)S(1)}, f32[32,512]{1,0:T(8,128)S(1)}, u32[]{:S(2)}, u32[]{:S(2)}) collective-permute-start(f32[32,512]{1,0:T(8,128)S(1)} %get-tuple-element.83._lower), channel_id=1, source_target_pairs={{16,12},{17,13}} | collective-permute-start | bytes 196616 | tf_op jit(solution)/shard_map/ppermute | solution.py:573
  19.9 0.0 collective-permute-done.11.next_in
  19.9 0.7 %collective-permute-start.13 = (f32[32,512]{1,0:T(8,128)S(1)}, f32[32,512]{1,0:T(8,128)S(1)}, u32[]{:S(2)}, u32[]{:S(2)}) collective-permute-start(f32[32,512]{1,0:T(8,128)S(1)} %get-tuple-element.87.rest_6_.lower), channel_id=1, source_target_pairs={{12,9},{13,8}} | collective-permute-start | bytes 196616 | tf_op jit(solution)/shard_map/ppermute | solution.py:428
  20.6 0.7 %collective-permute-start.12 = (f32[32,512]{1,0:T(8,128)S(1)}, f32[32,512]{1,0:T(8,128)S(1)}, u32[]{:S(2)}, u32[]{:S(2)}) collective-permute-start(f32[32,512]{1,0:T(8,128)S(1)} %get-tuple-element.87.rest_6_.lower), channel_id=1, source_target_pairs={{12,8},{13,9}} | collective-permute-start | bytes 196616 | tf_op jit(solution)/shard_map/ppermute | solution.py:573
  21.3 0.0 collective-permute-done.13.next_in
  21.3 0.0 collective-permute-done.15.other_rows
  21.3 0.2 shard_map.65
  21.6 0.0 collective-permute-done.12.own_in
  21.7 1.3 %collective-permute-start.16 = (f32[32,896]{1,0:T(8,128)S(1)}, f32[32,896]{1,0:T(8,128)S(1)}, u32[]{:S(2)}, u32[]{:S(2)}) collective-permute-start(f32[32,896]{1,0:T(8,128)S(1)} %get-tuple-element.97), channel_id=1, source_target_pairs={{9,0}} | collective-permute-start | bytes 344072 | tf_op jit(solution)/shard_map/ppermute | solution.py:567
  23.0 1.3 %collective-permute-start.17 = (f32[32,896]{1,0:T(8,128)S(1)}, f32[32,896]{1,0:T(8,128)S(1)}, u32[]{:S(2)}, u32[]{:S(2)}) collective-permute-start(f32[32,896]{1,0:T(8,128)S(1)} %get-tuple-element.98), channel_id=1, source_target_pairs={{8,0},{9,1}} | collective-permute-start | bytes 344072 | tf_op jit(solution)/shard_map/ppermute | solution.py:568
  24.3 0.7 %collective-permute-start.18 = (f32[32,896]{1,0:T(8,128)S(1)}, f32[32,896]{1,0:T(8,128)S(1)}, u32[]{:S(2)}, u32[]{:S(2)}) collective-permute-start(f32[32,896]{1,0:T(8,128)S(1)} %get-tuple-element.99), channel_id=1, source_target_pairs={{8,1}} | collective-permute-start | bytes 344072 | tf_op jit(solution)/shard_map/ppermute | solution.py:569
  25.0 0.7 %collective-permute-start.19 = (f32[32,896]{1,0:T(8,128)S(1)}, f32[32,896]{1,0:T(8,128)S(1)}, u32[]{:S(2)}, u32[]{:S(2)}) collective-permute-start(f32[32,896]{1,0:T(8,128)S(1)} %get-tuple-element.100), channel_id=1, source_target_pairs={{12,5},{13,4}} | collective-permute-start | bytes 344072 | tf_op jit(solution)/shard_map/ppermute | solution.py:428
  25.6 0.7 %collective-permute-start.20 = (f32[32,896]{1,0:T(8,128)S(1)}, f32[32,896]{1,0:T(8,128)S(1)}, u32[]{:S(2)}, u32[]{:S(2)}) collective-permute-start(f32[32,896]{1,0:T(8,128)S(1)} %get-tuple-element.101), channel_id=1, source_target_pairs={{12,4},{13,5}} | collective-permute-start | bytes 344072 | tf_op jit(solution)/shard_map/ppermute | solution.py:585
  26.3 22.8 %collective-permute-done.16.rest_0_ = f32[32,896]{1,0:T(8,128)S(1)} collective-permute-done((f32[32,896]{1,0:T(8,128)S(1)}, f32[32,896]{1,0:T(8,128)S(1)}, u32[]{:S(2)}, u32[]{:S(2)}) %collective-permute-start.16) | collective-permute-done | bytes 114720 | tf_op jit(solution)/shard_map/ppermute | solution.py:567
  49.1 0.3 collective-permute-done.17.rest_1_
  49.4 0.0 collective-permute-done.18.rest_2_
  49.4 0.3 shard_map.68
  49.7 1.3 %collective-permute-start.21 = (f32[32,512]{1,0:T(8,128)S(1)}, f32[32,512]{1,0:T(8,128)S(1)}, u32[]{:S(2)}, u32[]{:S(2)}) collective-permute-start(f32[32,512]{1,0:T(8,128)S(1)} %get-tuple-element.106), channel_id=1, source_target_pairs={{0,2},{1,3},{4,6},{5,7},{8,10},{9,11},{12,14},{13,15},{16,18},{17,... | collective-permute-start | bytes 196616 | tf_op jit(solution)/shard_map/ppermute | solution.py:615
  51.0 0.5 shard_map.69
  51.5 0.4 collective-permute-done.21
  51.9 0.6 %select_bitcast_fusion = f32[1,32,512]{2,1,0:T(8,128)} fusion(f32[32,512]{1,0:T(8,128)S(1)} %shard_map.69, f32[32,512]{1,0:T(8,128)S(1)} %collective-permute-done.21, pred[]{:T(512)S(6)} %eq.5), kind=kLoop, calls=%fused_computation | loop fusion | flops 16384 | bytes 196609 | tf_op jit(solution)/shard_map/broadcast_in_dim | solution.py:625
  (28 shorter events, 0.4 us)
Async XLA Ops:
  1.5 1.5 %copy-start = (f32[1,2,512,256]{3,2,1,0:T(8,128)S(1)}, f32[1,2,512,256]{3,2,1,0:T(8,128)}, u32[]{:S(2)}) copy-start(f32[1,2,512,256]{3,2,1,0:T(8,128)} %refs_4_.3) | copy-start | bytes 3145732
  1.5 1.5 %copy-start.1 = (s32[1,2,3]{2,1,0:T(2,128)S(1)}, s32[1,2,3]{2,1,0:T(2,128)}, u32[]{:S(2)}) copy-start(s32[1,2,3]{2,1,0:T(2,128)} %refs_0_.3) | copy-start | bytes 76
  1.5 4.9 %collective-permute-start.2 = (f32[32,512]{1,0:T(8,128)S(1)}, f32[32,512]{1,0:T(8,128)S(1)}, u32[]{:S(2)}, u32[]{:S(2)}) collective-permute-start(f32[32,512]{1,0:T(8,128)S(1)} %shard_map.52), channel_id=1, source_target_pairs={{30,29},{31,28}} | collective-permute-start | bytes 196616 | tf_op jit(solution)/shard_map/ppermute | solution.py:428
  2.3 4.1 %collective-permute-start.3 = (f32[32,512]{1,0:T(8,128)S(1)}, f32[32,512]{1,0:T(8,128)S(1)}, u32[]{:S(2)}, u32[]{:S(2)}) collective-permute-start(f32[32,512]{1,0:T(8,128)S(1)} %get-tuple-element.56.refs_1_.refs_6_.const), channel_id=1, source_target_pairs={{30,28},{31,29}} | collective-permute-start | bytes 196616 | tf_op jit(solution)/shard_map/ppermute | solution.py:468
  3.8 8.7 %collective-permute-start.1 = (f32[1,544,128]{2,1,0:T(8,128)S(1)}, f32[1,544,128]{2,1,0:T(8,128)S(1)}, u32[]{:S(2)}, u32[]{:S(2)}) collective-permute-start(f32[1,544,128]{2,1,0:T(8,128)S(1)} %shard_map.48._edges), channel_id=1, source_target_pairs={{2,1},{3,0},{6,5},{7,4},{10,9},{11,8},{14,13},{15,12},{18,17},{19,... | collective-permute-start | bytes 835592 | tf_op jit(solution)/shard_map/ppermute | solution.py:428
  5.1 7.2 %collective-permute-start = (f32[1088,256]{1,0:T(8,128)S(1)}, f32[1088,256]{1,0:T(8,128)S(1)}, u32[]{:S(2)}, u32[]{:S(2)}) collective-permute-start(f32[1088,256]{1,0:T(8,128)S(1)} %shard_map.49), channel_id=1, source_target_pairs={{2,0},{3,1},{6,4},{7,5},{10,8},{11,9},{14,12},{15,13},{18,16},{19,... | collective-permute-start | bytes 3342344 | tf_op jit(solution)/shard_map/ppermute | solution.py:499
  6.5 6.0 %collective-permute-start.5 = (f32[32,512]{1,0:T(8,128)S(1)}, f32[32,512]{1,0:T(8,128)S(1)}, u32[]{:S(2)}, u32[]{:S(2)}) collective-permute-start(f32[32,512]{1,0:T(8,128)S(1)} %get-tuple-element.67.refs_5_._lower), channel_id=1, source_target_pairs={{28,25},{29,24}} | collective-permute-start | bytes 196616 | tf_op jit(solution)/shard_map/ppermute | solution.py:428
  7.1 5.4 %collective-permute-start.4 = (f32[32,512]{1,0:T(8,128)S(1)}, f32[32,512]{1,0:T(8,128)S(1)}, u32[]{:S(2)}, u32[]{:S(2)}) collective-permute-start(f32[32,512]{1,0:T(8,128)S(1)} %get-tuple-element.67.refs_5_._lower), channel_id=1, source_target_pairs={{28,24},{29,25}} | collective-permute-start | bytes 196616 | tf_op jit(solution)/shard_map/ppermute | solution.py:573
  12.6 4.5 %collective-permute-start.7 = (f32[32,512]{1,0:T(8,128)S(1)}, f32[32,512]{1,0:T(8,128)S(1)}, u32[]{:S(2)}, u32[]{:S(2)}) collective-permute-start(f32[32,512]{1,0:T(8,128)S(1)} %get-tuple-element.75._lower), channel_id=1, source_target_pairs={{24,21},{25,20}} | collective-permute-start | bytes 196616 | tf_op jit(solution)/shard_map/ppermute | solution.py:428
  13.2 3.8 %collective-permute-start.6 = (f32[32,512]{1,0:T(8,128)S(1)}, f32[32,512]{1,0:T(8,128)S(1)}, u32[]{:S(2)}, u32[]{:S(2)}) collective-permute-start(f32[32,512]{1,0:T(8,128)S(1)} %get-tuple-element.75._lower), channel_id=1, source_target_pairs={{24,20},{25,21}} | collective-permute-start | bytes 196616 | tf_op jit(solution)/shard_map/ppermute | solution.py:573
  15.6 5.7 %collective-permute-start.14 = (f32[1088,256]{1,0:T(8,128)S(1)}, f32[1088,256]{1,0:T(8,128)S(1)}, u32[]{:S(2)}, u32[]{:S(2)}) collective-permute-start(f32[1088,256]{1,0:T(8,128)S(1)} %get-tuple-element.90), channel_id=1, source_target_pairs={{4,8},{5,9},{8,12},{9,13}} | collective-permute-start | bytes 3342344 | tf_op jit(solution)/shard_map/ppermute | solution.py:538
  16.3 5.0 %collective-permute-start.15 = (f32[512,256]{1,0:T(8,128)S(1)}, f32[512,256]{1,0:T(8,128)S(1)}, u32[]{:S(2)}, u32[]{:S(2)}) collective-permute-start(f32[512,256]{1,0:T(8,128)S(1)} %get-tuple-element.91), channel_id=1, source_target_pairs={{4,9},{5,8},{8,13},{9,12}} | collective-permute-start | bytes 1572872 | tf_op jit(solution)/shard_map/ppermute | solution.py:428
  17.1 1.3 %collective-permute-start.9 = (f32[32,512]{1,0:T(8,128)S(1)}, f32[32,512]{1,0:T(8,128)S(1)}, u32[]{:S(2)}, u32[]{:S(2)}) collective-permute-start(f32[32,512]{1,0:T(8,128)S(1)} %get-tuple-element.79._lower), channel_id=1, source_target_pairs={{20,17},{21,16}} | collective-permute-start | bytes 196616 | tf_op jit(solution)/shard_map/ppermute | solution.py:428
  17.8 0.7 %collective-permute-start.8 = (f32[32,512]{1,0:T(8,128)S(1)}, f32[32,512]{1,0:T(8,128)S(1)}, u32[]{:S(2)}, u32[]{:S(2)}) collective-permute-start(f32[32,512]{1,0:T(8,128)S(1)} %get-tuple-element.79._lower), channel_id=1, source_target_pairs={{20,16},{21,17}} | collective-permute-start | bytes 196616 | tf_op jit(solution)/shard_map/ppermute | solution.py:573
  18.5 1.3 %collective-permute-start.11 = (f32[32,512]{1,0:T(8,128)S(1)}, f32[32,512]{1,0:T(8,128)S(1)}, u32[]{:S(2)}, u32[]{:S(2)}) collective-permute-start(f32[32,512]{1,0:T(8,128)S(1)} %get-tuple-element.83._lower), channel_id=1, source_target_pairs={{16,13},{17,12}} | collective-permute-start | bytes 196616 | tf_op jit(solution)/shard_map/ppermute | solution.py:428
  19.2 0.7 %collective-permute-start.10 = (f32[32,512]{1,0:T(8,128)S(1)}, f32[32,512]{1,0:T(8,128)S(1)}, u32[]{:S(2)}, u32[]{:S(2)}) collective-permute-start(f32[32,512]{1,0:T(8,128)S(1)} %get-tuple-element.83._lower), channel_id=1, source_target_pairs={{16,12},{17,13}} | collective-permute-start | bytes 196616 | tf_op jit(solution)/shard_map/ppermute | solution.py:573
  19.9 1.3 %collective-permute-start.13 = (f32[32,512]{1,0:T(8,128)S(1)}, f32[32,512]{1,0:T(8,128)S(1)}, u32[]{:S(2)}, u32[]{:S(2)}) collective-permute-start(f32[32,512]{1,0:T(8,128)S(1)} %get-tuple-element.87.rest_6_.lower), channel_id=1, source_target_pairs={{12,9},{13,8}} | collective-permute-start | bytes 196616 | tf_op jit(solution)/shard_map/ppermute | solution.py:428
  20.6 1.0 %collective-permute-start.12 = (f32[32,512]{1,0:T(8,128)S(1)}, f32[32,512]{1,0:T(8,128)S(1)}, u32[]{:S(2)}, u32[]{:S(2)}) collective-permute-start(f32[32,512]{1,0:T(8,128)S(1)} %get-tuple-element.87.rest_6_.lower), channel_id=1, source_target_pairs={{12,8},{13,9}} | collective-permute-start | bytes 196616 | tf_op jit(solution)/shard_map/ppermute | solution.py:573
  21.7 27.4 %collective-permute-start.16 = (f32[32,896]{1,0:T(8,128)S(1)}, f32[32,896]{1,0:T(8,128)S(1)}, u32[]{:S(2)}, u32[]{:S(2)}) collective-permute-start(f32[32,896]{1,0:T(8,128)S(1)} %get-tuple-element.97), channel_id=1, source_target_pairs={{9,0}} | collective-permute-start | bytes 344072 | tf_op jit(solution)/shard_map/ppermute | solution.py:567
  23.0 26.4 %collective-permute-start.17 = (f32[32,896]{1,0:T(8,128)S(1)}, f32[32,896]{1,0:T(8,128)S(1)}, u32[]{:S(2)}, u32[]{:S(2)}) collective-permute-start(f32[32,896]{1,0:T(8,128)S(1)} %get-tuple-element.98), channel_id=1, source_target_pairs={{8,0},{9,1}} | collective-permute-start | bytes 344072 | tf_op jit(solution)/shard_map/ppermute | solution.py:568
  24.3 25.1 %collective-permute-start.18 = (f32[32,896]{1,0:T(8,128)S(1)}, f32[32,896]{1,0:T(8,128)S(1)}, u32[]{:S(2)}, u32[]{:S(2)}) collective-permute-start(f32[32,896]{1,0:T(8,128)S(1)} %get-tuple-element.99), channel_id=1, source_target_pairs={{8,1}} | collective-permute-start | bytes 344072 | tf_op jit(solution)/shard_map/ppermute | solution.py:569
  25.0 24.4 %collective-permute-start.19 = (f32[32,896]{1,0:T(8,128)S(1)}, f32[32,896]{1,0:T(8,128)S(1)}, u32[]{:S(2)}, u32[]{:S(2)}) collective-permute-start(f32[32,896]{1,0:T(8,128)S(1)} %get-tuple-element.100), channel_id=1, source_target_pairs={{12,5},{13,4}} | collective-permute-start | bytes 344072 | tf_op jit(solution)/shard_map/ppermute | solution.py:428
  25.6 23.7 %collective-permute-start.20 = (f32[32,896]{1,0:T(8,128)S(1)}, f32[32,896]{1,0:T(8,128)S(1)}, u32[]{:S(2)}, u32[]{:S(2)}) collective-permute-start(f32[32,896]{1,0:T(8,128)S(1)} %get-tuple-element.101), channel_id=1, source_target_pairs={{12,4},{13,5}} | collective-permute-start | bytes 344072 | tf_op jit(solution)/shard_map/ppermute | solution.py:585
  49.7 2.2 %collective-permute-start.21 = (f32[32,512]{1,0:T(8,128)S(1)}, f32[32,512]{1,0:T(8,128)S(1)}, u32[]{:S(2)}, u32[]{:S(2)}) collective-permute-start(f32[32,512]{1,0:T(8,128)S(1)} %get-tuple-element.106), channel_id=1, source_target_pairs={{0,2},{1,3},{4,6},{5,7},{8,10},{9,11},{12,14},{13,15},{16,18},{17,... | collective-permute-start | bytes 196616 | tf_op jit(solution)/shard_map/ppermute | solution.py:615

commit v16 on v15

--- a/solution.py
+++ b/solution.py
@@ -65,8 +65,13 @@
         const[:, at] = triple(high, low, inv_high[b], inv_low[b])
 
 
-def again_kernel(const, again):
-    again[...] = const[...]
+def copy_kernel(const, _after, copy):
+    copy[...] = const[...]
+
+
+def rim_of_kernel(sides, const, rim):
+    edge, sites = rim.shape[2], const.shape[1]
+    put_rim(sides, rim, lambda last: const[:, sites - edge :] if last else const[:, :edge])
 
 
 def fuse_kernel(late, *refs):
@@ -232,7 +237,7 @@
     @pl.when(lax.axis_index("tm") == 2 * mine)
     def _():
         mid[...] = jnp.zeros_like(mid)
-        load(sides, plain(next_in), own_in[...], edge, mid)
+        load(sides, lambda side, cut: next_in[side], own_in[...], edge, mid)
         upper[...] = own_in[...]
         for b in range(blocks):
             at, rows = slice(b * length, (b + 1) * length), slice(b * window, (b + 1) * window)
@@ -455,17 +460,24 @@
         ],
         compiler_params=PARAMS,
     )(*[pltpu.with_memory_space_constraint(a, pltpu.HBM) for a in (normals, inv_diag)])
-    again = pl.pallas_call(
-        again_kernel,
-        out_shape=shape((cols, sites), f32),
+    const_rim = pl.pallas_call(
+        functools.partial(rim_of_kernel, sides),
+        out_shape=shape((sides, cols, edge), f32),
         in_specs=[VMEM],
         out_specs=VMEM,
         compiler_params=PARAMS,
         cost_estimate=pl.CostEstimate(flops=5 * 10**9, bytes_accessed=0, transcendentals=0),
     )(const)
+    again = pl.pallas_call(
+        copy_kernel,
+        out_shape=shape((cols, sites), f32),
+        in_specs=[VMEM] * 2,
+        out_specs=VMEM,
+        compiler_params=PARAMS,
+    )(const, const_rim)
     odd, even = range(1, times, 2), range(0, times, 2)
-    first_next = cross(again, odd[-1:], even[-1:])
-    first_own = lax.ppermute(const, BOTH, link(odd[-1:], even[-1:]))
+    first_next = cross(const_rim, odd[-1:], even[-1:], True)
+    first_own = lax.ppermute(again, BOTH, link(odd[-1:], even[-1:]))
 
     def fused(late, extra, after=()):
         return pl.pallas_call(
@@ -475,7 +487,7 @@
             out_specs=(VMEM,) * (2 + len(extra)),
             compiler_params=PARAMS,
             cost_estimate=pl.CostEstimate(
-                flops=6 * (tall + cols * blocks) * length * length, bytes_accessed=16 * tall * length, transcendentals=0
+                flops=(6 if late else 150) * (tall + cols * blocks) * length * length, bytes_accessed=0, transcendentals=0
             ),
         )(fill_mask, const, inv_high, inv_low, lag_coupling, *after)
 

time: 53.2 us -> 53.3 us (level)
  no operation moved by 1% of the time
where the time goes in v16:
time: 53.3 us; the launch traced here: 52.5 us
  waiting for transfers between devices  27.9 us (52%)
  starting transfers between devices  18 us (34%)
  Pallas kernels  5.37 us (10%)
  other arithmetic  0.64 us (1%)
  between operations  0.54 us (1%)
    ppermute x1, waiting for transfers between devices, local(): first_in = lax.ppermute(to_next, BOTH, [(2 * source[0] + 1, 2 * target[0])])  22.7 us
    ppermute x9, starting transfers between devices, cross(): return lax.ppermute(value, BOTH, perm)  6.77 us
    ppermute x1, waiting for transfers between devices, local(): far = lax.ppermute(near, BOTH, link(odd[:-1], even[:-1]))  4.46 us
    ppermute x5, starting transfers between devices, local(): own_in = lax.ppermute(lower, BOTH, link(source, target))  3.32 us
    pallas_call x2, Pallas kernels, pair_matrix(): pl.pallas_call(functools.partial(pair_kernel, (pairs - 2, first), jumps),...  1.68 us
    pallas_call x1, Pallas kernels, local(): pl.pallas_call(const_kernel, out_shape=(shape((cols, sites), f32), shape(...  1.48 us
    ppermute x1, starting transfers between devices, local(): far = lax.ppermute(near, BOTH, link(odd[:-1], even[:-1]))  1.29 us
    ppermute x1, starting transfers between devices, local(): first_in = lax.ppermute(to_next, BOTH, [(2 * source[0] + 1, 2 * target[0])])  1.29 us
  transfers between devices with their start and end apart: 22, of which 4 were waited for; matrix products, arithmetic and copies ran while one was open for 0% of the time, Pallas kernels for 7%

profile of v16, /device:TPU:0, one launch (start us, length us, event | category | flops | bytes accessed | tf_op | source)
XLA Modules:
  0.0 52.5 jit_solution(1578425653480726826)
XLA Ops:
  0.0 1.5 %shard_map.46 = (f32[32,512]{1,0:T(8,128)S(1)}, bf16[2,256,256]{2,1,0:T(8,128)(2,1)S(1)}, bf16[2,256,256]{2,1,0:T(8,128)(2,1)S(1)}) custom-call(f32[1,32,512]{2,1,0:T(8,128)} %normals.1, f32[1,2,256,256]{3,2,1,0:T(8,128)} %inv.1), custom_call_target="tpu_custom_call" | custom-call | tf_op jit(solution)/shard_map/pallas_call | solution.py:448
  1.5 0.0 copy-start
  1.5 0.0 copy-start.1
  1.5 0.8 %collective-permute-start.2 = (f32[1,32,128]{2,1,0:T(8,128)S(1)}, f32[1,32,128]{2,1,0:T(8,128)S(1)}, u32[]{:S(2)}, u32[]{:S(2)}) collective-permute-start(f32[1,32,128]{2,1,0:T(8,128)S(1)} %shard_map.52._after), channel_id=1, source_target_pairs={{30,29},{31,28}} | collective-permute-start | bytes 49160 | tf_op jit(solution)/shard_map/ppermute | solution.py:433
  2.4 0.7 %collective-permute-start.3 = (f32[32,512]{1,0:T(8,128)S(1)}, f32[32,512]{1,0:T(8,128)S(1)}, u32[]{:S(2)}, u32[]{:S(2)}) collective-permute-start(f32[32,512]{1,0:T(8,128)S(1)} %shard_map.53), channel_id=1, source_target_pairs={{30,28},{31,29}} | collective-permute-start | bytes 196616 | tf_op jit(solution)/shard_map/ppermute | solution.py:480
  3.0 0.7 %shard_map.47 = (bf16[1024,256]{1,0:T(8,128)(2,1)S(1)}, bf16[1024,256]{1,0:T(8,128)(2,1)S(1)}, f32[1088,256]{1,0:T(8,128)S(1)}) custom-call(s32[1,2,3]{2,1,0:T(2,128)S(1)} %copy-done.1, f32[32,512]{1,0:T(8,128)S(1)} %get-tuple-element.56.refs_1_.refs_6_.const, bf16[2,256,256]{2,1,0:T(8,128)(2,1)S(1)} %get-tuple-element.57.refs_2_, ...), custom_call_target="tpu_custom_call" | custom-call | flops 10695475200 | tf_op jit(solution)/shard_map/pallas_call | solution.py:483
  3.8 1.3 %collective-permute-start.1 = (f32[1,544,128]{2,1,0:T(8,128)S(1)}, f32[1,544,128]{2,1,0:T(8,128)S(1)}, u32[]{:S(2)}, u32[]{:S(2)}) collective-permute-start(f32[1,544,128]{2,1,0:T(8,128)S(1)} %shard_map.48._edges), channel_id=1, source_target_pairs={{2,1},{3,0},{6,5},{7,4},{10,9},{11,8},{14,13},{15,12},{18,17},{19,... | collective-permute-start | bytes 835592 | tf_op jit(solution)/shard_map/ppermute | solution.py:433
  5.1 1.3 %collective-permute-start = (f32[1088,256]{1,0:T(8,128)S(1)}, f32[1088,256]{1,0:T(8,128)S(1)}, u32[]{:S(2)}, u32[]{:S(2)}) collective-permute-start(f32[1088,256]{1,0:T(8,128)S(1)} %shard_map.49), channel_id=1, source_target_pairs={{2,0},{3,1},{6,4},{7,5},{10,8},{11,9},{14,12},{15,13},{18,16},{19,... | collective-permute-start | bytes 3342344 | tf_op jit(solution)/shard_map/ppermute | solution.py:511
  6.4 0.0 collective-permute-done.2.next_in
  6.4 0.0 collective-permute-done.3.own_in
  6.5 0.7 %collective-permute-start.5 = (f32[32,512]{1,0:T(8,128)S(1)}, f32[32,512]{1,0:T(8,128)S(1)}, u32[]{:S(2)}, u32[]{:S(2)}) collective-permute-start(f32[32,512]{1,0:T(8,128)S(1)} %get-tuple-element.67.refs_5_._lower), channel_id=1, source_target_pairs={{28,25},{29,24}} | collective-permute-start | bytes 196616 | tf_op jit(solution)/shard_map/ppermute | solution.py:433
  7.2 0.7 %collective-permute-start.4 = (f32[32,512]{1,0:T(8,128)S(1)}, f32[32,512]{1,0:T(8,128)S(1)}, u32[]{:S(2)}, u32[]{:S(2)}) collective-permute-start(f32[32,512]{1,0:T(8,128)S(1)} %get-tuple-element.67.refs_5_._lower), channel_id=1, source_target_pairs={{28,24},{29,25}} | collective-permute-start | bytes 196616 | tf_op jit(solution)/shard_map/ppermute | solution.py:585
  7.9 4.5 %collective-permute-done.far.refs_0_.rest_5_ = f32[1088,256]{1,0:T(8,128)S(1)} collective-permute-done((f32[1088,256]{1,0:T(8,128)S(1)}, f32[1088,256]{1,0:T(8,128)S(1)}, u32[]{:S(2)}, u32[]{:S(2)}) %collective-permute-start) | collective-permute-done | bytes 1114144 | tf_op jit(solution)/shard_map/ppermute | solution.py:511
  12.3 0.1 shard_map.50
  12.5 0.0 collective-permute-done.1.refs_1_
  12.6 0.0 collective-permute-done.4.own_in
  12.6 0.7 %collective-permute-start.7 = (f32[32,512]{1,0:T(8,128)S(1)}, f32[32,512]{1,0:T(8,128)S(1)}, u32[]{:S(2)}, u32[]{:S(2)}) collective-permute-start(f32[32,512]{1,0:T(8,128)S(1)} %get-tuple-element.75._lower), channel_id=1, source_target_pairs={{24,21},{25,20}} | collective-permute-start | bytes 196616 | tf_op jit(solution)/shard_map/ppermute | solution.py:433
  13.3 0.7 %collective-permute-start.6 = (f32[32,512]{1,0:T(8,128)S(1)}, f32[32,512]{1,0:T(8,128)S(1)}, u32[]{:S(2)}, u32[]{:S(2)}) collective-permute-start(f32[32,512]{1,0:T(8,128)S(1)} %get-tuple-element.75._lower), channel_id=1, source_target_pairs={{24,20},{25,21}} | collective-permute-start | bytes 196616 | tf_op jit(solution)/shard_map/ppermute | solution.py:585
  13.9 1.7 %shard_map.51 = (bf16[2048,256]{1,0:T(8,128)(2,1)S(1)}, bf16[2048,256]{1,0:T(8,128)(2,1)S(1)}, f32[32,512]{1,0:T(8,128)S(1)}, f32[1088,256]{1,0:T(8,128)S(1)}, f32[512,256]{1,0:T(8,128)S(1)}) custom-call(f32[1088,256]{1,0:T(8,128)S(1)} %collective-permute-done.far.refs_0_.rest_5_, f32[1,544,128]{2,1,0:T(8,128)S(1)} %collective-permute-done.1.refs_1_, ...), custom_call_target="tpu_custom_call" | custom-call | flops 1000000000 | tf_op jit(solution)/shard_map/pallas_call | solution.py:534
  15.6 0.7 %collective-permute-start.14 = (f32[1088,256]{1,0:T(8,128)S(1)}, f32[1088,256]{1,0:T(8,128)S(1)}, u32[]{:S(2)}, u32[]{:S(2)}) collective-permute-start(f32[1088,256]{1,0:T(8,128)S(1)} %get-tuple-element.90), channel_id=1, source_target_pairs={{4,8},{5,9},{8,12},{9,13}} | collective-permute-start | bytes 3342344 | tf_op jit(solution)/shard_map/ppermute | solution.py:550
  16.3 0.7 %collective-permute-start.15 = (f32[512,256]{1,0:T(8,128)S(1)}, f32[512,256]{1,0:T(8,128)S(1)}, u32[]{:S(2)}, u32[]{:S(2)}) collective-permute-start(f32[512,256]{1,0:T(8,128)S(1)} %get-tuple-element.91), channel_id=1, source_target_pairs={{4,9},{5,8},{8,13},{9,12}} | collective-permute-start | bytes 1572872 | tf_op jit(solution)/shard_map/ppermute | solution.py:433
  17.0 0.0 collective-permute-done.7.next_in
  17.1 0.0 collective-permute-done.6.own_in
  17.1 0.7 %collective-permute-start.9 = (f32[32,512]{1,0:T(8,128)S(1)}, f32[32,512]{1,0:T(8,128)S(1)}, u32[]{:S(2)}, u32[]{:S(2)}) collective-permute-start(f32[32,512]{1,0:T(8,128)S(1)} %get-tuple-element.79._lower), channel_id=1, source_target_pairs={{20,17},{21,16}} | collective-permute-start | bytes 196616 | tf_op jit(solution)/shard_map/ppermute | solution.py:433
  17.8 0.7 %collective-permute-start.8 = (f32[32,512]{1,0:T(8,128)S(1)}, f32[32,512]{1,0:T(8,128)S(1)}, u32[]{:S(2)}, u32[]{:S(2)}) collective-permute-start(f32[32,512]{1,0:T(8,128)S(1)} %get-tuple-element.79._lower), channel_id=1, source_target_pairs={{20,16},{21,17}} | collective-permute-start | bytes 196616 | tf_op jit(solution)/shard_map/ppermute | solution.py:585
  18.5 0.0 collective-permute-done.8.own_in
  18.5 0.7 %collective-permute-start.11 = (f32[32,512]{1,0:T(8,128)S(1)}, f32[32,512]{1,0:T(8,128)S(1)}, u32[]{:S(2)}, u32[]{:S(2)}) collective-permute-start(f32[32,512]{1,0:T(8,128)S(1)} %get-tuple-element.83._lower), channel_id=1, source_target_pairs={{16,13},{17,12}} | collective-permute-start | bytes 196616 | tf_op jit(solution)/shard_map/ppermute | solution.py:433
  19.2 0.7 %collective-permute-start.10 = (f32[32,512]{1,0:T(8,128)S(1)}, f32[32,512]{1,0:T(8,128)S(1)}, u32[]{:S(2)}, u32[]{:S(2)}) collective-permute-start(f32[32,512]{1,0:T(8,128)S(1)} %get-tuple-element.83._lower), channel_id=1, source_target_pairs={{16,12},{17,13}} | collective-permute-start | bytes 196616 | tf_op jit(solution)/shard_map/ppermute | solution.py:585
  19.9 0.0 collective-permute-done.11.next_in
  20.0 0.7 %collective-permute-start.13 = (f32[32,512]{1,0:T(8,128)S(1)}, f32[32,512]{1,0:T(8,128)S(1)}, u32[]{:S(2)}, u32[]{:S(2)}) collective-permute-start(f32[32,512]{1,0:T(8,128)S(1)} %get-tuple-element.87.rest_6_.lower), channel_id=1, source_target_pairs={{12,9},{13,8}} | collective-permute-start | bytes 196616 | tf_op jit(solution)/shard_map/ppermute | solution.py:433
  20.6 0.7 %collective-permute-start.12 = (f32[32,512]{1,0:T(8,128)S(1)}, f32[32,512]{1,0:T(8,128)S(1)}, u32[]{:S(2)}, u32[]{:S(2)}) collective-permute-start(f32[32,512]{1,0:T(8,128)S(1)} %get-tuple-element.87.rest_6_.lower), channel_id=1, source_target_pairs={{12,8},{13,9}} | collective-permute-start | bytes 196616 | tf_op jit(solution)/shard_map/ppermute | solution.py:585
  21.3 0.0 collective-permute-done.13.next_in
  21.3 0.0 collective-permute-done.15.other_rows
  21.4 0.2 shard_map.66
  21.6 0.0 collective-permute-done.12.own_in
  21.7 1.3 %collective-permute-start.16 = (f32[32,896]{1,0:T(8,128)S(1)}, f32[32,896]{1,0:T(8,128)S(1)}, u32[]{:S(2)}, u32[]{:S(2)}) collective-permute-start(f32[32,896]{1,0:T(8,128)S(1)} %get-tuple-element.97), channel_id=1, source_target_pairs={{9,0}} | collective-permute-start | bytes 344072 | tf_op jit(solution)/shard_map/ppermute | solution.py:579
  23.0 1.3 %collective-permute-start.17 = (f32[32,896]{1,0:T(8,128)S(1)}, f32[32,896]{1,0:T(8,128)S(1)}, u32[]{:S(2)}, u32[]{:S(2)}) collective-permute-start(f32[32,896]{1,0:T(8,128)S(1)} %get-tuple-element.98), channel_id=1, source_target_pairs={{8,0},{9,1}} | collective-permute-start | bytes 344072 | tf_op jit(solution)/shard_map/ppermute | solution.py:580
  24.3 0.7 %collective-permute-start.18 = (f32[32,896]{1,0:T(8,128)S(1)}, f32[32,896]{1,0:T(8,128)S(1)}, u32[]{:S(2)}, u32[]{:S(2)}) collective-permute-start(f32[32,896]{1,0:T(8,128)S(1)} %get-tuple-element.99), channel_id=1, source_target_pairs={{8,1}} | collective-permute-start | bytes 344072 | tf_op jit(solution)/shard_map/ppermute | solution.py:581
  25.0 0.7 %collective-permute-start.19 = (f32[32,896]{1,0:T(8,128)S(1)}, f32[32,896]{1,0:T(8,128)S(1)}, u32[]{:S(2)}, u32[]{:S(2)}) collective-permute-start(f32[32,896]{1,0:T(8,128)S(1)} %get-tuple-element.100), channel_id=1, source_target_pairs={{12,5},{13,4}} | collective-permute-start | bytes 344072 | tf_op jit(solution)/shard_map/ppermute | solution.py:433
  25.7 0.7 %collective-permute-start.20 = (f32[32,896]{1,0:T(8,128)S(1)}, f32[32,896]{1,0:T(8,128)S(1)}, u32[]{:S(2)}, u32[]{:S(2)}) collective-permute-start(f32[32,896]{1,0:T(8,128)S(1)} %get-tuple-element.101), channel_id=1, source_target_pairs={{12,4},{13,5}} | collective-permute-start | bytes 344072 | tf_op jit(solution)/shard_map/ppermute | solution.py:597
  26.3 22.7 %collective-permute-done.16.rest_0_ = f32[32,896]{1,0:T(8,128)S(1)} collective-permute-done((f32[32,896]{1,0:T(8,128)S(1)}, f32[32,896]{1,0:T(8,128)S(1)}, u32[]{:S(2)}, u32[]{:S(2)}) %collective-permute-start.16) | collective-permute-done | bytes 114720 | tf_op jit(solution)/shard_map/ppermute | solution.py:579
  49.0 0.3 collective-permute-done.17.rest_1_
  49.4 0.0 collective-permute-done.20.rest_4_
  49.4 0.3 shard_map.69
  49.7 1.3 %collective-permute-start.21 = (f32[32,512]{1,0:T(8,128)S(1)}, f32[32,512]{1,0:T(8,128)S(1)}, u32[]{:S(2)}, u32[]{:S(2)}) collective-permute-start(f32[32,512]{1,0:T(8,128)S(1)} %get-tuple-element.106), channel_id=1, source_target_pairs={{0,2},{1,3},{4,6},{5,7},{8,10},{9,11},{12,14},{13,15},{16,18},{17,... | collective-permute-start | bytes 196616 | tf_op jit(solution)/shard_map/ppermute | solution.py:627
  51.0 0.5 shard_map.70
  51.5 0.4 collective-permute-done.21
  51.9 0.6 %select_bitcast_fusion = f32[1,32,512]{2,1,0:T(8,128)} fusion(f32[32,512]{1,0:T(8,128)S(1)} %shard_map.70, f32[32,512]{1,0:T(8,128)S(1)} %collective-permute-done.21, pred[]{:T(512)S(6)} %eq.5), kind=kLoop, calls=%fused_computation | loop fusion | flops 16384 | bytes 196609 | tf_op jit(solution)/shard_map/broadcast_in_dim | solution.py:637
  (29 shorter events, 0.4 us)
Async XLA Ops:
  1.5 1.5 %copy-start = (f32[1,2,512,256]{3,2,1,0:T(8,128)S(1)}, f32[1,2,512,256]{3,2,1,0:T(8,128)}, u32[]{:S(2)}) copy-start(f32[1,2,512,256]{3,2,1,0:T(8,128)} %refs_4_.3) | copy-start | bytes 3145732
  1.5 1.5 %copy-start.1 = (s32[1,2,3]{2,1,0:T(2,128)S(1)}, s32[1,2,3]{2,1,0:T(2,128)}, u32[]{:S(2)}) copy-start(s32[1,2,3]{2,1,0:T(2,128)} %refs_0_.3) | copy-start | bytes 76
  1.5 4.9 %collective-permute-start.2 = (f32[1,32,128]{2,1,0:T(8,128)S(1)}, f32[1,32,128]{2,1,0:T(8,128)S(1)}, u32[]{:S(2)}, u32[]{:S(2)}) collective-permute-start(f32[1,32,128]{2,1,0:T(8,128)S(1)} %shard_map.52._after), channel_id=1, source_target_pairs={{30,29},{31,28}} | collective-permute-start | bytes 49160 | tf_op jit(solution)/shard_map/ppermute | solution.py:433
  2.4 4.1 %collective-permute-start.3 = (f32[32,512]{1,0:T(8,128)S(1)}, f32[32,512]{1,0:T(8,128)S(1)}, u32[]{:S(2)}, u32[]{:S(2)}) collective-permute-start(f32[32,512]{1,0:T(8,128)S(1)} %shard_map.53), channel_id=1, source_target_pairs={{30,28},{31,29}} | collective-permute-start | bytes 196616 | tf_op jit(solution)/shard_map/ppermute | solution.py:480
  3.8 8.7 %collective-permute-start.1 = (f32[1,544,128]{2,1,0:T(8,128)S(1)}, f32[1,544,128]{2,1,0:T(8,128)S(1)}, u32[]{:S(2)}, u32[]{:S(2)}) collective-permute-start(f32[1,544,128]{2,1,0:T(8,128)S(1)} %shard_map.48._edges), channel_id=1, source_target_pairs={{2,1},{3,0},{6,5},{7,4},{10,9},{11,8},{14,13},{15,12},{18,17},{19,... | collective-permute-start | bytes 835592 | tf_op jit(solution)/shard_map/ppermute | solution.py:433
  5.1 7.2 %collective-permute-start = (f32[1088,256]{1,0:T(8,128)S(1)}, f32[1088,256]{1,0:T(8,128)S(1)}, u32[]{:S(2)}, u32[]{:S(2)}) collective-permute-start(f32[1088,256]{1,0:T(8,128)S(1)} %shard_map.49), channel_id=1, source_target_pairs={{2,0},{3,1},{6,4},{7,5},{10,8},{11,9},{14,12},{15,13},{18,16},{19,... | collective-permute-start | bytes 3342344 | tf_op jit(solution)/shard_map/ppermute | solution.py:511
  6.5 6.0 %collective-permute-start.5 = (f32[32,512]{1,0:T(8,128)S(1)}, f32[32,512]{1,0:T(8,128)S(1)}, u32[]{:S(2)}, u32[]{:S(2)}) collective-permute-start(f32[32,512]{1,0:T(8,128)S(1)} %get-tuple-element.67.refs_5_._lower), channel_id=1, source_target_pairs={{28,25},{29,24}} | collective-permute-start | bytes 196616 | tf_op jit(solution)/shard_map/ppermute | solution.py:433
  7.2 5.4 %collective-permute-start.4 = (f32[32,512]{1,0:T(8,128)S(1)}, f32[32,512]{1,0:T(8,128)S(1)}, u32[]{:S(2)}, u32[]{:S(2)}) collective-permute-start(f32[32,512]{1,0:T(8,128)S(1)} %get-tuple-element.67.refs_5_._lower), channel_id=1, source_target_pairs={{28,24},{29,25}} | collective-permute-start | bytes 196616 | tf_op jit(solution)/shard_map/ppermute | solution.py:585
  12.6 4.5 %collective-permute-start.7 = (f32[32,512]{1,0:T(8,128)S(1)}, f32[32,512]{1,0:T(8,128)S(1)}, u32[]{:S(2)}, u32[]{:S(2)}) collective-permute-start(f32[32,512]{1,0:T(8,128)S(1)} %get-tuple-element.75._lower), channel_id=1, source_target_pairs={{24,21},{25,20}} | collective-permute-start | bytes 196616 | tf_op jit(solution)/shard_map/ppermute | solution.py:433
  13.3 3.8 %collective-permute-start.6 = (f32[32,512]{1,0:T(8,128)S(1)}, f32[32,512]{1,0:T(8,128)S(1)}, u32[]{:S(2)}, u32[]{:S(2)}) collective-permute-start(f32[32,512]{1,0:T(8,128)S(1)} %get-tuple-element.75._lower), channel_id=1, source_target_pairs={{24,20},{25,21}} | collective-permute-start | bytes 196616 | tf_op jit(solution)/shard_map/ppermute | solution.py:585
  15.6 5.7 %collective-permute-start.14 = (f32[1088,256]{1,0:T(8,128)S(1)}, f32[1088,256]{1,0:T(8,128)S(1)}, u32[]{:S(2)}, u32[]{:S(2)}) collective-permute-start(f32[1088,256]{1,0:T(8,128)S(1)} %get-tuple-element.90), channel_id=1, source_target_pairs={{4,8},{5,9},{8,12},{9,13}} | collective-permute-start | bytes 3342344 | tf_op jit(solution)/shard_map/ppermute | solution.py:550
  16.3 5.0 %collective-permute-start.15 = (f32[512,256]{1,0:T(8,128)S(1)}, f32[512,256]{1,0:T(8,128)S(1)}, u32[]{:S(2)}, u32[]{:S(2)}) collective-permute-start(f32[512,256]{1,0:T(8,128)S(1)} %get-tuple-element.91), channel_id=1, source_target_pairs={{4,9},{5,8},{8,13},{9,12}} | collective-permute-start | bytes 1572872 | tf_op jit(solution)/shard_map/ppermute | solution.py:433
  17.1 1.3 %collective-permute-start.9 = (f32[32,512]{1,0:T(8,128)S(1)}, f32[32,512]{1,0:T(8,128)S(1)}, u32[]{:S(2)}, u32[]{:S(2)}) collective-permute-start(f32[32,512]{1,0:T(8,128)S(1)} %get-tuple-element.79._lower), channel_id=1, source_target_pairs={{20,17},{21,16}} | collective-permute-start | bytes 196616 | tf_op jit(solution)/shard_map/ppermute | solution.py:433
  17.8 0.7 %collective-permute-start.8 = (f32[32,512]{1,0:T(8,128)S(1)}, f32[32,512]{1,0:T(8,128)S(1)}, u32[]{:S(2)}, u32[]{:S(2)}) collective-permute-start(f32[32,512]{1,0:T(8,128)S(1)} %get-tuple-element.79._lower), channel_id=1, source_target_pairs={{20,16},{21,17}} | collective-permute-start | bytes 196616 | tf_op jit(solution)/shard_map/ppermute | solution.py:585
  18.5 1.3 %collective-permute-start.11 = (f32[32,512]{1,0:T(8,128)S(1)}, f32[32,512]{1,0:T(8,128)S(1)}, u32[]{:S(2)}, u32[]{:S(2)}) collective-permute-start(f32[32,512]{1,0:T(8,128)S(1)} %get-tuple-element.83._lower), channel_id=1, source_target_pairs={{16,13},{17,12}} | collective-permute-start | bytes 196616 | tf_op jit(solution)/shard_map/ppermute | solution.py:433
  19.2 0.7 %collective-permute-start.10 = (f32[32,512]{1,0:T(8,128)S(1)}, f32[32,512]{1,0:T(8,128)S(1)}, u32[]{:S(2)}, u32[]{:S(2)}) collective-permute-start(f32[32,512]{1,0:T(8,128)S(1)} %get-tuple-element.83._lower), channel_id=1, source_target_pairs={{16,12},{17,13}} | collective-permute-start | bytes 196616 | tf_op jit(solution)/shard_map/ppermute | solution.py:585
  20.0 1.3 %collective-permute-start.13 = (f32[32,512]{1,0:T(8,128)S(1)}, f32[32,512]{1,0:T(8,128)S(1)}, u32[]{:S(2)}, u32[]{:S(2)}) collective-permute-start(f32[32,512]{1,0:T(8,128)S(1)} %get-tuple-element.87.rest_6_.lower), channel_id=1, source_target_pairs={{12,9},{13,8}} | collective-permute-start | bytes 196616 | tf_op jit(solution)/shard_map/ppermute | solution.py:433
  20.6 1.0 %collective-permute-start.12 = (f32[32,512]{1,0:T(8,128)S(1)}, f32[32,512]{1,0:T(8,128)S(1)}, u32[]{:S(2)}, u32[]{:S(2)}) collective-permute-start(f32[32,512]{1,0:T(8,128)S(1)} %get-tuple-element.87.rest_6_.lower), channel_id=1, source_target_pairs={{12,8},{13,9}} | collective-permute-start | bytes 196616 | tf_op jit(solution)/shard_map/ppermute | solution.py:585
  21.7 27.3 %collective-permute-start.16 = (f32[32,896]{1,0:T(8,128)S(1)}, f32[32,896]{1,0:T(8,128)S(1)}, u32[]{:S(2)}, u32[]{:S(2)}) collective-permute-start(f32[32,896]{1,0:T(8,128)S(1)} %get-tuple-element.97), channel_id=1, source_target_pairs={{9,0}} | collective-permute-start | bytes 344072 | tf_op jit(solution)/shard_map/ppermute | solution.py:579
  23.0 26.4 %collective-permute-start.17 = (f32[32,896]{1,0:T(8,128)S(1)}, f32[32,896]{1,0:T(8,128)S(1)}, u32[]{:S(2)}, u32[]{:S(2)}) collective-permute-start(f32[32,896]{1,0:T(8,128)S(1)} %get-tuple-element.98), channel_id=1, source_target_pairs={{8,0},{9,1}} | collective-permute-start | bytes 344072 | tf_op jit(solution)/shard_map/ppermute | solution.py:580
  24.3 25.1 %collective-permute-start.18 = (f32[32,896]{1,0:T(8,128)S(1)}, f32[32,896]{1,0:T(8,128)S(1)}, u32[]{:S(2)}, u32[]{:S(2)}) collective-permute-start(f32[32,896]{1,0:T(8,128)S(1)} %get-tuple-element.99), channel_id=1, source_target_pairs={{8,1}} | collective-permute-start | bytes 344072 | tf_op jit(solution)/shard_map/ppermute | solution.py:581
  25.0 24.4 %collective-permute-start.19 = (f32[32,896]{1,0:T(8,128)S(1)}, f32[32,896]{1,0:T(8,128)S(1)}, u32[]{:S(2)}, u32[]{:S(2)}) collective-permute-start(f32[32,896]{1,0:T(8,128)S(1)} %get-tuple-element.100), channel_id=1, source_target_pairs={{12,5},{13,4}} | collective-permute-start | bytes 344072 | tf_op jit(solution)/shard_map/ppermute | solution.py:433
  25.7 23.7 %collective-permute-start.20 = (f32[32,896]{1,0:T(8,128)S(1)}, f32[32,896]{1,0:T(8,128)S(1)}, u32[]{:S(2)}, u32[]{:S(2)}) collective-permute-start(f32[32,896]{1,0:T(8,128)S(1)} %get-tuple-element.101), channel_id=1, source_target_pairs={{12,4},{13,5}} | collective-permute-start | bytes 344072 | tf_op jit(solution)/shard_map/ppermute | solution.py:597
  49.7 2.2 %collective-permute-start.21 = (f32[32,512]{1,0:T(8,128)S(1)}, f32[32,512]{1,0:T(8,128)S(1)}, u32[]{:S(2)}, u32[]{:S(2)}) collective-permute-start(f32[32,512]{1,0:T(8,128)S(1)} %get-tuple-element.106), channel_id=1, source_target_pairs={{0,2},{1,3},{4,6},{5,7},{8,10},{9,11},{12,14},{13,15},{16,18},{17,... | collective-permute-start | bytes 196616 | tf_op jit(solution)/shard_map/ppermute | solution.py:627

commit v17 on v16

--- a/solution.py
+++ b/solution.py
@@ -49,7 +49,15 @@
         rim[1] = columns(False)
 
 
-def const_kernel(normals, inv, const, inv_high, inv_low, normals_in, inv_in, sems):
+def const_kernel(which, normals, inv, *refs):
+    device = lax.axis_index("tm")
+    late = device == which[1]
+    odd = device % 2 == 1
+    active = {"odd": odd, "even": jnp.logical_not(odd | late), "late": late}[which[0]]
+    pl.when(active)(lambda: make_const(normals, inv, *refs[-6:]))
+
+
+def make_const(normals, inv, const, inv_high, inv_low, normals_in, inv_in, sems):
     blocks, length = inv.shape[1], inv.shape[2]
     moves = [pltpu.make_async_copy(normals.at[0], normals_in, sems.at[0])]
     for b in range(blocks):
@@ -76,8 +84,7 @@
 
 def fuse_kernel(late, *refs):
     here = lax.axis_index("tm") == late[0]
-    given = refs[:5] + refs[6:] if late[1] else refs
-    pl.when(here if late[1] else jnp.logical_not(here))(lambda: make_fused(*given))
+    pl.when(here if late[1] else jnp.logical_not(here))(lambda: make_fused(*refs))
 
 
 def make_fused(mask, const, inv_high, inv_low, lag, near_high, near_low, own=None):
@@ -445,21 +452,28 @@
     tall = blocks * window
     jump = 2
     jumps = rows == 2 and pairs > 5 and blocks == 2
-    const, inv_high, inv_low = pl.pallas_call(
-        const_kernel,
-        out_shape=(
-            shape((cols, sites), f32),
-            shape((blocks, length, length), bf16), shape((blocks, length, length), bf16),
-        ),
-        in_specs=[HBM] * 2,
-        out_specs=(VMEM,) * 3,
-        scratch_shapes=[
-            pltpu.VMEM(normals.shape[1:], f32),
-            pltpu.VMEM(inv_diag.shape[1:], f32),
-            pltpu.SemaphoreType.DMA((1 + blocks,)),
-        ],
-        compiler_params=PARAMS,
-    )(*[pltpu.with_memory_space_constraint(a, pltpu.HBM) for a in (normals, inv_diag)])
+
+    def consts(which, alias=(), after=()):
+        return pl.pallas_call(
+            functools.partial(const_kernel, (which, 2 * pairs - 4)),
+            out_shape=(
+                shape((cols, sites), f32),
+                shape((blocks, length, length), bf16), shape((blocks, length, length), bf16),
+            ),
+            in_specs=[HBM] * 2 + [VMEM] * (len(alias) + len(after)),
+            out_specs=(VMEM,) * 3,
+            scratch_shapes=[
+                pltpu.VMEM(normals.shape[1:], f32),
+                pltpu.VMEM(inv_diag.shape[1:], f32),
+                pltpu.SemaphoreType.DMA((1 + blocks,)),
+            ],
+            input_output_aliases={2 + i: i for i in range(len(alias))},
+            compiler_params=PARAMS,
+            cost_estimate=pl.CostEstimate(flops=10**9 if which == "late" else 0, bytes_accessed=0, transcendentals=0),
+        )(*[pltpu.with_memory_space_constraint(a, pltpu.HBM) for a in (normals, inv_diag)], *alias, *after)
+
+    odd_parts = consts("odd")
+    const = odd_parts[0]
     const_rim = pl.pallas_call(
         functools.partial(rim_of_kernel, sides),
         out_shape=shape((sides, cols, edge), f32),
@@ -479,19 +493,21 @@
     first_next = cross(const_rim, odd[-1:], even[-1:], True)
     first_own = lax.ppermute(again, BOTH, link(odd[-1:], even[-1:]))
 
-    def fused(late, extra, after=()):
+    const, inv_high, inv_low = consts("even", odd_parts, (const_rim, again))
+
+    def fused(late, extra, const, inv_high, inv_low):
         return pl.pallas_call(
             functools.partial(fuse_kernel, (2 * pairs - 4, late)),
             out_shape=(shape((tall, length), bf16), shape((tall, length), bf16), *extra),
-            in_specs=[VMEM] * (5 + len(after)),
+            in_specs=[VMEM] * 5,
             out_specs=(VMEM,) * (2 + len(extra)),
             compiler_params=PARAMS,
             cost_estimate=pl.CostEstimate(
                 flops=(6 if late else 150) * (tall + cols * blocks) * length * length, bytes_accessed=0, transcendentals=0
             ),
-        )(fill_mask, const, inv_high, inv_low, lag_coupling, *after)
-
-    near_high, near_low, near = fused(False, (shape((tall + blocks * cols, length), f32),))
+        )(fill_mask, const, inv_high, inv_low, lag_coupling)
+
+    near_high, near_low, near = fused(False, (shape((tall + blocks * cols, length), f32),), const, inv_high, inv_low)
     edges = pl.pallas_call(
         functools.partial(edge_kernel, sides, blocks, cols),
         out_shape=shape((sides, window + cols, edge), f32),
@@ -530,7 +546,7 @@
     )(far)
     packs = (shape((blocks * (sites + cols), length), f32), shape((halo + edge, length), f32)) if jumps else ()
 
-    def pair_matrix(first, jumps, packs, mine):
+    def pair_matrix(first, jumps, packs, mine, const):
         return pl.pallas_call(
             functools.partial(pair_kernel, (pairs - 2, first), jumps),
             out_shape=(
@@ -543,8 +559,9 @@
             cost_estimate=pl.CostEstimate(flops=10**9, bytes_accessed=0, transcendentals=0),
         )(far, rim, far_high, far_low, *mine, const)
 
-    early = pair_matrix(True, False, (), fused(True, (), (lower,)))
-    high, low, both, *packs = pair_matrix(False, jumps, packs, (near_high, near_low))
+    late_parts = consts("late", (), (lower,))
+    early = pair_matrix(True, False, (), fused(True, (), *late_parts), late_parts[0])
+    high, low, both, *packs = pair_matrix(False, jumps, packs, (near_high, near_low), const)
     if jumps:
         source, target = [2 * jump - 2, 2 * jump], [2 * jump, 2 * jump + 2]
         own_rows = lax.ppermute(packs[0], BOTH, link(source, target))

time: 53.3 us -> 53.3 us (level)
    pallas_call x1 -> x3, Pallas kernels: 1.48 us -> 1.57 us  [consts(): pl.pallas_call(functools.partial(const_kernel, (which, 2 * pairs - 4)), o...]
  transfers between devices with their start and end apart: 22 -> 22, of which waited for: 4 -> 4; matrix products, arithmetic and copies ran while one was open for 0% -> 0% of each run, Pallas kernels for 7% -> 10%
where the time goes in v17:
time: 53.3 us; the launch traced here: 52.6 us
  waiting for transfers between devices  27.9 us (52%)
  starting transfers between devices  18 us (34%)
  Pallas kernels  5.44 us (10%)
  other arithmetic  0.64 us (1%)
  between operations  0.56 us (1%)
    ppermute x1, waiting for transfers between devices, local(): first_in = lax.ppermute(to_next, BOTH, [(2 * source[0] + 1, 2 * target[0])])  22.7 us
    ppermute x9, starting transfers between devices, cross(): return lax.ppermute(value, BOTH, perm)  6.77 us
    ppermute x1, waiting for transfers between devices, local(): far = lax.ppermute(near, BOTH, link(odd[:-1], even[:-1]))  4.41 us
    ppermute x5, starting transfers between devices, local(): own_in = lax.ppermute(lower, BOTH, link(source, target))  3.32 us
    pallas_call x2, Pallas kernels, pair_matrix(): pl.pallas_call(functools.partial(pair_kernel, (pairs - 2, first), jumps),...  1.67 us
    pallas_call x3, Pallas kernels, consts(): pl.pallas_call(functools.partial(const_kernel, (which, 2 * pairs - 4)), o...  1.57 us
    ppermute x1, starting transfers between devices, local(): first_in = lax.ppermute(to_next, BOTH, [(2 * source[0] + 1, 2 * target[0])])  1.29 us
    ppermute x1, starting transfers between devices, local(): own_in = lax.ppermute(to_own, BOTH, link(source, target))  1.29 us
  transfers between devices with their start and end apart: 22, of which 4 were waited for; matrix products, arithmetic and copies ran while one was open for 0% of the time, Pallas kernels for 10%

profile of v17, /device:TPU:0, one launch (start us, length us, event | category | flops | bytes accessed | tf_op | source)
XLA Modules:
  0.0 52.6 jit_solution(18255203940791475398)
XLA Ops:
  0.1 0.0 copy-start
  0.1 0.0 copy-start.1
  0.1 0.8 %collective-permute-start.2 = (f32[1,32,128]{2,1,0:T(8,128)S(1)}, f32[1,32,128]{2,1,0:T(8,128)S(1)}, u32[]{:S(2)}, u32[]{:S(2)}) collective-permute-start(f32[1,32,128]{2,1,0:T(8,128)S(1)} %shard_map.47._after.refs_3_), channel_id=1, source_target_pairs={{30,29},{31,28}} | collective-permute-start | bytes 49160 | tf_op jit(solution)/shard_map/ppermute | solution.py:440
  0.9 0.7 %collective-permute-start.3 = (f32[32,512]{1,0:T(8,128)S(1)}, f32[32,512]{1,0:T(8,128)S(1)}, u32[]{:S(2)}, u32[]{:S(2)}) collective-permute-start(f32[32,512]{1,0:T(8,128)S(1)} %shard_map.48.refs_4_), channel_id=1, source_target_pairs={{30,28},{31,29}} | collective-permute-start | bytes 196616 | tf_op jit(solution)/shard_map/ppermute | solution.py:494
  1.6 1.5 %shard_map.49 = (f32[32,512]{1,0:T(8,128)S(1)}, bf16[2,256,256]{2,1,0:T(8,128)(2,1)S(1)}, bf16[2,256,256]{2,1,0:T(8,128)(2,1)S(1)}) custom-call(f32[1,32,512]{2,1,0:T(8,128)} %normals.5, f32[1,2,256,256]{3,2,1,0:T(8,128)} %inv.5, f32[32,512]{1,0:T(8,128)S(1)} %get-tuple-element.62.const.refs_0_, ...), custom_call_target="tpu_custom_call", output_to_operand_aliasing={{0}: (2, {}), {1}: (3, {}), {2}: (4, {})} | custom-call | tf_op jit(solution)/shard_map/pallas_call | solution.py:457
  3.1 0.7 %shard_map.50 = (bf16[1024,256]{1,0:T(8,128)(2,1)S(1)}, bf16[1024,256]{1,0:T(8,128)(2,1)S(1)}, f32[1088,256]{1,0:T(8,128)S(1)}) custom-call(s32[1,2,3]{2,1,0:T(2,128)S(1)} %copy-done.1, f32[32,512]{1,0:T(8,128)S(1)} %get-tuple-element.65.refs_1_.refs_6_.const, bf16[2,256,256]{2,1,0:T(8,128)(2,1)S(1)} %get-tuple-element.66.refs_2_, ...), custom_call_target="tpu_custom_call" | custom-call | flops 10695475200 | tf_op jit(solution)/shard_map/pallas_call | solution.py:499
  3.9 1.3 %collective-permute-start.1 = (f32[1,544,128]{2,1,0:T(8,128)S(1)}, f32[1,544,128]{2,1,0:T(8,128)S(1)}, u32[]{:S(2)}, u32[]{:S(2)}) collective-permute-start(f32[1,544,128]{2,1,0:T(8,128)S(1)} %shard_map.51._edges), channel_id=1, source_target_pairs={{2,1},{3,0},{6,5},{7,4},{10,9},{11,8},{14,13},{15,12},{18,17},{19,... | collective-permute-start | bytes 835592 | tf_op jit(solution)/shard_map/ppermute | solution.py:440
  5.2 1.3 %collective-permute-start = (f32[1088,256]{1,0:T(8,128)S(1)}, f32[1088,256]{1,0:T(8,128)S(1)}, u32[]{:S(2)}, u32[]{:S(2)}) collective-permute-start(f32[1088,256]{1,0:T(8,128)S(1)} %shard_map.52), channel_id=1, source_target_pairs={{2,0},{3,1},{6,4},{7,5},{10,8},{11,9},{14,12},{15,13},{18,16},{19,... | collective-permute-start | bytes 3342344 | tf_op jit(solution)/shard_map/ppermute | solution.py:527
  6.5 0.0 collective-permute-done.2.next_in
  6.5 0.0 collective-permute-done.3.own_in
  6.5 0.7 %collective-permute-start.5 = (f32[32,512]{1,0:T(8,128)S(1)}, f32[32,512]{1,0:T(8,128)S(1)}, u32[]{:S(2)}, u32[]{:S(2)}) collective-permute-start(f32[32,512]{1,0:T(8,128)S(1)} %get-tuple-element.76.refs_0_._lower), channel_id=1, source_target_pairs={{28,25},{29,24}} | collective-permute-start | bytes 196616 | tf_op jit(solution)/shard_map/ppermute | solution.py:440
  7.2 0.7 %collective-permute-start.4 = (f32[32,512]{1,0:T(8,128)S(1)}, f32[32,512]{1,0:T(8,128)S(1)}, u32[]{:S(2)}, u32[]{:S(2)}) collective-permute-start(f32[32,512]{1,0:T(8,128)S(1)} %get-tuple-element.76.refs_0_._lower), channel_id=1, source_target_pairs={{28,24},{29,25}} | collective-permute-start | bytes 196616 | tf_op jit(solution)/shard_map/ppermute | solution.py:602
  8.0 4.4 %collective-permute-done.far.refs_0_.rest_5_ = f32[1088,256]{1,0:T(8,128)S(1)} collective-permute-done((f32[1088,256]{1,0:T(8,128)S(1)}, f32[1088,256]{1,0:T(8,128)S(1)}, u32[]{:S(2)}, u32[]{:S(2)}) %collective-permute-start) | collective-permute-done | bytes 1114144 | tf_op jit(solution)/shard_map/ppermute | solution.py:527
  12.4 0.1 shard_map.53
  12.5 0.0 collective-permute-done.1.refs_1_
  12.5 0.0 collective-permute-done.5.next_in
  12.6 0.0 collective-permute-done.4.own_in
  12.6 0.7 %collective-permute-start.7 = (f32[32,512]{1,0:T(8,128)S(1)}, f32[32,512]{1,0:T(8,128)S(1)}, u32[]{:S(2)}, u32[]{:S(2)}) collective-permute-start(f32[32,512]{1,0:T(8,128)S(1)} %get-tuple-element.87._lower), channel_id=1, source_target_pairs={{24,21},{25,20}} | collective-permute-start | bytes 196616 | tf_op jit(solution)/shard_map/ppermute | solution.py:440
  13.3 0.7 %collective-permute-start.6 = (f32[32,512]{1,0:T(8,128)S(1)}, f32[32,512]{1,0:T(8,128)S(1)}, u32[]{:S(2)}, u32[]{:S(2)}) collective-permute-start(f32[32,512]{1,0:T(8,128)S(1)} %get-tuple-element.87._lower), channel_id=1, source_target_pairs={{24,20},{25,21}} | collective-permute-start | bytes 196616 | tf_op jit(solution)/shard_map/ppermute | solution.py:602
  14.0 1.6 %shard_map.54 = (bf16[2048,256]{1,0:T(8,128)(2,1)S(1)}, bf16[2048,256]{1,0:T(8,128)(2,1)S(1)}, f32[32,512]{1,0:T(8,128)S(1)}, f32[1088,256]{1,0:T(8,128)S(1)}, f32[512,256]{1,0:T(8,128)S(1)}) custom-call(f32[1088,256]{1,0:T(8,128)S(1)} %collective-permute-done.far.refs_0_.rest_5_, f32[1,544,128]{2,1,0:T(8,128)S(1)} %collective-permute-done.1.refs_1_, ...), custom_call_target="tpu_custom_call" | custom-call | flops 1000000000 | tf_op jit(solution)/shard_map/pallas_call | solution.py:550
  15.6 0.7 %collective-permute-start.14 = (f32[1088,256]{1,0:T(8,128)S(1)}, f32[1088,256]{1,0:T(8,128)S(1)}, u32[]{:S(2)}, u32[]{:S(2)}) collective-permute-start(f32[1088,256]{1,0:T(8,128)S(1)} %get-tuple-element.102), channel_id=1, source_target_pairs={{4,8},{5,9},{8,12},{9,13}} | collective-permute-start | bytes 3342344 | tf_op jit(solution)/shard_map/ppermute | solution.py:567
  16.4 0.7 %collective-permute-start.15 = (f32[512,256]{1,0:T(8,128)S(1)}, f32[512,256]{1,0:T(8,128)S(1)}, u32[]{:S(2)}, u32[]{:S(2)}) collective-permute-start(f32[512,256]{1,0:T(8,128)S(1)} %get-tuple-element.103), channel_id=1, source_target_pairs={{4,9},{5,8},{8,13},{9,12}} | collective-permute-start | bytes 1572872 | tf_op jit(solution)/shard_map/ppermute | solution.py:440
  17.1 0.0 collective-permute-done.7.next_in
  17.1 0.0 collective-permute-done.6.own_in
  17.1 0.7 %collective-permute-start.9 = (f32[32,512]{1,0:T(8,128)S(1)}, f32[32,512]{1,0:T(8,128)S(1)}, u32[]{:S(2)}, u32[]{:S(2)}) collective-permute-start(f32[32,512]{1,0:T(8,128)S(1)} %get-tuple-element.91._lower), channel_id=1, source_target_pairs={{20,17},{21,16}} | collective-permute-start | bytes 196616 | tf_op jit(solution)/shard_map/ppermute | solution.py:440
  17.8 0.7 %collective-permute-start.8 = (f32[32,512]{1,0:T(8,128)S(1)}, f32[32,512]{1,0:T(8,128)S(1)}, u32[]{:S(2)}, u32[]{:S(2)}) collective-permute-start(f32[32,512]{1,0:T(8,128)S(1)} %get-tuple-element.91._lower), channel_id=1, source_target_pairs={{20,16},{21,17}} | collective-permute-start | bytes 196616 | tf_op jit(solution)/shard_map/ppermute | solution.py:602
  18.5 0.0 collective-permute-done.9.next_in
  18.6 0.7 %collective-permute-start.11 = (f32[32,512]{1,0:T(8,128)S(1)}, f32[32,512]{1,0:T(8,128)S(1)}, u32[]{:S(2)}, u32[]{:S(2)}) collective-permute-start(f32[32,512]{1,0:T(8,128)S(1)} %get-tuple-element.95._lower), channel_id=1, source_target_pairs={{16,13},{17,12}} | collective-permute-start | bytes 196616 | tf_op jit(solution)/shard_map/ppermute | solution.py:440
  19.2 0.7 %collective-permute-start.10 = (f32[32,512]{1,0:T(8,128)S(1)}, f32[32,512]{1,0:T(8,128)S(1)}, u32[]{:S(2)}, u32[]{:S(2)}) collective-permute-start(f32[32,512]{1,0:T(8,128)S(1)} %get-tuple-element.95._lower), channel_id=1, source_target_pairs={{16,12},{17,13}} | collective-permute-start | bytes 196616 | tf_op jit(solution)/shard_map/ppermute | solution.py:602
  19.9 0.0 collective-permute-done.11.next_in
  19.9 0.0 collective-permute-done.10.own_in
  20.0 0.7 %collective-permute-start.13 = (f32[32,512]{1,0:T(8,128)S(1)}, f32[32,512]{1,0:T(8,128)S(1)}, u32[]{:S(2)}, u32[]{:S(2)}) collective-permute-start(f32[32,512]{1,0:T(8,128)S(1)} %get-tuple-element.99.rest_6_.lower), channel_id=1, source_target_pairs={{12,9},{13,8}} | collective-permute-start | bytes 196616 | tf_op jit(solution)/shard_map/ppermute | solution.py:440
  20.7 0.7 %collective-permute-start.12 = (f32[32,512]{1,0:T(8,128)S(1)}, f32[32,512]{1,0:T(8,128)S(1)}, u32[]{:S(2)}, u32[]{:S(2)}) collective-permute-start(f32[32,512]{1,0:T(8,128)S(1)} %get-tuple-element.99.rest_6_.lower), channel_id=1, source_target_pairs={{12,8},{13,9}} | collective-permute-start | bytes 196616 | tf_op jit(solution)/shard_map/ppermute | solution.py:602
  21.4 0.2 shard_map.68
  21.7 1.3 %collective-permute-start.16 = (f32[32,896]{1,0:T(8,128)S(1)}, f32[32,896]{1,0:T(8,128)S(1)}, u32[]{:S(2)}, u32[]{:S(2)}) collective-permute-start(f32[32,896]{1,0:T(8,128)S(1)} %get-tuple-element.109), channel_id=1, source_target_pairs={{9,0}} | collective-permute-start | bytes 344072 | tf_op jit(solution)/shard_map/ppermute | solution.py:596
  23.0 1.3 %collective-permute-start.17 = (f32[32,896]{1,0:T(8,128)S(1)}, f32[32,896]{1,0:T(8,128)S(1)}, u32[]{:S(2)}, u32[]{:S(2)}) collective-permute-start(f32[32,896]{1,0:T(8,128)S(1)} %get-tuple-element.110), channel_id=1, source_target_pairs={{8,0},{9,1}} | collective-permute-start | bytes 344072 | tf_op jit(solution)/shard_map/ppermute | solution.py:597
  24.3 0.7 %collective-permute-start.18 = (f32[32,896]{1,0:T(8,128)S(1)}, f32[32,896]{1,0:T(8,128)S(1)}, u32[]{:S(2)}, u32[]{:S(2)}) collective-permute-start(f32[32,896]{1,0:T(8,128)S(1)} %get-tuple-element.111), channel_id=1, source_target_pairs={{8,1}} | collective-permute-start | bytes 344072 | tf_op jit(solution)/shard_map/ppermute | solution.py:598
  25.0 0.7 %collective-permute-start.19 = (f32[32,896]{1,0:T(8,128)S(1)}, f32[32,896]{1,0:T(8,128)S(1)}, u32[]{:S(2)}, u32[]{:S(2)}) collective-permute-start(f32[32,896]{1,0:T(8,128)S(1)} %get-tuple-element.112), channel_id=1, source_target_pairs={{12,5},{13,4}} | collective-permute-start | bytes 344072 | tf_op jit(solution)/shard_map/ppermute | solution.py:440
  25.7 0.7 %collective-permute-start.20 = (f32[32,896]{1,0:T(8,128)S(1)}, f32[32,896]{1,0:T(8,128)S(1)}, u32[]{:S(2)}, u32[]{:S(2)}) collective-permute-start(f32[32,896]{1,0:T(8,128)S(1)} %get-tuple-element.113), channel_id=1, source_target_pairs={{12,4},{13,5}} | collective-permute-start | bytes 344072 | tf_op jit(solution)/shard_map/ppermute | solution.py:614
  26.4 22.7 %collective-permute-done.16.rest_0_ = f32[32,896]{1,0:T(8,128)S(1)} collective-permute-done((f32[32,896]{1,0:T(8,128)S(1)}, f32[32,896]{1,0:T(8,128)S(1)}, u32[]{:S(2)}, u32[]{:S(2)}) %collective-permute-start.16) | collective-permute-done | bytes 114720 | tf_op jit(solution)/shard_map/ppermute | solution.py:596
  49.1 0.3 collective-permute-done.17.rest_1_
  49.4 0.0 collective-permute-done.19.rest_3_
  49.4 0.0 collective-permute-done.20.rest_4_
  49.4 0.3 shard_map.71
  49.7 1.3 %collective-permute-start.21 = (f32[32,512]{1,0:T(8,128)S(1)}, f32[32,512]{1,0:T(8,128)S(1)}, u32[]{:S(2)}, u32[]{:S(2)}) collective-permute-start(f32[32,512]{1,0:T(8,128)S(1)} %get-tuple-element.118), channel_id=1, source_target_pairs={{0,2},{1,3},{4,6},{5,7},{8,10},{9,11},{12,14},{13,15},{16,18},{17,... | collective-permute-start | bytes 196616 | tf_op jit(solution)/shard_map/ppermute | solution.py:644
  51.1 0.5 shard_map.72
  51.5 0.4 collective-permute-done.21
  51.9 0.6 %select_bitcast_fusion = f32[1,32,512]{2,1,0:T(8,128)} fusion(f32[32,512]{1,0:T(8,128)S(1)} %shard_map.72, f32[32,512]{1,0:T(8,128)S(1)} %collective-permute-done.21, pred[]{:T(512)S(6)} %eq.5), kind=kLoop, calls=%fused_computation | loop fusion | flops 16384 | bytes 196609 | tf_op jit(solution)/shard_map/broadcast_in_dim | solution.py:654
  (31 shorter events, 0.5 us)
Async XLA Ops:
  0.1 3.0 %copy-start = (f32[1,2,512,256]{3,2,1,0:T(8,128)S(1)}, f32[1,2,512,256]{3,2,1,0:T(8,128)}, u32[]{:S(2)}) copy-start(f32[1,2,512,256]{3,2,1,0:T(8,128)} %refs_4_.3) | copy-start | bytes 3145732
  0.1 3.0 %copy-start.1 = (s32[1,2,3]{2,1,0:T(2,128)S(1)}, s32[1,2,3]{2,1,0:T(2,128)}, u32[]{:S(2)}) copy-start(s32[1,2,3]{2,1,0:T(2,128)} %refs_0_.3) | copy-start | bytes 76
  0.1 6.4 %collective-permute-start.2 = (f32[1,32,128]{2,1,0:T(8,128)S(1)}, f32[1,32,128]{2,1,0:T(8,128)S(1)}, u32[]{:S(2)}, u32[]{:S(2)}) collective-permute-start(f32[1,32,128]{2,1,0:T(8,128)S(1)} %shard_map.47._after.refs_3_), channel_id=1, source_target_pairs={{30,29},{31,28}} | collective-permute-start | bytes 49160 | tf_op jit(solution)/shard_map/ppermute | solution.py:440
  0.9 5.6 %collective-permute-start.3 = (f32[32,512]{1,0:T(8,128)S(1)}, f32[32,512]{1,0:T(8,128)S(1)}, u32[]{:S(2)}, u32[]{:S(2)}) collective-permute-start(f32[32,512]{1,0:T(8,128)S(1)} %shard_map.48.refs_4_), channel_id=1, source_target_pairs={{30,28},{31,29}} | collective-permute-start | bytes 196616 | tf_op jit(solution)/shard_map/ppermute | solution.py:494
  3.9 8.7 %collective-permute-start.1 = (f32[1,544,128]{2,1,0:T(8,128)S(1)}, f32[1,544,128]{2,1,0:T(8,128)S(1)}, u32[]{:S(2)}, u32[]{:S(2)}) collective-permute-start(f32[1,544,128]{2,1,0:T(8,128)S(1)} %shard_map.51._edges), channel_id=1, source_target_pairs={{2,1},{3,0},{6,5},{7,4},{10,9},{11,8},{14,13},{15,12},{18,17},{19,... | collective-permute-start | bytes 835592 | tf_op jit(solution)/shard_map/ppermute | solution.py:440
  5.2 7.2 %collective-permute-start = (f32[1088,256]{1,0:T(8,128)S(1)}, f32[1088,256]{1,0:T(8,128)S(1)}, u32[]{:S(2)}, u32[]{:S(2)}) collective-permute-start(f32[1088,256]{1,0:T(8,128)S(1)} %shard_map.52), channel_id=1, source_target_pairs={{2,0},{3,1},{6,4},{7,5},{10,8},{11,9},{14,12},{15,13},{18,16},{19,... | collective-permute-start | bytes 3342344 | tf_op jit(solution)/shard_map/ppermute | solution.py:527
  6.5 6.0 %collective-permute-start.5 = (f32[32,512]{1,0:T(8,128)S(1)}, f32[32,512]{1,0:T(8,128)S(1)}, u32[]{:S(2)}, u32[]{:S(2)}) collective-permute-start(f32[32,512]{1,0:T(8,128)S(1)} %get-tuple-element.76.refs_0_._lower), channel_id=1, source_target_pairs={{28,25},{29,24}} | collective-permute-start | bytes 196616 | tf_op jit(solution)/shard_map/ppermute | solution.py:440
  7.2 5.4 %collective-permute-start.4 = (f32[32,512]{1,0:T(8,128)S(1)}, f32[32,512]{1,0:T(8,128)S(1)}, u32[]{:S(2)}, u32[]{:S(2)}) collective-permute-start(f32[32,512]{1,0:T(8,128)S(1)} %get-tuple-element.76.refs_0_._lower), channel_id=1, source_target_pairs={{28,24},{29,25}} | collective-permute-start | bytes 196616 | tf_op jit(solution)/shard_map/ppermute | solution.py:602
  12.6 4.4 %collective-permute-start.7 = (f32[32,512]{1,0:T(8,128)S(1)}, f32[32,512]{1,0:T(8,128)S(1)}, u32[]{:S(2)}, u32[]{:S(2)}) collective-permute-start(f32[32,512]{1,0:T(8,128)S(1)} %get-tuple-element.87._lower), channel_id=1, source_target_pairs={{24,21},{25,20}} | collective-permute-start | bytes 196616 | tf_op jit(solution)/shard_map/ppermute | solution.py:440
  13.3 3.8 %collective-permute-start.6 = (f32[32,512]{1,0:T(8,128)S(1)}, f32[32,512]{1,0:T(8,128)S(1)}, u32[]{:S(2)}, u32[]{:S(2)}) collective-permute-start(f32[32,512]{1,0:T(8,128)S(1)} %get-tuple-element.87._lower), channel_id=1, source_target_pairs={{24,20},{25,21}} | collective-permute-start | bytes 196616 | tf_op jit(solution)/shard_map/ppermute | solution.py:602
  15.6 5.7 %collective-permute-start.14 = (f32[1088,256]{1,0:T(8,128)S(1)}, f32[1088,256]{1,0:T(8,128)S(1)}, u32[]{:S(2)}, u32[]{:S(2)}) collective-permute-start(f32[1088,256]{1,0:T(8,128)S(1)} %get-tuple-element.102), channel_id=1, source_target_pairs={{4,8},{5,9},{8,12},{9,13}} | collective-permute-start | bytes 3342344 | tf_op jit(solution)/shard_map/ppermute | solution.py:567
  16.4 5.0 %collective-permute-start.15 = (f32[512,256]{1,0:T(8,128)S(1)}, f32[512,256]{1,0:T(8,128)S(1)}, u32[]{:S(2)}, u32[]{:S(2)}) collective-permute-start(f32[512,256]{1,0:T(8,128)S(1)} %get-tuple-element.103), channel_id=1, source_target_pairs={{4,9},{5,8},{8,13},{9,12}} | collective-permute-start | bytes 1572872 | tf_op jit(solution)/shard_map/ppermute | solution.py:440
  17.1 1.3 %collective-permute-start.9 = (f32[32,512]{1,0:T(8,128)S(1)}, f32[32,512]{1,0:T(8,128)S(1)}, u32[]{:S(2)}, u32[]{:S(2)}) collective-permute-start(f32[32,512]{1,0:T(8,128)S(1)} %get-tuple-element.91._lower), channel_id=1, source_target_pairs={{20,17},{21,16}} | collective-permute-start | bytes 196616 | tf_op jit(solution)/shard_map/ppermute | solution.py:440
  17.8 0.7 %collective-permute-start.8 = (f32[32,512]{1,0:T(8,128)S(1)}, f32[32,512]{1,0:T(8,128)S(1)}, u32[]{:S(2)}, u32[]{:S(2)}) collective-permute-start(f32[32,512]{1,0:T(8,128)S(1)} %get-tuple-element.91._lower), channel_id=1, source_target_pairs={{20,16},{21,17}} | collective-permute-start | bytes 196616 | tf_op jit(solution)/shard_map/ppermute | solution.py:602
  18.6 1.3 %collective-permute-start.11 = (f32[32,512]{1,0:T(8,128)S(1)}, f32[32,512]{1,0:T(8,128)S(1)}, u32[]{:S(2)}, u32[]{:S(2)}) collective-permute-start(f32[32,512]{1,0:T(8,128)S(1)} %get-tuple-element.95._lower), channel_id=1, source_target_pairs={{16,13},{17,12}} | collective-permute-start | bytes 196616 | tf_op jit(solution)/shard_map/ppermute | solution.py:440
  19.2 0.7 %collective-permute-start.10 = (f32[32,512]{1,0:T(8,128)S(1)}, f32[32,512]{1,0:T(8,128)S(1)}, u32[]{:S(2)}, u32[]{:S(2)}) collective-permute-start(f32[32,512]{1,0:T(8,128)S(1)} %get-tuple-element.95._lower), channel_id=1, source_target_pairs={{16,12},{17,13}} | collective-permute-start | bytes 196616 | tf_op jit(solution)/shard_map/ppermute | solution.py:602
  20.0 1.3 %collective-permute-start.13 = (f32[32,512]{1,0:T(8,128)S(1)}, f32[32,512]{1,0:T(8,128)S(1)}, u32[]{:S(2)}, u32[]{:S(2)}) collective-permute-start(f32[32,512]{1,0:T(8,128)S(1)} %get-tuple-element.99.rest_6_.lower), channel_id=1, source_target_pairs={{12,9},{13,8}} | collective-permute-start | bytes 196616 | tf_op jit(solution)/shard_map/ppermute | solution.py:440
  20.7 1.0 %collective-permute-start.12 = (f32[32,512]{1,0:T(8,128)S(1)}, f32[32,512]{1,0:T(8,128)S(1)}, u32[]{:S(2)}, u32[]{:S(2)}) collective-permute-start(f32[32,512]{1,0:T(8,128)S(1)} %get-tuple-element.99.rest_6_.lower), channel_id=1, source_target_pairs={{12,8},{13,9}} | collective-permute-start | bytes 196616 | tf_op jit(solution)/shard_map/ppermute | solution.py:602
  21.7 27.4 %collective-permute-start.16 = (f32[32,896]{1,0:T(8,128)S(1)}, f32[32,896]{1,0:T(8,128)S(1)}, u32[]{:S(2)}, u32[]{:S(2)}) collective-permute-start(f32[32,896]{1,0:T(8,128)S(1)} %get-tuple-element.109), channel_id=1, source_target_pairs={{9,0}} | collective-permute-start | bytes 344072 | tf_op jit(solution)/shard_map/ppermute | solution.py:596
  23.0 26.4 %collective-permute-start.17 = (f32[32,896]{1,0:T(8,128)S(1)}, f32[32,896]{1,0:T(8,128)S(1)}, u32[]{:S(2)}, u32[]{:S(2)}) collective-permute-start(f32[32,896]{1,0:T(8,128)S(1)} %get-tuple-element.110), channel_id=1, source_target_pairs={{8,0},{9,1}} | collective-permute-start | bytes 344072 | tf_op jit(solution)/shard_map/ppermute | solution.py:597
  24.3 25.1 %collective-permute-start.18 = (f32[32,896]{1,0:T(8,128)S(1)}, f32[32,896]{1,0:T(8,128)S(1)}, u32[]{:S(2)}, u32[]{:S(2)}) collective-permute-start(f32[32,896]{1,0:T(8,128)S(1)} %get-tuple-element.111), channel_id=1, source_target_pairs={{8,1}} | collective-permute-start | bytes 344072 | tf_op jit(solution)/shard_map/ppermute | solution.py:598
  25.0 24.4 %collective-permute-start.19 = (f32[32,896]{1,0:T(8,128)S(1)}, f32[32,896]{1,0:T(8,128)S(1)}, u32[]{:S(2)}, u32[]{:S(2)}) collective-permute-start(f32[32,896]{1,0:T(8,128)S(1)} %get-tuple-element.112), channel_id=1, source_target_pairs={{12,5},{13,4}} | collective-permute-start | bytes 344072 | tf_op jit(solution)/shard_map/ppermute | solution.py:440
  25.7 23.7 %collective-permute-start.20 = (f32[32,896]{1,0:T(8,128)S(1)}, f32[32,896]{1,0:T(8,128)S(1)}, u32[]{:S(2)}, u32[]{:S(2)}) collective-permute-start(f32[32,896]{1,0:T(8,128)S(1)} %get-tuple-element.113), channel_id=1, source_target_pairs={{12,4},{13,5}} | collective-permute-start | bytes 344072 | tf_op jit(solution)/shard_map/ppermute | solution.py:614
  49.7 2.2 %collective-permute-start.21 = (f32[32,512]{1,0:T(8,128)S(1)}, f32[32,512]{1,0:T(8,128)S(1)}, u32[]{:S(2)}, u32[]{:S(2)}) collective-permute-start(f32[32,512]{1,0:T(8,128)S(1)} %get-tuple-element.118), channel_id=1, source_target_pairs={{0,2},{1,3},{4,6},{5,7},{8,10},{9,11},{12,14},{13,15},{16,18},{17,... | collective-permute-start | bytes 196616 | tf_op jit(solution)/shard_map/ppermute | solution.py:644

commit v18 on v17

--- a/solution.py
+++ b/solution.py
@@ -118,6 +118,21 @@
         return jnp.concatenate([own[b * window : (b + 1) * window, cut], own[at : at + cols, cut]])
 
     put_rim(sides, rim, columns)
+
+
+def merge_kernel(apart, far_in, rim_in, _far, _rim, _far_high, _far_low, far, rim, far_high, far_low):
+    @pl.when(lax.axis_index("tm") == apart)
+    def _():
+        far[...] = far_in[...]
+        rim[...] = rim_in[...]
+        far_high[...], far_low[...] = halves(far_in[: far_high.shape[0]])
+
+
+def pass_kernel(source, near_in, edges_in, _after, near, edges):
+    @pl.when(lax.axis_index("tm") == source)
+    def _():
+        near[...] = near_in[...]
+        edges[...] = edges_in[...]
 
 
 def split_kernel(far, far_high, far_low):
@@ -523,8 +538,11 @@
         input_output_aliases={0: 0},
         compiler_params=PARAMS,
     )(near, edges)
-    rim = cross(edges, odd[:-1], even[:-1], True)
-    far = lax.ppermute(near, BOTH, link(odd[:-1], even[:-1]))
+    apart = 2 * pairs - 6 if pairs > 3 else None
+    first_odd = [t for t in odd[:-1] if t - 1 != apart]
+    first_even = [t for t in even[:-1] if t != apart]
+    rim = cross(edges, first_odd, first_even, True)
+    far = lax.ppermute(near, BOTH, link(first_odd, first_even))
 
     blank = jnp.zeros((cols, sites), f32)
     upper, lower = pl.pallas_call(
@@ -556,11 +574,31 @@
             out_specs=(VMEM,) * (3 + len(packs)),
             scratch_shapes=[pltpu.VMEM((2 * window, length), f32)],
             compiler_params=PARAMS,
-            cost_estimate=pl.CostEstimate(flops=10**9, bytes_accessed=0, transcendentals=0),
+            cost_estimate=pl.CostEstimate(flops=50 * 10**9 if first else 10**9, bytes_accessed=0, transcendentals=0),
         )(far, rim, far_high, far_low, *mine, const)
 
     late_parts = consts("late", (), (lower,))
     early = pair_matrix(True, False, (), fused(True, (), *late_parts), late_parts[0])
+    if apart is not None:
+        given = (near, edges, lower)
+        near, edges = pl.pallas_call(
+            functools.partial(pass_kernel, apart + 1),
+            out_shape=(shape(near.shape, f32), shape(edges.shape, f32)),
+            in_specs=[VMEM] * 3,
+            out_specs=(VMEM,) * 2,
+            compiler_params=PARAMS,
+        )(*given)
+        far_in = lax.ppermute(near, BOTH, link([apart + 1], [apart]))
+        rim_in = cross(edges, [apart + 1], [apart], True)
+        merged = (far, rim, far_high, far_low)
+        far, rim, far_high, far_low = pl.pallas_call(
+            functools.partial(merge_kernel, apart),
+            out_shape=tuple(shape(v.shape, v.dtype) for v in merged),
+            in_specs=[VMEM] * 6,
+            out_specs=(VMEM,) * 4,
+            input_output_aliases={2 + i: i for i in range(4)},
+            compiler_params=PARAMS,
+        )(far_in, rim_in, *merged)
     high, low, both, *packs = pair_matrix(False, jumps, packs, (near_high, near_low), const)
     if jumps:
         source, target = [2 * jump - 2, 2 * jump], [2 * jump, 2 * jump + 2]

time: 53.3 us -> 53.3 us (level)
  starting transfers between devices: 18 us -> 19.4 us
  waiting for transfers between devices: 27.9 us -> 26.5 us
    ppermute x1, waiting for transfers between devices: 22.7 us -> 21.8 us  [local(): first_in = lax.ppermute(to_next, BOTH, [(2 * source[0] + 1, 2 * target[0])])]
    ppermute x1 -> x2, waiting for transfers between devices: 4.41 us -> 3.65 us  [the longest x1 3.65 us: local(): far = lax.ppermute(near, BOTH, link(first_odd, first_even))]
    ppermute x1 -> x2, starting transfers between devices: 1.29 us -> 2.02 us  [the longest x1 1.29 us: local(): far = lax.ppermute(near, BOTH, link(first_odd, first_even))]
    ppermute x9 -> x10, starting transfers between devices: 6.77 us -> 7.44 us  [cross(): return lax.ppermute(value, BOTH, perm)]
  transfers between devices with their start and end apart: 22 -> 24, of which waited for: 4 -> 4; matrix products, arithmetic and copies ran while one was open for 0% -> 0% of each run, Pallas kernels for 10% -> 10%
where the time goes in v18:
time: 53.3 us; the launch traced here: 52.6 us
  waiting for transfers between devices  26.5 us (50%)
  starting transfers between devices  19.4 us (36%)
  Pallas kernels  5.47 us (10%)
  other arithmetic  0.64 us (1%)
  between operations  0.61 us (1%)
    ppermute x1, waiting for transfers between devices, local(): first_in = lax.ppermute(to_next, BOTH, [(2 * source[0] + 1, 2 * target[0])])  21.8 us
    ppermute x10, starting transfers between devices, cross(): return lax.ppermute(value, BOTH, perm)  7.44 us
    ppermute x1, waiting for transfers between devices, local(): far = lax.ppermute(near, BOTH, link(first_odd, first_even))  3.65 us
    ppermute x5, starting transfers between devices, local(): own_in = lax.ppermute(lower, BOTH, link(source, target))  3.32 us
    pallas_call x2, Pallas kernels, pair_matrix(): pl.pallas_call(functools.partial(pair_kernel, (pairs - 2, first), jumps),...  1.67 us
    pallas_call x3, Pallas kernels, consts(): pl.pallas_call(functools.partial(const_kernel, (which, 2 * pairs - 4)), o...  1.57 us
    ppermute x1, starting transfers between devices, local(): far = lax.ppermute(near, BOTH, link(first_odd, first_even))  1.29 us
    ppermute x1, starting transfers between devices, local(): first_in = lax.ppermute(to_next, BOTH, [(2 * source[0] + 1, 2 * target[0])])  1.29 us
  transfers between devices with their start and end apart: 24, of which 4 were waited for; matrix products, arithmetic and copies ran while one was open for 0% of the time, Pallas kernels for 10%

profile of v18, /device:TPU:0, one launch (start us, length us, event | category | flops | bytes accessed | tf_op | source)
XLA Modules:
  0.0 52.6 jit_solution(8925138010745006546)
XLA Ops:
  0.1 0.0 copy-start
  0.1 0.0 copy-start.1
  0.1 0.8 %collective-permute-start = (f32[1,32,128]{2,1,0:T(8,128)S(1)}, f32[1,32,128]{2,1,0:T(8,128)S(1)}, u32[]{:S(2)}, u32[]{:S(2)}) collective-permute-start(f32[1,32,128]{2,1,0:T(8,128)S(1)} %shard_map.47._after.refs_3_), channel_id=1, source_target_pairs={{30,29},{31,28}} | collective-permute-start | bytes 49160 | tf_op jit(solution)/shard_map/ppermute | solution.py:455
  0.9 0.7 %collective-permute-start.1 = (f32[32,512]{1,0:T(8,128)S(1)}, f32[32,512]{1,0:T(8,128)S(1)}, u32[]{:S(2)}, u32[]{:S(2)}) collective-permute-start(f32[32,512]{1,0:T(8,128)S(1)} %shard_map.48.refs_4_), channel_id=1, source_target_pairs={{30,28},{31,29}} | collective-permute-start | bytes 196616 | tf_op jit(solution)/shard_map/ppermute | solution.py:509
  1.6 1.5 %shard_map.49 = (f32[32,512]{1,0:T(8,128)S(1)}, bf16[2,256,256]{2,1,0:T(8,128)(2,1)S(1)}, bf16[2,256,256]{2,1,0:T(8,128)(2,1)S(1)}) custom-call(f32[1,32,512]{2,1,0:T(8,128)} %normals.5, f32[1,2,256,256]{3,2,1,0:T(8,128)} %inv.5, f32[32,512]{1,0:T(8,128)S(1)} %get-tuple-element.68.const.refs_0_, ...), custom_call_target="tpu_custom_call", output_to_operand_aliasing={{0}: (2, {}), {1}: (3, {}), {2}: (4, {})} | custom-call | tf_op jit(solution)/shard_map/pallas_call | solution.py:472
  3.1 0.7 %shard_map.50 = (bf16[1024,256]{1,0:T(8,128)(2,1)S(1)}, bf16[1024,256]{1,0:T(8,128)(2,1)S(1)}, f32[1088,256]{1,0:T(8,128)S(1)}) custom-call(s32[1,2,3]{2,1,0:T(2,128)S(1)} %copy-done.1, f32[32,512]{1,0:T(8,128)S(1)} %get-tuple-element.71.refs_1_.const.refs_6_, bf16[2,256,256]{2,1,0:T(8,128)(2,1)S(1)} %get-tuple-element.72.refs_2_, ...), custom_call_target="tpu_custom_call" | custom-call | flops 10695475200 | tf_op jit(solution)/shard_map/pallas_call | solution.py:514
  3.8 1.3 %collective-permute-start.5 = (f32[1,544,128]{2,1,0:T(8,128)S(1)}, f32[1,544,128]{2,1,0:T(8,128)S(1)}, u32[]{:S(2)}, u32[]{:S(2)}) collective-permute-start(f32[1,544,128]{2,1,0:T(8,128)S(1)} %shard_map.51._edges.edges_in), channel_id=1, source_target_pairs={{2,1},{3,0},{6,5},{7,4},{10,9},{11,8},{14,13},{15,12},{18,17},{19,... | collective-permute-start | bytes 835592 | tf_op jit(solution)/shard_map/ppermute | solution.py:455
  5.2 1.3 %collective-permute-start.4 = (f32[1088,256]{1,0:T(8,128)S(1)}, f32[1088,256]{1,0:T(8,128)S(1)}, u32[]{:S(2)}, u32[]{:S(2)}) collective-permute-start(f32[1088,256]{1,0:T(8,128)S(1)} %shard_map.52.near_in), channel_id=1, source_target_pairs={{2,0},{3,1},{6,4},{7,5},{10,8},{11,9},{14,12},{15,13},{18,16},{19,... | collective-permute-start | bytes 3342344 | tf_op jit(solution)/shard_map/ppermute | solution.py:545
  6.5 0.0 collective-permute-done.next_in
  6.5 0.7 %collective-permute-start.7 = (f32[32,512]{1,0:T(8,128)S(1)}, f32[32,512]{1,0:T(8,128)S(1)}, u32[]{:S(2)}, u32[]{:S(2)}) collective-permute-start(f32[32,512]{1,0:T(8,128)S(1)} %get-tuple-element.77._after.refs_0_._lower), channel_id=1, source_target_pairs={{28,25},{29,24}} | collective-permute-start | bytes 196616 | tf_op jit(solution)/shard_map/ppermute | solution.py:455
  7.2 0.7 %collective-permute-start.6 = (f32[32,512]{1,0:T(8,128)S(1)}, f32[32,512]{1,0:T(8,128)S(1)}, u32[]{:S(2)}, u32[]{:S(2)}) collective-permute-start(f32[32,512]{1,0:T(8,128)S(1)} %get-tuple-element.77._after.refs_0_._lower), channel_id=1, source_target_pairs={{28,24},{29,25}} | collective-permute-start | bytes 196616 | tf_op jit(solution)/shard_map/ppermute | solution.py:640
  7.9 0.7 %collective-permute-start.2 = (f32[1088,256]{1,0:T(8,128)S(1)}, f32[1088,256]{1,0:T(8,128)S(1)}, u32[]{:S(2)}, u32[]{:S(2)}) collective-permute-start(f32[1088,256]{1,0:T(8,128)S(1)} %get-tuple-element.78), channel_id=1, source_target_pairs={{22,20},{23,21}} | collective-permute-start | bytes 3342344 | tf_op jit(solution)/shard_map/ppermute | solution.py:591
  8.7 3.6 %collective-permute-done.4.far._far.refs_0_ = f32[1088,256]{1,0:T(8,128)S(1)} collective-permute-done((f32[1088,256]{1,0:T(8,128)S(1)}, f32[1088,256]{1,0:T(8,128)S(1)}, u32[]{:S(2)}, u32[]{:S(2)}) %collective-permute-start.4) | collective-permute-done | bytes 1114144 | tf_op jit(solution)/shard_map/ppermute | solution.py:545
  12.4 0.7 %collective-permute-start.3 = (f32[1,544,128]{2,1,0:T(8,128)S(1)}, f32[1,544,128]{2,1,0:T(8,128)S(1)}, u32[]{:S(2)}, u32[]{:S(2)}) collective-permute-start(f32[1,544,128]{2,1,0:T(8,128)S(1)} %get-tuple-element.79), channel_id=1, source_target_pairs={{22,21},{23,20}} | collective-permute-start | bytes 835592 | tf_op jit(solution)/shard_map/ppermute | solution.py:455
  13.0 0.1 shard_map.55
  13.2 0.0 collective-permute-done.5._rim.refs_1_
  13.3 0.7 %collective-permute-start.9 = (f32[32,512]{1,0:T(8,128)S(1)}, f32[32,512]{1,0:T(8,128)S(1)}, u32[]{:S(2)}, u32[]{:S(2)}) collective-permute-start(f32[32,512]{1,0:T(8,128)S(1)} %get-tuple-element.99._lower), channel_id=1, source_target_pairs={{24,21},{25,20}} | collective-permute-start | bytes 196616 | tf_op jit(solution)/shard_map/ppermute | solution.py:455
  14.0 0.7 %collective-permute-start.8 = (f32[32,512]{1,0:T(8,128)S(1)}, f32[32,512]{1,0:T(8,128)S(1)}, u32[]{:S(2)}, u32[]{:S(2)}) collective-permute-start(f32[32,512]{1,0:T(8,128)S(1)} %get-tuple-element.99._lower), channel_id=1, source_target_pairs={{24,20},{25,21}} | collective-permute-start | bytes 196616 | tf_op jit(solution)/shard_map/ppermute | solution.py:640
  14.7 0.0 collective-permute-done.3.rim_in
  14.7 0.0 collective-permute-done.2.far_in
  14.7 1.6 %shard_map.57 = (bf16[2048,256]{1,0:T(8,128)(2,1)S(1)}, bf16[2048,256]{1,0:T(8,128)(2,1)S(1)}, f32[32,512]{1,0:T(8,128)S(1)}, f32[1088,256]{1,0:T(8,128)S(1)}, f32[512,256]{1,0:T(8,128)S(1)}) custom-call(f32[1088,256]{1,0:T(8,128)S(1)} %get-tuple-element.82.refs_0_.rest_5_, f32[1,544,128]{2,1,0:T(8,128)S(1)} %get-tuple-element.83.refs_1_, ...), custom_call_target="tpu_custom_call" | custom-call | flops 1000000000 | tf_op jit(solution)/shard_map/pallas_call | solution.py:568
  16.4 0.7 %collective-permute-start.16 = (f32[1088,256]{1,0:T(8,128)S(1)}, f32[1088,256]{1,0:T(8,128)S(1)}, u32[]{:S(2)}, u32[]{:S(2)}) collective-permute-start(f32[1088,256]{1,0:T(8,128)S(1)} %get-tuple-element.114), channel_id=1, source_target_pairs={{4,8},{5,9},{8,12},{9,13}} | collective-permute-start | bytes 3342344 | tf_op jit(solution)/shard_map/ppermute | solution.py:605
  17.1 0.7 %collective-permute-start.17 = (f32[512,256]{1,0:T(8,128)S(1)}, f32[512,256]{1,0:T(8,128)S(1)}, u32[]{:S(2)}, u32[]{:S(2)}) collective-permute-start(f32[512,256]{1,0:T(8,128)S(1)} %get-tuple-element.115), channel_id=1, source_target_pairs={{4,9},{5,8},{8,13},{9,12}} | collective-permute-start | bytes 1572872 | tf_op jit(solution)/shard_map/ppermute | solution.py:455
  17.8 0.0 collective-permute-done.9.next_in
  17.9 0.7 %collective-permute-start.11 = (f32[32,512]{1,0:T(8,128)S(1)}, f32[32,512]{1,0:T(8,128)S(1)}, u32[]{:S(2)}, u32[]{:S(2)}) collective-permute-start(f32[32,512]{1,0:T(8,128)S(1)} %get-tuple-element.103._lower), channel_id=1, source_target_pairs={{20,17},{21,16}} | collective-permute-start | bytes 196616 | tf_op jit(solution)/shard_map/ppermute | solution.py:455
  18.5 0.7 %collective-permute-start.10 = (f32[32,512]{1,0:T(8,128)S(1)}, f32[32,512]{1,0:T(8,128)S(1)}, u32[]{:S(2)}, u32[]{:S(2)}) collective-permute-start(f32[32,512]{1,0:T(8,128)S(1)} %get-tuple-element.103._lower), channel_id=1, source_target_pairs={{20,16},{21,17}} | collective-permute-start | bytes 196616 | tf_op jit(solution)/shard_map/ppermute | solution.py:640
  19.3 0.0 collective-permute-done.10.own_in
  19.3 0.7 %collective-permute-start.13 = (f32[32,512]{1,0:T(8,128)S(1)}, f32[32,512]{1,0:T(8,128)S(1)}, u32[]{:S(2)}, u32[]{:S(2)}) collective-permute-start(f32[32,512]{1,0:T(8,128)S(1)} %get-tuple-element.107._lower), channel_id=1, source_target_pairs={{16,13},{17,12}} | collective-permute-start | bytes 196616 | tf_op jit(solution)/shard_map/ppermute | solution.py:455
  20.0 0.7 %collective-permute-start.12 = (f32[32,512]{1,0:T(8,128)S(1)}, f32[32,512]{1,0:T(8,128)S(1)}, u32[]{:S(2)}, u32[]{:S(2)}) collective-permute-start(f32[32,512]{1,0:T(8,128)S(1)} %get-tuple-element.107._lower), channel_id=1, source_target_pairs={{16,12},{17,13}} | collective-permute-start | bytes 196616 | tf_op jit(solution)/shard_map/ppermute | solution.py:640
  20.6 0.0 collective-permute-done.13.next_in
  20.7 0.7 %collective-permute-start.15 = (f32[32,512]{1,0:T(8,128)S(1)}, f32[32,512]{1,0:T(8,128)S(1)}, u32[]{:S(2)}, u32[]{:S(2)}) collective-permute-start(f32[32,512]{1,0:T(8,128)S(1)} %get-tuple-element.111.rest_6_.lower), channel_id=1, source_target_pairs={{12,9},{13,8}} | collective-permute-start | bytes 196616 | tf_op jit(solution)/shard_map/ppermute | solution.py:455
  21.4 0.7 %collective-permute-start.14 = (f32[32,512]{1,0:T(8,128)S(1)}, f32[32,512]{1,0:T(8,128)S(1)}, u32[]{:S(2)}, u32[]{:S(2)}) collective-permute-start(f32[32,512]{1,0:T(8,128)S(1)} %get-tuple-element.111.rest_6_.lower), channel_id=1, source_target_pairs={{12,8},{13,9}} | collective-permute-start | bytes 196616 | tf_op jit(solution)/shard_map/ppermute | solution.py:640
  22.1 0.0 collective-permute-done.15.next_in
  22.1 0.0 collective-permute-done.17.other_rows
  22.1 0.0 collective-permute-done.16.own_rows.rest_0_
  22.1 0.2 shard_map.70
  22.5 1.3 %collective-permute-start.18 = (f32[32,896]{1,0:T(8,128)S(1)}, f32[32,896]{1,0:T(8,128)S(1)}, u32[]{:S(2)}, u32[]{:S(2)}) collective-permute-start(f32[32,896]{1,0:T(8,128)S(1)} %get-tuple-element.121), channel_id=1, source_target_pairs={{9,0}} | collective-permute-start | bytes 344072 | tf_op jit(solution)/shard_map/ppermute | solution.py:634
  23.8 1.3 %collective-permute-start.19 = (f32[32,896]{1,0:T(8,128)S(1)}, f32[32,896]{1,0:T(8,128)S(1)}, u32[]{:S(2)}, u32[]{:S(2)}) collective-permute-start(f32[32,896]{1,0:T(8,128)S(1)} %get-tuple-element.122), channel_id=1, source_target_pairs={{8,0},{9,1}} | collective-permute-start | bytes 344072 | tf_op jit(solution)/shard_map/ppermute | solution.py:635
  25.1 0.7 %collective-permute-start.20 = (f32[32,896]{1,0:T(8,128)S(1)}, f32[32,896]{1,0:T(8,128)S(1)}, u32[]{:S(2)}, u32[]{:S(2)}) collective-permute-start(f32[32,896]{1,0:T(8,128)S(1)} %get-tuple-element.123), channel_id=1, source_target_pairs={{8,1}} | collective-permute-start | bytes 344072 | tf_op jit(solution)/shard_map/ppermute | solution.py:636
  25.7 0.7 %collective-permute-start.21 = (f32[32,896]{1,0:T(8,128)S(1)}, f32[32,896]{1,0:T(8,128)S(1)}, u32[]{:S(2)}, u32[]{:S(2)}) collective-permute-start(f32[32,896]{1,0:T(8,128)S(1)} %get-tuple-element.124), channel_id=1, source_target_pairs={{12,5},{13,4}} | collective-permute-start | bytes 344072 | tf_op jit(solution)/shard_map/ppermute | solution.py:455
  26.4 0.7 %collective-permute-start.22 = (f32[32,896]{1,0:T(8,128)S(1)}, f32[32,896]{1,0:T(8,128)S(1)}, u32[]{:S(2)}, u32[]{:S(2)}) collective-permute-start(f32[32,896]{1,0:T(8,128)S(1)} %get-tuple-element.125), channel_id=1, source_target_pairs={{12,4},{13,5}} | collective-permute-start | bytes 344072 | tf_op jit(solution)/shard_map/ppermute | solution.py:652
  27.1 21.8 %collective-permute-done.18.rest_0_ = f32[32,896]{1,0:T(8,128)S(1)} collective-permute-done((f32[32,896]{1,0:T(8,128)S(1)}, f32[32,896]{1,0:T(8,128)S(1)}, u32[]{:S(2)}, u32[]{:S(2)}) %collective-permute-start.18) | collective-permute-done | bytes 114720 | tf_op jit(solution)/shard_map/ppermute | solution.py:634
  48.8 0.6 %collective-permute-done.19.rest_1_ = f32[32,896]{1,0:T(8,128)S(1)} collective-permute-done((f32[32,896]{1,0:T(8,128)S(1)}, f32[32,896]{1,0:T(8,128)S(1)}, u32[]{:S(2)}, u32[]{:S(2)}) %collective-permute-start.19) | collective-permute-done | bytes 114720 | tf_op jit(solution)/shard_map/ppermute | solution.py:635
  49.5 0.3 shard_map.73
  49.8 1.3 %collective-permute-start.23 = (f32[32,512]{1,0:T(8,128)S(1)}, f32[32,512]{1,0:T(8,128)S(1)}, u32[]{:S(2)}, u32[]{:S(2)}) collective-permute-start(f32[32,512]{1,0:T(8,128)S(1)} %get-tuple-element.130), channel_id=1, source_target_pairs={{0,2},{1,3},{4,6},{5,7},{8,10},{9,11},{12,14},{13,15},{16,18},{17,... | collective-permute-start | bytes 196616 | tf_op jit(solution)/shard_map/ppermute | solution.py:682
  51.1 0.5 shard_map.74
  51.6 0.4 collective-permute-done.23
  52.0 0.6 %select_bitcast_fusion = f32[1,32,512]{2,1,0:T(8,128)} fusion(f32[32,512]{1,0:T(8,128)S(1)} %shard_map.74, f32[32,512]{1,0:T(8,128)S(1)} %collective-permute-done.23, pred[]{:T(512)S(6)} %eq.5), kind=kLoop, calls=%fused_computation | loop fusion | flops 16384 | bytes 196609 | tf_op jit(solution)/shard_map/broadcast_in_dim | solution.py:692
  (37 shorter events, 0.5 us)
Async XLA Ops:
  0.1 3.0 %copy-start = (f32[1,2,512,256]{3,2,1,0:T(8,128)S(1)}, f32[1,2,512,256]{3,2,1,0:T(8,128)}, u32[]{:S(2)}) copy-start(f32[1,2,512,256]{3,2,1,0:T(8,128)} %refs_4_.3) | copy-start | bytes 3145732
  0.1 3.0 %copy-start.1 = (s32[1,2,3]{2,1,0:T(2,128)S(1)}, s32[1,2,3]{2,1,0:T(2,128)}, u32[]{:S(2)}) copy-start(s32[1,2,3]{2,1,0:T(2,128)} %refs_0_.3) | copy-start | bytes 76
  0.1 6.4 %collective-permute-start = (f32[1,32,128]{2,1,0:T(8,128)S(1)}, f32[1,32,128]{2,1,0:T(8,128)S(1)}, u32[]{:S(2)}, u32[]{:S(2)}) collective-permute-start(f32[1,32,128]{2,1,0:T(8,128)S(1)} %shard_map.47._after.refs_3_), channel_id=1, source_target_pairs={{30,29},{31,28}} | collective-permute-start | bytes 49160 | tf_op jit(solution)/shard_map/ppermute | solution.py:455
  0.9 5.6 %collective-permute-start.1 = (f32[32,512]{1,0:T(8,128)S(1)}, f32[32,512]{1,0:T(8,128)S(1)}, u32[]{:S(2)}, u32[]{:S(2)}) collective-permute-start(f32[32,512]{1,0:T(8,128)S(1)} %shard_map.48.refs_4_), channel_id=1, source_target_pairs={{30,28},{31,29}} | collective-permute-start | bytes 196616 | tf_op jit(solution)/shard_map/ppermute | solution.py:509
  3.8 9.3 %collective-permute-start.5 = (f32[1,544,128]{2,1,0:T(8,128)S(1)}, f32[1,544,128]{2,1,0:T(8,128)S(1)}, u32[]{:S(2)}, u32[]{:S(2)}) collective-permute-start(f32[1,544,128]{2,1,0:T(8,128)S(1)} %shard_map.51._edges.edges_in), channel_id=1, source_target_pairs={{2,1},{3,0},{6,5},{7,4},{10,9},{11,8},{14,13},{15,12},{18,17},{19,... | collective-permute-start | bytes 835592 | tf_op jit(solution)/shard_map/ppermute | solution.py:455
  5.2 7.2 %collective-permute-start.4 = (f32[1088,256]{1,0:T(8,128)S(1)}, f32[1088,256]{1,0:T(8,128)S(1)}, u32[]{:S(2)}, u32[]{:S(2)}) collective-permute-start(f32[1088,256]{1,0:T(8,128)S(1)} %shard_map.52.near_in), channel_id=1, source_target_pairs={{2,0},{3,1},{6,4},{7,5},{10,8},{11,9},{14,12},{15,13},{18,16},{19,... | collective-permute-start | bytes 3342344 | tf_op jit(solution)/shard_map/ppermute | solution.py:545
  6.5 6.7 %collective-permute-start.7 = (f32[32,512]{1,0:T(8,128)S(1)}, f32[32,512]{1,0:T(8,128)S(1)}, u32[]{:S(2)}, u32[]{:S(2)}) collective-permute-start(f32[32,512]{1,0:T(8,128)S(1)} %get-tuple-element.77._after.refs_0_._lower), channel_id=1, source_target_pairs={{28,25},{29,24}} | collective-permute-start | bytes 196616 | tf_op jit(solution)/shard_map/ppermute | solution.py:455
  7.2 6.1 %collective-permute-start.6 = (f32[32,512]{1,0:T(8,128)S(1)}, f32[32,512]{1,0:T(8,128)S(1)}, u32[]{:S(2)}, u32[]{:S(2)}) collective-permute-start(f32[32,512]{1,0:T(8,128)S(1)} %get-tuple-element.77._after.refs_0_._lower), channel_id=1, source_target_pairs={{28,24},{29,25}} | collective-permute-start | bytes 196616 | tf_op jit(solution)/shard_map/ppermute | solution.py:640
  7.9 6.8 %collective-permute-start.2 = (f32[1088,256]{1,0:T(8,128)S(1)}, f32[1088,256]{1,0:T(8,128)S(1)}, u32[]{:S(2)}, u32[]{:S(2)}) collective-permute-start(f32[1088,256]{1,0:T(8,128)S(1)} %get-tuple-element.78), channel_id=1, source_target_pairs={{22,20},{23,21}} | collective-permute-start | bytes 3342344 | tf_op jit(solution)/shard_map/ppermute | solution.py:591
  12.4 2.3 %collective-permute-start.3 = (f32[1,544,128]{2,1,0:T(8,128)S(1)}, f32[1,544,128]{2,1,0:T(8,128)S(1)}, u32[]{:S(2)}, u32[]{:S(2)}) collective-permute-start(f32[1,544,128]{2,1,0:T(8,128)S(1)} %get-tuple-element.79), channel_id=1, source_target_pairs={{22,21},{23,20}} | collective-permute-start | bytes 835592 | tf_op jit(solution)/shard_map/ppermute | solution.py:455
  13.3 4.5 %collective-permute-start.9 = (f32[32,512]{1,0:T(8,128)S(1)}, f32[32,512]{1,0:T(8,128)S(1)}, u32[]{:S(2)}, u32[]{:S(2)}) collective-permute-start(f32[32,512]{1,0:T(8,128)S(1)} %get-tuple-element.99._lower), channel_id=1, source_target_pairs={{24,21},{25,20}} | collective-permute-start | bytes 196616 | tf_op jit(solution)/shard_map/ppermute | solution.py:455
  14.0 3.9 %collective-permute-start.8 = (f32[32,512]{1,0:T(8,128)S(1)}, f32[32,512]{1,0:T(8,128)S(1)}, u32[]{:S(2)}, u32[]{:S(2)}) collective-permute-start(f32[32,512]{1,0:T(8,128)S(1)} %get-tuple-element.99._lower), channel_id=1, source_target_pairs={{24,20},{25,21}} | collective-permute-start | bytes 196616 | tf_op jit(solution)/shard_map/ppermute | solution.py:640
  16.4 5.7 %collective-permute-start.16 = (f32[1088,256]{1,0:T(8,128)S(1)}, f32[1088,256]{1,0:T(8,128)S(1)}, u32[]{:S(2)}, u32[]{:S(2)}) collective-permute-start(f32[1088,256]{1,0:T(8,128)S(1)} %get-tuple-element.114), channel_id=1, source_target_pairs={{4,8},{5,9},{8,12},{9,13}} | collective-permute-start | bytes 3342344 | tf_op jit(solution)/shard_map/ppermute | solution.py:605
  17.1 5.0 %collective-permute-start.17 = (f32[512,256]{1,0:T(8,128)S(1)}, f32[512,256]{1,0:T(8,128)S(1)}, u32[]{:S(2)}, u32[]{:S(2)}) collective-permute-start(f32[512,256]{1,0:T(8,128)S(1)} %get-tuple-element.115), channel_id=1, source_target_pairs={{4,9},{5,8},{8,13},{9,12}} | collective-permute-start | bytes 1572872 | tf_op jit(solution)/shard_map/ppermute | solution.py:455
  17.9 1.3 %collective-permute-start.11 = (f32[32,512]{1,0:T(8,128)S(1)}, f32[32,512]{1,0:T(8,128)S(1)}, u32[]{:S(2)}, u32[]{:S(2)}) collective-permute-start(f32[32,512]{1,0:T(8,128)S(1)} %get-tuple-element.103._lower), channel_id=1, source_target_pairs={{20,17},{21,16}} | collective-permute-start | bytes 196616 | tf_op jit(solution)/shard_map/ppermute | solution.py:455
  18.5 0.7 %collective-permute-start.10 = (f32[32,512]{1,0:T(8,128)S(1)}, f32[32,512]{1,0:T(8,128)S(1)}, u32[]{:S(2)}, u32[]{:S(2)}) collective-permute-start(f32[32,512]{1,0:T(8,128)S(1)} %get-tuple-element.103._lower), channel_id=1, source_target_pairs={{20,16},{21,17}} | collective-permute-start | bytes 196616 | tf_op jit(solution)/shard_map/ppermute | solution.py:640
  19.3 1.3 %collective-permute-start.13 = (f32[32,512]{1,0:T(8,128)S(1)}, f32[32,512]{1,0:T(8,128)S(1)}, u32[]{:S(2)}, u32[]{:S(2)}) collective-permute-start(f32[32,512]{1,0:T(8,128)S(1)} %get-tuple-element.107._lower), channel_id=1, source_target_pairs={{16,13},{17,12}} | collective-permute-start | bytes 196616 | tf_op jit(solution)/shard_map/ppermute | solution.py:455
  20.0 0.7 %collective-permute-start.12 = (f32[32,512]{1,0:T(8,128)S(1)}, f32[32,512]{1,0:T(8,128)S(1)}, u32[]{:S(2)}, u32[]{:S(2)}) collective-permute-start(f32[32,512]{1,0:T(8,128)S(1)} %get-tuple-element.107._lower), channel_id=1, source_target_pairs={{16,12},{17,13}} | collective-permute-start | bytes 196616 | tf_op jit(solution)/shard_map/ppermute | solution.py:640
  20.7 1.3 %collective-permute-start.15 = (f32[32,512]{1,0:T(8,128)S(1)}, f32[32,512]{1,0:T(8,128)S(1)}, u32[]{:S(2)}, u32[]{:S(2)}) collective-permute-start(f32[32,512]{1,0:T(8,128)S(1)} %get-tuple-element.111.rest_6_.lower), channel_id=1, source_target_pairs={{12,9},{13,8}} | collective-permute-start | bytes 196616 | tf_op jit(solution)/shard_map/ppermute | solution.py:455
  21.4 1.0 %collective-permute-start.14 = (f32[32,512]{1,0:T(8,128)S(1)}, f32[32,512]{1,0:T(8,128)S(1)}, u32[]{:S(2)}, u32[]{:S(2)}) collective-permute-start(f32[32,512]{1,0:T(8,128)S(1)} %get-tuple-element.111.rest_6_.lower), channel_id=1, source_target_pairs={{12,8},{13,9}} | collective-permute-start | bytes 196616 | tf_op jit(solution)/shard_map/ppermute | solution.py:640
  22.5 26.4 %collective-permute-start.18 = (f32[32,896]{1,0:T(8,128)S(1)}, f32[32,896]{1,0:T(8,128)S(1)}, u32[]{:S(2)}, u32[]{:S(2)}) collective-permute-start(f32[32,896]{1,0:T(8,128)S(1)} %get-tuple-element.121), channel_id=1, source_target_pairs={{9,0}} | collective-permute-start | bytes 344072 | tf_op jit(solution)/shard_map/ppermute | solution.py:634
  23.8 25.7 %collective-permute-start.19 = (f32[32,896]{1,0:T(8,128)S(1)}, f32[32,896]{1,0:T(8,128)S(1)}, u32[]{:S(2)}, u32[]{:S(2)}) collective-permute-start(f32[32,896]{1,0:T(8,128)S(1)} %get-tuple-element.122), channel_id=1, source_target_pairs={{8,0},{9,1}} | collective-permute-start | bytes 344072 | tf_op jit(solution)/shard_map/ppermute | solution.py:635
  25.1 24.4 %collective-permute-start.20 = (f32[32,896]{1,0:T(8,128)S(1)}, f32[32,896]{1,0:T(8,128)S(1)}, u32[]{:S(2)}, u32[]{:S(2)}) collective-permute-start(f32[32,896]{1,0:T(8,128)S(1)} %get-tuple-element.123), channel_id=1, source_target_pairs={{8,1}} | collective-permute-start | bytes 344072 | tf_op jit(solution)/shard_map/ppermute | solution.py:636
  25.7 23.7 %collective-permute-start.21 = (f32[32,896]{1,0:T(8,128)S(1)}, f32[32,896]{1,0:T(8,128)S(1)}, u32[]{:S(2)}, u32[]{:S(2)}) collective-permute-start(f32[32,896]{1,0:T(8,128)S(1)} %get-tuple-element.124), channel_id=1, source_target_pairs={{12,5},{13,4}} | collective-permute-start | bytes 344072 | tf_op jit(solution)/shard_map/ppermute | solution.py:455
  26.4 23.0 %collective-permute-start.22 = (f32[32,896]{1,0:T(8,128)S(1)}, f32[32,896]{1,0:T(8,128)S(1)}, u32[]{:S(2)}, u32[]{:S(2)}) collective-permute-start(f32[32,896]{1,0:T(8,128)S(1)} %get-tuple-element.125), channel_id=1, source_target_pairs={{12,4},{13,5}} | collective-permute-start | bytes 344072 | tf_op jit(solution)/shard_map/ppermute | solution.py:652
  49.8 2.2 %collective-permute-start.23 = (f32[32,512]{1,0:T(8,128)S(1)}, f32[32,512]{1,0:T(8,128)S(1)}, u32[]{:S(2)}, u32[]{:S(2)}) collective-permute-start(f32[32,512]{1,0:T(8,128)S(1)} %get-tuple-element.130), channel_id=1, source_target_pairs={{0,2},{1,3},{4,6},{5,7},{8,10},{9,11},{12,14},{13,15},{16,18},{17,... | collective-permute-start | bytes 196616 | tf_op jit(solution)/shard_map/ppermute | solution.py:682

commit v19 on v15

--- a/solution.py
+++ b/solution.py
@@ -222,7 +222,8 @@
     return lambda side, cut: next_in[:, cut] if len(next_in.shape) == 2 else next_in[side, :, cut]
 
 
-def top_kernel(mine, sides, next_in, own_in, const, near_high, near_low, _upper, _lower, upper, lower, mid):
+def top_kernel(mine, sides, next_in, own_in, const, near_high, near_low, _upper, _lower, upper, lower, *rest):
+    mid = rest[-1]
     sites = lower.shape[1]
     length = near_high.shape[1]
     blocks = sites // length
@@ -238,6 +239,10 @@
             at, rows = slice(b * length, (b + 1) * length), slice(b * window, (b + 1) * window)
             product = stacked_dot(mid, slice(b * length, b * length + window), near_high[rows], near_low[rows])
             lower[:, at] = const[:, at] - product
+        if len(rest) > 1:
+            halo = rest[0].shape[1]
+            start = pl.multiple_of(jnp.where(lax.axis_index("row") == 0, sites - halo, 0), 128)
+            rest[0][...] = lower[:, pl.ds(start, halo)]
 
 
 def step(both, high, low, late, lower):
@@ -251,8 +256,11 @@
 def load_rims(sides, next_in, sites, halo, late):
     for side in range(sides):
         on_right = 1 - jnp.minimum(lax.axis_index("row"), 1).astype(jnp.int32) if sides == 1 else side
-        start = pl.multiple_of((1 - on_right) * (sites - halo), 128)
-        keep(late, pl.multiple_of(on_right * (halo + sites), 128), plain(next_in)(side, pl.ds(start, halo)))
+        if next_in.shape[-1] == halo:
+            value = next_in[...]
+        else:
+            value = plain(next_in)(side, pl.ds(pl.multiple_of((1 - on_right) * (sites - halo), 128), halo))
+        keep(late, pl.multiple_of(on_right * (halo + sites), 128), value)
 
 
 def rim_kernel(mine, sides, next_in, both, high, low, _late, late, base):
@@ -298,8 +306,14 @@
         lower[:, at] = base[:, at] + stacked_dot(late, slice(halo, halo + sites), high[rows], low[rows])
 
 
-def chain_kernel(mine, own_in, base, high, low, _late, _lower, late, lower):
-    pl.when(lax.axis_index("tm") == 2 * mine)(lambda: add_own(own_in, base, high, low, late, lower))
+def chain_kernel(mine, own_in, base, high, low, _late, _lower, late, lower, near=None):
+    @pl.when(lax.axis_index("tm") == 2 * mine)
+    def _():
+        add_own(own_in, base, high, low, late, lower)
+        if near is not None:
+            sites, halo = lower.shape[1], near.shape[1]
+            start = pl.multiple_of(jnp.where(lax.axis_index("row") == 0, sites - halo, 0), 128)
+            near[...] = lower[:, pl.ds(start, halo)]
 
 
 def rows_kernel(own_rows, other_rows, own_high, own_low, other_high, other_low):
@@ -499,11 +513,12 @@
     far = lax.ppermute(near, BOTH, link(odd[:-1], even[:-1]))
 
     blank = jnp.zeros((cols, sites), f32)
-    upper, lower = pl.pallas_call(
+    near_shape = (shape((cols, halo), f32),) if sides == 1 else ()
+    upper, lower, *near = pl.pallas_call(
         functools.partial(top_kernel, pairs - 1, sides),
-        out_shape=(shape((cols, sites), f32),) * 2,
+        out_shape=(shape((cols, sites), f32),) * 2 + near_shape,
         in_specs=[VMEM] * 7,
-        out_specs=(VMEM,) * 2,
+        out_specs=(VMEM,) * (2 + len(near_shape)),
         scratch_shapes=[pltpu.VMEM((2 * cols, sites + 2 * edge), bf16)],
         input_output_aliases={5: 0, 6: 1},
         compiler_params=PARAMS,
@@ -569,7 +584,7 @@
             next_in = lax.ppermute(to_last, BOTH, [(2 * source[0], 2 * target[0] + 1)])
             break
         source, target = [2 * mine], [2 * mine - 2]
-        next_in = cross(lower, source, target)
+        next_in = cross(near[0] if near else lower, source, target)
         own_in = lax.ppermute(lower, BOTH, link(source, target))
         if jumps and mine == jump + 1:
             beside = pl.pallas_call(
@@ -602,10 +617,11 @@
                 parts + parts[:1],
             )
         else:
-            late, lower = turn(
+            late, lower, *near = turn(
                 functools.partial(chain_kernel, mine),
                 (own_in, base, *here[:2]),
                 (late, lower),
+                extra=[shape((cols, halo), f32)] if sides == 1 and mine == pairs - 2 else [],
                 flops=50 * 10**9 if jumps and mine == pairs - 3 else 0,
             )
     given = (first_in, own_in, next_in, beside_next, beside_own) if jumps else (own_in, next_in)

time: 53.2 us -> 53.2 us (level)
  no operation moved by 1% of the time
where the time goes in v19:
time: 53.2 us; the launch traced here: 52.5 us
  waiting for transfers between devices  28 us (53%)
  starting transfers between devices  18 us (34%)
  Pallas kernels  5.36 us (10%)
  other arithmetic  0.64 us (1%)
    ppermute x1, waiting for transfers between devices, local(): first_in = lax.ppermute(to_next, BOTH, [(2 * source[0] + 1, 2 * target[0])])  22.8 us
    ppermute x9, starting transfers between devices, cross(): return lax.ppermute(value, BOTH, perm)  6.77 us
    ppermute x1, waiting for transfers between devices, local(): far = lax.ppermute(near, BOTH, link(odd[:-1], even[:-1]))  4.46 us
    ppermute x5, starting transfers between devices, local(): own_in = lax.ppermute(lower, BOTH, link(source, target))  3.32 us
    pallas_call x2, Pallas kernels, pair_matrix(): pl.pallas_call(functools.partial(pair_kernel, (pairs - 2, first), jumps),...  1.69 us
    pallas_call x1, Pallas kernels, local(): pl.pallas_call(const_kernel, out_shape=(shape((cols, sites), f32), shape(...  1.48 us
    ppermute x1, starting transfers between devices, local(): far = lax.ppermute(near, BOTH, link(odd[:-1], even[:-1]))  1.29 us
    ppermute x1, starting transfers between devices, local(): first_in = lax.ppermute(to_next, BOTH, [(2 * source[0] + 1, 2 * target[0])])  1.29 us
  transfers between devices with their start and end apart: 22, of which 4 were waited for; matrix products, arithmetic and copies ran while one was open for 0% of the time, Pallas kernels for 7%

profile of v19, /device:TPU:0, one launch (start us, length us, event | category | flops | bytes accessed | tf_op | source)
XLA Modules:
  0.0 52.5 jit_solution(10190248070037180074)
XLA Ops:
  0.0 1.5 %shard_map.46 = (f32[32,512]{1,0:T(8,128)S(1)}, bf16[2,256,256]{2,1,0:T(8,128)(2,1)S(1)}, bf16[2,256,256]{2,1,0:T(8,128)(2,1)S(1)}) custom-call(f32[1,32,512]{2,1,0:T(8,128)} %normals.1, f32[1,2,256,256]{3,2,1,0:T(8,128)} %inv.1), custom_call_target="tpu_custom_call" | custom-call | tf_op jit(solution)/shard_map/pallas_call | solution.py:457
  1.5 0.0 copy-start
  1.5 0.0 copy-start.1
  1.5 0.8 %collective-permute-start.2 = (f32[32,512]{1,0:T(8,128)S(1)}, f32[32,512]{1,0:T(8,128)S(1)}, u32[]{:S(2)}, u32[]{:S(2)}) collective-permute-start(f32[32,512]{1,0:T(8,128)S(1)} %shard_map.52), channel_id=1, source_target_pairs={{30,29},{31,28}} | collective-permute-start | bytes 196616 | tf_op jit(solution)/shard_map/ppermute | solution.py:442
  2.3 0.7 %collective-permute-start.3 = (f32[32,512]{1,0:T(8,128)S(1)}, f32[32,512]{1,0:T(8,128)S(1)}, u32[]{:S(2)}, u32[]{:S(2)}) collective-permute-start(f32[32,512]{1,0:T(8,128)S(1)} %get-tuple-element.58.refs_1_.refs_6_.const), channel_id=1, source_target_pairs={{30,28},{31,29}} | collective-permute-start | bytes 196616 | tf_op jit(solution)/shard_map/ppermute | solution.py:482
  3.0 0.7 %shard_map.47 = (bf16[1024,256]{1,0:T(8,128)(2,1)S(1)}, bf16[1024,256]{1,0:T(8,128)(2,1)S(1)}, f32[1088,256]{1,0:T(8,128)S(1)}) custom-call(s32[1,2,3]{2,1,0:T(2,128)S(1)} %copy-done.1, f32[32,512]{1,0:T(8,128)S(1)} %get-tuple-element.58.refs_1_.refs_6_.const, bf16[2,256,256]{2,1,0:T(8,128)(2,1)S(1)} %get-tuple-element.59.refs_2_, ...), custom_call_target="tpu_custom_call" | custom-call | flops 427819008 | bytes 4194304 | tf_op jit(solution)/shard_map/pallas_call | solution.py:485
  3.8 1.3 %collective-permute-start.1 = (f32[1,544,128]{2,1,0:T(8,128)S(1)}, f32[1,544,128]{2,1,0:T(8,128)S(1)}, u32[]{:S(2)}, u32[]{:S(2)}) collective-permute-start(f32[1,544,128]{2,1,0:T(8,128)S(1)} %shard_map.48._edges), channel_id=1, source_target_pairs={{2,1},{3,0},{6,5},{7,4},{10,9},{11,8},{14,13},{15,12},{18,17},{19,... | collective-permute-start | bytes 835592 | tf_op jit(solution)/shard_map/ppermute | solution.py:442
  5.1 1.3 %collective-permute-start = (f32[1088,256]{1,0:T(8,128)S(1)}, f32[1088,256]{1,0:T(8,128)S(1)}, u32[]{:S(2)}, u32[]{:S(2)}) collective-permute-start(f32[1088,256]{1,0:T(8,128)S(1)} %shard_map.49), channel_id=1, source_target_pairs={{2,0},{3,1},{6,4},{7,5},{10,8},{11,9},{14,12},{15,13},{18,16},{19,... | collective-permute-start | bytes 3342344 | tf_op jit(solution)/shard_map/ppermute | solution.py:513
  6.4 0.0 collective-permute-done.2.next_in
  6.4 0.0 collective-permute-done.3.own_in
  6.5 0.7 %collective-permute-start.5 = (f32[32,384]{1,0:T(8,128)S(1)}, f32[32,384]{1,0:T(8,128)S(1)}, u32[]{:S(2)}, u32[]{:S(2)}) collective-permute-start(f32[32,384]{1,0:T(8,128)S(1)} %get-tuple-element.70), channel_id=1, source_target_pairs={{28,25},{29,24}} | collective-permute-start | bytes 147464 | tf_op jit(solution)/shard_map/ppermute | solution.py:442
  7.1 0.7 %collective-permute-start.4 = (f32[32,512]{1,0:T(8,128)S(1)}, f32[32,512]{1,0:T(8,128)S(1)}, u32[]{:S(2)}, u32[]{:S(2)}) collective-permute-start(f32[32,512]{1,0:T(8,128)S(1)} %get-tuple-element.69.refs_5_._lower), channel_id=1, source_target_pairs={{28,24},{29,25}} | collective-permute-start | bytes 196616 | tf_op jit(solution)/shard_map/ppermute | solution.py:588
  7.8 4.5 %collective-permute-done.far.refs_0_.rest_5_ = f32[1088,256]{1,0:T(8,128)S(1)} collective-permute-done((f32[1088,256]{1,0:T(8,128)S(1)}, f32[1088,256]{1,0:T(8,128)S(1)}, u32[]{:S(2)}, u32[]{:S(2)}) %collective-permute-start) | collective-permute-done | bytes 1114144 | tf_op jit(solution)/shard_map/ppermute | solution.py:513
  12.3 0.1 shard_map.50
  12.4 0.0 collective-permute-done.1.refs_1_
  12.6 0.7 %collective-permute-start.7 = (f32[32,384]{1,0:T(8,128)S(1)}, f32[32,384]{1,0:T(8,128)S(1)}, u32[]{:S(2)}, u32[]{:S(2)}) collective-permute-start(f32[32,384]{1,0:T(8,128)S(1)} %get-tuple-element.79), channel_id=1, source_target_pairs={{24,21},{25,20}} | collective-permute-start | bytes 147464 | tf_op jit(solution)/shard_map/ppermute | solution.py:442
  13.2 0.7 %collective-permute-start.6 = (f32[32,512]{1,0:T(8,128)S(1)}, f32[32,512]{1,0:T(8,128)S(1)}, u32[]{:S(2)}, u32[]{:S(2)}) collective-permute-start(f32[32,512]{1,0:T(8,128)S(1)} %get-tuple-element.78._lower), channel_id=1, source_target_pairs={{24,20},{25,21}} | collective-permute-start | bytes 196616 | tf_op jit(solution)/shard_map/ppermute | solution.py:588
  13.9 1.7 %shard_map.51 = (bf16[2048,256]{1,0:T(8,128)(2,1)S(1)}, bf16[2048,256]{1,0:T(8,128)(2,1)S(1)}, f32[32,512]{1,0:T(8,128)S(1)}, f32[1088,256]{1,0:T(8,128)S(1)}, f32[512,256]{1,0:T(8,128)S(1)}) custom-call(f32[1088,256]{1,0:T(8,128)S(1)} %collective-permute-done.far.refs_0_.rest_5_, f32[1,544,128]{2,1,0:T(8,128)S(1)} %collective-permute-done.1.refs_1_, ...), custom_call_target="tpu_custom_call" | custom-call | flops 1000000000 | tf_op jit(solution)/shard_map/pallas_call | solution.py:537
  15.6 0.7 %collective-permute-start.14 = (f32[1088,256]{1,0:T(8,128)S(1)}, f32[1088,256]{1,0:T(8,128)S(1)}, u32[]{:S(2)}, u32[]{:S(2)}) collective-permute-start(f32[1088,256]{1,0:T(8,128)S(1)} %get-tuple-element.94), channel_id=1, source_target_pairs={{4,8},{5,9},{8,12},{9,13}} | collective-permute-start | bytes 3342344 | tf_op jit(solution)/shard_map/ppermute | solution.py:553
  16.3 0.7 %collective-permute-start.15 = (f32[512,256]{1,0:T(8,128)S(1)}, f32[512,256]{1,0:T(8,128)S(1)}, u32[]{:S(2)}, u32[]{:S(2)}) collective-permute-start(f32[512,256]{1,0:T(8,128)S(1)} %get-tuple-element.95), channel_id=1, source_target_pairs={{4,9},{5,8},{8,13},{9,12}} | collective-permute-start | bytes 1572872 | tf_op jit(solution)/shard_map/ppermute | solution.py:442
  17.0 0.0 collective-permute-done.7.next_in
  17.1 0.7 %collective-permute-start.9 = (f32[32,512]{1,0:T(8,128)S(1)}, f32[32,512]{1,0:T(8,128)S(1)}, u32[]{:S(2)}, u32[]{:S(2)}) collective-permute-start(f32[32,512]{1,0:T(8,128)S(1)} %get-tuple-element.83._lower), channel_id=1, source_target_pairs={{20,17},{21,16}} | collective-permute-start | bytes 196616 | tf_op jit(solution)/shard_map/ppermute | solution.py:442
  17.8 0.7 %collective-permute-start.8 = (f32[32,512]{1,0:T(8,128)S(1)}, f32[32,512]{1,0:T(8,128)S(1)}, u32[]{:S(2)}, u32[]{:S(2)}) collective-permute-start(f32[32,512]{1,0:T(8,128)S(1)} %get-tuple-element.83._lower), channel_id=1, source_target_pairs={{20,16},{21,17}} | collective-permute-start | bytes 196616 | tf_op jit(solution)/shard_map/ppermute | solution.py:588
  18.4 0.0 collective-permute-done.9.next_in
  18.5 0.0 collective-permute-done.8.own_in
  18.5 0.7 %collective-permute-start.11 = (f32[32,512]{1,0:T(8,128)S(1)}, f32[32,512]{1,0:T(8,128)S(1)}, u32[]{:S(2)}, u32[]{:S(2)}) collective-permute-start(f32[32,512]{1,0:T(8,128)S(1)} %get-tuple-element.87._lower), channel_id=1, source_target_pairs={{16,13},{17,12}} | collective-permute-start | bytes 196616 | tf_op jit(solution)/shard_map/ppermute | solution.py:442
  19.2 0.7 %collective-permute-start.10 = (f32[32,512]{1,0:T(8,128)S(1)}, f32[32,512]{1,0:T(8,128)S(1)}, u32[]{:S(2)}, u32[]{:S(2)}) collective-permute-start(f32[32,512]{1,0:T(8,128)S(1)} %get-tuple-element.87._lower), channel_id=1, source_target_pairs={{16,12},{17,13}} | collective-permute-start | bytes 196616 | tf_op jit(solution)/shard_map/ppermute | solution.py:588
  19.9 0.7 %collective-permute-start.13 = (f32[32,512]{1,0:T(8,128)S(1)}, f32[32,512]{1,0:T(8,128)S(1)}, u32[]{:S(2)}, u32[]{:S(2)}) collective-permute-start(f32[32,512]{1,0:T(8,128)S(1)} %get-tuple-element.91.rest_6_.lower), channel_id=1, source_target_pairs={{12,9},{13,8}} | collective-permute-start | bytes 196616 | tf_op jit(solution)/shard_map/ppermute | solution.py:442
  20.6 0.7 %collective-permute-start.12 = (f32[32,512]{1,0:T(8,128)S(1)}, f32[32,512]{1,0:T(8,128)S(1)}, u32[]{:S(2)}, u32[]{:S(2)}) collective-permute-start(f32[32,512]{1,0:T(8,128)S(1)} %get-tuple-element.91.rest_6_.lower), channel_id=1, source_target_pairs={{12,8},{13,9}} | collective-permute-start | bytes 196616 | tf_op jit(solution)/shard_map/ppermute | solution.py:588
  21.3 0.0 collective-permute-done.13.next_in
  21.3 0.0 collective-permute-done.15.other_rows
  21.3 0.0 collective-permute-done.14.own_rows.rest_0_
  21.3 0.2 shard_map.65
  21.6 0.0 collective-permute-done.12.own_in
  21.7 1.3 %collective-permute-start.16 = (f32[32,896]{1,0:T(8,128)S(1)}, f32[32,896]{1,0:T(8,128)S(1)}, u32[]{:S(2)}, u32[]{:S(2)}) collective-permute-start(f32[32,896]{1,0:T(8,128)S(1)} %get-tuple-element.101), channel_id=1, source_target_pairs={{9,0}} | collective-permute-start | bytes 344072 | tf_op jit(solution)/shard_map/ppermute | solution.py:582
  23.0 1.3 %collective-permute-start.17 = (f32[32,896]{1,0:T(8,128)S(1)}, f32[32,896]{1,0:T(8,128)S(1)}, u32[]{:S(2)}, u32[]{:S(2)}) collective-permute-start(f32[32,896]{1,0:T(8,128)S(1)} %get-tuple-element.102), channel_id=1, source_target_pairs={{8,0},{9,1}} | collective-permute-start | bytes 344072 | tf_op jit(solution)/shard_map/ppermute | solution.py:583
  24.3 0.7 %collective-permute-start.18 = (f32[32,896]{1,0:T(8,128)S(1)}, f32[32,896]{1,0:T(8,128)S(1)}, u32[]{:S(2)}, u32[]{:S(2)}) collective-permute-start(f32[32,896]{1,0:T(8,128)S(1)} %get-tuple-element.103), channel_id=1, source_target_pairs={{8,1}} | collective-permute-start | bytes 344072 | tf_op jit(solution)/shard_map/ppermute | solution.py:584
  25.0 0.7 %collective-permute-start.19 = (f32[32,896]{1,0:T(8,128)S(1)}, f32[32,896]{1,0:T(8,128)S(1)}, u32[]{:S(2)}, u32[]{:S(2)}) collective-permute-start(f32[32,896]{1,0:T(8,128)S(1)} %get-tuple-element.104), channel_id=1, source_target_pairs={{12,5},{13,4}} | collective-permute-start | bytes 344072 | tf_op jit(solution)/shard_map/ppermute | solution.py:442
  25.6 0.7 %collective-permute-start.20 = (f32[32,896]{1,0:T(8,128)S(1)}, f32[32,896]{1,0:T(8,128)S(1)}, u32[]{:S(2)}, u32[]{:S(2)}) collective-permute-start(f32[32,896]{1,0:T(8,128)S(1)} %get-tuple-element.105), channel_id=1, source_target_pairs={{12,4},{13,5}} | collective-permute-start | bytes 344072 | tf_op jit(solution)/shard_map/ppermute | solution.py:600
  26.3 22.8 %collective-permute-done.16.rest_0_ = f32[32,896]{1,0:T(8,128)S(1)} collective-permute-done((f32[32,896]{1,0:T(8,128)S(1)}, f32[32,896]{1,0:T(8,128)S(1)}, u32[]{:S(2)}, u32[]{:S(2)}) %collective-permute-start.16) | collective-permute-done | bytes 114720 | tf_op jit(solution)/shard_map/ppermute | solution.py:582
  49.1 0.2 collective-permute-done.17.rest_1_
  49.4 0.0 collective-permute-done.19.rest_3_
  49.4 0.0 collective-permute-done.20.rest_4_
  49.4 0.3 shard_map.68
  49.7 1.3 %collective-permute-start.21 = (f32[32,512]{1,0:T(8,128)S(1)}, f32[32,512]{1,0:T(8,128)S(1)}, u32[]{:S(2)}, u32[]{:S(2)}) collective-permute-start(f32[32,512]{1,0:T(8,128)S(1)} %get-tuple-element.110), channel_id=1, source_target_pairs={{0,2},{1,3},{4,6},{5,7},{8,10},{9,11},{12,14},{13,15},{16,18},{17,... | collective-permute-start | bytes 196616 | tf_op jit(solution)/shard_map/ppermute | solution.py:631
  51.0 0.5 shard_map.69
  51.5 0.4 collective-permute-done.21
  51.9 0.6 %select_bitcast_fusion = f32[1,32,512]{2,1,0:T(8,128)} fusion(f32[32,512]{1,0:T(8,128)S(1)} %shard_map.69, f32[32,512]{1,0:T(8,128)S(1)} %collective-permute-done.21, pred[]{:T(512)S(6)} %eq.5), kind=kLoop, calls=%fused_computation | loop fusion | flops 16384 | bytes 196609 | tf_op jit(solution)/shard_map/broadcast_in_dim | solution.py:641
  (28 shorter events, 0.4 us)
Async XLA Ops:
  1.5 1.5 %copy-start = (f32[1,2,512,256]{3,2,1,0:T(8,128)S(1)}, f32[1,2,512,256]{3,2,1,0:T(8,128)}, u32[]{:S(2)}) copy-start(f32[1,2,512,256]{3,2,1,0:T(8,128)} %refs_4_.3) | copy-start | bytes 3145732
  1.5 1.5 %copy-start.1 = (s32[1,2,3]{2,1,0:T(2,128)S(1)}, s32[1,2,3]{2,1,0:T(2,128)}, u32[]{:S(2)}) copy-start(s32[1,2,3]{2,1,0:T(2,128)} %refs_0_.3) | copy-start | bytes 76
  1.5 4.9 %collective-permute-start.2 = (f32[32,512]{1,0:T(8,128)S(1)}, f32[32,512]{1,0:T(8,128)S(1)}, u32[]{:S(2)}, u32[]{:S(2)}) collective-permute-start(f32[32,512]{1,0:T(8,128)S(1)} %shard_map.52), channel_id=1, source_target_pairs={{30,29},{31,28}} | collective-permute-start | bytes 196616 | tf_op jit(solution)/shard_map/ppermute | solution.py:442
  2.3 4.1 %collective-permute-start.3 = (f32[32,512]{1,0:T(8,128)S(1)}, f32[32,512]{1,0:T(8,128)S(1)}, u32[]{:S(2)}, u32[]{:S(2)}) collective-permute-start(f32[32,512]{1,0:T(8,128)S(1)} %get-tuple-element.58.refs_1_.refs_6_.const), channel_id=1, source_target_pairs={{30,28},{31,29}} | collective-permute-start | bytes 196616 | tf_op jit(solution)/shard_map/ppermute | solution.py:482
  3.8 8.7 %collective-permute-start.1 = (f32[1,544,128]{2,1,0:T(8,128)S(1)}, f32[1,544,128]{2,1,0:T(8,128)S(1)}, u32[]{:S(2)}, u32[]{:S(2)}) collective-permute-start(f32[1,544,128]{2,1,0:T(8,128)S(1)} %shard_map.48._edges), channel_id=1, source_target_pairs={{2,1},{3,0},{6,5},{7,4},{10,9},{11,8},{14,13},{15,12},{18,17},{19,... | collective-permute-start | bytes 835592 | tf_op jit(solution)/shard_map/ppermute | solution.py:442
  5.1 7.2 %collective-permute-start = (f32[1088,256]{1,0:T(8,128)S(1)}, f32[1088,256]{1,0:T(8,128)S(1)}, u32[]{:S(2)}, u32[]{:S(2)}) collective-permute-start(f32[1088,256]{1,0:T(8,128)S(1)} %shard_map.49), channel_id=1, source_target_pairs={{2,0},{3,1},{6,4},{7,5},{10,8},{11,9},{14,12},{15,13},{18,16},{19,... | collective-permute-start | bytes 3342344 | tf_op jit(solution)/shard_map/ppermute | solution.py:513
  6.5 6.0 %collective-permute-start.5 = (f32[32,384]{1,0:T(8,128)S(1)}, f32[32,384]{1,0:T(8,128)S(1)}, u32[]{:S(2)}, u32[]{:S(2)}) collective-permute-start(f32[32,384]{1,0:T(8,128)S(1)} %get-tuple-element.70), channel_id=1, source_target_pairs={{28,25},{29,24}} | collective-permute-start | bytes 147464 | tf_op jit(solution)/shard_map/ppermute | solution.py:442
  7.1 5.4 %collective-permute-start.4 = (f32[32,512]{1,0:T(8,128)S(1)}, f32[32,512]{1,0:T(8,128)S(1)}, u32[]{:S(2)}, u32[]{:S(2)}) collective-permute-start(f32[32,512]{1,0:T(8,128)S(1)} %get-tuple-element.69.refs_5_._lower), channel_id=1, source_target_pairs={{28,24},{29,25}} | collective-permute-start | bytes 196616 | tf_op jit(solution)/shard_map/ppermute | solution.py:588
  12.6 4.5 %collective-permute-start.7 = (f32[32,384]{1,0:T(8,128)S(1)}, f32[32,384]{1,0:T(8,128)S(1)}, u32[]{:S(2)}, u32[]{:S(2)}) collective-permute-start(f32[32,384]{1,0:T(8,128)S(1)} %get-tuple-element.79), channel_id=1, source_target_pairs={{24,21},{25,20}} | collective-permute-start | bytes 147464 | tf_op jit(solution)/shard_map/ppermute | solution.py:442
  13.2 3.8 %collective-permute-start.6 = (f32[32,512]{1,0:T(8,128)S(1)}, f32[32,512]{1,0:T(8,128)S(1)}, u32[]{:S(2)}, u32[]{:S(2)}) collective-permute-start(f32[32,512]{1,0:T(8,128)S(1)} %get-tuple-element.78._lower), channel_id=1, source_target_pairs={{24,20},{25,21}} | collective-permute-start | bytes 196616 | tf_op jit(solution)/shard_map/ppermute | solution.py:588
  15.6 5.7 %collective-permute-start.14 = (f32[1088,256]{1,0:T(8,128)S(1)}, f32[1088,256]{1,0:T(8,128)S(1)}, u32[]{:S(2)}, u32[]{:S(2)}) collective-permute-start(f32[1088,256]{1,0:T(8,128)S(1)} %get-tuple-element.94), channel_id=1, source_target_pairs={{4,8},{5,9},{8,12},{9,13}} | collective-permute-start | bytes 3342344 | tf_op jit(solution)/shard_map/ppermute | solution.py:553
  16.3 5.0 %collective-permute-start.15 = (f32[512,256]{1,0:T(8,128)S(1)}, f32[512,256]{1,0:T(8,128)S(1)}, u32[]{:S(2)}, u32[]{:S(2)}) collective-permute-start(f32[512,256]{1,0:T(8,128)S(1)} %get-tuple-element.95), channel_id=1, source_target_pairs={{4,9},{5,8},{8,13},{9,12}} | collective-permute-start | bytes 1572872 | tf_op jit(solution)/shard_map/ppermute | solution.py:442
  17.1 1.3 %collective-permute-start.9 = (f32[32,512]{1,0:T(8,128)S(1)}, f32[32,512]{1,0:T(8,128)S(1)}, u32[]{:S(2)}, u32[]{:S(2)}) collective-permute-start(f32[32,512]{1,0:T(8,128)S(1)} %get-tuple-element.83._lower), channel_id=1, source_target_pairs={{20,17},{21,16}} | collective-permute-start | bytes 196616 | tf_op jit(solution)/shard_map/ppermute | solution.py:442
  17.8 0.7 %collective-permute-start.8 = (f32[32,512]{1,0:T(8,128)S(1)}, f32[32,512]{1,0:T(8,128)S(1)}, u32[]{:S(2)}, u32[]{:S(2)}) collective-permute-start(f32[32,512]{1,0:T(8,128)S(1)} %get-tuple-element.83._lower), channel_id=1, source_target_pairs={{20,16},{21,17}} | collective-permute-start | bytes 196616 | tf_op jit(solution)/shard_map/ppermute | solution.py:588
  18.5 1.3 %collective-permute-start.11 = (f32[32,512]{1,0:T(8,128)S(1)}, f32[32,512]{1,0:T(8,128)S(1)}, u32[]{:S(2)}, u32[]{:S(2)}) collective-permute-start(f32[32,512]{1,0:T(8,128)S(1)} %get-tuple-element.87._lower), channel_id=1, source_target_pairs={{16,13},{17,12}} | collective-permute-start | bytes 196616 | tf_op jit(solution)/shard_map/ppermute | solution.py:442
  19.2 0.7 %collective-permute-start.10 = (f32[32,512]{1,0:T(8,128)S(1)}, f32[32,512]{1,0:T(8,128)S(1)}, u32[]{:S(2)}, u32[]{:S(2)}) collective-permute-start(f32[32,512]{1,0:T(8,128)S(1)} %get-tuple-element.87._lower), channel_id=1, source_target_pairs={{16,12},{17,13}} | collective-permute-start | bytes 196616 | tf_op jit(solution)/shard_map/ppermute | solution.py:588
  19.9 1.3 %collective-permute-start.13 = (f32[32,512]{1,0:T(8,128)S(1)}, f32[32,512]{1,0:T(8,128)S(1)}, u32[]{:S(2)}, u32[]{:S(2)}) collective-permute-start(f32[32,512]{1,0:T(8,128)S(1)} %get-tuple-element.91.rest_6_.lower), channel_id=1, source_target_pairs={{12,9},{13,8}} | collective-permute-start | bytes 196616 | tf_op jit(solution)/shard_map/ppermute | solution.py:442
  20.6 1.0 %collective-permute-start.12 = (f32[32,512]{1,0:T(8,128)S(1)}, f32[32,512]{1,0:T(8,128)S(1)}, u32[]{:S(2)}, u32[]{:S(2)}) collective-permute-start(f32[32,512]{1,0:T(8,128)S(1)} %get-tuple-element.91.rest_6_.lower), channel_id=1, source_target_pairs={{12,8},{13,9}} | collective-permute-start | bytes 196616 | tf_op jit(solution)/shard_map/ppermute | solution.py:588
  21.7 27.5 %collective-permute-start.16 = (f32[32,896]{1,0:T(8,128)S(1)}, f32[32,896]{1,0:T(8,128)S(1)}, u32[]{:S(2)}, u32[]{:S(2)}) collective-permute-start(f32[32,896]{1,0:T(8,128)S(1)} %get-tuple-element.101), channel_id=1, source_target_pairs={{9,0}} | collective-permute-start | bytes 344072 | tf_op jit(solution)/shard_map/ppermute | solution.py:582
  23.0 26.4 %collective-permute-start.17 = (f32[32,896]{1,0:T(8,128)S(1)}, f32[32,896]{1,0:T(8,128)S(1)}, u32[]{:S(2)}, u32[]{:S(2)}) collective-permute-start(f32[32,896]{1,0:T(8,128)S(1)} %get-tuple-element.102), channel_id=1, source_target_pairs={{8,0},{9,1}} | collective-permute-start | bytes 344072 | tf_op jit(solution)/shard_map/ppermute | solution.py:583
  24.3 25.1 %collective-permute-start.18 = (f32[32,896]{1,0:T(8,128)S(1)}, f32[32,896]{1,0:T(8,128)S(1)}, u32[]{:S(2)}, u32[]{:S(2)}) collective-permute-start(f32[32,896]{1,0:T(8,128)S(1)} %get-tuple-element.103), channel_id=1, source_target_pairs={{8,1}} | collective-permute-start | bytes 344072 | tf_op jit(solution)/shard_map/ppermute | solution.py:584
  25.0 24.4 %collective-permute-start.19 = (f32[32,896]{1,0:T(8,128)S(1)}, f32[32,896]{1,0:T(8,128)S(1)}, u32[]{:S(2)}, u32[]{:S(2)}) collective-permute-start(f32[32,896]{1,0:T(8,128)S(1)} %get-tuple-element.104), channel_id=1, source_target_pairs={{12,5},{13,4}} | collective-permute-start | bytes 344072 | tf_op jit(solution)/shard_map/ppermute | solution.py:442
  25.6 23.7 %collective-permute-start.20 = (f32[32,896]{1,0:T(8,128)S(1)}, f32[32,896]{1,0:T(8,128)S(1)}, u32[]{:S(2)}, u32[]{:S(2)}) collective-permute-start(f32[32,896]{1,0:T(8,128)S(1)} %get-tuple-element.105), channel_id=1, source_target_pairs={{12,4},{13,5}} | collective-permute-start | bytes 344072 | tf_op jit(solution)/shard_map/ppermute | solution.py:600
  49.7 2.2 %collective-permute-start.21 = (f32[32,512]{1,0:T(8,128)S(1)}, f32[32,512]{1,0:T(8,128)S(1)}, u32[]{:S(2)}, u32[]{:S(2)}) collective-permute-start(f32[32,512]{1,0:T(8,128)S(1)} %get-tuple-element.110), channel_id=1, source_target_pairs={{0,2},{1,3},{4,6},{5,7},{8,10},{9,11},{12,14},{13,15},{16,18},{17,... | collective-permute-start | bytes 196616 | tf_op jit(solution)/shard_map/ppermute | solution.py:631

commit v20 on v19

--- a/solution.py
+++ b/solution.py
@@ -65,8 +65,13 @@
         const[:, at] = triple(high, low, inv_high[b], inv_low[b])
 
 
-def again_kernel(const, again):
-    again[...] = const[...]
+def copy_kernel(const, _after, copy):
+    copy[...] = const[...]
+
+
+def rim_of_kernel(sides, const, rim):
+    edge, sites = rim.shape[2], const.shape[1]
+    put_rim(sides, rim, lambda last: const[:, sites - edge :] if last else const[:, :edge])
 
 
 def fuse_kernel(late, *refs):
@@ -233,7 +238,7 @@
     @pl.when(lax.axis_index("tm") == 2 * mine)
     def _():
         mid[...] = jnp.zeros_like(mid)
-        load(sides, plain(next_in), own_in[...], edge, mid)
+        load(sides, lambda side, cut: next_in[side], own_in[...], edge, mid)
         upper[...] = own_in[...]
         for b in range(blocks):
             at, rows = slice(b * length, (b + 1) * length), slice(b * window, (b + 1) * window)
@@ -469,17 +474,24 @@
         ],
         compiler_params=PARAMS,
     )(*[pltpu.with_memory_space_constraint(a, pltpu.HBM) for a in (normals, inv_diag)])
-    again = pl.pallas_call(
-        again_kernel,
-        out_shape=shape((cols, sites), f32),
+    const_rim = pl.pallas_call(
+        functools.partial(rim_of_kernel, sides),
+        out_shape=shape((sides, cols, edge), f32),
         in_specs=[VMEM],
         out_specs=VMEM,
         compiler_params=PARAMS,
         cost_estimate=pl.CostEstimate(flops=5 * 10**9, bytes_accessed=0, transcendentals=0),
     )(const)
+    again = pl.pallas_call(
+        copy_kernel,
+        out_shape=shape((cols, sites), f32),
+        in_specs=[VMEM] * 2,
+        out_specs=VMEM,
+        compiler_params=PARAMS,
+    )(const, const_rim)
     odd, even = range(1, times, 2), range(0, times, 2)
-    first_next = cross(again, odd[-1:], even[-1:])
-    first_own = lax.ppermute(const, BOTH, link(odd[-1:], even[-1:]))
+    first_next = cross(const_rim, odd[-1:], even[-1:], True)
+    first_own = lax.ppermute(again, BOTH, link(odd[-1:], even[-1:]))
 
     def fused(late, extra, after=()):
         return pl.pallas_call(
@@ -489,7 +501,7 @@
             out_specs=(VMEM,) * (2 + len(extra)),
             compiler_params=PARAMS,
             cost_estimate=pl.CostEstimate(
-                flops=6 * (tall + cols * blocks) * length * length, bytes_accessed=16 * tall * length, transcendentals=0
+                flops=(6 if late else 150) * (tall + cols * blocks) * length * length, bytes_accessed=0, transcendentals=0
             ),
         )(fill_mask, const, inv_high, inv_low, lag_coupling, *after)
 

time: 53.2 us -> 53.2 us (level)
  no operation moved by 1% of the time
where the time goes in v20:
time: 53.2 us; the launch traced here: 52.5 us
  waiting for transfers between devices  27.9 us (52%)
  starting transfers between devices  18 us (34%)
  Pallas kernels  5.37 us (10%)
  other arithmetic  0.64 us (1%)
  between operations  0.54 us (1%)
    ppermute x1, waiting for transfers between devices, local(): first_in = lax.ppermute(to_next, BOTH, [(2 * source[0] + 1, 2 * target[0])])  22.7 us
    ppermute x9, starting transfers between devices, cross(): return lax.ppermute(value, BOTH, perm)  6.77 us
    ppermute x1, waiting for transfers between devices, local(): far = lax.ppermute(near, BOTH, link(odd[:-1], even[:-1]))  4.46 us
    ppermute x5, starting transfers between devices, local(): own_in = lax.ppermute(lower, BOTH, link(source, target))  3.32 us
    pallas_call x2, Pallas kernels, pair_matrix(): pl.pallas_call(functools.partial(pair_kernel, (pairs - 2, first), jumps),...  1.68 us
    pallas_call x1, Pallas kernels, local(): pl.pallas_call(const_kernel, out_shape=(shape((cols, sites), f32), shape(...  1.48 us
    ppermute x1, starting transfers between devices, local(): first_in = lax.ppermute(to_next, BOTH, [(2 * source[0] + 1, 2 * target[0])])  1.29 us
    ppermute x1, starting transfers between devices, local(): own_in = lax.ppermute(to_own, BOTH, link(source, target))  1.29 us
  transfers between devices with their start and end apart: 22, of which 4 were waited for; matrix products, arithmetic and copies ran while one was open for 0% of the time, Pallas kernels for 7%

profile of v20, /device:TPU:0, one launch (start us, length us, event | category | flops | bytes accessed | tf_op | source)
XLA Modules:
  0.0 52.5 jit_solution(13448692091379476856)
XLA Ops:
  0.0 1.5 %shard_map.46 = (f32[32,512]{1,0:T(8,128)S(1)}, bf16[2,256,256]{2,1,0:T(8,128)(2,1)S(1)}, bf16[2,256,256]{2,1,0:T(8,128)(2,1)S(1)}) custom-call(f32[1,32,512]{2,1,0:T(8,128)} %normals.1, f32[1,2,256,256]{3,2,1,0:T(8,128)} %inv.1), custom_call_target="tpu_custom_call" | custom-call | tf_op jit(solution)/shard_map/pallas_call | solution.py:462
  1.5 0.0 copy-start
  1.5 0.0 copy-start.1
  1.5 0.8 %collective-permute-start.2 = (f32[1,32,128]{2,1,0:T(8,128)S(1)}, f32[1,32,128]{2,1,0:T(8,128)S(1)}, u32[]{:S(2)}, u32[]{:S(2)}) collective-permute-start(f32[1,32,128]{2,1,0:T(8,128)S(1)} %shard_map.52._after), channel_id=1, source_target_pairs={{30,29},{31,28}} | collective-permute-start | bytes 49160 | tf_op jit(solution)/shard_map/ppermute | solution.py:447
  2.4 0.7 %collective-permute-start.3 = (f32[32,512]{1,0:T(8,128)S(1)}, f32[32,512]{1,0:T(8,128)S(1)}, u32[]{:S(2)}, u32[]{:S(2)}) collective-permute-start(f32[32,512]{1,0:T(8,128)S(1)} %shard_map.53), channel_id=1, source_target_pairs={{30,28},{31,29}} | collective-permute-start | bytes 196616 | tf_op jit(solution)/shard_map/ppermute | solution.py:494
  3.0 0.7 %shard_map.47 = (bf16[1024,256]{1,0:T(8,128)(2,1)S(1)}, bf16[1024,256]{1,0:T(8,128)(2,1)S(1)}, f32[1088,256]{1,0:T(8,128)S(1)}) custom-call(s32[1,2,3]{2,1,0:T(2,128)S(1)} %copy-done.1, f32[32,512]{1,0:T(8,128)S(1)} %get-tuple-element.58.refs_1_.refs_6_.const, bf16[2,256,256]{2,1,0:T(8,128)(2,1)S(1)} %get-tuple-element.59.refs_2_, ...), custom_call_target="tpu_custom_call" | custom-call | flops 10695475200 | tf_op jit(solution)/shard_map/pallas_call | solution.py:497
  3.8 1.3 %collective-permute-start.1 = (f32[1,544,128]{2,1,0:T(8,128)S(1)}, f32[1,544,128]{2,1,0:T(8,128)S(1)}, u32[]{:S(2)}, u32[]{:S(2)}) collective-permute-start(f32[1,544,128]{2,1,0:T(8,128)S(1)} %shard_map.48._edges), channel_id=1, source_target_pairs={{2,1},{3,0},{6,5},{7,4},{10,9},{11,8},{14,13},{15,12},{18,17},{19,... | collective-permute-start | bytes 835592 | tf_op jit(solution)/shard_map/ppermute | solution.py:447
  5.1 1.3 %collective-permute-start = (f32[1088,256]{1,0:T(8,128)S(1)}, f32[1088,256]{1,0:T(8,128)S(1)}, u32[]{:S(2)}, u32[]{:S(2)}) collective-permute-start(f32[1088,256]{1,0:T(8,128)S(1)} %shard_map.49), channel_id=1, source_target_pairs={{2,0},{3,1},{6,4},{7,5},{10,8},{11,9},{14,12},{15,13},{18,16},{19,... | collective-permute-start | bytes 3342344 | tf_op jit(solution)/shard_map/ppermute | solution.py:525
  6.4 0.0 collective-permute-done.2.next_in
  6.4 0.0 collective-permute-done.3.own_in
  6.5 0.7 %collective-permute-start.5 = (f32[32,384]{1,0:T(8,128)S(1)}, f32[32,384]{1,0:T(8,128)S(1)}, u32[]{:S(2)}, u32[]{:S(2)}) collective-permute-start(f32[32,384]{1,0:T(8,128)S(1)} %get-tuple-element.70), channel_id=1, source_target_pairs={{28,25},{29,24}} | collective-permute-start | bytes 147464 | tf_op jit(solution)/shard_map/ppermute | solution.py:447
  7.2 0.7 %collective-permute-start.4 = (f32[32,512]{1,0:T(8,128)S(1)}, f32[32,512]{1,0:T(8,128)S(1)}, u32[]{:S(2)}, u32[]{:S(2)}) collective-permute-start(f32[32,512]{1,0:T(8,128)S(1)} %get-tuple-element.69.refs_5_._lower), channel_id=1, source_target_pairs={{28,24},{29,25}} | collective-permute-start | bytes 196616 | tf_op jit(solution)/shard_map/ppermute | solution.py:600
  7.9 4.5 %collective-permute-done.far.refs_0_.rest_5_ = f32[1088,256]{1,0:T(8,128)S(1)} collective-permute-done((f32[1088,256]{1,0:T(8,128)S(1)}, f32[1088,256]{1,0:T(8,128)S(1)}, u32[]{:S(2)}, u32[]{:S(2)}) %collective-permute-start) | collective-permute-done | bytes 1114144 | tf_op jit(solution)/shard_map/ppermute | solution.py:525
  12.3 0.1 shard_map.50
  12.5 0.0 collective-permute-done.1.refs_1_
  12.5 0.0 collective-permute-done.5.next_in
  12.6 0.0 collective-permute-done.4.own_in
  12.6 0.7 %collective-permute-start.7 = (f32[32,384]{1,0:T(8,128)S(1)}, f32[32,384]{1,0:T(8,128)S(1)}, u32[]{:S(2)}, u32[]{:S(2)}) collective-permute-start(f32[32,384]{1,0:T(8,128)S(1)} %get-tuple-element.79), channel_id=1, source_target_pairs={{24,21},{25,20}} | collective-permute-start | bytes 147464 | tf_op jit(solution)/shard_map/ppermute | solution.py:447
  13.3 0.7 %collective-permute-start.6 = (f32[32,512]{1,0:T(8,128)S(1)}, f32[32,512]{1,0:T(8,128)S(1)}, u32[]{:S(2)}, u32[]{:S(2)}) collective-permute-start(f32[32,512]{1,0:T(8,128)S(1)} %get-tuple-element.78._lower), channel_id=1, source_target_pairs={{24,20},{25,21}} | collective-permute-start | bytes 196616 | tf_op jit(solution)/shard_map/ppermute | solution.py:600
  13.9 1.7 %shard_map.51 = (bf16[2048,256]{1,0:T(8,128)(2,1)S(1)}, bf16[2048,256]{1,0:T(8,128)(2,1)S(1)}, f32[32,512]{1,0:T(8,128)S(1)}, f32[1088,256]{1,0:T(8,128)S(1)}, f32[512,256]{1,0:T(8,128)S(1)}) custom-call(f32[1088,256]{1,0:T(8,128)S(1)} %collective-permute-done.far.refs_0_.rest_5_, f32[1,544,128]{2,1,0:T(8,128)S(1)} %collective-permute-done.1.refs_1_, ...), custom_call_target="tpu_custom_call" | custom-call | flops 1000000000 | tf_op jit(solution)/shard_map/pallas_call | solution.py:549
  15.6 0.7 %collective-permute-start.14 = (f32[1088,256]{1,0:T(8,128)S(1)}, f32[1088,256]{1,0:T(8,128)S(1)}, u32[]{:S(2)}, u32[]{:S(2)}) collective-permute-start(f32[1088,256]{1,0:T(8,128)S(1)} %get-tuple-element.94), channel_id=1, source_target_pairs={{4,8},{5,9},{8,12},{9,13}} | collective-permute-start | bytes 3342344 | tf_op jit(solution)/shard_map/ppermute | solution.py:565
  16.3 0.7 %collective-permute-start.15 = (f32[512,256]{1,0:T(8,128)S(1)}, f32[512,256]{1,0:T(8,128)S(1)}, u32[]{:S(2)}, u32[]{:S(2)}) collective-permute-start(f32[512,256]{1,0:T(8,128)S(1)} %get-tuple-element.95), channel_id=1, source_target_pairs={{4,9},{5,8},{8,13},{9,12}} | collective-permute-start | bytes 1572872 | tf_op jit(solution)/shard_map/ppermute | solution.py:447
  17.0 0.0 collective-permute-done.7.next_in
  17.1 0.0 collective-permute-done.6.own_in
  17.1 0.7 %collective-permute-start.9 = (f32[32,512]{1,0:T(8,128)S(1)}, f32[32,512]{1,0:T(8,128)S(1)}, u32[]{:S(2)}, u32[]{:S(2)}) collective-permute-start(f32[32,512]{1,0:T(8,128)S(1)} %get-tuple-element.83._lower), channel_id=1, source_target_pairs={{20,17},{21,16}} | collective-permute-start | bytes 196616 | tf_op jit(solution)/shard_map/ppermute | solution.py:447
  17.8 0.7 %collective-permute-start.8 = (f32[32,512]{1,0:T(8,128)S(1)}, f32[32,512]{1,0:T(8,128)S(1)}, u32[]{:S(2)}, u32[]{:S(2)}) collective-permute-start(f32[32,512]{1,0:T(8,128)S(1)} %get-tuple-element.83._lower), channel_id=1, source_target_pairs={{20,16},{21,17}} | collective-permute-start | bytes 196616 | tf_op jit(solution)/shard_map/ppermute | solution.py:600
  18.5 0.0 collective-permute-done.9.next_in
  18.5 0.7 %collective-permute-start.11 = (f32[32,512]{1,0:T(8,128)S(1)}, f32[32,512]{1,0:T(8,128)S(1)}, u32[]{:S(2)}, u32[]{:S(2)}) collective-permute-start(f32[32,512]{1,0:T(8,128)S(1)} %get-tuple-element.87._lower), channel_id=1, source_target_pairs={{16,13},{17,12}} | collective-permute-start | bytes 196616 | tf_op jit(solution)/shard_map/ppermute | solution.py:447
  19.2 0.7 %collective-permute-start.10 = (f32[32,512]{1,0:T(8,128)S(1)}, f32[32,512]{1,0:T(8,128)S(1)}, u32[]{:S(2)}, u32[]{:S(2)}) collective-permute-start(f32[32,512]{1,0:T(8,128)S(1)} %get-tuple-element.87._lower), channel_id=1, source_target_pairs={{16,12},{17,13}} | collective-permute-start | bytes 196616 | tf_op jit(solution)/shard_map/ppermute | solution.py:600
  19.9 0.0 collective-permute-done.11.next_in
  19.9 0.0 collective-permute-done.10.own_in
  20.0 0.7 %collective-permute-start.13 = (f32[32,512]{1,0:T(8,128)S(1)}, f32[32,512]{1,0:T(8,128)S(1)}, u32[]{:S(2)}, u32[]{:S(2)}) collective-permute-start(f32[32,512]{1,0:T(8,128)S(1)} %get-tuple-element.91.rest_6_.lower), channel_id=1, source_target_pairs={{12,9},{13,8}} | collective-permute-start | bytes 196616 | tf_op jit(solution)/shard_map/ppermute | solution.py:447
  20.6 0.7 %collective-permute-start.12 = (f32[32,512]{1,0:T(8,128)S(1)}, f32[32,512]{1,0:T(8,128)S(1)}, u32[]{:S(2)}, u32[]{:S(2)}) collective-permute-start(f32[32,512]{1,0:T(8,128)S(1)} %get-tuple-element.91.rest_6_.lower), channel_id=1, source_target_pairs={{12,8},{13,9}} | collective-permute-start | bytes 196616 | tf_op jit(solution)/shard_map/ppermute | solution.py:600
  21.3 0.0 collective-permute-done.14.own_rows.rest_0_
  21.4 0.2 shard_map.66
  21.7 1.3 %collective-permute-start.16 = (f32[32,896]{1,0:T(8,128)S(1)}, f32[32,896]{1,0:T(8,128)S(1)}, u32[]{:S(2)}, u32[]{:S(2)}) collective-permute-start(f32[32,896]{1,0:T(8,128)S(1)} %get-tuple-element.101), channel_id=1, source_target_pairs={{9,0}} | collective-permute-start | bytes 344072 | tf_op jit(solution)/shard_map/ppermute | solution.py:594
  23.0 1.3 %collective-permute-start.17 = (f32[32,896]{1,0:T(8,128)S(1)}, f32[32,896]{1,0:T(8,128)S(1)}, u32[]{:S(2)}, u32[]{:S(2)}) collective-permute-start(f32[32,896]{1,0:T(8,128)S(1)} %get-tuple-element.102), channel_id=1, source_target_pairs={{8,0},{9,1}} | collective-permute-start | bytes 344072 | tf_op jit(solution)/shard_map/ppermute | solution.py:595
  24.3 0.7 %collective-permute-start.18 = (f32[32,896]{1,0:T(8,128)S(1)}, f32[32,896]{1,0:T(8,128)S(1)}, u32[]{:S(2)}, u32[]{:S(2)}) collective-permute-start(f32[32,896]{1,0:T(8,128)S(1)} %get-tuple-element.103), channel_id=1, source_target_pairs={{8,1}} | collective-permute-start | bytes 344072 | tf_op jit(solution)/shard_map/ppermute | solution.py:596
  25.0 0.7 %collective-permute-start.19 = (f32[32,896]{1,0:T(8,128)S(1)}, f32[32,896]{1,0:T(8,128)S(1)}, u32[]{:S(2)}, u32[]{:S(2)}) collective-permute-start(f32[32,896]{1,0:T(8,128)S(1)} %get-tuple-element.104), channel_id=1, source_target_pairs={{12,5},{13,4}} | collective-permute-start | bytes 344072 | tf_op jit(solution)/shard_map/ppermute | solution.py:447
  25.7 0.7 %collective-permute-start.20 = (f32[32,896]{1,0:T(8,128)S(1)}, f32[32,896]{1,0:T(8,128)S(1)}, u32[]{:S(2)}, u32[]{:S(2)}) collective-permute-start(f32[32,896]{1,0:T(8,128)S(1)} %get-tuple-element.105), channel_id=1, source_target_pairs={{12,4},{13,5}} | collective-permute-start | bytes 344072 | tf_op jit(solution)/shard_map/ppermute | solution.py:612
  26.3 22.7 %collective-permute-done.16.rest_0_ = f32[32,896]{1,0:T(8,128)S(1)} collective-permute-done((f32[32,896]{1,0:T(8,128)S(1)}, f32[32,896]{1,0:T(8,128)S(1)}, u32[]{:S(2)}, u32[]{:S(2)}) %collective-permute-start.16) | collective-permute-done | bytes 114720 | tf_op jit(solution)/shard_map/ppermute | solution.py:594
  49.0 0.3 collective-permute-done.17.rest_1_
  49.4 0.0 collective-permute-done.20.rest_4_
  49.4 0.3 shard_map.69
  49.7 1.3 %collective-permute-start.21 = (f32[32,512]{1,0:T(8,128)S(1)}, f32[32,512]{1,0:T(8,128)S(1)}, u32[]{:S(2)}, u32[]{:S(2)}) collective-permute-start(f32[32,512]{1,0:T(8,128)S(1)} %get-tuple-element.110), channel_id=1, source_target_pairs={{0,2},{1,3},{4,6},{5,7},{8,10},{9,11},{12,14},{13,15},{16,18},{17,... | collective-permute-start | bytes 196616 | tf_op jit(solution)/shard_map/ppermute | solution.py:643
  51.0 0.5 shard_map.70
  51.5 0.4 collective-permute-done.21
  51.9 0.6 %select_bitcast_fusion = f32[1,32,512]{2,1,0:T(8,128)} fusion(f32[32,512]{1,0:T(8,128)S(1)} %shard_map.70, f32[32,512]{1,0:T(8,128)S(1)} %collective-permute-done.21, pred[]{:T(512)S(6)} %eq.5), kind=kLoop, calls=%fused_computation | loop fusion | flops 16384 | bytes 196609 | tf_op jit(solution)/shard_map/broadcast_in_dim | solution.py:653
  (29 shorter events, 0.4 us)
Async XLA Ops:
  1.5 1.5 %copy-start = (f32[1,2,512,256]{3,2,1,0:T(8,128)S(1)}, f32[1,2,512,256]{3,2,1,0:T(8,128)}, u32[]{:S(2)}) copy-start(f32[1,2,512,256]{3,2,1,0:T(8,128)} %refs_4_.3) | copy-start | bytes 3145732
  1.5 1.5 %copy-start.1 = (s32[1,2,3]{2,1,0:T(2,128)S(1)}, s32[1,2,3]{2,1,0:T(2,128)}, u32[]{:S(2)}) copy-start(s32[1,2,3]{2,1,0:T(2,128)} %refs_0_.3) | copy-start | bytes 76
  1.5 4.9 %collective-permute-start.2 = (f32[1,32,128]{2,1,0:T(8,128)S(1)}, f32[1,32,128]{2,1,0:T(8,128)S(1)}, u32[]{:S(2)}, u32[]{:S(2)}) collective-permute-start(f32[1,32,128]{2,1,0:T(8,128)S(1)} %shard_map.52._after), channel_id=1, source_target_pairs={{30,29},{31,28}} | collective-permute-start | bytes 49160 | tf_op jit(solution)/shard_map/ppermute | solution.py:447
  2.4 4.1 %collective-permute-start.3 = (f32[32,512]{1,0:T(8,128)S(1)}, f32[32,512]{1,0:T(8,128)S(1)}, u32[]{:S(2)}, u32[]{:S(2)}) collective-permute-start(f32[32,512]{1,0:T(8,128)S(1)} %shard_map.53), channel_id=1, source_target_pairs={{30,28},{31,29}} | collective-permute-start | bytes 196616 | tf_op jit(solution)/shard_map/ppermute | solution.py:494
  3.8 8.7 %collective-permute-start.1 = (f32[1,544,128]{2,1,0:T(8,128)S(1)}, f32[1,544,128]{2,1,0:T(8,128)S(1)}, u32[]{:S(2)}, u32[]{:S(2)}) collective-permute-start(f32[1,544,128]{2,1,0:T(8,128)S(1)} %shard_map.48._edges), channel_id=1, source_target_pairs={{2,1},{3,0},{6,5},{7,4},{10,9},{11,8},{14,13},{15,12},{18,17},{19,... | collective-permute-start | bytes 835592 | tf_op jit(solution)/shard_map/ppermute | solution.py:447
  5.1 7.2 %collective-permute-start = (f32[1088,256]{1,0:T(8,128)S(1)}, f32[1088,256]{1,0:T(8,128)S(1)}, u32[]{:S(2)}, u32[]{:S(2)}) collective-permute-start(f32[1088,256]{1,0:T(8,128)S(1)} %shard_map.49), channel_id=1, source_target_pairs={{2,0},{3,1},{6,4},{7,5},{10,8},{11,9},{14,12},{15,13},{18,16},{19,... | collective-permute-start | bytes 3342344 | tf_op jit(solution)/shard_map/ppermute | solution.py:525
  6.5 6.0 %collective-permute-start.5 = (f32[32,384]{1,0:T(8,128)S(1)}, f32[32,384]{1,0:T(8,128)S(1)}, u32[]{:S(2)}, u32[]{:S(2)}) collective-permute-start(f32[32,384]{1,0:T(8,128)S(1)} %get-tuple-element.70), channel_id=1, source_target_pairs={{28,25},{29,24}} | collective-permute-start | bytes 147464 | tf_op jit(solution)/shard_map/ppermute | solution.py:447
  7.2 5.4 %collective-permute-start.4 = (f32[32,512]{1,0:T(8,128)S(1)}, f32[32,512]{1,0:T(8,128)S(1)}, u32[]{:S(2)}, u32[]{:S(2)}) collective-permute-start(f32[32,512]{1,0:T(8,128)S(1)} %get-tuple-element.69.refs_5_._lower), channel_id=1, source_target_pairs={{28,24},{29,25}} | collective-permute-start | bytes 196616 | tf_op jit(solution)/shard_map/ppermute | solution.py:600
  12.6 4.5 %collective-permute-start.7 = (f32[32,384]{1,0:T(8,128)S(1)}, f32[32,384]{1,0:T(8,128)S(1)}, u32[]{:S(2)}, u32[]{:S(2)}) collective-permute-start(f32[32,384]{1,0:T(8,128)S(1)} %get-tuple-element.79), channel_id=1, source_target_pairs={{24,21},{25,20}} | collective-permute-start | bytes 147464 | tf_op jit(solution)/shard_map/ppermute | solution.py:447
  13.3 3.8 %collective-permute-start.6 = (f32[32,512]{1,0:T(8,128)S(1)}, f32[32,512]{1,0:T(8,128)S(1)}, u32[]{:S(2)}, u32[]{:S(2)}) collective-permute-start(f32[32,512]{1,0:T(8,128)S(1)} %get-tuple-element.78._lower), channel_id=1, source_target_pairs={{24,20},{25,21}} | collective-permute-start | bytes 196616 | tf_op jit(solution)/shard_map/ppermute | solution.py:600
  15.6 5.7 %collective-permute-start.14 = (f32[1088,256]{1,0:T(8,128)S(1)}, f32[1088,256]{1,0:T(8,128)S(1)}, u32[]{:S(2)}, u32[]{:S(2)}) collective-permute-start(f32[1088,256]{1,0:T(8,128)S(1)} %get-tuple-element.94), channel_id=1, source_target_pairs={{4,8},{5,9},{8,12},{9,13}} | collective-permute-start | bytes 3342344 | tf_op jit(solution)/shard_map/ppermute | solution.py:565
  16.3 5.0 %collective-permute-start.15 = (f32[512,256]{1,0:T(8,128)S(1)}, f32[512,256]{1,0:T(8,128)S(1)}, u32[]{:S(2)}, u32[]{:S(2)}) collective-permute-start(f32[512,256]{1,0:T(8,128)S(1)} %get-tuple-element.95), channel_id=1, source_target_pairs={{4,9},{5,8},{8,13},{9,12}} | collective-permute-start | bytes 1572872 | tf_op jit(solution)/shard_map/ppermute | solution.py:447
  17.1 1.3 %collective-permute-start.9 = (f32[32,512]{1,0:T(8,128)S(1)}, f32[32,512]{1,0:T(8,128)S(1)}, u32[]{:S(2)}, u32[]{:S(2)}) collective-permute-start(f32[32,512]{1,0:T(8,128)S(1)} %get-tuple-element.83._lower), channel_id=1, source_target_pairs={{20,17},{21,16}} | collective-permute-start | bytes 196616 | tf_op jit(solution)/shard_map/ppermute | solution.py:447
  17.8 0.7 %collective-permute-start.8 = (f32[32,512]{1,0:T(8,128)S(1)}, f32[32,512]{1,0:T(8,128)S(1)}, u32[]{:S(2)}, u32[]{:S(2)}) collective-permute-start(f32[32,512]{1,0:T(8,128)S(1)} %get-tuple-element.83._lower), channel_id=1, source_target_pairs={{20,16},{21,17}} | collective-permute-start | bytes 196616 | tf_op jit(solution)/shard_map/ppermute | solution.py:600
  18.5 1.3 %collective-permute-start.11 = (f32[32,512]{1,0:T(8,128)S(1)}, f32[32,512]{1,0:T(8,128)S(1)}, u32[]{:S(2)}, u32[]{:S(2)}) collective-permute-start(f32[32,512]{1,0:T(8,128)S(1)} %get-tuple-element.87._lower), channel_id=1, source_target_pairs={{16,13},{17,12}} | collective-permute-start | bytes 196616 | tf_op jit(solution)/shard_map/ppermute | solution.py:447
  19.2 0.7 %collective-permute-start.10 = (f32[32,512]{1,0:T(8,128)S(1)}, f32[32,512]{1,0:T(8,128)S(1)}, u32[]{:S(2)}, u32[]{:S(2)}) collective-permute-start(f32[32,512]{1,0:T(8,128)S(1)} %get-tuple-element.87._lower), channel_id=1, source_target_pairs={{16,12},{17,13}} | collective-permute-start | bytes 196616 | tf_op jit(solution)/shard_map/ppermute | solution.py:600
  20.0 1.3 %collective-permute-start.13 = (f32[32,512]{1,0:T(8,128)S(1)}, f32[32,512]{1,0:T(8,128)S(1)}, u32[]{:S(2)}, u32[]{:S(2)}) collective-permute-start(f32[32,512]{1,0:T(8,128)S(1)} %get-tuple-element.91.rest_6_.lower), channel_id=1, source_target_pairs={{12,9},{13,8}} | collective-permute-start | bytes 196616 | tf_op jit(solution)/shard_map/ppermute | solution.py:447
  20.6 1.0 %collective-permute-start.12 = (f32[32,512]{1,0:T(8,128)S(1)}, f32[32,512]{1,0:T(8,128)S(1)}, u32[]{:S(2)}, u32[]{:S(2)}) collective-permute-start(f32[32,512]{1,0:T(8,128)S(1)} %get-tuple-element.91.rest_6_.lower), channel_id=1, source_target_pairs={{12,8},{13,9}} | collective-permute-start | bytes 196616 | tf_op jit(solution)/shard_map/ppermute | solution.py:600
  21.7 27.3 %collective-permute-start.16 = (f32[32,896]{1,0:T(8,128)S(1)}, f32[32,896]{1,0:T(8,128)S(1)}, u32[]{:S(2)}, u32[]{:S(2)}) collective-permute-start(f32[32,896]{1,0:T(8,128)S(1)} %get-tuple-element.101), channel_id=1, source_target_pairs={{9,0}} | collective-permute-start | bytes 344072 | tf_op jit(solution)/shard_map/ppermute | solution.py:594
  23.0 26.4 %collective-permute-start.17 = (f32[32,896]{1,0:T(8,128)S(1)}, f32[32,896]{1,0:T(8,128)S(1)}, u32[]{:S(2)}, u32[]{:S(2)}) collective-permute-start(f32[32,896]{1,0:T(8,128)S(1)} %get-tuple-element.102), channel_id=1, source_target_pairs={{8,0},{9,1}} | collective-permute-start | bytes 344072 | tf_op jit(solution)/shard_map/ppermute | solution.py:595
  24.3 25.1 %collective-permute-start.18 = (f32[32,896]{1,0:T(8,128)S(1)}, f32[32,896]{1,0:T(8,128)S(1)}, u32[]{:S(2)}, u32[]{:S(2)}) collective-permute-start(f32[32,896]{1,0:T(8,128)S(1)} %get-tuple-element.103), channel_id=1, source_target_pairs={{8,1}} | collective-permute-start | bytes 344072 | tf_op jit(solution)/shard_map/ppermute | solution.py:596
  25.0 24.4 %collective-permute-start.19 = (f32[32,896]{1,0:T(8,128)S(1)}, f32[32,896]{1,0:T(8,128)S(1)}, u32[]{:S(2)}, u32[]{:S(2)}) collective-permute-start(f32[32,896]{1,0:T(8,128)S(1)} %get-tuple-element.104), channel_id=1, source_target_pairs={{12,5},{13,4}} | collective-permute-start | bytes 344072 | tf_op jit(solution)/shard_map/ppermute | solution.py:447
  25.7 23.7 %collective-permute-start.20 = (f32[32,896]{1,0:T(8,128)S(1)}, f32[32,896]{1,0:T(8,128)S(1)}, u32[]{:S(2)}, u32[]{:S(2)}) collective-permute-start(f32[32,896]{1,0:T(8,128)S(1)} %get-tuple-element.105), channel_id=1, source_target_pairs={{12,4},{13,5}} | collective-permute-start | bytes 344072 | tf_op jit(solution)/shard_map/ppermute | solution.py:612
  49.7 2.2 %collective-permute-start.21 = (f32[32,512]{1,0:T(8,128)S(1)}, f32[32,512]{1,0:T(8,128)S(1)}, u32[]{:S(2)}, u32[]{:S(2)}) collective-permute-start(f32[32,512]{1,0:T(8,128)S(1)} %get-tuple-element.110), channel_id=1, source_target_pairs={{0,2},{1,3},{4,6},{5,7},{8,10},{9,11},{12,14},{13,15},{16,18},{17,... | collective-permute-start | bytes 196616 | tf_op jit(solution)/shard_map/ppermute | solution.py:643

commit v21 on v19

--- a/solution.py
+++ b/solution.py
@@ -273,6 +273,21 @@
     @pl.when(lax.axis_index("tm") == 2 * mine)
     def _():
         load_rims(sides, next_in, sites, halo, late)
+        if sides == 1 and blocks == 2:
+            left = lax.axis_index("row") != 0
+            wide = halo - edge
+            pieces = []
+            for count, on_left, on_right in (
+                (edge, (0, 0), (span - edge, span - edge)),
+                (edge, (span, length), (2 * span - halo, length + span - halo)),
+                (wide, (edge, edge), (2 * span - wide, length + span - wide)),
+            ):
+                rows, source = (pl.multiple_of(jnp.where(left, x, y), edge) for x, y in zip(on_left, on_right))
+                cut = pl.ds(rows, count)
+                pieces.append(stacked_dot(late, pl.ds(source, count), high[cut], low[cut]))
+            base[:, :length] = both[:, :length] + pieces[0] + jnp.where(left, pieces[2], 0.0)
+            base[:, length:] = both[:, length:] + pieces[1] + jnp.where(left, 0.0, pieces[2])
+            return
         cuts = [cuts_of(blocks, length, sites, span, last) for last in (False, True)]
         for b in range(blocks):
             value = both[:, b * length : (b + 1) * length]

time: 53.2 us -> 53.2 us (level)
  no operation moved by 1% of the time
where the time goes in v21:
time: 53.2 us; the launch traced here: 52.5 us
  waiting for transfers between devices  28 us (53%)
  starting transfers between devices  18 us (34%)
  Pallas kernels  5.36 us (10%)
  other arithmetic  0.64 us (1%)
    ppermute x1, waiting for transfers between devices, local(): first_in = lax.ppermute(to_next, BOTH, [(2 * source[0] + 1, 2 * target[0])])  22.8 us
    ppermute x9, starting transfers between devices, cross(): return lax.ppermute(value, BOTH, perm)  6.77 us
    ppermute x1, waiting for transfers between devices, local(): far = lax.ppermute(near, BOTH, link(odd[:-1], even[:-1]))  4.46 us
    ppermute x5, starting transfers between devices, local(): own_in = lax.ppermute(lower, BOTH, link(source, target))  3.32 us
    pallas_call x2, Pallas kernels, pair_matrix(): pl.pallas_call(functools.partial(pair_kernel, (pairs - 2, first), jumps),...  1.69 us
    pallas_call x1, Pallas kernels, local(): pl.pallas_call(const_kernel, out_shape=(shape((cols, sites), f32), shape(...  1.48 us
    ppermute x1, starting transfers between devices, local(): far = lax.ppermute(near, BOTH, link(odd[:-1], even[:-1]))  1.29 us
    ppermute x1, starting transfers between devices, local(): first_in = lax.ppermute(to_next, BOTH, [(2 * source[0] + 1, 2 * target[0])])  1.29 us
  transfers between devices with their start and end apart: 22, of which 4 were waited for; matrix products, arithmetic and copies ran while one was open for 0% of the time, Pallas kernels for 7%

profile of v21, /device:TPU:0, one launch (start us, length us, event | category | flops | bytes accessed | tf_op | source)
XLA Modules:
  0.0 52.5 jit_solution(5544014152714842111)
XLA Ops:
  0.0 1.5 %shard_map.46 = (f32[32,512]{1,0:T(8,128)S(1)}, bf16[2,256,256]{2,1,0:T(8,128)(2,1)S(1)}, bf16[2,256,256]{2,1,0:T(8,128)(2,1)S(1)}) custom-call(f32[1,32,512]{2,1,0:T(8,128)} %normals.1, f32[1,2,256,256]{3,2,1,0:T(8,128)} %inv.1), custom_call_target="tpu_custom_call" | custom-call | tf_op jit(solution)/shard_map/pallas_call | solution.py:472
  1.5 0.0 copy-start
  1.5 0.0 copy-start.1
  1.5 0.8 %collective-permute-start.2 = (f32[32,512]{1,0:T(8,128)S(1)}, f32[32,512]{1,0:T(8,128)S(1)}, u32[]{:S(2)}, u32[]{:S(2)}) collective-permute-start(f32[32,512]{1,0:T(8,128)S(1)} %shard_map.52), channel_id=1, source_target_pairs={{30,29},{31,28}} | collective-permute-start | bytes 196616 | tf_op jit(solution)/shard_map/ppermute | solution.py:457
  2.3 0.7 %collective-permute-start.3 = (f32[32,512]{1,0:T(8,128)S(1)}, f32[32,512]{1,0:T(8,128)S(1)}, u32[]{:S(2)}, u32[]{:S(2)}) collective-permute-start(f32[32,512]{1,0:T(8,128)S(1)} %get-tuple-element.58.refs_1_.refs_6_.const), channel_id=1, source_target_pairs={{30,28},{31,29}} | collective-permute-start | bytes 196616 | tf_op jit(solution)/shard_map/ppermute | solution.py:497
  3.0 0.7 %shard_map.47 = (bf16[1024,256]{1,0:T(8,128)(2,1)S(1)}, bf16[1024,256]{1,0:T(8,128)(2,1)S(1)}, f32[1088,256]{1,0:T(8,128)S(1)}) custom-call(s32[1,2,3]{2,1,0:T(2,128)S(1)} %copy-done.1, f32[32,512]{1,0:T(8,128)S(1)} %get-tuple-element.58.refs_1_.refs_6_.const, bf16[2,256,256]{2,1,0:T(8,128)(2,1)S(1)} %get-tuple-element.59.refs_2_, ...), custom_call_target="tpu_custom_call" | custom-call | flops 427819008 | bytes 4194304 | tf_op jit(solution)/shard_map/pallas_call | solution.py:500
  3.8 1.3 %collective-permute-start.1 = (f32[1,544,128]{2,1,0:T(8,128)S(1)}, f32[1,544,128]{2,1,0:T(8,128)S(1)}, u32[]{:S(2)}, u32[]{:S(2)}) collective-permute-start(f32[1,544,128]{2,1,0:T(8,128)S(1)} %shard_map.48._edges), channel_id=1, source_target_pairs={{2,1},{3,0},{6,5},{7,4},{10,9},{11,8},{14,13},{15,12},{18,17},{19,... | collective-permute-start | bytes 835592 | tf_op jit(solution)/shard_map/ppermute | solution.py:457
  5.1 1.3 %collective-permute-start = (f32[1088,256]{1,0:T(8,128)S(1)}, f32[1088,256]{1,0:T(8,128)S(1)}, u32[]{:S(2)}, u32[]{:S(2)}) collective-permute-start(f32[1088,256]{1,0:T(8,128)S(1)} %shard_map.49), channel_id=1, source_target_pairs={{2,0},{3,1},{6,4},{7,5},{10,8},{11,9},{14,12},{15,13},{18,16},{19,... | collective-permute-start | bytes 3342344 | tf_op jit(solution)/shard_map/ppermute | solution.py:528
  6.4 0.0 collective-permute-done.2.next_in
  6.4 0.0 collective-permute-done.3.own_in
  6.5 0.7 %collective-permute-start.5 = (f32[32,384]{1,0:T(8,128)S(1)}, f32[32,384]{1,0:T(8,128)S(1)}, u32[]{:S(2)}, u32[]{:S(2)}) collective-permute-start(f32[32,384]{1,0:T(8,128)S(1)} %get-tuple-element.70), channel_id=1, source_target_pairs={{28,25},{29,24}} | collective-permute-start | bytes 147464 | tf_op jit(solution)/shard_map/ppermute | solution.py:457
  7.1 0.7 %collective-permute-start.4 = (f32[32,512]{1,0:T(8,128)S(1)}, f32[32,512]{1,0:T(8,128)S(1)}, u32[]{:S(2)}, u32[]{:S(2)}) collective-permute-start(f32[32,512]{1,0:T(8,128)S(1)} %get-tuple-element.69.refs_5_._lower), channel_id=1, source_target_pairs={{28,24},{29,25}} | collective-permute-start | bytes 196616 | tf_op jit(solution)/shard_map/ppermute | solution.py:603
  7.8 4.5 %collective-permute-done.far.refs_0_.rest_5_ = f32[1088,256]{1,0:T(8,128)S(1)} collective-permute-done((f32[1088,256]{1,0:T(8,128)S(1)}, f32[1088,256]{1,0:T(8,128)S(1)}, u32[]{:S(2)}, u32[]{:S(2)}) %collective-permute-start) | collective-permute-done | bytes 1114144 | tf_op jit(solution)/shard_map/ppermute | solution.py:528
  12.3 0.1 shard_map.50
  12.4 0.0 collective-permute-done.1.refs_1_
  12.6 0.7 %collective-permute-start.7 = (f32[32,384]{1,0:T(8,128)S(1)}, f32[32,384]{1,0:T(8,128)S(1)}, u32[]{:S(2)}, u32[]{:S(2)}) collective-permute-start(f32[32,384]{1,0:T(8,128)S(1)} %get-tuple-element.79), channel_id=1, source_target_pairs={{24,21},{25,20}} | collective-permute-start | bytes 147464 | tf_op jit(solution)/shard_map/ppermute | solution.py:457
  13.2 0.7 %collective-permute-start.6 = (f32[32,512]{1,0:T(8,128)S(1)}, f32[32,512]{1,0:T(8,128)S(1)}, u32[]{:S(2)}, u32[]{:S(2)}) collective-permute-start(f32[32,512]{1,0:T(8,128)S(1)} %get-tuple-element.78._lower), channel_id=1, source_target_pairs={{24,20},{25,21}} | collective-permute-start | bytes 196616 | tf_op jit(solution)/shard_map/ppermute | solution.py:603
  13.9 1.7 %shard_map.51 = (bf16[2048,256]{1,0:T(8,128)(2,1)S(1)}, bf16[2048,256]{1,0:T(8,128)(2,1)S(1)}, f32[32,512]{1,0:T(8,128)S(1)}, f32[1088,256]{1,0:T(8,128)S(1)}, f32[512,256]{1,0:T(8,128)S(1)}) custom-call(f32[1088,256]{1,0:T(8,128)S(1)} %collective-permute-done.far.refs_0_.rest_5_, f32[1,544,128]{2,1,0:T(8,128)S(1)} %collective-permute-done.1.refs_1_, ...), custom_call_target="tpu_custom_call" | custom-call | flops 1000000000 | tf_op jit(solution)/shard_map/pallas_call | solution.py:552
  15.6 0.7 %collective-permute-start.14 = (f32[1088,256]{1,0:T(8,128)S(1)}, f32[1088,256]{1,0:T(8,128)S(1)}, u32[]{:S(2)}, u32[]{:S(2)}) collective-permute-start(f32[1088,256]{1,0:T(8,128)S(1)} %get-tuple-element.94), channel_id=1, source_target_pairs={{4,8},{5,9},{8,12},{9,13}} | collective-permute-start | bytes 3342344 | tf_op jit(solution)/shard_map/ppermute | solution.py:568
  16.3 0.7 %collective-permute-start.15 = (f32[512,256]{1,0:T(8,128)S(1)}, f32[512,256]{1,0:T(8,128)S(1)}, u32[]{:S(2)}, u32[]{:S(2)}) collective-permute-start(f32[512,256]{1,0:T(8,128)S(1)} %get-tuple-element.95), channel_id=1, source_target_pairs={{4,9},{5,8},{8,13},{9,12}} | collective-permute-start | bytes 1572872 | tf_op jit(solution)/shard_map/ppermute | solution.py:457
  17.0 0.0 collective-permute-done.7.next_in
  17.1 0.7 %collective-permute-start.9 = (f32[32,512]{1,0:T(8,128)S(1)}, f32[32,512]{1,0:T(8,128)S(1)}, u32[]{:S(2)}, u32[]{:S(2)}) collective-permute-start(f32[32,512]{1,0:T(8,128)S(1)} %get-tuple-element.83._lower), channel_id=1, source_target_pairs={{20,17},{21,16}} | collective-permute-start | bytes 196616 | tf_op jit(solution)/shard_map/ppermute | solution.py:457
  17.8 0.7 %collective-permute-start.8 = (f32[32,512]{1,0:T(8,128)S(1)}, f32[32,512]{1,0:T(8,128)S(1)}, u32[]{:S(2)}, u32[]{:S(2)}) collective-permute-start(f32[32,512]{1,0:T(8,128)S(1)} %get-tuple-element.83._lower), channel_id=1, source_target_pairs={{20,16},{21,17}} | collective-permute-start | bytes 196616 | tf_op jit(solution)/shard_map/ppermute | solution.py:603
  18.4 0.0 collective-permute-done.9.next_in
  18.5 0.0 collective-permute-done.8.own_in
  18.5 0.7 %collective-permute-start.11 = (f32[32,512]{1,0:T(8,128)S(1)}, f32[32,512]{1,0:T(8,128)S(1)}, u32[]{:S(2)}, u32[]{:S(2)}) collective-permute-start(f32[32,512]{1,0:T(8,128)S(1)} %get-tuple-element.87._lower), channel_id=1, source_target_pairs={{16,13},{17,12}} | collective-permute-start | bytes 196616 | tf_op jit(solution)/shard_map/ppermute | solution.py:457
  19.2 0.7 %collective-permute-start.10 = (f32[32,512]{1,0:T(8,128)S(1)}, f32[32,512]{1,0:T(8,128)S(1)}, u32[]{:S(2)}, u32[]{:S(2)}) collective-permute-start(f32[32,512]{1,0:T(8,128)S(1)} %get-tuple-element.87._lower), channel_id=1, source_target_pairs={{16,12},{17,13}} | collective-permute-start | bytes 196616 | tf_op jit(solution)/shard_map/ppermute | solution.py:603
  19.9 0.7 %collective-permute-start.13 = (f32[32,512]{1,0:T(8,128)S(1)}, f32[32,512]{1,0:T(8,128)S(1)}, u32[]{:S(2)}, u32[]{:S(2)}) collective-permute-start(f32[32,512]{1,0:T(8,128)S(1)} %get-tuple-element.91.rest_6_.lower), channel_id=1, source_target_pairs={{12,9},{13,8}} | collective-permute-start | bytes 196616 | tf_op jit(solution)/shard_map/ppermute | solution.py:457
  20.6 0.7 %collective-permute-start.12 = (f32[32,512]{1,0:T(8,128)S(1)}, f32[32,512]{1,0:T(8,128)S(1)}, u32[]{:S(2)}, u32[]{:S(2)}) collective-permute-start(f32[32,512]{1,0:T(8,128)S(1)} %get-tuple-element.91.rest_6_.lower), channel_id=1, source_target_pairs={{12,8},{13,9}} | collective-permute-start | bytes 196616 | tf_op jit(solution)/shard_map/ppermute | solution.py:603
  21.3 0.0 collective-permute-done.13.next_in
  21.3 0.0 collective-permute-done.15.other_rows
  21.3 0.0 collective-permute-done.14.own_rows.rest_0_
  21.3 0.2 shard_map.65
  21.6 0.0 collective-permute-done.12.own_in
  21.7 1.3 %collective-permute-start.16 = (f32[32,896]{1,0:T(8,128)S(1)}, f32[32,896]{1,0:T(8,128)S(1)}, u32[]{:S(2)}, u32[]{:S(2)}) collective-permute-start(f32[32,896]{1,0:T(8,128)S(1)} %get-tuple-element.101), channel_id=1, source_target_pairs={{9,0}} | collective-permute-start | bytes 344072 | tf_op jit(solution)/shard_map/ppermute | solution.py:597
  23.0 1.3 %collective-permute-start.17 = (f32[32,896]{1,0:T(8,128)S(1)}, f32[32,896]{1,0:T(8,128)S(1)}, u32[]{:S(2)}, u32[]{:S(2)}) collective-permute-start(f32[32,896]{1,0:T(8,128)S(1)} %get-tuple-element.102), channel_id=1, source_target_pairs={{8,0},{9,1}} | collective-permute-start | bytes 344072 | tf_op jit(solution)/shard_map/ppermute | solution.py:598
  24.3 0.7 %collective-permute-start.18 = (f32[32,896]{1,0:T(8,128)S(1)}, f32[32,896]{1,0:T(8,128)S(1)}, u32[]{:S(2)}, u32[]{:S(2)}) collective-permute-start(f32[32,896]{1,0:T(8,128)S(1)} %get-tuple-element.103), channel_id=1, source_target_pairs={{8,1}} | collective-permute-start | bytes 344072 | tf_op jit(solution)/shard_map/ppermute | solution.py:599
  25.0 0.7 %collective-permute-start.19 = (f32[32,896]{1,0:T(8,128)S(1)}, f32[32,896]{1,0:T(8,128)S(1)}, u32[]{:S(2)}, u32[]{:S(2)}) collective-permute-start(f32[32,896]{1,0:T(8,128)S(1)} %get-tuple-element.104), channel_id=1, source_target_pairs={{12,5},{13,4}} | collective-permute-start | bytes 344072 | tf_op jit(solution)/shard_map/ppermute | solution.py:457
  25.6 0.7 %collective-permute-start.20 = (f32[32,896]{1,0:T(8,128)S(1)}, f32[32,896]{1,0:T(8,128)S(1)}, u32[]{:S(2)}, u32[]{:S(2)}) collective-permute-start(f32[32,896]{1,0:T(8,128)S(1)} %get-tuple-element.105), channel_id=1, source_target_pairs={{12,4},{13,5}} | collective-permute-start | bytes 344072 | tf_op jit(solution)/shard_map/ppermute | solution.py:615
  26.3 22.8 %collective-permute-done.16.rest_0_ = f32[32,896]{1,0:T(8,128)S(1)} collective-permute-done((f32[32,896]{1,0:T(8,128)S(1)}, f32[32,896]{1,0:T(8,128)S(1)}, u32[]{:S(2)}, u32[]{:S(2)}) %collective-permute-start.16) | collective-permute-done | bytes 114720 | tf_op jit(solution)/shard_map/ppermute | solution.py:597
  49.1 0.2 collective-permute-done.17.rest_1_
  49.4 0.0 collective-permute-done.19.rest_3_
  49.4 0.0 collective-permute-done.20.rest_4_
  49.4 0.3 shard_map.68
  49.7 1.3 %collective-permute-start.21 = (f32[32,512]{1,0:T(8,128)S(1)}, f32[32,512]{1,0:T(8,128)S(1)}, u32[]{:S(2)}, u32[]{:S(2)}) collective-permute-start(f32[32,512]{1,0:T(8,128)S(1)} %get-tuple-element.110), channel_id=1, source_target_pairs={{0,2},{1,3},{4,6},{5,7},{8,10},{9,11},{12,14},{13,15},{16,18},{17,... | collective-permute-start | bytes 196616 | tf_op jit(solution)/shard_map/ppermute | solution.py:646
  51.0 0.5 shard_map.69
  51.5 0.4 collective-permute-done.21
  51.9 0.6 %select_bitcast_fusion = f32[1,32,512]{2,1,0:T(8,128)} fusion(f32[32,512]{1,0:T(8,128)S(1)} %shard_map.69, f32[32,512]{1,0:T(8,128)S(1)} %collective-permute-done.21, pred[]{:T(512)S(6)} %eq.5), kind=kLoop, calls=%fused_computation | loop fusion | flops 16384 | bytes 196609 | tf_op jit(solution)/shard_map/broadcast_in_dim | solution.py:656
  (28 shorter events, 0.4 us)
Async XLA Ops:
  1.5 1.5 %copy-start = (f32[1,2,512,256]{3,2,1,0:T(8,128)S(1)}, f32[1,2,512,256]{3,2,1,0:T(8,128)}, u32[]{:S(2)}) copy-start(f32[1,2,512,256]{3,2,1,0:T(8,128)} %refs_4_.3) | copy-start | bytes 3145732
  1.5 1.5 %copy-start.1 = (s32[1,2,3]{2,1,0:T(2,128)S(1)}, s32[1,2,3]{2,1,0:T(2,128)}, u32[]{:S(2)}) copy-start(s32[1,2,3]{2,1,0:T(2,128)} %refs_0_.3) | copy-start | bytes 76
  1.5 4.9 %collective-permute-start.2 = (f32[32,512]{1,0:T(8,128)S(1)}, f32[32,512]{1,0:T(8,128)S(1)}, u32[]{:S(2)}, u32[]{:S(2)}) collective-permute-start(f32[32,512]{1,0:T(8,128)S(1)} %shard_map.52), channel_id=1, source_target_pairs={{30,29},{31,28}} | collective-permute-start | bytes 196616 | tf_op jit(solution)/shard_map/ppermute | solution.py:457
  2.3 4.1 %collective-permute-start.3 = (f32[32,512]{1,0:T(8,128)S(1)}, f32[32,512]{1,0:T(8,128)S(1)}, u32[]{:S(2)}, u32[]{:S(2)}) collective-permute-start(f32[32,512]{1,0:T(8,128)S(1)} %get-tuple-element.58.refs_1_.refs_6_.const), channel_id=1, source_target_pairs={{30,28},{31,29}} | collective-permute-start | bytes 196616 | tf_op jit(solution)/shard_map/ppermute | solution.py:497
  3.8 8.7 %collective-permute-start.1 = (f32[1,544,128]{2,1,0:T(8,128)S(1)}, f32[1,544,128]{2,1,0:T(8,128)S(1)}, u32[]{:S(2)}, u32[]{:S(2)}) collective-permute-start(f32[1,544,128]{2,1,0:T(8,128)S(1)} %shard_map.48._edges), channel_id=1, source_target_pairs={{2,1},{3,0},{6,5},{7,4},{10,9},{11,8},{14,13},{15,12},{18,17},{19,... | collective-permute-start | bytes 835592 | tf_op jit(solution)/shard_map/ppermute | solution.py:457
  5.1 7.2 %collective-permute-start = (f32[1088,256]{1,0:T(8,128)S(1)}, f32[1088,256]{1,0:T(8,128)S(1)}, u32[]{:S(2)}, u32[]{:S(2)}) collective-permute-start(f32[1088,256]{1,0:T(8,128)S(1)} %shard_map.49), channel_id=1, source_target_pairs={{2,0},{3,1},{6,4},{7,5},{10,8},{11,9},{14,12},{15,13},{18,16},{19,... | collective-permute-start | bytes 3342344 | tf_op jit(solution)/shard_map/ppermute | solution.py:528
  6.5 6.0 %collective-permute-start.5 = (f32[32,384]{1,0:T(8,128)S(1)}, f32[32,384]{1,0:T(8,128)S(1)}, u32[]{:S(2)}, u32[]{:S(2)}) collective-permute-start(f32[32,384]{1,0:T(8,128)S(1)} %get-tuple-element.70), channel_id=1, source_target_pairs={{28,25},{29,24}} | collective-permute-start | bytes 147464 | tf_op jit(solution)/shard_map/ppermute | solution.py:457
  7.1 5.4 %collective-permute-start.4 = (f32[32,512]{1,0:T(8,128)S(1)}, f32[32,512]{1,0:T(8,128)S(1)}, u32[]{:S(2)}, u32[]{:S(2)}) collective-permute-start(f32[32,512]{1,0:T(8,128)S(1)} %get-tuple-element.69.refs_5_._lower), channel_id=1, source_target_pairs={{28,24},{29,25}} | collective-permute-start | bytes 196616 | tf_op jit(solution)/shard_map/ppermute | solution.py:603
  12.6 4.5 %collective-permute-start.7 = (f32[32,384]{1,0:T(8,128)S(1)}, f32[32,384]{1,0:T(8,128)S(1)}, u32[]{:S(2)}, u32[]{:S(2)}) collective-permute-start(f32[32,384]{1,0:T(8,128)S(1)} %get-tuple-element.79), channel_id=1, source_target_pairs={{24,21},{25,20}} | collective-permute-start | bytes 147464 | tf_op jit(solution)/shard_map/ppermute | solution.py:457
  13.2 3.8 %collective-permute-start.6 = (f32[32,512]{1,0:T(8,128)S(1)}, f32[32,512]{1,0:T(8,128)S(1)}, u32[]{:S(2)}, u32[]{:S(2)}) collective-permute-start(f32[32,512]{1,0:T(8,128)S(1)} %get-tuple-element.78._lower), channel_id=1, source_target_pairs={{24,20},{25,21}} | collective-permute-start | bytes 196616 | tf_op jit(solution)/shard_map/ppermute | solution.py:603
  15.6 5.7 %collective-permute-start.14 = (f32[1088,256]{1,0:T(8,128)S(1)}, f32[1088,256]{1,0:T(8,128)S(1)}, u32[]{:S(2)}, u32[]{:S(2)}) collective-permute-start(f32[1088,256]{1,0:T(8,128)S(1)} %get-tuple-element.94), channel_id=1, source_target_pairs={{4,8},{5,9},{8,12},{9,13}} | collective-permute-start | bytes 3342344 | tf_op jit(solution)/shard_map/ppermute | solution.py:568
  16.3 5.0 %collective-permute-start.15 = (f32[512,256]{1,0:T(8,128)S(1)}, f32[512,256]{1,0:T(8,128)S(1)}, u32[]{:S(2)}, u32[]{:S(2)}) collective-permute-start(f32[512,256]{1,0:T(8,128)S(1)} %get-tuple-element.95), channel_id=1, source_target_pairs={{4,9},{5,8},{8,13},{9,12}} | collective-permute-start | bytes 1572872 | tf_op jit(solution)/shard_map/ppermute | solution.py:457
  17.1 1.3 %collective-permute-start.9 = (f32[32,512]{1,0:T(8,128)S(1)}, f32[32,512]{1,0:T(8,128)S(1)}, u32[]{:S(2)}, u32[]{:S(2)}) collective-permute-start(f32[32,512]{1,0:T(8,128)S(1)} %get-tuple-element.83._lower), channel_id=1, source_target_pairs={{20,17},{21,16}} | collective-permute-start | bytes 196616 | tf_op jit(solution)/shard_map/ppermute | solution.py:457
  17.8 0.7 %collective-permute-start.8 = (f32[32,512]{1,0:T(8,128)S(1)}, f32[32,512]{1,0:T(8,128)S(1)}, u32[]{:S(2)}, u32[]{:S(2)}) collective-permute-start(f32[32,512]{1,0:T(8,128)S(1)} %get-tuple-element.83._lower), channel_id=1, source_target_pairs={{20,16},{21,17}} | collective-permute-start | bytes 196616 | tf_op jit(solution)/shard_map/ppermute | solution.py:603
  18.5 1.3 %collective-permute-start.11 = (f32[32,512]{1,0:T(8,128)S(1)}, f32[32,512]{1,0:T(8,128)S(1)}, u32[]{:S(2)}, u32[]{:S(2)}) collective-permute-start(f32[32,512]{1,0:T(8,128)S(1)} %get-tuple-element.87._lower), channel_id=1, source_target_pairs={{16,13},{17,12}} | collective-permute-start | bytes 196616 | tf_op jit(solution)/shard_map/ppermute | solution.py:457
  19.2 0.7 %collective-permute-start.10 = (f32[32,512]{1,0:T(8,128)S(1)}, f32[32,512]{1,0:T(8,128)S(1)}, u32[]{:S(2)}, u32[]{:S(2)}) collective-permute-start(f32[32,512]{1,0:T(8,128)S(1)} %get-tuple-element.87._lower), channel_id=1, source_target_pairs={{16,12},{17,13}} | collective-permute-start | bytes 196616 | tf_op jit(solution)/shard_map/ppermute | solution.py:603
  19.9 1.3 %collective-permute-start.13 = (f32[32,512]{1,0:T(8,128)S(1)}, f32[32,512]{1,0:T(8,128)S(1)}, u32[]{:S(2)}, u32[]{:S(2)}) collective-permute-start(f32[32,512]{1,0:T(8,128)S(1)} %get-tuple-element.91.rest_6_.lower), channel_id=1, source_target_pairs={{12,9},{13,8}} | collective-permute-start | bytes 196616 | tf_op jit(solution)/shard_map/ppermute | solution.py:457
  20.6 1.0 %collective-permute-start.12 = (f32[32,512]{1,0:T(8,128)S(1)}, f32[32,512]{1,0:T(8,128)S(1)}, u32[]{:S(2)}, u32[]{:S(2)}) collective-permute-start(f32[32,512]{1,0:T(8,128)S(1)} %get-tuple-element.91.rest_6_.lower), channel_id=1, source_target_pairs={{12,8},{13,9}} | collective-permute-start | bytes 196616 | tf_op jit(solution)/shard_map/ppermute | solution.py:603
  21.7 27.5 %collective-permute-start.16 = (f32[32,896]{1,0:T(8,128)S(1)}, f32[32,896]{1,0:T(8,128)S(1)}, u32[]{:S(2)}, u32[]{:S(2)}) collective-permute-start(f32[32,896]{1,0:T(8,128)S(1)} %get-tuple-element.101), channel_id=1, source_target_pairs={{9,0}} | collective-permute-start | bytes 344072 | tf_op jit(solution)/shard_map/ppermute | solution.py:597
  23.0 26.4 %collective-permute-start.17 = (f32[32,896]{1,0:T(8,128)S(1)}, f32[32,896]{1,0:T(8,128)S(1)}, u32[]{:S(2)}, u32[]{:S(2)}) collective-permute-start(f32[32,896]{1,0:T(8,128)S(1)} %get-tuple-element.102), channel_id=1, source_target_pairs={{8,0},{9,1}} | collective-permute-start | bytes 344072 | tf_op jit(solution)/shard_map/ppermute | solution.py:598
  24.3 25.1 %collective-permute-start.18 = (f32[32,896]{1,0:T(8,128)S(1)}, f32[32,896]{1,0:T(8,128)S(1)}, u32[]{:S(2)}, u32[]{:S(2)}) collective-permute-start(f32[32,896]{1,0:T(8,128)S(1)} %get-tuple-element.103), channel_id=1, source_target_pairs={{8,1}} | collective-permute-start | bytes 344072 | tf_op jit(solution)/shard_map/ppermute | solution.py:599
  25.0 24.4 %collective-permute-start.19 = (f32[32,896]{1,0:T(8,128)S(1)}, f32[32,896]{1,0:T(8,128)S(1)}, u32[]{:S(2)}, u32[]{:S(2)}) collective-permute-start(f32[32,896]{1,0:T(8,128)S(1)} %get-tuple-element.104), channel_id=1, source_target_pairs={{12,5},{13,4}} | collective-permute-start | bytes 344072 | tf_op jit(solution)/shard_map/ppermute | solution.py:457
  25.6 23.7 %collective-permute-start.20 = (f32[32,896]{1,0:T(8,128)S(1)}, f32[32,896]{1,0:T(8,128)S(1)}, u32[]{:S(2)}, u32[]{:S(2)}) collective-permute-start(f32[32,896]{1,0:T(8,128)S(1)} %get-tuple-element.105), channel_id=1, source_target_pairs={{12,4},{13,5}} | collective-permute-start | bytes 344072 | tf_op jit(solution)/shard_map/ppermute | solution.py:615
  49.7 2.2 %collective-permute-start.21 = (f32[32,512]{1,0:T(8,128)S(1)}, f32[32,512]{1,0:T(8,128)S(1)}, u32[]{:S(2)}, u32[]{:S(2)}) collective-permute-start(f32[32,512]{1,0:T(8,128)S(1)} %get-tuple-element.110), channel_id=1, source_target_pairs={{0,2},{1,3},{4,6},{5,7},{8,10},{9,11},{12,14},{13,15},{16,18},{17,... | collective-permute-start | bytes 196616 | tf_op jit(solution)/shard_map/ppermute | solution.py:646
